TPU v7x, 32 devices: a whole 2x2x4 slice. The times are simulated.
32 devices in a mesh: sec: 4 (over x, core), px: 2 (over y), py: 4 (over z).
Axes of the slice: x: 2, y: 2, z: 4, core: 2. Of those that a mesh axis runs over, the one named last changes fastest.
Arguments:
- background: bfloat16 [2, 4, 512, 8192], P(None, 'sec', 'px', 'py'), may hold values from -6 to 6
- src_pos: int32 [16], replicated, may hold values from 0 to 1048575
- coupling: bfloat16 [4, 512, 512], P('sec', 'px'), may hold values from 0.3984375 to 1
- x_factor: bfloat16 [4, 2, 512, 512], P('sec', None, ('px', 'py')), may hold values from -1.25 to 1.25, as said below
- y_factor: bfloat16 [4, 2, 512, 512], P('sec', None, ('px', 'py')), may hold values from -1.25 to 1.25, as said below
Outputs:
- sweep_out: bfloat16 [2, 4, 512, 8192], P(None, 'sec', 'px', 'py')
Inputs may be any that keep to these rules, and one draw needn't show every extreme that they name: `x_factor`: factor entries; each is a dense complex matrix. `y_factor`: factor entries; each is a dense complex matrix.
All inputs are finite; a program needn't handle non-finite values.
Results may differ from a plain program's by a relative error of at most 0.02.
Values may be sent and summed in bfloat16 or wider, within the bound.
No kernel may reach another device: no remote copies, remote signals or barrier semaphores. Data moves between devices by JAX's collectives and lax.ppermute only.
A program may use at most 64 MiB of HBM per device.

v0:
```python
import functools

import jax
import jax.numpy as jnp
from jax import lax
from jax.experimental import pallas as pl
from jax.experimental.pallas import tpu as pltpu
from jax.sharding import PartitionSpec as P

source_amplitude = 8.0
vmem_bytes = 40 * 1024 * 1024
bf16 = jnp.bfloat16
f32 = jnp.float32
anywhere = pl.BlockSpec(memory_space=pl.ANY)
in_smem = pl.BlockSpec(memory_space=pltpu.SMEM)
in_vmem = pl.BlockSpec(memory_space=pltpu.VMEM)


def shifted(x, axis, by):
    peers = lax.axis_size(axis)
    pairs = [(i, i + by) for i in range(peers) if 0 <= i + by < peers]
    return lax.ppermute(x, axis, pairs)


def complex_block(factor):
    upper = jnp.concatenate([factor[0], -factor[1]], axis=1)
    lower = jnp.concatenate([factor[1], factor[0]], axis=1)
    return jnp.concatenate([upper, lower], axis=0)


def y_transform(real_turned, imag_turned, field_in):
    real_part = jnp.dot(field_in[0], real_turned, preferred_element_type=jnp.float32) - jnp.dot(
        field_in[1], imag_turned, preferred_element_type=jnp.float32
    )
    imag_part = jnp.dot(field_in[0], imag_turned, preferred_element_type=jnp.float32) + jnp.dot(
        field_in[1], real_turned, preferred_element_type=jnp.float32
    )
    return jnp.stack([real_part, imag_part]).astype(jnp.bfloat16)


def x_transform(x_block, field_in):
    planes, rows_all, width = field_in.shape
    output = jnp.dot(
        x_block, field_in.reshape(planes * rows_all, width), preferred_element_type=jnp.float32
    )
    return output.astype(jnp.bfloat16).reshape(planes, rows_all, width)


def scale_rows(field_in, weights, width):
    planes, rows_here, merged = field_in.shape
    spread = field_in.astype(jnp.float32).reshape(planes, rows_here, merged // width, width)
    return (spread * weights.astype(jnp.float32)[None, :, None, :]).reshape(
        planes, rows_here, merged
    )


def pick_batch(field, batch_count, batch_index):
    planes, rows_here, merged = field.shape
    split_field = field.reshape(planes, rows_here, batch_count, merged // batch_count)
    return lax.dynamic_index_in_dim(split_field, batch_index, 2, keepdims=False)


def place_batch(field, piece, batch_count, batch_index):
    planes, rows_here, merged = field.shape
    split_field = field.reshape(planes, rows_here, batch_count, merged // batch_count)
    shaped = piece.reshape(planes, rows_here, 1, merged // batch_count)
    updated = lax.dynamic_update_slice_in_dim(split_field, shaped, batch_index, 2)
    return updated.reshape(planes, rows_here, merged)


def on_device_by_layer(background, src_pos, coupling, x_factor, y_factor):
    source_count = src_pos.shape[0]
    sec_count = lax.axis_size("sec")
    sec_index = lax.axis_index("sec")
    grid_y = lax.axis_size("py")
    own_x = lax.axis_index("px")
    own_y = lax.axis_index("py")
    local_sources = source_count // grid_y
    x_pieces, y_pieces = (
        lax.all_gather(x_factor[0], ("px", "py"), axis=1, tiled=True),
        lax.all_gather(y_factor[0], ("px", "py"), axis=1, tiled=True),
    )
    x_block = complex_block(x_pieces)
    real_turned = y_pieces[0].T
    imag_turned = y_pieces[1].T
    local_field = background[:, 0]
    local_weights = coupling[0]
    rows_here = local_field.shape[1]
    full_cols = y_factor.shape[3]
    plane_cells = x_factor.shape[3] * full_cols
    own_sources = lax.dynamic_slice_in_dim(src_pos, own_y * local_sources, local_sources)
    layer_of = own_sources // plane_cells
    remainder = own_sources % plane_cells
    row_of = remainder // full_cols
    column_of = remainder % full_cols
    row_start = own_x * rows_here
    row_hit = row_of[None, :] == row_start + jnp.arange(rows_here, dtype=jnp.int32)[:, None]
    col_hit = column_of[:, None] == jnp.arange(full_cols, dtype=jnp.int32)[None, :]
    layer_hit = layer_of == sec_index
    delta = (row_hit[:, :, None] & col_hit[None, :, :] & layer_hit[None, :, None]).astype(
        jnp.float32
    )
    delta = (delta * source_amplitude).reshape(rows_here, local_sources * full_cols)
    real_rhs = local_field[0].astype(jnp.float32) + delta
    rhs_field = jnp.stack([real_rhs, local_field[1].astype(jnp.float32)])

    def apply_front(field_in):
        turned = y_transform(real_turned, imag_turned, field_in)
        line_field = lax.all_to_all(turned, "px", split_axis=2, concat_axis=1, tiled=True)
        finished = x_transform(x_block, line_field)
        return lax.all_to_all(finished, "px", split_axis=1, concat_axis=2, tiled=True)

    forward_field = jnp.zeros(local_field.shape, jnp.bfloat16)
    outgoing = pick_batch(forward_field, sec_count, 0)
    for step in range(2 * sec_count - 1):
        incoming = shifted(outgoing, "sec", 1)
        batch_index = step - sec_index
        active = (batch_index >= 0) & (batch_index < sec_count)
        clamped = jnp.clip(batch_index, 0, sec_count - 1)
        rhs_batch = pick_batch(rhs_field, sec_count, clamped)
        reduced = (rhs_batch - scale_rows(incoming, local_weights, full_cols)).astype(jnp.bfloat16)
        candidate = apply_front(reduced)
        previous = pick_batch(forward_field, sec_count, clamped)
        kept = jnp.where(active, candidate, previous)
        forward_field = place_batch(forward_field, kept, sec_count, clamped)
        outgoing = candidate
    sweep_field = forward_field
    for step in range(2 * sec_count - 2):
        send_index = jnp.clip(step - (sec_count - 1 - sec_index), 0, sec_count - 1)
        own_batch = pick_batch(sweep_field, sec_count, send_index)
        sent_field = scale_rows(own_batch, local_weights, full_cols).astype(jnp.bfloat16)
        incoming = shifted(sent_field, "sec", -1)
        batch_index = step - (sec_count - 2 - sec_index)
        active = (batch_index >= 0) & (batch_index < sec_count) & (sec_index <= sec_count - 2)
        clamped = jnp.clip(batch_index, 0, sec_count - 1)
        solved = apply_front(incoming)
        forward_batch = pick_batch(forward_field, sec_count, clamped)
        candidate = (forward_batch.astype(jnp.float32) - solved.astype(jnp.float32)).astype(
            jnp.bfloat16
        )
        previous = pick_batch(sweep_field, sec_count, clamped)
        kept = jnp.where(active, candidate, previous)
        sweep_field = place_batch(sweep_field, kept, sec_count, clamped)
    return sweep_field[:, None]


def start_all(copies):
    for copy in copies:
        copy.start()


def wait_all(copies):
    for copy in copies:
        copy.wait()


def row_chunks(order, step):
    step = min(step, order)
    return [slice(first, first + step) for first in range(0, order, step)]


def pack_kernel(place, field, *rest):
    pieces, sems = rest[:-1], rest[-1]
    copies = []
    for index, piece in enumerate(pieces):
        width = piece.shape[2]
        offset = pl.multiple_of(place[index] * width, width)
        copies.append(
            pltpu.make_async_copy(field.at[:, :, pl.ds(offset, width)], piece, sems.at[index])
        )
    start_all(copies)
    wait_all(copies)


def unpack_kernel(place, *rest):
    pieces, field, sems = rest[:-2], rest[-2], rest[-1]
    copies = []
    for index, piece in enumerate(pieces):
        width = piece.shape[2]
        offset = pl.multiple_of(place[index] * width, width)
        copies.append(
            pltpu.make_async_copy(piece, field.at[:, :, pl.ds(offset, width)], sems.at[index])
        )
    start_all(copies)
    wait_all(copies)


class Factors:
    def __init__(self, gathered, slot_from, slot, plain, crossed, sems):
        order = gathered.shape[-1]
        left, right = pl.ds(0, order), pl.ds(order, order)
        self.order, self.slot = order, slot
        self.plain, self.crossed = plain, crossed
        self.copies = []
        for which in range(2):
            real = gathered.at[:, slot_from, 2 * which]
            imag = gathered.at[:, slot_from, 2 * which + 1]
            ends = (
                (real, plain, left),
                (imag, plain, right),
                (imag, crossed, left),
                (real, crossed, right),
            )
            self.copies.append(
                [
                    pltpu.make_async_copy(
                        source, target.at[slot, which, :, :, half], sems.at[slot, which, index]
                    )
                    for index, (source, target, half) in enumerate(ends)
                ]
            )

    def start(self):
        start_all(self.copies[1])
        start_all(self.copies[0])

    def ready(self, which):
        wait_all(self.copies[which])
        right = slice(self.order, 2 * self.order)
        self.plain[self.slot, which, :, :, right] = -self.plain[self.slot, which, :, :, right]

    def apply(self, beside, below, store, fresh):
        order = self.order
        turned = (((1,), (1,)), ((), ()))
        if fresh:
            self.ready(1)
        for plane, ref in enumerate((self.plain, self.crossed)):
            blocks, height = ref.shape[2:4]
            for columns in row_chunks(order, 256):
                rows = ref[self.slot, 1, columns.start // height : columns.stop // height]
                rows = rows.reshape(columns.stop - columns.start, 2 * order)
                part = lax.dot_general(beside[...], rows, turned, preferred_element_type=f32)
                below[plane * order : (plane + 1) * order, columns] = part.astype(bf16)
        if fresh:
            self.ready(0)
        for plane, ref in enumerate((self.plain, self.crossed)):
            matrix = ref[self.slot, 0].reshape(order, 2 * order)
            for columns in row_chunks(order, 256):
                store(
                    plane,
                    columns,
                    jnp.dot(matrix, below[:, columns], preferred_element_type=f32),
                )


def rows_of(blocked, slot, rows):
    height = blocked.shape[2]
    part = blocked[slot, rows.start // height : rows.stop // height]
    return part.reshape(rows.stop - rows.start, part.shape[-1])


def reduce_into(beside, rhs, info, slot, weights, incoming):
    order = beside.shape[0]
    for plane in range(2):
        for rows in row_chunks(order, 128):
            values = rhs[slot, plane, rows].astype(f32)
            if plane == 0:
                row = lax.broadcasted_iota(jnp.int32, values.shape, 0) + rows.start
                column = lax.broadcasted_iota(jnp.int32, values.shape, 1)
                hit = (row == info[1]) & (column == info[2]) & (info[0] == slot)
                values = values + jnp.where(hit, f32(source_amplitude), f32(0.0))
            scaled = rows_of(weights, slot, rows).astype(f32) * incoming(plane, rows)
            beside[rows, plane * order : (plane + 1) * order] = (values - scaled).astype(bf16)


def sent_into(beside, weights, slot, field):
    order = beside.shape[0]
    for plane in range(2):
        for rows in row_chunks(order, 128):
            scaled = rows_of(weights, slot, rows).astype(f32) * field(plane, rows)
            beside[rows, plane * order : (plane + 1) * order] = scaled.astype(bf16)


def subtract_into(target, forward):
    def store(plane, columns, values):
        solved = values.astype(bf16).astype(f32)
        target[plane, :, columns] = (forward(plane, columns).astype(f32) - solved).astype(bf16)

    return store


def round_into(target):
    def store(plane, columns, values):
        target[plane, :, columns] = values.astype(bf16)

    return store


def rhs_copies(info, pieces, rhs, sems):
    copies = []
    for index, piece in enumerate(pieces):
        height = piece.shape[1]
        rows = pl.ds(pl.multiple_of(info[5 + 2 * index] * height, height), height)
        copies.append(
            pltpu.make_async_copy(piece, rhs.at[info[4 + 2 * index], :, rows, :], sems.at[index])
        )
    return copies


def weight_copies(info, gathered, weights, sems):
    return [
        pltpu.make_async_copy(gathered.at[:, info[12 + slot], 4], weights.at[slot], sems.at[slot])
        for slot in range(2)
    ]


def layer_factors(info, gathered, plain, crossed, sems):
    return [Factors(gathered, info[12 + slot], slot, plain, crossed, sems) for slot in range(2)]


def first_kernel(info, gathered, p0, p1, p2, p3, w_low, w_high, plain, crossed, weights, rhs,
                 beside, below, sems, fsems):
    @pl.when(info[3] == 0)
    def _():
        low, high = layer_factors(info, gathered, plain, crossed, fsems)
        early = rhs_copies(info, (p0, p1, p2, p3), rhs, sems)
        early += weight_copies(info, gathered, weights, sems.at[pl.ds(4, 2)])
        start_all(early)
        low.start()
        high.start()
        wait_all(early)
        reduce_into(beside, rhs, info, 0, weights, lambda plane, rows: f32(0.0))
        low.apply(beside, below, round_into(w_low), True)
        reduce_into(
            beside, rhs, info, 1, weights, lambda plane, rows: w_low[plane, rows].astype(f32)
        )
        high.apply(beside, below, round_into(w_high), True)


def last_kernel(info, gathered, p0, p1, p2, p3, incoming, field, sent, plain, crossed, weights, rhs,
                arrived, kept, beside, below, sems, fsems, osems):
    @pl.when(info[3] == 1)
    def _():
        low, high = layer_factors(info, gathered, plain, crossed, fsems)
        early = rhs_copies(info, (p0, p1, p2, p3), rhs, sems)
        early += weight_copies(info, gathered, weights, sems.at[pl.ds(4, 2)])
        early.append(pltpu.make_async_copy(incoming, arrived, sems.at[6]))
        start_all(early)
        low.start()
        high.start()
        wait_all(early)
        order = beside.shape[0]
        reduce_into(
            beside, rhs, info, 0, weights, lambda plane, rows: arrived[plane, rows].astype(f32)
        )
        w_low, w_high = kept.at[0], kept.at[1]
        low.apply(beside, below, round_into(w_low), True)
        reduce_into(
            beside, rhs, info, 1, weights, lambda plane, rows: w_low[plane, rows].astype(f32)
        )
        high.apply(beside, below, round_into(w_high), True)
        out_high = pltpu.make_async_copy(w_high, field.at[1], osems.at[1])
        out_high.start()
        sent_into(beside, weights, 1, lambda plane, rows: w_high[plane, rows].astype(f32))
        low.apply(
            beside,
            below,
            subtract_into(w_low, lambda plane, columns: w_low[plane, :, columns]),
            False,
        )
        out_low = pltpu.make_async_copy(w_low, field.at[0], osems.at[0])
        out_low.start()
        sent_into(beside, weights, 0, lambda plane, rows: w_low[plane, rows].astype(f32))
        for plane in range(2):
            sent[plane] = beside[:, plane * order : (plane + 1) * order]
        out_high.wait()
        out_low.wait()


def back_kernel(info, gathered, w_low, w_high, incoming, field, p0, p1, p2, p3, plain, crossed,
                weights, kept, beside, below, sems, fsems, osems):
    pieces = (p0, p1, p2, p3)

    def piece_copies(source):
        copies = []
        for index, piece in enumerate(pieces):
            height = piece.shape[1]
            rows = pl.ds(pl.multiple_of(info[5 + 2 * index] * height, height), height)
            copies.append(
                pltpu.make_async_copy(
                    source.at[info[4 + 2 * index], :, rows, :], piece, osems.at[index]
                )
            )
        return copies

    @pl.when(info[3] == 0)
    def _():
        low, high = layer_factors(info, gathered, plain, crossed, fsems)
        order = beside.shape[0]
        columns = [pl.ds(plane * order, order) for plane in range(2)]
        early = [
            pltpu.make_async_copy(incoming.at[plane], beside.at[:, columns[plane]], sems.at[plane])
            for plane in range(2)
        ]
        start_all(early)
        high.start()
        later = weight_copies(info, gathered, weights, sems.at[pl.ds(2, 2)])
        later.append(pltpu.make_async_copy(w_low, kept.at[0], sems.at[4]))
        later.append(pltpu.make_async_copy(w_high, kept.at[1], sems.at[5]))
        start_all(later)
        low.start()
        wait_all(early)
        wait_all(later)
        u_low, u_high = kept.at[0], kept.at[1]
        high.apply(
            beside,
            below,
            subtract_into(u_high, lambda plane, columns: u_high[plane, :, columns]),
            True,
        )
        sent_into(beside, weights, 1, lambda plane, rows: u_high[plane, rows].astype(f32))
        low.apply(
            beside,
            below,
            subtract_into(u_low, lambda plane, columns: u_low[plane, :, columns]),
            True,
        )
        copies = piece_copies(kept)
        start_all(copies)
        wait_all(copies)

    @pl.when(info[3] != 0)
    def _():
        copies = piece_copies(field)
        start_all(copies)
        wait_all(copies)


def on_device(background, src_pos, coupling, x_factor, y_factor):
    px_count = lax.axis_size("px")
    sec_index, own_x, own_y = (lax.axis_index(axis) for axis in ("sec", "px", "py"))
    group, member = sec_index // 2, sec_index % 2
    groups = lax.axis_size("sec") // 2
    order = y_factor.shape[3]
    field = background[:, 0]
    rows_here = field.shape[1]
    height = x_factor.shape[2]
    params = pltpu.CompilerParams(vmem_limit_bytes=vmem_bytes)
    rounds = [(a, b) for a in range(groups) for b in range(px_count)]

    def pairs(a, b):
        return [
            ((2 * x + c) * px_count + y, (2 * ((c + a) % 2) + x) * px_count + (y + b) % px_count)
            for x in range(groups)
            for c in range(2)
            for y in range(px_count)
        ]

    def back_pairs(a, b):
        return [(target, source) for source, target in pairs(a, b)]

    shard_weights = lax.dynamic_slice_in_dim(coupling[0], own_y * height, height)
    shard = jnp.concatenate([x_factor[0], y_factor[0], shard_weights[None]], axis=0)
    shards = [lax.ppermute(shard, ("sec", "px"), pairs(a, 0)) for a in range(2)]
    gathered = lax.all_gather(jnp.stack(shards), ("px", "py"), axis=0, tiled=False)

    sends_to = jnp.stack(
        [((member + a) % 2) * px_count + (own_x + b) % px_count for a, b in rounds]
    ).astype(jnp.int32)
    piece_shape = jax.ShapeDtypeStruct((2, rows_here, order), bf16)
    pieces = pl.pallas_call(
        pack_kernel,
        out_shape=[piece_shape] * len(rounds),
        in_specs=[in_smem, anywhere],
        out_specs=[anywhere] * len(rounds),
        scratch_shapes=[pltpu.SemaphoreType.DMA((len(rounds),))],
        compiler_params=params,
    )(sends_to, field)
    pieces = [
        lax.ppermute(piece, ("sec", "px"), pairs(a, b)) for piece, (a, b) in zip(pieces, rounds)
    ]

    own_source = src_pos[own_y * groups * px_count + group * px_count + own_x]
    plane_cells = x_factor.shape[3] * order
    layer = own_source // plane_cells
    remainder = own_source % plane_cells
    entries = [
        jnp.where(layer // 2 == member, layer % 2, -1),
        remainder // order,
        remainder % order,
        member,
    ]
    for a, b in rounds:
        entries += [(group + a) % 2, (own_x - b) % px_count]
    entries += [group, (group + 1) % 2]
    info = jnp.stack([jnp.asarray(entry, jnp.int32) for entry in entries])

    full_shape = jax.ShapeDtypeStruct((2, order, order), bf16)
    blocks = gathered.shape[0]
    factor_scratch = pltpu.VMEM((2, 2, blocks, height, 2 * order), bf16)
    weight_scratch = pltpu.VMEM((2, blocks, height, order), bf16)
    field_scratch = pltpu.VMEM((2, 2, order, order), bf16)
    beside_scratch = pltpu.VMEM((order, 2 * order), bf16)
    below_scratch = pltpu.VMEM((2 * order, order), bf16)
    factor_sems = pltpu.SemaphoreType.DMA((2, 2, 4))
    solve_flops = 16 * order**3
    w_low, w_high = pl.pallas_call(
        first_kernel,
        out_shape=[full_shape] * 2,
        in_specs=[in_smem] + [anywhere] * 5,
        out_specs=[in_vmem] * 2,
        scratch_shapes=[
            factor_scratch,
            factor_scratch,
            weight_scratch,
            field_scratch,
            beside_scratch,
            below_scratch,
            pltpu.SemaphoreType.DMA((6,)),
            factor_sems,
        ],
        compiler_params=params,
        cost_estimate=pl.CostEstimate(
            flops=2 * solve_flops, bytes_accessed=16 * order * order * 2, transcendentals=0
        ),
    )(info, gathered, *pieces)

    up = [(2 * x, 2 * x + 1) for x in range(groups)]
    incoming = lax.ppermute(w_high, "sec", up)
    solved, sent = pl.pallas_call(
        last_kernel,
        out_shape=[jax.ShapeDtypeStruct((2, 2, order, order), bf16), full_shape],
        in_specs=[in_smem] + [anywhere] * 6,
        out_specs=[anywhere, in_vmem],
        scratch_shapes=[
            factor_scratch,
            factor_scratch,
            weight_scratch,
            field_scratch,
            pltpu.VMEM((2, order, order), bf16),
            field_scratch,
            beside_scratch,
            below_scratch,
            pltpu.SemaphoreType.DMA((7,)),
            factor_sems,
            pltpu.SemaphoreType.DMA((2,)),
        ],
        compiler_params=params,
        cost_estimate=pl.CostEstimate(
            flops=3 * solve_flops, bytes_accessed=16 * order * order * 2, transcendentals=0
        ),
    )(info, gathered, *pieces, incoming)

    down = [(target, source) for source, target in up]
    incoming = lax.ppermute(sent, "sec", down)
    results = pl.pallas_call(
        back_kernel,
        out_shape=[piece_shape] * len(rounds),
        in_specs=[in_smem] + [anywhere] * 5,
        out_specs=[anywhere] * len(rounds),
        scratch_shapes=[
            factor_scratch,
            factor_scratch,
            weight_scratch,
            field_scratch,
            beside_scratch,
            below_scratch,
            pltpu.SemaphoreType.DMA((6,)),
            factor_sems,
            pltpu.SemaphoreType.DMA((len(rounds),)),
        ],
        compiler_params=params,
        cost_estimate=pl.CostEstimate(
            flops=2 * solve_flops, bytes_accessed=16 * order * order * 2, transcendentals=0
        ),
    )(info, gathered, w_low, w_high, incoming, solved)
    results = [
        lax.ppermute(piece, ("sec", "px"), back_pairs(a, b)) for piece, (a, b) in zip(results, rounds)
    ]
    output = pl.pallas_call(
        unpack_kernel,
        out_shape=jax.ShapeDtypeStruct(field.shape, bf16),
        in_specs=[in_smem] + [anywhere] * len(rounds),
        out_specs=anywhere,
        scratch_shapes=[pltpu.SemaphoreType.DMA((len(rounds),))],
        compiler_params=params,
    )(sends_to, *results)
    return output[:, None]


def chip_plan_fits(mesh):
    return mesh.shape["sec"] == 4 and mesh.shape["px"] == 2


def solution(mesh):
    placed = (
        P(None, "sec", "px", "py"),
        P(),
        P("sec", "px", None),
        P("sec", None, ("px", "py"), None),
        P("sec", None, ("px", "py"), None),
    )
    return jax.shard_map(
        on_device if chip_plan_fits(mesh) else on_device_by_layer,
        mesh=mesh,
        in_specs=placed,
        out_specs=P(None, "sec", "px", "py"),
        check_vma=False,
    )
```

profile of v0, /device:TPU:1, one launch (start us, length us, event | category | flops | bytes accessed | tf_op | source)
XLA Modules:
  0.0 193.2 jit_solution(16606594339210435689)
XLA Ops:
  6.5 0.9 copy-done
  7.5 1.0 pad_maximum_fusion.1
  8.6 4.5 %collective-permute-start = (bf16[5,64,512]{2,1,0:T(8,128)(2,1)S(1)}, bf16[5,64,512]{2,1,0:T(8,128)(2,1)S(1)}, u32[]{:S(2)}, u32[]{:S(2)}) collective-permute-start(bf16[5,64,512]{2,1,0:T(8,128)(2,1)S(1)} %pad_maximum_fusion.1), channel_id=1, source_target_pairs={{0,0},{4,4},{8,16},{12,20},{16,8},{20,12},{24,24},{28,28},{1,1},{5... | collective-permute-start | bytes 983048 | tf_op jit(solution)/shard_map/ppermute | solution.py:454
  13.0 2.6 %collective-permute-done.1 = bf16[5,64,512]{2,1,0:T(8,128)(2,1)S(1)} collective-permute-done((bf16[5,64,512]{2,1,0:T(8,128)(2,1)S(1)}, bf16[5,64,512]{2,1,0:T(8,128)(2,1)S(1)}, u32[]{:S(2)}, u32[]{:S(2)}) %collective-permute-start.1) | collective-permute-done | bytes 327712 | tf_op jit(solution)/shard_map/ppermute | solution.py:454
  15.7 3.5 %collective-permute-done = bf16[5,64,512]{2,1,0:T(8,128)(2,1)S(1)} collective-permute-done((bf16[5,64,512]{2,1,0:T(8,128)(2,1)S(1)}, bf16[5,64,512]{2,1,0:T(8,128)(2,1)S(1)}, u32[]{:S(2)}, u32[]{:S(2)}) %collective-permute-start) | collective-permute-done | bytes 327712 | tf_op jit(solution)/shard_map/ppermute | solution.py:454
  19.2 0.9 pad_maximum_fusion
  20.3 1.9 shard_map.55
  22.2 4.4 %collective-permute-start.2 = (bf16[2,256,512]{2,1,0:T(8,128)(2,1)}, bf16[2,256,512]{2,1,0:T(8,128)(2,1)S(1)}, u32[]{:S(2)}, u32[]{:S(2)}) collective-permute-start(bf16[2,256,512]{2,1,0:T(8,128)(2,1)} %get-tuple-element.17), channel_id=1, source_target_pairs={{0,0},{4,4},{8,16},{12,20},{16,8},{20,12},{24,24},{28,28},{1,1},{5... | collective-permute-start | bytes 1572872 | tf_op jit(solution)/shard_map/ppermute | solution.py:470
  26.6 1.0 collective-permute-start.3
  27.6 2.2 %collective-permute-start.5 = (bf16[2,256,512]{2,1,0:T(8,128)(2,1)}, bf16[2,256,512]{2,1,0:T(8,128)(2,1)S(1)}, u32[]{:S(2)}, u32[]{:S(2)}) collective-permute-start(bf16[2,256,512]{2,1,0:T(8,128)(2,1)} %get-tuple-element.20), channel_id=1, source_target_pairs={{0,20},{4,16},{8,4},{12,0},{16,28},{20,24},{24,12},{28,8},{1,21},{... | collective-permute-start | bytes 1572872 | tf_op jit(solution)/shard_map/ppermute | solution.py:470
  29.9 0.7 dynamic_slice.6
  33.4 4.0 %collective-permute-done.2.p0 = bf16[2,256,512]{2,1,0:T(8,128)(2,1)S(1)} collective-permute-done((bf16[2,256,512]{2,1,0:T(8,128)(2,1)}, bf16[2,256,512]{2,1,0:T(8,128)(2,1)S(1)}, u32[]{:S(2)}, u32[]{:S(2)}) %collective-permute-start.2) | collective-permute-done | bytes 524320 | tf_op jit(solution)/shard_map/ppermute | solution.py:470
  37.4 12.9 %collective-permute-done.3.p1 = bf16[2,256,512]{2,1,0:T(8,128)(2,1)S(1)} collective-permute-done((bf16[2,256,512]{2,1,0:T(8,128)(2,1)}, bf16[2,256,512]{2,1,0:T(8,128)(2,1)S(1)}, u32[]{:S(2)}, u32[]{:S(2)}) %collective-permute-start.3) | collective-permute-done | bytes 524320 | tf_op jit(solution)/shard_map/ppermute | solution.py:470
  50.3 4.7 %collective-permute-done.5.p3 = bf16[2,256,512]{2,1,0:T(8,128)(2,1)S(1)} collective-permute-done((bf16[2,256,512]{2,1,0:T(8,128)(2,1)}, bf16[2,256,512]{2,1,0:T(8,128)(2,1)S(1)}, u32[]{:S(2)}, u32[]{:S(2)}) %collective-permute-start.5) | collective-permute-done | bytes 524320 | tf_op jit(solution)/shard_map/ppermute | solution.py:470
  54.9 0.8 copy-done.3
  55.7 63.1 %all-gather.3.cloned.1.call-done = bf16[16,5,64,512]{3,2,1,0:T(8,128)(2,1)} async-done(((bf16[2,5,64,512]{3,2,1,0:T(8,128)(2,1)}), bf16[16,5,64,512]{3,2,1,0:T(8,128)(2,1)}) %all-gather.3.cloned.1.call-update) | async-done | bytes 5242896 | tf_op jit(solution)/shard_map/all_gather | solution.py:455
  118.8 2.5 %copy-done.2 = bf16[16,5,64,512]{3,2,1,0:T(8,128)(2,1)S(1)} copy-done((bf16[16,5,64,512]{3,2,1,0:T(8,128)(2,1)S(1)}, bf16[16,5,64,512]{3,2,1,0:T(8,128)(2,1)}, u32[]{:S(2)}) %copy-start.2) | copy-done | bytes 5242904
  121.3 1.0 copy-done.4
  122.3 0.7 shard_map.56
  123.1 1.3 collective-permute-start.6
  124.4 10.9 %collective-permute-done.6.incoming = bf16[2,512,512]{2,1,0:T(8,128)(2,1)S(1)} collective-permute-done((bf16[2,512,512]{2,1,0:T(8,128)(2,1)S(1)}, bf16[2,512,512]{2,1,0:T(8,128)(2,1)S(1)}, u32[]{:S(2)}, u32[]{:S(2)}) %collective-permute-start.6) | collective-permute-done | bytes 1048608 | tf_op jit(solution)/shard_map/ppermute | solution.py:519
  135.3 11.2 %shard_map.57 = (bf16[2,2,512,512]{3,2,1,0:T(8,128)(2,1)S(1)}, bf16[2,512,512]{2,1,0:T(8,128)(2,1)S(1)}) custom-call(s32[14]{0:T(128)S(1)} %stack.73.info, bf16[8,2,5,64,512]{4,3,2,1,0:T(8,128)(2,1)S(1)} %bitcast.25, bf16[2,256,512]{2,1,0:T(8,128)(2,1)S(1)} %collective-permute-done.2.p0, bf16[2,256,512]{2,1,0:T(8,128)(2,1)S(1)} %collective-permute-done.3.p1, ...), custom_call_target="tpu_custom_call" | custom-call | flops 6442450944 | bytes 8388608 | tf_op jit(solution)/shard_map/pallas_call | solution.py:520
  146.6 1.4 collective-permute-start.7
  147.9 2.2 %collective-permute-done.7.incoming = bf16[2,512,512]{2,1,0:T(8,128)(2,1)S(1)} collective-permute-done((bf16[2,512,512]{2,1,0:T(8,128)(2,1)S(1)}, bf16[2,512,512]{2,1,0:T(8,128)(2,1)S(1)}, u32[]{:S(2)}, u32[]{:S(2)}) %collective-permute-start.7) | collective-permute-done | bytes 1048608 | tf_op jit(solution)/shard_map/ppermute | solution.py:545
  150.1 0.9 shard_map.58
  151.1 10.3 %collective-permute-start.8 = (bf16[2,256,512]{2,1,0:T(8,128)(2,1)S(1)}, bf16[2,256,512]{2,1,0:T(8,128)(2,1)S(1)}, u32[]{:S(2)}, u32[]{:S(2)}) collective-permute-start(bf16[2,256,512]{2,1,0:T(8,128)(2,1)S(1)} %get-tuple-element.25), channel_id=1, source_target_pairs={{0,0},{4,4},{16,8},{20,12},{8,16},{12,20},{24,24},{28,28},{1,1},{5... | collective-permute-start | bytes 1572872 | tf_op jit(solution)/shard_map/ppermute | solution.py:568
  161.5 2.7 %collective-permute-start.11 = (bf16[2,256,512]{2,1,0:T(8,128)(2,1)S(1)}, bf16[2,256,512]{2,1,0:T(8,128)(2,1)S(1)}, u32[]{:S(2)}, u32[]{:S(2)}) collective-permute-start(bf16[2,256,512]{2,1,0:T(8,128)(2,1)S(1)} %get-tuple-element.28), channel_id=1, source_target_pairs={{20,0},{16,4},{4,8},{0,12},{28,16},{24,20},{12,24},{8,28},{21,1},{... | collective-permute-start | bytes 1572872 | tf_op jit(solution)/shard_map/ppermute | solution.py:568
  164.2 4.0 %collective-permute-done.8.rest_0_ = bf16[2,256,512]{2,1,0:T(8,128)(2,1)S(1)} collective-permute-done((bf16[2,256,512]{2,1,0:T(8,128)(2,1)S(1)}, bf16[2,256,512]{2,1,0:T(8,128)(2,1)S(1)}, u32[]{:S(2)}, u32[]{:S(2)}) %collective-permute-start.8) | collective-permute-done | bytes 524320 | tf_op jit(solution)/shard_map/ppermute | solution.py:568
  168.2 5.7 %collective-permute-done.9.rest_1_ = bf16[2,256,512]{2,1,0:T(8,128)(2,1)S(1)} collective-permute-done((bf16[2,256,512]{2,1,0:T(8,128)(2,1)S(1)}, bf16[2,256,512]{2,1,0:T(8,128)(2,1)S(1)}, u32[]{:S(2)}, u32[]{:S(2)}) %collective-permute-start.9) | collective-permute-done | bytes 524320 | tf_op jit(solution)/shard_map/ppermute | solution.py:568
  174.0 4.8 %collective-permute-done.10.rest_2_ = bf16[2,256,512]{2,1,0:T(8,128)(2,1)S(1)} collective-permute-done((bf16[2,256,512]{2,1,0:T(8,128)(2,1)S(1)}, bf16[2,256,512]{2,1,0:T(8,128)(2,1)S(1)}, u32[]{:S(2)}, u32[]{:S(2)}) %collective-permute-start.10) | collective-permute-done | bytes 524320 | tf_op jit(solution)/shard_map/ppermute | solution.py:568
  178.8 5.6 %collective-permute-done.11.rest_3_ = bf16[2,256,512]{2,1,0:T(8,128)(2,1)S(1)} collective-permute-done((bf16[2,256,512]{2,1,0:T(8,128)(2,1)S(1)}, bf16[2,256,512]{2,1,0:T(8,128)(2,1)S(1)}, u32[]{:S(2)}, u32[]{:S(2)}) %collective-permute-start.11) | collective-permute-done | bytes 524320 | tf_op jit(solution)/shard_map/ppermute | solution.py:568
  184.4 1.9 shard_map.59
  (18 shorter events, 0.4 us)
Async XLA Ops:
  6.5 1.0 copy-start
  6.5 13.7 %copy-start.1 = (bf16[2,1,256,2048]{3,2,1,0:T(8,128)(2,1)S(1)}, bf16[2,1,256,2048]{3,2,1,0:T(8,128)(2,1)}, u32[]{:S(2)}) copy-start(bf16[2,1,256,2048]{3,2,1,0:T(8,128)(2,1)} %param.5) | copy-start | bytes 6291460
  6.5 112.3 %all-gather.3.cloned.1.call-start = ((), (), s32[]{:S(2)}) async-start(), calls=%async_computation | async-start | bytes 5898240 | tf_op jit(solution)/shard_map/all_gather | solution.py:455
  8.5 7.2 %collective-permute-start.1 = (bf16[5,64,512]{2,1,0:T(8,128)(2,1)S(1)}, bf16[5,64,512]{2,1,0:T(8,128)(2,1)S(1)}, u32[]{:S(2)}, u32[]{:S(2)}) collective-permute-start(bf16[5,64,512]{2,1,0:T(8,128)(2,1)S(1)} %pad_maximum_fusion.1), channel_id=1, source_target_pairs={{0,16},{4,20},{8,0},{12,4},{16,24},{20,28},{24,8},{28,12},{1,17},{... | collective-permute-start | bytes 983048 | tf_op jit(solution)/shard_map/ppermute | solution.py:454
  8.6 10.6 %collective-permute-start = (bf16[5,64,512]{2,1,0:T(8,128)(2,1)S(1)}, bf16[5,64,512]{2,1,0:T(8,128)(2,1)S(1)}, u32[]{:S(2)}, u32[]{:S(2)}) collective-permute-start(bf16[5,64,512]{2,1,0:T(8,128)(2,1)S(1)} %pad_maximum_fusion.1), channel_id=1, source_target_pairs={{0,0},{4,4},{8,16},{12,20},{16,8},{20,12},{24,24},{28,28},{1,1},{5... | collective-permute-start | bytes 983048 | tf_op jit(solution)/shard_map/ppermute | solution.py:454
  19.2 10.7 %copy-start.5 = (s32[16]{0:T(128)S(1)}, s32[16]{0:T(128)}, u32[]{:S(2)}) copy-start(s32[16]{0:T(128)} %param.6) | copy-start | bytes 196
  22.2 15.2 %collective-permute-start.2 = (bf16[2,256,512]{2,1,0:T(8,128)(2,1)}, bf16[2,256,512]{2,1,0:T(8,128)(2,1)S(1)}, u32[]{:S(2)}, u32[]{:S(2)}) collective-permute-start(bf16[2,256,512]{2,1,0:T(8,128)(2,1)} %get-tuple-element.17), channel_id=1, source_target_pairs={{0,0},{4,4},{8,16},{12,20},{16,8},{20,12},{24,24},{28,28},{1,1},{5... | collective-permute-start | bytes 1572872 | tf_op jit(solution)/shard_map/ppermute | solution.py:470
  26.6 23.7 %collective-permute-start.3 = (bf16[2,256,512]{2,1,0:T(8,128)(2,1)}, bf16[2,256,512]{2,1,0:T(8,128)(2,1)S(1)}, u32[]{:S(2)}, u32[]{:S(2)}) collective-permute-start(bf16[2,256,512]{2,1,0:T(8,128)(2,1)} %get-tuple-element.18), channel_id=1, source_target_pairs={{0,4},{4,0},{8,20},{12,16},{16,12},{20,8},{24,28},{28,24},{1,5},{5... | collective-permute-start | bytes 1572872 | tf_op jit(solution)/shard_map/ppermute | solution.py:470
  27.6 22.6 %collective-permute-start.4 = (bf16[2,256,512]{2,1,0:T(8,128)(2,1)}, bf16[2,256,512]{2,1,0:T(8,128)(2,1)S(1)}, u32[]{:S(2)}, u32[]{:S(2)}) collective-permute-start(bf16[2,256,512]{2,1,0:T(8,128)(2,1)} %get-tuple-element.19), channel_id=1, source_target_pairs={{0,16},{4,20},{8,0},{12,4},{16,24},{20,28},{24,8},{28,12},{1,17},{... | collective-permute-start | bytes 1572872 | tf_op jit(solution)/shard_map/ppermute | solution.py:470
  27.6 27.3 %collective-permute-start.5 = (bf16[2,256,512]{2,1,0:T(8,128)(2,1)}, bf16[2,256,512]{2,1,0:T(8,128)(2,1)S(1)}, u32[]{:S(2)}, u32[]{:S(2)}) collective-permute-start(bf16[2,256,512]{2,1,0:T(8,128)(2,1)} %get-tuple-element.20), channel_id=1, source_target_pairs={{0,20},{4,16},{8,4},{12,0},{16,28},{20,24},{24,12},{28,8},{1,21},{... | collective-permute-start | bytes 1572872 | tf_op jit(solution)/shard_map/ppermute | solution.py:470
  54.9 0.8 copy-start.3
  118.8 2.5 %copy-start.2 = (bf16[16,5,64,512]{3,2,1,0:T(8,128)(2,1)S(1)}, bf16[16,5,64,512]{3,2,1,0:T(8,128)(2,1)}, u32[]{:S(2)}) copy-start(bf16[16,5,64,512]{3,2,1,0:T(8,128)(2,1)} %all-gather.3.cloned.1.call-done) | copy-start | bytes 15728644
  121.3 1.0 copy-start.4
  123.1 12.2 %collective-permute-start.6 = (bf16[2,512,512]{2,1,0:T(8,128)(2,1)S(1)}, bf16[2,512,512]{2,1,0:T(8,128)(2,1)S(1)}, u32[]{:S(2)}, u32[]{:S(2)}) collective-permute-start(bf16[2,512,512]{2,1,0:T(8,128)(2,1)S(1)} %get-tuple-element.22.w_high), channel_id=1, source_target_pairs={{0,8},{16,24},{1,9},{17,25},{2,10},{18,26},{3,11},{19,27},{4,12},{... | collective-permute-start | bytes 3145736 | tf_op jit(solution)/shard_map/ppermute | solution.py:519
  146.6 3.6 %collective-permute-start.7 = (bf16[2,512,512]{2,1,0:T(8,128)(2,1)S(1)}, bf16[2,512,512]{2,1,0:T(8,128)(2,1)S(1)}, u32[]{:S(2)}, u32[]{:S(2)}) collective-permute-start(bf16[2,512,512]{2,1,0:T(8,128)(2,1)S(1)} %get-tuple-element.23), channel_id=1, source_target_pairs={{8,0},{24,16},{9,1},{25,17},{10,2},{26,18},{11,3},{27,19},{12,4},{... | collective-permute-start | bytes 3145736 | tf_op jit(solution)/shard_map/ppermute | solution.py:545
  151.1 17.2 %collective-permute-start.8 = (bf16[2,256,512]{2,1,0:T(8,128)(2,1)S(1)}, bf16[2,256,512]{2,1,0:T(8,128)(2,1)S(1)}, u32[]{:S(2)}, u32[]{:S(2)}) collective-permute-start(bf16[2,256,512]{2,1,0:T(8,128)(2,1)S(1)} %get-tuple-element.25), channel_id=1, source_target_pairs={{0,0},{4,4},{16,8},{20,12},{8,16},{12,20},{24,24},{28,28},{1,1},{5... | collective-permute-start | bytes 1572872 | tf_op jit(solution)/shard_map/ppermute | solution.py:568
  161.4 12.6 %collective-permute-start.9 = (bf16[2,256,512]{2,1,0:T(8,128)(2,1)S(1)}, bf16[2,256,512]{2,1,0:T(8,128)(2,1)S(1)}, u32[]{:S(2)}, u32[]{:S(2)}) collective-permute-start(bf16[2,256,512]{2,1,0:T(8,128)(2,1)S(1)} %get-tuple-element.26), channel_id=1, source_target_pairs={{4,0},{0,4},{20,8},{16,12},{12,16},{8,20},{28,24},{24,28},{5,1},{1... | collective-permute-start | bytes 1572872 | tf_op jit(solution)/shard_map/ppermute | solution.py:568
  161.5 17.3 %collective-permute-start.10 = (bf16[2,256,512]{2,1,0:T(8,128)(2,1)S(1)}, bf16[2,256,512]{2,1,0:T(8,128)(2,1)S(1)}, u32[]{:S(2)}, u32[]{:S(2)}) collective-permute-start(bf16[2,256,512]{2,1,0:T(8,128)(2,1)S(1)} %get-tuple-element.27), channel_id=1, source_target_pairs={{16,0},{20,4},{0,8},{4,12},{24,16},{28,20},{8,24},{12,28},{17,1},{... | collective-permute-start | bytes 1572872 | tf_op jit(solution)/shard_map/ppermute | solution.py:568
  161.5 22.9 %collective-permute-start.11 = (bf16[2,256,512]{2,1,0:T(8,128)(2,1)S(1)}, bf16[2,256,512]{2,1,0:T(8,128)(2,1)S(1)}, u32[]{:S(2)}, u32[]{:S(2)}) collective-permute-start(bf16[2,256,512]{2,1,0:T(8,128)(2,1)S(1)} %get-tuple-element.28), channel_id=1, source_target_pairs={{20,0},{16,4},{4,8},{0,12},{28,16},{24,20},{12,24},{8,28},{21,1},{... | collective-permute-start | bytes 1572872 | tf_op jit(solution)/shard_map/ppermute | solution.py:568
Sparse Core Ops, SparseCore 0:
  20.3 98.4 all-gather.2
where the time goes:
time: 195 us; the launch traced here: 193 us
  waiting for transfers between devices  124 us (64%)
  starting transfers between devices  28 us (14%)
  Pallas kernels  16.7 us (9%)
  between operations  16.4 us (8%)
  local copies, waits for them, and re-layouts  6.03 us (3%)
  other arithmetic  1.98 us (1%)
    all_gather x1, waiting for transfers between devices, on_device(): lax.all_gather(jnp.stack(shards), ('px', 'py'), axis=0, tiled=False)  63.1 us
    ppermute x4, waiting for transfers between devices, on_device(): lax.ppermute(piece, ('sec', 'px'), pairs(a, b))  21.5 us
    ppermute x4, waiting for transfers between devices, on_device(): lax.ppermute(piece, ('sec', 'px'), back_pairs(a, b))  20.2 us
    ppermute x4, starting transfers between devices, on_device(): lax.ppermute(piece, ('sec', 'px'), back_pairs(a, b))  13.1 us
    pallas_call x1, Pallas kernels, on_device(): pl.pallas_call(last_kernel, out_shape=[jax.ShapeDtypeStruct((2, 2, order,...  11.2 us
    ppermute x1, waiting for transfers between devices, on_device(): incoming = lax.ppermute(w_high, 'sec', up)  10.9 us
    ppermute x4, starting transfers between devices, on_device(): lax.ppermute(piece, ('sec', 'px'), pairs(a, b))  7.66 us
    ppermute x2, waiting for transfers between devices, on_device(): shards = [lax.ppermute(shard, ('sec', 'px'), pairs(a, 0)) for a in range(2)]  6.18 us
  transfers between devices with their start and end apart: 13, of which 12 were waited for; matrix products, arithmetic and copies ran while one was open for 0% of the time, Pallas kernels for 1%

commit v1 on v0

--- a/solution.py
+++ b/solution.py
@@ -8,12 +8,14 @@
 from jax.sharding import PartitionSpec as P
 
 source_amplitude = 8.0
-vmem_bytes = 40 * 1024 * 1024
+vmem_bytes = 60 * 1024 * 1024
 bf16 = jnp.bfloat16
 f32 = jnp.float32
 anywhere = pl.BlockSpec(memory_space=pl.ANY)
 in_smem = pl.BlockSpec(memory_space=pltpu.SMEM)
 in_vmem = pl.BlockSpec(memory_space=pltpu.VMEM)
+
+info_member, info_piece, info_slot, info_half, info_block = 3, 4, 12, 14, 16
 
 
 def shifted(x, axis, by):
@@ -185,68 +187,92 @@
     wait_all(copies)
 
 
+def stack_kernel(info, own, first, second, third, x_column, y_column, sems):
+    height = own.shape[1]
+    copies = []
+    for turn, block in enumerate((own, first, second, third)):
+        rows = pl.ds(pl.multiple_of(info[info_block + turn] * height, height), height)
+        for which, column in enumerate((x_column, y_column)):
+            copies.append(
+                pltpu.make_async_copy(
+                    block.at[pl.ds(2 * which, 2)], column.at[:, rows, :], sems.at[turn, which]
+                )
+            )
+    start_all(copies)
+    wait_all(copies)
+
+
+def weight_kernel(info, own, first, second, third, weights, sems):
+    height = own.shape[1]
+    half_height = weights.shape[1] // 2
+    copies = []
+    for turn, block in enumerate((own, first, second, third)):
+        for index in range(block.shape[0]):
+            slot, half = info[info_piece + 2 * index], info[info_piece + 2 * index + 1]
+            start = half * half_height + info[info_block + turn] * height
+            rows = pl.ds(pl.multiple_of(start, height), height)
+            copies.append(
+                pltpu.make_async_copy(
+                    block.at[index], weights.at[slot, rows, :], sems.at[turn, index]
+                )
+            )
+    start_all(copies)
+    wait_all(copies)
+
+
 class Factors:
-    def __init__(self, gathered, slot_from, slot, plain, crossed, sems):
-        order = gathered.shape[-1]
+    def __init__(self, info, columns, plain, crossed, sems):
+        order = plain.shape[2]
+        self.order, self.plain, self.crossed, self.sems = order, plain, crossed, sems
+        self.columns = columns
         left, right = pl.ds(0, order), pl.ds(order, order)
-        self.order, self.slot = order, slot
-        self.plain, self.crossed = plain, crossed
-        self.copies = []
-        for which in range(2):
-            real = gathered.at[:, slot_from, 2 * which]
-            imag = gathered.at[:, slot_from, 2 * which + 1]
-            ends = (
-                (real, plain, left),
-                (imag, plain, right),
-                (imag, crossed, left),
-                (real, crossed, right),
-            )
-            self.copies.append(
-                [
+        self.ends = ((0, plain, left), (1, plain, right), (1, crossed, left), (0, crossed, right))
+        height = columns[0][0].shape[1]
+        for which in (1, 0):
+            for index, column in enumerate(columns[which]):
+                slot, half = info[info_slot + index // 2], info[info_half + index % 2]
+                rows = pl.ds(pl.multiple_of(half * height, height), height)
+                for end, (plane, target, side) in enumerate(self.ends):
                     pltpu.make_async_copy(
-                        source, target.at[slot, which, :, :, half], sems.at[slot, which, index]
-                    )
-                    for index, (source, target, half) in enumerate(ends)
-                ]
-            )
-
-    def start(self):
-        start_all(self.copies[1])
-        start_all(self.copies[0])
-
-    def ready(self, which):
-        wait_all(self.copies[which])
+                        column.at[plane],
+                        target.at[slot, which, rows, side],
+                        sems.at[slot, which, index % 2, end],
+                    ).start()
+
+    def ready(self, slot, which):
+        column = self.columns[which][0]
+        height = column.shape[1]
+        for half in range(2):
+            rows = pl.ds(half * height, height)
+            for end, (plane, target, side) in enumerate(self.ends):
+                pltpu.make_async_copy(
+                    column.at[plane],
+                    target.at[slot, which, rows, side],
+                    self.sems.at[slot, which, half, end],
+                ).wait()
         right = slice(self.order, 2 * self.order)
-        self.plain[self.slot, which, :, :, right] = -self.plain[self.slot, which, :, :, right]
-
-    def apply(self, beside, below, store, fresh):
+        self.plain[slot, which, :, right] = -self.plain[slot, which, :, right]
+
+    def apply(self, slot, beside, below, store, fresh):
         order = self.order
         turned = (((1,), (1,)), ((), ()))
         if fresh:
-            self.ready(1)
+            self.ready(slot, 1)
         for plane, ref in enumerate((self.plain, self.crossed)):
-            blocks, height = ref.shape[2:4]
             for columns in row_chunks(order, 256):
-                rows = ref[self.slot, 1, columns.start // height : columns.stop // height]
-                rows = rows.reshape(columns.stop - columns.start, 2 * order)
-                part = lax.dot_general(beside[...], rows, turned, preferred_element_type=f32)
+                part = lax.dot_general(
+                    beside[...], ref[slot, 1, columns], turned, preferred_element_type=f32
+                )
                 below[plane * order : (plane + 1) * order, columns] = part.astype(bf16)
         if fresh:
-            self.ready(0)
+            self.ready(slot, 0)
         for plane, ref in enumerate((self.plain, self.crossed)):
-            matrix = ref[self.slot, 0].reshape(order, 2 * order)
             for columns in row_chunks(order, 256):
                 store(
                     plane,
                     columns,
-                    jnp.dot(matrix, below[:, columns], preferred_element_type=f32),
+                    jnp.dot(ref[slot, 0], below[:, columns], preferred_element_type=f32),
                 )
-
-
-def rows_of(blocked, slot, rows):
-    height = blocked.shape[2]
-    part = blocked[slot, rows.start // height : rows.stop // height]
-    return part.reshape(rows.stop - rows.start, part.shape[-1])
 
 
 def reduce_into(beside, rhs, info, slot, weights, incoming):
@@ -259,7 +285,7 @@
                 column = lax.broadcasted_iota(jnp.int32, values.shape, 1)
                 hit = (row == info[1]) & (column == info[2]) & (info[0] == slot)
                 values = values + jnp.where(hit, f32(source_amplitude), f32(0.0))
-            scaled = rows_of(weights, slot, rows).astype(f32) * incoming(plane, rows)
+            scaled = weights[slot, rows].astype(f32) * incoming(plane, rows)
             beside[rows, plane * order : (plane + 1) * order] = (values - scaled).astype(bf16)
 
 
@@ -267,7 +293,7 @@
     order = beside.shape[0]
     for plane in range(2):
         for rows in row_chunks(order, 128):
-            scaled = rows_of(weights, slot, rows).astype(f32) * field(plane, rows)
+            scaled = weights[slot, rows].astype(f32) * field(plane, rows)
             beside[rows, plane * order : (plane + 1) * order] = scaled.astype(bf16)
 
 
@@ -290,69 +316,54 @@
     copies = []
     for index, piece in enumerate(pieces):
         height = piece.shape[1]
-        rows = pl.ds(pl.multiple_of(info[5 + 2 * index] * height, height), height)
-        copies.append(
-            pltpu.make_async_copy(piece, rhs.at[info[4 + 2 * index], :, rows, :], sems.at[index])
-        )
+        slot, half = info[info_piece + 2 * index], info[info_piece + 2 * index + 1]
+        rows = pl.ds(pl.multiple_of(half * height, height), height)
+        copies.append(pltpu.make_async_copy(piece, rhs.at[slot, :, rows, :], sems.at[index]))
     return copies
 
 
-def weight_copies(info, gathered, weights, sems):
-    return [
-        pltpu.make_async_copy(gathered.at[:, info[12 + slot], 4], weights.at[slot], sems.at[slot])
-        for slot in range(2)
-    ]
-
-
-def layer_factors(info, gathered, plain, crossed, sems):
-    return [Factors(gathered, info[12 + slot], slot, plain, crossed, sems) for slot in range(2)]
-
-
-def first_kernel(info, gathered, p0, p1, p2, p3, w_low, w_high, plain, crossed, weights, rhs,
-                 beside, below, sems, fsems):
-    @pl.when(info[3] == 0)
+def first_kernel(info, x0, x1, x2, x3, y0, y1, y2, y3, coupling, p0, p1, p2, p3, w_low, w_high,
+                 plain, crossed, weights, rhs, beside, below, sems, fsems):
+    @pl.when(info[info_member] == 0)
     def _():
-        low, high = layer_factors(info, gathered, plain, crossed, fsems)
         early = rhs_copies(info, (p0, p1, p2, p3), rhs, sems)
-        early += weight_copies(info, gathered, weights, sems.at[pl.ds(4, 2)])
+        early.append(pltpu.make_async_copy(coupling, weights, sems.at[4]))
         start_all(early)
-        low.start()
-        high.start()
+        factors = Factors(info, ((x0, x1, x2, x3), (y0, y1, y2, y3)), plain, crossed, fsems)
         wait_all(early)
         reduce_into(beside, rhs, info, 0, weights, lambda plane, rows: f32(0.0))
-        low.apply(beside, below, round_into(w_low), True)
+        factors.apply(0, beside, below, round_into(w_low), True)
         reduce_into(
             beside, rhs, info, 1, weights, lambda plane, rows: w_low[plane, rows].astype(f32)
         )
-        high.apply(beside, below, round_into(w_high), True)
-
-
-def last_kernel(info, gathered, p0, p1, p2, p3, incoming, field, sent, plain, crossed, weights, rhs,
-                arrived, kept, beside, below, sems, fsems, osems):
-    @pl.when(info[3] == 1)
+        factors.apply(1, beside, below, round_into(w_high), True)
+
+
+def last_kernel(info, x0, x1, x2, x3, y0, y1, y2, y3, coupling, p0, p1, p2, p3, incoming, field,
+                sent, plain, crossed, weights, rhs, arrived, kept, beside, below, sems, fsems, osems):
+    @pl.when(info[info_member] == 1)
     def _():
-        low, high = layer_factors(info, gathered, plain, crossed, fsems)
         early = rhs_copies(info, (p0, p1, p2, p3), rhs, sems)
-        early += weight_copies(info, gathered, weights, sems.at[pl.ds(4, 2)])
-        early.append(pltpu.make_async_copy(incoming, arrived, sems.at[6]))
+        early.append(pltpu.make_async_copy(coupling, weights, sems.at[4]))
+        early.append(pltpu.make_async_copy(incoming, arrived, sems.at[5]))
         start_all(early)
-        low.start()
-        high.start()
+        factors = Factors(info, ((x0, x1, x2, x3), (y0, y1, y2, y3)), plain, crossed, fsems)
         wait_all(early)
         order = beside.shape[0]
         reduce_into(
             beside, rhs, info, 0, weights, lambda plane, rows: arrived[plane, rows].astype(f32)
         )
         w_low, w_high = kept.at[0], kept.at[1]
-        low.apply(beside, below, round_into(w_low), True)
+        factors.apply(0, beside, below, round_into(w_low), True)
         reduce_into(
             beside, rhs, info, 1, weights, lambda plane, rows: w_low[plane, rows].astype(f32)
         )
-        high.apply(beside, below, round_into(w_high), True)
+        factors.apply(1, beside, below, round_into(w_high), True)
         out_high = pltpu.make_async_copy(w_high, field.at[1], osems.at[1])
         out_high.start()
         sent_into(beside, weights, 1, lambda plane, rows: w_high[plane, rows].astype(f32))
-        low.apply(
+        factors.apply(
+            0,
             beside,
             below,
             subtract_into(w_low, lambda plane, columns: w_low[plane, :, columns]),
@@ -367,25 +378,21 @@
         out_low.wait()
 
 
-def back_kernel(info, gathered, w_low, w_high, incoming, field, p0, p1, p2, p3, plain, crossed,
-                weights, kept, beside, below, sems, fsems, osems):
-    pieces = (p0, p1, p2, p3)
-
+def back_kernel(info, x0, x1, x2, x3, y0, y1, y2, y3, coupling, w_low, w_high, incoming, field,
+                p0, p1, p2, p3, plain, crossed, weights, kept, beside, below, sems, fsems, osems):
     def piece_copies(source):
         copies = []
-        for index, piece in enumerate(pieces):
+        for index, piece in enumerate((p0, p1, p2, p3)):
             height = piece.shape[1]
-            rows = pl.ds(pl.multiple_of(info[5 + 2 * index] * height, height), height)
+            slot, half = info[info_piece + 2 * index], info[info_piece + 2 * index + 1]
+            rows = pl.ds(pl.multiple_of(half * height, height), height)
             copies.append(
-                pltpu.make_async_copy(
-                    source.at[info[4 + 2 * index], :, rows, :], piece, osems.at[index]
-                )
+                pltpu.make_async_copy(source.at[slot, :, rows, :], piece, osems.at[index])
             )
         return copies
 
-    @pl.when(info[3] == 0)
+    @pl.when(info[info_member] == 0)
     def _():
-        low, high = layer_factors(info, gathered, plain, crossed, fsems)
         order = beside.shape[0]
         columns = [pl.ds(plane * order, order) for plane in range(2)]
         early = [
@@ -393,23 +400,26 @@
             for plane in range(2)
         ]
         start_all(early)
-        high.start()
-        later = weight_copies(info, gathered, weights, sems.at[pl.ds(2, 2)])
-        later.append(pltpu.make_async_copy(w_low, kept.at[0], sems.at[4]))
-        later.append(pltpu.make_async_copy(w_high, kept.at[1], sems.at[5]))
+        factors = Factors(info, ((x0, x1, x2, x3), (y0, y1, y2, y3)), plain, crossed, fsems)
+        later = [
+            pltpu.make_async_copy(coupling, weights, sems.at[2]),
+            pltpu.make_async_copy(w_low, kept.at[0], sems.at[3]),
+            pltpu.make_async_copy(w_high, kept.at[1], sems.at[4]),
+        ]
         start_all(later)
-        low.start()
         wait_all(early)
         wait_all(later)
         u_low, u_high = kept.at[0], kept.at[1]
-        high.apply(
+        factors.apply(
+            1,
             beside,
             below,
             subtract_into(u_high, lambda plane, columns: u_high[plane, :, columns]),
             True,
         )
         sent_into(beside, weights, 1, lambda plane, rows: u_high[plane, rows].astype(f32))
-        low.apply(
+        factors.apply(
+            0,
             beside,
             below,
             subtract_into(u_low, lambda plane, columns: u_low[plane, :, columns]),
@@ -419,7 +429,7 @@
         start_all(copies)
         wait_all(copies)
 
-    @pl.when(info[3] != 0)
+    @pl.when(info[info_member] != 0)
     def _():
         copies = piece_copies(field)
         start_all(copies)
@@ -449,11 +459,31 @@
     def back_pairs(a, b):
         return [(target, source) for source, target in pairs(a, b)]
 
-    shard_weights = lax.dynamic_slice_in_dim(coupling[0], own_y * height, height)
-    shard = jnp.concatenate([x_factor[0], y_factor[0], shard_weights[None]], axis=0)
-    shards = [lax.ppermute(shard, ("sec", "px"), pairs(a, 0)) for a in range(2)]
-    gathered = lax.all_gather(jnp.stack(shards), ("px", "py"), axis=0, tiled=False)
-
+    own_source = src_pos[own_y * groups * px_count + group * px_count + own_x]
+    plane_cells = x_factor.shape[3] * order
+    layer = own_source // plane_cells
+    remainder = own_source % plane_cells
+    py_count = lax.axis_size("py")
+    entries = [
+        jnp.where(layer // 2 == member, layer % 2, -1),
+        remainder // order,
+        remainder % order,
+        member,
+    ]
+    for a, b in rounds:
+        entries += [(group + a) % 2, (own_x - b) % px_count]
+    entries += [group, (group + 1) % 2, own_x, (own_x + 1) % 2]
+    entries += [(own_y - turn) % py_count for turn in range(py_count)]
+    info = jnp.stack([jnp.asarray(entry, jnp.int32) for entry in entries])
+
+    def rotated(block):
+        return [block] + [
+            lax.ppermute(block, "py", [(z, (z + turn) % py_count) for z in range(py_count)])
+            for turn in range(1, py_count)
+        ]
+
+    shard = jnp.concatenate([x_factor[0], y_factor[0]], axis=0)
+    shards = rotated(shard)
     sends_to = jnp.stack(
         [((member + a) % 2) * px_count + (own_x + b) % px_count for a, b in rounds]
     ).astype(jnp.int32)
@@ -470,34 +500,54 @@
         lax.ppermute(piece, ("sec", "px"), pairs(a, b)) for piece, (a, b) in zip(pieces, rounds)
     ]
 
-    own_source = src_pos[own_y * groups * px_count + group * px_count + own_x]
-    plane_cells = x_factor.shape[3] * order
-    layer = own_source // plane_cells
-    remainder = own_source % plane_cells
-    entries = [
-        jnp.where(layer // 2 == member, layer % 2, -1),
-        remainder // order,
-        remainder % order,
-        member,
-    ]
-    for a, b in rounds:
-        entries += [(group + a) % 2, (own_x - b) % px_count]
-    entries += [group, (group + 1) % 2]
-    info = jnp.stack([jnp.asarray(entry, jnp.int32) for entry in entries])
+    column_shape = jax.ShapeDtypeStruct((2, rows_here, order), bf16)
+    x_column, y_column = pl.pallas_call(
+        stack_kernel,
+        out_shape=[column_shape] * 2,
+        in_specs=[in_smem] + [anywhere] * 4,
+        out_specs=[anywhere] * 2,
+        scratch_shapes=[pltpu.SemaphoreType.DMA((4, 2))],
+        compiler_params=params,
+    )(info, *shards)
+
+    own_weights = lax.dynamic_slice_in_dim(coupling[0], own_y * height, height)
+    own_weights = jnp.stack([lax.ppermute(own_weights, ("sec", "px"), pairs(a, b)) for a, b in rounds])
+    weights = pl.pallas_call(
+        weight_kernel,
+        out_shape=jax.ShapeDtypeStruct((2, order, order), bf16),
+        in_specs=[in_smem] + [anywhere] * 4,
+        out_specs=anywhere,
+        scratch_shapes=[pltpu.SemaphoreType.DMA((4, 4))],
+        compiler_params=params,
+    )(info, *rotated(own_weights))
+
+    def across(block, a):
+        return lax.ppermute(block, ("sec", "px"), pairs(a, 0))
+
+    def aside(block):
+        return lax.ppermute(block, "px", [(y, (y + 1) % 2) for y in range(2)])
+
+    x_aside = aside(x_column)
+    y_near = [across(y_column, a) for a in range(2)]
+    x_near = [across(x_column, a) for a in range(2)]
+    y_far = [aside(block) for block in y_near]
+    x_far = [across(x_aside, a) for a in range(2)]
+    factors = []
+    for near, far in ((x_near, x_far), (y_near, y_far)):
+        factors += [near[0], far[0], near[1], far[1]]
 
     full_shape = jax.ShapeDtypeStruct((2, order, order), bf16)
-    blocks = gathered.shape[0]
-    factor_scratch = pltpu.VMEM((2, 2, blocks, height, 2 * order), bf16)
-    weight_scratch = pltpu.VMEM((2, blocks, height, order), bf16)
+    factor_scratch = pltpu.VMEM((2, 2, order, 2 * order), bf16)
+    weight_scratch = pltpu.VMEM((2, order, order), bf16)
     field_scratch = pltpu.VMEM((2, 2, order, order), bf16)
     beside_scratch = pltpu.VMEM((order, 2 * order), bf16)
     below_scratch = pltpu.VMEM((2 * order, order), bf16)
-    factor_sems = pltpu.SemaphoreType.DMA((2, 2, 4))
+    factor_sems = pltpu.SemaphoreType.DMA((2, 2, 2, 4))
     solve_flops = 16 * order**3
     w_low, w_high = pl.pallas_call(
         first_kernel,
         out_shape=[full_shape] * 2,
-        in_specs=[in_smem] + [anywhere] * 5,
+        in_specs=[in_smem] + [anywhere] * 13,
         out_specs=[in_vmem] * 2,
         scratch_shapes=[
             factor_scratch,
@@ -513,14 +563,14 @@
         cost_estimate=pl.CostEstimate(
             flops=2 * solve_flops, bytes_accessed=16 * order * order * 2, transcendentals=0
         ),
-    )(info, gathered, *pieces)
+    )(info, *factors, weights, *pieces)
 
     up = [(2 * x, 2 * x + 1) for x in range(groups)]
     incoming = lax.ppermute(w_high, "sec", up)
     solved, sent = pl.pallas_call(
         last_kernel,
         out_shape=[jax.ShapeDtypeStruct((2, 2, order, order), bf16), full_shape],
-        in_specs=[in_smem] + [anywhere] * 6,
+        in_specs=[in_smem] + [anywhere] * 14,
         out_specs=[anywhere, in_vmem],
         scratch_shapes=[
             factor_scratch,
@@ -539,14 +589,14 @@
         cost_estimate=pl.CostEstimate(
             flops=3 * solve_flops, bytes_accessed=16 * order * order * 2, transcendentals=0
         ),
-    )(info, gathered, *pieces, incoming)
+    )(info, *factors, weights, *pieces, incoming)
 
     down = [(target, source) for source, target in up]
     incoming = lax.ppermute(sent, "sec", down)
     results = pl.pallas_call(
         back_kernel,
         out_shape=[piece_shape] * len(rounds),
-        in_specs=[in_smem] + [anywhere] * 5,
+        in_specs=[in_smem] + [anywhere] * 13,
         out_specs=[anywhere] * len(rounds),
         scratch_shapes=[
             factor_scratch,
@@ -563,7 +613,7 @@
         cost_estimate=pl.CostEstimate(
             flops=2 * solve_flops, bytes_accessed=16 * order * order * 2, transcendentals=0
         ),
-    )(info, gathered, w_low, w_high, incoming, solved)
+    )(info, *factors, weights, w_low, w_high, incoming, solved)
     results = [
         lax.ppermute(piece, ("sec", "px"), back_pairs(a, b)) for piece, (a, b) in zip(results, rounds)
     ]
@@ -579,7 +629,7 @@
 
 
 def chip_plan_fits(mesh):
-    return mesh.shape["sec"] == 4 and mesh.shape["px"] == 2
+    return mesh.shape["sec"] == 4 and mesh.shape["px"] == 2 and mesh.shape["py"] == 4
 
 
 def solution(mesh):

time: 195 us -> 398 us (2.04)
  Pallas kernels: 16.7 us -> 282 us
  waiting for transfers between devices: 124 us -> 54 us
  starting transfers between devices: 28 us -> 47.1 us
  between operations: 16.4 us -> 3.19 us
    pallas_call x0 -> x2, Pallas kernels: none -> 67.3 us  [the longest x1 33.7 us: on_device(): pl.pallas_call(weight_kernel, out_shape=jax.ShapeDtypeStruct((2, order, o...]
    pallas_call x1, Pallas kernels: 0.95 us -> 65.7 us  [on_device(): pl.pallas_call(back_kernel, out_shape=[piece_shape] * len(rounds), in_spe...]
    pallas_call x1, Pallas kernels: 1.89 us -> 65.3 us  [on_device(): pl.pallas_call(unpack_kernel, out_shape=jax.ShapeDtypeStruct(field.shape,...]
    pallas_call x1, Pallas kernels: 1.92 us -> 65.3 us  [on_device(): pl.pallas_call(pack_kernel, out_shape=[piece_shape] * len(rounds), in_spe...]
    all_gather x1 -> x0, waiting for transfers between devices: 63.1 us -> none  [on_device(): lax.all_gather(jnp.stack(shards), ('px', 'py'), axis=0, tiled=False)]
    ppermute x2 -> x19, starting transfers between devices: 4.54 us -> 32.1 us  [the longest x6 12.8 us: across(): return lax.ppermute(block, ('sec', 'px'), pairs(a, 0))]
    ppermute x4, waiting for transfers between devices: 21.5 us -> 12.8 us  [on_device(): lax.ppermute(piece, ('sec', 'px'), pairs(a, b))]
    ppermute x4, starting transfers between devices: 13.1 us -> 4.9 us  [on_device(): lax.ppermute(piece, ('sec', 'px'), back_pairs(a, b))]
  transfers between devices with their start and end apart: 13 -> 29, of which waited for: 12 -> 9; matrix products, arithmetic and copies ran while one was open for 0% -> 1% of each run, Pallas kernels for 1% -> 34%
where the time goes in v1:
time: 398 us; the launch traced here: 393 us
  Pallas kernels  282 us (71%)
  waiting for transfers between devices  54 us (14%)
  starting transfers between devices  47.1 us (12%)
  local copies, waits for them, and re-layouts  4.98 us (1%)
    pallas_call x1, Pallas kernels, on_device(): pl.pallas_call(back_kernel, out_shape=[piece_shape] * len(rounds), in_spe...  65.7 us
    pallas_call x1, Pallas kernels, on_device(): pl.pallas_call(unpack_kernel, out_shape=jax.ShapeDtypeStruct(field.shape,...  65.3 us
    pallas_call x1, Pallas kernels, on_device(): pl.pallas_call(pack_kernel, out_shape=[piece_shape] * len(rounds), in_spe...  65.3 us
    pallas_call x1, Pallas kernels, on_device(): pl.pallas_call(weight_kernel, out_shape=jax.ShapeDtypeStruct((2, order, o...  33.7 us
    pallas_call x1, Pallas kernels, on_device(): pl.pallas_call(stack_kernel, out_shape=[column_shape] * 2, in_specs=[in_s...  33.6 us
    ppermute x4, waiting for transfers between devices, on_device(): lax.ppermute(piece, ('sec', 'px'), back_pairs(a, b))  20.3 us
    pallas_call x1, Pallas kernels, on_device(): pl.pallas_call(last_kernel, out_shape=[jax.ShapeDtypeStruct((2, 2, order,...  16.2 us
    ppermute x1, waiting for transfers between devices, on_device(): incoming = lax.ppermute(w_high, 'sec', up)  14 us
  transfers between devices with their start and end apart: 29, of which 9 were waited for; matrix products, arithmetic and copies ran while one was open for 1% of the time, Pallas kernels for 34%

profile of v1, /device:TPU:1, one launch (start us, length us, event | category | flops | bytes accessed | tf_op | source)
XLA Modules:
  0.0 393.0 jit_solution(6060151637800120592)
XLA Ops:
  1.0 2.6 collective-permute-start.15
  4.6 3.4 collective-permute-start.2
  8.0 1.6 collective-permute-start.14
  9.6 3.6 collective-permute-start.12
  15.2 1.9 collective-permute-start.18
  17.1 65.3 %shard_map.57 = (bf16[2,256,512]{2,1,0:T(8,128)(2,1)}, bf16[2,256,512]{2,1,0:T(8,128)(2,1)}, bf16[2,256,512]{2,1,0:T(8,128)(2,1)}, bf16[2,256,512]{2,1,0:T(8,128)(2,1)}) custom-call(s32[4]{0:T(128)} %pad_add_fusion.place, bf16[2,256,2048]{2,1,0:T(8,128)(2,1)} %bitcast.32), custom_call_target="tpu_custom_call" | custom-call | tf_op jit(solution)/shard_map/pallas_call | solution.py:491
  82.5 2.8 collective-permute-start.19
  85.3 1.9 collective-permute-start.20
  88.3 1.5 collective-permute-start.16
  93.6 33.6 %shard_map.55 = (bf16[2,256,512]{2,1,0:T(8,128)(2,1)}, bf16[2,256,512]{2,1,0:T(8,128)(2,1)}) custom-call(s32[20]{0:T(128)} %stack.103.info, bf16[4,64,512]{2,1,0:T(8,128)(2,1)} %copy-done.2, bf16[4,64,512]{2,1,0:T(8,128)(2,1)} %copy-done.12, bf16[4,64,512]{2,1,0:T(8,128)(2,1)} %copy-done.11, bf16[4,64,512]{2,1,0:T(8,128)(2,1)} %copy-done.10), custom_call_target="tpu_custom_call" | custom-call | tf_op jit(solution)/shard_map/pallas_call | solution.py:504
  127.3 2.8 collective-permute-start.22
  130.1 1.9 collective-permute-start.8
  132.0 1.3 collective-permute-start.4
  133.3 12.8 %collective-permute-done.22.p3 = bf16[2,256,512]{2,1,0:T(8,128)(2,1)S(1)} collective-permute-done((bf16[2,256,512]{2,1,0:T(8,128)(2,1)}, bf16[2,256,512]{2,1,0:T(8,128)(2,1)S(1)}, u32[]{:S(2)}, u32[]{:S(2)}) %collective-permute-start.22) | collective-permute-done | bytes 524320 | tf_op jit(solution)/shard_map/ppermute | solution.py:500
  146.1 1.9 collective-permute-start.3
  149.7 3.8 collective-permute-done.4
  153.4 2.3 collective-permute-start.7
  155.8 6.6 %collective-permute-start.5 = (bf16[2,256,512]{2,1,0:T(8,128)(2,1)}, bf16[2,256,512]{2,1,0:T(8,128)(2,1)}, u32[]{:S(2)}, u32[]{:S(2)}) collective-permute-start(bf16[2,256,512]{2,1,0:T(8,128)(2,1)} %collective-permute-done.4), channel_id=1, source_target_pairs={{0,0},{4,4},{8,16},{12,20},{16,8},{20,12},{24,24},{28,28},{1,1},{5... | collective-permute-start | bytes 1572872 | tf_op jit(solution)/shard_map/ppermute | solution.py:525
  162.5 33.7 %shard_map.56.coupling = bf16[2,512,512]{2,1,0:T(8,128)(2,1)} custom-call(s32[20]{0:T(128)} %stack.103.info, bf16[4,64,512]{2,1,0:T(8,128)(2,1)} %copy-done.1, bf16[4,64,512]{2,1,0:T(8,128)(2,1)} %copy-done.9, bf16[4,64,512]{2,1,0:T(8,128)(2,1)} %copy-done.8, bf16[4,64,512]{2,1,0:T(8,128)(2,1)} %copy-done.7), custom_call_target="tpu_custom_call" | custom-call | tf_op jit(solution)/shard_map/pallas_call | solution.py:515
  196.3 2.3 shard_map.58
  199.9 14.0 %collective-permute-done.23.incoming = bf16[2,512,512]{2,1,0:T(8,128)(2,1)S(1)} collective-permute-done((bf16[2,512,512]{2,1,0:T(8,128)(2,1)}, bf16[2,512,512]{2,1,0:T(8,128)(2,1)S(1)}, u32[]{:S(2)}, u32[]{:S(2)}) %collective-permute-start.23) | collective-permute-done | bytes 1048608 | tf_op jit(solution)/shard_map/ppermute | solution.py:569
  214.9 16.2 %shard_map.59 = (bf16[2,2,512,512]{3,2,1,0:T(8,128)(2,1)}, bf16[2,512,512]{2,1,0:T(8,128)(2,1)}) custom-call(s32[20]{0:T(128)} %stack.103.info, bf16[2,256,512]{2,1,0:T(8,128)(2,1)} %collective-permute-done.3.x0, bf16[2,256,512]{2,1,0:T(8,128)(2,1)} %collective-permute-done.5.x1, bf16[2,256,512]{2,1,0:T(8,128)(2,1)} %collective-permute-done.6.x2, ...), custom_call_target="tpu_custom_call" | custom-call | flops 6442450944 | bytes 8388608 | tf_op jit(solution)/shard_map/pallas_call | solution.py:570
  231.1 1.4 collective-permute-start.24
  232.4 2.4 collective-permute-done.24.incoming
  235.8 65.7 %shard_map.60 = (bf16[2,256,512]{2,1,0:T(8,128)(2,1)}, bf16[2,256,512]{2,1,0:T(8,128)(2,1)}, bf16[2,256,512]{2,1,0:T(8,128)(2,1)}, bf16[2,256,512]{2,1,0:T(8,128)(2,1)}) custom-call(s32[20]{0:T(128)} %stack.103.info, bf16[2,256,512]{2,1,0:T(8,128)(2,1)} %collective-permute-done.3.x0, bf16[2,256,512]{2,1,0:T(8,128)(2,1)} %collective-permute-done.5.x1, ...), custom_call_target="tpu_custom_call" | custom-call | flops 4294967296 | bytes 8388608 | tf_op jit(solution)/shard_map/pallas_call | solution.py:596
  301.5 1.9 collective-permute-start.25
  303.4 2.8 collective-permute-start.26
  306.4 5.8 %collective-permute-done.25.rest_0_ = bf16[2,256,512]{2,1,0:T(8,128)(2,1)S(1)} collective-permute-done((bf16[2,256,512]{2,1,0:T(8,128)(2,1)}, bf16[2,256,512]{2,1,0:T(8,128)(2,1)S(1)}, u32[]{:S(2)}, u32[]{:S(2)}) %collective-permute-start.25) | collective-permute-done | bytes 524320 | tf_op jit(solution)/shard_map/ppermute | solution.py:618
  312.2 6.8 %collective-permute-done.26.rest_1_ = bf16[2,256,512]{2,1,0:T(8,128)(2,1)S(1)} collective-permute-done((bf16[2,256,512]{2,1,0:T(8,128)(2,1)}, bf16[2,256,512]{2,1,0:T(8,128)(2,1)S(1)}, u32[]{:S(2)}, u32[]{:S(2)}) %collective-permute-start.26) | collective-permute-done | bytes 524320 | tf_op jit(solution)/shard_map/ppermute | solution.py:618
  319.0 2.1 collective-permute-done.27.rest_2_
  321.1 5.6 %collective-permute-done.28.rest_3_ = bf16[2,256,512]{2,1,0:T(8,128)(2,1)S(1)} collective-permute-done((bf16[2,256,512]{2,1,0:T(8,128)(2,1)}, bf16[2,256,512]{2,1,0:T(8,128)(2,1)S(1)}, u32[]{:S(2)}, u32[]{:S(2)}) %collective-permute-start.28) | collective-permute-done | bytes 524320 | tf_op jit(solution)/shard_map/ppermute | solution.py:618
  327.5 65.3 %shard_map.61 = bf16[2,256,2048]{2,1,0:T(8,128)(2,1)} custom-call(s32[4]{0:T(128)} %pad_add_fusion.place, bf16[2,256,512]{2,1,0:T(8,128)(2,1)} %copy-done.3, bf16[2,256,512]{2,1,0:T(8,128)(2,1)} %copy-done.4, bf16[2,256,512]{2,1,0:T(8,128)(2,1)} %copy-done.5, bf16[2,256,512]{2,1,0:T(8,128)(2,1)} %copy-done.6), custom_call_target="tpu_custom_call" | custom-call | tf_op jit(solution)/shard_map/pallas_call | solution.py:620
  (81 shorter events, 12.2 us)
Async XLA Ops:
  0.0 89.8 %copy-start.20 = (s32[16]{0:T(128)S(1)}, s32[16]{0:T(128)}, u32[]{:S(2)}) copy-start(s32[16]{0:T(128)} %param.6) | copy-start | bytes 196
  1.0 8.6 %collective-permute-start.15 = (bf16[64,512]{1,0:T(8,128)(2,1)S(1)}, bf16[64,512]{1,0:T(8,128)(2,1)S(1)}, u32[]{:S(2)}, u32[]{:S(2)}) collective-permute-start(bf16[64,512]{1,0:T(8,128)(2,1)S(1)} %dynamic-slice_bitcast_fusion), channel_id=1, source_target_pairs={{0,20},{4,16},{8,4},{12,0},{16,28},{20,24},{24,12},{28,8},{1,21},{... | collective-permute-start | bytes 196616 | tf_op jit(solution)/shard_map/ppermute | solution.py:514
  4.6 89.1 %copy-start.2 = (bf16[4,64,512]{2,1,0:T(8,128)(2,1)}, bf16[4,64,512]{2,1,0:T(8,128)(2,1)S(1)}, u32[]{:S(2)}) copy-start(bf16[4,64,512]{2,1,0:T(8,128)(2,1)S(1)} %pad_maximum_fusion.own) | copy-start | bytes 786436
  4.6 80.7 %collective-permute-start.2 = (bf16[4,64,512]{2,1,0:T(8,128)(2,1)S(1)}, bf16[4,64,512]{2,1,0:T(8,128)(2,1)S(1)}, u32[]{:S(2)}, u32[]{:S(2)}) collective-permute-start(bf16[4,64,512]{2,1,0:T(8,128)(2,1)S(1)} %pad_maximum_fusion.own), channel_id=1, source_target_pairs={{0,3},{1,0},{2,1},{3,2},{4,7},{5,4},{6,5},{7,6},{8,11},{9,8},{10,9... | collective-permute-start | bytes 786440 | tf_op jit(solution)/shard_map/ppermute | solution.py:481
  8.0 79.2 %collective-permute-start.1 = (bf16[4,64,512]{2,1,0:T(8,128)(2,1)S(1)}, bf16[4,64,512]{2,1,0:T(8,128)(2,1)S(1)}, u32[]{:S(2)}, u32[]{:S(2)}) collective-permute-start(bf16[4,64,512]{2,1,0:T(8,128)(2,1)S(1)} %pad_maximum_fusion.own), channel_id=1, source_target_pairs={{0,2},{1,3},{2,0},{3,1},{4,6},{5,7},{6,4},{7,5},{8,10},{9,11},{10,... | collective-permute-start | bytes 786440 | tf_op jit(solution)/shard_map/ppermute | solution.py:481
  8.0 5.8 %collective-permute-start.14 = (bf16[64,512]{1,0:T(8,128)(2,1)S(1)}, bf16[64,512]{1,0:T(8,128)(2,1)S(1)}, u32[]{:S(2)}, u32[]{:S(2)}) collective-permute-start(bf16[64,512]{1,0:T(8,128)(2,1)S(1)} %dynamic-slice_bitcast_fusion), channel_id=1, source_target_pairs={{0,16},{4,20},{8,0},{12,4},{16,24},{20,28},{24,8},{28,12},{1,17},{... | collective-permute-start | bytes 196616 | tf_op jit(solution)/shard_map/ppermute | solution.py:514
  9.6 4.9 %collective-permute-start.13 = (bf16[64,512]{1,0:T(8,128)(2,1)S(1)}, bf16[64,512]{1,0:T(8,128)(2,1)S(1)}, u32[]{:S(2)}, u32[]{:S(2)}) collective-permute-start(bf16[64,512]{1,0:T(8,128)(2,1)S(1)} %dynamic-slice_bitcast_fusion), channel_id=1, source_target_pairs={{0,4},{4,0},{8,20},{12,16},{16,12},{20,8},{24,28},{28,24},{1,5},{5... | collective-permute-start | bytes 196616 | tf_op jit(solution)/shard_map/ppermute | solution.py:514
  9.6 5.6 %collective-permute-start.12 = (bf16[64,512]{1,0:T(8,128)(2,1)S(1)}, bf16[64,512]{1,0:T(8,128)(2,1)S(1)}, u32[]{:S(2)}, u32[]{:S(2)}) collective-permute-start(bf16[64,512]{1,0:T(8,128)(2,1)S(1)} %dynamic-slice_bitcast_fusion), channel_id=1, source_target_pairs={{0,0},{4,4},{8,16},{12,20},{16,8},{20,12},{24,24},{28,28},{1,1},{5... | collective-permute-start | bytes 196616 | tf_op jit(solution)/shard_map/ppermute | solution.py:514
  13.8 73.4 %collective-permute-start = (bf16[4,64,512]{2,1,0:T(8,128)(2,1)S(1)}, bf16[4,64,512]{2,1,0:T(8,128)(2,1)S(1)}, u32[]{:S(2)}, u32[]{:S(2)}) collective-permute-start(bf16[4,64,512]{2,1,0:T(8,128)(2,1)S(1)} %pad_maximum_fusion.own), channel_id=1, source_target_pairs={{0,1},{1,2},{2,3},{3,0},{4,5},{5,6},{6,7},{7,4},{8,9},{9,10},{10,1... | collective-permute-start | bytes 786440 | tf_op jit(solution)/shard_map/ppermute | solution.py:481
  15.2 147.2 %copy-start.1 = (bf16[4,64,512]{2,1,0:T(8,128)(2,1)}, bf16[4,64,512]{2,1,0:T(8,128)(2,1)S(1)}, u32[]{:S(2)}) copy-start(bf16[4,64,512]{2,1,0:T(8,128)(2,1)S(1)} %pad_maximum_fusion.1.own) | copy-start | bytes 786436
  15.2 73.1 %collective-permute-start.18 = (bf16[4,64,512]{2,1,0:T(8,128)(2,1)S(1)}, bf16[4,64,512]{2,1,0:T(8,128)(2,1)S(1)}, u32[]{:S(2)}, u32[]{:S(2)}) collective-permute-start(bf16[4,64,512]{2,1,0:T(8,128)(2,1)S(1)} %pad_maximum_fusion.1.own), channel_id=1, source_target_pairs={{0,3},{1,0},{2,1},{3,2},{4,7},{5,4},{6,5},{7,6},{8,11},{9,8},{10,9... | collective-permute-start | bytes 786440 | tf_op jit(solution)/shard_map/ppermute | solution.py:481
  82.5 47.6 %collective-permute-start.19 = (bf16[2,256,512]{2,1,0:T(8,128)(2,1)}, bf16[2,256,512]{2,1,0:T(8,128)(2,1)S(1)}, u32[]{:S(2)}, u32[]{:S(2)}) collective-permute-start(bf16[2,256,512]{2,1,0:T(8,128)(2,1)} %get-tuple-element.21), channel_id=1, source_target_pairs={{0,0},{4,4},{8,16},{12,20},{16,8},{20,12},{24,24},{28,28},{1,1},{5... | collective-permute-start | bytes 1572872 | tf_op jit(solution)/shard_map/ppermute | solution.py:500
  85.3 46.7 %collective-permute-start.20 = (bf16[2,256,512]{2,1,0:T(8,128)(2,1)}, bf16[2,256,512]{2,1,0:T(8,128)(2,1)S(1)}, u32[]{:S(2)}, u32[]{:S(2)}) collective-permute-start(bf16[2,256,512]{2,1,0:T(8,128)(2,1)} %get-tuple-element.22), channel_id=1, source_target_pairs={{0,4},{4,0},{8,20},{12,16},{16,12},{20,8},{24,28},{28,24},{1,5},{5... | collective-permute-start | bytes 1572872 | tf_op jit(solution)/shard_map/ppermute | solution.py:500
  87.2 46.2 %collective-permute-start.21 = (bf16[2,256,512]{2,1,0:T(8,128)(2,1)}, bf16[2,256,512]{2,1,0:T(8,128)(2,1)}, u32[]{:S(2)}, u32[]{:S(2)}) collective-permute-start(bf16[2,256,512]{2,1,0:T(8,128)(2,1)} %get-tuple-element.23), channel_id=1, source_target_pairs={{0,16},{4,20},{8,0},{12,4},{16,24},{20,28},{24,8},{28,12},{1,17},{... | collective-permute-start | bytes 1572872 | tf_op jit(solution)/shard_map/ppermute | solution.py:500
  87.2 40.1 %collective-permute-start.17 = (bf16[4,64,512]{2,1,0:T(8,128)(2,1)S(1)}, bf16[4,64,512]{2,1,0:T(8,128)(2,1)S(1)}, u32[]{:S(2)}, u32[]{:S(2)}) collective-permute-start(bf16[4,64,512]{2,1,0:T(8,128)(2,1)S(1)} %pad_maximum_fusion.1.own), channel_id=1, source_target_pairs={{0,2},{1,3},{2,0},{3,1},{4,6},{5,7},{6,4},{7,5},{8,10},{9,11},{10,... | collective-permute-start | bytes 786440 | tf_op jit(solution)/shard_map/ppermute | solution.py:481
  88.3 41.7 %collective-permute-start.16 = (bf16[4,64,512]{2,1,0:T(8,128)(2,1)S(1)}, bf16[4,64,512]{2,1,0:T(8,128)(2,1)S(1)}, u32[]{:S(2)}, u32[]{:S(2)}) collective-permute-start(bf16[4,64,512]{2,1,0:T(8,128)(2,1)S(1)} %pad_maximum_fusion.1.own), channel_id=1, source_target_pairs={{0,1},{1,2},{2,3},{3,0},{4,5},{5,6},{6,7},{7,4},{8,9},{9,10},{10,1... | collective-permute-start | bytes 786440 | tf_op jit(solution)/shard_map/ppermute | solution.py:481
  127.3 18.8 %collective-permute-start.22 = (bf16[2,256,512]{2,1,0:T(8,128)(2,1)}, bf16[2,256,512]{2,1,0:T(8,128)(2,1)S(1)}, u32[]{:S(2)}, u32[]{:S(2)}) collective-permute-start(bf16[2,256,512]{2,1,0:T(8,128)(2,1)} %get-tuple-element.24), channel_id=1, source_target_pairs={{0,20},{4,16},{8,4},{12,0},{16,28},{20,24},{24,12},{28,8},{1,21},{... | collective-permute-start | bytes 1572872 | tf_op jit(solution)/shard_map/ppermute | solution.py:500
  130.0 18.0 %collective-permute-start.10 = (bf16[2,256,512]{2,1,0:T(8,128)(2,1)}, bf16[2,256,512]{2,1,0:T(8,128)(2,1)S(1)}, u32[]{:S(2)}, u32[]{:S(2)}) collective-permute-start(bf16[2,256,512]{2,1,0:T(8,128)(2,1)} %get-tuple-element.20), channel_id=1, source_target_pairs={{0,16},{4,20},{8,0},{12,4},{16,24},{20,28},{24,8},{28,12},{1,17},{... | collective-permute-start | bytes 1572872 | tf_op jit(solution)/shard_map/ppermute | solution.py:525
  130.1 19.2 %collective-permute-start.8 = (bf16[2,256,512]{2,1,0:T(8,128)(2,1)}, bf16[2,256,512]{2,1,0:T(8,128)(2,1)S(1)}, u32[]{:S(2)}, u32[]{:S(2)}) collective-permute-start(bf16[2,256,512]{2,1,0:T(8,128)(2,1)} %get-tuple-element.20), channel_id=1, source_target_pairs={{0,0},{4,4},{8,16},{12,20},{16,8},{20,12},{24,24},{28,28},{1,1},{5... | collective-permute-start | bytes 1572872 | tf_op jit(solution)/shard_map/ppermute | solution.py:525
  132.0 21.4 %collective-permute-start.4 = (bf16[2,256,512]{2,1,0:T(8,128)(2,1)}, bf16[2,256,512]{2,1,0:T(8,128)(2,1)}, u32[]{:S(2)}, u32[]{:S(2)}) collective-permute-start(bf16[2,256,512]{2,1,0:T(8,128)(2,1)} %get-tuple-element.19), channel_id=1, source_target_pairs={{0,4},{4,0},{1,5},{5,1},{2,6},{6,2},{3,7},{7,3},{8,12},{12,8},{9,1... | collective-permute-start | bytes 1572872 | tf_op jit(solution)/shard_map/ppermute | solution.py:528
  133.3 22.5 %collective-permute-start.6 = (bf16[2,256,512]{2,1,0:T(8,128)(2,1)}, bf16[2,256,512]{2,1,0:T(8,128)(2,1)}, u32[]{:S(2)}, u32[]{:S(2)}) collective-permute-start(bf16[2,256,512]{2,1,0:T(8,128)(2,1)} %get-tuple-element.19), channel_id=1, source_target_pairs={{0,16},{4,20},{8,0},{12,4},{16,24},{20,28},{24,8},{28,12},{1,17},{... | collective-permute-start | bytes 1572872 | tf_op jit(solution)/shard_map/ppermute | solution.py:525
  146.1 50.0 %collective-permute-start.3 = (bf16[2,256,512]{2,1,0:T(8,128)(2,1)}, bf16[2,256,512]{2,1,0:T(8,128)(2,1)}, u32[]{:S(2)}, u32[]{:S(2)}) collective-permute-start(bf16[2,256,512]{2,1,0:T(8,128)(2,1)} %get-tuple-element.19), channel_id=1, source_target_pairs={{0,0},{4,4},{8,16},{12,20},{16,8},{20,12},{24,24},{28,28},{1,1},{5... | collective-permute-start | bytes 1572872 | tf_op jit(solution)/shard_map/ppermute | solution.py:525
  148.1 48.1 %collective-permute-start.11 = (bf16[2,256,512]{2,1,0:T(8,128)(2,1)S(1)}, bf16[2,256,512]{2,1,0:T(8,128)(2,1)}, u32[]{:S(2)}, u32[]{:S(2)}) collective-permute-start(bf16[2,256,512]{2,1,0:T(8,128)(2,1)S(1)} %collective-permute-done.10.y2), channel_id=1, source_target_pairs={{0,4},{4,0},{1,5},{5,1},{2,6},{6,2},{3,7},{7,3},{8,12},{12,8},{9,1... | collective-permute-start | bytes 1572872 | tf_op jit(solution)/shard_map/ppermute | solution.py:528
  149.3 46.9 %collective-permute-start.9 = (bf16[2,256,512]{2,1,0:T(8,128)(2,1)S(1)}, bf16[2,256,512]{2,1,0:T(8,128)(2,1)}, u32[]{:S(2)}, u32[]{:S(2)}) collective-permute-start(bf16[2,256,512]{2,1,0:T(8,128)(2,1)S(1)} %collective-permute-done.8.y0), channel_id=1, source_target_pairs={{0,4},{4,0},{1,5},{5,1},{2,6},{6,2},{3,7},{7,3},{8,12},{12,8},{9,1... | collective-permute-start | bytes 1572872 | tf_op jit(solution)/shard_map/ppermute | solution.py:528
  153.4 42.8 %collective-permute-start.7 = (bf16[2,256,512]{2,1,0:T(8,128)(2,1)}, bf16[2,256,512]{2,1,0:T(8,128)(2,1)}, u32[]{:S(2)}, u32[]{:S(2)}) collective-permute-start(bf16[2,256,512]{2,1,0:T(8,128)(2,1)} %collective-permute-done.4), channel_id=1, source_target_pairs={{0,16},{4,20},{8,0},{12,4},{16,24},{20,28},{24,8},{28,12},{1,17},{... | collective-permute-start | bytes 1572872 | tf_op jit(solution)/shard_map/ppermute | solution.py:525
  155.8 40.4 %collective-permute-start.5 = (bf16[2,256,512]{2,1,0:T(8,128)(2,1)}, bf16[2,256,512]{2,1,0:T(8,128)(2,1)}, u32[]{:S(2)}, u32[]{:S(2)}) collective-permute-start(bf16[2,256,512]{2,1,0:T(8,128)(2,1)} %collective-permute-done.4), channel_id=1, source_target_pairs={{0,0},{4,4},{8,16},{12,20},{16,8},{20,12},{24,24},{28,28},{1,1},{5... | collective-permute-start | bytes 1572872 | tf_op jit(solution)/shard_map/ppermute | solution.py:525
  198.6 15.3 %collective-permute-start.23 = (bf16[2,512,512]{2,1,0:T(8,128)(2,1)}, bf16[2,512,512]{2,1,0:T(8,128)(2,1)S(1)}, u32[]{:S(2)}, u32[]{:S(2)}) collective-permute-start(bf16[2,512,512]{2,1,0:T(8,128)(2,1)} %get-tuple-element.26.w_high), channel_id=1, source_target_pairs={{0,8},{16,24},{1,9},{17,25},{2,10},{18,26},{3,11},{19,27},{4,12},{... | collective-permute-start | bytes 3145736 | tf_op jit(solution)/shard_map/ppermute | solution.py:569
  231.1 3.8 collective-permute-start.24
  301.5 10.7 %collective-permute-start.25 = (bf16[2,256,512]{2,1,0:T(8,128)(2,1)}, bf16[2,256,512]{2,1,0:T(8,128)(2,1)S(1)}, u32[]{:S(2)}, u32[]{:S(2)}) collective-permute-start(bf16[2,256,512]{2,1,0:T(8,128)(2,1)} %get-tuple-element.29), channel_id=1, source_target_pairs={{0,0},{4,4},{16,8},{20,12},{8,16},{12,20},{24,24},{28,28},{1,1},{5... | collective-permute-start | bytes 1572872 | tf_op jit(solution)/shard_map/ppermute | solution.py:618
  303.4 15.5 %collective-permute-start.26 = (bf16[2,256,512]{2,1,0:T(8,128)(2,1)}, bf16[2,256,512]{2,1,0:T(8,128)(2,1)S(1)}, u32[]{:S(2)}, u32[]{:S(2)}) collective-permute-start(bf16[2,256,512]{2,1,0:T(8,128)(2,1)} %get-tuple-element.30), channel_id=1, source_target_pairs={{4,0},{0,4},{20,8},{16,12},{12,16},{8,20},{28,24},{24,28},{5,1},{1... | collective-permute-start | bytes 1572872 | tf_op jit(solution)/shard_map/ppermute | solution.py:618
  306.3 14.9 %collective-permute-start.27 = (bf16[2,256,512]{2,1,0:T(8,128)(2,1)}, bf16[2,256,512]{2,1,0:T(8,128)(2,1)S(1)}, u32[]{:S(2)}, u32[]{:S(2)}) collective-permute-start(bf16[2,256,512]{2,1,0:T(8,128)(2,1)} %get-tuple-element.31), channel_id=1, source_target_pairs={{16,0},{20,4},{0,8},{4,12},{24,16},{28,20},{8,24},{12,28},{17,1},{... | collective-permute-start | bytes 1572872 | tf_op jit(solution)/shard_map/ppermute | solution.py:618
  306.3 20.5 %collective-permute-start.28 = (bf16[2,256,512]{2,1,0:T(8,128)(2,1)}, bf16[2,256,512]{2,1,0:T(8,128)(2,1)S(1)}, u32[]{:S(2)}, u32[]{:S(2)}) collective-permute-start(bf16[2,256,512]{2,1,0:T(8,128)(2,1)} %get-tuple-element.32), channel_id=1, source_target_pairs={{20,0},{16,4},{4,8},{0,12},{28,16},{24,20},{12,24},{8,28},{21,1},{... | collective-permute-start | bytes 1572872 | tf_op jit(solution)/shard_map/ppermute | solution.py:618
  (18 other events, 423.3 us)

commit v2 on v1

--- a/solution.py
+++ b/solution.py
@@ -8,7 +8,7 @@
 from jax.sharding import PartitionSpec as P
 
 source_amplitude = 8.0
-vmem_bytes = 60 * 1024 * 1024
+vmem_bytes = 32 * 1024 * 1024
 bf16 = jnp.bfloat16
 f32 = jnp.float32
 anywhere = pl.BlockSpec(memory_space=pl.ANY)
@@ -221,62 +221,72 @@
 
 
 class Factors:
-    def __init__(self, info, columns, plain, crossed, sems):
-        order = plain.shape[2]
-        self.order, self.plain, self.crossed, self.sems = order, plain, crossed, sems
-        self.columns = columns
-        left, right = pl.ds(0, order), pl.ds(order, order)
-        self.ends = ((0, plain, left), (1, plain, right), (1, crossed, left), (0, crossed, right))
+    def __init__(self, info, columns, held, sems):
+        self.order, self.held, self.sems, self.columns = held.shape[2], held, sems, columns
         height = columns[0][0].shape[1]
         for which in (1, 0):
             for index, column in enumerate(columns[which]):
                 slot, half = info[info_slot + index // 2], info[info_half + index % 2]
                 rows = pl.ds(pl.multiple_of(half * height, height), height)
-                for end, (plane, target, side) in enumerate(self.ends):
-                    pltpu.make_async_copy(
-                        column.at[plane],
-                        target.at[slot, which, rows, side],
-                        sems.at[slot, which, index % 2, end],
-                    ).start()
+                for plane in range(2):
+                    self.copy(column, plane, slot, which, rows, index % 2).start()
+
+    def copy(self, column, plane, slot, which, rows, half):
+        target = self.held.at[slot, which, rows, pl.ds(plane * self.order, self.order)]
+        return pltpu.make_async_copy(
+            column.at[plane], target, self.sems.at[slot, which, half, plane]
+        )
 
     def ready(self, slot, which):
         column = self.columns[which][0]
         height = column.shape[1]
         for half in range(2):
-            rows = pl.ds(half * height, height)
-            for end, (plane, target, side) in enumerate(self.ends):
-                pltpu.make_async_copy(
-                    column.at[plane],
-                    target.at[slot, which, rows, side],
-                    self.sems.at[slot, which, half, end],
-                ).wait()
-        right = slice(self.order, 2 * self.order)
-        self.plain[slot, which, :, right] = -self.plain[slot, which, :, right]
+            for plane in range(2):
+                rows = pl.ds(half * height, height)
+                self.copy(column, plane, slot, which, rows, half).wait()
 
     def apply(self, slot, beside, below, store, fresh):
         order = self.order
         turned = (((1,), (1,)), ((), ()))
         if fresh:
             self.ready(slot, 1)
-        for plane, ref in enumerate((self.plain, self.crossed)):
-            for columns in row_chunks(order, 256):
-                part = lax.dot_general(
-                    beside[...], ref[slot, 1, columns], turned, preferred_element_type=f32
-                )
-                below[plane * order : (plane + 1) * order, columns] = part.astype(bf16)
+        for columns in row_chunks(order, 256):
+            part = lax.dot_general(
+                beside[...], self.held[slot, 1, columns], turned, preferred_element_type=f32
+            ).astype(bf16)
+            real, imag = part[:order], part[order:]
+            further = slice(columns.start + order, columns.stop + order)
+            below[:order, columns] = real
+            below[:order, further] = imag
+            below[order:, columns] = -imag
+            below[order:, further] = real
         if fresh:
             self.ready(slot, 0)
-        for plane, ref in enumerate((self.plain, self.crossed)):
+        for plane in range(2):
             for columns in row_chunks(order, 256):
+                along = slice(columns.start + plane * order, columns.stop + plane * order)
                 store(
                     plane,
                     columns,
-                    jnp.dot(ref[slot, 0], below[:, columns], preferred_element_type=f32),
+                    jnp.dot(self.held[slot, 0], below[:, along], preferred_element_type=f32),
                 )
 
 
+def put_beside(beside, plane, rows, values):
+    order = beside.shape[0] // 2
+    left, right = slice(0, order), slice(order, 2 * order)
+    lower = slice(rows.start + order, rows.stop + order)
+    values = values.astype(bf16)
+    if plane == 0:
+        beside[rows, left] = values
+        beside[lower, right] = values
+    else:
+        beside[rows, right] = -values
+        beside[lower, left] = values
+
+
 def reduce_into(beside, rhs, info, slot, weights, incoming):
-    order = beside.shape[0]
+    order = beside.shape[0] // 2
     for plane in range(2):
         for rows in row_chunks(order, 128):
             values = rhs[slot, plane, rows].astype(f32)
@@ -286,15 +296,15 @@
                 hit = (row == info[1]) & (column == info[2]) & (info[0] == slot)
                 values = values + jnp.where(hit, f32(source_amplitude), f32(0.0))
             scaled = weights[slot, rows].astype(f32) * incoming(plane, rows)
-            beside[rows, plane * order : (plane + 1) * order] = (values - scaled).astype(bf16)
+            put_beside(beside, plane, rows, values - scaled)
 
 
 def sent_into(beside, weights, slot, field):
-    order = beside.shape[0]
+    order = beside.shape[0] // 2
     for plane in range(2):
         for rows in row_chunks(order, 128):
             scaled = weights[slot, rows].astype(f32) * field(plane, rows)
-            beside[rows, plane * order : (plane + 1) * order] = scaled.astype(bf16)
+            put_beside(beside, plane, rows, scaled)
 
 
 def subtract_into(target, forward):
@@ -323,13 +333,13 @@
 
 
 def first_kernel(info, x0, x1, x2, x3, y0, y1, y2, y3, coupling, p0, p1, p2, p3, w_low, w_high,
-                 plain, crossed, weights, rhs, beside, below, sems, fsems):
+                 held, weights, rhs, beside, below, sems, fsems):
     @pl.when(info[info_member] == 0)
     def _():
         early = rhs_copies(info, (p0, p1, p2, p3), rhs, sems)
         early.append(pltpu.make_async_copy(coupling, weights, sems.at[4]))
         start_all(early)
-        factors = Factors(info, ((x0, x1, x2, x3), (y0, y1, y2, y3)), plain, crossed, fsems)
+        factors = Factors(info, ((x0, x1, x2, x3), (y0, y1, y2, y3)), held, fsems)
         wait_all(early)
         reduce_into(beside, rhs, info, 0, weights, lambda plane, rows: f32(0.0))
         factors.apply(0, beside, below, round_into(w_low), True)
@@ -340,16 +350,16 @@
 
 
 def last_kernel(info, x0, x1, x2, x3, y0, y1, y2, y3, coupling, p0, p1, p2, p3, incoming, field,
-                sent, plain, crossed, weights, rhs, arrived, kept, beside, below, sems, fsems, osems):
+                sent, held, weights, rhs, arrived, kept, beside, below, sems, fsems, osems):
     @pl.when(info[info_member] == 1)
     def _():
         early = rhs_copies(info, (p0, p1, p2, p3), rhs, sems)
         early.append(pltpu.make_async_copy(coupling, weights, sems.at[4]))
         early.append(pltpu.make_async_copy(incoming, arrived, sems.at[5]))
         start_all(early)
-        factors = Factors(info, ((x0, x1, x2, x3), (y0, y1, y2, y3)), plain, crossed, fsems)
+        factors = Factors(info, ((x0, x1, x2, x3), (y0, y1, y2, y3)), held, fsems)
         wait_all(early)
-        order = beside.shape[0]
+        order = beside.shape[0] // 2
         reduce_into(
             beside, rhs, info, 0, weights, lambda plane, rows: arrived[plane, rows].astype(f32)
         )
@@ -373,42 +383,29 @@
         out_low.start()
         sent_into(beside, weights, 0, lambda plane, rows: w_low[plane, rows].astype(f32))
         for plane in range(2):
-            sent[plane] = beside[:, plane * order : (plane + 1) * order]
+            sent[plane] = beside[plane * order : (plane + 1) * order, :order]
         out_high.wait()
         out_low.wait()
 
 
 def back_kernel(info, x0, x1, x2, x3, y0, y1, y2, y3, coupling, w_low, w_high, incoming, field,
-                p0, p1, p2, p3, plain, crossed, weights, kept, beside, below, sems, fsems, osems):
-    def piece_copies(source):
-        copies = []
-        for index, piece in enumerate((p0, p1, p2, p3)):
-            height = piece.shape[1]
-            slot, half = info[info_piece + 2 * index], info[info_piece + 2 * index + 1]
-            rows = pl.ds(pl.multiple_of(half * height, height), height)
-            copies.append(
-                pltpu.make_async_copy(source.at[slot, :, rows, :], piece, osems.at[index])
-            )
-        return copies
-
+                p0, p1, p2, p3, held, weights, kept, arrived, beside, below, sems, fsems, osems):
     @pl.when(info[info_member] == 0)
     def _():
-        order = beside.shape[0]
-        columns = [pl.ds(plane * order, order) for plane in range(2)]
-        early = [
-            pltpu.make_async_copy(incoming.at[plane], beside.at[:, columns[plane]], sems.at[plane])
-            for plane in range(2)
+        early = [pltpu.make_async_copy(incoming, arrived, sems.at[0])]
+        start_all(early)
+        factors = Factors(info, ((x0, x1, x2, x3), (y0, y1, y2, y3)), held, fsems)
+        early += [
+            pltpu.make_async_copy(coupling, weights, sems.at[1]),
+            pltpu.make_async_copy(w_low, kept.at[0], sems.at[2]),
+            pltpu.make_async_copy(w_high, kept.at[1], sems.at[3]),
         ]
-        start_all(early)
-        factors = Factors(info, ((x0, x1, x2, x3), (y0, y1, y2, y3)), plain, crossed, fsems)
-        later = [
-            pltpu.make_async_copy(coupling, weights, sems.at[2]),
-            pltpu.make_async_copy(w_low, kept.at[0], sems.at[3]),
-            pltpu.make_async_copy(w_high, kept.at[1], sems.at[4]),
-        ]
-        start_all(later)
+        start_all(early[1:])
         wait_all(early)
-        wait_all(later)
+        order = beside.shape[0] // 2
+        for plane in range(2):
+            for rows in row_chunks(order, 128):
+                put_beside(beside, plane, rows, arrived[plane, rows])
         u_low, u_high = kept.at[0], kept.at[1]
         factors.apply(
             1,
@@ -425,15 +422,21 @@
             subtract_into(u_low, lambda plane, columns: u_low[plane, :, columns]),
             True,
         )
-        copies = piece_copies(kept)
-        start_all(copies)
-        wait_all(copies)
 
     @pl.when(info[info_member] != 0)
     def _():
-        copies = piece_copies(field)
-        start_all(copies)
-        wait_all(copies)
+        finished = pltpu.make_async_copy(field, kept, sems.at[0])
+        finished.start()
+        finished.wait()
+
+    copies = []
+    for index, piece in enumerate((p0, p1, p2, p3)):
+        height = piece.shape[1]
+        slot, half = info[info_piece + 2 * index], info[info_piece + 2 * index + 1]
+        rows = pl.ds(pl.multiple_of(half * height, height), height)
+        copies.append(pltpu.make_async_copy(kept.at[slot, :, rows, :], piece, osems.at[index]))
+    start_all(copies)
+    wait_all(copies)
 
 
 def on_device(background, src_pos, coupling, x_factor, y_factor):
@@ -492,7 +495,7 @@
         pack_kernel,
         out_shape=[piece_shape] * len(rounds),
         in_specs=[in_smem, anywhere],
-        out_specs=[anywhere] * len(rounds),
+        out_specs=[in_vmem] * len(rounds),
         scratch_shapes=[pltpu.SemaphoreType.DMA((len(rounds),))],
         compiler_params=params,
     )(sends_to, field)
@@ -505,7 +508,7 @@
         stack_kernel,
         out_shape=[column_shape] * 2,
         in_specs=[in_smem] + [anywhere] * 4,
-        out_specs=[anywhere] * 2,
+        out_specs=[in_vmem] * 2,
         scratch_shapes=[pltpu.SemaphoreType.DMA((4, 2))],
         compiler_params=params,
     )(info, *shards)
@@ -516,7 +519,7 @@
         weight_kernel,
         out_shape=jax.ShapeDtypeStruct((2, order, order), bf16),
         in_specs=[in_smem] + [anywhere] * 4,
-        out_specs=anywhere,
+        out_specs=in_vmem,
         scratch_shapes=[pltpu.SemaphoreType.DMA((4, 4))],
         compiler_params=params,
     )(info, *rotated(own_weights))
@@ -538,11 +541,12 @@
 
     full_shape = jax.ShapeDtypeStruct((2, order, order), bf16)
     factor_scratch = pltpu.VMEM((2, 2, order, 2 * order), bf16)
+    arrived_scratch = pltpu.VMEM((2, order, order), bf16)
     weight_scratch = pltpu.VMEM((2, order, order), bf16)
     field_scratch = pltpu.VMEM((2, 2, order, order), bf16)
-    beside_scratch = pltpu.VMEM((order, 2 * order), bf16)
-    below_scratch = pltpu.VMEM((2 * order, order), bf16)
-    factor_sems = pltpu.SemaphoreType.DMA((2, 2, 2, 4))
+    beside_scratch = pltpu.VMEM((2 * order, 2 * order), bf16)
+    below_scratch = beside_scratch
+    factor_sems = pltpu.SemaphoreType.DMA((2, 2, 2, 2))
     solve_flops = 16 * order**3
     w_low, w_high = pl.pallas_call(
         first_kernel,
@@ -550,7 +554,6 @@
         in_specs=[in_smem] + [anywhere] * 13,
         out_specs=[in_vmem] * 2,
         scratch_shapes=[
-            factor_scratch,
             factor_scratch,
             weight_scratch,
             field_scratch,
@@ -574,10 +577,9 @@
         out_specs=[anywhere, in_vmem],
         scratch_shapes=[
             factor_scratch,
-            factor_scratch,
             weight_scratch,
             field_scratch,
-            pltpu.VMEM((2, order, order), bf16),
+            arrived_scratch,
             field_scratch,
             beside_scratch,
             below_scratch,
@@ -600,9 +602,9 @@
         out_specs=[anywhere] * len(rounds),
         scratch_shapes=[
             factor_scratch,
-            factor_scratch,
             weight_scratch,
             field_scratch,
+            arrived_scratch,
             beside_scratch,
             below_scratch,
             pltpu.SemaphoreType.DMA((6,)),
@@ -621,7 +623,7 @@
         unpack_kernel,
         out_shape=jax.ShapeDtypeStruct(field.shape, bf16),
         in_specs=[in_smem] + [anywhere] * len(rounds),
-        out_specs=anywhere,
+        out_specs=in_vmem,
         scratch_shapes=[pltpu.SemaphoreType.DMA((len(rounds),))],
         compiler_params=params,
     )(sends_to, *results)

time: 398 us -> 168 us (0.42)
  Pallas kernels: 282 us -> 20.8 us
  waiting for transfers between devices: 54 us -> 79.1 us
  starting transfers between devices: 47.1 us -> 58.1 us
    pallas_call x1, Pallas kernels: 65.7 us -> 1.09 us  [on_device(): pl.pallas_call(back_kernel, out_shape=[piece_shape] * len(rounds), in_spe...]
    pallas_call x1, Pallas kernels: 65.3 us -> 2.06 us  [on_device(): pl.pallas_call(pack_kernel, out_shape=[piece_shape] * len(rounds), in_spe...]
    pallas_call x1, Pallas kernels: 65.3 us -> 2.21 us  [on_device(): pl.pallas_call(unpack_kernel, out_shape=jax.ShapeDtypeStruct(field.shape,...]
    pallas_call x1, Pallas kernels: 33.6 us -> 1.31 us  [on_device(): pl.pallas_call(stack_kernel, out_shape=[column_shape] * 2, in_specs=[in_s...]
    pallas_call x1, Pallas kernels: 33.7 us -> 2.32 us  [on_device(): pl.pallas_call(weight_kernel, out_shape=jax.ShapeDtypeStruct((2, order, o...]
    ppermute x6, waiting for transfers between devices: 0.02 us -> 16.7 us  [rotated(): lax.ppermute(block, 'py', [(z, (z + turn) % py_count) for z in range(py_c...]
    ppermute x3, waiting for transfers between devices: 3.78 us -> 18 us  [aside(): return lax.ppermute(block, 'px', [(y, (y + 1) % 2) for y in range(2)])]
    ppermute x4, starting transfers between devices: 4.9 us -> 13.5 us  [on_device(): lax.ppermute(piece, ('sec', 'px'), back_pairs(a, b))]
  transfers between devices with their start and end apart: 29 -> 29, of which waited for: 9 -> 14; matrix products, arithmetic and copies ran while one was open for 1% -> 1% of each run, Pallas kernels for 34% -> 3%
where the time goes in v2:
time: 168 us; the launch traced here: 166 us
  waiting for transfers between devices  79.1 us (47%)
  starting transfers between devices  58.1 us (35%)
  Pallas kernels  20.8 us (12%)
  local copies, waits for them, and re-layouts  4.02 us (2%)
  between operations  2.81 us (2%)
    ppermute x4, waiting for transfers between devices, on_device(): lax.ppermute(piece, ('sec', 'px'), back_pairs(a, b))  20.2 us
    ppermute x3, waiting for transfers between devices, aside(): return lax.ppermute(block, 'px', [(y, (y + 1) % 2) for y in range(2)])  18 us
    ppermute x6, waiting for transfers between devices, rotated(): lax.ppermute(block, 'py', [(z, (z + turn) % py_count) for z in range(py_c...  16.7 us
    ppermute x4, starting transfers between devices, on_device(): lax.ppermute(piece, ('sec', 'px'), back_pairs(a, b))  13.5 us
    ppermute x4, waiting for transfers between devices, on_device(): lax.ppermute(piece, ('sec', 'px'), pairs(a, b))  12.9 us
    ppermute x6, starting transfers between devices, across(): return lax.ppermute(block, ('sec', 'px'), pairs(a, 0))  11.2 us
    pallas_call x1, Pallas kernels, on_device(): pl.pallas_call(last_kernel, out_shape=[jax.ShapeDtypeStruct((2, 2, order,...  11.1 us
    ppermute x6, starting transfers between devices, rotated(): lax.ppermute(block, 'py', [(z, (z + turn) % py_count) for z in range(py_c...  10.5 us
  transfers between devices with their start and end apart: 29, of which 14 were waited for; matrix products, arithmetic and copies ran while one was open for 1% of the time, Pallas kernels for 3%

profile of v2, /device:TPU:1, one launch (start us, length us, event | category | flops | bytes accessed | tf_op | source)
XLA Modules:
  0.0 165.9 jit_solution(13152668722161236663)
XLA Ops:
  1.0 2.6 %collective-permute-start.15 = (bf16[64,512]{1,0:T(8,128)(2,1)S(1)}, bf16[64,512]{1,0:T(8,128)(2,1)S(1)}, u32[]{:S(2)}, u32[]{:S(2)}) collective-permute-start(bf16[64,512]{1,0:T(8,128)(2,1)S(1)} %dynamic-slice_bitcast_fusion), channel_id=1, source_target_pairs={{0,20},{4,16},{8,4},{12,0},{16,28},{20,24},{24,12},{28,8},{1,21},{... | collective-permute-start | bytes 196616 | tf_op jit(solution)/shard_map/ppermute | solution.py:517
  4.6 3.4 %collective-permute-start.2 = (bf16[4,64,512]{2,1,0:T(8,128)(2,1)S(1)}, bf16[4,64,512]{2,1,0:T(8,128)(2,1)S(1)}, u32[]{:S(2)}, u32[]{:S(2)}) collective-permute-start(bf16[4,64,512]{2,1,0:T(8,128)(2,1)S(1)} %pad_maximum_fusion.own), channel_id=1, source_target_pairs={{0,3},{1,0},{2,1},{3,2},{4,7},{5,4},{6,5},{7,6},{8,11},{9,8},{10,9... | collective-permute-start | bytes 786440 | tf_op jit(solution)/shard_map/ppermute | solution.py:484
  8.0 1.6 collective-permute-start.14
  9.6 3.6 %collective-permute-start.12 = (bf16[64,512]{1,0:T(8,128)(2,1)S(1)}, bf16[64,512]{1,0:T(8,128)(2,1)S(1)}, u32[]{:S(2)}, u32[]{:S(2)}) collective-permute-start(bf16[64,512]{1,0:T(8,128)(2,1)S(1)} %dynamic-slice_bitcast_fusion), channel_id=1, source_target_pairs={{0,0},{4,4},{8,16},{12,20},{16,8},{20,12},{24,24},{28,28},{1,1},{5... | collective-permute-start | bytes 196616 | tf_op jit(solution)/shard_map/ppermute | solution.py:517
  15.2 1.4 collective-permute-start.18
  16.6 1.6 copy-done.1
  18.2 2.1 %shard_map.57 = (bf16[2,256,512]{2,1,0:T(8,128)(2,1)}, bf16[2,256,512]{2,1,0:T(8,128)(2,1)}, bf16[2,256,512]{2,1,0:T(8,128)(2,1)}, bf16[2,256,512]{2,1,0:T(8,128)(2,1)S(1)}) custom-call(s32[4]{0:T(128)S(1)} %pad_add_fusion.place, bf16[2,256,2048]{2,1,0:T(8,128)(2,1)S(1)} %bitcast.32), custom_call_target="tpu_custom_call" | custom-call | tf_op jit(solution)/shard_map/pallas_call | solution.py:494
  21.1 3.3 %collective-permute-start.19 = (bf16[2,256,512]{2,1,0:T(8,128)(2,1)}, bf16[2,256,512]{2,1,0:T(8,128)(2,1)S(1)}, u32[]{:S(2)}, u32[]{:S(2)}) collective-permute-start(bf16[2,256,512]{2,1,0:T(8,128)(2,1)} %get-tuple-element.21), channel_id=1, source_target_pairs={{0,0},{4,4},{8,16},{12,20},{16,8},{20,12},{24,24},{28,28},{1,1},{5... | collective-permute-start | bytes 1572872 | tf_op jit(solution)/shard_map/ppermute | solution.py:503
  24.4 1.4 collective-permute-start.20
  25.7 3.3 %collective-permute-done.1.second = bf16[4,64,512]{2,1,0:T(8,128)(2,1)S(1)} collective-permute-done((bf16[4,64,512]{2,1,0:T(8,128)(2,1)S(1)}, bf16[4,64,512]{2,1,0:T(8,128)(2,1)S(1)}, u32[]{:S(2)}, u32[]{:S(2)}) %collective-permute-start.1) | collective-permute-done | bytes 262176 | tf_op jit(solution)/shard_map/ppermute | solution.py:484
  29.0 4.1 %collective-permute-start.21 = (bf16[2,256,512]{2,1,0:T(8,128)(2,1)}, bf16[2,256,512]{2,1,0:T(8,128)(2,1)}, u32[]{:S(2)}, u32[]{:S(2)}) collective-permute-start(bf16[2,256,512]{2,1,0:T(8,128)(2,1)} %get-tuple-element.23), channel_id=1, source_target_pairs={{0,16},{4,20},{8,0},{12,4},{16,24},{20,28},{24,8},{28,12},{1,17},{... | collective-permute-start | bytes 1572872 | tf_op jit(solution)/shard_map/ppermute | solution.py:503
  33.1 5.0 %collective-permute-start.17 = (bf16[4,64,512]{2,1,0:T(8,128)(2,1)S(1)}, bf16[4,64,512]{2,1,0:T(8,128)(2,1)S(1)}, u32[]{:S(2)}, u32[]{:S(2)}) collective-permute-start(bf16[4,64,512]{2,1,0:T(8,128)(2,1)S(1)} %pad_maximum_fusion.1.own), channel_id=1, source_target_pairs={{0,2},{1,3},{2,0},{3,1},{4,6},{5,7},{6,4},{7,5},{8,10},{9,11},{10,... | collective-permute-start | bytes 786440 | tf_op jit(solution)/shard_map/ppermute | solution.py:484
  42.5 13.4 %collective-permute-done.17.second = bf16[4,64,512]{2,1,0:T(8,128)(2,1)S(1)} collective-permute-done((bf16[4,64,512]{2,1,0:T(8,128)(2,1)S(1)}, bf16[4,64,512]{2,1,0:T(8,128)(2,1)S(1)}, u32[]{:S(2)}, u32[]{:S(2)}) %collective-permute-start.17) | collective-permute-done | bytes 262176 | tf_op jit(solution)/shard_map/ppermute | solution.py:484
  57.5 2.1 %collective-permute-start.8 = (bf16[2,256,512]{2,1,0:T(8,128)(2,1)S(1)}, bf16[2,256,512]{2,1,0:T(8,128)(2,1)S(1)}, u32[]{:S(2)}, u32[]{:S(2)}) collective-permute-start(bf16[2,256,512]{2,1,0:T(8,128)(2,1)S(1)} %get-tuple-element.20), channel_id=1, source_target_pairs={{0,0},{4,4},{8,16},{12,20},{16,8},{20,12},{24,24},{28,28},{1,1},{5... | collective-permute-start | bytes 1572872 | tf_op jit(solution)/shard_map/ppermute | solution.py:528
  60.9 12.9 %collective-permute-done.22.p3 = bf16[2,256,512]{2,1,0:T(8,128)(2,1)S(1)} collective-permute-done((bf16[2,256,512]{2,1,0:T(8,128)(2,1)}, bf16[2,256,512]{2,1,0:T(8,128)(2,1)S(1)}, u32[]{:S(2)}, u32[]{:S(2)}) %collective-permute-start.22) | collective-permute-done | bytes 524320 | tf_op jit(solution)/shard_map/ppermute | solution.py:503
  73.8 2.1 %collective-permute-start.3 = (bf16[2,256,512]{2,1,0:T(8,128)(2,1)S(1)}, bf16[2,256,512]{2,1,0:T(8,128)(2,1)S(1)}, u32[]{:S(2)}, u32[]{:S(2)}) collective-permute-start(bf16[2,256,512]{2,1,0:T(8,128)(2,1)S(1)} %get-tuple-element.19), channel_id=1, source_target_pairs={{0,0},{4,4},{8,16},{12,20},{16,8},{20,12},{24,24},{28,28},{1,1},{5... | collective-permute-start | bytes 1572872 | tf_op jit(solution)/shard_map/ppermute | solution.py:528
  75.9 1.4 collective-permute-start.11
  77.5 6.1 %collective-permute-done.4 = bf16[2,256,512]{2,1,0:T(8,128)(2,1)S(1)} collective-permute-done((bf16[2,256,512]{2,1,0:T(8,128)(2,1)S(1)}, bf16[2,256,512]{2,1,0:T(8,128)(2,1)S(1)}, u32[]{:S(2)}, u32[]{:S(2)}) %collective-permute-start.4) | collective-permute-done | bytes 524320 | tf_op jit(solution)/shard_map/ppermute | solution.py:531
  83.6 6.2 %collective-permute-start.5 = (bf16[2,256,512]{2,1,0:T(8,128)(2,1)S(1)}, bf16[2,256,512]{2,1,0:T(8,128)(2,1)S(1)}, u32[]{:S(2)}, u32[]{:S(2)}) collective-permute-start(bf16[2,256,512]{2,1,0:T(8,128)(2,1)S(1)} %collective-permute-done.4), channel_id=1, source_target_pairs={{0,0},{4,4},{8,16},{12,20},{16,8},{20,12},{24,24},{28,28},{1,1},{5... | collective-permute-start | bytes 1572872 | tf_op jit(solution)/shard_map/ppermute | solution.py:528
  89.8 2.3 %shard_map.56.coupling = bf16[2,512,512]{2,1,0:T(8,128)(2,1)S(1)} custom-call(s32[20]{0:T(128)S(1)} %stack.103.info, bf16[4,64,512]{2,1,0:T(8,128)(2,1)S(1)} %pad_maximum_fusion.1.own, bf16[4,64,512]{2,1,0:T(8,128)(2,1)S(1)} %collective-permute-done.16.first, bf16[4,64,512]{2,1,0:T(8,128)(2,1)S(1)} %collective-permute-done.17.second, ...), custom_call_target="tpu_custom_call" | custom-call | tf_op jit(solution)/shard_map/pallas_call | solution.py:518
  92.1 2.7 %collective-permute-done.11.y3 = bf16[2,256,512]{2,1,0:T(8,128)(2,1)S(1)} collective-permute-done((bf16[2,256,512]{2,1,0:T(8,128)(2,1)S(1)}, bf16[2,256,512]{2,1,0:T(8,128)(2,1)S(1)}, u32[]{:S(2)}, u32[]{:S(2)}) %collective-permute-start.11) | collective-permute-done | bytes 524320 | tf_op jit(solution)/shard_map/ppermute | solution.py:531
  94.8 9.2 %collective-permute-done.9.y1 = bf16[2,256,512]{2,1,0:T(8,128)(2,1)S(1)} collective-permute-done((bf16[2,256,512]{2,1,0:T(8,128)(2,1)S(1)}, bf16[2,256,512]{2,1,0:T(8,128)(2,1)S(1)}, u32[]{:S(2)}, u32[]{:S(2)}) %collective-permute-start.9) | collective-permute-done | bytes 524320 | tf_op jit(solution)/shard_map/ppermute | solution.py:531
  106.1 8.0 %collective-permute-done.23.incoming = bf16[2,512,512]{2,1,0:T(8,128)(2,1)S(1)} collective-permute-done((bf16[2,512,512]{2,1,0:T(8,128)(2,1)S(1)}, bf16[2,512,512]{2,1,0:T(8,128)(2,1)S(1)}, u32[]{:S(2)}, u32[]{:S(2)}) %collective-permute-start.23) | collective-permute-done | bytes 1048608 | tf_op jit(solution)/shard_map/ppermute | solution.py:572
  114.1 11.1 %shard_map.59 = (bf16[2,2,512,512]{3,2,1,0:T(8,128)(2,1)S(1)}, bf16[2,512,512]{2,1,0:T(8,128)(2,1)S(1)}) custom-call(s32[20]{0:T(128)S(1)} %stack.103.info, bf16[2,256,512]{2,1,0:T(8,128)(2,1)S(1)} %collective-permute-done.3.x0, bf16[2,256,512]{2,1,0:T(8,128)(2,1)S(1)} %collective-permute-done.5.x1, bf16[2,256,512]{2,1,0:T(8,128)(2,1)S(1)} %collective-permute-done.6.x2, ...), custom_call_target="tpu_custom_call" | custom-call | flops 6442450944 | bytes 8388608 | tf_op jit(solution)/shard_map/pallas_call | solution.py:573
  126.5 2.2 %collective-permute-done.24.incoming = bf16[2,512,512]{2,1,0:T(8,128)(2,1)S(1)} collective-permute-done((bf16[2,512,512]{2,1,0:T(8,128)(2,1)S(1)}, bf16[2,512,512]{2,1,0:T(8,128)(2,1)S(1)}, u32[]{:S(2)}, u32[]{:S(2)}) %collective-permute-start.24) | collective-permute-done | bytes 1048608 | tf_op jit(solution)/shard_map/ppermute | solution.py:597
  129.8 10.7 %collective-permute-start.25 = (bf16[2,256,512]{2,1,0:T(8,128)(2,1)S(1)}, bf16[2,256,512]{2,1,0:T(8,128)(2,1)S(1)}, u32[]{:S(2)}, u32[]{:S(2)}) collective-permute-start(bf16[2,256,512]{2,1,0:T(8,128)(2,1)S(1)} %get-tuple-element.29), channel_id=1, source_target_pairs={{0,0},{4,4},{16,8},{20,12},{8,16},{12,20},{24,24},{28,28},{1,1},{5... | collective-permute-start | bytes 1572872 | tf_op jit(solution)/shard_map/ppermute | solution.py:620
  140.6 2.7 %collective-permute-start.28 = (bf16[2,256,512]{2,1,0:T(8,128)(2,1)S(1)}, bf16[2,256,512]{2,1,0:T(8,128)(2,1)S(1)}, u32[]{:S(2)}, u32[]{:S(2)}) collective-permute-start(bf16[2,256,512]{2,1,0:T(8,128)(2,1)S(1)} %get-tuple-element.32), channel_id=1, source_target_pairs={{20,0},{16,4},{4,8},{0,12},{28,16},{24,20},{12,24},{8,28},{21,1},{... | collective-permute-start | bytes 1572872 | tf_op jit(solution)/shard_map/ppermute | solution.py:620
  143.4 4.0 %collective-permute-done.25.rest_0_ = bf16[2,256,512]{2,1,0:T(8,128)(2,1)S(1)} collective-permute-done((bf16[2,256,512]{2,1,0:T(8,128)(2,1)S(1)}, bf16[2,256,512]{2,1,0:T(8,128)(2,1)S(1)}, u32[]{:S(2)}, u32[]{:S(2)}) %collective-permute-start.25) | collective-permute-done | bytes 524320 | tf_op jit(solution)/shard_map/ppermute | solution.py:620
  147.4 5.6 %collective-permute-done.26.rest_1_ = bf16[2,256,512]{2,1,0:T(8,128)(2,1)S(1)} collective-permute-done((bf16[2,256,512]{2,1,0:T(8,128)(2,1)S(1)}, bf16[2,256,512]{2,1,0:T(8,128)(2,1)S(1)}, u32[]{:S(2)}, u32[]{:S(2)}) %collective-permute-start.26) | collective-permute-done | bytes 524320 | tf_op jit(solution)/shard_map/ppermute | solution.py:620
  153.0 4.9 %collective-permute-done.27.rest_2_ = bf16[2,256,512]{2,1,0:T(8,128)(2,1)S(1)} collective-permute-done((bf16[2,256,512]{2,1,0:T(8,128)(2,1)S(1)}, bf16[2,256,512]{2,1,0:T(8,128)(2,1)S(1)}, u32[]{:S(2)}, u32[]{:S(2)}) %collective-permute-start.27) | collective-permute-done | bytes 524320 | tf_op jit(solution)/shard_map/ppermute | solution.py:620
  157.9 5.6 %collective-permute-done.28.rest_3_ = bf16[2,256,512]{2,1,0:T(8,128)(2,1)S(1)} collective-permute-done((bf16[2,256,512]{2,1,0:T(8,128)(2,1)S(1)}, bf16[2,256,512]{2,1,0:T(8,128)(2,1)S(1)}, u32[]{:S(2)}, u32[]{:S(2)}) %collective-permute-start.28) | collective-permute-done | bytes 524320 | tf_op jit(solution)/shard_map/ppermute | solution.py:620
  163.5 2.2 %shard_map.61 = bf16[2,256,2048]{2,1,0:T(8,128)(2,1)} custom-call(s32[4]{0:T(128)S(1)} %pad_add_fusion.place, bf16[2,256,512]{2,1,0:T(8,128)(2,1)S(1)} %collective-permute-done.25.rest_0_, bf16[2,256,512]{2,1,0:T(8,128)(2,1)S(1)} %collective-permute-done.26.rest_1_, bf16[2,256,512]{2,1,0:T(8,128)(2,1)S(1)} %collective-permute-done.27.rest_2_, ...), custom_call_target="tpu_custom_call" | custom-call | tf_op jit(solution)/shard_map/pallas_call | solution.py:622
  (47 shorter events, 14.4 us)
Async XLA Ops:
  0.0 1.0 copy-start
  0.0 38.1 %copy-start.3 = (s32[16]{0:T(128)S(1)}, s32[16]{0:T(128)}, u32[]{:S(2)}) copy-start(s32[16]{0:T(128)} %param.6) | copy-start | bytes 196
  1.0 8.6 %collective-permute-start.15 = (bf16[64,512]{1,0:T(8,128)(2,1)S(1)}, bf16[64,512]{1,0:T(8,128)(2,1)S(1)}, u32[]{:S(2)}, u32[]{:S(2)}) collective-permute-start(bf16[64,512]{1,0:T(8,128)(2,1)S(1)} %dynamic-slice_bitcast_fusion), channel_id=1, source_target_pairs={{0,20},{4,16},{8,4},{12,0},{16,28},{20,24},{24,12},{28,8},{1,21},{... | collective-permute-start | bytes 196616 | tf_op jit(solution)/shard_map/ppermute | solution.py:517
  4.6 19.8 %collective-permute-start.2 = (bf16[4,64,512]{2,1,0:T(8,128)(2,1)S(1)}, bf16[4,64,512]{2,1,0:T(8,128)(2,1)S(1)}, u32[]{:S(2)}, u32[]{:S(2)}) collective-permute-start(bf16[4,64,512]{2,1,0:T(8,128)(2,1)S(1)} %pad_maximum_fusion.own), channel_id=1, source_target_pairs={{0,3},{1,0},{2,1},{3,2},{4,7},{5,4},{6,5},{7,6},{8,11},{9,8},{10,9... | collective-permute-start | bytes 786440 | tf_op jit(solution)/shard_map/ppermute | solution.py:484
  8.0 21.1 %collective-permute-start.1 = (bf16[4,64,512]{2,1,0:T(8,128)(2,1)S(1)}, bf16[4,64,512]{2,1,0:T(8,128)(2,1)S(1)}, u32[]{:S(2)}, u32[]{:S(2)}) collective-permute-start(bf16[4,64,512]{2,1,0:T(8,128)(2,1)S(1)} %pad_maximum_fusion.own), channel_id=1, source_target_pairs={{0,2},{1,3},{2,0},{3,1},{4,6},{5,7},{6,4},{7,5},{8,10},{9,11},{10,... | collective-permute-start | bytes 786440 | tf_op jit(solution)/shard_map/ppermute | solution.py:484
  8.0 5.3 %collective-permute-start.14 = (bf16[64,512]{1,0:T(8,128)(2,1)S(1)}, bf16[64,512]{1,0:T(8,128)(2,1)S(1)}, u32[]{:S(2)}, u32[]{:S(2)}) collective-permute-start(bf16[64,512]{1,0:T(8,128)(2,1)S(1)} %dynamic-slice_bitcast_fusion), channel_id=1, source_target_pairs={{0,16},{4,20},{8,0},{12,4},{16,24},{20,28},{24,8},{28,12},{1,17},{... | collective-permute-start | bytes 196616 | tf_op jit(solution)/shard_map/ppermute | solution.py:517
  9.6 4.6 %collective-permute-start.13 = (bf16[64,512]{1,0:T(8,128)(2,1)S(1)}, bf16[64,512]{1,0:T(8,128)(2,1)S(1)}, u32[]{:S(2)}, u32[]{:S(2)}) collective-permute-start(bf16[64,512]{1,0:T(8,128)(2,1)S(1)} %dynamic-slice_bitcast_fusion), channel_id=1, source_target_pairs={{0,4},{4,0},{8,20},{12,16},{16,12},{20,8},{24,28},{28,24},{1,5},{5... | collective-permute-start | bytes 196616 | tf_op jit(solution)/shard_map/ppermute | solution.py:517
  9.6 5.6 %collective-permute-start.12 = (bf16[64,512]{1,0:T(8,128)(2,1)S(1)}, bf16[64,512]{1,0:T(8,128)(2,1)S(1)}, u32[]{:S(2)}, u32[]{:S(2)}) collective-permute-start(bf16[64,512]{1,0:T(8,128)(2,1)S(1)} %dynamic-slice_bitcast_fusion), channel_id=1, source_target_pairs={{0,0},{4,4},{8,16},{12,20},{16,8},{20,12},{24,24},{28,28},{1,1},{5... | collective-permute-start | bytes 196616 | tf_op jit(solution)/shard_map/ppermute | solution.py:517
  13.2 19.9 %collective-permute-start = (bf16[4,64,512]{2,1,0:T(8,128)(2,1)S(1)}, bf16[4,64,512]{2,1,0:T(8,128)(2,1)S(1)}, u32[]{:S(2)}, u32[]{:S(2)}) collective-permute-start(bf16[4,64,512]{2,1,0:T(8,128)(2,1)S(1)} %pad_maximum_fusion.own), channel_id=1, source_target_pairs={{0,1},{1,2},{2,3},{3,0},{4,5},{5,6},{6,7},{7,4},{8,9},{9,10},{10,1... | collective-permute-start | bytes 786440 | tf_op jit(solution)/shard_map/ppermute | solution.py:484
  15.2 22.9 %collective-permute-start.18 = (bf16[4,64,512]{2,1,0:T(8,128)(2,1)S(1)}, bf16[4,64,512]{2,1,0:T(8,128)(2,1)S(1)}, u32[]{:S(2)}, u32[]{:S(2)}) collective-permute-start(bf16[4,64,512]{2,1,0:T(8,128)(2,1)S(1)} %pad_maximum_fusion.1.own), channel_id=1, source_target_pairs={{0,3},{1,0},{2,1},{3,2},{4,7},{5,4},{6,5},{7,6},{8,11},{9,8},{10,9... | collective-permute-start | bytes 786440 | tf_op jit(solution)/shard_map/ppermute | solution.py:484
  16.6 1.6 copy-start.1
  21.1 36.5 %collective-permute-start.19 = (bf16[2,256,512]{2,1,0:T(8,128)(2,1)}, bf16[2,256,512]{2,1,0:T(8,128)(2,1)S(1)}, u32[]{:S(2)}, u32[]{:S(2)}) collective-permute-start(bf16[2,256,512]{2,1,0:T(8,128)(2,1)} %get-tuple-element.21), channel_id=1, source_target_pairs={{0,0},{4,4},{8,16},{12,20},{16,8},{20,12},{24,24},{28,28},{1,1},{5... | collective-permute-start | bytes 1572872 | tf_op jit(solution)/shard_map/ppermute | solution.py:503
  24.4 35.3 %collective-permute-start.20 = (bf16[2,256,512]{2,1,0:T(8,128)(2,1)}, bf16[2,256,512]{2,1,0:T(8,128)(2,1)S(1)}, u32[]{:S(2)}, u32[]{:S(2)}) collective-permute-start(bf16[2,256,512]{2,1,0:T(8,128)(2,1)} %get-tuple-element.22), channel_id=1, source_target_pairs={{0,4},{4,0},{8,20},{12,16},{16,12},{20,8},{24,28},{28,24},{1,5},{5... | collective-permute-start | bytes 1572872 | tf_op jit(solution)/shard_map/ppermute | solution.py:503
  29.0 31.9 %collective-permute-start.21 = (bf16[2,256,512]{2,1,0:T(8,128)(2,1)}, bf16[2,256,512]{2,1,0:T(8,128)(2,1)}, u32[]{:S(2)}, u32[]{:S(2)}) collective-permute-start(bf16[2,256,512]{2,1,0:T(8,128)(2,1)} %get-tuple-element.23), channel_id=1, source_target_pairs={{0,16},{4,20},{8,0},{12,4},{16,24},{20,28},{24,8},{28,12},{1,17},{... | collective-permute-start | bytes 1572872 | tf_op jit(solution)/shard_map/ppermute | solution.py:503
  33.1 22.8 %collective-permute-start.17 = (bf16[4,64,512]{2,1,0:T(8,128)(2,1)S(1)}, bf16[4,64,512]{2,1,0:T(8,128)(2,1)S(1)}, u32[]{:S(2)}, u32[]{:S(2)}) collective-permute-start(bf16[4,64,512]{2,1,0:T(8,128)(2,1)S(1)} %pad_maximum_fusion.1.own), channel_id=1, source_target_pairs={{0,2},{1,3},{2,0},{3,1},{4,6},{5,7},{6,4},{7,5},{8,10},{9,11},{10,... | collective-permute-start | bytes 786440 | tf_op jit(solution)/shard_map/ppermute | solution.py:484
  38.1 18.6 %collective-permute-start.16 = (bf16[4,64,512]{2,1,0:T(8,128)(2,1)S(1)}, bf16[4,64,512]{2,1,0:T(8,128)(2,1)S(1)}, u32[]{:S(2)}, u32[]{:S(2)}) collective-permute-start(bf16[4,64,512]{2,1,0:T(8,128)(2,1)S(1)} %pad_maximum_fusion.1.own), channel_id=1, source_target_pairs={{0,1},{1,2},{2,3},{3,0},{4,5},{5,6},{6,7},{7,4},{8,9},{9,10},{10,1... | collective-permute-start | bytes 786440 | tf_op jit(solution)/shard_map/ppermute | solution.py:484
  55.9 17.9 %collective-permute-start.22 = (bf16[2,256,512]{2,1,0:T(8,128)(2,1)}, bf16[2,256,512]{2,1,0:T(8,128)(2,1)S(1)}, u32[]{:S(2)}, u32[]{:S(2)}) collective-permute-start(bf16[2,256,512]{2,1,0:T(8,128)(2,1)} %copy-done.2), channel_id=1, source_target_pairs={{0,20},{4,16},{8,4},{12,0},{16,28},{20,24},{24,12},{28,8},{1,21},{... | collective-permute-start | bytes 1572872 | tf_op jit(solution)/shard_map/ppermute | solution.py:503
  56.7 19.2 %collective-permute-start.10 = (bf16[2,256,512]{2,1,0:T(8,128)(2,1)S(1)}, bf16[2,256,512]{2,1,0:T(8,128)(2,1)S(1)}, u32[]{:S(2)}, u32[]{:S(2)}) collective-permute-start(bf16[2,256,512]{2,1,0:T(8,128)(2,1)S(1)} %get-tuple-element.20), channel_id=1, source_target_pairs={{0,16},{4,20},{8,0},{12,4},{16,24},{20,28},{24,8},{28,12},{1,17},{... | collective-permute-start | bytes 1572872 | tf_op jit(solution)/shard_map/ppermute | solution.py:528
  57.5 19.8 %collective-permute-start.8 = (bf16[2,256,512]{2,1,0:T(8,128)(2,1)S(1)}, bf16[2,256,512]{2,1,0:T(8,128)(2,1)S(1)}, u32[]{:S(2)}, u32[]{:S(2)}) collective-permute-start(bf16[2,256,512]{2,1,0:T(8,128)(2,1)S(1)} %get-tuple-element.20), channel_id=1, source_target_pairs={{0,0},{4,4},{8,16},{12,20},{16,8},{20,12},{24,24},{28,28},{1,1},{5... | collective-permute-start | bytes 1572872 | tf_op jit(solution)/shard_map/ppermute | solution.py:528
  59.6 23.9 %collective-permute-start.4 = (bf16[2,256,512]{2,1,0:T(8,128)(2,1)S(1)}, bf16[2,256,512]{2,1,0:T(8,128)(2,1)S(1)}, u32[]{:S(2)}, u32[]{:S(2)}) collective-permute-start(bf16[2,256,512]{2,1,0:T(8,128)(2,1)S(1)} %get-tuple-element.19), channel_id=1, source_target_pairs={{0,4},{4,0},{1,5},{5,1},{2,6},{6,2},{3,7},{7,3},{8,12},{12,8},{9,1... | collective-permute-start | bytes 1572872 | tf_op jit(solution)/shard_map/ppermute | solution.py:531
  60.9 22.6 %collective-permute-start.6 = (bf16[2,256,512]{2,1,0:T(8,128)(2,1)S(1)}, bf16[2,256,512]{2,1,0:T(8,128)(2,1)S(1)}, u32[]{:S(2)}, u32[]{:S(2)}) collective-permute-start(bf16[2,256,512]{2,1,0:T(8,128)(2,1)S(1)} %get-tuple-element.19), channel_id=1, source_target_pairs={{0,16},{4,20},{8,0},{12,4},{16,24},{20,28},{24,8},{28,12},{1,17},{... | collective-permute-start | bytes 1572872 | tf_op jit(solution)/shard_map/ppermute | solution.py:528
  73.8 18.3 %collective-permute-start.3 = (bf16[2,256,512]{2,1,0:T(8,128)(2,1)S(1)}, bf16[2,256,512]{2,1,0:T(8,128)(2,1)S(1)}, u32[]{:S(2)}, u32[]{:S(2)}) collective-permute-start(bf16[2,256,512]{2,1,0:T(8,128)(2,1)S(1)} %get-tuple-element.19), channel_id=1, source_target_pairs={{0,0},{4,4},{8,16},{12,20},{16,8},{20,12},{24,24},{28,28},{1,1},{5... | collective-permute-start | bytes 1572872 | tf_op jit(solution)/shard_map/ppermute | solution.py:528
  75.9 18.9 %collective-permute-start.11 = (bf16[2,256,512]{2,1,0:T(8,128)(2,1)S(1)}, bf16[2,256,512]{2,1,0:T(8,128)(2,1)S(1)}, u32[]{:S(2)}, u32[]{:S(2)}) collective-permute-start(bf16[2,256,512]{2,1,0:T(8,128)(2,1)S(1)} %collective-permute-done.10.y2), channel_id=1, source_target_pairs={{0,4},{4,0},{1,5},{5,1},{2,6},{6,2},{3,7},{7,3},{8,12},{12,8},{9,1... | collective-permute-start | bytes 1572872 | tf_op jit(solution)/shard_map/ppermute | solution.py:531
  77.4 26.6 %collective-permute-start.9 = (bf16[2,256,512]{2,1,0:T(8,128)(2,1)S(1)}, bf16[2,256,512]{2,1,0:T(8,128)(2,1)S(1)}, u32[]{:S(2)}, u32[]{:S(2)}) collective-permute-start(bf16[2,256,512]{2,1,0:T(8,128)(2,1)S(1)} %collective-permute-done.8.y0), channel_id=1, source_target_pairs={{0,4},{4,0},{1,5},{5,1},{2,6},{6,2},{3,7},{7,3},{8,12},{12,8},{9,1... | collective-permute-start | bytes 1572872 | tf_op jit(solution)/shard_map/ppermute | solution.py:531
  83.6 20.4 %collective-permute-start.7 = (bf16[2,256,512]{2,1,0:T(8,128)(2,1)S(1)}, bf16[2,256,512]{2,1,0:T(8,128)(2,1)S(1)}, u32[]{:S(2)}, u32[]{:S(2)}) collective-permute-start(bf16[2,256,512]{2,1,0:T(8,128)(2,1)S(1)} %collective-permute-done.4), channel_id=1, source_target_pairs={{0,16},{4,20},{8,0},{12,4},{16,24},{20,28},{24,8},{28,12},{1,17},{... | collective-permute-start | bytes 1572872 | tf_op jit(solution)/shard_map/ppermute | solution.py:528
  83.6 20.4 %collective-permute-start.5 = (bf16[2,256,512]{2,1,0:T(8,128)(2,1)S(1)}, bf16[2,256,512]{2,1,0:T(8,128)(2,1)S(1)}, u32[]{:S(2)}, u32[]{:S(2)}) collective-permute-start(bf16[2,256,512]{2,1,0:T(8,128)(2,1)S(1)} %collective-permute-done.4), channel_id=1, source_target_pairs={{0,0},{4,4},{8,16},{12,20},{16,8},{20,12},{24,24},{28,28},{1,1},{5... | collective-permute-start | bytes 1572872 | tf_op jit(solution)/shard_map/ppermute | solution.py:528
  104.8 9.3 %collective-permute-start.23 = (bf16[2,512,512]{2,1,0:T(8,128)(2,1)S(1)}, bf16[2,512,512]{2,1,0:T(8,128)(2,1)S(1)}, u32[]{:S(2)}, u32[]{:S(2)}) collective-permute-start(bf16[2,512,512]{2,1,0:T(8,128)(2,1)S(1)} %get-tuple-element.26.w_high), channel_id=1, source_target_pairs={{0,8},{16,24},{1,9},{17,25},{2,10},{18,26},{3,11},{19,27},{4,12},{... | collective-permute-start | bytes 3145736 | tf_op jit(solution)/shard_map/ppermute | solution.py:572
  125.2 3.6 %collective-permute-start.24 = (bf16[2,512,512]{2,1,0:T(8,128)(2,1)S(1)}, bf16[2,512,512]{2,1,0:T(8,128)(2,1)S(1)}, u32[]{:S(2)}, u32[]{:S(2)}) collective-permute-start(bf16[2,512,512]{2,1,0:T(8,128)(2,1)S(1)} %get-tuple-element.27), channel_id=1, source_target_pairs={{8,0},{24,16},{9,1},{25,17},{10,2},{26,18},{11,3},{27,19},{12,4},{... | collective-permute-start | bytes 3145736 | tf_op jit(solution)/shard_map/ppermute | solution.py:597
  129.8 17.6 %collective-permute-start.25 = (bf16[2,256,512]{2,1,0:T(8,128)(2,1)S(1)}, bf16[2,256,512]{2,1,0:T(8,128)(2,1)S(1)}, u32[]{:S(2)}, u32[]{:S(2)}) collective-permute-start(bf16[2,256,512]{2,1,0:T(8,128)(2,1)S(1)} %get-tuple-element.29), channel_id=1, source_target_pairs={{0,0},{4,4},{16,8},{20,12},{8,16},{12,20},{24,24},{28,28},{1,1},{5... | collective-permute-start | bytes 1572872 | tf_op jit(solution)/shard_map/ppermute | solution.py:620
  140.5 12.5 %collective-permute-start.26 = (bf16[2,256,512]{2,1,0:T(8,128)(2,1)S(1)}, bf16[2,256,512]{2,1,0:T(8,128)(2,1)S(1)}, u32[]{:S(2)}, u32[]{:S(2)}) collective-permute-start(bf16[2,256,512]{2,1,0:T(8,128)(2,1)S(1)} %get-tuple-element.30), channel_id=1, source_target_pairs={{4,0},{0,4},{20,8},{16,12},{12,16},{8,20},{28,24},{24,28},{5,1},{1... | collective-permute-start | bytes 1572872 | tf_op jit(solution)/shard_map/ppermute | solution.py:620
  140.6 17.3 %collective-permute-start.27 = (bf16[2,256,512]{2,1,0:T(8,128)(2,1)S(1)}, bf16[2,256,512]{2,1,0:T(8,128)(2,1)S(1)}, u32[]{:S(2)}, u32[]{:S(2)}) collective-permute-start(bf16[2,256,512]{2,1,0:T(8,128)(2,1)S(1)} %get-tuple-element.31), channel_id=1, source_target_pairs={{16,0},{20,4},{0,8},{4,12},{24,16},{28,20},{8,24},{12,28},{17,1},{... | collective-permute-start | bytes 1572872 | tf_op jit(solution)/shard_map/ppermute | solution.py:620
  140.6 22.9 %collective-permute-start.28 = (bf16[2,256,512]{2,1,0:T(8,128)(2,1)S(1)}, bf16[2,256,512]{2,1,0:T(8,128)(2,1)S(1)}, u32[]{:S(2)}, u32[]{:S(2)}) collective-permute-start(bf16[2,256,512]{2,1,0:T(8,128)(2,1)S(1)} %get-tuple-element.32), channel_id=1, source_target_pairs={{20,0},{16,4},{4,8},{0,12},{28,16},{24,20},{12,24},{8,28},{21,1},{... | collective-permute-start | bytes 1572872 | tf_op jit(solution)/shard_map/ppermute | solution.py:620
  (1 other events, 0.8 us)

commit v3 on v2

--- a/solution.py
+++ b/solution.py
@@ -161,8 +161,8 @@
     return [slice(first, first + step) for first in range(0, order, step)]
 
 
-def pack_kernel(place, field, *rest):
-    pieces, sems = rest[:-1], rest[-1]
+def pack_kernel(place, field, coupling, *rest):
+    pieces, own_rows, sems = rest[:-2], rest[-2], rest[-1]
     copies = []
     for index, piece in enumerate(pieces):
         width = piece.shape[2]
@@ -170,6 +170,9 @@
         copies.append(
             pltpu.make_async_copy(field.at[:, :, pl.ds(offset, width)], piece, sems.at[index])
         )
+    height = own_rows.shape[0]
+    rows = pl.ds(pl.multiple_of(place[len(pieces)] * height, height), height)
+    copies.append(pltpu.make_async_copy(coupling.at[rows], own_rows, sems.at[len(pieces)]))
     start_all(copies)
     wait_all(copies)
 
@@ -187,7 +190,8 @@
     wait_all(copies)
 
 
-def stack_kernel(info, own, first, second, third, x_column, y_column, sems):
+def stack_kernel(info, own, first, second, third, c0, c1, c2, c3, x_column, y_column, rows_held,
+                 sems, csems):
     height = own.shape[1]
     copies = []
     for turn, block in enumerate((own, first, second, third)):
@@ -198,6 +202,8 @@
                     block.at[pl.ds(2 * which, 2)], column.at[:, rows, :], sems.at[turn, which]
                 )
             )
+    for index, rows_of in enumerate((c0, c1, c2, c3)):
+        copies.append(pltpu.make_async_copy(rows_of, rows_held.at[index], csems.at[index]))
     start_all(copies)
     wait_all(copies)
 
@@ -220,6 +226,10 @@
     wait_all(copies)
 
 
+def halves(*pairs):
+    return [pair.at[half] for pair in pairs for half in range(2)]
+
+
 class Factors:
     def __init__(self, info, columns, held, sems):
         self.order, self.held, self.sems, self.columns = held.shape[2], held, sems, columns
@@ -250,7 +260,7 @@
         turned = (((1,), (1,)), ((), ()))
         if fresh:
             self.ready(slot, 1)
-        for columns in row_chunks(order, 256):
+        for columns in row_chunks(order, 512):
             part = lax.dot_general(
                 beside[...], self.held[slot, 1, columns], turned, preferred_element_type=f32
             ).astype(bf16)
@@ -263,7 +273,7 @@
         if fresh:
             self.ready(slot, 0)
         for plane in range(2):
-            for columns in row_chunks(order, 256):
+            for columns in row_chunks(order, 512):
                 along = slice(columns.start + plane * order, columns.stop + plane * order)
                 store(
                     plane,
@@ -290,13 +300,26 @@
     for plane in range(2):
         for rows in row_chunks(order, 128):
             values = rhs[slot, plane, rows].astype(f32)
-            if plane == 0:
-                row = lax.broadcasted_iota(jnp.int32, values.shape, 0) + rows.start
-                column = lax.broadcasted_iota(jnp.int32, values.shape, 1)
-                hit = (row == info[1]) & (column == info[2]) & (info[0] == slot)
-                values = values + jnp.where(hit, f32(source_amplitude), f32(0.0))
-            scaled = weights[slot, rows].astype(f32) * incoming(plane, rows)
+            scaled = weights[slot, rows].astype(f32) * incoming(plane, rows, slice(None))
             put_beside(beside, plane, rows, values - scaled)
+
+    @pl.when(info[0] == slot)
+    def _():
+        tall, wide = 16, 128
+        top = pl.multiple_of(info[1] // tall * tall, tall)
+        left = pl.multiple_of(info[2] // wide * wide, wide)
+        rows, columns = pl.ds(top, tall), pl.ds(left, wide)
+        values = rhs[slot, 0, rows, columns].astype(f32)
+        row = lax.broadcasted_iota(jnp.int32, values.shape, 0) + top
+        column = lax.broadcasted_iota(jnp.int32, values.shape, 1) + left
+        hit = (row == info[1]) & (column == info[2])
+        values = values + jnp.where(hit, f32(source_amplitude), f32(0.0))
+        scaled = weights[slot, rows, columns].astype(f32) * incoming(0, rows, columns)
+        values = (values - scaled).astype(bf16)
+        beside[rows, columns] = values
+        lower = pl.ds(pl.multiple_of(order + top, tall), tall)
+        further = pl.ds(pl.multiple_of(order + left, wide), wide)
+        beside[lower, further] = values
 
 
 def sent_into(beside, weights, slot, field):
@@ -332,24 +355,24 @@
     return copies
 
 
-def first_kernel(info, x0, x1, x2, x3, y0, y1, y2, y3, coupling, p0, p1, p2, p3, w_low, w_high,
+def first_kernel(info, x0, x1, y0, y1, y2, y3, coupling, p0, p1, p2, p3, w_low, w_high,
                  held, weights, rhs, beside, below, sems, fsems):
     @pl.when(info[info_member] == 0)
     def _():
         early = rhs_copies(info, (p0, p1, p2, p3), rhs, sems)
         early.append(pltpu.make_async_copy(coupling, weights, sems.at[4]))
         start_all(early)
-        factors = Factors(info, ((x0, x1, x2, x3), (y0, y1, y2, y3)), held, fsems)
+        factors = Factors(info, (halves(x0, x1), (y0, y1, y2, y3)), held, fsems)
         wait_all(early)
-        reduce_into(beside, rhs, info, 0, weights, lambda plane, rows: f32(0.0))
+        reduce_into(beside, rhs, info, 0, weights, lambda *where: f32(0.0))
         factors.apply(0, beside, below, round_into(w_low), True)
         reduce_into(
-            beside, rhs, info, 1, weights, lambda plane, rows: w_low[plane, rows].astype(f32)
+            beside, rhs, info, 1, weights, lambda *where: w_low[where].astype(f32)
         )
         factors.apply(1, beside, below, round_into(w_high), True)
 
 
-def last_kernel(info, x0, x1, x2, x3, y0, y1, y2, y3, coupling, p0, p1, p2, p3, incoming, field,
+def last_kernel(info, x0, x1, y0, y1, y2, y3, coupling, p0, p1, p2, p3, incoming, field,
                 sent, held, weights, rhs, arrived, kept, beside, below, sems, fsems, osems):
     @pl.when(info[info_member] == 1)
     def _():
@@ -357,16 +380,16 @@
         early.append(pltpu.make_async_copy(coupling, weights, sems.at[4]))
         early.append(pltpu.make_async_copy(incoming, arrived, sems.at[5]))
         start_all(early)
-        factors = Factors(info, ((x0, x1, x2, x3), (y0, y1, y2, y3)), held, fsems)
+        factors = Factors(info, (halves(x0, x1), (y0, y1, y2, y3)), held, fsems)
         wait_all(early)
         order = beside.shape[0] // 2
         reduce_into(
-            beside, rhs, info, 0, weights, lambda plane, rows: arrived[plane, rows].astype(f32)
+            beside, rhs, info, 0, weights, lambda *where: arrived[where].astype(f32)
         )
         w_low, w_high = kept.at[0], kept.at[1]
         factors.apply(0, beside, below, round_into(w_low), True)
         reduce_into(
-            beside, rhs, info, 1, weights, lambda plane, rows: w_low[plane, rows].astype(f32)
+            beside, rhs, info, 1, weights, lambda *where: w_low[where].astype(f32)
         )
         factors.apply(1, beside, below, round_into(w_high), True)
         out_high = pltpu.make_async_copy(w_high, field.at[1], osems.at[1])
@@ -388,13 +411,13 @@
         out_low.wait()
 
 
-def back_kernel(info, x0, x1, x2, x3, y0, y1, y2, y3, coupling, w_low, w_high, incoming, field,
+def back_kernel(info, x0, x1, y0, y1, y2, y3, coupling, w_low, w_high, incoming, field,
                 p0, p1, p2, p3, held, weights, kept, arrived, beside, below, sems, fsems, osems):
     @pl.when(info[info_member] == 0)
     def _():
         early = [pltpu.make_async_copy(incoming, arrived, sems.at[0])]
         start_all(early)
-        factors = Factors(info, ((x0, x1, x2, x3), (y0, y1, y2, y3)), held, fsems)
+        factors = Factors(info, (halves(x0, x1), (y0, y1, y2, y3)), held, fsems)
         early += [
             pltpu.make_async_copy(coupling, weights, sems.at[1]),
             pltpu.make_async_copy(w_low, kept.at[0], sems.at[2]),
@@ -488,33 +511,44 @@
     shard = jnp.concatenate([x_factor[0], y_factor[0]], axis=0)
     shards = rotated(shard)
     sends_to = jnp.stack(
-        [((member + a) % 2) * px_count + (own_x + b) % px_count for a, b in rounds]
+        [((member + a) % 2) * px_count + (own_x + b) % px_count for a, b in rounds] + [own_y]
     ).astype(jnp.int32)
     piece_shape = jax.ShapeDtypeStruct((2, rows_here, order), bf16)
-    pieces = pl.pallas_call(
+    *pieces, own_rows = pl.pallas_call(
         pack_kernel,
-        out_shape=[piece_shape] * len(rounds),
-        in_specs=[in_smem, anywhere],
-        out_specs=[in_vmem] * len(rounds),
-        scratch_shapes=[pltpu.SemaphoreType.DMA((len(rounds),))],
+        out_shape=[piece_shape] * len(rounds) + [jax.ShapeDtypeStruct((height, order), bf16)],
+        in_specs=[in_smem, anywhere, anywhere],
+        out_specs=[in_vmem] * (len(rounds) + 1),
+        scratch_shapes=[pltpu.SemaphoreType.DMA((len(rounds) + 1,))],
         compiler_params=params,
-    )(sends_to, field)
+    )(sends_to, field, coupling[0])
     pieces = [
         lax.ppermute(piece, ("sec", "px"), pairs(a, b)) for piece, (a, b) in zip(pieces, rounds)
     ]
+    layer_rows = [lax.ppermute(own_rows, ("sec", "px"), pairs(a, b)) for a, b in rounds]
 
     column_shape = jax.ShapeDtypeStruct((2, rows_here, order), bf16)
-    x_column, y_column = pl.pallas_call(
+    x_column, y_column, rows_held = pl.pallas_call(
         stack_kernel,
-        out_shape=[column_shape] * 2,
-        in_specs=[in_smem] + [anywhere] * 4,
-        out_specs=[in_vmem] * 2,
-        scratch_shapes=[pltpu.SemaphoreType.DMA((4, 2))],
+        out_shape=[column_shape] * 2 + [jax.ShapeDtypeStruct((4, height, order), bf16)],
+        in_specs=[in_smem] + [anywhere] * 8,
+        out_specs=[in_vmem] * 3,
+        scratch_shapes=[pltpu.SemaphoreType.DMA((4, 2)), pltpu.SemaphoreType.DMA((4,))],
         compiler_params=params,
-    )(info, *shards)
-
-    own_weights = lax.dynamic_slice_in_dim(coupling[0], own_y * height, height)
-    own_weights = jnp.stack([lax.ppermute(own_weights, ("sec", "px"), pairs(a, b)) for a, b in rounds])
+    )(info, *shards, *layer_rows)
+
+    def across(block, a):
+        return lax.ppermute(block, ("sec", "px"), pairs(a, 0))
+
+    def aside(block):
+        return lax.ppermute(block, "px", [(y, (y + 1) % 2) for y in range(2)])
+
+    x_aside = aside(x_column)
+    y_near = [across(y_column, a) for a in range(2)]
+    y_far = [aside(block) for block in y_near]
+    x_both = jnp.stack([x_column, x_aside])
+    x_across = [across(x_both, a) for a in range(2)]
+    factors = x_across + [y_near[0], y_far[0], y_near[1], y_far[1]]
     weights = pl.pallas_call(
         weight_kernel,
         out_shape=jax.ShapeDtypeStruct((2, order, order), bf16),
@@ -522,22 +556,7 @@
         out_specs=in_vmem,
         scratch_shapes=[pltpu.SemaphoreType.DMA((4, 4))],
         compiler_params=params,
-    )(info, *rotated(own_weights))
-
-    def across(block, a):
-        return lax.ppermute(block, ("sec", "px"), pairs(a, 0))
-
-    def aside(block):
-        return lax.ppermute(block, "px", [(y, (y + 1) % 2) for y in range(2)])
-
-    x_aside = aside(x_column)
-    y_near = [across(y_column, a) for a in range(2)]
-    x_near = [across(x_column, a) for a in range(2)]
-    y_far = [aside(block) for block in y_near]
-    x_far = [across(x_aside, a) for a in range(2)]
-    factors = []
-    for near, far in ((x_near, x_far), (y_near, y_far)):
-        factors += [near[0], far[0], near[1], far[1]]
+    )(info, *rotated(rows_held))
 
     full_shape = jax.ShapeDtypeStruct((2, order, order), bf16)
     factor_scratch = pltpu.VMEM((2, 2, order, 2 * order), bf16)
@@ -551,7 +570,7 @@
     w_low, w_high = pl.pallas_call(
         first_kernel,
         out_shape=[full_shape] * 2,
-        in_specs=[in_smem] + [anywhere] * 13,
+        in_specs=[in_smem] + [anywhere] * 11,
         out_specs=[in_vmem] * 2,
         scratch_shapes=[
             factor_scratch,
@@ -573,7 +592,7 @@
     solved, sent = pl.pallas_call(
         last_kernel,
         out_shape=[jax.ShapeDtypeStruct((2, 2, order, order), bf16), full_shape],
-        in_specs=[in_smem] + [anywhere] * 14,
+        in_specs=[in_smem] + [anywhere] * 12,
         out_specs=[anywhere, in_vmem],
         scratch_shapes=[
             factor_scratch,
@@ -598,7 +617,7 @@
     results = pl.pallas_call(
         back_kernel,
         out_shape=[piece_shape] * len(rounds),
-        in_specs=[in_smem] + [anywhere] * 13,
+        in_specs=[in_smem] + [anywhere] * 11,
         out_specs=[anywhere] * len(rounds),
         scratch_shapes=[
             factor_scratch,

time: 168 us -> 166 us (0.988)
  the two profiles are of different devices: /device:TPU:1 before, /device:TPU:8 now
where the time goes in v3:
time: 166 us
  waiting for transfers between devices  93.7 us (56%)
  starting transfers between devices  42.8 us (26%)
  Pallas kernels  22.1 us (13%)
  local copies, waits for them, and re-layouts  3.31 us (2%)
  between operations  2.91 us (2%)
    ppermute x4, waiting for transfers between devices, on_device(): lax.ppermute(piece, ('sec', 'px'), pairs(a, b))  24 us
    ppermute x4, waiting for transfers between devices, on_device(): lax.ppermute(piece, ('sec', 'px'), back_pairs(a, b))  23.6 us
    ppermute x3, waiting for transfers between devices, aside(): return lax.ppermute(block, 'px', [(y, (y + 1) % 2) for y in range(2)])  12.9 us
    ppermute x1, waiting for transfers between devices, on_device(): incoming = lax.ppermute(sent, 'sec', down)  12.2 us
    ppermute x6, starting transfers between devices, rotated(): lax.ppermute(block, 'py', [(z, (z + turn) % py_count) for z in range(py_c...  12 us
    ppermute x6, waiting for transfers between devices, rotated(): lax.ppermute(block, 'py', [(z, (z + turn) % py_count) for z in range(py_c...  9.05 us
    ppermute x4, starting transfers between devices, on_device(): lax.ppermute(piece, ('sec', 'px'), back_pairs(a, b))  8.22 us
    ppermute x4, starting transfers between devices, on_device(): lax.ppermute(piece, ('sec', 'px'), pairs(a, b))  8 us
  transfers between devices with their start and end apart: 27, of which 15 were waited for; matrix products, arithmetic and copies ran while one was open for 1% of the time, Pallas kernels for 2%

profile of v3, /device:TPU:8, one launch (start us, length us, event | category | flops | bytes accessed | tf_op | source)
XLA Modules:
  0.0 165.9 jit_solution(17358529854430726351)
XLA Ops:
  1.1 3.0 %collective-permute-start.1 = (bf16[4,64,512]{2,1,0:T(8,128)(2,1)S(1)}, bf16[4,64,512]{2,1,0:T(8,128)(2,1)S(1)}, u32[]{:S(2)}, u32[]{:S(2)}) collective-permute-start(bf16[4,64,512]{2,1,0:T(8,128)(2,1)S(1)} %pad_maximum_fusion.1.own), channel_id=1, source_target_pairs={{0,2},{1,3},{2,0},{3,1},{4,6},{5,7},{6,4},{7,5},{8,10},{9,11},{10,... | collective-permute-start | bytes 786440 | tf_op jit(solution)/shard_map/ppermute | solution.py:507
  4.1 2.5 %collective-permute-start = (bf16[4,64,512]{2,1,0:T(8,128)(2,1)S(1)}, bf16[4,64,512]{2,1,0:T(8,128)(2,1)S(1)}, u32[]{:S(2)}, u32[]{:S(2)}) collective-permute-start(bf16[4,64,512]{2,1,0:T(8,128)(2,1)S(1)} %pad_maximum_fusion.1.own), channel_id=1, source_target_pairs={{0,1},{1,2},{2,3},{3,0},{4,5},{5,6},{6,7},{7,4},{8,9},{9,10},{10,1... | collective-permute-start | bytes 786440 | tf_op jit(solution)/shard_map/ppermute | solution.py:507
  6.7 1.6 copy-done
  10.2 2.5 %collective-permute-start.6 = (bf16[64,512]{1,0:T(8,128)(2,1)S(1)}, bf16[64,512]{1,0:T(8,128)(2,1)S(1)}, u32[]{:S(2)}, u32[]{:S(2)}) collective-permute-start(bf16[64,512]{1,0:T(8,128)(2,1)S(1)} %get-tuple-element.21), channel_id=1, source_target_pairs={{0,20},{4,16},{8,4},{12,0},{16,28},{20,24},{24,12},{28,8},{1,21},{... | collective-permute-start | bytes 196616 | tf_op jit(solution)/shard_map/ppermute | solution.py:528
  12.7 1.9 %collective-permute-done.6.c3 = bf16[64,512]{1,0:T(8,128)(2,1)S(1)} collective-permute-done((bf16[64,512]{1,0:T(8,128)(2,1)S(1)}, bf16[64,512]{1,0:T(8,128)(2,1)S(1)}, u32[]{:S(2)}, u32[]{:S(2)}) %collective-permute-start.6) | collective-permute-done | bytes 65568 | tf_op jit(solution)/shard_map/ppermute | solution.py:528
  19.6 1.9 %collective-permute-done.2.third = bf16[4,64,512]{2,1,0:T(8,128)(2,1)S(1)} collective-permute-done((bf16[4,64,512]{2,1,0:T(8,128)(2,1)S(1)}, bf16[4,64,512]{2,1,0:T(8,128)(2,1)S(1)}, u32[]{:S(2)}, u32[]{:S(2)}) %collective-permute-start.2) | collective-permute-done | bytes 262176 | tf_op jit(solution)/shard_map/ppermute | solution.py:507
  21.5 4.7 %collective-permute-done.first = bf16[4,64,512]{2,1,0:T(8,128)(2,1)S(1)} collective-permute-done((bf16[4,64,512]{2,1,0:T(8,128)(2,1)S(1)}, bf16[4,64,512]{2,1,0:T(8,128)(2,1)S(1)}, u32[]{:S(2)}, u32[]{:S(2)}) %collective-permute-start) | collective-permute-done | bytes 262176 | tf_op jit(solution)/shard_map/ppermute | solution.py:507
  26.3 1.7 %shard_map.56 = (bf16[2,256,512]{2,1,0:T(8,128)(2,1)S(1)}, bf16[2,256,512]{2,1,0:T(8,128)(2,1)S(1)}, bf16[4,64,512]{2,1,0:T(8,128)(2,1)S(1)}) custom-call(s32[20]{0:T(128)S(1)} %stack.101.info, bf16[4,64,512]{2,1,0:T(8,128)(2,1)S(1)} %pad_maximum_fusion.1.own, bf16[4,64,512]{2,1,0:T(8,128)(2,1)S(1)} %collective-permute-done.first, ...), custom_call_target="tpu_custom_call" | custom-call | tf_op jit(solution)/shard_map/pallas_call | solution.py:531
  28.0 1.6 collective-permute-start.7
  32.0 2.8 %collective-permute-start.15 = (bf16[4,64,512]{2,1,0:T(8,128)(2,1)S(1)}, bf16[4,64,512]{2,1,0:T(8,128)(2,1)S(1)}, u32[]{:S(2)}, u32[]{:S(2)}) collective-permute-start(bf16[4,64,512]{2,1,0:T(8,128)(2,1)S(1)} %get-tuple-element.24.own), channel_id=1, source_target_pairs={{0,2},{1,3},{2,0},{3,1},{4,6},{5,7},{6,4},{7,5},{8,10},{9,11},{10,... | collective-permute-start | bytes 786440 | tf_op jit(solution)/shard_map/ppermute | solution.py:507
  34.8 12.0 %collective-permute-done.7 = bf16[2,256,512]{2,1,0:T(8,128)(2,1)S(1)} collective-permute-done((bf16[2,256,512]{2,1,0:T(8,128)(2,1)S(1)}, bf16[2,256,512]{2,1,0:T(8,128)(2,1)S(1)}, u32[]{:S(2)}, u32[]{:S(2)}) %collective-permute-start.7) | collective-permute-done | bytes 524320 | tf_op jit(solution)/shard_map/ppermute | solution.py:544
  46.7 2.5 %collective-permute-start.14 = (bf16[4,64,512]{2,1,0:T(8,128)(2,1)S(1)}, bf16[4,64,512]{2,1,0:T(8,128)(2,1)S(1)}, u32[]{:S(2)}, u32[]{:S(2)}) collective-permute-start(bf16[4,64,512]{2,1,0:T(8,128)(2,1)S(1)} %get-tuple-element.24.own), channel_id=1, source_target_pairs={{0,1},{1,2},{2,3},{3,0},{4,5},{5,6},{6,7},{7,4},{8,9},{9,10},{10,1... | collective-permute-start | bytes 786440 | tf_op jit(solution)/shard_map/ppermute | solution.py:507
  49.3 3.3 %collective-permute-start.19 = (bf16[2,256,512]{2,1,0:T(8,128)(2,1)S(1)}, bf16[2,256,512]{2,1,0:T(8,128)(2,1)S(1)}, u32[]{:S(2)}, u32[]{:S(2)}) collective-permute-start(bf16[2,256,512]{2,1,0:T(8,128)(2,1)S(1)} %get-tuple-element.27), channel_id=1, source_target_pairs={{0,16},{4,20},{8,0},{12,4},{16,24},{20,28},{24,8},{28,12},{1,17},{... | collective-permute-start | bytes 1572872 | tf_op jit(solution)/shard_map/ppermute | solution.py:526
  52.7 2.3 %collective-permute-done.14.first = bf16[4,64,512]{2,1,0:T(8,128)(2,1)S(1)} collective-permute-done((bf16[4,64,512]{2,1,0:T(8,128)(2,1)S(1)}, bf16[4,64,512]{2,1,0:T(8,128)(2,1)S(1)}, u32[]{:S(2)}, u32[]{:S(2)}) %collective-permute-start.14) | collective-permute-done | bytes 262176 | tf_op jit(solution)/shard_map/ppermute | solution.py:507
  55.7 2.6 %collective-permute-start.9 = (bf16[2,2,256,512]{3,2,1,0:T(8,128)(2,1)S(1)}, bf16[2,2,256,512]{3,2,1,0:T(8,128)(2,1)S(1)}, u32[]{:S(2)}, u32[]{:S(2)}) collective-permute-start(bf16[2,2,256,512]{3,2,1,0:T(8,128)(2,1)S(1)} %pad_maximum_fusion), channel_id=1, source_target_pairs={{0,16},{4,20},{8,0},{12,4},{16,24},{20,28},{24,8},{28,12},{1,17},{... | collective-permute-start | bytes 3145736 | tf_op jit(solution)/shard_map/ppermute | solution.py:541
  59.8 3.4 %collective-permute-start.20 = (bf16[2,256,512]{2,1,0:T(8,128)(2,1)S(1)}, bf16[2,256,512]{2,1,0:T(8,128)(2,1)S(1)}, u32[]{:S(2)}, u32[]{:S(2)}) collective-permute-start(bf16[2,256,512]{2,1,0:T(8,128)(2,1)S(1)} %get-tuple-element.28), channel_id=1, source_target_pairs={{0,20},{4,16},{8,4},{12,0},{16,28},{20,24},{24,12},{28,8},{1,21},{... | collective-permute-start | bytes 1572872 | tf_op jit(solution)/shard_map/ppermute | solution.py:526
  63.2 7.8 %collective-permute-done.12.y2 = bf16[2,256,512]{2,1,0:T(8,128)(2,1)S(1)} collective-permute-done((bf16[2,256,512]{2,1,0:T(8,128)(2,1)S(1)}, bf16[2,256,512]{2,1,0:T(8,128)(2,1)S(1)}, u32[]{:S(2)}, u32[]{:S(2)}) %collective-permute-start.12) | collective-permute-done | bytes 524320 | tf_op jit(solution)/shard_map/ppermute | solution.py:541
  71.0 1.5 collective-permute-start.13
  73.1 2.3 %shard_map.57.coupling = bf16[2,512,512]{2,1,0:T(8,128)(2,1)S(1)} custom-call(s32[20]{0:T(128)S(1)} %stack.101.info, bf16[4,64,512]{2,1,0:T(8,128)(2,1)S(1)} %get-tuple-element.24.own, bf16[4,64,512]{2,1,0:T(8,128)(2,1)S(1)} %collective-permute-done.14.first, bf16[4,64,512]{2,1,0:T(8,128)(2,1)S(1)} %collective-permute-done.15.second, ...), custom_call_target="tpu_custom_call" | custom-call | tf_op jit(solution)/shard_map/pallas_call | solution.py:552
  75.4 23.3 %collective-permute-done.20.p3 = bf16[2,256,512]{2,1,0:T(8,128)(2,1)S(1)} collective-permute-done((bf16[2,256,512]{2,1,0:T(8,128)(2,1)S(1)}, bf16[2,256,512]{2,1,0:T(8,128)(2,1)S(1)}, u32[]{:S(2)}, u32[]{:S(2)}) %collective-permute-start.20) | collective-permute-done | bytes 524320 | tf_op jit(solution)/shard_map/ppermute | solution.py:526
  99.7 7.0 %shard_map.58 = (bf16[2,512,512]{2,1,0:T(8,128)(2,1)S(1)}, bf16[2,512,512]{2,1,0:T(8,128)(2,1)S(1)}) custom-call(s32[20]{0:T(128)S(1)} %stack.101.info, bf16[2,2,256,512]{3,2,1,0:T(8,128)(2,1)S(1)} %collective-permute-done.8.x0, bf16[2,2,256,512]{3,2,1,0:T(8,128)(2,1)S(1)} %collective-permute-done.9.x1, bf16[2,256,512]{2,1,0:T(8,128)(2,1)S(1)} %collective-permute-done.10.y0, ...), custom_call_target="tpu_custom_call" | custom-call | flops 4294967296 | bytes 8388608 | tf_op jit(solution)/shard_map/pallas_call | solution.py:570
  106.7 1.4 collective-permute-start.21
  108.0 2.2 %collective-permute-done.21.incoming = bf16[2,512,512]{2,1,0:T(8,128)(2,1)S(1)} collective-permute-done((bf16[2,512,512]{2,1,0:T(8,128)(2,1)S(1)}, bf16[2,512,512]{2,1,0:T(8,128)(2,1)S(1)}, u32[]{:S(2)}, u32[]{:S(2)}) %collective-permute-start.21) | collective-permute-done | bytes 1048608 | tf_op jit(solution)/shard_map/ppermute | solution.py:591
  111.2 1.3 collective-permute-start.22
  112.5 12.2 %collective-permute-done.22.incoming = bf16[2,512,512]{2,1,0:T(8,128)(2,1)S(1)} collective-permute-done((bf16[2,512,512]{2,1,0:T(8,128)(2,1)S(1)}, bf16[2,512,512]{2,1,0:T(8,128)(2,1)S(1)}, u32[]{:S(2)}, u32[]{:S(2)}) %collective-permute-start.22) | collective-permute-done | bytes 1048608 | tf_op jit(solution)/shard_map/ppermute | solution.py:616
  124.7 7.0 %shard_map.60 = (bf16[2,256,512]{2,1,0:T(8,128)(2,1)S(1)}, bf16[2,256,512]{2,1,0:T(8,128)(2,1)S(1)}, bf16[2,256,512]{2,1,0:T(8,128)(2,1)S(1)}, bf16[2,256,512]{2,1,0:T(8,128)(2,1)S(1)}) custom-call(s32[20]{0:T(128)S(1)} %stack.101.info, bf16[2,2,256,512]{3,2,1,0:T(8,128)(2,1)S(1)} %collective-permute-done.8.x0, ...), custom_call_target="tpu_custom_call" | custom-call | flops 4294967296 | bytes 8388608 | tf_op jit(solution)/shard_map/pallas_call | solution.py:617
  132.4 2.6 %collective-permute-start.24 = (bf16[2,256,512]{2,1,0:T(8,128)(2,1)S(1)}, bf16[2,256,512]{2,1,0:T(8,128)(2,1)S(1)}, u32[]{:S(2)}, u32[]{:S(2)}) collective-permute-start(bf16[2,256,512]{2,1,0:T(8,128)(2,1)S(1)} %get-tuple-element.34), channel_id=1, source_target_pairs={{4,0},{0,4},{20,8},{16,12},{12,16},{8,20},{28,24},{24,28},{5,1},{1... | collective-permute-start | bytes 1572872 | tf_op jit(solution)/shard_map/ppermute | solution.py:639
  135.0 4.7 %collective-permute-start.25 = (bf16[2,256,512]{2,1,0:T(8,128)(2,1)S(1)}, bf16[2,256,512]{2,1,0:T(8,128)(2,1)S(1)}, u32[]{:S(2)}, u32[]{:S(2)}) collective-permute-start(bf16[2,256,512]{2,1,0:T(8,128)(2,1)S(1)} %get-tuple-element.35), channel_id=1, source_target_pairs={{16,0},{20,4},{0,8},{4,12},{24,16},{28,20},{8,24},{12,28},{17,1},{... | collective-permute-start | bytes 1572872 | tf_op jit(solution)/shard_map/ppermute | solution.py:639
  139.9 2.2 %collective-permute-done.24.rest_1_ = bf16[2,256,512]{2,1,0:T(8,128)(2,1)S(1)} collective-permute-done((bf16[2,256,512]{2,1,0:T(8,128)(2,1)S(1)}, bf16[2,256,512]{2,1,0:T(8,128)(2,1)S(1)}, u32[]{:S(2)}, u32[]{:S(2)}) %collective-permute-start.24) | collective-permute-done | bytes 524320 | tf_op jit(solution)/shard_map/ppermute | solution.py:639
  142.1 14.6 %collective-permute-done.25.rest_2_ = bf16[2,256,512]{2,1,0:T(8,128)(2,1)S(1)} collective-permute-done((bf16[2,256,512]{2,1,0:T(8,128)(2,1)S(1)}, bf16[2,256,512]{2,1,0:T(8,128)(2,1)S(1)}, u32[]{:S(2)}, u32[]{:S(2)}) %collective-permute-start.25) | collective-permute-done | bytes 524320 | tf_op jit(solution)/shard_map/ppermute | solution.py:639
  156.7 6.8 %collective-permute-done.26.rest_3_ = bf16[2,256,512]{2,1,0:T(8,128)(2,1)S(1)} collective-permute-done((bf16[2,256,512]{2,1,0:T(8,128)(2,1)S(1)}, bf16[2,256,512]{2,1,0:T(8,128)(2,1)S(1)}, u32[]{:S(2)}, u32[]{:S(2)}) %collective-permute-start.26) | collective-permute-done | bytes 524320 | tf_op jit(solution)/shard_map/ppermute | solution.py:639
  163.5 2.2 %shard_map.61 = bf16[2,256,2048]{2,1,0:T(8,128)(2,1)} custom-call(s32[5]{0:T(128)S(1)} %stack.85.place, bf16[2,256,512]{2,1,0:T(8,128)(2,1)S(1)} %collective-permute-done.23.rest_0_, bf16[2,256,512]{2,1,0:T(8,128)(2,1)S(1)} %collective-permute-done.24.rest_1_, bf16[2,256,512]{2,1,0:T(8,128)(2,1)S(1)} %collective-permute-done.25.rest_2_, ...), custom_call_target="tpu_custom_call" | custom-call | tf_op jit(solution)/shard_map/pallas_call | solution.py:641
  (40 shorter events, 13.6 us)
Async XLA Ops:
  0.0 16.4 %copy-start.2 = (s32[16]{0:T(128)S(1)}, s32[16]{0:T(128)}, u32[]{:S(2)}) copy-start(s32[16]{0:T(128)} %param.6) | copy-start | bytes 196
  1.0 20.5 %collective-permute-start.2 = (bf16[4,64,512]{2,1,0:T(8,128)(2,1)S(1)}, bf16[4,64,512]{2,1,0:T(8,128)(2,1)S(1)}, u32[]{:S(2)}, u32[]{:S(2)}) collective-permute-start(bf16[4,64,512]{2,1,0:T(8,128)(2,1)S(1)} %pad_maximum_fusion.1.own), channel_id=1, source_target_pairs={{0,3},{1,0},{2,1},{3,2},{4,7},{5,4},{6,5},{7,6},{8,11},{9,8},{10,9... | collective-permute-start | bytes 786440 | tf_op jit(solution)/shard_map/ppermute | solution.py:507
  1.1 20.5 %collective-permute-start.1 = (bf16[4,64,512]{2,1,0:T(8,128)(2,1)S(1)}, bf16[4,64,512]{2,1,0:T(8,128)(2,1)S(1)}, u32[]{:S(2)}, u32[]{:S(2)}) collective-permute-start(bf16[4,64,512]{2,1,0:T(8,128)(2,1)S(1)} %pad_maximum_fusion.1.own), channel_id=1, source_target_pairs={{0,2},{1,3},{2,0},{3,1},{4,6},{5,7},{6,4},{7,5},{8,10},{9,11},{10,... | collective-permute-start | bytes 786440 | tf_op jit(solution)/shard_map/ppermute | solution.py:507
  4.1 22.2 %collective-permute-start = (bf16[4,64,512]{2,1,0:T(8,128)(2,1)S(1)}, bf16[4,64,512]{2,1,0:T(8,128)(2,1)S(1)}, u32[]{:S(2)}, u32[]{:S(2)}) collective-permute-start(bf16[4,64,512]{2,1,0:T(8,128)(2,1)S(1)} %pad_maximum_fusion.1.own), channel_id=1, source_target_pairs={{0,1},{1,2},{2,3},{3,0},{4,5},{5,6},{6,7},{7,4},{8,9},{9,10},{10,1... | collective-permute-start | bytes 786440 | tf_op jit(solution)/shard_map/ppermute | solution.py:507
  6.7 1.6 copy-start
  8.3 0.9 copy-start.1
  10.2 4.4 %collective-permute-start.6 = (bf16[64,512]{1,0:T(8,128)(2,1)S(1)}, bf16[64,512]{1,0:T(8,128)(2,1)S(1)}, u32[]{:S(2)}, u32[]{:S(2)}) collective-permute-start(bf16[64,512]{1,0:T(8,128)(2,1)S(1)} %get-tuple-element.21), channel_id=1, source_target_pairs={{0,20},{4,16},{8,4},{12,0},{16,28},{20,24},{24,12},{28,8},{1,21},{... | collective-permute-start | bytes 196616 | tf_op jit(solution)/shard_map/ppermute | solution.py:528
  12.7 3.0 %collective-permute-start.5 = (bf16[64,512]{1,0:T(8,128)(2,1)S(1)}, bf16[64,512]{1,0:T(8,128)(2,1)S(1)}, u32[]{:S(2)}, u32[]{:S(2)}) collective-permute-start(bf16[64,512]{1,0:T(8,128)(2,1)S(1)} %get-tuple-element.21), channel_id=1, source_target_pairs={{0,16},{4,20},{8,0},{12,4},{16,24},{20,28},{24,8},{28,12},{1,17},{... | collective-permute-start | bytes 196616 | tf_op jit(solution)/shard_map/ppermute | solution.py:528
  14.6 5.0 %collective-permute-start.4 = (bf16[64,512]{1,0:T(8,128)(2,1)S(1)}, bf16[64,512]{1,0:T(8,128)(2,1)S(1)}, u32[]{:S(2)}, u32[]{:S(2)}) collective-permute-start(bf16[64,512]{1,0:T(8,128)(2,1)S(1)} %get-tuple-element.21), channel_id=1, source_target_pairs={{0,4},{4,0},{8,20},{12,16},{16,12},{20,8},{24,28},{28,24},{1,5},{5... | collective-permute-start | bytes 196616 | tf_op jit(solution)/shard_map/ppermute | solution.py:528
  15.7 3.9 %collective-permute-start.3 = (bf16[64,512]{1,0:T(8,128)(2,1)S(1)}, bf16[64,512]{1,0:T(8,128)(2,1)S(1)}, u32[]{:S(2)}, u32[]{:S(2)}) collective-permute-start(bf16[64,512]{1,0:T(8,128)(2,1)S(1)} %get-tuple-element.21), channel_id=1, source_target_pairs={{0,0},{4,4},{8,16},{12,20},{16,8},{20,12},{24,24},{28,28},{1,1},{5... | collective-permute-start | bytes 196616 | tf_op jit(solution)/shard_map/ppermute | solution.py:528
  28.0 18.7 %collective-permute-start.7 = (bf16[2,256,512]{2,1,0:T(8,128)(2,1)S(1)}, bf16[2,256,512]{2,1,0:T(8,128)(2,1)S(1)}, u32[]{:S(2)}, u32[]{:S(2)}) collective-permute-start(bf16[2,256,512]{2,1,0:T(8,128)(2,1)S(1)} %get-tuple-element.22), channel_id=1, source_target_pairs={{0,4},{4,0},{1,5},{5,1},{2,6},{6,2},{3,7},{7,3},{8,12},{12,8},{9,1... | collective-permute-start | bytes 1572872 | tf_op jit(solution)/shard_map/ppermute | solution.py:544
  29.6 26.1 %collective-permute-start.17 = (bf16[2,256,512]{2,1,0:T(8,128)(2,1)S(1)}, bf16[2,256,512]{2,1,0:T(8,128)(2,1)S(1)}, u32[]{:S(2)}, u32[]{:S(2)}) collective-permute-start(bf16[2,256,512]{2,1,0:T(8,128)(2,1)S(1)} %get-tuple-element.25), channel_id=1, source_target_pairs={{0,0},{4,4},{8,16},{12,20},{16,8},{20,12},{24,24},{28,28},{1,1},{5... | collective-permute-start | bytes 1572872 | tf_op jit(solution)/shard_map/ppermute | solution.py:526
  30.3 28.1 %collective-permute-start.18 = (bf16[2,256,512]{2,1,0:T(8,128)(2,1)S(1)}, bf16[2,256,512]{2,1,0:T(8,128)(2,1)S(1)}, u32[]{:S(2)}, u32[]{:S(2)}) collective-permute-start(bf16[2,256,512]{2,1,0:T(8,128)(2,1)S(1)} %get-tuple-element.26), channel_id=1, source_target_pairs={{0,4},{4,0},{8,20},{12,16},{16,12},{20,8},{24,28},{28,24},{1,5},{5... | collective-permute-start | bytes 1572872 | tf_op jit(solution)/shard_map/ppermute | solution.py:526
  30.8 18.5 %collective-permute-start.16 = (bf16[4,64,512]{2,1,0:T(8,128)(2,1)S(1)}, bf16[4,64,512]{2,1,0:T(8,128)(2,1)S(1)}, u32[]{:S(2)}, u32[]{:S(2)}) collective-permute-start(bf16[4,64,512]{2,1,0:T(8,128)(2,1)S(1)} %get-tuple-element.24.own), channel_id=1, source_target_pairs={{0,3},{1,0},{2,1},{3,2},{4,7},{5,4},{6,5},{7,6},{8,11},{9,8},{10,9... | collective-permute-start | bytes 786440 | tf_op jit(solution)/shard_map/ppermute | solution.py:507
  32.0 20.7 %collective-permute-start.15 = (bf16[4,64,512]{2,1,0:T(8,128)(2,1)S(1)}, bf16[4,64,512]{2,1,0:T(8,128)(2,1)S(1)}, u32[]{:S(2)}, u32[]{:S(2)}) collective-permute-start(bf16[4,64,512]{2,1,0:T(8,128)(2,1)S(1)} %get-tuple-element.24.own), channel_id=1, source_target_pairs={{0,2},{1,3},{2,0},{3,1},{4,6},{5,7},{6,4},{7,5},{8,10},{9,11},{10,... | collective-permute-start | bytes 786440 | tf_op jit(solution)/shard_map/ppermute | solution.py:507
  46.7 8.3 %collective-permute-start.14 = (bf16[4,64,512]{2,1,0:T(8,128)(2,1)S(1)}, bf16[4,64,512]{2,1,0:T(8,128)(2,1)S(1)}, u32[]{:S(2)}, u32[]{:S(2)}) collective-permute-start(bf16[4,64,512]{2,1,0:T(8,128)(2,1)S(1)} %get-tuple-element.24.own), channel_id=1, source_target_pairs={{0,1},{1,2},{2,3},{3,0},{4,5},{5,6},{6,7},{7,4},{8,9},{9,10},{10,1... | collective-permute-start | bytes 786440 | tf_op jit(solution)/shard_map/ppermute | solution.py:507
  49.3 10.5 %collective-permute-start.19 = (bf16[2,256,512]{2,1,0:T(8,128)(2,1)S(1)}, bf16[2,256,512]{2,1,0:T(8,128)(2,1)S(1)}, u32[]{:S(2)}, u32[]{:S(2)}) collective-permute-start(bf16[2,256,512]{2,1,0:T(8,128)(2,1)S(1)} %get-tuple-element.27), channel_id=1, source_target_pairs={{0,16},{4,20},{8,0},{12,4},{16,24},{20,28},{24,8},{28,12},{1,17},{... | collective-permute-start | bytes 1572872 | tf_op jit(solution)/shard_map/ppermute | solution.py:526
  52.6 18.4 %collective-permute-start.12 = (bf16[2,256,512]{2,1,0:T(8,128)(2,1)S(1)}, bf16[2,256,512]{2,1,0:T(8,128)(2,1)S(1)}, u32[]{:S(2)}, u32[]{:S(2)}) collective-permute-start(bf16[2,256,512]{2,1,0:T(8,128)(2,1)S(1)} %get-tuple-element.23), channel_id=1, source_target_pairs={{0,16},{4,20},{8,0},{12,4},{16,24},{20,28},{24,8},{28,12},{1,17},{... | collective-permute-start | bytes 1572872 | tf_op jit(solution)/shard_map/ppermute | solution.py:541
  55.0 17.5 %collective-permute-start.10 = (bf16[2,256,512]{2,1,0:T(8,128)(2,1)S(1)}, bf16[2,256,512]{2,1,0:T(8,128)(2,1)S(1)}, u32[]{:S(2)}, u32[]{:S(2)}) collective-permute-start(bf16[2,256,512]{2,1,0:T(8,128)(2,1)S(1)} %get-tuple-element.23), channel_id=1, source_target_pairs={{0,0},{4,4},{8,16},{12,20},{16,8},{20,12},{24,24},{28,28},{1,1},{5... | collective-permute-start | bytes 1572872 | tf_op jit(solution)/shard_map/ppermute | solution.py:541
  55.7 43.9 %collective-permute-start.9 = (bf16[2,2,256,512]{3,2,1,0:T(8,128)(2,1)S(1)}, bf16[2,2,256,512]{3,2,1,0:T(8,128)(2,1)S(1)}, u32[]{:S(2)}, u32[]{:S(2)}) collective-permute-start(bf16[2,2,256,512]{3,2,1,0:T(8,128)(2,1)S(1)} %pad_maximum_fusion), channel_id=1, source_target_pairs={{0,16},{4,20},{8,0},{12,4},{16,24},{20,28},{24,8},{28,12},{1,17},{... | collective-permute-start | bytes 3145736 | tf_op jit(solution)/shard_map/ppermute | solution.py:541
  58.3 41.3 %collective-permute-start.8 = (bf16[2,2,256,512]{3,2,1,0:T(8,128)(2,1)S(1)}, bf16[2,2,256,512]{3,2,1,0:T(8,128)(2,1)S(1)}, u32[]{:S(2)}, u32[]{:S(2)}) collective-permute-start(bf16[2,2,256,512]{3,2,1,0:T(8,128)(2,1)S(1)} %pad_maximum_fusion), channel_id=1, source_target_pairs={{0,0},{4,4},{8,16},{12,20},{16,8},{20,12},{24,24},{28,28},{1,1},{5... | collective-permute-start | bytes 3145736 | tf_op jit(solution)/shard_map/ppermute | solution.py:541
  59.8 38.9 %collective-permute-start.20 = (bf16[2,256,512]{2,1,0:T(8,128)(2,1)S(1)}, bf16[2,256,512]{2,1,0:T(8,128)(2,1)S(1)}, u32[]{:S(2)}, u32[]{:S(2)}) collective-permute-start(bf16[2,256,512]{2,1,0:T(8,128)(2,1)S(1)} %get-tuple-element.28), channel_id=1, source_target_pairs={{0,20},{4,16},{8,4},{12,0},{16,28},{20,24},{24,12},{28,8},{1,21},{... | collective-permute-start | bytes 1572872 | tf_op jit(solution)/shard_map/ppermute | solution.py:526
  71.0 27.7 %collective-permute-start.13 = (bf16[2,256,512]{2,1,0:T(8,128)(2,1)S(1)}, bf16[2,256,512]{2,1,0:T(8,128)(2,1)S(1)}, u32[]{:S(2)}, u32[]{:S(2)}) collective-permute-start(bf16[2,256,512]{2,1,0:T(8,128)(2,1)S(1)} %collective-permute-done.12.y2), channel_id=1, source_target_pairs={{0,4},{4,0},{1,5},{5,1},{2,6},{6,2},{3,7},{7,3},{8,12},{12,8},{9,1... | collective-permute-start | bytes 1572872 | tf_op jit(solution)/shard_map/ppermute | solution.py:544
  72.6 27.1 %collective-permute-start.11 = (bf16[2,256,512]{2,1,0:T(8,128)(2,1)S(1)}, bf16[2,256,512]{2,1,0:T(8,128)(2,1)S(1)}, u32[]{:S(2)}, u32[]{:S(2)}) collective-permute-start(bf16[2,256,512]{2,1,0:T(8,128)(2,1)S(1)} %collective-permute-done.10.y0), channel_id=1, source_target_pairs={{0,4},{4,0},{1,5},{5,1},{2,6},{6,2},{3,7},{7,3},{8,12},{12,8},{9,1... | collective-permute-start | bytes 1572872 | tf_op jit(solution)/shard_map/ppermute | solution.py:544
  106.7 3.6 %collective-permute-start.21 = (bf16[2,512,512]{2,1,0:T(8,128)(2,1)S(1)}, bf16[2,512,512]{2,1,0:T(8,128)(2,1)S(1)}, u32[]{:S(2)}, u32[]{:S(2)}) collective-permute-start(bf16[2,512,512]{2,1,0:T(8,128)(2,1)S(1)} %get-tuple-element.30.w_high), channel_id=1, source_target_pairs={{0,8},{16,24},{1,9},{17,25},{2,10},{18,26},{3,11},{19,27},{4,12},{... | collective-permute-start | bytes 3145736 | tf_op jit(solution)/shard_map/ppermute | solution.py:591
  111.2 13.5 %collective-permute-start.22 = (bf16[2,512,512]{2,1,0:T(8,128)(2,1)S(1)}, bf16[2,512,512]{2,1,0:T(8,128)(2,1)S(1)}, u32[]{:S(2)}, u32[]{:S(2)}) collective-permute-start(bf16[2,512,512]{2,1,0:T(8,128)(2,1)S(1)} %get-tuple-element.31), channel_id=1, source_target_pairs={{8,0},{24,16},{9,1},{25,17},{10,2},{26,18},{11,3},{27,19},{12,4},{... | collective-permute-start | bytes 3145736 | tf_op jit(solution)/shard_map/ppermute | solution.py:616
  131.7 8.2 %collective-permute-start.23 = (bf16[2,256,512]{2,1,0:T(8,128)(2,1)S(1)}, bf16[2,256,512]{2,1,0:T(8,128)(2,1)S(1)}, u32[]{:S(2)}, u32[]{:S(2)}) collective-permute-start(bf16[2,256,512]{2,1,0:T(8,128)(2,1)S(1)} %get-tuple-element.33), channel_id=1, source_target_pairs={{0,0},{4,4},{16,8},{20,12},{8,16},{12,20},{24,24},{28,28},{1,1},{5... | collective-permute-start | bytes 1572872 | tf_op jit(solution)/shard_map/ppermute | solution.py:639
  132.4 9.7 %collective-permute-start.24 = (bf16[2,256,512]{2,1,0:T(8,128)(2,1)S(1)}, bf16[2,256,512]{2,1,0:T(8,128)(2,1)S(1)}, u32[]{:S(2)}, u32[]{:S(2)}) collective-permute-start(bf16[2,256,512]{2,1,0:T(8,128)(2,1)S(1)} %get-tuple-element.34), channel_id=1, source_target_pairs={{4,0},{0,4},{20,8},{16,12},{12,16},{8,20},{28,24},{24,28},{5,1},{1... | collective-permute-start | bytes 1572872 | tf_op jit(solution)/shard_map/ppermute | solution.py:639
  135.0 21.8 %collective-permute-start.25 = (bf16[2,256,512]{2,1,0:T(8,128)(2,1)S(1)}, bf16[2,256,512]{2,1,0:T(8,128)(2,1)S(1)}, u32[]{:S(2)}, u32[]{:S(2)}) collective-permute-start(bf16[2,256,512]{2,1,0:T(8,128)(2,1)S(1)} %get-tuple-element.35), channel_id=1, source_target_pairs={{16,0},{20,4},{0,8},{4,12},{24,16},{28,20},{8,24},{12,28},{17,1},{... | collective-permute-start | bytes 1572872 | tf_op jit(solution)/shard_map/ppermute | solution.py:639
  139.7 23.9 %collective-permute-start.26 = (bf16[2,256,512]{2,1,0:T(8,128)(2,1)S(1)}, bf16[2,256,512]{2,1,0:T(8,128)(2,1)S(1)}, u32[]{:S(2)}, u32[]{:S(2)}) collective-permute-start(bf16[2,256,512]{2,1,0:T(8,128)(2,1)S(1)} %get-tuple-element.36), channel_id=1, source_target_pairs={{20,0},{16,4},{4,8},{0,12},{28,16},{24,20},{12,24},{8,28},{21,1},{... | collective-permute-start | bytes 1572872 | tf_op jit(solution)/shard_map/ppermute | solution.py:639

commit v4 on v3

--- a/solution.py
+++ b/solution.py
@@ -15,7 +15,7 @@
 in_smem = pl.BlockSpec(memory_space=pltpu.SMEM)
 in_vmem = pl.BlockSpec(memory_space=pltpu.VMEM)
 
-info_member, info_piece, info_slot, info_half, info_block = 3, 4, 12, 14, 16
+info_member, info_piece, info_slot, info_half = 3, 4, 12, 14
 
 
 def shifted(x, axis, by):
@@ -161,18 +161,35 @@
     return [slice(first, first + step) for first in range(0, order, step)]
 
 
-def pack_kernel(place, field, coupling, *rest):
-    pieces, own_rows, sems = rest[:-2], rest[-2], rest[-1]
+def pack_kernel(place, field, coupling, x_factor, y_factor, *rest):
+    pieces, (blocks, sems, csems, fsems) = rest[:-4], rest[-4:]
     copies = []
+    height = x_factor.shape[1]
+    own = pl.ds(pl.multiple_of(place[len(pieces)] * height, height), height)
     for index, piece in enumerate(pieces):
-        width = piece.shape[2]
+        width = piece.shape[1]
         offset = pl.multiple_of(place[index] * width, width)
+        rows_here = field.shape[1]
+        for plane in range(2):
+            copies.append(
+                pltpu.make_async_copy(
+                    field.at[plane, :, pl.ds(offset, width)],
+                    piece.at[pl.ds(plane * rows_here, rows_here)],
+                    sems.at[index, plane],
+                )
+            )
         copies.append(
-            pltpu.make_async_copy(field.at[:, :, pl.ds(offset, width)], piece, sems.at[index])
-        )
-    height = own_rows.shape[0]
-    rows = pl.ds(pl.multiple_of(place[len(pieces)] * height, height), height)
-    copies.append(pltpu.make_async_copy(coupling.at[rows], own_rows, sems.at[len(pieces)]))
+            pltpu.make_async_copy(
+                coupling.at[own], piece.at[pl.ds(2 * rows_here, height)], csems.at[index]
+            )
+        )
+    for target in range(blocks.shape[0]):
+        for which, factor in enumerate((x_factor, y_factor)):
+            copies.append(
+                pltpu.make_async_copy(
+                    factor, blocks.at[target, pl.ds(2 * which, 2)], fsems.at[target, which]
+                )
+            )
     start_all(copies)
     wait_all(copies)
 
@@ -190,40 +207,56 @@
     wait_all(copies)
 
 
-def stack_kernel(info, own, first, second, third, c0, c1, c2, c3, x_column, y_column, rows_held,
-                 sems, csems):
-    height = own.shape[1]
+def column_kernel(blocks, p0, p1, p2, p3, x_column, y_column, sems):
+    height = blocks.shape[2]
     copies = []
-    for turn, block in enumerate((own, first, second, third)):
-        rows = pl.ds(pl.multiple_of(info[info_block + turn] * height, height), height)
+    for index in range(blocks.shape[0]):
+        rows = pl.ds(index * height, height)
         for which, column in enumerate((x_column, y_column)):
             copies.append(
                 pltpu.make_async_copy(
-                    block.at[pl.ds(2 * which, 2)], column.at[:, rows, :], sems.at[turn, which]
-                )
-            )
-    for index, rows_of in enumerate((c0, c1, c2, c3)):
-        copies.append(pltpu.make_async_copy(rows_of, rows_held.at[index], csems.at[index]))
-    start_all(copies)
-    wait_all(copies)
-
-
-def weight_kernel(info, own, first, second, third, weights, sems):
-    height = own.shape[1]
-    half_height = weights.shape[1] // 2
-    copies = []
-    for turn, block in enumerate((own, first, second, third)):
-        for index in range(block.shape[0]):
-            slot, half = info[info_piece + 2 * index], info[info_piece + 2 * index + 1]
-            start = half * half_height + info[info_block + turn] * height
-            rows = pl.ds(pl.multiple_of(start, height), height)
-            copies.append(
-                pltpu.make_async_copy(
-                    block.at[index], weights.at[slot, rows, :], sems.at[turn, index]
+                    blocks.at[index, pl.ds(2 * which, 2)],
+                    column.at[:, rows, :],
+                    sems.at[index, which],
                 )
             )
     start_all(copies)
     wait_all(copies)
+
+
+def both_kernel(x_column, x_aside, y0, y1, p0, p1, p2, p3, x_both, rows_held, sems, csems):
+    copies = [
+        pltpu.make_async_copy(x_column, x_both.at[0], sems.at[0]),
+        pltpu.make_async_copy(x_aside, x_both.at[1], sems.at[1]),
+    ]
+    height = rows_held.shape[2]
+    for target in range(rows_held.shape[0]):
+        for index, piece in enumerate((p0, p1, p2, p3)):
+            copies.append(
+                pltpu.make_async_copy(
+                    piece.at[pl.ds(piece.shape[0] - height, height)],
+                    rows_held.at[target, index],
+                    csems.at[target, index],
+                )
+            )
+    start_all(copies)
+    wait_all(copies)
+
+
+def weight_copies(info, blocks, weights, sems):
+    height = blocks.shape[2]
+    half_height = weights.shape[1] // 2
+    copies = []
+    for index in range(blocks.shape[0]):
+        for turn in range(blocks.shape[1]):
+            slot, half = info[info_piece + 2 * turn], info[info_piece + 2 * turn + 1]
+            rows = pl.ds(pl.multiple_of(half * half_height + index * height, height), height)
+            copies.append(
+                pltpu.make_async_copy(
+                    blocks.at[index, turn], weights.at[slot, rows, :], sems.at[index, turn]
+                )
+            )
+    return copies
 
 
 def halves(*pairs):
@@ -347,20 +380,27 @@
 
 def rhs_copies(info, pieces, rhs, sems):
     copies = []
+    height = rhs.shape[2] // 2
     for index, piece in enumerate(pieces):
-        height = piece.shape[1]
         slot, half = info[info_piece + 2 * index], info[info_piece + 2 * index + 1]
         rows = pl.ds(pl.multiple_of(half * height, height), height)
-        copies.append(pltpu.make_async_copy(piece, rhs.at[slot, :, rows, :], sems.at[index]))
+        for plane in range(2):
+            copies.append(
+                pltpu.make_async_copy(
+                    piece.at[pl.ds(plane * height, height)],
+                    rhs.at[slot, plane, rows, :],
+                    sems.at[2 * index + plane],
+                )
+            )
     return copies
 
 
 def first_kernel(info, x0, x1, y0, y1, y2, y3, coupling, p0, p1, p2, p3, w_low, w_high,
-                 held, weights, rhs, beside, below, sems, fsems):
+                 held, weights, rhs, beside, below, sems, csems, fsems):
     @pl.when(info[info_member] == 0)
     def _():
         early = rhs_copies(info, (p0, p1, p2, p3), rhs, sems)
-        early.append(pltpu.make_async_copy(coupling, weights, sems.at[4]))
+        early += weight_copies(info, coupling, weights, csems)
         start_all(early)
         factors = Factors(info, (halves(x0, x1), (y0, y1, y2, y3)), held, fsems)
         wait_all(early)
@@ -373,12 +413,13 @@
 
 
 def last_kernel(info, x0, x1, y0, y1, y2, y3, coupling, p0, p1, p2, p3, incoming, field,
-                sent, held, weights, rhs, arrived, kept, beside, below, sems, fsems, osems):
+                sent, held, weights, rhs, arrived, kept, beside, below, sems, csems, fsems,
+                osems):
     @pl.when(info[info_member] == 1)
     def _():
         early = rhs_copies(info, (p0, p1, p2, p3), rhs, sems)
-        early.append(pltpu.make_async_copy(coupling, weights, sems.at[4]))
-        early.append(pltpu.make_async_copy(incoming, arrived, sems.at[5]))
+        early += weight_copies(info, coupling, weights, csems)
+        early.append(pltpu.make_async_copy(incoming, arrived, sems.at[8]))
         start_all(early)
         factors = Factors(info, (halves(x0, x1), (y0, y1, y2, y3)), held, fsems)
         wait_all(early)
@@ -412,14 +453,15 @@
 
 
 def back_kernel(info, x0, x1, y0, y1, y2, y3, coupling, w_low, w_high, incoming, field,
-                p0, p1, p2, p3, held, weights, kept, arrived, beside, below, sems, fsems, osems):
+                p0, p1, p2, p3, held, weights, kept, arrived, beside, below, sems, csems, fsems,
+                osems):
     @pl.when(info[info_member] == 0)
     def _():
         early = [pltpu.make_async_copy(incoming, arrived, sems.at[0])]
         start_all(early)
         factors = Factors(info, (halves(x0, x1), (y0, y1, y2, y3)), held, fsems)
+        early += weight_copies(info, coupling, weights, csems)
         early += [
-            pltpu.make_async_copy(coupling, weights, sems.at[1]),
             pltpu.make_async_copy(w_low, kept.at[0], sems.at[2]),
             pltpu.make_async_copy(w_high, kept.at[1], sems.at[3]),
         ]
@@ -499,43 +541,39 @@
     for a, b in rounds:
         entries += [(group + a) % 2, (own_x - b) % px_count]
     entries += [group, (group + 1) % 2, own_x, (own_x + 1) % 2]
-    entries += [(own_y - turn) % py_count for turn in range(py_count)]
     info = jnp.stack([jnp.asarray(entry, jnp.int32) for entry in entries])
 
-    def rotated(block):
-        return [block] + [
-            lax.ppermute(block, "py", [(z, (z + turn) % py_count) for z in range(py_count)])
-            for turn in range(1, py_count)
-        ]
-
-    shard = jnp.concatenate([x_factor[0], y_factor[0]], axis=0)
-    shards = rotated(shard)
     sends_to = jnp.stack(
         [((member + a) % 2) * px_count + (own_x + b) % px_count for a, b in rounds] + [own_y]
     ).astype(jnp.int32)
     piece_shape = jax.ShapeDtypeStruct((2, rows_here, order), bf16)
-    *pieces, own_rows = pl.pallas_call(
+    *pieces, blocks = pl.pallas_call(
         pack_kernel,
-        out_shape=[piece_shape] * len(rounds) + [jax.ShapeDtypeStruct((height, order), bf16)],
-        in_specs=[in_smem, anywhere, anywhere],
+        out_shape=[jax.ShapeDtypeStruct((2 * rows_here + height, order), bf16)] * len(rounds)
+        + [jax.ShapeDtypeStruct((py_count, 4, height, order), bf16)],
+        in_specs=[in_smem] + [anywhere] * 4,
         out_specs=[in_vmem] * (len(rounds) + 1),
-        scratch_shapes=[pltpu.SemaphoreType.DMA((len(rounds) + 1,))],
+        scratch_shapes=[
+            pltpu.SemaphoreType.DMA((len(rounds), 2)),
+            pltpu.SemaphoreType.DMA((len(rounds),)),
+            pltpu.SemaphoreType.DMA((py_count, 2)),
+        ],
         compiler_params=params,
-    )(sends_to, field, coupling[0])
+    )(sends_to, field, coupling[0], x_factor[0], y_factor[0])
     pieces = [
         lax.ppermute(piece, ("sec", "px"), pairs(a, b)) for piece, (a, b) in zip(pieces, rounds)
     ]
-    layer_rows = [lax.ppermute(own_rows, ("sec", "px"), pairs(a, b)) for a, b in rounds]
+    blocks = lax.all_to_all(blocks, "py", split_axis=0, concat_axis=0, tiled=True)
 
     column_shape = jax.ShapeDtypeStruct((2, rows_here, order), bf16)
-    x_column, y_column, rows_held = pl.pallas_call(
-        stack_kernel,
-        out_shape=[column_shape] * 2 + [jax.ShapeDtypeStruct((4, height, order), bf16)],
-        in_specs=[in_smem] + [anywhere] * 8,
-        out_specs=[in_vmem] * 3,
-        scratch_shapes=[pltpu.SemaphoreType.DMA((4, 2)), pltpu.SemaphoreType.DMA((4,))],
+    x_column, y_column = pl.pallas_call(
+        column_kernel,
+        out_shape=[column_shape] * 2,
+        in_specs=[anywhere] * 5,
+        out_specs=[in_vmem] * 2,
+        scratch_shapes=[pltpu.SemaphoreType.DMA((py_count, 2))],
         compiler_params=params,
-    )(info, *shards, *layer_rows)
+    )(blocks, *pieces)
 
     def across(block, a):
         return lax.ppermute(block, ("sec", "px"), pairs(a, 0))
@@ -545,18 +583,24 @@
 
     x_aside = aside(x_column)
     y_near = [across(y_column, a) for a in range(2)]
+    x_both, rows_held = pl.pallas_call(
+        both_kernel,
+        out_shape=[
+            jax.ShapeDtypeStruct((2, 2, rows_here, order), bf16),
+            jax.ShapeDtypeStruct((py_count, len(rounds), height, order), bf16),
+        ],
+        in_specs=[anywhere] * 8,
+        out_specs=[in_vmem] * 2,
+        scratch_shapes=[
+            pltpu.SemaphoreType.DMA((2,)),
+            pltpu.SemaphoreType.DMA((py_count, len(rounds))),
+        ],
+        compiler_params=params,
+    )(x_column, x_aside, *y_near, *pieces)
     y_far = [aside(block) for block in y_near]
-    x_both = jnp.stack([x_column, x_aside])
     x_across = [across(x_both, a) for a in range(2)]
+    weights = lax.all_to_all(rows_held, "py", split_axis=0, concat_axis=0, tiled=True)
     factors = x_across + [y_near[0], y_far[0], y_near[1], y_far[1]]
-    weights = pl.pallas_call(
-        weight_kernel,
-        out_shape=jax.ShapeDtypeStruct((2, order, order), bf16),
-        in_specs=[in_smem] + [anywhere] * 4,
-        out_specs=in_vmem,
-        scratch_shapes=[pltpu.SemaphoreType.DMA((4, 4))],
-        compiler_params=params,
-    )(info, *rotated(rows_held))
 
     full_shape = jax.ShapeDtypeStruct((2, order, order), bf16)
     factor_scratch = pltpu.VMEM((2, 2, order, 2 * order), bf16)
@@ -578,7 +622,8 @@
             field_scratch,
             beside_scratch,
             below_scratch,
-            pltpu.SemaphoreType.DMA((6,)),
+            pltpu.SemaphoreType.DMA((9,)),
+            pltpu.SemaphoreType.DMA((4, 4)),
             factor_sems,
         ],
         compiler_params=params,
@@ -602,7 +647,8 @@
             field_scratch,
             beside_scratch,
             below_scratch,
-            pltpu.SemaphoreType.DMA((7,)),
+            pltpu.SemaphoreType.DMA((9,)),
+            pltpu.SemaphoreType.DMA((4, 4)),
             factor_sems,
             pltpu.SemaphoreType.DMA((2,)),
         ],
@@ -626,7 +672,8 @@
             arrived_scratch,
             beside_scratch,
             below_scratch,
-            pltpu.SemaphoreType.DMA((6,)),
+            pltpu.SemaphoreType.DMA((9,)),
+            pltpu.SemaphoreType.DMA((4, 4)),
             factor_sems,
             pltpu.SemaphoreType.DMA((len(rounds),)),
         ],

time: 166 us -> 170 us (1.024)
  the two profiles are of different devices: /device:TPU:8 before, /device:TPU:1 now
where the time goes in v4:
time: 170 us; the launch traced here: 169 us
  waiting for transfers between devices  90.8 us (53%)
  starting transfers between devices  41.5 us (24%)
  Pallas kernels  23 us (14%)
  local copies, waits for them, and re-layouts  10.9 us (6%)
  between operations  2.93 us (2%)
    ppermute x4, waiting for transfers between devices, on_device(): lax.ppermute(piece, ('sec', 'px'), pairs(a, b))  24.4 us
    ppermute x4, waiting for transfers between devices, on_device(): lax.ppermute(piece, ('sec', 'px'), back_pairs(a, b))  22.6 us
    ppermute x3, waiting for transfers between devices, aside(): return lax.ppermute(block, 'px', [(y, (y + 1) % 2) for y in range(2)])  22.1 us
    ppermute x1, waiting for transfers between devices, on_device(): incoming = lax.ppermute(w_high, 'sec', up)  14.1 us
    pallas_call x1, Pallas kernels, on_device(): pl.pallas_call(last_kernel, out_shape=[jax.ShapeDtypeStruct((2, 2, order,...  12.4 us
    ppermute x4, starting transfers between devices, on_device(): lax.ppermute(piece, ('sec', 'px'), back_pairs(a, b))  10.9 us
    unnamed x30, local copies, waits for them, and re-layouts  10.2 us
    ppermute x4, starting transfers between devices, across(): return lax.ppermute(block, ('sec', 'px'), pairs(a, 0))  8.47 us
  transfers between devices with their start and end apart: 19, of which 15 were waited for; matrix products, arithmetic and copies ran while one was open for 0% of the time, Pallas kernels for 0%

profile of v4, /device:TPU:1, one launch (start us, length us, event | category | flops | bytes accessed | tf_op | source)
XLA Modules:
  0.0 169.2 jit_solution(6631788712429965501)
XLA Ops:
  0.1 1.6 copy-done
  4.4 3.8 %shard_map.55 = (bf16[576,512]{1,0:T(8,128)(2,1)}, bf16[576,512]{1,0:T(8,128)(2,1)}, bf16[576,512]{1,0:T(8,128)(2,1)}, bf16[576,512]{1,0:T(8,128)(2,1)S(1)}, bf16[4,4,64,512]{3,2,1,0:T(8,128)(2,1)S(1)}) custom-call(s32[5]{0:T(128)S(1)} %stack.64.place, bf16[2,256,2048]{2,1,0:T(8,128)(2,1)S(1)} %bitcast.24, bf16[256,512]{1,0:T(8,128)(2,1)S(1)} %bitcast.25, ...), custom_call_target="tpu_custom_call" | custom-call | tf_op jit(solution)/shard_map/pallas_call | solution.py:550
  10.0 5.4 %all-to-all-start = ((bf16[4,4,64,512]{3,2,1,0:T(8,128)(2,1)}), bf16[4,4,64,512]{3,2,1,0:T(8,128)(2,1)S(1)}, u32[]{:S(2)}, u32[]{:S(2)}) async-start(bf16[4,4,64,512]{3,2,1,0:T(8,128)(2,1)} %copy-done.2), calls=%async_computation | async-start | bytes 2097152 | tf_op jit(solution)/shard_map/all_to_all | solution.py:566
  15.5 3.9 %collective-permute-start = (bf16[576,512]{1,0:T(8,128)(2,1)}, bf16[576,512]{1,0:T(8,128)(2,1)S(1)}, u32[]{:S(2)}, u32[]{:S(2)}) collective-permute-start(bf16[576,512]{1,0:T(8,128)(2,1)} %get-tuple-element.23), channel_id=1, source_target_pairs={{0,0},{4,4},{8,16},{12,20},{16,8},{20,12},{24,24},{28,28},{1,1},{5... | collective-permute-start | bytes 1769480 | tf_op jit(solution)/shard_map/ppermute | solution.py:564
  20.4 2.2 %collective-permute-start.3 = (bf16[576,512]{1,0:T(8,128)(2,1)}, bf16[576,512]{1,0:T(8,128)(2,1)S(1)}, u32[]{:S(2)}, u32[]{:S(2)}) collective-permute-start(bf16[576,512]{1,0:T(8,128)(2,1)} %copy-done.13), channel_id=1, source_target_pairs={{0,20},{4,16},{8,4},{12,0},{16,28},{20,24},{24,12},{28,8},{1,21},{... | collective-permute-start | bytes 1769480 | tf_op jit(solution)/shard_map/ppermute | solution.py:564
  22.7 8.8 %collective-permute-done.p0 = bf16[576,512]{1,0:T(8,128)(2,1)S(1)} collective-permute-done((bf16[576,512]{1,0:T(8,128)(2,1)}, bf16[576,512]{1,0:T(8,128)(2,1)S(1)}, u32[]{:S(2)}, u32[]{:S(2)}) %collective-permute-start) | collective-permute-done | bytes 589856 | tf_op jit(solution)/shard_map/ppermute | solution.py:564
  31.5 14.3 %collective-permute-done.1.p1 = bf16[576,512]{1,0:T(8,128)(2,1)S(1)} collective-permute-done((bf16[576,512]{1,0:T(8,128)(2,1)}, bf16[576,512]{1,0:T(8,128)(2,1)S(1)}, u32[]{:S(2)}, u32[]{:S(2)}) %collective-permute-start.1) | collective-permute-done | bytes 589856 | tf_op jit(solution)/shard_map/ppermute | solution.py:564
  45.8 1.3 collective-permute-done.3.p3
  48.2 1.3 collective-permute-start.6
  49.5 2.5 %collective-permute-start.5 = (bf16[2,256,512]{2,1,0:T(8,128)(2,1)S(1)}, bf16[2,256,512]{2,1,0:T(8,128)(2,1)S(1)}, u32[]{:S(2)}, u32[]{:S(2)}) collective-permute-start(bf16[2,256,512]{2,1,0:T(8,128)(2,1)S(1)} %get-tuple-element.28), channel_id=1, source_target_pairs={{0,0},{4,4},{8,16},{12,20},{16,8},{20,12},{24,24},{28,28},{1,1},{5... | collective-permute-start | bytes 1572872 | tf_op jit(solution)/shard_map/ppermute | solution.py:579
  52.1 9.7 %collective-permute-done.4.x_aside = bf16[2,256,512]{2,1,0:T(8,128)(2,1)S(1)} collective-permute-done((bf16[2,256,512]{2,1,0:T(8,128)(2,1)S(1)}, bf16[2,256,512]{2,1,0:T(8,128)(2,1)S(1)}, u32[]{:S(2)}, u32[]{:S(2)}) %collective-permute-start.4) | collective-permute-done | bytes 524320 | tf_op jit(solution)/shard_map/ppermute | solution.py:582
  62.5 1.6 shard_map.57
  66.1 4.9 %all-to-all-start.1 = ((bf16[4,4,64,512]{3,2,1,0:T(8,128)(2,1)}), bf16[4,4,64,512]{3,2,1,0:T(8,128)(2,1)S(1)}, u32[]{:S(2)}, u32[]{:S(2)}) async-start(bf16[4,4,64,512]{3,2,1,0:T(8,128)(2,1)} %copy-done.1), calls=%async_computation.1 | async-start | bytes 2097152 | tf_op jit(solution)/shard_map/all_to_all | solution.py:602
  71.1 4.6 %collective-permute-start.7 = (bf16[2,2,256,512]{3,2,1,0:T(8,128)(2,1)}, bf16[2,2,256,512]{3,2,1,0:T(8,128)(2,1)}, u32[]{:S(2)}, u32[]{:S(2)}) collective-permute-start(bf16[2,2,256,512]{3,2,1,0:T(8,128)(2,1)} %copy-done.12), channel_id=1, source_target_pairs={{0,0},{4,4},{8,16},{12,20},{16,8},{20,12},{24,24},{28,28},{1,1},{5... | collective-permute-start | bytes 3145736 | tf_op jit(solution)/shard_map/ppermute | solution.py:579
  75.7 1.3 collective-permute-start.10
  80.5 3.8 %collective-permute-done.10.y3 = bf16[2,256,512]{2,1,0:T(8,128)(2,1)} collective-permute-done((bf16[2,256,512]{2,1,0:T(8,128)(2,1)}, bf16[2,256,512]{2,1,0:T(8,128)(2,1)}, u32[]{:S(2)}, u32[]{:S(2)}) %collective-permute-start.10) | collective-permute-done | bytes 524320 | tf_op jit(solution)/shard_map/ppermute | solution.py:582
  84.3 8.5 %collective-permute-done.9.y1 = bf16[2,256,512]{2,1,0:T(8,128)(2,1)} collective-permute-done((bf16[2,256,512]{2,1,0:T(8,128)(2,1)}, bf16[2,256,512]{2,1,0:T(8,128)(2,1)}, u32[]{:S(2)}, u32[]{:S(2)}) %collective-permute-start.9) | collective-permute-done | bytes 524320 | tf_op jit(solution)/shard_map/ppermute | solution.py:582
  93.0 4.7 %collective-permute-done.7.x0 = bf16[2,2,256,512]{3,2,1,0:T(8,128)(2,1)} collective-permute-done((bf16[2,2,256,512]{3,2,1,0:T(8,128)(2,1)}, bf16[2,2,256,512]{3,2,1,0:T(8,128)(2,1)}, u32[]{:S(2)}, u32[]{:S(2)}) %collective-permute-start.7) | collective-permute-done | bytes 1048608 | tf_op jit(solution)/shard_map/ppermute | solution.py:579
  100.7 1.3 collective-permute-start.11
  102.0 14.1 %collective-permute-done.11.incoming = bf16[2,512,512]{2,1,0:T(8,128)(2,1)S(1)} collective-permute-done((bf16[2,512,512]{2,1,0:T(8,128)(2,1)S(1)}, bf16[2,512,512]{2,1,0:T(8,128)(2,1)S(1)}, u32[]{:S(2)}, u32[]{:S(2)}) %collective-permute-start.11) | collective-permute-done | bytes 1048608 | tf_op jit(solution)/shard_map/ppermute | solution.py:636
  116.1 12.4 %shard_map.59 = (bf16[2,2,512,512]{3,2,1,0:T(8,128)(2,1)S(1)}, bf16[2,512,512]{2,1,0:T(8,128)(2,1)S(1)}) custom-call(s32[16]{0:T(128)S(1)} %stack.76.info, bf16[2,2,256,512]{3,2,1,0:T(8,128)(2,1)} %collective-permute-done.7.x0, bf16[2,2,256,512]{3,2,1,0:T(8,128)(2,1)} %collective-permute-done.8.x1, bf16[2,256,512]{2,1,0:T(8,128)(2,1)S(1)} %copy-done.8, ...), custom_call_target="tpu_custom_call" | custom-call | flops 6442450944 | bytes 8388608 | tf_op jit(solution)/shard_map/pallas_call | solution.py:637
  128.5 1.4 collective-permute-start.12
  129.9 2.2 %collective-permute-done.12.incoming = bf16[2,512,512]{2,1,0:T(8,128)(2,1)S(1)} collective-permute-done((bf16[2,512,512]{2,1,0:T(8,128)(2,1)S(1)}, bf16[2,512,512]{2,1,0:T(8,128)(2,1)S(1)}, u32[]{:S(2)}, u32[]{:S(2)}) %collective-permute-start.12) | collective-permute-done | bytes 1048608 | tf_op jit(solution)/shard_map/ppermute | solution.py:662
  132.1 1.3 shard_map.60
  133.3 8.1 %collective-permute-start.13 = (bf16[2,256,512]{2,1,0:T(8,128)(2,1)S(1)}, bf16[2,256,512]{2,1,0:T(8,128)(2,1)S(1)}, u32[]{:S(2)}, u32[]{:S(2)}) collective-permute-start(bf16[2,256,512]{2,1,0:T(8,128)(2,1)S(1)} %get-tuple-element.35), channel_id=1, source_target_pairs={{0,0},{4,4},{16,8},{20,12},{8,16},{12,20},{24,24},{28,28},{1,1},{5... | collective-permute-start | bytes 1572872 | tf_op jit(solution)/shard_map/ppermute | solution.py:686
  141.4 1.0 collective-permute-start.14
  142.5 1.8 %collective-permute-start.16 = (bf16[2,256,512]{2,1,0:T(8,128)(2,1)S(1)}, bf16[2,256,512]{2,1,0:T(8,128)(2,1)S(1)}, u32[]{:S(2)}, u32[]{:S(2)}) collective-permute-start(bf16[2,256,512]{2,1,0:T(8,128)(2,1)S(1)} %get-tuple-element.38), channel_id=1, source_target_pairs={{20,0},{16,4},{4,8},{0,12},{28,16},{24,20},{12,24},{8,28},{21,1},{... | collective-permute-start | bytes 1572872 | tf_op jit(solution)/shard_map/ppermute | solution.py:686
  144.2 4.3 %collective-permute-done.13.rest_0_ = bf16[2,256,512]{2,1,0:T(8,128)(2,1)S(1)} collective-permute-done((bf16[2,256,512]{2,1,0:T(8,128)(2,1)S(1)}, bf16[2,256,512]{2,1,0:T(8,128)(2,1)S(1)}, u32[]{:S(2)}, u32[]{:S(2)}) %collective-permute-start.13) | collective-permute-done | bytes 524320 | tf_op jit(solution)/shard_map/ppermute | solution.py:686
  148.6 6.4 %collective-permute-done.14.rest_1_ = bf16[2,256,512]{2,1,0:T(8,128)(2,1)S(1)} collective-permute-done((bf16[2,256,512]{2,1,0:T(8,128)(2,1)S(1)}, bf16[2,256,512]{2,1,0:T(8,128)(2,1)S(1)}, u32[]{:S(2)}, u32[]{:S(2)}) %collective-permute-start.14) | collective-permute-done | bytes 524320 | tf_op jit(solution)/shard_map/ppermute | solution.py:686
  155.0 3.8 %collective-permute-done.15.rest_2_ = bf16[2,256,512]{2,1,0:T(8,128)(2,1)S(1)} collective-permute-done((bf16[2,256,512]{2,1,0:T(8,128)(2,1)S(1)}, bf16[2,256,512]{2,1,0:T(8,128)(2,1)S(1)}, u32[]{:S(2)}, u32[]{:S(2)}) %collective-permute-start.15) | collective-permute-done | bytes 524320 | tf_op jit(solution)/shard_map/ppermute | solution.py:686
  158.8 8.0 %collective-permute-done.16.rest_3_ = bf16[2,256,512]{2,1,0:T(8,128)(2,1)S(1)} collective-permute-done((bf16[2,256,512]{2,1,0:T(8,128)(2,1)S(1)}, bf16[2,256,512]{2,1,0:T(8,128)(2,1)S(1)}, u32[]{:S(2)}, u32[]{:S(2)}) %collective-permute-start.16) | collective-permute-done | bytes 524320 | tf_op jit(solution)/shard_map/ppermute | solution.py:686
  166.8 2.2 %shard_map.61 = bf16[2,256,2048]{2,1,0:T(8,128)(2,1)} custom-call(s32[5]{0:T(128)S(1)} %stack.64.place, bf16[2,256,512]{2,1,0:T(8,128)(2,1)S(1)} %collective-permute-done.13.rest_0_, bf16[2,256,512]{2,1,0:T(8,128)(2,1)S(1)} %collective-permute-done.14.rest_1_, bf16[2,256,512]{2,1,0:T(8,128)(2,1)S(1)} %collective-permute-done.15.rest_2_, ...), custom_call_target="tpu_custom_call" | custom-call | tf_op jit(solution)/shard_map/pallas_call | solution.py:688
  (46 shorter events, 13.6 us)
Async XLA Ops:
  0.1 1.6 copy-start
  1.7 0.9 copy-start.9
  3.5 0.9 copy-start.11
  8.2 1.0 copy-start.2
  10.0 37.1 %all-to-all-start = ((bf16[4,4,64,512]{3,2,1,0:T(8,128)(2,1)}), bf16[4,4,64,512]{3,2,1,0:T(8,128)(2,1)S(1)}, u32[]{:S(2)}, u32[]{:S(2)}) async-start(bf16[4,4,64,512]{3,2,1,0:T(8,128)(2,1)} %copy-done.2), calls=%async_computation | async-start | bytes 2097152 | tf_op jit(solution)/shard_map/all_to_all | solution.py:566
  15.5 16.1 %collective-permute-start = (bf16[576,512]{1,0:T(8,128)(2,1)}, bf16[576,512]{1,0:T(8,128)(2,1)S(1)}, u32[]{:S(2)}, u32[]{:S(2)}) collective-permute-start(bf16[576,512]{1,0:T(8,128)(2,1)} %get-tuple-element.23), channel_id=1, source_target_pairs={{0,0},{4,4},{8,16},{12,20},{16,8},{20,12},{24,24},{28,28},{1,1},{5... | collective-permute-start | bytes 1769480 | tf_op jit(solution)/shard_map/ppermute | solution.py:564
  19.4 26.4 %collective-permute-start.1 = (bf16[576,512]{1,0:T(8,128)(2,1)}, bf16[576,512]{1,0:T(8,128)(2,1)S(1)}, u32[]{:S(2)}, u32[]{:S(2)}) collective-permute-start(bf16[576,512]{1,0:T(8,128)(2,1)} %get-tuple-element.24), channel_id=1, source_target_pairs={{0,4},{4,0},{8,20},{12,16},{16,12},{20,8},{24,28},{28,24},{1,5},{5... | collective-permute-start | bytes 1769480 | tf_op jit(solution)/shard_map/ppermute | solution.py:564
  20.4 25.3 %collective-permute-start.2 = (bf16[576,512]{1,0:T(8,128)(2,1)}, bf16[576,512]{1,0:T(8,128)(2,1)S(1)}, u32[]{:S(2)}, u32[]{:S(2)}) collective-permute-start(bf16[576,512]{1,0:T(8,128)(2,1)} %get-tuple-element.25), channel_id=1, source_target_pairs={{0,16},{4,20},{8,0},{12,4},{16,24},{20,28},{24,8},{28,12},{1,17},{... | collective-permute-start | bytes 1769480 | tf_op jit(solution)/shard_map/ppermute | solution.py:564
  20.4 26.6 %collective-permute-start.3 = (bf16[576,512]{1,0:T(8,128)(2,1)}, bf16[576,512]{1,0:T(8,128)(2,1)S(1)}, u32[]{:S(2)}, u32[]{:S(2)}) collective-permute-start(bf16[576,512]{1,0:T(8,128)(2,1)} %copy-done.13), channel_id=1, source_target_pairs={{0,20},{4,16},{8,4},{12,0},{16,28},{20,24},{24,12},{28,8},{1,21},{... | collective-permute-start | bytes 1769480 | tf_op jit(solution)/shard_map/ppermute | solution.py:564
  47.9 14.0 %collective-permute-start.4 = (bf16[2,256,512]{2,1,0:T(8,128)(2,1)S(1)}, bf16[2,256,512]{2,1,0:T(8,128)(2,1)S(1)}, u32[]{:S(2)}, u32[]{:S(2)}) collective-permute-start(bf16[2,256,512]{2,1,0:T(8,128)(2,1)S(1)} %get-tuple-element.27.x_column), channel_id=1, source_target_pairs={{0,4},{4,0},{1,5},{5,1},{2,6},{6,2},{3,7},{7,3},{8,12},{12,8},{9,1... | collective-permute-start | bytes 1572872 | tf_op jit(solution)/shard_map/ppermute | solution.py:582
  48.2 13.6 %collective-permute-start.6 = (bf16[2,256,512]{2,1,0:T(8,128)(2,1)S(1)}, bf16[2,256,512]{2,1,0:T(8,128)(2,1)S(1)}, u32[]{:S(2)}, u32[]{:S(2)}) collective-permute-start(bf16[2,256,512]{2,1,0:T(8,128)(2,1)S(1)} %get-tuple-element.28), channel_id=1, source_target_pairs={{0,16},{4,20},{8,0},{12,4},{16,24},{20,28},{24,8},{28,12},{1,17},{... | collective-permute-start | bytes 1572872 | tf_op jit(solution)/shard_map/ppermute | solution.py:579
  49.5 13.0 %collective-permute-start.5 = (bf16[2,256,512]{2,1,0:T(8,128)(2,1)S(1)}, bf16[2,256,512]{2,1,0:T(8,128)(2,1)S(1)}, u32[]{:S(2)}, u32[]{:S(2)}) collective-permute-start(bf16[2,256,512]{2,1,0:T(8,128)(2,1)S(1)} %get-tuple-element.28), channel_id=1, source_target_pairs={{0,0},{4,4},{8,16},{12,20},{16,8},{20,12},{24,24},{28,28},{1,1},{5... | collective-permute-start | bytes 1572872 | tf_op jit(solution)/shard_map/ppermute | solution.py:579
  61.8 2.3 %copy-start.3 = (bf16[2,256,512]{2,1,0:T(8,128)(2,1)}, bf16[2,256,512]{2,1,0:T(8,128)(2,1)S(1)}, u32[]{:S(2)}) copy-start(bf16[2,256,512]{2,1,0:T(8,128)(2,1)S(1)} %collective-permute-done.6.y1.y2) | copy-start | bytes 1572868
  62.5 1.6 copy-start.6
  64.1 1.0 copy-start.1
  65.1 1.0 copy-start.12
  66.1 11.1 %copy-start.14 = (s32[16]{0:T(128)S(1)}, s32[16]{0:T(128)}, u32[]{:S(2)}) copy-start(s32[16]{0:T(128)} %param.6) | copy-start | bytes 196
  66.1 31.6 %all-to-all-start.1 = ((bf16[4,4,64,512]{3,2,1,0:T(8,128)(2,1)}), bf16[4,4,64,512]{3,2,1,0:T(8,128)(2,1)S(1)}, u32[]{:S(2)}, u32[]{:S(2)}) async-start(bf16[4,4,64,512]{3,2,1,0:T(8,128)(2,1)} %copy-done.1), calls=%async_computation.1 | async-start | bytes 2097152 | tf_op jit(solution)/shard_map/all_to_all | solution.py:602
  71.0 21.9 %collective-permute-start.8 = (bf16[2,2,256,512]{3,2,1,0:T(8,128)(2,1)}, bf16[2,2,256,512]{3,2,1,0:T(8,128)(2,1)}, u32[]{:S(2)}, u32[]{:S(2)}) collective-permute-start(bf16[2,2,256,512]{3,2,1,0:T(8,128)(2,1)} %copy-done.12), channel_id=1, source_target_pairs={{0,16},{4,20},{8,0},{12,4},{16,24},{20,28},{24,8},{28,12},{1,17},{... | collective-permute-start | bytes 3145736 | tf_op jit(solution)/shard_map/ppermute | solution.py:579
  71.1 26.5 %collective-permute-start.7 = (bf16[2,2,256,512]{3,2,1,0:T(8,128)(2,1)}, bf16[2,2,256,512]{3,2,1,0:T(8,128)(2,1)}, u32[]{:S(2)}, u32[]{:S(2)}) collective-permute-start(bf16[2,2,256,512]{3,2,1,0:T(8,128)(2,1)} %copy-done.12), channel_id=1, source_target_pairs={{0,0},{4,4},{8,16},{12,20},{16,8},{20,12},{24,24},{28,28},{1,1},{5... | collective-permute-start | bytes 3145736 | tf_op jit(solution)/shard_map/ppermute | solution.py:579
  75.7 8.6 %collective-permute-start.10 = (bf16[2,256,512]{2,1,0:T(8,128)(2,1)}, bf16[2,256,512]{2,1,0:T(8,128)(2,1)}, u32[]{:S(2)}, u32[]{:S(2)}) collective-permute-start(bf16[2,256,512]{2,1,0:T(8,128)(2,1)} %copy-done.3), channel_id=1, source_target_pairs={{0,4},{4,0},{1,5},{5,1},{2,6},{6,2},{3,7},{7,3},{8,12},{12,8},{9,1... | collective-permute-start | bytes 1572872 | tf_op jit(solution)/shard_map/ppermute | solution.py:582
  77.0 15.8 %collective-permute-start.9 = (bf16[2,256,512]{2,1,0:T(8,128)(2,1)}, bf16[2,256,512]{2,1,0:T(8,128)(2,1)}, u32[]{:S(2)}, u32[]{:S(2)}) collective-permute-start(bf16[2,256,512]{2,1,0:T(8,128)(2,1)} %copy-done.6), channel_id=1, source_target_pairs={{0,4},{4,0},{1,5},{5,1},{2,6},{6,2},{3,7},{7,3},{8,12},{12,8},{9,1... | collective-permute-start | bytes 1572872 | tf_op jit(solution)/shard_map/ppermute | solution.py:582
  97.7 1.0 copy-start.4
  98.7 1.0 copy-start.7
  99.7 16.3 %copy-start.5 = (bf16[2,256,512]{2,1,0:T(8,128)(2,1)S(1)}, bf16[2,256,512]{2,1,0:T(8,128)(2,1)}, u32[]{:S(2)}) copy-start(bf16[2,256,512]{2,1,0:T(8,128)(2,1)} %copy-done.3) | copy-start | bytes 1572868
  99.7 16.3 %copy-start.8 = (bf16[2,256,512]{2,1,0:T(8,128)(2,1)S(1)}, bf16[2,256,512]{2,1,0:T(8,128)(2,1)}, u32[]{:S(2)}) copy-start(bf16[2,256,512]{2,1,0:T(8,128)(2,1)} %copy-done.6) | copy-start | bytes 1572868
  100.7 15.4 %collective-permute-start.11 = (bf16[2,512,512]{2,1,0:T(8,128)(2,1)S(1)}, bf16[2,512,512]{2,1,0:T(8,128)(2,1)S(1)}, u32[]{:S(2)}, u32[]{:S(2)}) collective-permute-start(bf16[2,512,512]{2,1,0:T(8,128)(2,1)S(1)} %get-tuple-element.32.w_high), channel_id=1, source_target_pairs={{0,8},{16,24},{1,9},{17,25},{2,10},{18,26},{3,11},{19,27},{4,12},{... | collective-permute-start | bytes 3145736 | tf_op jit(solution)/shard_map/ppermute | solution.py:636
  128.5 3.6 %collective-permute-start.12 = (bf16[2,512,512]{2,1,0:T(8,128)(2,1)S(1)}, bf16[2,512,512]{2,1,0:T(8,128)(2,1)S(1)}, u32[]{:S(2)}, u32[]{:S(2)}) collective-permute-start(bf16[2,512,512]{2,1,0:T(8,128)(2,1)S(1)} %get-tuple-element.33), channel_id=1, source_target_pairs={{8,0},{24,16},{9,1},{25,17},{10,2},{26,18},{11,3},{27,19},{12,4},{... | collective-permute-start | bytes 3145736 | tf_op jit(solution)/shard_map/ppermute | solution.py:662
  133.3 15.2 %collective-permute-start.13 = (bf16[2,256,512]{2,1,0:T(8,128)(2,1)S(1)}, bf16[2,256,512]{2,1,0:T(8,128)(2,1)S(1)}, u32[]{:S(2)}, u32[]{:S(2)}) collective-permute-start(bf16[2,256,512]{2,1,0:T(8,128)(2,1)S(1)} %get-tuple-element.35), channel_id=1, source_target_pairs={{0,0},{4,4},{16,8},{20,12},{8,16},{12,20},{24,24},{28,28},{1,1},{5... | collective-permute-start | bytes 1572872 | tf_op jit(solution)/shard_map/ppermute | solution.py:686
  141.4 13.5 %collective-permute-start.14 = (bf16[2,256,512]{2,1,0:T(8,128)(2,1)S(1)}, bf16[2,256,512]{2,1,0:T(8,128)(2,1)S(1)}, u32[]{:S(2)}, u32[]{:S(2)}) collective-permute-start(bf16[2,256,512]{2,1,0:T(8,128)(2,1)S(1)} %get-tuple-element.36), channel_id=1, source_target_pairs={{4,0},{0,4},{20,8},{16,12},{12,16},{8,20},{28,24},{24,28},{5,1},{1... | collective-permute-start | bytes 1572872 | tf_op jit(solution)/shard_map/ppermute | solution.py:686
  142.5 16.3 %collective-permute-start.15 = (bf16[2,256,512]{2,1,0:T(8,128)(2,1)S(1)}, bf16[2,256,512]{2,1,0:T(8,128)(2,1)S(1)}, u32[]{:S(2)}, u32[]{:S(2)}) collective-permute-start(bf16[2,256,512]{2,1,0:T(8,128)(2,1)S(1)} %get-tuple-element.37), channel_id=1, source_target_pairs={{16,0},{20,4},{0,8},{4,12},{24,16},{28,20},{8,24},{12,28},{17,1},{... | collective-permute-start | bytes 1572872 | tf_op jit(solution)/shard_map/ppermute | solution.py:686
  142.5 24.3 %collective-permute-start.16 = (bf16[2,256,512]{2,1,0:T(8,128)(2,1)S(1)}, bf16[2,256,512]{2,1,0:T(8,128)(2,1)S(1)}, u32[]{:S(2)}, u32[]{:S(2)}) collective-permute-start(bf16[2,256,512]{2,1,0:T(8,128)(2,1)S(1)} %get-tuple-element.38), channel_id=1, source_target_pairs={{20,0},{16,4},{4,8},{0,12},{28,16},{24,20},{12,24},{8,28},{21,1},{... | collective-permute-start | bytes 1572872 | tf_op jit(solution)/shard_map/ppermute | solution.py:686
  (2 other events, 1.7 us)

commit v5 on v4

--- a/solution.py
+++ b/solution.py
@@ -15,7 +15,7 @@
 in_smem = pl.BlockSpec(memory_space=pltpu.SMEM)
 in_vmem = pl.BlockSpec(memory_space=pltpu.VMEM)
 
-info_member, info_piece, info_slot, info_half = 3, 4, 12, 14
+info_member, info_piece, info_slot, info_half, info_block = 3, 4, 12, 14, 16
 
 
 def shifted(x, axis, by):
@@ -161,15 +161,15 @@
     return [slice(first, first + step) for first in range(0, order, step)]
 
 
-def pack_kernel(place, field, coupling, x_factor, y_factor, *rest):
-    pieces, (blocks, sems, csems, fsems) = rest[:-4], rest[-4:]
+def pack_kernel(place, field, coupling, *rest):
+    pieces, (sems, csems) = rest[:-2], rest[-2:]
     copies = []
-    height = x_factor.shape[1]
-    own = pl.ds(pl.multiple_of(place[len(pieces)] * height, height), height)
     for index, piece in enumerate(pieces):
         width = piece.shape[1]
         offset = pl.multiple_of(place[index] * width, width)
         rows_here = field.shape[1]
+        height = piece.shape[0] - 2 * rows_here
+        own = pl.ds(pl.multiple_of(place[len(pieces)] * height, height), height)
         for plane in range(2):
             copies.append(
                 pltpu.make_async_copy(
@@ -183,13 +183,6 @@
                 coupling.at[own], piece.at[pl.ds(2 * rows_here, height)], csems.at[index]
             )
         )
-    for target in range(blocks.shape[0]):
-        for which, factor in enumerate((x_factor, y_factor)):
-            copies.append(
-                pltpu.make_async_copy(
-                    factor, blocks.at[target, pl.ds(2 * which, 2)], fsems.at[target, which]
-                )
-            )
     start_all(copies)
     wait_all(copies)
 
@@ -207,53 +200,52 @@
     wait_all(copies)
 
 
-def column_kernel(blocks, p0, p1, p2, p3, x_column, y_column, sems):
-    height = blocks.shape[2]
+def column_kernel(blocks, p0, p1, p2, p3, x_column, y_turned, rows_held, sems, csems):
+    count, planes, height, order = blocks.shape
     copies = []
-    for index in range(blocks.shape[0]):
-        rows = pl.ds(index * height, height)
-        for which, column in enumerate((x_column, y_column)):
+    for index in range(count):
+        copies.append(
+            pltpu.make_async_copy(
+                blocks.at[index, pl.ds(0, 2)],
+                x_column.at[:, pl.ds(index * height, height), :],
+                sems.at[index],
+            )
+        )
+    for index, piece in enumerate((p0, p1, p2, p3)):
+        copies.append(
+            pltpu.make_async_copy(
+                piece.at[pl.ds(piece.shape[0] - height, height)], rows_held.at[index], csems.at[index]
+            )
+        )
+    start_all(copies)
+    for plane in range(2):
+        column = blocks[:, 2 + plane].reshape(count * height, order)
+        y_turned[plane] = column.astype(f32).T.astype(bf16)
+    wait_all(copies)
+
+
+def both_kernel(x_column, x_aside, y0, y1, rows_held, rows_next, x_both, y_both, rows_both, sems):
+    copies = []
+    for target, parts in ((x_both, (x_column, x_aside)), (y_both, (y0, y1)), (rows_both, (rows_held, rows_next))):
+        for index, part in enumerate(parts):
+            copies.append(pltpu.make_async_copy(part, target.at[index], sems.at[len(copies)]))
+    start_all(copies)
+    wait_all(copies)
+
+
+def weight_copies(info, near, far, weights, sems):
+    height = near.shape[2]
+    half_height = weights.shape[1] // 2
+    copies = []
+    for index in range(4):
+        block = (near if index < 2 else far).at[index % 2]
+        for turn in range(near.shape[1]):
+            slot, half = info[info_piece + 2 * turn], info[info_piece + 2 * turn + 1]
+            start = half * half_height + info[info_block + index] * height
+            rows = pl.ds(pl.multiple_of(start, height), height)
             copies.append(
                 pltpu.make_async_copy(
-                    blocks.at[index, pl.ds(2 * which, 2)],
-                    column.at[:, rows, :],
-                    sems.at[index, which],
-                )
-            )
-    start_all(copies)
-    wait_all(copies)
-
-
-def both_kernel(x_column, x_aside, y0, y1, p0, p1, p2, p3, x_both, rows_held, sems, csems):
-    copies = [
-        pltpu.make_async_copy(x_column, x_both.at[0], sems.at[0]),
-        pltpu.make_async_copy(x_aside, x_both.at[1], sems.at[1]),
-    ]
-    height = rows_held.shape[2]
-    for target in range(rows_held.shape[0]):
-        for index, piece in enumerate((p0, p1, p2, p3)):
-            copies.append(
-                pltpu.make_async_copy(
-                    piece.at[pl.ds(piece.shape[0] - height, height)],
-                    rows_held.at[target, index],
-                    csems.at[target, index],
-                )
-            )
-    start_all(copies)
-    wait_all(copies)
-
-
-def weight_copies(info, blocks, weights, sems):
-    height = blocks.shape[2]
-    half_height = weights.shape[1] // 2
-    copies = []
-    for index in range(blocks.shape[0]):
-        for turn in range(blocks.shape[1]):
-            slot, half = info[info_piece + 2 * turn], info[info_piece + 2 * turn + 1]
-            rows = pl.ds(pl.multiple_of(half * half_height + index * height, height), height)
-            copies.append(
-                pltpu.make_async_copy(
-                    blocks.at[index, turn], weights.at[slot, rows, :], sems.at[index, turn]
+                    block.at[turn], weights.at[slot, rows, :], sems.at[index, turn]
                 )
             )
     return copies
@@ -264,38 +256,36 @@
 
 
 class Factors:
-    def __init__(self, info, columns, held, sems):
-        self.order, self.held, self.sems, self.columns = held.shape[2], held, sems, columns
-        height = columns[0][0].shape[1]
+    def __init__(self, info, x_columns, y_columns, held_x, held_y, sems):
+        self.order, self.held_x, self.held_y = held_x.shape[1], held_x, held_y
+        self.sems, self.columns = sems, (x_columns, y_columns)
         for which in (1, 0):
-            for index, column in enumerate(columns[which]):
+            for index, column in enumerate(self.columns[which]):
                 slot, half = info[info_slot + index // 2], info[info_half + index % 2]
-                rows = pl.ds(pl.multiple_of(half * height, height), height)
                 for plane in range(2):
-                    self.copy(column, plane, slot, which, rows, index % 2).start()
-
-    def copy(self, column, plane, slot, which, rows, half):
-        target = self.held.at[slot, which, rows, pl.ds(plane * self.order, self.order)]
+                    self.copy(column, which, plane, slot, half, index % 2).start()
+
+    def copy(self, column, which, plane, slot, half, place):
+        size = self.order // 2
+        part = pl.ds(half * size if isinstance(half, int) else pl.multiple_of(half * size, size), size)
+        across = pl.ds(plane * self.order, self.order)
+        target = self.held_y.at[slot, across, part] if which else self.held_x.at[slot, part, across]
         return pltpu.make_async_copy(
-            column.at[plane], target, self.sems.at[slot, which, half, plane]
+            column.at[plane], target, self.sems.at[slot, which, place, plane]
         )
 
     def ready(self, slot, which):
-        column = self.columns[which][0]
-        height = column.shape[1]
-        for half in range(2):
+        for place in range(2):
             for plane in range(2):
-                rows = pl.ds(half * height, height)
-                self.copy(column, plane, slot, which, rows, half).wait()
+                self.copy(self.columns[which][0], which, plane, slot, place, place).wait()
 
     def apply(self, slot, beside, below, store, fresh):
         order = self.order
-        turned = (((1,), (1,)), ((), ()))
         if fresh:
             self.ready(slot, 1)
-        for columns in row_chunks(order, 512):
-            part = lax.dot_general(
-                beside[...], self.held[slot, 1, columns], turned, preferred_element_type=f32
+        for columns in row_chunks(order, 256):
+            part = jnp.dot(
+                beside[...], self.held_y[slot, :, columns], preferred_element_type=f32
             ).astype(bf16)
             real, imag = part[:order], part[order:]
             further = slice(columns.start + order, columns.stop + order)
@@ -306,12 +296,12 @@
         if fresh:
             self.ready(slot, 0)
         for plane in range(2):
-            for columns in row_chunks(order, 512):
+            for columns in row_chunks(order, 256):
                 along = slice(columns.start + plane * order, columns.stop + plane * order)
                 store(
                     plane,
                     columns,
-                    jnp.dot(self.held[slot, 0], below[:, along], preferred_element_type=f32),
+                    jnp.dot(self.held_x[slot], below[:, along], preferred_element_type=f32),
                 )
 
 
@@ -395,14 +385,16 @@
     return copies
 
 
-def first_kernel(info, x0, x1, y0, y1, y2, y3, coupling, p0, p1, p2, p3, w_low, w_high,
-                 held, weights, rhs, beside, below, sems, csems, fsems):
+def first_kernel(info, x0, x1, y0, y1, y2, near, far, p0, p1, p2, p3, w_low, w_high,
+                 held_x, held_y, weights, rhs, beside, below, sems, csems, fsems):
     @pl.when(info[info_member] == 0)
     def _():
         early = rhs_copies(info, (p0, p1, p2, p3), rhs, sems)
-        early += weight_copies(info, coupling, weights, csems)
+        early += weight_copies(info, near, far, weights, csems)
         start_all(early)
-        factors = Factors(info, (halves(x0, x1), (y0, y1, y2, y3)), held, fsems)
+        factors = Factors(
+            info, halves(x0, x1), (y0, y2.at[0], y1, y2.at[1]), held_x, held_y, fsems
+        )
         wait_all(early)
         reduce_into(beside, rhs, info, 0, weights, lambda *where: f32(0.0))
         factors.apply(0, beside, below, round_into(w_low), True)
@@ -412,16 +404,18 @@
         factors.apply(1, beside, below, round_into(w_high), True)
 
 
-def last_kernel(info, x0, x1, y0, y1, y2, y3, coupling, p0, p1, p2, p3, incoming, field,
-                sent, held, weights, rhs, arrived, kept, beside, below, sems, csems, fsems,
+def last_kernel(info, x0, x1, y0, y1, y2, near, far, p0, p1, p2, p3, incoming, field,
+                sent, held_x, held_y, weights, rhs, arrived, kept, beside, below, sems, csems, fsems,
                 osems):
     @pl.when(info[info_member] == 1)
     def _():
         early = rhs_copies(info, (p0, p1, p2, p3), rhs, sems)
-        early += weight_copies(info, coupling, weights, csems)
+        early += weight_copies(info, near, far, weights, csems)
         early.append(pltpu.make_async_copy(incoming, arrived, sems.at[8]))
         start_all(early)
-        factors = Factors(info, (halves(x0, x1), (y0, y1, y2, y3)), held, fsems)
+        factors = Factors(
+            info, halves(x0, x1), (y0, y2.at[0], y1, y2.at[1]), held_x, held_y, fsems
+        )
         wait_all(early)
         order = beside.shape[0] // 2
         reduce_into(
@@ -452,15 +446,17 @@
         out_low.wait()
 
 
-def back_kernel(info, x0, x1, y0, y1, y2, y3, coupling, w_low, w_high, incoming, field,
-                p0, p1, p2, p3, held, weights, kept, arrived, beside, below, sems, csems, fsems,
+def back_kernel(info, x0, x1, y0, y1, y2, near, far, w_low, w_high, incoming, field,
+                p0, p1, p2, p3, held_x, held_y, weights, kept, arrived, beside, below, sems, csems, fsems,
                 osems):
     @pl.when(info[info_member] == 0)
     def _():
         early = [pltpu.make_async_copy(incoming, arrived, sems.at[0])]
         start_all(early)
-        factors = Factors(info, (halves(x0, x1), (y0, y1, y2, y3)), held, fsems)
-        early += weight_copies(info, coupling, weights, csems)
+        factors = Factors(
+            info, halves(x0, x1), (y0, y2.at[0], y1, y2.at[1]), held_x, held_y, fsems
+        )
+        early += weight_copies(info, near, far, weights, csems)
         early += [
             pltpu.make_async_copy(w_low, kept.at[0], sems.at[2]),
             pltpu.make_async_copy(w_high, kept.at[1], sems.at[3]),
@@ -541,37 +537,44 @@
     for a, b in rounds:
         entries += [(group + a) % 2, (own_x - b) % px_count]
     entries += [group, (group + 1) % 2, own_x, (own_x + 1) % 2]
+    pair = own_y // 2 * 2
+    entries += [own_y, pair + (own_y + 1) % 2, (own_y + 2) % 4, (pair + 2) % 4 + (own_y + 1) % 2]
     info = jnp.stack([jnp.asarray(entry, jnp.int32) for entry in entries])
 
     sends_to = jnp.stack(
         [((member + a) % 2) * px_count + (own_x + b) % px_count for a, b in rounds] + [own_y]
     ).astype(jnp.int32)
     piece_shape = jax.ShapeDtypeStruct((2, rows_here, order), bf16)
-    *pieces, blocks = pl.pallas_call(
+    shard = jnp.concatenate([x_factor[0], y_factor[0]], axis=0)
+    blocks = jnp.broadcast_to(shard[None], (py_count,) + shard.shape)
+    blocks = lax.all_to_all(blocks, "py", split_axis=0, concat_axis=0, tiled=True)
+    pieces = pl.pallas_call(
         pack_kernel,
-        out_shape=[jax.ShapeDtypeStruct((2 * rows_here + height, order), bf16)] * len(rounds)
-        + [jax.ShapeDtypeStruct((py_count, 4, height, order), bf16)],
-        in_specs=[in_smem] + [anywhere] * 4,
-        out_specs=[in_vmem] * (len(rounds) + 1),
+        out_shape=[jax.ShapeDtypeStruct((2 * rows_here + height, order), bf16)] * len(rounds),
+        in_specs=[in_smem] + [anywhere] * 2,
+        out_specs=[in_vmem] * len(rounds),
         scratch_shapes=[
             pltpu.SemaphoreType.DMA((len(rounds), 2)),
             pltpu.SemaphoreType.DMA((len(rounds),)),
-            pltpu.SemaphoreType.DMA((py_count, 2)),
         ],
-        compiler_params=params,
-    )(sends_to, field, coupling[0], x_factor[0], y_factor[0])
+        compiler_params=pltpu.CompilerParams(vmem_limit_bytes=60 * 1024 * 1024),
+    )(sends_to, field, coupling[0])
     pieces = [
         lax.ppermute(piece, ("sec", "px"), pairs(a, b)) for piece, (a, b) in zip(pieces, rounds)
     ]
-    blocks = lax.all_to_all(blocks, "py", split_axis=0, concat_axis=0, tiled=True)
 
     column_shape = jax.ShapeDtypeStruct((2, rows_here, order), bf16)
-    x_column, y_column = pl.pallas_call(
+    turned_shape = jax.ShapeDtypeStruct((2, order, rows_here), bf16)
+    rows_shape = jax.ShapeDtypeStruct((len(rounds), height, order), bf16)
+    x_column, y_turned, rows_held = pl.pallas_call(
         column_kernel,
-        out_shape=[column_shape] * 2,
-        in_specs=[anywhere] * 5,
-        out_specs=[in_vmem] * 2,
-        scratch_shapes=[pltpu.SemaphoreType.DMA((py_count, 2))],
+        out_shape=[column_shape, turned_shape, rows_shape],
+        in_specs=[in_vmem] + [anywhere] * 4,
+        out_specs=[in_vmem] * 3,
+        scratch_shapes=[
+            pltpu.SemaphoreType.DMA((py_count,)),
+            pltpu.SemaphoreType.DMA((len(rounds),)),
+        ],
         compiler_params=params,
     )(blocks, *pieces)
 
@@ -581,29 +584,31 @@
     def aside(block):
         return lax.ppermute(block, "px", [(y, (y + 1) % 2) for y in range(2)])
 
+    def over_z(block, bit):
+        return lax.ppermute(block, "py", [(z, z ^ bit) for z in range(py_count)])
+
+    y_near = [across(y_turned, a) for a in range(2)]
     x_aside = aside(x_column)
-    y_near = [across(y_column, a) for a in range(2)]
-    x_both, rows_held = pl.pallas_call(
+    rows_next = over_z(rows_held, 1)
+    twice = [
+        jax.ShapeDtypeStruct((2,) + one.shape, bf16) for one in (column_shape, turned_shape, rows_shape)
+    ]
+    x_both, y_both, rows_both = pl.pallas_call(
         both_kernel,
-        out_shape=[
-            jax.ShapeDtypeStruct((2, 2, rows_here, order), bf16),
-            jax.ShapeDtypeStruct((py_count, len(rounds), height, order), bf16),
-        ],
-        in_specs=[anywhere] * 8,
-        out_specs=[in_vmem] * 2,
-        scratch_shapes=[
-            pltpu.SemaphoreType.DMA((2,)),
-            pltpu.SemaphoreType.DMA((py_count, len(rounds))),
-        ],
+        out_shape=twice,
+        in_specs=[anywhere] * 6,
+        out_specs=[in_vmem] * 3,
+        scratch_shapes=[pltpu.SemaphoreType.DMA((6,))],
         compiler_params=params,
-    )(x_column, x_aside, *y_near, *pieces)
-    y_far = [aside(block) for block in y_near]
+    )(x_column, x_aside, *y_near, rows_held, rows_next)
+    y_far = aside(y_both)
     x_across = [across(x_both, a) for a in range(2)]
-    weights = lax.all_to_all(rows_held, "py", split_axis=0, concat_axis=0, tiled=True)
-    factors = x_across + [y_near[0], y_far[0], y_near[1], y_far[1]]
+    rows_far = over_z(rows_both, 2)
+    factors = x_across + [*y_near, y_far, rows_both, rows_far]
 
     full_shape = jax.ShapeDtypeStruct((2, order, order), bf16)
-    factor_scratch = pltpu.VMEM((2, 2, order, 2 * order), bf16)
+    x_scratch = pltpu.VMEM((2, order, 2 * order), bf16)
+    y_scratch = pltpu.VMEM((2, 2 * order, order), bf16)
     arrived_scratch = pltpu.VMEM((2, order, order), bf16)
     weight_scratch = pltpu.VMEM((2, order, order), bf16)
     field_scratch = pltpu.VMEM((2, 2, order, order), bf16)
@@ -617,7 +622,8 @@
         in_specs=[in_smem] + [anywhere] * 11,
         out_specs=[in_vmem] * 2,
         scratch_shapes=[
-            factor_scratch,
+            x_scratch,
+            y_scratch,
             weight_scratch,
             field_scratch,
             beside_scratch,
@@ -630,7 +636,7 @@
         cost_estimate=pl.CostEstimate(
             flops=2 * solve_flops, bytes_accessed=16 * order * order * 2, transcendentals=0
         ),
-    )(info, *factors, weights, *pieces)
+    )(info, *factors, *pieces)
 
     up = [(2 * x, 2 * x + 1) for x in range(groups)]
     incoming = lax.ppermute(w_high, "sec", up)
@@ -640,7 +646,8 @@
         in_specs=[in_smem] + [anywhere] * 12,
         out_specs=[anywhere, in_vmem],
         scratch_shapes=[
-            factor_scratch,
+            x_scratch,
+            y_scratch,
             weight_scratch,
             field_scratch,
             arrived_scratch,
@@ -656,7 +663,7 @@
         cost_estimate=pl.CostEstimate(
             flops=3 * solve_flops, bytes_accessed=16 * order * order * 2, transcendentals=0
         ),
-    )(info, *factors, weights, *pieces, incoming)
+    )(info, *factors, *pieces, incoming)
 
     down = [(target, source) for source, target in up]
     incoming = lax.ppermute(sent, "sec", down)
@@ -666,7 +673,8 @@
         in_specs=[in_smem] + [anywhere] * 11,
         out_specs=[anywhere] * len(rounds),
         scratch_shapes=[
-            factor_scratch,
+            x_scratch,
+            y_scratch,
             weight_scratch,
             field_scratch,
             arrived_scratch,
@@ -681,7 +689,7 @@
         cost_estimate=pl.CostEstimate(
             flops=2 * solve_flops, bytes_accessed=16 * order * order * 2, transcendentals=0
         ),
-    )(info, *factors, weights, w_low, w_high, incoming, solved)
+    )(info, *factors, w_low, w_high, incoming, solved)
     results = [
         lax.ppermute(piece, ("sec", "px"), back_pairs(a, b)) for piece, (a, b) in zip(results, rounds)
     ]

time: 170 us -> 159 us (0.935)
  local copies, waits for them, and re-layouts: 10.9 us -> 2.37 us
  waiting for transfers between devices: 90.8 us -> 88.5 us
    ppermute x0 -> x2, waiting for transfers between devices: none -> 24.7 us  [over_z(): return lax.ppermute(block, 'py', [(z, z ^ bit) for z in range(py_count)])]
    ppermute x3 -> x2, waiting for transfers between devices: 22.1 us -> 1.72 us  [aside(): return lax.ppermute(block, 'px', [(y, (y + 1) % 2) for y in range(2)])]
    unnamed x30 -> x4, local copies, waits for them, and re-layouts: 10.2 us -> 0.01 us
    all_to_all x1 -> x0, starting transfers between devices: 4.94 us -> none  [on_device(): lax.all_to_all(rows_held, 'py', split_axis=0, concat_axis=0, tiled=True)]
    ppermute x4, waiting for transfers between devices: 5.49 us -> 0.67 us  [across(): return lax.ppermute(block, ('sec', 'px'), pairs(a, 0))]
    ppermute x0 -> x2, starting transfers between devices: none -> 4.52 us  [over_z(): return lax.ppermute(block, 'py', [(z, z ^ bit) for z in range(py_count)])]
    ppermute x1, waiting for transfers between devices: 14.1 us -> 12 us  [on_device(): incoming = lax.ppermute(w_high, 'sec', up)]
  transfers between devices with their start and end apart: 19 -> 19, of which waited for: 15 -> 13; matrix products, arithmetic and copies ran while one was open for 0% -> 1% of each run, Pallas kernels for 0% -> 2%
where the time goes in v5:
time: 159 us; the launch traced here: 158 us
  waiting for transfers between devices  88.5 us (56%)
  starting transfers between devices  41.1 us (26%)
  Pallas kernels  22.3 us (14%)
  between operations  2.74 us (2%)
  local copies, waits for them, and re-layouts  2.37 us (1%)
    ppermute x2, waiting for transfers between devices, over_z(): return lax.ppermute(block, 'py', [(z, z ^ bit) for z in range(py_count)])  24.7 us
    ppermute x4, waiting for transfers between devices, on_device(): lax.ppermute(piece, ('sec', 'px'), pairs(a, b))  24.4 us
    ppermute x4, waiting for transfers between devices, on_device(): lax.ppermute(piece, ('sec', 'px'), back_pairs(a, b))  22.7 us
    ppermute x1, waiting for transfers between devices, on_device(): incoming = lax.ppermute(w_high, 'sec', up)  12 us
    pallas_call x1, Pallas kernels, on_device(): pl.pallas_call(last_kernel, out_shape=[jax.ShapeDtypeStruct((2, 2, order,...  11.4 us
    ppermute x4, starting transfers between devices, on_device(): lax.ppermute(piece, ('sec', 'px'), back_pairs(a, b))  11.1 us
    ppermute x4, starting transfers between devices, across(): return lax.ppermute(block, ('sec', 'px'), pairs(a, 0))  8.47 us
    ppermute x4, starting transfers between devices, on_device(): lax.ppermute(piece, ('sec', 'px'), pairs(a, b))  7.23 us
  transfers between devices with their start and end apart: 19, of which 13 were waited for; matrix products, arithmetic and copies ran while one was open for 1% of the time, Pallas kernels for 2%

profile of v5, /device:TPU:1, one launch (start us, length us, event | category | flops | bytes accessed | tf_op | source)
XLA Modules:
  0.0 157.9 jit_solution(1143369713145844224)
XLA Ops:
  1.0 1.1 broadcast_in_dim.4
  2.1 5.4 %all-to-all-start = ((bf16[4,4,64,512]{3,2,1,0:T(8,128)(2,1)}), bf16[4,4,64,512]{3,2,1,0:T(8,128)(2,1)S(1)}, u32[]{:S(2)}, u32[]{:S(2)}) async-start(bf16[4,4,64,512]{3,2,1,0:T(8,128)(2,1)} %broadcast_in_dim.4), calls=%async_computation | async-start | bytes 2097152 | tf_op jit(solution)/shard_map/all_to_all | solution.py:550
  8.1 3.8 %shard_map.55 = (bf16[576,512]{1,0:T(8,128)(2,1)}, bf16[576,512]{1,0:T(8,128)(2,1)}, bf16[576,512]{1,0:T(8,128)(2,1)}, bf16[576,512]{1,0:T(8,128)(2,1)}) custom-call(s32[5]{0:T(128)} %stack.74.place, bf16[2,256,2048]{2,1,0:T(8,128)(2,1)} %bitcast.27, bf16[256,512]{1,0:T(8,128)(2,1)} %bitcast.28), custom_call_target="tpu_custom_call" | custom-call | tf_op jit(solution)/shard_map/pallas_call | solution.py:551
  11.9 4.0 %collective-permute-start = (bf16[576,512]{1,0:T(8,128)(2,1)}, bf16[576,512]{1,0:T(8,128)(2,1)S(1)}, u32[]{:S(2)}, u32[]{:S(2)}) collective-permute-start(bf16[576,512]{1,0:T(8,128)(2,1)} %get-tuple-element.23), channel_id=1, source_target_pairs={{0,0},{4,4},{8,16},{12,20},{16,8},{20,12},{24,24},{28,28},{1,1},{5... | collective-permute-start | bytes 1769480 | tf_op jit(solution)/shard_map/ppermute | solution.py:563
  15.8 1.0 collective-permute-start.1
  16.9 2.2 %collective-permute-start.3 = (bf16[576,512]{1,0:T(8,128)(2,1)}, bf16[576,512]{1,0:T(8,128)(2,1)S(1)}, u32[]{:S(2)}, u32[]{:S(2)}) collective-permute-start(bf16[576,512]{1,0:T(8,128)(2,1)} %get-tuple-element.26), channel_id=1, source_target_pairs={{0,20},{4,16},{8,4},{12,0},{16,28},{20,24},{24,12},{28,8},{1,21},{... | collective-permute-start | bytes 1769480 | tf_op jit(solution)/shard_map/ppermute | solution.py:563
  19.1 8.8 %collective-permute-done.p0 = bf16[576,512]{1,0:T(8,128)(2,1)S(1)} collective-permute-done((bf16[576,512]{1,0:T(8,128)(2,1)}, bf16[576,512]{1,0:T(8,128)(2,1)S(1)}, u32[]{:S(2)}, u32[]{:S(2)}) %collective-permute-start) | collective-permute-done | bytes 589856 | tf_op jit(solution)/shard_map/ppermute | solution.py:563
  27.9 14.3 %collective-permute-done.1.p1 = bf16[576,512]{1,0:T(8,128)(2,1)S(1)} collective-permute-done((bf16[576,512]{1,0:T(8,128)(2,1)}, bf16[576,512]{1,0:T(8,128)(2,1)S(1)}, u32[]{:S(2)}, u32[]{:S(2)}) %collective-permute-start.1) | collective-permute-done | bytes 589856 | tf_op jit(solution)/shard_map/ppermute | solution.py:563
  42.2 1.3 collective-permute-done.3.p3
  44.9 1.3 collective-permute-start.6
  46.2 2.5 %collective-permute-start.5 = (bf16[2,512,256]{2,1,0:T(8,128)(2,1)S(1)}, bf16[2,512,256]{2,1,0:T(8,128)(2,1)S(1)}, u32[]{:S(2)}, u32[]{:S(2)}) collective-permute-start(bf16[2,512,256]{2,1,0:T(8,128)(2,1)S(1)} %get-tuple-element.28), channel_id=1, source_target_pairs={{0,0},{4,4},{8,16},{12,20},{16,8},{20,12},{24,24},{28,28},{1,1},{5... | collective-permute-start | bytes 1572872 | tf_op jit(solution)/shard_map/ppermute | solution.py:582
  48.7 1.8 %collective-permute-start.7 = (bf16[4,64,512]{2,1,0:T(8,128)(2,1)S(1)}, bf16[4,64,512]{2,1,0:T(8,128)(2,1)S(1)}, u32[]{:S(2)}, u32[]{:S(2)}) collective-permute-start(bf16[4,64,512]{2,1,0:T(8,128)(2,1)S(1)} %get-tuple-element.29.rows_held), channel_id=1, source_target_pairs={{0,1},{1,0},{2,3},{3,2},{4,5},{5,4},{6,7},{7,6},{8,9},{9,8},{10,11... | collective-permute-start | bytes 786440 | tf_op jit(solution)/shard_map/ppermute | solution.py:588
  50.5 6.2 %collective-permute-done.7.rows_next = bf16[4,64,512]{2,1,0:T(8,128)(2,1)S(1)} collective-permute-done((bf16[4,64,512]{2,1,0:T(8,128)(2,1)S(1)}, bf16[4,64,512]{2,1,0:T(8,128)(2,1)S(1)}, u32[]{:S(2)}, u32[]{:S(2)}) %collective-permute-start.7) | collective-permute-done | bytes 262176 | tf_op jit(solution)/shard_map/ppermute | solution.py:588
  56.8 1.7 %collective-permute-done.4.x_aside = bf16[2,256,512]{2,1,0:T(8,128)(2,1)S(1)} collective-permute-done((bf16[2,256,512]{2,1,0:T(8,128)(2,1)S(1)}, bf16[2,256,512]{2,1,0:T(8,128)(2,1)S(1)}, u32[]{:S(2)}, u32[]{:S(2)}) %collective-permute-start.4) | collective-permute-done | bytes 524320 | tf_op jit(solution)/shard_map/ppermute | solution.py:585
  59.1 1.7 %shard_map.57 = (bf16[2,2,256,512]{3,2,1,0:T(8,128)(2,1)}, bf16[2,2,512,256]{3,2,1,0:T(8,128)(2,1)}, bf16[2,4,64,512]{3,2,1,0:T(8,128)(2,1)}) custom-call(bf16[2,256,512]{2,1,0:T(8,128)(2,1)S(1)} %get-tuple-element.27.x_column, bf16[2,256,512]{2,1,0:T(8,128)(2,1)S(1)} %collective-permute-done.4.x_aside, bf16[2,512,256]{2,1,0:T(8,128)(2,1)S(1)} %collective-permute-done.5.y0, ...), custom_call_target="tpu_custom_call" | custom-call | tf_op jit(solution)/shard_map/pallas_call | solution.py:596
  60.9 1.3 collective-permute-start.10
  62.2 4.7 %collective-permute-start.8 = (bf16[2,2,256,512]{3,2,1,0:T(8,128)(2,1)}, bf16[2,2,256,512]{3,2,1,0:T(8,128)(2,1)}, u32[]{:S(2)}, u32[]{:S(2)}) collective-permute-start(bf16[2,2,256,512]{3,2,1,0:T(8,128)(2,1)} %get-tuple-element.30), channel_id=1, source_target_pairs={{0,0},{4,4},{8,16},{12,20},{16,8},{20,12},{24,24},{28,28},{1,1},{5... | collective-permute-start | bytes 3145736 | tf_op jit(solution)/shard_map/ppermute | solution.py:582
  66.8 2.7 %collective-permute-start.11 = (bf16[2,4,64,512]{3,2,1,0:T(8,128)(2,1)}, bf16[2,4,64,512]{3,2,1,0:T(8,128)(2,1)}, u32[]{:S(2)}, u32[]{:S(2)}) collective-permute-start(bf16[2,4,64,512]{3,2,1,0:T(8,128)(2,1)} %get-tuple-element.32.near), channel_id=1, source_target_pairs={{0,2},{1,3},{2,0},{3,1},{4,6},{5,7},{6,4},{7,5},{8,10},{9,11},{10,... | collective-permute-start | bytes 1572872 | tf_op jit(solution)/shard_map/ppermute | solution.py:588
  72.6 18.5 %collective-permute-done.11.far = bf16[2,4,64,512]{3,2,1,0:T(8,128)(2,1)} collective-permute-done((bf16[2,4,64,512]{3,2,1,0:T(8,128)(2,1)}, bf16[2,4,64,512]{3,2,1,0:T(8,128)(2,1)}, u32[]{:S(2)}, u32[]{:S(2)}) %collective-permute-start.11) | collective-permute-done | bytes 524320 | tf_op jit(solution)/shard_map/ppermute | solution.py:588
  92.1 1.3 collective-permute-start.12
  93.4 12.0 %collective-permute-done.12.incoming = bf16[2,512,512]{2,1,0:T(8,128)(2,1)S(1)} collective-permute-done((bf16[2,512,512]{2,1,0:T(8,128)(2,1)S(1)}, bf16[2,512,512]{2,1,0:T(8,128)(2,1)S(1)}, u32[]{:S(2)}, u32[]{:S(2)}) %collective-permute-start.12) | collective-permute-done | bytes 1048608 | tf_op jit(solution)/shard_map/ppermute | solution.py:642
  105.4 11.4 %shard_map.59 = (bf16[2,2,512,512]{3,2,1,0:T(8,128)(2,1)S(1)}, bf16[2,512,512]{2,1,0:T(8,128)(2,1)S(1)}) custom-call(s32[20]{0:T(128)S(1)} %stack.89.info, bf16[2,2,256,512]{3,2,1,0:T(8,128)(2,1)} %collective-permute-done.8.x0, bf16[2,2,256,512]{3,2,1,0:T(8,128)(2,1)} %collective-permute-done.9.x1, bf16[2,512,256]{2,1,0:T(8,128)(2,1)S(1)} %collective-permute-done.5.y0, ...), custom_call_target="tpu_custom_call" | custom-call | flops 6442450944 | bytes 8388608 | tf_op jit(solution)/shard_map/pallas_call | solution.py:643
  116.8 1.4 collective-permute-start.13
  118.2 2.2 %collective-permute-done.13.incoming = bf16[2,512,512]{2,1,0:T(8,128)(2,1)S(1)} collective-permute-done((bf16[2,512,512]{2,1,0:T(8,128)(2,1)S(1)}, bf16[2,512,512]{2,1,0:T(8,128)(2,1)S(1)}, u32[]{:S(2)}, u32[]{:S(2)}) %collective-permute-start.13) | collective-permute-done | bytes 1048608 | tf_op jit(solution)/shard_map/ppermute | solution.py:669
  120.4 1.3 shard_map.60
  121.7 8.3 %collective-permute-start.14 = (bf16[2,256,512]{2,1,0:T(8,128)(2,1)S(1)}, bf16[2,256,512]{2,1,0:T(8,128)(2,1)S(1)}, u32[]{:S(2)}, u32[]{:S(2)}) collective-permute-start(bf16[2,256,512]{2,1,0:T(8,128)(2,1)S(1)} %get-tuple-element.37), channel_id=1, source_target_pairs={{0,0},{4,4},{16,8},{20,12},{8,16},{12,20},{24,24},{28,28},{1,1},{5... | collective-permute-start | bytes 1572872 | tf_op jit(solution)/shard_map/ppermute | solution.py:694
  130.1 2.7 %collective-permute-start.17 = (bf16[2,256,512]{2,1,0:T(8,128)(2,1)S(1)}, bf16[2,256,512]{2,1,0:T(8,128)(2,1)S(1)}, u32[]{:S(2)}, u32[]{:S(2)}) collective-permute-start(bf16[2,256,512]{2,1,0:T(8,128)(2,1)S(1)} %get-tuple-element.40), channel_id=1, source_target_pairs={{20,0},{16,4},{4,8},{0,12},{28,16},{24,20},{12,24},{8,28},{21,1},{... | collective-permute-start | bytes 1572872 | tf_op jit(solution)/shard_map/ppermute | solution.py:694
  132.8 4.3 %collective-permute-done.14.rest_0_ = bf16[2,256,512]{2,1,0:T(8,128)(2,1)S(1)} collective-permute-done((bf16[2,256,512]{2,1,0:T(8,128)(2,1)S(1)}, bf16[2,256,512]{2,1,0:T(8,128)(2,1)S(1)}, u32[]{:S(2)}, u32[]{:S(2)}) %collective-permute-start.14) | collective-permute-done | bytes 524320 | tf_op jit(solution)/shard_map/ppermute | solution.py:694
  137.1 5.4 %collective-permute-done.15.rest_1_ = bf16[2,256,512]{2,1,0:T(8,128)(2,1)S(1)} collective-permute-done((bf16[2,256,512]{2,1,0:T(8,128)(2,1)S(1)}, bf16[2,256,512]{2,1,0:T(8,128)(2,1)S(1)}, u32[]{:S(2)}, u32[]{:S(2)}) %collective-permute-start.15) | collective-permute-done | bytes 524320 | tf_op jit(solution)/shard_map/ppermute | solution.py:694
  142.5 4.9 %collective-permute-done.16.rest_2_ = bf16[2,256,512]{2,1,0:T(8,128)(2,1)S(1)} collective-permute-done((bf16[2,256,512]{2,1,0:T(8,128)(2,1)S(1)}, bf16[2,256,512]{2,1,0:T(8,128)(2,1)S(1)}, u32[]{:S(2)}, u32[]{:S(2)}) %collective-permute-start.16) | collective-permute-done | bytes 524320 | tf_op jit(solution)/shard_map/ppermute | solution.py:694
  147.3 8.2 %collective-permute-done.17.rest_3_ = bf16[2,256,512]{2,1,0:T(8,128)(2,1)S(1)} collective-permute-done((bf16[2,256,512]{2,1,0:T(8,128)(2,1)S(1)}, bf16[2,256,512]{2,1,0:T(8,128)(2,1)S(1)}, u32[]{:S(2)}, u32[]{:S(2)}) %collective-permute-start.17) | collective-permute-done | bytes 524320 | tf_op jit(solution)/shard_map/ppermute | solution.py:694
  155.5 2.2 %shard_map.61 = bf16[2,256,2048]{2,1,0:T(8,128)(2,1)} custom-call(s32[5]{0:T(128)S(1)} %copy-done, bf16[2,256,512]{2,1,0:T(8,128)(2,1)S(1)} %collective-permute-done.14.rest_0_, bf16[2,256,512]{2,1,0:T(8,128)(2,1)S(1)} %collective-permute-done.15.rest_1_, bf16[2,256,512]{2,1,0:T(8,128)(2,1)S(1)} %collective-permute-done.16.rest_2_, ...), custom_call_target="tpu_custom_call" | custom-call | tf_op jit(solution)/shard_map/pallas_call | solution.py:696
  (22 shorter events, 5.3 us)
Async XLA Ops:
  2.1 41.5 %all-to-all-start = ((bf16[4,4,64,512]{3,2,1,0:T(8,128)(2,1)}), bf16[4,4,64,512]{3,2,1,0:T(8,128)(2,1)S(1)}, u32[]{:S(2)}, u32[]{:S(2)}) async-start(bf16[4,4,64,512]{3,2,1,0:T(8,128)(2,1)} %broadcast_in_dim.4), calls=%async_computation | async-start | bytes 2097152 | tf_op jit(solution)/shard_map/all_to_all | solution.py:550
  11.9 16.1 %collective-permute-start = (bf16[576,512]{1,0:T(8,128)(2,1)}, bf16[576,512]{1,0:T(8,128)(2,1)S(1)}, u32[]{:S(2)}, u32[]{:S(2)}) collective-permute-start(bf16[576,512]{1,0:T(8,128)(2,1)} %get-tuple-element.23), channel_id=1, source_target_pairs={{0,0},{4,4},{8,16},{12,20},{16,8},{20,12},{24,24},{28,28},{1,1},{5... | collective-permute-start | bytes 1769480 | tf_op jit(solution)/shard_map/ppermute | solution.py:563
  15.8 26.4 %collective-permute-start.1 = (bf16[576,512]{1,0:T(8,128)(2,1)}, bf16[576,512]{1,0:T(8,128)(2,1)S(1)}, u32[]{:S(2)}, u32[]{:S(2)}) collective-permute-start(bf16[576,512]{1,0:T(8,128)(2,1)} %get-tuple-element.24), channel_id=1, source_target_pairs={{0,4},{4,0},{8,20},{12,16},{16,12},{20,8},{24,28},{28,24},{1,5},{5... | collective-permute-start | bytes 1769480 | tf_op jit(solution)/shard_map/ppermute | solution.py:563
  16.9 25.3 %collective-permute-start.2 = (bf16[576,512]{1,0:T(8,128)(2,1)}, bf16[576,512]{1,0:T(8,128)(2,1)S(1)}, u32[]{:S(2)}, u32[]{:S(2)}) collective-permute-start(bf16[576,512]{1,0:T(8,128)(2,1)} %get-tuple-element.25), channel_id=1, source_target_pairs={{0,16},{4,20},{8,0},{12,4},{16,24},{20,28},{24,8},{28,12},{1,17},{... | collective-permute-start | bytes 1769480 | tf_op jit(solution)/shard_map/ppermute | solution.py:563
  16.9 26.6 %collective-permute-start.3 = (bf16[576,512]{1,0:T(8,128)(2,1)}, bf16[576,512]{1,0:T(8,128)(2,1)S(1)}, u32[]{:S(2)}, u32[]{:S(2)}) collective-permute-start(bf16[576,512]{1,0:T(8,128)(2,1)} %get-tuple-element.26), channel_id=1, source_target_pairs={{0,20},{4,16},{8,4},{12,0},{16,28},{20,24},{24,12},{28,8},{1,21},{... | collective-permute-start | bytes 1769480 | tf_op jit(solution)/shard_map/ppermute | solution.py:563
  44.5 25.1 %copy-start.1 = (s32[16]{0:T(128)S(1)}, s32[16]{0:T(128)}, u32[]{:S(2)}) copy-start(s32[16]{0:T(128)} %param.6) | copy-start | bytes 196
  44.5 14.0 %collective-permute-start.4 = (bf16[2,256,512]{2,1,0:T(8,128)(2,1)S(1)}, bf16[2,256,512]{2,1,0:T(8,128)(2,1)S(1)}, u32[]{:S(2)}, u32[]{:S(2)}) collective-permute-start(bf16[2,256,512]{2,1,0:T(8,128)(2,1)S(1)} %get-tuple-element.27.x_column), channel_id=1, source_target_pairs={{0,4},{4,0},{1,5},{5,1},{2,6},{6,2},{3,7},{7,3},{8,12},{12,8},{9,1... | collective-permute-start | bytes 1572872 | tf_op jit(solution)/shard_map/ppermute | solution.py:585
  44.9 13.6 %collective-permute-start.6 = (bf16[2,512,256]{2,1,0:T(8,128)(2,1)S(1)}, bf16[2,512,256]{2,1,0:T(8,128)(2,1)S(1)}, u32[]{:S(2)}, u32[]{:S(2)}) collective-permute-start(bf16[2,512,256]{2,1,0:T(8,128)(2,1)S(1)} %get-tuple-element.28), channel_id=1, source_target_pairs={{0,16},{4,20},{8,0},{12,4},{16,24},{20,28},{24,8},{28,12},{1,17},{... | collective-permute-start | bytes 1572872 | tf_op jit(solution)/shard_map/ppermute | solution.py:582
  46.2 13.0 %collective-permute-start.5 = (bf16[2,512,256]{2,1,0:T(8,128)(2,1)S(1)}, bf16[2,512,256]{2,1,0:T(8,128)(2,1)S(1)}, u32[]{:S(2)}, u32[]{:S(2)}) collective-permute-start(bf16[2,512,256]{2,1,0:T(8,128)(2,1)S(1)} %get-tuple-element.28), channel_id=1, source_target_pairs={{0,0},{4,4},{8,16},{12,20},{16,8},{20,12},{24,24},{28,28},{1,1},{5... | collective-permute-start | bytes 1572872 | tf_op jit(solution)/shard_map/ppermute | solution.py:582
  48.7 8.0 %collective-permute-start.7 = (bf16[4,64,512]{2,1,0:T(8,128)(2,1)S(1)}, bf16[4,64,512]{2,1,0:T(8,128)(2,1)S(1)}, u32[]{:S(2)}, u32[]{:S(2)}) collective-permute-start(bf16[4,64,512]{2,1,0:T(8,128)(2,1)S(1)} %get-tuple-element.29.rows_held), channel_id=1, source_target_pairs={{0,1},{1,0},{2,3},{3,2},{4,5},{5,4},{6,7},{7,6},{8,9},{9,8},{10,11... | collective-permute-start | bytes 786440 | tf_op jit(solution)/shard_map/ppermute | solution.py:588
  60.9 30.2 %collective-permute-start.10 = (bf16[2,2,512,256]{3,2,1,0:T(8,128)(2,1)}, bf16[2,2,512,256]{3,2,1,0:T(8,128)(2,1)}, u32[]{:S(2)}, u32[]{:S(2)}) collective-permute-start(bf16[2,2,512,256]{3,2,1,0:T(8,128)(2,1)} %get-tuple-element.31), channel_id=1, source_target_pairs={{0,4},{4,0},{1,5},{5,1},{2,6},{6,2},{3,7},{7,3},{8,12},{12,8},{9,1... | collective-permute-start | bytes 3145736 | tf_op jit(solution)/shard_map/ppermute | solution.py:585
  62.2 28.9 %collective-permute-start.9 = (bf16[2,2,256,512]{3,2,1,0:T(8,128)(2,1)}, bf16[2,2,256,512]{3,2,1,0:T(8,128)(2,1)}, u32[]{:S(2)}, u32[]{:S(2)}) collective-permute-start(bf16[2,2,256,512]{3,2,1,0:T(8,128)(2,1)} %get-tuple-element.30), channel_id=1, source_target_pairs={{0,16},{4,20},{8,0},{12,4},{16,24},{20,28},{24,8},{28,12},{1,17},{... | collective-permute-start | bytes 3145736 | tf_op jit(solution)/shard_map/ppermute | solution.py:582
  62.2 28.9 %collective-permute-start.8 = (bf16[2,2,256,512]{3,2,1,0:T(8,128)(2,1)}, bf16[2,2,256,512]{3,2,1,0:T(8,128)(2,1)}, u32[]{:S(2)}, u32[]{:S(2)}) collective-permute-start(bf16[2,2,256,512]{3,2,1,0:T(8,128)(2,1)} %get-tuple-element.30), channel_id=1, source_target_pairs={{0,0},{4,4},{8,16},{12,20},{16,8},{20,12},{24,24},{28,28},{1,1},{5... | collective-permute-start | bytes 3145736 | tf_op jit(solution)/shard_map/ppermute | solution.py:582
  66.8 24.3 %collective-permute-start.11 = (bf16[2,4,64,512]{3,2,1,0:T(8,128)(2,1)}, bf16[2,4,64,512]{3,2,1,0:T(8,128)(2,1)}, u32[]{:S(2)}, u32[]{:S(2)}) collective-permute-start(bf16[2,4,64,512]{3,2,1,0:T(8,128)(2,1)} %get-tuple-element.32.near), channel_id=1, source_target_pairs={{0,2},{1,3},{2,0},{3,1},{4,6},{5,7},{6,4},{7,5},{8,10},{9,11},{10,... | collective-permute-start | bytes 1572872 | tf_op jit(solution)/shard_map/ppermute | solution.py:588
  92.1 13.3 %collective-permute-start.12 = (bf16[2,512,512]{2,1,0:T(8,128)(2,1)S(1)}, bf16[2,512,512]{2,1,0:T(8,128)(2,1)S(1)}, u32[]{:S(2)}, u32[]{:S(2)}) collective-permute-start(bf16[2,512,512]{2,1,0:T(8,128)(2,1)S(1)} %get-tuple-element.34.w_high), channel_id=1, source_target_pairs={{0,8},{16,24},{1,9},{17,25},{2,10},{18,26},{3,11},{19,27},{4,12},{... | collective-permute-start | bytes 3145736 | tf_op jit(solution)/shard_map/ppermute | solution.py:642
  116.8 3.6 %collective-permute-start.13 = (bf16[2,512,512]{2,1,0:T(8,128)(2,1)S(1)}, bf16[2,512,512]{2,1,0:T(8,128)(2,1)S(1)}, u32[]{:S(2)}, u32[]{:S(2)}) collective-permute-start(bf16[2,512,512]{2,1,0:T(8,128)(2,1)S(1)} %get-tuple-element.35), channel_id=1, source_target_pairs={{8,0},{24,16},{9,1},{25,17},{10,2},{26,18},{11,3},{27,19},{12,4},{... | collective-permute-start | bytes 3145736 | tf_op jit(solution)/shard_map/ppermute | solution.py:669
  120.4 35.2 %copy-start = (s32[5]{0:T(128)S(1)}, s32[5]{0:T(128)}, u32[]{:S(2)}) copy-start(s32[5]{0:T(128)} %stack.74.place) | copy-start | bytes 64
  121.7 15.5 %collective-permute-start.14 = (bf16[2,256,512]{2,1,0:T(8,128)(2,1)S(1)}, bf16[2,256,512]{2,1,0:T(8,128)(2,1)S(1)}, u32[]{:S(2)}, u32[]{:S(2)}) collective-permute-start(bf16[2,256,512]{2,1,0:T(8,128)(2,1)S(1)} %get-tuple-element.37), channel_id=1, source_target_pairs={{0,0},{4,4},{16,8},{20,12},{8,16},{12,20},{24,24},{28,28},{1,1},{5... | collective-permute-start | bytes 1572872 | tf_op jit(solution)/shard_map/ppermute | solution.py:694
  130.0 12.5 %collective-permute-start.15 = (bf16[2,256,512]{2,1,0:T(8,128)(2,1)S(1)}, bf16[2,256,512]{2,1,0:T(8,128)(2,1)S(1)}, u32[]{:S(2)}, u32[]{:S(2)}) collective-permute-start(bf16[2,256,512]{2,1,0:T(8,128)(2,1)S(1)} %get-tuple-element.38), channel_id=1, source_target_pairs={{4,0},{0,4},{20,8},{16,12},{12,16},{8,20},{28,24},{24,28},{5,1},{1... | collective-permute-start | bytes 1572872 | tf_op jit(solution)/shard_map/ppermute | solution.py:694
  130.0 17.3 %collective-permute-start.16 = (bf16[2,256,512]{2,1,0:T(8,128)(2,1)S(1)}, bf16[2,256,512]{2,1,0:T(8,128)(2,1)S(1)}, u32[]{:S(2)}, u32[]{:S(2)}) collective-permute-start(bf16[2,256,512]{2,1,0:T(8,128)(2,1)S(1)} %get-tuple-element.39), channel_id=1, source_target_pairs={{16,0},{20,4},{0,8},{4,12},{24,16},{28,20},{8,24},{12,28},{17,1},{... | collective-permute-start | bytes 1572872 | tf_op jit(solution)/shard_map/ppermute | solution.py:694
  130.1 25.5 %collective-permute-start.17 = (bf16[2,256,512]{2,1,0:T(8,128)(2,1)S(1)}, bf16[2,256,512]{2,1,0:T(8,128)(2,1)S(1)}, u32[]{:S(2)}, u32[]{:S(2)}) collective-permute-start(bf16[2,256,512]{2,1,0:T(8,128)(2,1)S(1)} %get-tuple-element.40), channel_id=1, source_target_pairs={{20,0},{16,4},{4,8},{0,12},{28,16},{24,20},{12,24},{8,28},{21,1},{... | collective-permute-start | bytes 1572872 | tf_op jit(solution)/shard_map/ppermute | solution.py:694

commit v6 on v5

v6 whole, which is shorter than its diff:
```python
import functools

import jax
import jax.numpy as jnp
from jax import lax
from jax.experimental import pallas as pl
from jax.experimental.pallas import tpu as pltpu
from jax.sharding import PartitionSpec as P

source_amplitude = 8.0
vmem_bytes = 32 * 1024 * 1024
bf16 = jnp.bfloat16
f32 = jnp.float32
anywhere = pl.BlockSpec(memory_space=pl.ANY)
in_smem = pl.BlockSpec(memory_space=pltpu.SMEM)
in_vmem = pl.BlockSpec(memory_space=pltpu.VMEM)

info_member, info_piece, info_slot, info_half, info_block, info_self = 3, 4, 12, 14, 16, 20


def shifted(x, axis, by):
    peers = lax.axis_size(axis)
    pairs = [(i, i + by) for i in range(peers) if 0 <= i + by < peers]
    return lax.ppermute(x, axis, pairs)


def complex_block(factor):
    upper = jnp.concatenate([factor[0], -factor[1]], axis=1)
    lower = jnp.concatenate([factor[1], factor[0]], axis=1)
    return jnp.concatenate([upper, lower], axis=0)


def y_transform(real_turned, imag_turned, field_in):
    real_part = jnp.dot(field_in[0], real_turned, preferred_element_type=jnp.float32) - jnp.dot(
        field_in[1], imag_turned, preferred_element_type=jnp.float32
    )
    imag_part = jnp.dot(field_in[0], imag_turned, preferred_element_type=jnp.float32) + jnp.dot(
        field_in[1], real_turned, preferred_element_type=jnp.float32
    )
    return jnp.stack([real_part, imag_part]).astype(jnp.bfloat16)


def x_transform(x_block, field_in):
    planes, rows_all, width = field_in.shape
    output = jnp.dot(
        x_block, field_in.reshape(planes * rows_all, width), preferred_element_type=jnp.float32
    )
    return output.astype(jnp.bfloat16).reshape(planes, rows_all, width)


def scale_rows(field_in, weights, width):
    planes, rows_here, merged = field_in.shape
    spread = field_in.astype(jnp.float32).reshape(planes, rows_here, merged // width, width)
    return (spread * weights.astype(jnp.float32)[None, :, None, :]).reshape(
        planes, rows_here, merged
    )


def pick_batch(field, batch_count, batch_index):
    planes, rows_here, merged = field.shape
    split_field = field.reshape(planes, rows_here, batch_count, merged // batch_count)
    return lax.dynamic_index_in_dim(split_field, batch_index, 2, keepdims=False)


def place_batch(field, piece, batch_count, batch_index):
    planes, rows_here, merged = field.shape
    split_field = field.reshape(planes, rows_here, batch_count, merged // batch_count)
    shaped = piece.reshape(planes, rows_here, 1, merged // batch_count)
    updated = lax.dynamic_update_slice_in_dim(split_field, shaped, batch_index, 2)
    return updated.reshape(planes, rows_here, merged)


def on_device_by_layer(background, src_pos, coupling, x_factor, y_factor):
    source_count = src_pos.shape[0]
    sec_count = lax.axis_size("sec")
    sec_index = lax.axis_index("sec")
    grid_y = lax.axis_size("py")
    own_x = lax.axis_index("px")
    own_y = lax.axis_index("py")
    local_sources = source_count // grid_y
    x_pieces, y_pieces = (
        lax.all_gather(x_factor[0], ("px", "py"), axis=1, tiled=True),
        lax.all_gather(y_factor[0], ("px", "py"), axis=1, tiled=True),
    )
    x_block = complex_block(x_pieces)
    real_turned = y_pieces[0].T
    imag_turned = y_pieces[1].T
    local_field = background[:, 0]
    local_weights = coupling[0]
    rows_here = local_field.shape[1]
    full_cols = y_factor.shape[3]
    plane_cells = x_factor.shape[3] * full_cols
    own_sources = lax.dynamic_slice_in_dim(src_pos, own_y * local_sources, local_sources)
    layer_of = own_sources // plane_cells
    remainder = own_sources % plane_cells
    row_of = remainder // full_cols
    column_of = remainder % full_cols
    row_start = own_x * rows_here
    row_hit = row_of[None, :] == row_start + jnp.arange(rows_here, dtype=jnp.int32)[:, None]
    col_hit = column_of[:, None] == jnp.arange(full_cols, dtype=jnp.int32)[None, :]
    layer_hit = layer_of == sec_index
    delta = (row_hit[:, :, None] & col_hit[None, :, :] & layer_hit[None, :, None]).astype(
        jnp.float32
    )
    delta = (delta * source_amplitude).reshape(rows_here, local_sources * full_cols)
    real_rhs = local_field[0].astype(jnp.float32) + delta
    rhs_field = jnp.stack([real_rhs, local_field[1].astype(jnp.float32)])

    def apply_front(field_in):
        turned = y_transform(real_turned, imag_turned, field_in)
        line_field = lax.all_to_all(turned, "px", split_axis=2, concat_axis=1, tiled=True)
        finished = x_transform(x_block, line_field)
        return lax.all_to_all(finished, "px", split_axis=1, concat_axis=2, tiled=True)

    forward_field = jnp.zeros(local_field.shape, jnp.bfloat16)
    outgoing = pick_batch(forward_field, sec_count, 0)
    for step in range(2 * sec_count - 1):
        incoming = shifted(outgoing, "sec", 1)
        batch_index = step - sec_index
        active = (batch_index >= 0) & (batch_index < sec_count)
        clamped = jnp.clip(batch_index, 0, sec_count - 1)
        rhs_batch = pick_batch(rhs_field, sec_count, clamped)
        reduced = (rhs_batch - scale_rows(incoming, local_weights, full_cols)).astype(jnp.bfloat16)
        candidate = apply_front(reduced)
        previous = pick_batch(forward_field, sec_count, clamped)
        kept = jnp.where(active, candidate, previous)
        forward_field = place_batch(forward_field, kept, sec_count, clamped)
        outgoing = candidate
    sweep_field = forward_field
    for step in range(2 * sec_count - 2):
        send_index = jnp.clip(step - (sec_count - 1 - sec_index), 0, sec_count - 1)
        own_batch = pick_batch(sweep_field, sec_count, send_index)
        sent_field = scale_rows(own_batch, local_weights, full_cols).astype(jnp.bfloat16)
        incoming = shifted(sent_field, "sec", -1)
        batch_index = step - (sec_count - 2 - sec_index)
        active = (batch_index >= 0) & (batch_index < sec_count) & (sec_index <= sec_count - 2)
        clamped = jnp.clip(batch_index, 0, sec_count - 1)
        solved = apply_front(incoming)
        forward_batch = pick_batch(forward_field, sec_count, clamped)
        candidate = (forward_batch.astype(jnp.float32) - solved.astype(jnp.float32)).astype(
            jnp.bfloat16
        )
        previous = pick_batch(sweep_field, sec_count, clamped)
        kept = jnp.where(active, candidate, previous)
        sweep_field = place_batch(sweep_field, kept, sec_count, clamped)
    return sweep_field[:, None]


def start_all(copies):
    for copy in copies:
        copy.start()


def wait_all(copies):
    for copy in copies:
        copy.wait()


def row_chunks(order, step):
    step = min(step, order)
    return [slice(first, first + step) for first in range(0, order, step)]


class Either:
    def __init__(self, flag, own, received, target, sem):
        self.flag = flag
        self.own = pltpu.make_async_copy(own, target, sem)
        self.received = pltpu.make_async_copy(received, target, sem)

    def start(self):
        @pl.when(self.flag != 0)
        def _():
            self.own.start()

        @pl.when(self.flag == 0)
        def _():
            self.received.start()

    def wait(self):
        self.received.wait()


def pack_kernel(place, field, coupling, x_factor, y_factor, *rest):
    pieces, (blocks, held, shard, sems, csems, osems, fsems) = rest[:-7], rest[-7:]
    rows_here = field.shape[1]
    height = x_factor.shape[1]
    own = pl.ds(pl.multiple_of(place[len(pieces)] * height, height), height)
    factors = [
        pltpu.make_async_copy(factor, shard.at[pl.ds(2 * which, 2)], fsems.at[which])
        for which, factor in enumerate((x_factor, y_factor))
    ]
    start_all(factors)
    incoming = []
    for index, piece in enumerate(pieces):
        width = piece.shape[1]
        offset = pl.multiple_of(place[index] * width, width)
        copies = [
            pltpu.make_async_copy(
                field.at[plane, :, pl.ds(offset, width)],
                held.at[index, pl.ds(plane * rows_here, rows_here)],
                sems.at[index, plane],
            )
            for plane in range(2)
        ]
        copies.append(
            pltpu.make_async_copy(
                coupling.at[own], held.at[index, pl.ds(2 * rows_here, height)], csems.at[index]
            )
        )
        start_all(copies)
        incoming.append(copies)
    outgoing = []
    wait_all(factors)
    for target in range(blocks.shape[0]):
        outgoing.append(pltpu.make_async_copy(shard, blocks.at[target], fsems.at[2 + target]))
        outgoing[-1].start()
    for index, piece in enumerate(pieces):
        wait_all(incoming[index])
        outgoing.append(pltpu.make_async_copy(held.at[index], piece, osems.at[index]))
        outgoing[-1].start()
    wait_all(outgoing)


def unpack_kernel(place, own, *rest):
    pieces, field, sems = rest[:-2], rest[-2], rest[-1]
    copies = []
    for index, piece in enumerate(pieces):
        width = piece.shape[2]
        offset = pl.multiple_of(place[index] * width, width)
        target = field.at[:, :, pl.ds(offset, width)]
        if index:
            copies.append(pltpu.make_async_copy(piece, target, sems.at[index]))
        else:
            copies.append(Either(place[len(pieces) + 1], own, piece, target, sems.at[index]))
    start_all(copies)
    wait_all(copies)


def column_kernel(info, blocks, own, p0, p1, p2, p3, x_column, y_column, rows_held, sems, csems):
    count, planes, height, order = blocks.shape
    copies = []
    for index in range(count):
        for which, column in enumerate((x_column, y_column)):
            copies.append(
                pltpu.make_async_copy(
                    blocks.at[index, pl.ds(2 * which, 2)],
                    column.at[:, pl.ds(index * height, height), :],
                    sems.at[index, which],
                )
            )
    last = pl.ds(own.shape[0] - height, height)
    copies.append(Either(info[info_self], own.at[last], p0.at[last], rows_held.at[0], csems.at[0]))
    for index, piece in enumerate((p1, p2, p3)):
        copies.append(
            pltpu.make_async_copy(piece.at[last], rows_held.at[index + 1], csems.at[index + 1])
        )
    start_all(copies)
    wait_all(copies)


def both_kernel(info, x_column, x_aside, y_column, y0, y1, rows_held, rows_next, x_both, y_both,
                rows_both, sems):
    copies = [
        pltpu.make_async_copy(x_column, x_both.at[0], sems.at[0]),
        pltpu.make_async_copy(x_aside, x_both.at[1], sems.at[1]),
        Either(info[info_self], y_column, y0, y_both.at[0], sems.at[2]),
        pltpu.make_async_copy(y1, y_both.at[1], sems.at[3]),
        pltpu.make_async_copy(rows_held, rows_both.at[0], sems.at[4]),
        pltpu.make_async_copy(rows_next, rows_both.at[1], sems.at[5]),
    ]
    start_all(copies)
    wait_all(copies)


def weight_copies(info, near, far, weights, sems):
    height = near.shape[2]
    half_height = weights.shape[1] // 2
    copies = []
    for index in range(4):
        block = (near if index < 2 else far).at[index % 2]
        for turn in range(near.shape[1]):
            slot, half = info[info_piece + 2 * turn], info[info_piece + 2 * turn + 1]
            start = half * half_height + info[info_block + index] * height
            rows = pl.ds(pl.multiple_of(start, height), height)
            copies.append(
                pltpu.make_async_copy(
                    block.at[turn], weights.at[slot, rows, :], sems.at[index, turn]
                )
            )
    return copies


class Factors:
    def __init__(self, info, x_both, x0, x1, y_both, y_far, held, sems):
        self.order, self.held, self.sems = held.shape[2], held, sems
        self.column = x_both.at[0]
        for which in (1, 0):
            for turn in range(2):
                for far in range(2):
                    slot, half = info[info_slot + turn], info[info_half + far]
                    for plane in range(2):
                        ends = self.ends(which, plane, slot, half, far)
                        if which:
                            source = (y_far if far else y_both).at[turn, plane]
                            pltpu.make_async_copy(source, *ends).start()
                        elif turn:
                            pltpu.make_async_copy(x1.at[far, plane], *ends).start()
                        else:
                            own, received = x_both.at[far, plane], x0.at[far, plane]
                            Either(info[info_self], own, received, *ends).start()

    def ends(self, which, plane, slot, half, far):
        height = self.order // 2
        rows = pl.ds(pl.multiple_of(half * height, height), height)
        target = self.held.at[slot, which, rows, pl.ds(plane * self.order, self.order)]
        return target, self.sems.at[slot, which, far, plane]

    def ready(self, slot, which):
        for far in range(2):
            for plane in range(2):
                ends = self.ends(which, plane, slot, far, far)
                pltpu.make_async_copy(self.column.at[plane], *ends).wait()

    def apply(self, slot, source, below, store, fresh):
        order = self.order
        turned = (((1,), (1,)), ((), ()))
        if fresh:
            self.ready(slot, 1)
        for rows in row_chunks(order, 256):
            real, imag = source(0, rows), source(1, rows)
            upper = jnp.concatenate([real, -imag], axis=1)
            lower = jnp.concatenate([imag, real], axis=1)
            part = lax.dot_general(
                jnp.concatenate([upper, lower], axis=0),
                self.held[slot, 1],
                turned,
                preferred_element_type=f32,
            ).astype(bf16)
            height = rows.stop - rows.start
            real, imag = part[:height], part[height:]
            further = slice(rows.start + order, rows.stop + order)
            below[rows, :order] = real
            below[rows, order:] = imag
            below[further, :order] = -imag
            below[further, order:] = real
        if fresh:
            self.ready(slot, 0)
        for plane in range(2):
            for columns in row_chunks(order, 256):
                along = slice(columns.start + plane * order, columns.stop + plane * order)
                store(
                    plane,
                    columns,
                    jnp.dot(self.held[slot, 0], below[:, along], preferred_element_type=f32),
                )


def reduced(rhs, info, slot, weights, incoming):
    def source(plane, rows):
        values = rhs[slot, plane, rows].astype(f32)
        if plane == 0:
            row = lax.broadcasted_iota(jnp.int32, values.shape, 0) + rows.start
            column = lax.broadcasted_iota(jnp.int32, (1, values.shape[1]), 1)
            hit = (column == info[2]) & (info[0] == slot)
            cell = jnp.where(hit, f32(source_amplitude), f32(0.0))
            values = values + jnp.where(row == info[1], cell, f32(0.0))
        scaled = weights[slot, rows].astype(f32) * incoming(plane, rows)
        return (values - scaled).astype(bf16)

    return source


def sent(weights, slot, field):
    def source(plane, rows):
        scaled = weights[slot, rows].astype(f32) * field[plane, rows].astype(f32)
        return scaled.astype(bf16)

    return source


def subtract_into(target):
    def store(plane, columns, values):
        solved = values.astype(bf16).astype(f32)
        forward = target[plane, :, columns].astype(f32)
        target[plane, :, columns] = (forward - solved).astype(bf16)

    return store


def round_into(target):
    def store(plane, columns, values):
        target[plane, :, columns] = values.astype(bf16)

    return store


def rhs_copies(info, own, pieces, rhs, sems):
    copies = []
    height = rhs.shape[2] // 2
    for index, piece in enumerate(pieces):
        slot, half = info[info_piece + 2 * index], info[info_piece + 2 * index + 1]
        rows = pl.ds(pl.multiple_of(half * height, height), height)
        for plane in range(2):
            part = pl.ds(plane * height, height)
            ends = (rhs.at[slot, plane, rows, :], sems.at[2 * index + plane])
            if index:
                copies.append(pltpu.make_async_copy(piece.at[part], *ends))
            else:
                copies.append(Either(info[info_self], own.at[part], piece.at[part], *ends))
    return copies


def first_kernel(info, xb, x0, x1, yb, yf, near, far, own, p0, p1, p2, p3, w_low, w_high, held,
                 weights, rhs, below, sems, csems, fsems):
    @pl.when(info[info_member] == 0)
    def _():
        early = rhs_copies(info, own, (p0, p1, p2, p3), rhs, sems)
        early += weight_copies(info, near, far, weights, csems)
        start_all(early)
        factors = Factors(info, xb, x0, x1, yb, yf, held, fsems)
        wait_all(early)
        zero = reduced(rhs, info, 0, weights, lambda plane, rows: f32(0.0))
        factors.apply(0, zero, below, round_into(w_low), True)
        one = reduced(rhs, info, 1, weights, lambda plane, rows: w_low[plane, rows].astype(f32))
        factors.apply(1, one, below, round_into(w_high), True)


def last_kernel(info, xb, x0, x1, yb, yf, near, far, own, p0, p1, p2, p3, incoming, field, back,
                held, weights, rhs, arrived, kept, below, sems, csems, fsems, osems):
    @pl.when(info[info_member] == 1)
    def _():
        early = rhs_copies(info, own, (p0, p1, p2, p3), rhs, sems)
        early += weight_copies(info, near, far, weights, csems)
        early.append(pltpu.make_async_copy(incoming, arrived, sems.at[8]))
        start_all(early)
        factors = Factors(info, xb, x0, x1, yb, yf, held, fsems)
        wait_all(early)
        low, high = kept.at[0], kept.at[1]
        two = reduced(rhs, info, 0, weights, lambda plane, rows: arrived[plane, rows].astype(f32))
        factors.apply(0, two, below, round_into(low), True)
        three = reduced(rhs, info, 1, weights, lambda plane, rows: low[plane, rows].astype(f32))
        factors.apply(1, three, below, round_into(high), True)
        out_high = pltpu.make_async_copy(high, field.at[1], osems.at[1])
        out_high.start()
        factors.apply(0, sent(weights, 1, high), below, subtract_into(low), False)
        out_low = pltpu.make_async_copy(low, field.at[0], osems.at[0])
        out_low.start()
        last = sent(weights, 0, low)
        for plane in range(2):
            for rows in row_chunks(weights.shape[1], 256):
                back[plane, rows] = last(plane, rows)
        out_high.wait()
        out_low.wait()


def back_kernel(info, xb, x0, x1, yb, yf, near, far, w_low, w_high, incoming, field, p0, p1, p2, p3,
                held, weights, kept, arrived, below, sems, csems, fsems, osems):
    @pl.when(info[info_member] == 0)
    def _():
        early = [pltpu.make_async_copy(incoming, arrived, sems.at[0])]
        start_all(early)
        factors = Factors(info, xb, x0, x1, yb, yf, held, fsems)
        early += weight_copies(info, near, far, weights, csems)
        early += [
            pltpu.make_async_copy(w_low, kept.at[0], sems.at[2]),
            pltpu.make_async_copy(w_high, kept.at[1], sems.at[3]),
        ]
        start_all(early[1:])
        wait_all(early)
        low, high = kept.at[0], kept.at[1]
        one = lambda plane, rows: arrived[plane, rows]
        factors.apply(1, one, below, subtract_into(high), True)
        factors.apply(0, sent(weights, 1, high), below, subtract_into(low), True)

    @pl.when(info[info_member] != 0)
    def _():
        finished = pltpu.make_async_copy(field, kept, sems.at[0])
        finished.start()
        finished.wait()

    copies = []
    for index, piece in enumerate((p0, p1, p2, p3)):
        height = piece.shape[1]
        slot, half = info[info_piece + 2 * index], info[info_piece + 2 * index + 1]
        rows = pl.ds(pl.multiple_of(half * height, height), height)
        copies.append(pltpu.make_async_copy(kept.at[slot, :, rows, :], piece, osems.at[index]))
    start_all(copies)
    wait_all(copies)


def on_device(background, src_pos, coupling, x_factor, y_factor):
    px_count = lax.axis_size("px")
    sec_index, own_x, own_y = (lax.axis_index(axis) for axis in ("sec", "px", "py"))
    group, member = sec_index // 2, sec_index % 2
    groups = lax.axis_size("sec") // 2
    order = y_factor.shape[3]
    field = background[:, 0]
    rows_here = field.shape[1]
    height = x_factor.shape[2]
    params = pltpu.CompilerParams(vmem_limit_bytes=vmem_bytes)
    rounds = [(a, b) for a in range(groups) for b in range(px_count)]

    def pairs(a, b):
        return [
            ((2 * x + c) * px_count + y, (2 * ((c + a) % 2) + x) * px_count + (y + b) % px_count)
            for x in range(groups)
            for c in range(2)
            for y in range(px_count)
            if (a, b, x) != (0, 0, c)
        ]

    def back_pairs(a, b):
        return [(target, source) for source, target in pairs(a, b)]

    own_source = src_pos[own_y * groups * px_count + group * px_count + own_x]
    plane_cells = x_factor.shape[3] * order
    layer = own_source // plane_cells
    remainder = own_source % plane_cells
    py_count = lax.axis_size("py")
    entries = [
        jnp.where(layer // 2 == member, layer % 2, -1),
        remainder // order,
        remainder % order,
        member,
    ]
    for a, b in rounds:
        entries += [(group + a) % 2, (own_x - b) % px_count]
    entries += [group, (group + 1) % 2, own_x, (own_x + 1) % 2]
    pair = own_y // 2 * 2
    entries += [own_y, pair + (own_y + 1) % 2, (own_y + 2) % 4, (pair + 2) % 4 + (own_y + 1) % 2]
    entries += [group == member]
    info = jnp.stack([jnp.asarray(entry, jnp.int32) for entry in entries])

    sends_to = jnp.stack(
        [((member + a) % 2) * px_count + (own_x + b) % px_count for a, b in rounds]
        + [own_y, group == member]
    ).astype(jnp.int32)
    piece_shape = jax.ShapeDtypeStruct((2, rows_here, order), bf16)
    *packed, blocks = pl.pallas_call(
        pack_kernel,
        out_shape=[jax.ShapeDtypeStruct((2 * rows_here + height, order), bf16)] * len(rounds)
        + [jax.ShapeDtypeStruct((py_count, 4, height, order), bf16)],
        in_specs=[in_smem] + [anywhere] * 4,
        out_specs=[anywhere] * (len(rounds) + 1),
        scratch_shapes=[
            pltpu.VMEM((len(rounds), 2 * rows_here + height, order), bf16),
            pltpu.VMEM((4, height, order), bf16),
            pltpu.SemaphoreType.DMA((len(rounds), 2)),
            pltpu.SemaphoreType.DMA((len(rounds),)),
            pltpu.SemaphoreType.DMA((len(rounds),)),
            pltpu.SemaphoreType.DMA((2 + py_count,)),
        ],
        compiler_params=pltpu.CompilerParams(vmem_limit_bytes=60 * 1024 * 1024),
    )(sends_to, field, coupling[0], x_factor[0], y_factor[0])
    pieces = [
        lax.ppermute(piece, ("sec", "px"), pairs(a, b)) for piece, (a, b) in zip(packed, rounds)
    ]
    blocks = lax.all_to_all(blocks, "py", split_axis=0, concat_axis=0, tiled=True)

    column_shape = jax.ShapeDtypeStruct((2, rows_here, order), bf16)
    rows_shape = jax.ShapeDtypeStruct((len(rounds), height, order), bf16)
    x_column, y_column, rows_held = pl.pallas_call(
        column_kernel,
        out_shape=[column_shape, column_shape, rows_shape],
        in_specs=[in_smem] + [anywhere] * 6,
        out_specs=[in_vmem] * 3,
        scratch_shapes=[
            pltpu.SemaphoreType.DMA((py_count, 2)),
            pltpu.SemaphoreType.DMA((len(rounds),)),
        ],
        compiler_params=params,
    )(info, blocks, packed[0], *pieces)

    def across(block, a):
        return lax.ppermute(block, ("sec", "px"), pairs(a, 0))

    def aside(block):
        return lax.ppermute(block, "px", [(y, (y + 1) % 2) for y in range(2)])

    def over_z(block, bit):
        return lax.ppermute(block, "py", [(z, z ^ bit) for z in range(py_count)])

    y_near = [across(y_column, a) for a in range(2)]
    x_aside = aside(x_column)
    rows_next = over_z(rows_held, 1)
    twice = [
        jax.ShapeDtypeStruct((2,) + one.shape, bf16) for one in (column_shape, column_shape, rows_shape)
    ]
    x_both, y_both, rows_both = pl.pallas_call(
        both_kernel,
        out_shape=twice,
        in_specs=[in_smem] + [anywhere] * 7,
        out_specs=[in_vmem] * 3,
        scratch_shapes=[pltpu.SemaphoreType.DMA((6,))],
        compiler_params=params,
    )(info, x_column, x_aside, y_column, *y_near, rows_held, rows_next)
    y_far = aside(y_both)
    x_across = [across(x_both, a) for a in range(2)]
    rows_far = over_z(rows_both, 2)
    factors = [x_both, *x_across, y_both, y_far, rows_both, rows_far]

    full_shape = jax.ShapeDtypeStruct((2, order, order), bf16)
    factor_scratch = pltpu.VMEM((2, 2, order, 2 * order), bf16)
    arrived_scratch = pltpu.VMEM((2, order, order), bf16)
    weight_scratch = pltpu.VMEM((2, order, order), bf16)
    field_scratch = pltpu.VMEM((2, 2, order, order), bf16)
    below_scratch = pltpu.VMEM((2 * order, 2 * order), bf16)
    factor_sems = pltpu.SemaphoreType.DMA((2, 2, 2, 2))
    solve_flops = 16 * order**3
    w_low, w_high = pl.pallas_call(
        first_kernel,
        out_shape=[full_shape] * 2,
        in_specs=[in_smem] + [anywhere] * 12,
        out_specs=[in_vmem] * 2,
        scratch_shapes=[
            factor_scratch,
            weight_scratch,
            field_scratch,
            below_scratch,
            pltpu.SemaphoreType.DMA((9,)),
            pltpu.SemaphoreType.DMA((4, 4)),
            factor_sems,
        ],
        compiler_params=params,
        cost_estimate=pl.CostEstimate(
            flops=2 * solve_flops, bytes_accessed=16 * order * order * 2, transcendentals=0
        ),
    )(info, *factors, packed[0], *pieces)

    up = [(2 * x, 2 * x + 1) for x in range(groups)]
    incoming = lax.ppermute(w_high, "sec", up)
    solved, back = pl.pallas_call(
        last_kernel,
        out_shape=[jax.ShapeDtypeStruct((2, 2, order, order), bf16), full_shape],
        in_specs=[in_smem] + [anywhere] * 13,
        out_specs=[anywhere, in_vmem],
        scratch_shapes=[
            factor_scratch,
            weight_scratch,
            field_scratch,
            arrived_scratch,
            field_scratch,
            below_scratch,
            pltpu.SemaphoreType.DMA((9,)),
            pltpu.SemaphoreType.DMA((4, 4)),
            factor_sems,
            pltpu.SemaphoreType.DMA((2,)),
        ],
        compiler_params=params,
        cost_estimate=pl.CostEstimate(
            flops=3 * solve_flops, bytes_accessed=16 * order * order * 2, transcendentals=0
        ),
    )(info, *factors, packed[0], *pieces, incoming)

    down = [(target, source) for source, target in up]
    incoming = lax.ppermute(back, "sec", down)
    results = pl.pallas_call(
        back_kernel,
        out_shape=[piece_shape] * len(rounds),
        in_specs=[in_smem] + [anywhere] * 11,
        out_specs=[anywhere] * len(rounds),
        scratch_shapes=[
            factor_scratch,
            weight_scratch,
            field_scratch,
            arrived_scratch,
            below_scratch,
            pltpu.SemaphoreType.DMA((9,)),
            pltpu.SemaphoreType.DMA((4, 4)),
            factor_sems,
            pltpu.SemaphoreType.DMA((len(rounds),)),
        ],
        compiler_params=params,
        cost_estimate=pl.CostEstimate(
            flops=2 * solve_flops, bytes_accessed=16 * order * order * 2, transcendentals=0
        ),
    )(info, *factors, w_low, w_high, incoming, solved)
    received = [
        lax.ppermute(piece, ("sec", "px"), back_pairs(a, b)) for piece, (a, b) in zip(results, rounds)
    ]
    output = pl.pallas_call(
        unpack_kernel,
        out_shape=jax.ShapeDtypeStruct(field.shape, bf16),
        in_specs=[in_smem] + [anywhere] * (len(rounds) + 1),
        out_specs=in_vmem,
        scratch_shapes=[pltpu.SemaphoreType.DMA((len(rounds),))],
        compiler_params=params,
    )(sends_to, results[0], *received)
    return output[:, None]


def chip_plan_fits(mesh):
    return mesh.shape["sec"] == 4 and mesh.shape["px"] == 2 and mesh.shape["py"] == 4


def solution(mesh):
    placed = (
        P(None, "sec", "px", "py"),
        P(),
        P("sec", "px", None),
        P("sec", None, ("px", "py"), None),
        P("sec", None, ("px", "py"), None),
    )
    return jax.shard_map(
        on_device if chip_plan_fits(mesh) else on_device_by_layer,
        mesh=mesh,
        in_specs=placed,
        out_specs=P(None, "sec", "px", "py"),
        check_vma=False,
    )
```

time: 159 us -> 151 us (0.950)
  waiting for transfers between devices: 88.5 us -> 80.8 us
    ppermute x4, waiting for transfers between devices: 24.4 us -> 19.4 us  [on_device(): lax.ppermute(piece, ('sec', 'px'), pairs(a, b))]
    ppermute x4, waiting for transfers between devices: 22.7 us -> 18.1 us  [on_device(): lax.ppermute(piece, ('sec', 'px'), back_pairs(a, b))]
    ppermute x2, waiting for transfers between devices: 24.7 us -> 29.1 us  [over_z(): return lax.ppermute(block, 'py', [(z, z ^ bit) for z in range(py_count)])]
    ppermute x1, waiting for transfers between devices: 12 us -> 9.66 us  [on_device(): incoming = lax.ppermute(w_high, 'sec', up)]
  transfers between devices with their start and end apart: 19 -> 19, of which waited for: 13 -> 12; matrix products, arithmetic and copies ran while one was open for 1% -> 0% of each run, Pallas kernels for 2% -> 0%
where the time goes in v6:
time: 151 us
  waiting for transfers between devices  80.8 us (54%)
  starting transfers between devices  42.4 us (28%)
  Pallas kernels  23.3 us (15%)
  between operations  3.09 us (2%)
    ppermute x2, waiting for transfers between devices, over_z(): return lax.ppermute(block, 'py', [(z, z ^ bit) for z in range(py_count)])  29.1 us
    ppermute x4, waiting for transfers between devices, on_device(): lax.ppermute(piece, ('sec', 'px'), pairs(a, b))  19.4 us
    ppermute x4, waiting for transfers between devices, on_device(): lax.ppermute(piece, ('sec', 'px'), back_pairs(a, b))  18.1 us
    ppermute x4, starting transfers between devices, on_device(): lax.ppermute(piece, ('sec', 'px'), back_pairs(a, b))  12.6 us
    pallas_call x1, Pallas kernels, on_device(): pl.pallas_call(last_kernel, out_shape=[jax.ShapeDtypeStruct((2, 2, order,...  11.5 us
    ppermute x1, waiting for transfers between devices, on_device(): incoming = lax.ppermute(w_high, 'sec', up)  9.66 us
    ppermute x4, starting transfers between devices, across(): return lax.ppermute(block, ('sec', 'px'), pairs(a, 0))  8.85 us
    ppermute x4, starting transfers between devices, on_device(): lax.ppermute(piece, ('sec', 'px'), pairs(a, b))  6.88 us
  transfers between devices with their start and end apart: 19, of which 12 were waited for; matrix products, arithmetic and copies ran while one was open for 0% of the time, Pallas kernels for 0%

profile of v6, /device:TPU:1, one launch (start us, length us, event | category | flops | bytes accessed | tf_op | source)
XLA Modules:
  0.0 150.8 jit_solution(2464591195428595224)
XLA Ops:
  0.0 0.6 stack.83.place
  0.6 4.4 %shard_map.55 = (bf16[576,512]{1,0:T(8,128)(2,1)}, bf16[576,512]{1,0:T(8,128)(2,1)}, bf16[576,512]{1,0:T(8,128)(2,1)}, bf16[576,512]{1,0:T(8,128)(2,1)}, bf16[4,4,64,512]{3,2,1,0:T(8,128)(2,1)}) custom-call(s32[6]{0:T(128)} %stack.83.place, bf16[2,256,2048]{2,1,0:T(8,128)(2,1)} %bitcast.28, bf16[256,512]{1,0:T(8,128)(2,1)} %bitcast.29, ...), custom_call_target="tpu_custom_call" | custom-call | tf_op jit(solution)/shard_map/pallas_call | solution.py:539
  5.0 5.6 %all-to-all-start = ((bf16[4,4,64,512]{3,2,1,0:T(8,128)(2,1)}), bf16[4,4,64,512]{3,2,1,0:T(8,128)(2,1)S(1)}, u32[]{:S(2)}, u32[]{:S(2)}) async-start(bf16[4,4,64,512]{3,2,1,0:T(8,128)(2,1)} %get-tuple-element.24), calls=%async_computation | async-start | bytes 2097152 | tf_op jit(solution)/shard_map/all_to_all | solution.py:558
  10.6 3.0 %collective-permute-start.1 = (bf16[576,512]{1,0:T(8,128)(2,1)}, bf16[576,512]{1,0:T(8,128)(2,1)S(1)}, u32[]{:S(2)}, u32[]{:S(2)}) collective-permute-start(bf16[576,512]{1,0:T(8,128)(2,1)} %get-tuple-element.26), channel_id=1, source_target_pairs={{0,4},{4,0},{8,20},{12,16},{16,12},{20,8},{24,28},{28,24},{1,5},{5... | collective-permute-start | bytes 1769480 | tf_op jit(solution)/shard_map/ppermute | solution.py:556
  14.1 3.3 %collective-permute-start = (bf16[576,512]{1,0:T(8,128)(2,1)S(1)}, bf16[576,512]{1,0:T(8,128)(2,1)}, u32[]{:S(2)}, u32[]{:S(2)}) collective-permute-start(bf16[576,512]{1,0:T(8,128)(2,1)S(1)} %copy-done), channel_id=1, source_target_pairs={{8,16},{12,20},{16,8},{20,12},{9,17},{13,21},{17,9},{21,13},{10,18... | collective-permute-start | bytes 1769480 | tf_op jit(solution)/shard_map/ppermute | solution.py:556
  17.6 0.6 dynamic_slice.3
  20.9 5.8 %collective-permute-done.1.p1 = bf16[576,512]{1,0:T(8,128)(2,1)S(1)} collective-permute-done((bf16[576,512]{1,0:T(8,128)(2,1)}, bf16[576,512]{1,0:T(8,128)(2,1)S(1)}, u32[]{:S(2)}, u32[]{:S(2)}) %collective-permute-start.1) | collective-permute-done | bytes 589856 | tf_op jit(solution)/shard_map/ppermute | solution.py:556
  26.7 2.4 %collective-permute-done.2.p2 = bf16[576,512]{1,0:T(8,128)(2,1)S(1)} collective-permute-done((bf16[576,512]{1,0:T(8,128)(2,1)}, bf16[576,512]{1,0:T(8,128)(2,1)S(1)}, u32[]{:S(2)}, u32[]{:S(2)}) %collective-permute-start.2) | collective-permute-done | bytes 589856 | tf_op jit(solution)/shard_map/ppermute | solution.py:556
  29.2 11.2 %collective-permute-done.3.p3 = bf16[576,512]{1,0:T(8,128)(2,1)S(1)} collective-permute-done((bf16[576,512]{1,0:T(8,128)(2,1)}, bf16[576,512]{1,0:T(8,128)(2,1)S(1)}, u32[]{:S(2)}, u32[]{:S(2)}) %collective-permute-start.3) | collective-permute-done | bytes 589856 | tf_op jit(solution)/shard_map/ppermute | solution.py:556
  40.3 2.2 %shard_map.56 = (bf16[2,256,512]{2,1,0:T(8,128)(2,1)S(1)}, bf16[2,256,512]{2,1,0:T(8,128)(2,1)S(1)}, bf16[4,64,512]{2,1,0:T(8,128)(2,1)S(1)}) custom-call(s32[21]{0:T(128)S(1)} %stack.98.info, bf16[4,4,64,512]{3,2,1,0:T(8,128)(2,1)S(1)} %all-to-all-done.blocks, bf16[576,512]{1,0:T(8,128)(2,1)S(1)} %copy-done, bf16[576,512]{1,0:T(8,128)(2,1)} %collective-permute-done.p0, ...), custom_call_target="tpu_custom_call" | custom-call | tf_op jit(solution)/shard_map/pallas_call | solution.py:562
  42.5 0.9 collective-permute-start.4
  43.5 4.2 %collective-permute-start.5 = (bf16[2,256,512]{2,1,0:T(8,128)(2,1)S(1)}, bf16[2,256,512]{2,1,0:T(8,128)(2,1)S(1)}, u32[]{:S(2)}, u32[]{:S(2)}) collective-permute-start(bf16[2,256,512]{2,1,0:T(8,128)(2,1)S(1)} %get-tuple-element.30.y_column), channel_id=1, source_target_pairs={{8,16},{12,20},{16,8},{20,12},{9,17},{13,21},{17,9},{21,13},{10,18... | collective-permute-start | bytes 1572872 | tf_op jit(solution)/shard_map/ppermute | solution.py:575
  47.7 1.8 %collective-permute-start.7 = (bf16[4,64,512]{2,1,0:T(8,128)(2,1)S(1)}, bf16[4,64,512]{2,1,0:T(8,128)(2,1)S(1)}, u32[]{:S(2)}, u32[]{:S(2)}) collective-permute-start(bf16[4,64,512]{2,1,0:T(8,128)(2,1)S(1)} %get-tuple-element.31.rows_held), channel_id=1, source_target_pairs={{0,1},{1,0},{2,3},{3,2},{4,5},{5,4},{6,7},{7,6},{8,9},{9,8},{10,11... | collective-permute-start | bytes 786440 | tf_op jit(solution)/shard_map/ppermute | solution.py:581
  49.5 6.2 %collective-permute-done.7.rows_next = bf16[4,64,512]{2,1,0:T(8,128)(2,1)S(1)} collective-permute-done((bf16[4,64,512]{2,1,0:T(8,128)(2,1)S(1)}, bf16[4,64,512]{2,1,0:T(8,128)(2,1)S(1)}, u32[]{:S(2)}, u32[]{:S(2)}) %collective-permute-start.7) | collective-permute-done | bytes 262176 | tf_op jit(solution)/shard_map/ppermute | solution.py:581
  55.9 2.1 %collective-permute-done.5.y0 = bf16[2,256,512]{2,1,0:T(8,128)(2,1)S(1)} collective-permute-done((bf16[2,256,512]{2,1,0:T(8,128)(2,1)S(1)}, bf16[2,256,512]{2,1,0:T(8,128)(2,1)S(1)}, u32[]{:S(2)}, u32[]{:S(2)}) %collective-permute-start.5) | collective-permute-done | bytes 524320 | tf_op jit(solution)/shard_map/ppermute | solution.py:575
  58.1 0.8 shard_map.57
  59.2 4.7 %collective-permute-start.8 = (bf16[2,2,256,512]{3,2,1,0:T(8,128)(2,1)S(1)}, bf16[2,2,256,512]{3,2,1,0:T(8,128)(2,1)S(1)}, u32[]{:S(2)}, u32[]{:S(2)}) collective-permute-start(bf16[2,2,256,512]{3,2,1,0:T(8,128)(2,1)S(1)} %get-tuple-element.32.xb), channel_id=1, source_target_pairs={{8,16},{12,20},{16,8},{20,12},{9,17},{13,21},{17,9},{21,13},{10,18... | collective-permute-start | bytes 3145736 | tf_op jit(solution)/shard_map/ppermute | solution.py:575
  63.8 2.9 %collective-permute-start.11 = (bf16[2,4,64,512]{3,2,1,0:T(8,128)(2,1)S(1)}, bf16[2,4,64,512]{3,2,1,0:T(8,128)(2,1)S(1)}, u32[]{:S(2)}, u32[]{:S(2)}) collective-permute-start(bf16[2,4,64,512]{3,2,1,0:T(8,128)(2,1)S(1)} %get-tuple-element.34.near), channel_id=1, source_target_pairs={{0,2},{1,3},{2,0},{3,1},{4,6},{5,7},{6,4},{7,5},{8,10},{9,11},{10,... | collective-permute-start | bytes 1572872 | tf_op jit(solution)/shard_map/ppermute | solution.py:581
  66.7 22.8 %collective-permute-done.11.far = bf16[2,4,64,512]{3,2,1,0:T(8,128)(2,1)S(1)} collective-permute-done((bf16[2,4,64,512]{3,2,1,0:T(8,128)(2,1)S(1)}, bf16[2,4,64,512]{3,2,1,0:T(8,128)(2,1)S(1)}, u32[]{:S(2)}, u32[]{:S(2)}) %collective-permute-start.11) | collective-permute-done | bytes 524320 | tf_op jit(solution)/shard_map/ppermute | solution.py:581
  89.5 0.9 shard_map.58
  90.5 1.3 collective-permute-start.12
  91.8 9.7 %collective-permute-done.12.incoming = bf16[2,512,512]{2,1,0:T(8,128)(2,1)S(1)} collective-permute-done((bf16[2,512,512]{2,1,0:T(8,128)(2,1)S(1)}, bf16[2,512,512]{2,1,0:T(8,128)(2,1)S(1)}, u32[]{:S(2)}, u32[]{:S(2)}) %collective-permute-start.12) | collective-permute-done | bytes 1048608 | tf_op jit(solution)/shard_map/ppermute | solution.py:631
  101.4 11.5 %shard_map.59 = (bf16[2,2,512,512]{3,2,1,0:T(8,128)(2,1)S(1)}, bf16[2,512,512]{2,1,0:T(8,128)(2,1)S(1)}) custom-call(s32[21]{0:T(128)S(1)} %stack.98.info, bf16[2,2,256,512]{3,2,1,0:T(8,128)(2,1)S(1)} %get-tuple-element.32.xb, bf16[2,2,256,512]{3,2,1,0:T(8,128)(2,1)S(1)} %collective-permute-done.8.x0, ...), custom_call_target="tpu_custom_call" | custom-call | flops 6442450944 | bytes 8388608 | tf_op jit(solution)/shard_map/pallas_call | solution.py:632
  113.0 1.4 collective-permute-start.13
  114.3 2.2 %collective-permute-done.13.incoming = bf16[2,512,512]{2,1,0:T(8,128)(2,1)S(1)} collective-permute-done((bf16[2,512,512]{2,1,0:T(8,128)(2,1)S(1)}, bf16[2,512,512]{2,1,0:T(8,128)(2,1)S(1)}, u32[]{:S(2)}, u32[]{:S(2)}) %collective-permute-start.13) | collective-permute-done | bytes 1048608 | tf_op jit(solution)/shard_map/ppermute | solution.py:656
  116.5 1.3 shard_map.60
  117.8 6.9 %collective-permute-start.15 = (bf16[2,256,512]{2,1,0:T(8,128)(2,1)S(1)}, bf16[2,256,512]{2,1,0:T(8,128)(2,1)S(1)}, u32[]{:S(2)}, u32[]{:S(2)}) collective-permute-start(bf16[2,256,512]{2,1,0:T(8,128)(2,1)S(1)} %get-tuple-element.40), channel_id=1, source_target_pairs={{4,0},{0,4},{20,8},{16,12},{12,16},{8,20},{28,24},{24,28},{5,1},{1... | collective-permute-start | bytes 1572872 | tf_op jit(solution)/shard_map/ppermute | solution.py:679
  124.9 5.5 %collective-permute-start.14 = (bf16[2,256,512]{2,1,0:T(8,128)(2,1)S(1)}, bf16[2,256,512]{2,1,0:T(8,128)(2,1)S(1)}, u32[]{:S(2)}, u32[]{:S(2)}) collective-permute-start(bf16[2,256,512]{2,1,0:T(8,128)(2,1)S(1)} %get-tuple-element.39.own), channel_id=1, source_target_pairs={{16,8},{20,12},{8,16},{12,20},{17,9},{21,13},{9,17},{13,21},{18,10... | collective-permute-start | bytes 1572872 | tf_op jit(solution)/shard_map/ppermute | solution.py:679
  130.4 1.3 collective-permute-done.15.rest_1_
  131.7 4.8 %collective-permute-done.16.rest_2_ = bf16[2,256,512]{2,1,0:T(8,128)(2,1)S(1)} collective-permute-done((bf16[2,256,512]{2,1,0:T(8,128)(2,1)S(1)}, bf16[2,256,512]{2,1,0:T(8,128)(2,1)S(1)}, u32[]{:S(2)}, u32[]{:S(2)}) %collective-permute-start.16) | collective-permute-done | bytes 524320 | tf_op jit(solution)/shard_map/ppermute | solution.py:679
  136.5 11.9 %collective-permute-done.17.rest_3_ = bf16[2,256,512]{2,1,0:T(8,128)(2,1)S(1)} collective-permute-done((bf16[2,256,512]{2,1,0:T(8,128)(2,1)S(1)}, bf16[2,256,512]{2,1,0:T(8,128)(2,1)S(1)}, u32[]{:S(2)}, u32[]{:S(2)}) %collective-permute-start.17) | collective-permute-done | bytes 524320 | tf_op jit(solution)/shard_map/ppermute | solution.py:679
  148.5 2.2 %shard_map.61 = bf16[2,256,2048]{2,1,0:T(8,128)(2,1)} custom-call(s32[6]{0:T(128)S(1)} %copy-done.1, bf16[2,256,512]{2,1,0:T(8,128)(2,1)S(1)} %get-tuple-element.39.own, bf16[2,256,512]{2,1,0:T(8,128)(2,1)S(1)} %collective-permute-done.14.rest_0_, bf16[2,256,512]{2,1,0:T(8,128)(2,1)S(1)} %collective-permute-done.15.rest_1_, ...), custom_call_target="tpu_custom_call" | custom-call | tf_op jit(solution)/shard_map/pallas_call | solution.py:681
  (22 shorter events, 1.4 us)
Async XLA Ops:
  0.6 16.9 %copy-start.2 = (s32[16]{0:T(128)S(1)}, s32[16]{0:T(128)}, u32[]{:S(2)}) copy-start(s32[16]{0:T(128)} %param.6) | copy-start | bytes 196
  5.0 9.1 %copy-start = (bf16[576,512]{1,0:T(8,128)(2,1)S(1)}, bf16[576,512]{1,0:T(8,128)(2,1)}, u32[]{:S(2)}) copy-start(bf16[576,512]{1,0:T(8,128)(2,1)} %get-tuple-element.25.own) | copy-start | bytes 1769476
  5.0 35.4 %all-to-all-start = ((bf16[4,4,64,512]{3,2,1,0:T(8,128)(2,1)}), bf16[4,4,64,512]{3,2,1,0:T(8,128)(2,1)S(1)}, u32[]{:S(2)}, u32[]{:S(2)}) async-start(bf16[4,4,64,512]{3,2,1,0:T(8,128)(2,1)} %get-tuple-element.24), calls=%async_computation | async-start | bytes 2097152 | tf_op jit(solution)/shard_map/all_to_all | solution.py:558
  10.6 16.2 %collective-permute-start.1 = (bf16[576,512]{1,0:T(8,128)(2,1)}, bf16[576,512]{1,0:T(8,128)(2,1)S(1)}, u32[]{:S(2)}, u32[]{:S(2)}) collective-permute-start(bf16[576,512]{1,0:T(8,128)(2,1)} %get-tuple-element.26), channel_id=1, source_target_pairs={{0,4},{4,0},{8,20},{12,16},{16,12},{20,8},{24,28},{28,24},{1,5},{5... | collective-permute-start | bytes 1769480 | tf_op jit(solution)/shard_map/ppermute | solution.py:556
  13.6 15.6 %collective-permute-start.2 = (bf16[576,512]{1,0:T(8,128)(2,1)}, bf16[576,512]{1,0:T(8,128)(2,1)S(1)}, u32[]{:S(2)}, u32[]{:S(2)}) collective-permute-start(bf16[576,512]{1,0:T(8,128)(2,1)} %get-tuple-element.27), channel_id=1, source_target_pairs={{0,16},{4,20},{8,0},{12,4},{16,24},{20,28},{24,8},{28,12},{1,17},{... | collective-permute-start | bytes 1769480 | tf_op jit(solution)/shard_map/ppermute | solution.py:556
  13.6 26.8 %collective-permute-start.3 = (bf16[576,512]{1,0:T(8,128)(2,1)}, bf16[576,512]{1,0:T(8,128)(2,1)S(1)}, u32[]{:S(2)}, u32[]{:S(2)}) collective-permute-start(bf16[576,512]{1,0:T(8,128)(2,1)} %get-tuple-element.28), channel_id=1, source_target_pairs={{0,20},{4,16},{8,4},{12,0},{16,28},{20,24},{24,12},{28,8},{1,21},{... | collective-permute-start | bytes 1769480 | tf_op jit(solution)/shard_map/ppermute | solution.py:556
  14.1 26.2 %collective-permute-start = (bf16[576,512]{1,0:T(8,128)(2,1)S(1)}, bf16[576,512]{1,0:T(8,128)(2,1)}, u32[]{:S(2)}, u32[]{:S(2)}) collective-permute-start(bf16[576,512]{1,0:T(8,128)(2,1)S(1)} %copy-done), channel_id=1, source_target_pairs={{8,16},{12,20},{16,8},{20,12},{9,17},{13,21},{17,9},{21,13},{10,18... | collective-permute-start | bytes 1769480 | tf_op jit(solution)/shard_map/ppermute | solution.py:556
  42.5 13.4 %collective-permute-start.4 = (bf16[2,256,512]{2,1,0:T(8,128)(2,1)S(1)}, bf16[2,256,512]{2,1,0:T(8,128)(2,1)S(1)}, u32[]{:S(2)}, u32[]{:S(2)}) collective-permute-start(bf16[2,256,512]{2,1,0:T(8,128)(2,1)S(1)} %get-tuple-element.29.x_column), channel_id=1, source_target_pairs={{0,4},{4,0},{1,5},{5,1},{2,6},{6,2},{3,7},{7,3},{8,12},{12,8},{9,1... | collective-permute-start | bytes 1572872 | tf_op jit(solution)/shard_map/ppermute | solution.py:578
  43.5 12.5 %collective-permute-start.6 = (bf16[2,256,512]{2,1,0:T(8,128)(2,1)S(1)}, bf16[2,256,512]{2,1,0:T(8,128)(2,1)S(1)}, u32[]{:S(2)}, u32[]{:S(2)}) collective-permute-start(bf16[2,256,512]{2,1,0:T(8,128)(2,1)S(1)} %get-tuple-element.30.y_column), channel_id=1, source_target_pairs={{0,16},{4,20},{8,0},{12,4},{16,24},{20,28},{24,8},{28,12},{1,17},{... | collective-permute-start | bytes 1572872 | tf_op jit(solution)/shard_map/ppermute | solution.py:575
  43.5 14.6 %collective-permute-start.5 = (bf16[2,256,512]{2,1,0:T(8,128)(2,1)S(1)}, bf16[2,256,512]{2,1,0:T(8,128)(2,1)S(1)}, u32[]{:S(2)}, u32[]{:S(2)}) collective-permute-start(bf16[2,256,512]{2,1,0:T(8,128)(2,1)S(1)} %get-tuple-element.30.y_column), channel_id=1, source_target_pairs={{8,16},{12,20},{16,8},{20,12},{9,17},{13,21},{17,9},{21,13},{10,18... | collective-permute-start | bytes 1572872 | tf_op jit(solution)/shard_map/ppermute | solution.py:575
  47.7 8.0 %collective-permute-start.7 = (bf16[4,64,512]{2,1,0:T(8,128)(2,1)S(1)}, bf16[4,64,512]{2,1,0:T(8,128)(2,1)S(1)}, u32[]{:S(2)}, u32[]{:S(2)}) collective-permute-start(bf16[4,64,512]{2,1,0:T(8,128)(2,1)S(1)} %get-tuple-element.31.rows_held), channel_id=1, source_target_pairs={{0,1},{1,0},{2,3},{3,2},{4,5},{5,4},{6,7},{7,6},{8,9},{9,8},{10,11... | collective-permute-start | bytes 786440 | tf_op jit(solution)/shard_map/ppermute | solution.py:581
  58.9 30.6 %collective-permute-start.10 = (bf16[2,2,256,512]{3,2,1,0:T(8,128)(2,1)S(1)}, bf16[2,2,256,512]{3,2,1,0:T(8,128)(2,1)S(1)}, u32[]{:S(2)}, u32[]{:S(2)}) collective-permute-start(bf16[2,2,256,512]{3,2,1,0:T(8,128)(2,1)S(1)} %get-tuple-element.33.yb), channel_id=1, source_target_pairs={{0,4},{4,0},{1,5},{5,1},{2,6},{6,2},{3,7},{7,3},{8,12},{12,8},{9,1... | collective-permute-start | bytes 3145736 | tf_op jit(solution)/shard_map/ppermute | solution.py:578
  59.2 30.3 %collective-permute-start.9 = (bf16[2,2,256,512]{3,2,1,0:T(8,128)(2,1)S(1)}, bf16[2,2,256,512]{3,2,1,0:T(8,128)(2,1)S(1)}, u32[]{:S(2)}, u32[]{:S(2)}) collective-permute-start(bf16[2,2,256,512]{3,2,1,0:T(8,128)(2,1)S(1)} %get-tuple-element.32.xb), channel_id=1, source_target_pairs={{0,16},{4,20},{8,0},{12,4},{16,24},{20,28},{24,8},{28,12},{1,17},{... | collective-permute-start | bytes 3145736 | tf_op jit(solution)/shard_map/ppermute | solution.py:575
  59.2 30.3 %collective-permute-start.8 = (bf16[2,2,256,512]{3,2,1,0:T(8,128)(2,1)S(1)}, bf16[2,2,256,512]{3,2,1,0:T(8,128)(2,1)S(1)}, u32[]{:S(2)}, u32[]{:S(2)}) collective-permute-start(bf16[2,2,256,512]{3,2,1,0:T(8,128)(2,1)S(1)} %get-tuple-element.32.xb), channel_id=1, source_target_pairs={{8,16},{12,20},{16,8},{20,12},{9,17},{13,21},{17,9},{21,13},{10,18... | collective-permute-start | bytes 3145736 | tf_op jit(solution)/shard_map/ppermute | solution.py:575
  63.8 25.7 %collective-permute-start.11 = (bf16[2,4,64,512]{3,2,1,0:T(8,128)(2,1)S(1)}, bf16[2,4,64,512]{3,2,1,0:T(8,128)(2,1)S(1)}, u32[]{:S(2)}, u32[]{:S(2)}) collective-permute-start(bf16[2,4,64,512]{3,2,1,0:T(8,128)(2,1)S(1)} %get-tuple-element.34.near), channel_id=1, source_target_pairs={{0,2},{1,3},{2,0},{3,1},{4,6},{5,7},{6,4},{7,5},{8,10},{9,11},{10,... | collective-permute-start | bytes 1572872 | tf_op jit(solution)/shard_map/ppermute | solution.py:581
  90.5 11.0 %collective-permute-start.12 = (bf16[2,512,512]{2,1,0:T(8,128)(2,1)S(1)}, bf16[2,512,512]{2,1,0:T(8,128)(2,1)S(1)}, u32[]{:S(2)}, u32[]{:S(2)}) collective-permute-start(bf16[2,512,512]{2,1,0:T(8,128)(2,1)S(1)} %get-tuple-element.36.w_high), channel_id=1, source_target_pairs={{0,8},{16,24},{1,9},{17,25},{2,10},{18,26},{3,11},{19,27},{4,12},{... | collective-permute-start | bytes 3145736 | tf_op jit(solution)/shard_map/ppermute | solution.py:631
  113.0 3.6 %collective-permute-start.13 = (bf16[2,512,512]{2,1,0:T(8,128)(2,1)S(1)}, bf16[2,512,512]{2,1,0:T(8,128)(2,1)S(1)}, u32[]{:S(2)}, u32[]{:S(2)}) collective-permute-start(bf16[2,512,512]{2,1,0:T(8,128)(2,1)S(1)} %get-tuple-element.37), channel_id=1, source_target_pairs={{8,0},{24,16},{9,1},{25,17},{10,2},{26,18},{11,3},{27,19},{12,4},{... | collective-permute-start | bytes 3145736 | tf_op jit(solution)/shard_map/ppermute | solution.py:656
  116.5 31.9 %copy-start.1 = (s32[6]{0:T(128)S(1)}, s32[6]{0:T(128)}, u32[]{:S(2)}) copy-start(s32[6]{0:T(128)} %stack.83.place) | copy-start | bytes 76
  117.8 13.9 %collective-permute-start.15 = (bf16[2,256,512]{2,1,0:T(8,128)(2,1)S(1)}, bf16[2,256,512]{2,1,0:T(8,128)(2,1)S(1)}, u32[]{:S(2)}, u32[]{:S(2)}) collective-permute-start(bf16[2,256,512]{2,1,0:T(8,128)(2,1)S(1)} %get-tuple-element.40), channel_id=1, source_target_pairs={{4,0},{0,4},{20,8},{16,12},{12,16},{8,20},{28,24},{24,28},{5,1},{1... | collective-permute-start | bytes 1572872 | tf_op jit(solution)/shard_map/ppermute | solution.py:679
  124.7 11.8 %collective-permute-start.16 = (bf16[2,256,512]{2,1,0:T(8,128)(2,1)S(1)}, bf16[2,256,512]{2,1,0:T(8,128)(2,1)S(1)}, u32[]{:S(2)}, u32[]{:S(2)}) collective-permute-start(bf16[2,256,512]{2,1,0:T(8,128)(2,1)S(1)} %get-tuple-element.41), channel_id=1, source_target_pairs={{16,0},{20,4},{0,8},{4,12},{24,16},{28,20},{8,24},{12,28},{17,1},{... | collective-permute-start | bytes 1572872 | tf_op jit(solution)/shard_map/ppermute | solution.py:679
  124.7 23.7 %collective-permute-start.17 = (bf16[2,256,512]{2,1,0:T(8,128)(2,1)S(1)}, bf16[2,256,512]{2,1,0:T(8,128)(2,1)S(1)}, u32[]{:S(2)}, u32[]{:S(2)}) collective-permute-start(bf16[2,256,512]{2,1,0:T(8,128)(2,1)S(1)} %get-tuple-element.42), channel_id=1, source_target_pairs={{20,0},{16,4},{4,8},{0,12},{28,16},{24,20},{12,24},{8,28},{21,1},{... | collective-permute-start | bytes 1572872 | tf_op jit(solution)/shard_map/ppermute | solution.py:679
  124.9 23.6 %collective-permute-start.14 = (bf16[2,256,512]{2,1,0:T(8,128)(2,1)S(1)}, bf16[2,256,512]{2,1,0:T(8,128)(2,1)S(1)}, u32[]{:S(2)}, u32[]{:S(2)}) collective-permute-start(bf16[2,256,512]{2,1,0:T(8,128)(2,1)S(1)} %get-tuple-element.39.own), channel_id=1, source_target_pairs={{16,8},{20,12},{8,16},{12,20},{17,9},{21,13},{9,17},{13,21},{18,10... | collective-permute-start | bytes 1572872 | tf_op jit(solution)/shard_map/ppermute | solution.py:679

commit v7 on v6

--- a/solution.py
+++ b/solution.py
@@ -258,68 +258,113 @@
     wait_all(copies)
 
 
-def both_kernel(info, x_column, x_aside, y_column, y0, y1, rows_held, rows_next, x_both, y_both,
-                rows_both, sems):
+def both_kernel(info, x_column, x_aside, y_column, y0, y1, rows_next, x_both, y_both, sems):
     copies = [
         pltpu.make_async_copy(x_column, x_both.at[0], sems.at[0]),
         pltpu.make_async_copy(x_aside, x_both.at[1], sems.at[1]),
         Either(info[info_self], y_column, y0, y_both.at[0], sems.at[2]),
         pltpu.make_async_copy(y1, y_both.at[1], sems.at[3]),
-        pltpu.make_async_copy(rows_held, rows_both.at[0], sems.at[4]),
-        pltpu.make_async_copy(rows_next, rows_both.at[1], sems.at[5]),
     ]
     start_all(copies)
     wait_all(copies)
 
 
-def weight_copies(info, near, far, weights, sems):
-    height = near.shape[2]
-    half_height = weights.shape[1] // 2
-    copies = []
-    for index in range(4):
-        block = (near if index < 2 else far).at[index % 2]
-        for turn in range(near.shape[1]):
-            slot, half = info[info_piece + 2 * turn], info[info_piece + 2 * turn + 1]
-            start = half * half_height + info[info_block + index] * height
-            rows = pl.ds(pl.multiple_of(start, height), height)
-            copies.append(
-                pltpu.make_async_copy(
-                    block.at[turn], weights.at[slot, rows, :], sems.at[index, turn]
+class Layers:
+    def __init__(self, info, x_parts, y_parts, row_blocks, held, weights, sems, csems):
+        self.info, self.order = info, held.shape[2]
+        self.x_parts, self.y_parts, self.row_blocks = x_parts, y_parts, row_blocks
+        self.held, self.weights, self.sems, self.csems = held, weights, sems, csems
+
+    def half_rows(self, far):
+        height = self.order // 2
+        return pl.ds(pl.multiple_of(self.info[info_half + far] * height, height), height)
+
+    def factor_copies(self, slot, which, parts):
+        return [
+            pltpu.make_async_copy(
+                part.at[plane],
+                self.held.at[
+                    slot, which, self.half_rows(far), pl.ds(plane * self.order, self.order)
+                ],
+                self.sems.at[slot, which, far, plane],
+            )
+            for far, part in enumerate(parts)
+            for plane in range(2)
+        ]
+
+    def y_copies(self, slot):
+        turn = self.info[info_slot + slot]
+        return self.factor_copies(slot, 1, [part.at[turn] for part in self.y_parts])
+
+    def start_y(self, slot):
+        start_all(self.y_copies(slot))
+
+    def start_x(self, slot):
+        own, first, second = self.x_parts
+        turn, same = self.info[info_slot + slot], self.info[info_self]
+        for hit, part in (
+            ((turn == 0) & (same != 0), own),
+            ((turn == 0) & (same == 0), first),
+            (turn == 1, second),
+        ):
+
+            @pl.when(hit)
+            def _():
+                start_all(self.factor_copies(slot, 0, [part.at[0], part.at[1]]))
+
+    def ready(self, slot, which):
+        part = self.x_parts[0].at[0]
+        wait_all(self.factor_copies(slot, which, [part, part]))
+
+    def weight_copies(self, slot):
+        height = self.row_blocks[0].shape[1]
+        copies = []
+        for index, block in enumerate(self.row_blocks):
+            for far in range(2):
+                turn = 2 * self.info[info_slot + slot] + far
+                start = self.info[info_half + far] * (self.order // 2)
+                start = start + self.info[info_block + index] * height
+                rows = pl.ds(pl.multiple_of(start, height), height)
+                copies.append(
+                    pltpu.make_async_copy(
+                        block.at[turn], self.weights.at[slot, rows, :], self.csems.at[slot, index, far]
+                    )
                 )
+        return copies
+
+    def rhs_copies(self, slot, pair, rhs, sems):
+        height = self.order // 2
+        return [
+            pltpu.make_async_copy(
+                piece.at[pl.ds(plane * height, height)],
+                rhs.at[slot, plane, self.half_rows(far), :],
+                sems.at[slot, far, plane],
             )
-    return copies
-
-
-class Factors:
-    def __init__(self, info, x_both, x0, x1, y_both, y_far, held, sems):
-        self.order, self.held, self.sems = held.shape[2], held, sems
-        self.column = x_both.at[0]
-        for which in (1, 0):
-            for turn in range(2):
-                for far in range(2):
-                    slot, half = info[info_slot + turn], info[info_half + far]
-                    for plane in range(2):
-                        ends = self.ends(which, plane, slot, half, far)
-                        if which:
-                            source = (y_far if far else y_both).at[turn, plane]
-                            pltpu.make_async_copy(source, *ends).start()
-                        elif turn:
-                            pltpu.make_async_copy(x1.at[far, plane], *ends).start()
-                        else:
-                            own, received = x_both.at[far, plane], x0.at[far, plane]
-                            Either(info[info_self], own, received, *ends).start()
-
-    def ends(self, which, plane, slot, half, far):
-        height = self.order // 2
-        rows = pl.ds(pl.multiple_of(half * height, height), height)
-        target = self.held.at[slot, which, rows, pl.ds(plane * self.order, self.order)]
-        return target, self.sems.at[slot, which, far, plane]
-
-    def ready(self, slot, which):
-        for far in range(2):
-            for plane in range(2):
-                ends = self.ends(which, plane, slot, far, far)
-                pltpu.make_async_copy(self.column.at[plane], *ends).wait()
+            for far, piece in enumerate(pair)
+            for plane in range(2)
+        ]
+
+    def start_rhs(self, slot, own, pieces, rhs, sems):
+        turn, same = self.info[info_slot + slot], self.info[info_self]
+        for hit, pair in (
+            ((turn == 0) & (same != 0), (own, pieces[1])),
+            ((turn == 0) & (same == 0), pieces[:2]),
+            (turn == 1, pieces[2:]),
+        ):
+
+            @pl.when(hit)
+            def _():
+                start_all(self.rhs_copies(slot, pair, rhs, sems))
+
+    def start(self, slot, own, pieces, rhs, sems):
+        self.start_y(slot)
+        self.start_rhs(slot, own, pieces, rhs, sems)
+        start_all(self.weight_copies(slot))
+        self.start_x(slot)
+
+    def wait(self, slot, own, pieces, rhs, sems):
+        wait_all(self.rhs_copies(slot, pieces[:2], rhs, sems))
+        wait_all(self.weight_copies(slot))
 
     def apply(self, slot, source, below, store, fresh):
         order = self.order
@@ -378,11 +423,10 @@
     return source
 
 
-def subtract_into(target):
+def subtract_into(target, forward):
     def store(plane, columns, values):
         solved = values.astype(bf16).astype(f32)
-        forward = target[plane, :, columns].astype(f32)
-        target[plane, :, columns] = (forward - solved).astype(bf16)
+        target[plane, :, columns] = (forward[plane, :, columns].astype(f32) - solved).astype(bf16)
 
     return store
 
@@ -394,98 +438,82 @@
     return store
 
 
-def rhs_copies(info, own, pieces, rhs, sems):
-    copies = []
-    height = rhs.shape[2] // 2
-    for index, piece in enumerate(pieces):
-        slot, half = info[info_piece + 2 * index], info[info_piece + 2 * index + 1]
-        rows = pl.ds(pl.multiple_of(half * height, height), height)
-        for plane in range(2):
-            part = pl.ds(plane * height, height)
-            ends = (rhs.at[slot, plane, rows, :], sems.at[2 * index + plane])
-            if index:
-                copies.append(pltpu.make_async_copy(piece.at[part], *ends))
-            else:
-                copies.append(Either(info[info_self], own.at[part], piece.at[part], *ends))
-    return copies
-
-
-def first_kernel(info, xb, x0, x1, yb, yf, near, far, own, p0, p1, p2, p3, w_low, w_high, held,
-                 weights, rhs, below, sems, csems, fsems):
+def first_kernel(info, xb, x0, x1, yb, yf, c0, c1, c2, c3, own, p0, p1, p2, p3, w_low, w_high,
+                 held, weights, rhs, below, sems, csems, fsems):
     @pl.when(info[info_member] == 0)
     def _():
-        early = rhs_copies(info, own, (p0, p1, p2, p3), rhs, sems)
-        early += weight_copies(info, near, far, weights, csems)
-        start_all(early)
-        factors = Factors(info, xb, x0, x1, yb, yf, held, fsems)
-        wait_all(early)
+        layers = Layers(info, (xb, x0, x1), (yb, yf), (c0, c1, c2, c3), held, weights, fsems, csems)
+        fields = (own, (p0, p1, p2, p3), rhs, sems)
+        layers.start(0, *fields)
+        layers.start(1, *fields)
+        layers.wait(0, *fields)
         zero = reduced(rhs, info, 0, weights, lambda plane, rows: f32(0.0))
-        factors.apply(0, zero, below, round_into(w_low), True)
+        layers.apply(0, zero, below, round_into(w_low), True)
+        layers.wait(1, *fields)
         one = reduced(rhs, info, 1, weights, lambda plane, rows: w_low[plane, rows].astype(f32))
-        factors.apply(1, one, below, round_into(w_high), True)
-
-
-def last_kernel(info, xb, x0, x1, yb, yf, near, far, own, p0, p1, p2, p3, incoming, field, back,
-                held, weights, rhs, arrived, kept, below, sems, csems, fsems, osems):
+        layers.apply(1, one, below, round_into(w_high), True)
+
+
+def last_kernel(info, xb, x0, x1, yb, yf, c0, c1, c2, c3, own, p0, p1, p2, p3, arrived, field, back,
+                held, weights, rhs, forward, below, sems, csems, fsems):
     @pl.when(info[info_member] == 1)
     def _():
-        early = rhs_copies(info, own, (p0, p1, p2, p3), rhs, sems)
-        early += weight_copies(info, near, far, weights, csems)
-        early.append(pltpu.make_async_copy(incoming, arrived, sems.at[8]))
-        start_all(early)
-        factors = Factors(info, xb, x0, x1, yb, yf, held, fsems)
-        wait_all(early)
-        low, high = kept.at[0], kept.at[1]
+        layers = Layers(info, (xb, x0, x1), (yb, yf), (c0, c1, c2, c3), held, weights, fsems, csems)
+        fields = (own, (p0, p1, p2, p3), rhs, sems)
+        layers.start(0, *fields)
+        layers.start(1, *fields)
+        layers.wait(0, *fields)
+        low, high = field.at[0], field.at[1]
         two = reduced(rhs, info, 0, weights, lambda plane, rows: arrived[plane, rows].astype(f32))
-        factors.apply(0, two, below, round_into(low), True)
-        three = reduced(rhs, info, 1, weights, lambda plane, rows: low[plane, rows].astype(f32))
-        factors.apply(1, three, below, round_into(high), True)
-        out_high = pltpu.make_async_copy(high, field.at[1], osems.at[1])
-        out_high.start()
-        factors.apply(0, sent(weights, 1, high), below, subtract_into(low), False)
-        out_low = pltpu.make_async_copy(low, field.at[0], osems.at[0])
-        out_low.start()
+        layers.apply(0, two, below, round_into(forward), True)
+        layers.wait(1, *fields)
+        three = reduced(rhs, info, 1, weights, lambda plane, rows: forward[plane, rows].astype(f32))
+        layers.apply(1, three, below, round_into(high), True)
+        layers.apply(0, sent(weights, 1, high), below, subtract_into(low, forward), False)
         last = sent(weights, 0, low)
         for plane in range(2):
             for rows in row_chunks(weights.shape[1], 256):
                 back[plane, rows] = last(plane, rows)
-        out_high.wait()
-        out_low.wait()
-
-
-def back_kernel(info, xb, x0, x1, yb, yf, near, far, w_low, w_high, incoming, field, p0, p1, p2, p3,
-                held, weights, kept, arrived, below, sems, csems, fsems, osems):
+
+
+def back_kernel(info, xb, x0, x1, yb, yf, c0, c1, c2, c3, w_low, w_high, arrived, field,
+                p0, p1, p2, p3, held, weights, kept, below, csems, fsems, osems):
+    def start_pieces(source, slot):
+        for index, piece in enumerate((p0, p1, p2, p3)):
+            height = piece.shape[1]
+            half = info[info_piece + 2 * index + 1]
+            rows = pl.ds(pl.multiple_of(half * height, height), height)
+
+            @pl.when(info[info_piece + 2 * index] == slot)
+            def _():
+                pltpu.make_async_copy(source.at[slot, :, rows, :], piece, osems.at[index]).start()
+
     @pl.when(info[info_member] == 0)
     def _():
-        early = [pltpu.make_async_copy(incoming, arrived, sems.at[0])]
-        start_all(early)
-        factors = Factors(info, xb, x0, x1, yb, yf, held, fsems)
-        early += weight_copies(info, near, far, weights, csems)
-        early += [
-            pltpu.make_async_copy(w_low, kept.at[0], sems.at[2]),
-            pltpu.make_async_copy(w_high, kept.at[1], sems.at[3]),
-        ]
-        start_all(early[1:])
-        wait_all(early)
+        layers = Layers(info, (xb, x0, x1), (yb, yf), (c0, c1, c2, c3), held, weights, fsems, csems)
+        layers.start_y(1)
+        layers.start_x(1)
+        high_rows = layers.weight_copies(1)
+        start_all(high_rows)
+        layers.start_y(0)
+        layers.start_x(0)
         low, high = kept.at[0], kept.at[1]
-        one = lambda plane, rows: arrived[plane, rows]
-        factors.apply(1, one, below, subtract_into(high), True)
-        factors.apply(0, sent(weights, 1, high), below, subtract_into(low), True)
+        layers.apply(
+            1, lambda plane, rows: arrived[plane, rows], below, subtract_into(high, w_high), True
+        )
+        start_pieces(kept, 1)
+        wait_all(high_rows)
+        layers.apply(0, sent(weights, 1, high), below, subtract_into(low, w_low), True)
+        start_pieces(kept, 0)
 
     @pl.when(info[info_member] != 0)
     def _():
-        finished = pltpu.make_async_copy(field, kept, sems.at[0])
-        finished.start()
-        finished.wait()
-
-    copies = []
+        start_pieces(field, 1)
+        start_pieces(field, 0)
+
     for index, piece in enumerate((p0, p1, p2, p3)):
-        height = piece.shape[1]
-        slot, half = info[info_piece + 2 * index], info[info_piece + 2 * index + 1]
-        rows = pl.ds(pl.multiple_of(half * height, height), height)
-        copies.append(pltpu.make_async_copy(kept.at[slot, :, rows, :], piece, osems.at[index]))
-    start_all(copies)
-    wait_all(copies)
+        part = kept.at[0, :, pl.ds(0, piece.shape[1]), :]
+        pltpu.make_async_copy(part, piece, osems.at[index]).wait()
 
 
 def on_device(background, src_pos, coupling, x_factor, y_factor):
@@ -583,97 +611,92 @@
     y_near = [across(y_column, a) for a in range(2)]
     x_aside = aside(x_column)
     rows_next = over_z(rows_held, 1)
-    twice = [
-        jax.ShapeDtypeStruct((2,) + one.shape, bf16) for one in (column_shape, column_shape, rows_shape)
-    ]
-    x_both, y_both, rows_both = pl.pallas_call(
+    rows_far = over_z(rows_held, 2)
+    x_both, y_both = pl.pallas_call(
         both_kernel,
-        out_shape=twice,
-        in_specs=[in_smem] + [anywhere] * 7,
-        out_specs=[in_vmem] * 3,
-        scratch_shapes=[pltpu.SemaphoreType.DMA((6,))],
+        out_shape=[jax.ShapeDtypeStruct((2,) + column_shape.shape, bf16)] * 2,
+        in_specs=[in_smem] + [anywhere] * 6,
+        out_specs=[in_vmem] * 2,
+        scratch_shapes=[pltpu.SemaphoreType.DMA((4,))],
         compiler_params=params,
-    )(info, x_column, x_aside, y_column, *y_near, rows_held, rows_next)
+    )(info, x_column, x_aside, y_column, *y_near, rows_next)
     y_far = aside(y_both)
     x_across = [across(x_both, a) for a in range(2)]
-    rows_far = over_z(rows_both, 2)
-    factors = [x_both, *x_across, y_both, y_far, rows_both, rows_far]
+    factors = [x_both, *x_across, y_both, y_far, rows_held, rows_next, rows_far, over_z(rows_next, 2)]
 
     full_shape = jax.ShapeDtypeStruct((2, order, order), bf16)
     factor_scratch = pltpu.VMEM((2, 2, order, 2 * order), bf16)
-    arrived_scratch = pltpu.VMEM((2, order, order), bf16)
     weight_scratch = pltpu.VMEM((2, order, order), bf16)
     field_scratch = pltpu.VMEM((2, 2, order, order), bf16)
     below_scratch = pltpu.VMEM((2 * order, 2 * order), bf16)
     factor_sems = pltpu.SemaphoreType.DMA((2, 2, 2, 2))
+    weight_sems = pltpu.SemaphoreType.DMA((2, py_count, 2))
+    field_sems = pltpu.SemaphoreType.DMA((2, 2, 2))
     solve_flops = 16 * order**3
+    fields = (packed[0], *pieces)
+
+    def cost(solves):
+        return pl.CostEstimate(
+            flops=solves * solve_flops, bytes_accessed=16 * order * order * 2, transcendentals=0
+        )
+
     w_low, w_high = pl.pallas_call(
         first_kernel,
         out_shape=[full_shape] * 2,
-        in_specs=[in_smem] + [anywhere] * 12,
+        in_specs=[in_smem] + [anywhere] * 14,
         out_specs=[in_vmem] * 2,
         scratch_shapes=[
             factor_scratch,
             weight_scratch,
             field_scratch,
             below_scratch,
-            pltpu.SemaphoreType.DMA((9,)),
-            pltpu.SemaphoreType.DMA((4, 4)),
+            field_sems,
+            weight_sems,
             factor_sems,
         ],
         compiler_params=params,
-        cost_estimate=pl.CostEstimate(
-            flops=2 * solve_flops, bytes_accessed=16 * order * order * 2, transcendentals=0
-        ),
-    )(info, *factors, packed[0], *pieces)
+        cost_estimate=cost(2),
+    )(info, *factors, *fields)
 
     up = [(2 * x, 2 * x + 1) for x in range(groups)]
     incoming = lax.ppermute(w_high, "sec", up)
     solved, back = pl.pallas_call(
         last_kernel,
         out_shape=[jax.ShapeDtypeStruct((2, 2, order, order), bf16), full_shape],
-        in_specs=[in_smem] + [anywhere] * 13,
-        out_specs=[anywhere, in_vmem],
+        in_specs=[in_smem] + [anywhere] * 14 + [in_vmem],
+        out_specs=[in_vmem] * 2,
         scratch_shapes=[
             factor_scratch,
             weight_scratch,
             field_scratch,
-            arrived_scratch,
-            field_scratch,
+            pltpu.VMEM((2, order, order), bf16),
             below_scratch,
-            pltpu.SemaphoreType.DMA((9,)),
-            pltpu.SemaphoreType.DMA((4, 4)),
+            field_sems,
+            weight_sems,
             factor_sems,
-            pltpu.SemaphoreType.DMA((2,)),
         ],
         compiler_params=params,
-        cost_estimate=pl.CostEstimate(
-            flops=3 * solve_flops, bytes_accessed=16 * order * order * 2, transcendentals=0
-        ),
-    )(info, *factors, packed[0], *pieces, incoming)
+        cost_estimate=cost(3),
+    )(info, *factors, *fields, incoming)
 
     down = [(target, source) for source, target in up]
     incoming = lax.ppermute(back, "sec", down)
     results = pl.pallas_call(
         back_kernel,
         out_shape=[piece_shape] * len(rounds),
-        in_specs=[in_smem] + [anywhere] * 11,
+        in_specs=[in_smem] + [anywhere] * 9 + [in_vmem] * 3 + [anywhere],
         out_specs=[anywhere] * len(rounds),
         scratch_shapes=[
             factor_scratch,
             weight_scratch,
             field_scratch,
-            arrived_scratch,
             below_scratch,
-            pltpu.SemaphoreType.DMA((9,)),
-            pltpu.SemaphoreType.DMA((4, 4)),
+            weight_sems,
             factor_sems,
             pltpu.SemaphoreType.DMA((len(rounds),)),
         ],
         compiler_params=params,
-        cost_estimate=pl.CostEstimate(
-            flops=2 * solve_flops, bytes_accessed=16 * order * order * 2, transcendentals=0
-        ),
+        cost_estimate=cost(2),
     )(info, *factors, w_low, w_high, incoming, solved)
     received = [
         lax.ppermute(piece, ("sec", "px"), back_pairs(a, b)) for piece, (a, b) in zip(results, rounds)

time: 151 us -> 149 us (0.987)
    ppermute x2 -> x3, waiting for transfers between devices: 29.1 us -> 29 us  [over_z(): return lax.ppermute(block, 'py', [(z, z ^ bit) for z in range(py_count)])]
    ppermute x2 -> x3, starting transfers between devices: 4.64 us -> 4.72 us  [over_z(): return lax.ppermute(block, 'py', [(z, z ^ bit) for z in range(py_count)])]
  transfers between devices with their start and end apart: 19 -> 20, of which waited for: 12 -> 13; matrix products, arithmetic and copies ran while one was open for 0% -> 0% of each run, Pallas kernels for 0% -> 0%
where the time goes in v7:
time: 149 us
  waiting for transfers between devices  80.8 us (54%)
  starting transfers between devices  41.5 us (28%)
  Pallas kernels  22.3 us (15%)
  between operations  2.74 us (2%)
    ppermute x3, waiting for transfers between devices, over_z(): return lax.ppermute(block, 'py', [(z, z ^ bit) for z in range(py_count)])  29 us
    ppermute x4, waiting for transfers between devices, on_device(): lax.ppermute(piece, ('sec', 'px'), pairs(a, b))  19.8 us
    ppermute x4, waiting for transfers between devices, on_device(): lax.ppermute(piece, ('sec', 'px'), back_pairs(a, b))  18.1 us
    ppermute x4, starting transfers between devices, on_device(): lax.ppermute(piece, ('sec', 'px'), back_pairs(a, b))  11.6 us
    pallas_call x1, Pallas kernels, on_device(): pl.pallas_call(last_kernel, out_shape=[jax.ShapeDtypeStruct((2, 2, order,...  10.8 us
    ppermute x1, waiting for transfers between devices, on_device(): incoming = lax.ppermute(w_high, 'sec', up)  9.37 us
    ppermute x4, starting transfers between devices, across(): return lax.ppermute(block, ('sec', 'px'), pairs(a, 0))  8.85 us
    ppermute x4, starting transfers between devices, on_device(): lax.ppermute(piece, ('sec', 'px'), pairs(a, b))  6.88 us
  transfers between devices with their start and end apart: 20, of which 13 were waited for; matrix products, arithmetic and copies ran while one was open for 0% of the time, Pallas kernels for 0%

profile of v7, /device:TPU:1, one launch (start us, length us, event | category | flops | bytes accessed | tf_op | source)
XLA Modules:
  0.0 148.6 jit_solution(8786916644760523688)
XLA Ops:
  0.0 0.6 stack.83.place
  0.6 4.4 %shard_map.55 = (bf16[576,512]{1,0:T(8,128)(2,1)}, bf16[576,512]{1,0:T(8,128)(2,1)}, bf16[576,512]{1,0:T(8,128)(2,1)}, bf16[576,512]{1,0:T(8,128)(2,1)}, bf16[4,4,64,512]{3,2,1,0:T(8,128)(2,1)}) custom-call(s32[6]{0:T(128)} %stack.83.place, bf16[2,256,2048]{2,1,0:T(8,128)(2,1)} %bitcast.28, bf16[256,512]{1,0:T(8,128)(2,1)} %bitcast.29, ...), custom_call_target="tpu_custom_call" | custom-call | tf_op jit(solution)/shard_map/pallas_call | solution.py:567
  5.0 5.6 %all-to-all-start = ((bf16[4,4,64,512]{3,2,1,0:T(8,128)(2,1)}), bf16[4,4,64,512]{3,2,1,0:T(8,128)(2,1)S(1)}, u32[]{:S(2)}, u32[]{:S(2)}) async-start(bf16[4,4,64,512]{3,2,1,0:T(8,128)(2,1)} %get-tuple-element.23), calls=%async_computation | async-start | bytes 2097152 | tf_op jit(solution)/shard_map/all_to_all | solution.py:586
  10.5 3.0 %collective-permute-start.1 = (bf16[576,512]{1,0:T(8,128)(2,1)}, bf16[576,512]{1,0:T(8,128)(2,1)S(1)}, u32[]{:S(2)}, u32[]{:S(2)}) collective-permute-start(bf16[576,512]{1,0:T(8,128)(2,1)} %get-tuple-element.25), channel_id=1, source_target_pairs={{0,4},{4,0},{8,20},{12,16},{16,12},{20,8},{24,28},{28,24},{1,5},{5... | collective-permute-start | bytes 1769480 | tf_op jit(solution)/shard_map/ppermute | solution.py:584
  14.1 3.3 %collective-permute-start = (bf16[576,512]{1,0:T(8,128)(2,1)S(1)}, bf16[576,512]{1,0:T(8,128)(2,1)}, u32[]{:S(2)}, u32[]{:S(2)}) collective-permute-start(bf16[576,512]{1,0:T(8,128)(2,1)S(1)} %copy-done), channel_id=1, source_target_pairs={{8,16},{12,20},{16,8},{20,12},{9,17},{13,21},{17,9},{21,13},{10,18... | collective-permute-start | bytes 1769480 | tf_op jit(solution)/shard_map/ppermute | solution.py:584
  20.5 6.2 %collective-permute-done.1.p1 = bf16[576,512]{1,0:T(8,128)(2,1)S(1)} collective-permute-done((bf16[576,512]{1,0:T(8,128)(2,1)}, bf16[576,512]{1,0:T(8,128)(2,1)S(1)}, u32[]{:S(2)}, u32[]{:S(2)}) %collective-permute-start.1) | collective-permute-done | bytes 589856 | tf_op jit(solution)/shard_map/ppermute | solution.py:584
  26.7 2.4 %collective-permute-done.2.p2 = bf16[576,512]{1,0:T(8,128)(2,1)S(1)} collective-permute-done((bf16[576,512]{1,0:T(8,128)(2,1)}, bf16[576,512]{1,0:T(8,128)(2,1)S(1)}, u32[]{:S(2)}, u32[]{:S(2)}) %collective-permute-start.2) | collective-permute-done | bytes 589856 | tf_op jit(solution)/shard_map/ppermute | solution.py:584
  29.2 11.2 %collective-permute-done.3.p3 = bf16[576,512]{1,0:T(8,128)(2,1)S(1)} collective-permute-done((bf16[576,512]{1,0:T(8,128)(2,1)}, bf16[576,512]{1,0:T(8,128)(2,1)S(1)}, u32[]{:S(2)}, u32[]{:S(2)}) %collective-permute-start.3) | collective-permute-done | bytes 589856 | tf_op jit(solution)/shard_map/ppermute | solution.py:584
  40.3 2.2 %shard_map.56 = (bf16[2,256,512]{2,1,0:T(8,128)(2,1)S(1)}, bf16[2,256,512]{2,1,0:T(8,128)(2,1)S(1)}, bf16[4,64,512]{2,1,0:T(8,128)(2,1)S(1)}) custom-call(s32[21]{0:T(128)S(1)} %stack.98.info, bf16[4,4,64,512]{3,2,1,0:T(8,128)(2,1)S(1)} %all-to-all-done.blocks, bf16[576,512]{1,0:T(8,128)(2,1)S(1)} %copy-done, bf16[576,512]{1,0:T(8,128)(2,1)} %collective-permute-done.p0, ...), custom_call_target="tpu_custom_call" | custom-call | tf_op jit(solution)/shard_map/pallas_call | solution.py:590
  42.5 0.9 collective-permute-start.4
  43.4 4.2 %collective-permute-start.5 = (bf16[2,256,512]{2,1,0:T(8,128)(2,1)S(1)}, bf16[2,256,512]{2,1,0:T(8,128)(2,1)S(1)}, u32[]{:S(2)}, u32[]{:S(2)}) collective-permute-start(bf16[2,256,512]{2,1,0:T(8,128)(2,1)S(1)} %get-tuple-element.29.y_column), channel_id=1, source_target_pairs={{8,16},{12,20},{16,8},{20,12},{9,17},{13,21},{17,9},{21,13},{10,18... | collective-permute-start | bytes 1572872 | tf_op jit(solution)/shard_map/ppermute | solution.py:603
  47.6 1.8 %collective-permute-start.7 = (bf16[4,64,512]{2,1,0:T(8,128)(2,1)S(1)}, bf16[4,64,512]{2,1,0:T(8,128)(2,1)S(1)}, u32[]{:S(2)}, u32[]{:S(2)}) collective-permute-start(bf16[4,64,512]{2,1,0:T(8,128)(2,1)S(1)} %get-tuple-element.30.c0), channel_id=1, source_target_pairs={{0,1},{1,0},{2,3},{3,2},{4,5},{5,4},{6,7},{7,6},{8,9},{9,8},{10,11... | collective-permute-start | bytes 786440 | tf_op jit(solution)/shard_map/ppermute | solution.py:609
  49.4 6.2 %collective-permute-done.7.rows_next.c1 = bf16[4,64,512]{2,1,0:T(8,128)(2,1)S(1)} collective-permute-done((bf16[4,64,512]{2,1,0:T(8,128)(2,1)S(1)}, bf16[4,64,512]{2,1,0:T(8,128)(2,1)S(1)}, u32[]{:S(2)}, u32[]{:S(2)}) %collective-permute-start.7) | collective-permute-done | bytes 262176 | tf_op jit(solution)/shard_map/ppermute | solution.py:609
  55.9 2.1 %collective-permute-done.5.y0 = bf16[2,256,512]{2,1,0:T(8,128)(2,1)S(1)} collective-permute-done((bf16[2,256,512]{2,1,0:T(8,128)(2,1)S(1)}, bf16[2,256,512]{2,1,0:T(8,128)(2,1)S(1)}, u32[]{:S(2)}, u32[]{:S(2)}) %collective-permute-start.5) | collective-permute-done | bytes 524320 | tf_op jit(solution)/shard_map/ppermute | solution.py:603
  58.1 0.7 shard_map.57
  59.1 4.7 %collective-permute-start.8 = (bf16[2,2,256,512]{3,2,1,0:T(8,128)(2,1)S(1)}, bf16[2,2,256,512]{3,2,1,0:T(8,128)(2,1)S(1)}, u32[]{:S(2)}, u32[]{:S(2)}) collective-permute-start(bf16[2,2,256,512]{3,2,1,0:T(8,128)(2,1)S(1)} %get-tuple-element.31.xb), channel_id=1, source_target_pairs={{8,16},{12,20},{16,8},{20,12},{9,17},{13,21},{17,9},{21,13},{10,18... | collective-permute-start | bytes 3145736 | tf_op jit(solution)/shard_map/ppermute | solution.py:603
  63.8 2.9 %collective-permute-start.11 = (bf16[4,64,512]{2,1,0:T(8,128)(2,1)S(1)}, bf16[4,64,512]{2,1,0:T(8,128)(2,1)S(1)}, u32[]{:S(2)}, u32[]{:S(2)}) collective-permute-start(bf16[4,64,512]{2,1,0:T(8,128)(2,1)S(1)} %get-tuple-element.30.c0), channel_id=1, source_target_pairs={{0,2},{1,3},{2,0},{3,1},{4,6},{5,7},{6,4},{7,5},{8,10},{9,11},{10,... | collective-permute-start | bytes 786440 | tf_op jit(solution)/shard_map/ppermute | solution.py:609
  66.7 18.0 %collective-permute-done.11.c2 = bf16[4,64,512]{2,1,0:T(8,128)(2,1)S(1)} collective-permute-done((bf16[4,64,512]{2,1,0:T(8,128)(2,1)S(1)}, bf16[4,64,512]{2,1,0:T(8,128)(2,1)S(1)}, u32[]{:S(2)}, u32[]{:S(2)}) %collective-permute-start.11) | collective-permute-done | bytes 262176 | tf_op jit(solution)/shard_map/ppermute | solution.py:609
  84.7 4.8 %collective-permute-done.12.c3 = bf16[4,64,512]{2,1,0:T(8,128)(2,1)S(1)} collective-permute-done((bf16[4,64,512]{2,1,0:T(8,128)(2,1)S(1)}, bf16[4,64,512]{2,1,0:T(8,128)(2,1)S(1)}, u32[]{:S(2)}, u32[]{:S(2)}) %collective-permute-start.12) | collective-permute-done | bytes 262176 | tf_op jit(solution)/shard_map/ppermute | solution.py:609
  89.4 0.9 shard_map.58
  90.4 1.3 collective-permute-start.13
  91.7 9.4 %collective-permute-done.13.arrived = bf16[2,512,512]{2,1,0:T(8,128)(2,1)S(1)} collective-permute-done((bf16[2,512,512]{2,1,0:T(8,128)(2,1)S(1)}, bf16[2,512,512]{2,1,0:T(8,128)(2,1)S(1)}, u32[]{:S(2)}, u32[]{:S(2)}) %collective-permute-start.13) | collective-permute-done | bytes 1048608 | tf_op jit(solution)/shard_map/ppermute | solution.py:662
  101.0 10.8 %shard_map.59 = (bf16[2,2,512,512]{3,2,1,0:T(8,128)(2,1)S(1)}, bf16[2,512,512]{2,1,0:T(8,128)(2,1)S(1)}) custom-call(s32[21]{0:T(128)S(1)} %stack.98.info, bf16[2,2,256,512]{3,2,1,0:T(8,128)(2,1)S(1)} %get-tuple-element.31.xb, bf16[2,2,256,512]{3,2,1,0:T(8,128)(2,1)S(1)} %collective-permute-done.8.x0, ...), custom_call_target="tpu_custom_call" | custom-call | flops 6442450944 | bytes 8388608 | tf_op jit(solution)/shard_map/pallas_call | solution.py:663
  111.8 1.4 collective-permute-start.14
  113.2 2.2 %collective-permute-done.14.arrived = bf16[2,512,512]{2,1,0:T(8,128)(2,1)S(1)} collective-permute-done((bf16[2,512,512]{2,1,0:T(8,128)(2,1)S(1)}, bf16[2,512,512]{2,1,0:T(8,128)(2,1)S(1)}, u32[]{:S(2)}, u32[]{:S(2)}) %collective-permute-start.14) | collective-permute-done | bytes 1048608 | tf_op jit(solution)/shard_map/ppermute | solution.py:683
  115.4 1.1 shard_map.60
  116.5 6.0 %collective-permute-start.16 = (bf16[2,256,512]{2,1,0:T(8,128)(2,1)S(1)}, bf16[2,256,512]{2,1,0:T(8,128)(2,1)S(1)}, u32[]{:S(2)}, u32[]{:S(2)}) collective-permute-start(bf16[2,256,512]{2,1,0:T(8,128)(2,1)S(1)} %get-tuple-element.38), channel_id=1, source_target_pairs={{4,0},{0,4},{20,8},{16,12},{12,16},{8,20},{28,24},{24,28},{5,1},{1... | collective-permute-start | bytes 1572872 | tf_op jit(solution)/shard_map/ppermute | solution.py:702
  122.6 5.5 %collective-permute-start.15 = (bf16[2,256,512]{2,1,0:T(8,128)(2,1)S(1)}, bf16[2,256,512]{2,1,0:T(8,128)(2,1)S(1)}, u32[]{:S(2)}, u32[]{:S(2)}) collective-permute-start(bf16[2,256,512]{2,1,0:T(8,128)(2,1)S(1)} %get-tuple-element.37.own), channel_id=1, source_target_pairs={{16,8},{20,12},{8,16},{12,20},{17,9},{21,13},{9,17},{13,21},{18,10... | collective-permute-start | bytes 1572872 | tf_op jit(solution)/shard_map/ppermute | solution.py:702
  128.1 1.3 collective-permute-done.16.rest_1_
  129.4 4.8 %collective-permute-done.17.rest_2_ = bf16[2,256,512]{2,1,0:T(8,128)(2,1)S(1)} collective-permute-done((bf16[2,256,512]{2,1,0:T(8,128)(2,1)S(1)}, bf16[2,256,512]{2,1,0:T(8,128)(2,1)S(1)}, u32[]{:S(2)}, u32[]{:S(2)}) %collective-permute-start.17) | collective-permute-done | bytes 524320 | tf_op jit(solution)/shard_map/ppermute | solution.py:702
  134.2 11.9 %collective-permute-done.18.rest_3_ = bf16[2,256,512]{2,1,0:T(8,128)(2,1)S(1)} collective-permute-done((bf16[2,256,512]{2,1,0:T(8,128)(2,1)S(1)}, bf16[2,256,512]{2,1,0:T(8,128)(2,1)S(1)}, u32[]{:S(2)}, u32[]{:S(2)}) %collective-permute-start.18) | collective-permute-done | bytes 524320 | tf_op jit(solution)/shard_map/ppermute | solution.py:702
  146.2 2.2 %shard_map.61 = bf16[2,256,2048]{2,1,0:T(8,128)(2,1)} custom-call(s32[6]{0:T(128)S(1)} %copy-done.1, bf16[2,256,512]{2,1,0:T(8,128)(2,1)S(1)} %get-tuple-element.37.own, bf16[2,256,512]{2,1,0:T(8,128)(2,1)S(1)} %collective-permute-done.15.rest_0_, bf16[2,256,512]{2,1,0:T(8,128)(2,1)S(1)} %collective-permute-done.16.rest_1_, ...), custom_call_target="tpu_custom_call" | custom-call | tf_op jit(solution)/shard_map/pallas_call | solution.py:704
  (24 shorter events, 2.0 us)
Async XLA Ops:
  0.6 17.0 %copy-start.2 = (s32[16]{0:T(128)S(1)}, s32[16]{0:T(128)}, u32[]{:S(2)}) copy-start(s32[16]{0:T(128)} %param.6) | copy-start | bytes 196
  5.0 9.1 %copy-start = (bf16[576,512]{1,0:T(8,128)(2,1)S(1)}, bf16[576,512]{1,0:T(8,128)(2,1)}, u32[]{:S(2)}) copy-start(bf16[576,512]{1,0:T(8,128)(2,1)} %get-tuple-element.24.own) | copy-start | bytes 1769476
  5.0 35.4 %all-to-all-start = ((bf16[4,4,64,512]{3,2,1,0:T(8,128)(2,1)}), bf16[4,4,64,512]{3,2,1,0:T(8,128)(2,1)S(1)}, u32[]{:S(2)}, u32[]{:S(2)}) async-start(bf16[4,4,64,512]{3,2,1,0:T(8,128)(2,1)} %get-tuple-element.23), calls=%async_computation | async-start | bytes 2097152 | tf_op jit(solution)/shard_map/all_to_all | solution.py:586
  10.5 16.2 %collective-permute-start.1 = (bf16[576,512]{1,0:T(8,128)(2,1)}, bf16[576,512]{1,0:T(8,128)(2,1)S(1)}, u32[]{:S(2)}, u32[]{:S(2)}) collective-permute-start(bf16[576,512]{1,0:T(8,128)(2,1)} %get-tuple-element.25), channel_id=1, source_target_pairs={{0,4},{4,0},{8,20},{12,16},{16,12},{20,8},{24,28},{28,24},{1,5},{5... | collective-permute-start | bytes 1769480 | tf_op jit(solution)/shard_map/ppermute | solution.py:584
  13.5 15.6 %collective-permute-start.2 = (bf16[576,512]{1,0:T(8,128)(2,1)}, bf16[576,512]{1,0:T(8,128)(2,1)S(1)}, u32[]{:S(2)}, u32[]{:S(2)}) collective-permute-start(bf16[576,512]{1,0:T(8,128)(2,1)} %get-tuple-element.26), channel_id=1, source_target_pairs={{0,16},{4,20},{8,0},{12,4},{16,24},{20,28},{24,8},{28,12},{1,17},{... | collective-permute-start | bytes 1769480 | tf_op jit(solution)/shard_map/ppermute | solution.py:584
  13.5 26.8 %collective-permute-start.3 = (bf16[576,512]{1,0:T(8,128)(2,1)}, bf16[576,512]{1,0:T(8,128)(2,1)S(1)}, u32[]{:S(2)}, u32[]{:S(2)}) collective-permute-start(bf16[576,512]{1,0:T(8,128)(2,1)} %get-tuple-element.27), channel_id=1, source_target_pairs={{0,20},{4,16},{8,4},{12,0},{16,28},{20,24},{24,12},{28,8},{1,21},{... | collective-permute-start | bytes 1769480 | tf_op jit(solution)/shard_map/ppermute | solution.py:584
  14.1 26.2 %collective-permute-start = (bf16[576,512]{1,0:T(8,128)(2,1)S(1)}, bf16[576,512]{1,0:T(8,128)(2,1)}, u32[]{:S(2)}, u32[]{:S(2)}) collective-permute-start(bf16[576,512]{1,0:T(8,128)(2,1)S(1)} %copy-done), channel_id=1, source_target_pairs={{8,16},{12,20},{16,8},{20,12},{9,17},{13,21},{17,9},{21,13},{10,18... | collective-permute-start | bytes 1769480 | tf_op jit(solution)/shard_map/ppermute | solution.py:584
  42.5 13.4 %collective-permute-start.4 = (bf16[2,256,512]{2,1,0:T(8,128)(2,1)S(1)}, bf16[2,256,512]{2,1,0:T(8,128)(2,1)S(1)}, u32[]{:S(2)}, u32[]{:S(2)}) collective-permute-start(bf16[2,256,512]{2,1,0:T(8,128)(2,1)S(1)} %get-tuple-element.28.x_column), channel_id=1, source_target_pairs={{0,4},{4,0},{1,5},{5,1},{2,6},{6,2},{3,7},{7,3},{8,12},{12,8},{9,1... | collective-permute-start | bytes 1572872 | tf_op jit(solution)/shard_map/ppermute | solution.py:606
  43.4 12.5 %collective-permute-start.6 = (bf16[2,256,512]{2,1,0:T(8,128)(2,1)S(1)}, bf16[2,256,512]{2,1,0:T(8,128)(2,1)S(1)}, u32[]{:S(2)}, u32[]{:S(2)}) collective-permute-start(bf16[2,256,512]{2,1,0:T(8,128)(2,1)S(1)} %get-tuple-element.29.y_column), channel_id=1, source_target_pairs={{0,16},{4,20},{8,0},{12,4},{16,24},{20,28},{24,8},{28,12},{1,17},{... | collective-permute-start | bytes 1572872 | tf_op jit(solution)/shard_map/ppermute | solution.py:603
  43.4 14.6 %collective-permute-start.5 = (bf16[2,256,512]{2,1,0:T(8,128)(2,1)S(1)}, bf16[2,256,512]{2,1,0:T(8,128)(2,1)S(1)}, u32[]{:S(2)}, u32[]{:S(2)}) collective-permute-start(bf16[2,256,512]{2,1,0:T(8,128)(2,1)S(1)} %get-tuple-element.29.y_column), channel_id=1, source_target_pairs={{8,16},{12,20},{16,8},{20,12},{9,17},{13,21},{17,9},{21,13},{10,18... | collective-permute-start | bytes 1572872 | tf_op jit(solution)/shard_map/ppermute | solution.py:603
  47.6 8.0 %collective-permute-start.7 = (bf16[4,64,512]{2,1,0:T(8,128)(2,1)S(1)}, bf16[4,64,512]{2,1,0:T(8,128)(2,1)S(1)}, u32[]{:S(2)}, u32[]{:S(2)}) collective-permute-start(bf16[4,64,512]{2,1,0:T(8,128)(2,1)S(1)} %get-tuple-element.30.c0), channel_id=1, source_target_pairs={{0,1},{1,0},{2,3},{3,2},{4,5},{5,4},{6,7},{7,6},{8,9},{9,8},{10,11... | collective-permute-start | bytes 786440 | tf_op jit(solution)/shard_map/ppermute | solution.py:609
  58.8 30.6 %collective-permute-start.10 = (bf16[2,2,256,512]{3,2,1,0:T(8,128)(2,1)S(1)}, bf16[2,2,256,512]{3,2,1,0:T(8,128)(2,1)S(1)}, u32[]{:S(2)}, u32[]{:S(2)}) collective-permute-start(bf16[2,2,256,512]{3,2,1,0:T(8,128)(2,1)S(1)} %get-tuple-element.32.yb), channel_id=1, source_target_pairs={{0,4},{4,0},{1,5},{5,1},{2,6},{6,2},{3,7},{7,3},{8,12},{12,8},{9,1... | collective-permute-start | bytes 3145736 | tf_op jit(solution)/shard_map/ppermute | solution.py:606
  59.1 30.3 %collective-permute-start.9 = (bf16[2,2,256,512]{3,2,1,0:T(8,128)(2,1)S(1)}, bf16[2,2,256,512]{3,2,1,0:T(8,128)(2,1)S(1)}, u32[]{:S(2)}, u32[]{:S(2)}) collective-permute-start(bf16[2,2,256,512]{3,2,1,0:T(8,128)(2,1)S(1)} %get-tuple-element.31.xb), channel_id=1, source_target_pairs={{0,16},{4,20},{8,0},{12,4},{16,24},{20,28},{24,8},{28,12},{1,17},{... | collective-permute-start | bytes 3145736 | tf_op jit(solution)/shard_map/ppermute | solution.py:603
  59.1 30.3 %collective-permute-start.8 = (bf16[2,2,256,512]{3,2,1,0:T(8,128)(2,1)S(1)}, bf16[2,2,256,512]{3,2,1,0:T(8,128)(2,1)S(1)}, u32[]{:S(2)}, u32[]{:S(2)}) collective-permute-start(bf16[2,2,256,512]{3,2,1,0:T(8,128)(2,1)S(1)} %get-tuple-element.31.xb), channel_id=1, source_target_pairs={{8,16},{12,20},{16,8},{20,12},{9,17},{13,21},{17,9},{21,13},{10,18... | collective-permute-start | bytes 3145736 | tf_op jit(solution)/shard_map/ppermute | solution.py:603
  63.8 20.9 %collective-permute-start.11 = (bf16[4,64,512]{2,1,0:T(8,128)(2,1)S(1)}, bf16[4,64,512]{2,1,0:T(8,128)(2,1)S(1)}, u32[]{:S(2)}, u32[]{:S(2)}) collective-permute-start(bf16[4,64,512]{2,1,0:T(8,128)(2,1)S(1)} %get-tuple-element.30.c0), channel_id=1, source_target_pairs={{0,2},{1,3},{2,0},{3,1},{4,6},{5,7},{6,4},{7,5},{8,10},{9,11},{10,... | collective-permute-start | bytes 786440 | tf_op jit(solution)/shard_map/ppermute | solution.py:609
  66.6 22.8 %collective-permute-start.12 = (bf16[4,64,512]{2,1,0:T(8,128)(2,1)S(1)}, bf16[4,64,512]{2,1,0:T(8,128)(2,1)S(1)}, u32[]{:S(2)}, u32[]{:S(2)}) collective-permute-start(bf16[4,64,512]{2,1,0:T(8,128)(2,1)S(1)} %collective-permute-done.7.rows_next.c1), channel_id=1, source_target_pairs={{0,2},{1,3},{2,0},{3,1},{4,6},{5,7},{6,4},{7,5},{8,10},{9,11},{10,... | collective-permute-start | bytes 786440 | tf_op jit(solution)/shard_map/ppermute | solution.py:609
  90.4 10.7 %collective-permute-start.13 = (bf16[2,512,512]{2,1,0:T(8,128)(2,1)S(1)}, bf16[2,512,512]{2,1,0:T(8,128)(2,1)S(1)}, u32[]{:S(2)}, u32[]{:S(2)}) collective-permute-start(bf16[2,512,512]{2,1,0:T(8,128)(2,1)S(1)} %get-tuple-element.34.w_high), channel_id=1, source_target_pairs={{0,8},{16,24},{1,9},{17,25},{2,10},{18,26},{3,11},{19,27},{4,12},{... | collective-permute-start | bytes 3145736 | tf_op jit(solution)/shard_map/ppermute | solution.py:662
  111.8 3.6 %collective-permute-start.14 = (bf16[2,512,512]{2,1,0:T(8,128)(2,1)S(1)}, bf16[2,512,512]{2,1,0:T(8,128)(2,1)S(1)}, u32[]{:S(2)}, u32[]{:S(2)}) collective-permute-start(bf16[2,512,512]{2,1,0:T(8,128)(2,1)S(1)} %get-tuple-element.35), channel_id=1, source_target_pairs={{8,0},{24,16},{9,1},{25,17},{10,2},{26,18},{11,3},{27,19},{12,4},{... | collective-permute-start | bytes 3145736 | tf_op jit(solution)/shard_map/ppermute | solution.py:683
  115.4 30.8 %copy-start.1 = (s32[6]{0:T(128)S(1)}, s32[6]{0:T(128)}, u32[]{:S(2)}) copy-start(s32[6]{0:T(128)} %stack.83.place) | copy-start | bytes 76
  116.5 12.9 %collective-permute-start.16 = (bf16[2,256,512]{2,1,0:T(8,128)(2,1)S(1)}, bf16[2,256,512]{2,1,0:T(8,128)(2,1)S(1)}, u32[]{:S(2)}, u32[]{:S(2)}) collective-permute-start(bf16[2,256,512]{2,1,0:T(8,128)(2,1)S(1)} %get-tuple-element.38), channel_id=1, source_target_pairs={{4,0},{0,4},{20,8},{16,12},{12,16},{8,20},{28,24},{24,28},{5,1},{1... | collective-permute-start | bytes 1572872 | tf_op jit(solution)/shard_map/ppermute | solution.py:702
  122.4 11.8 %collective-permute-start.17 = (bf16[2,256,512]{2,1,0:T(8,128)(2,1)S(1)}, bf16[2,256,512]{2,1,0:T(8,128)(2,1)S(1)}, u32[]{:S(2)}, u32[]{:S(2)}) collective-permute-start(bf16[2,256,512]{2,1,0:T(8,128)(2,1)S(1)} %get-tuple-element.39), channel_id=1, source_target_pairs={{16,0},{20,4},{0,8},{4,12},{24,16},{28,20},{8,24},{12,28},{17,1},{... | collective-permute-start | bytes 1572872 | tf_op jit(solution)/shard_map/ppermute | solution.py:702
  122.4 23.7 %collective-permute-start.18 = (bf16[2,256,512]{2,1,0:T(8,128)(2,1)S(1)}, bf16[2,256,512]{2,1,0:T(8,128)(2,1)S(1)}, u32[]{:S(2)}, u32[]{:S(2)}) collective-permute-start(bf16[2,256,512]{2,1,0:T(8,128)(2,1)S(1)} %get-tuple-element.40), channel_id=1, source_target_pairs={{20,0},{16,4},{4,8},{0,12},{28,16},{24,20},{12,24},{8,28},{21,1},{... | collective-permute-start | bytes 1572872 | tf_op jit(solution)/shard_map/ppermute | solution.py:702
  122.6 23.6 %collective-permute-start.15 = (bf16[2,256,512]{2,1,0:T(8,128)(2,1)S(1)}, bf16[2,256,512]{2,1,0:T(8,128)(2,1)S(1)}, u32[]{:S(2)}, u32[]{:S(2)}) collective-permute-start(bf16[2,256,512]{2,1,0:T(8,128)(2,1)S(1)} %get-tuple-element.37.own), channel_id=1, source_target_pairs={{16,8},{20,12},{8,16},{12,20},{17,9},{21,13},{9,17},{13,21},{18,10... | collective-permute-start | bytes 1572872 | tf_op jit(solution)/shard_map/ppermute | solution.py:702

commit v8 on v7

--- a/solution.py
+++ b/solution.py
@@ -180,45 +180,30 @@
         self.received.wait()
 
 
-def pack_kernel(place, field, coupling, x_factor, y_factor, *rest):
-    pieces, (blocks, held, shard, sems, csems, osems, fsems) = rest[:-7], rest[-7:]
+def pack_kernel(place, field, coupling, *rest):
+    pieces, (sems, csems) = rest[:-2], rest[-2:]
     rows_here = field.shape[1]
-    height = x_factor.shape[1]
+    height = pieces[0].shape[0] - 2 * rows_here
     own = pl.ds(pl.multiple_of(place[len(pieces)] * height, height), height)
-    factors = [
-        pltpu.make_async_copy(factor, shard.at[pl.ds(2 * which, 2)], fsems.at[which])
-        for which, factor in enumerate((x_factor, y_factor))
-    ]
-    start_all(factors)
-    incoming = []
+    copies = []
     for index, piece in enumerate(pieces):
         width = piece.shape[1]
         offset = pl.multiple_of(place[index] * width, width)
-        copies = [
-            pltpu.make_async_copy(
-                field.at[plane, :, pl.ds(offset, width)],
-                held.at[index, pl.ds(plane * rows_here, rows_here)],
-                sems.at[index, plane],
+        for plane in range(2):
+            copies.append(
+                pltpu.make_async_copy(
+                    field.at[plane, :, pl.ds(offset, width)],
+                    piece.at[pl.ds(plane * rows_here, rows_here)],
+                    sems.at[index, plane],
+                )
             )
-            for plane in range(2)
-        ]
         copies.append(
             pltpu.make_async_copy(
-                coupling.at[own], held.at[index, pl.ds(2 * rows_here, height)], csems.at[index]
+                coupling.at[own], piece.at[pl.ds(2 * rows_here, height)], csems.at[index]
             )
         )
-        start_all(copies)
-        incoming.append(copies)
-    outgoing = []
-    wait_all(factors)
-    for target in range(blocks.shape[0]):
-        outgoing.append(pltpu.make_async_copy(shard, blocks.at[target], fsems.at[2 + target]))
-        outgoing[-1].start()
-    for index, piece in enumerate(pieces):
-        wait_all(incoming[index])
-        outgoing.append(pltpu.make_async_copy(held.at[index], piece, osems.at[index]))
-        outgoing[-1].start()
-    wait_all(outgoing)
+    start_all(copies)
+    wait_all(copies)
 
 
 def unpack_kernel(place, own, *rest):
@@ -258,7 +243,7 @@
     wait_all(copies)
 
 
-def both_kernel(info, x_column, x_aside, y_column, y0, y1, rows_next, x_both, y_both, sems):
+def both_kernel(info, x_column, x_aside, y_column, y0, y1, rows_next, rows_far, x_both, y_both, sems):
     copies = [
         pltpu.make_async_copy(x_column, x_both.at[0], sems.at[0]),
         pltpu.make_async_copy(x_aside, x_both.at[1], sems.at[1]),
@@ -369,7 +354,7 @@
     def apply(self, slot, source, below, store, fresh):
         order = self.order
         turned = (((1,), (1,)), ((), ()))
-        if fresh:
+        if 1 in fresh:
             self.ready(slot, 1)
         for rows in row_chunks(order, 256):
             real, imag = source(0, rows), source(1, rows)
@@ -388,7 +373,7 @@
             below[rows, order:] = imag
             below[further, :order] = -imag
             below[further, order:] = real
-        if fresh:
+        if 0 in fresh:
             self.ready(slot, 0)
         for plane in range(2):
             for columns in row_chunks(order, 256):
@@ -445,13 +430,14 @@
         layers = Layers(info, (xb, x0, x1), (yb, yf), (c0, c1, c2, c3), held, weights, fsems, csems)
         fields = (own, (p0, p1, p2, p3), rhs, sems)
         layers.start(0, *fields)
+        layers.wait(0, *fields)
+        layers.ready(0, 1)
         layers.start(1, *fields)
-        layers.wait(0, *fields)
         zero = reduced(rhs, info, 0, weights, lambda plane, rows: f32(0.0))
-        layers.apply(0, zero, below, round_into(w_low), True)
+        layers.apply(0, zero, below, round_into(w_low), (0,))
         layers.wait(1, *fields)
         one = reduced(rhs, info, 1, weights, lambda plane, rows: w_low[plane, rows].astype(f32))
-        layers.apply(1, one, below, round_into(w_high), True)
+        layers.apply(1, one, below, round_into(w_high), (0, 1))
 
 
 def last_kernel(info, xb, x0, x1, yb, yf, c0, c1, c2, c3, own, p0, p1, p2, p3, arrived, field, back,
@@ -461,15 +447,16 @@
         layers = Layers(info, (xb, x0, x1), (yb, yf), (c0, c1, c2, c3), held, weights, fsems, csems)
         fields = (own, (p0, p1, p2, p3), rhs, sems)
         layers.start(0, *fields)
+        layers.wait(0, *fields)
+        layers.ready(0, 1)
         layers.start(1, *fields)
-        layers.wait(0, *fields)
         low, high = field.at[0], field.at[1]
         two = reduced(rhs, info, 0, weights, lambda plane, rows: arrived[plane, rows].astype(f32))
-        layers.apply(0, two, below, round_into(forward), True)
+        layers.apply(0, two, below, round_into(forward), (0,))
         layers.wait(1, *fields)
         three = reduced(rhs, info, 1, weights, lambda plane, rows: forward[plane, rows].astype(f32))
-        layers.apply(1, three, below, round_into(high), True)
-        layers.apply(0, sent(weights, 1, high), below, subtract_into(low, forward), False)
+        layers.apply(1, three, below, round_into(high), (0, 1))
+        layers.apply(0, sent(weights, 1, high), below, subtract_into(low, forward), ())
         last = sent(weights, 0, low)
         for plane in range(2):
             for rows in row_chunks(weights.shape[1], 256):
@@ -493,17 +480,18 @@
         layers = Layers(info, (xb, x0, x1), (yb, yf), (c0, c1, c2, c3), held, weights, fsems, csems)
         layers.start_y(1)
         layers.start_x(1)
+        layers.ready(1, 1)
         high_rows = layers.weight_copies(1)
         start_all(high_rows)
         layers.start_y(0)
         layers.start_x(0)
         low, high = kept.at[0], kept.at[1]
         layers.apply(
-            1, lambda plane, rows: arrived[plane, rows], below, subtract_into(high, w_high), True
+            1, lambda plane, rows: arrived[plane, rows], below, subtract_into(high, w_high), (0,)
         )
         start_pieces(kept, 1)
         wait_all(high_rows)
-        layers.apply(0, sent(weights, 1, high), below, subtract_into(low, w_low), True)
+        layers.apply(0, sent(weights, 1, high), below, subtract_into(low, w_low), (0, 1))
         start_pieces(kept, 0)
 
     @pl.when(info[info_member] != 0)
@@ -564,22 +552,19 @@
         + [own_y, group == member]
     ).astype(jnp.int32)
     piece_shape = jax.ShapeDtypeStruct((2, rows_here, order), bf16)
-    *packed, blocks = pl.pallas_call(
+    shard = jnp.concatenate([x_factor[0], y_factor[0]], axis=0)
+    blocks = jnp.broadcast_to(shard[None], (py_count,) + shard.shape)
+    packed = pl.pallas_call(
         pack_kernel,
-        out_shape=[jax.ShapeDtypeStruct((2 * rows_here + height, order), bf16)] * len(rounds)
-        + [jax.ShapeDtypeStruct((py_count, 4, height, order), bf16)],
-        in_specs=[in_smem] + [anywhere] * 4,
-        out_specs=[anywhere] * (len(rounds) + 1),
+        out_shape=[jax.ShapeDtypeStruct((2 * rows_here + height, order), bf16)] * len(rounds),
+        in_specs=[in_smem] + [anywhere] * 2,
+        out_specs=[in_vmem] * len(rounds),
         scratch_shapes=[
-            pltpu.VMEM((len(rounds), 2 * rows_here + height, order), bf16),
-            pltpu.VMEM((4, height, order), bf16),
             pltpu.SemaphoreType.DMA((len(rounds), 2)),
             pltpu.SemaphoreType.DMA((len(rounds),)),
-            pltpu.SemaphoreType.DMA((len(rounds),)),
-            pltpu.SemaphoreType.DMA((2 + py_count,)),
         ],
-        compiler_params=pltpu.CompilerParams(vmem_limit_bytes=60 * 1024 * 1024),
-    )(sends_to, field, coupling[0], x_factor[0], y_factor[0])
+        compiler_params=params,
+    )(sends_to, field, coupling[0])
     pieces = [
         lax.ppermute(piece, ("sec", "px"), pairs(a, b)) for piece, (a, b) in zip(packed, rounds)
     ]
@@ -615,11 +600,11 @@
     x_both, y_both = pl.pallas_call(
         both_kernel,
         out_shape=[jax.ShapeDtypeStruct((2,) + column_shape.shape, bf16)] * 2,
-        in_specs=[in_smem] + [anywhere] * 6,
+        in_specs=[in_smem] + [anywhere] * 7,
         out_specs=[in_vmem] * 2,
         scratch_shapes=[pltpu.SemaphoreType.DMA((4,))],
         compiler_params=params,
-    )(info, x_column, x_aside, y_column, *y_near, rows_next)
+    )(info, x_column, x_aside, y_column, *y_near, rows_next, rows_far)
     y_far = aside(y_both)
     x_across = [across(x_both, a) for a in range(2)]
     factors = [x_both, *x_across, y_both, y_far, rows_held, rows_next, rows_far, over_z(rows_next, 2)]
@@ -705,7 +690,7 @@
         unpack_kernel,
         out_shape=jax.ShapeDtypeStruct(field.shape, bf16),
         in_specs=[in_smem] + [anywhere] * (len(rounds) + 1),
-        out_specs=in_vmem,
+        out_specs=anywhere,
         scratch_shapes=[pltpu.SemaphoreType.DMA((len(rounds),))],
         compiler_params=params,
     )(sends_to, results[0], *received)

time: 149 us -> 150 us (level)
  Pallas kernels: 22.3 us -> 19.7 us
  waiting for transfers between devices: 80.8 us -> 83.2 us
    ppermute x2, waiting for transfers between devices: 0.24 us -> 7.6 us  [aside(): return lax.ppermute(block, 'px', [(y, (y + 1) % 2) for y in range(2)])]
    ppermute x3, waiting for transfers between devices: 29 us -> 23.7 us  [over_z(): return lax.ppermute(block, 'py', [(z, z ^ bit) for z in range(py_count)])]
    ppermute x4, starting transfers between devices: 8.85 us -> 6.77 us  [across(): return lax.ppermute(block, ('sec', 'px'), pairs(a, 0))]
    pallas_call x1, Pallas kernels: 4.38 us -> 2.58 us  [on_device(): pl.pallas_call(pack_kernel, out_shape=[jax.ShapeDtypeStruct((2 * rows_her...]
    ppermute x4, waiting for transfers between devices: 18.1 us -> 19.6 us  [on_device(): lax.ppermute(piece, ('sec', 'px'), back_pairs(a, b))]
  transfers between devices with their start and end apart: 20 -> 20, of which waited for: 13 -> 13; matrix products, arithmetic and copies ran while one was open for 0% -> 1% of each run, Pallas kernels for 0% -> 2%
where the time goes in v8:
time: 150 us
  waiting for transfers between devices  83.2 us (55%)
  starting transfers between devices  40.6 us (27%)
  Pallas kernels  19.7 us (13%)
  between operations  3.09 us (2%)
  local copies, waits for them, and re-layouts  1.88 us (1%)
    ppermute x3, waiting for transfers between devices, over_z(): return lax.ppermute(block, 'py', [(z, z ^ bit) for z in range(py_count)])  23.7 us
    ppermute x4, waiting for transfers between devices, on_device(): lax.ppermute(piece, ('sec', 'px'), back_pairs(a, b))  19.6 us
    ppermute x4, waiting for transfers between devices, on_device(): lax.ppermute(piece, ('sec', 'px'), pairs(a, b))  19.4 us
    ppermute x4, starting transfers between devices, on_device(): lax.ppermute(piece, ('sec', 'px'), back_pairs(a, b))  12.4 us
    pallas_call x1, Pallas kernels, on_device(): pl.pallas_call(last_kernel, out_shape=[jax.ShapeDtypeStruct((2, 2, order,...  10.8 us
    ppermute x1, waiting for transfers between devices, on_device(): incoming = lax.ppermute(w_high, 'sec', up)  9.81 us
    ppermute x2, waiting for transfers between devices, aside(): return lax.ppermute(block, 'px', [(y, (y + 1) % 2) for y in range(2)])  7.6 us
    ppermute x4, starting transfers between devices, on_device(): lax.ppermute(piece, ('sec', 'px'), pairs(a, b))  6.94 us
  transfers between devices with their start and end apart: 20, of which 13 were waited for; matrix products, arithmetic and copies ran while one was open for 1% of the time, Pallas kernels for 2%

profile of v8, /device:TPU:1, one launch (start us, length us, event | category | flops | bytes accessed | tf_op | source)
XLA Modules:
  0.0 149.7 jit_solution(13214441651969254933)
XLA Ops:
  0.0 1.1 pad_maximum_fusion
  1.1 1.1 broadcast_in_dim.4
  2.2 5.6 %all-to-all-start = ((bf16[4,4,64,512]{3,2,1,0:T(8,128)(2,1)}), bf16[4,4,64,512]{3,2,1,0:T(8,128)(2,1)S(1)}, u32[]{:S(2)}, u32[]{:S(2)}) async-start(bf16[4,4,64,512]{3,2,1,0:T(8,128)(2,1)} %broadcast_in_dim.4), calls=%async_computation | async-start | bytes 2097152 | tf_op jit(solution)/shard_map/all_to_all | solution.py:571
  7.9 2.6 %shard_map.55 = (bf16[576,512]{1,0:T(8,128)(2,1)}, bf16[576,512]{1,0:T(8,128)(2,1)}, bf16[576,512]{1,0:T(8,128)(2,1)}, bf16[576,512]{1,0:T(8,128)(2,1)}) custom-call(s32[6]{0:T(128)S(1)} %stack.83.place, bf16[2,256,2048]{2,1,0:T(8,128)(2,1)S(1)} %bitcast.28, bf16[256,512]{1,0:T(8,128)(2,1)S(1)} %bitcast.29), custom_call_target="tpu_custom_call" | custom-call | tf_op jit(solution)/shard_map/pallas_call | solution.py:557
  10.5 3.1 %collective-permute-start.1 = (bf16[576,512]{1,0:T(8,128)(2,1)}, bf16[576,512]{1,0:T(8,128)(2,1)S(1)}, u32[]{:S(2)}, u32[]{:S(2)}) collective-permute-start(bf16[576,512]{1,0:T(8,128)(2,1)} %get-tuple-element.23), channel_id=1, source_target_pairs={{0,4},{4,0},{8,20},{12,16},{16,12},{20,8},{24,28},{28,24},{1,5},{5... | collective-permute-start | bytes 1769480 | tf_op jit(solution)/shard_map/ppermute | solution.py:569
  14.1 3.3 %collective-permute-start = (bf16[576,512]{1,0:T(8,128)(2,1)}, bf16[576,512]{1,0:T(8,128)(2,1)S(1)}, u32[]{:S(2)}, u32[]{:S(2)}) collective-permute-start(bf16[576,512]{1,0:T(8,128)(2,1)} %get-tuple-element.22.own), channel_id=1, source_target_pairs={{8,16},{12,20},{16,8},{20,12},{9,17},{13,21},{17,9},{21,13},{10,18... | collective-permute-start | bytes 1769480 | tf_op jit(solution)/shard_map/ppermute | solution.py:569
  20.9 5.8 %collective-permute-done.1.p1 = bf16[576,512]{1,0:T(8,128)(2,1)S(1)} collective-permute-done((bf16[576,512]{1,0:T(8,128)(2,1)}, bf16[576,512]{1,0:T(8,128)(2,1)S(1)}, u32[]{:S(2)}, u32[]{:S(2)}) %collective-permute-start.1) | collective-permute-done | bytes 589856 | tf_op jit(solution)/shard_map/ppermute | solution.py:569
  26.7 2.4 %collective-permute-done.2.p2 = bf16[576,512]{1,0:T(8,128)(2,1)S(1)} collective-permute-done((bf16[576,512]{1,0:T(8,128)(2,1)}, bf16[576,512]{1,0:T(8,128)(2,1)S(1)}, u32[]{:S(2)}, u32[]{:S(2)}) %collective-permute-start.2) | collective-permute-done | bytes 589856 | tf_op jit(solution)/shard_map/ppermute | solution.py:569
  29.1 11.2 %collective-permute-done.3.p3 = bf16[576,512]{1,0:T(8,128)(2,1)S(1)} collective-permute-done((bf16[576,512]{1,0:T(8,128)(2,1)}, bf16[576,512]{1,0:T(8,128)(2,1)S(1)}, u32[]{:S(2)}, u32[]{:S(2)}) %collective-permute-start.3) | collective-permute-done | bytes 589856 | tf_op jit(solution)/shard_map/ppermute | solution.py:569
  40.3 1.7 %shard_map.56 = (bf16[2,256,512]{2,1,0:T(8,128)(2,1)S(1)}, bf16[2,256,512]{2,1,0:T(8,128)(2,1)S(1)}, bf16[4,64,512]{2,1,0:T(8,128)(2,1)S(1)}) custom-call(s32[21]{0:T(128)S(1)} %stack.98.info, bf16[4,4,64,512]{3,2,1,0:T(8,128)(2,1)S(1)} %all-to-all-done.blocks, bf16[576,512]{1,0:T(8,128)(2,1)} %get-tuple-element.22.own, ...), custom_call_target="tpu_custom_call" | custom-call | tf_op jit(solution)/shard_map/pallas_call | solution.py:575
  42.0 0.9 collective-permute-start.4
  43.0 4.2 %collective-permute-start.5 = (bf16[2,256,512]{2,1,0:T(8,128)(2,1)S(1)}, bf16[2,256,512]{2,1,0:T(8,128)(2,1)S(1)}, u32[]{:S(2)}, u32[]{:S(2)}) collective-permute-start(bf16[2,256,512]{2,1,0:T(8,128)(2,1)S(1)} %get-tuple-element.27.y_column), channel_id=1, source_target_pairs={{8,16},{12,20},{16,8},{20,12},{9,17},{13,21},{17,9},{21,13},{10,18... | collective-permute-start | bytes 1572872 | tf_op jit(solution)/shard_map/ppermute | solution.py:588
  47.1 2.7 %collective-permute-start.8 = (bf16[4,64,512]{2,1,0:T(8,128)(2,1)S(1)}, bf16[4,64,512]{2,1,0:T(8,128)(2,1)S(1)}, u32[]{:S(2)}, u32[]{:S(2)}) collective-permute-start(bf16[4,64,512]{2,1,0:T(8,128)(2,1)S(1)} %get-tuple-element.28.c0), channel_id=1, source_target_pairs={{0,2},{1,3},{2,0},{3,1},{4,6},{5,7},{6,4},{7,5},{8,10},{9,11},{10,... | collective-permute-start | bytes 786440 | tf_op jit(solution)/shard_map/ppermute | solution.py:594
  49.8 1.2 collective-permute-start.7
  51.0 10.5 %collective-permute-done.8.rows_far.c2 = bf16[4,64,512]{2,1,0:T(8,128)(2,1)S(1)} collective-permute-done((bf16[4,64,512]{2,1,0:T(8,128)(2,1)S(1)}, bf16[4,64,512]{2,1,0:T(8,128)(2,1)S(1)}, u32[]{:S(2)}, u32[]{:S(2)}) %collective-permute-start.8) | collective-permute-done | bytes 262176 | tf_op jit(solution)/shard_map/ppermute | solution.py:594
  63.8 1.9 %collective-permute-start.9 = (bf16[2,2,256,512]{3,2,1,0:T(8,128)(2,1)S(1)}, bf16[2,2,256,512]{3,2,1,0:T(8,128)(2,1)S(1)}, u32[]{:S(2)}, u32[]{:S(2)}) collective-permute-start(bf16[2,2,256,512]{3,2,1,0:T(8,128)(2,1)S(1)} %get-tuple-element.29.xb), channel_id=1, source_target_pairs={{8,16},{12,20},{16,8},{20,12},{9,17},{13,21},{17,9},{21,13},{10,18... | collective-permute-start | bytes 3145736 | tf_op jit(solution)/shard_map/ppermute | solution.py:588
  65.8 1.2 collective-permute-start.12
  67.0 12.7 %collective-permute-done.12.c3 = bf16[4,64,512]{2,1,0:T(8,128)(2,1)S(1)} collective-permute-done((bf16[4,64,512]{2,1,0:T(8,128)(2,1)S(1)}, bf16[4,64,512]{2,1,0:T(8,128)(2,1)S(1)}, u32[]{:S(2)}, u32[]{:S(2)}) %collective-permute-start.12) | collective-permute-done | bytes 262176 | tf_op jit(solution)/shard_map/ppermute | solution.py:594
  79.6 7.6 %collective-permute-done.11.yf = bf16[2,2,256,512]{3,2,1,0:T(8,128)(2,1)S(1)} collective-permute-done((bf16[2,2,256,512]{3,2,1,0:T(8,128)(2,1)S(1)}, bf16[2,2,256,512]{3,2,1,0:T(8,128)(2,1)S(1)}, u32[]{:S(2)}, u32[]{:S(2)}) %collective-permute-start.11) | collective-permute-done | bytes 1048608 | tf_op jit(solution)/shard_map/ppermute | solution.py:591
  88.1 0.9 shard_map.58
  89.0 1.3 collective-permute-start.13
  90.3 9.8 %collective-permute-done.13.arrived = bf16[2,512,512]{2,1,0:T(8,128)(2,1)S(1)} collective-permute-done((bf16[2,512,512]{2,1,0:T(8,128)(2,1)S(1)}, bf16[2,512,512]{2,1,0:T(8,128)(2,1)S(1)}, u32[]{:S(2)}, u32[]{:S(2)}) %collective-permute-start.13) | collective-permute-done | bytes 1048608 | tf_op jit(solution)/shard_map/ppermute | solution.py:647
  100.1 10.8 %shard_map.59 = (bf16[2,2,512,512]{3,2,1,0:T(8,128)(2,1)S(1)}, bf16[2,512,512]{2,1,0:T(8,128)(2,1)S(1)}) custom-call(s32[21]{0:T(128)S(1)} %stack.98.info, bf16[2,2,256,512]{3,2,1,0:T(8,128)(2,1)S(1)} %get-tuple-element.29.xb, bf16[2,2,256,512]{3,2,1,0:T(8,128)(2,1)S(1)} %collective-permute-done.9.x0, ...), custom_call_target="tpu_custom_call" | custom-call | flops 6442450944 | bytes 8388608 | tf_op jit(solution)/shard_map/pallas_call | solution.py:648
  111.0 1.4 collective-permute-start.14
  112.3 2.2 %collective-permute-done.14.arrived = bf16[2,512,512]{2,1,0:T(8,128)(2,1)S(1)} collective-permute-done((bf16[2,512,512]{2,1,0:T(8,128)(2,1)S(1)}, bf16[2,512,512]{2,1,0:T(8,128)(2,1)S(1)}, u32[]{:S(2)}, u32[]{:S(2)}) %collective-permute-start.14) | collective-permute-done | bytes 1048608 | tf_op jit(solution)/shard_map/ppermute | solution.py:668
  114.5 1.1 shard_map.60
  115.6 8.3 %collective-permute-start.16 = (bf16[2,256,512]{2,1,0:T(8,128)(2,1)S(1)}, bf16[2,256,512]{2,1,0:T(8,128)(2,1)S(1)}, u32[]{:S(2)}, u32[]{:S(2)}) collective-permute-start(bf16[2,256,512]{2,1,0:T(8,128)(2,1)S(1)} %get-tuple-element.36), channel_id=1, source_target_pairs={{4,0},{0,4},{20,8},{16,12},{12,16},{8,20},{28,24},{24,28},{5,1},{1... | collective-permute-start | bytes 1572872 | tf_op jit(solution)/shard_map/ppermute | solution.py:687
  124.1 3.9 %collective-permute-start.15 = (bf16[2,256,512]{2,1,0:T(8,128)(2,1)S(1)}, bf16[2,256,512]{2,1,0:T(8,128)(2,1)S(1)}, u32[]{:S(2)}, u32[]{:S(2)}) collective-permute-start(bf16[2,256,512]{2,1,0:T(8,128)(2,1)S(1)} %get-tuple-element.35.own), channel_id=1, source_target_pairs={{16,8},{20,12},{8,16},{12,20},{17,9},{21,13},{9,17},{13,21},{18,10... | collective-permute-start | bytes 1572872 | tf_op jit(solution)/shard_map/ppermute | solution.py:687
  128.0 3.0 %collective-permute-done.16.rest_1_ = bf16[2,256,512]{2,1,0:T(8,128)(2,1)S(1)} collective-permute-done((bf16[2,256,512]{2,1,0:T(8,128)(2,1)S(1)}, bf16[2,256,512]{2,1,0:T(8,128)(2,1)S(1)}, u32[]{:S(2)}, u32[]{:S(2)}) %collective-permute-start.16) | collective-permute-done | bytes 524320 | tf_op jit(solution)/shard_map/ppermute | solution.py:687
  130.9 4.8 %collective-permute-done.17.rest_2_ = bf16[2,256,512]{2,1,0:T(8,128)(2,1)S(1)} collective-permute-done((bf16[2,256,512]{2,1,0:T(8,128)(2,1)S(1)}, bf16[2,256,512]{2,1,0:T(8,128)(2,1)S(1)}, u32[]{:S(2)}, u32[]{:S(2)}) %collective-permute-start.17) | collective-permute-done | bytes 524320 | tf_op jit(solution)/shard_map/ppermute | solution.py:687
  135.8 11.8 %collective-permute-done.18.rest_3_ = bf16[2,256,512]{2,1,0:T(8,128)(2,1)S(1)} collective-permute-done((bf16[2,256,512]{2,1,0:T(8,128)(2,1)S(1)}, bf16[2,256,512]{2,1,0:T(8,128)(2,1)S(1)}, u32[]{:S(2)}, u32[]{:S(2)}) %collective-permute-start.18) | collective-permute-done | bytes 524320 | tf_op jit(solution)/shard_map/ppermute | solution.py:687
  147.6 1.9 %shard_map.61 = bf16[2,256,2048]{2,1,0:T(8,128)(2,1)} custom-call(s32[6]{0:T(128)S(1)} %stack.83.place, bf16[2,256,512]{2,1,0:T(8,128)(2,1)S(1)} %get-tuple-element.35.own, bf16[2,256,512]{2,1,0:T(8,128)(2,1)S(1)} %collective-permute-done.15.rest_0_, bf16[2,256,512]{2,1,0:T(8,128)(2,1)S(1)} %collective-permute-done.16.rest_1_, ...), custom_call_target="tpu_custom_call" | custom-call | tf_op jit(solution)/shard_map/pallas_call | solution.py:689
  (26 shorter events, 4.7 us)
Async XLA Ops:
  0.0 7.9 %copy-start.1 = (bf16[1,256,512]{2,1,0:T(8,128)(2,1)S(1)}, bf16[1,256,512]{2,1,0:T(8,128)(2,1)}, u32[]{:S(2)}) copy-start(bf16[1,256,512]{2,1,0:T(8,128)(2,1)} %param.7) | copy-start | bytes 786436
  0.0 7.9 %copy-start = (bf16[2,1,256,2048]{3,2,1,0:T(8,128)(2,1)S(1)}, bf16[2,1,256,2048]{3,2,1,0:T(8,128)(2,1)}, u32[]{:S(2)}) copy-start(bf16[2,1,256,2048]{3,2,1,0:T(8,128)(2,1)} %param.5) | copy-start | bytes 6291460
  2.2 15.3 %copy-start.2 = (s32[16]{0:T(128)S(1)}, s32[16]{0:T(128)}, u32[]{:S(2)}) copy-start(s32[16]{0:T(128)} %param.6) | copy-start | bytes 196
  2.2 38.1 %all-to-all-start = ((bf16[4,4,64,512]{3,2,1,0:T(8,128)(2,1)}), bf16[4,4,64,512]{3,2,1,0:T(8,128)(2,1)S(1)}, u32[]{:S(2)}, u32[]{:S(2)}) async-start(bf16[4,4,64,512]{3,2,1,0:T(8,128)(2,1)} %broadcast_in_dim.4), calls=%async_computation | async-start | bytes 2097152 | tf_op jit(solution)/shard_map/all_to_all | solution.py:571
  10.5 16.3 %collective-permute-start.1 = (bf16[576,512]{1,0:T(8,128)(2,1)}, bf16[576,512]{1,0:T(8,128)(2,1)S(1)}, u32[]{:S(2)}, u32[]{:S(2)}) collective-permute-start(bf16[576,512]{1,0:T(8,128)(2,1)} %get-tuple-element.23), channel_id=1, source_target_pairs={{0,4},{4,0},{8,20},{12,16},{16,12},{20,8},{24,28},{28,24},{1,5},{5... | collective-permute-start | bytes 1769480 | tf_op jit(solution)/shard_map/ppermute | solution.py:569
  13.5 15.6 %collective-permute-start.2 = (bf16[576,512]{1,0:T(8,128)(2,1)}, bf16[576,512]{1,0:T(8,128)(2,1)S(1)}, u32[]{:S(2)}, u32[]{:S(2)}) collective-permute-start(bf16[576,512]{1,0:T(8,128)(2,1)} %get-tuple-element.24), channel_id=1, source_target_pairs={{0,16},{4,20},{8,0},{12,4},{16,24},{20,28},{24,8},{28,12},{1,17},{... | collective-permute-start | bytes 1769480 | tf_op jit(solution)/shard_map/ppermute | solution.py:569
  13.5 26.8 %collective-permute-start.3 = (bf16[576,512]{1,0:T(8,128)(2,1)}, bf16[576,512]{1,0:T(8,128)(2,1)S(1)}, u32[]{:S(2)}, u32[]{:S(2)}) collective-permute-start(bf16[576,512]{1,0:T(8,128)(2,1)} %get-tuple-element.25), channel_id=1, source_target_pairs={{0,20},{4,16},{8,4},{12,0},{16,28},{20,24},{24,12},{28,8},{1,21},{... | collective-permute-start | bytes 1769480 | tf_op jit(solution)/shard_map/ppermute | solution.py:569
  14.1 26.2 %collective-permute-start = (bf16[576,512]{1,0:T(8,128)(2,1)}, bf16[576,512]{1,0:T(8,128)(2,1)S(1)}, u32[]{:S(2)}, u32[]{:S(2)}) collective-permute-start(bf16[576,512]{1,0:T(8,128)(2,1)} %get-tuple-element.22.own), channel_id=1, source_target_pairs={{8,16},{12,20},{16,8},{20,12},{9,17},{13,21},{17,9},{21,13},{10,18... | collective-permute-start | bytes 1769480 | tf_op jit(solution)/shard_map/ppermute | solution.py:569
  42.0 20.1 %collective-permute-start.4 = (bf16[2,256,512]{2,1,0:T(8,128)(2,1)S(1)}, bf16[2,256,512]{2,1,0:T(8,128)(2,1)S(1)}, u32[]{:S(2)}, u32[]{:S(2)}) collective-permute-start(bf16[2,256,512]{2,1,0:T(8,128)(2,1)S(1)} %get-tuple-element.26.x_column), channel_id=1, source_target_pairs={{0,4},{4,0},{1,5},{5,1},{2,6},{6,2},{3,7},{7,3},{8,12},{12,8},{9,1... | collective-permute-start | bytes 1572872 | tf_op jit(solution)/shard_map/ppermute | solution.py:591
  43.0 19.1 %collective-permute-start.6 = (bf16[2,256,512]{2,1,0:T(8,128)(2,1)S(1)}, bf16[2,256,512]{2,1,0:T(8,128)(2,1)S(1)}, u32[]{:S(2)}, u32[]{:S(2)}) collective-permute-start(bf16[2,256,512]{2,1,0:T(8,128)(2,1)S(1)} %get-tuple-element.27.y_column), channel_id=1, source_target_pairs={{0,16},{4,20},{8,0},{12,4},{16,24},{20,28},{24,8},{28,12},{1,17},{... | collective-permute-start | bytes 1572872 | tf_op jit(solution)/shard_map/ppermute | solution.py:588
  43.0 19.1 %collective-permute-start.5 = (bf16[2,256,512]{2,1,0:T(8,128)(2,1)S(1)}, bf16[2,256,512]{2,1,0:T(8,128)(2,1)S(1)}, u32[]{:S(2)}, u32[]{:S(2)}) collective-permute-start(bf16[2,256,512]{2,1,0:T(8,128)(2,1)S(1)} %get-tuple-element.27.y_column), channel_id=1, source_target_pairs={{8,16},{12,20},{16,8},{20,12},{9,17},{13,21},{17,9},{21,13},{10,18... | collective-permute-start | bytes 1572872 | tf_op jit(solution)/shard_map/ppermute | solution.py:588
  47.1 14.4 %collective-permute-start.8 = (bf16[4,64,512]{2,1,0:T(8,128)(2,1)S(1)}, bf16[4,64,512]{2,1,0:T(8,128)(2,1)S(1)}, u32[]{:S(2)}, u32[]{:S(2)}) collective-permute-start(bf16[4,64,512]{2,1,0:T(8,128)(2,1)S(1)} %get-tuple-element.28.c0), channel_id=1, source_target_pairs={{0,2},{1,3},{2,0},{3,1},{4,6},{5,7},{6,4},{7,5},{8,10},{9,11},{10,... | collective-permute-start | bytes 786440 | tf_op jit(solution)/shard_map/ppermute | solution.py:594
  49.8 12.2 %collective-permute-start.7 = (bf16[4,64,512]{2,1,0:T(8,128)(2,1)S(1)}, bf16[4,64,512]{2,1,0:T(8,128)(2,1)S(1)}, u32[]{:S(2)}, u32[]{:S(2)}) collective-permute-start(bf16[4,64,512]{2,1,0:T(8,128)(2,1)S(1)} %get-tuple-element.28.c0), channel_id=1, source_target_pairs={{0,1},{1,0},{2,3},{3,2},{4,5},{5,4},{6,7},{7,6},{8,9},{9,8},{10,11... | collective-permute-start | bytes 786440 | tf_op jit(solution)/shard_map/ppermute | solution.py:594
  62.8 24.4 %collective-permute-start.11 = (bf16[2,2,256,512]{3,2,1,0:T(8,128)(2,1)S(1)}, bf16[2,2,256,512]{3,2,1,0:T(8,128)(2,1)S(1)}, u32[]{:S(2)}, u32[]{:S(2)}) collective-permute-start(bf16[2,2,256,512]{3,2,1,0:T(8,128)(2,1)S(1)} %get-tuple-element.30.yb), channel_id=1, source_target_pairs={{0,4},{4,0},{1,5},{5,1},{2,6},{6,2},{3,7},{7,3},{8,12},{12,8},{9,1... | collective-permute-start | bytes 3145736 | tf_op jit(solution)/shard_map/ppermute | solution.py:591
  63.2 24.1 %collective-permute-start.10 = (bf16[2,2,256,512]{3,2,1,0:T(8,128)(2,1)S(1)}, bf16[2,2,256,512]{3,2,1,0:T(8,128)(2,1)S(1)}, u32[]{:S(2)}, u32[]{:S(2)}) collective-permute-start(bf16[2,2,256,512]{3,2,1,0:T(8,128)(2,1)S(1)} %get-tuple-element.29.xb), channel_id=1, source_target_pairs={{0,16},{4,20},{8,0},{12,4},{16,24},{20,28},{24,8},{28,12},{1,17},{... | collective-permute-start | bytes 3145736 | tf_op jit(solution)/shard_map/ppermute | solution.py:588
  63.8 24.2 %collective-permute-start.9 = (bf16[2,2,256,512]{3,2,1,0:T(8,128)(2,1)S(1)}, bf16[2,2,256,512]{3,2,1,0:T(8,128)(2,1)S(1)}, u32[]{:S(2)}, u32[]{:S(2)}) collective-permute-start(bf16[2,2,256,512]{3,2,1,0:T(8,128)(2,1)S(1)} %get-tuple-element.29.xb), channel_id=1, source_target_pairs={{8,16},{12,20},{16,8},{20,12},{9,17},{13,21},{17,9},{21,13},{10,18... | collective-permute-start | bytes 3145736 | tf_op jit(solution)/shard_map/ppermute | solution.py:588
  65.8 13.9 %collective-permute-start.12 = (bf16[4,64,512]{2,1,0:T(8,128)(2,1)S(1)}, bf16[4,64,512]{2,1,0:T(8,128)(2,1)S(1)}, u32[]{:S(2)}, u32[]{:S(2)}) collective-permute-start(bf16[4,64,512]{2,1,0:T(8,128)(2,1)S(1)} %collective-permute-done.7.rows_next.c1), channel_id=1, source_target_pairs={{0,2},{1,3},{2,0},{3,1},{4,6},{5,7},{6,4},{7,5},{8,10},{9,11},{10,... | collective-permute-start | bytes 786440 | tf_op jit(solution)/shard_map/ppermute | solution.py:594
  89.0 11.1 %collective-permute-start.13 = (bf16[2,512,512]{2,1,0:T(8,128)(2,1)S(1)}, bf16[2,512,512]{2,1,0:T(8,128)(2,1)S(1)}, u32[]{:S(2)}, u32[]{:S(2)}) collective-permute-start(bf16[2,512,512]{2,1,0:T(8,128)(2,1)S(1)} %get-tuple-element.32.w_high), channel_id=1, source_target_pairs={{0,8},{16,24},{1,9},{17,25},{2,10},{18,26},{3,11},{19,27},{4,12},{... | collective-permute-start | bytes 3145736 | tf_op jit(solution)/shard_map/ppermute | solution.py:647
  111.0 3.6 %collective-permute-start.14 = (bf16[2,512,512]{2,1,0:T(8,128)(2,1)S(1)}, bf16[2,512,512]{2,1,0:T(8,128)(2,1)S(1)}, u32[]{:S(2)}, u32[]{:S(2)}) collective-permute-start(bf16[2,512,512]{2,1,0:T(8,128)(2,1)S(1)} %get-tuple-element.33), channel_id=1, source_target_pairs={{8,0},{24,16},{9,1},{25,17},{10,2},{26,18},{11,3},{27,19},{12,4},{... | collective-permute-start | bytes 3145736 | tf_op jit(solution)/shard_map/ppermute | solution.py:668
  115.6 15.3 %collective-permute-start.16 = (bf16[2,256,512]{2,1,0:T(8,128)(2,1)S(1)}, bf16[2,256,512]{2,1,0:T(8,128)(2,1)S(1)}, u32[]{:S(2)}, u32[]{:S(2)}) collective-permute-start(bf16[2,256,512]{2,1,0:T(8,128)(2,1)S(1)} %get-tuple-element.36), channel_id=1, source_target_pairs={{4,0},{0,4},{20,8},{16,12},{12,16},{8,20},{28,24},{24,28},{5,1},{1... | collective-permute-start | bytes 1572872 | tf_op jit(solution)/shard_map/ppermute | solution.py:687
  124.0 11.8 %collective-permute-start.17 = (bf16[2,256,512]{2,1,0:T(8,128)(2,1)S(1)}, bf16[2,256,512]{2,1,0:T(8,128)(2,1)S(1)}, u32[]{:S(2)}, u32[]{:S(2)}) collective-permute-start(bf16[2,256,512]{2,1,0:T(8,128)(2,1)S(1)} %get-tuple-element.37), channel_id=1, source_target_pairs={{16,0},{20,4},{0,8},{4,12},{24,16},{28,20},{8,24},{12,28},{17,1},{... | collective-permute-start | bytes 1572872 | tf_op jit(solution)/shard_map/ppermute | solution.py:687
  124.0 23.6 %collective-permute-start.18 = (bf16[2,256,512]{2,1,0:T(8,128)(2,1)S(1)}, bf16[2,256,512]{2,1,0:T(8,128)(2,1)S(1)}, u32[]{:S(2)}, u32[]{:S(2)}) collective-permute-start(bf16[2,256,512]{2,1,0:T(8,128)(2,1)S(1)} %get-tuple-element.38), channel_id=1, source_target_pairs={{20,0},{16,4},{4,8},{0,12},{28,16},{24,20},{12,24},{8,28},{21,1},{... | collective-permute-start | bytes 1572872 | tf_op jit(solution)/shard_map/ppermute | solution.py:687
  124.1 23.5 %collective-permute-start.15 = (bf16[2,256,512]{2,1,0:T(8,128)(2,1)S(1)}, bf16[2,256,512]{2,1,0:T(8,128)(2,1)S(1)}, u32[]{:S(2)}, u32[]{:S(2)}) collective-permute-start(bf16[2,256,512]{2,1,0:T(8,128)(2,1)S(1)} %get-tuple-element.35.own), channel_id=1, source_target_pairs={{16,8},{20,12},{8,16},{12,20},{17,9},{21,13},{9,17},{13,21},{18,10... | collective-permute-start | bytes 1572872 | tf_op jit(solution)/shard_map/ppermute | solution.py:687

commit v9 on v8

--- a/solution.py
+++ b/solution.py
@@ -15,7 +15,7 @@
 in_smem = pl.BlockSpec(memory_space=pltpu.SMEM)
 in_vmem = pl.BlockSpec(memory_space=pltpu.VMEM)
 
-info_member, info_piece, info_slot, info_half, info_block, info_self = 3, 4, 12, 14, 16, 20
+info_member, info_piece, info_slot, info_half, info_block, info_self = 3, 4, 12, 14, 16, 18
 
 
 def shifted(x, axis, by):
@@ -233,7 +233,8 @@
                     sems.at[index, which],
                 )
             )
-    last = pl.ds(own.shape[0] - height, height)
+    tall = rows_held.shape[1]
+    last = pl.ds(own.shape[0] - tall, tall)
     copies.append(Either(info[info_self], own.at[last], p0.at[last], rows_held.at[0], csems.at[0]))
     for index, piece in enumerate((p1, p2, p3)):
         copies.append(
@@ -243,7 +244,7 @@
     wait_all(copies)
 
 
-def both_kernel(info, x_column, x_aside, y_column, y0, y1, rows_next, rows_far, x_both, y_both, sems):
+def both_kernel(info, x_column, x_aside, y_column, y0, y1, rows_next, x_both, y_both, sems):
     copies = [
         pltpu.make_async_copy(x_column, x_both.at[0], sems.at[0]),
         pltpu.make_async_copy(x_aside, x_both.at[1], sems.at[1]),
@@ -256,7 +257,7 @@
 
 class Layers:
     def __init__(self, info, x_parts, y_parts, row_blocks, held, weights, sems, csems):
-        self.info, self.order = info, held.shape[2]
+        self.info, self.order = info, held.shape[1]
         self.x_parts, self.y_parts, self.row_blocks = x_parts, y_parts, row_blocks
         self.held, self.weights, self.sems, self.csems = held, weights, sems, csems
 
@@ -264,25 +265,16 @@
         height = self.order // 2
         return pl.ds(pl.multiple_of(self.info[info_half + far] * height, height), height)
 
-    def factor_copies(self, slot, which, parts):
+    def x_copies(self, slot, part):
         return [
             pltpu.make_async_copy(
-                part.at[plane],
-                self.held.at[
-                    slot, which, self.half_rows(far), pl.ds(plane * self.order, self.order)
-                ],
-                self.sems.at[slot, which, far, plane],
+                part.at[far, plane],
+                self.held.at[slot, self.half_rows(far), pl.ds(plane * self.order, self.order)],
+                self.sems.at[slot, far, plane],
             )
-            for far, part in enumerate(parts)
+            for far in range(2)
             for plane in range(2)
         ]
-
-    def y_copies(self, slot):
-        turn = self.info[info_slot + slot]
-        return self.factor_copies(slot, 1, [part.at[turn] for part in self.y_parts])
-
-    def start_y(self, slot):
-        start_all(self.y_copies(slot))
 
     def start_x(self, slot):
         own, first, second = self.x_parts
@@ -295,11 +287,10 @@
 
             @pl.when(hit)
             def _():
-                start_all(self.factor_copies(slot, 0, [part.at[0], part.at[1]]))
-
-    def ready(self, slot, which):
-        part = self.x_parts[0].at[0]
-        wait_all(self.factor_copies(slot, which, [part, part]))
+                start_all(self.x_copies(slot, part))
+
+    def ready_x(self, slot):
+        wait_all(self.x_copies(slot, self.x_parts[0]))
 
     def weight_copies(self, slot):
         height = self.row_blocks[0].shape[1]
@@ -342,7 +333,6 @@
                 start_all(self.rhs_copies(slot, pair, rhs, sems))
 
     def start(self, slot, own, pieces, rhs, sems):
-        self.start_y(slot)
         self.start_rhs(slot, own, pieces, rhs, sems)
         start_all(self.weight_copies(slot))
         self.start_x(slot)
@@ -354,34 +344,35 @@
     def apply(self, slot, source, below, store, fresh):
         order = self.order
         turned = (((1,), (1,)), ((), ()))
-        if 1 in fresh:
-            self.ready(slot, 1)
+        turn = self.info[info_slot + slot]
         for rows in row_chunks(order, 256):
             real, imag = source(0, rows), source(1, rows)
             upper = jnp.concatenate([real, -imag], axis=1)
             lower = jnp.concatenate([imag, real], axis=1)
-            part = lax.dot_general(
-                jnp.concatenate([upper, lower], axis=0),
-                self.held[slot, 1],
-                turned,
-                preferred_element_type=f32,
-            ).astype(bf16)
+            both = jnp.concatenate([upper, lower], axis=0)
             height = rows.stop - rows.start
-            real, imag = part[:height], part[height:]
             further = slice(rows.start + order, rows.stop + order)
-            below[rows, :order] = real
-            below[rows, order:] = imag
-            below[further, :order] = -imag
-            below[further, order:] = real
-        if 0 in fresh:
-            self.ready(slot, 0)
+            for far, part in enumerate(self.y_parts):
+                right = jnp.concatenate([part[turn, 0], part[turn, 1]], axis=1)
+                product = lax.dot_general(
+                    both, right, turned, preferred_element_type=f32
+                ).astype(bf16)
+                start = self.info[info_half + far] * (order // 2)
+                columns = pl.ds(pl.multiple_of(start, order // 2), order // 2)
+                beyond = pl.ds(pl.multiple_of(order + start, order // 2), order // 2)
+                below[rows, columns] = product[:height]
+                below[rows, beyond] = product[height:]
+                below[further, columns] = -product[height:]
+                below[further, beyond] = product[:height]
+        if fresh:
+            self.ready_x(slot)
         for plane in range(2):
             for columns in row_chunks(order, 256):
                 along = slice(columns.start + plane * order, columns.stop + plane * order)
                 store(
                     plane,
                     columns,
-                    jnp.dot(self.held[slot, 0], below[:, along], preferred_element_type=f32),
+                    jnp.dot(self.held[slot], below[:, along], preferred_element_type=f32),
                 )
 
 
@@ -423,47 +414,45 @@
     return store
 
 
-def first_kernel(info, xb, x0, x1, yb, yf, c0, c1, c2, c3, own, p0, p1, p2, p3, w_low, w_high,
+def first_kernel(info, xb, x0, x1, yb, yf, c0, c1, own, p0, p1, p2, p3, w_low, w_high,
                  held, weights, rhs, below, sems, csems, fsems):
     @pl.when(info[info_member] == 0)
     def _():
-        layers = Layers(info, (xb, x0, x1), (yb, yf), (c0, c1, c2, c3), held, weights, fsems, csems)
+        layers = Layers(info, (xb, x0, x1), (yb, yf), (c0, c1), held, weights, fsems, csems)
         fields = (own, (p0, p1, p2, p3), rhs, sems)
         layers.start(0, *fields)
         layers.wait(0, *fields)
-        layers.ready(0, 1)
         layers.start(1, *fields)
         zero = reduced(rhs, info, 0, weights, lambda plane, rows: f32(0.0))
-        layers.apply(0, zero, below, round_into(w_low), (0,))
+        layers.apply(0, zero, below, round_into(w_low), True)
         layers.wait(1, *fields)
         one = reduced(rhs, info, 1, weights, lambda plane, rows: w_low[plane, rows].astype(f32))
-        layers.apply(1, one, below, round_into(w_high), (0, 1))
-
-
-def last_kernel(info, xb, x0, x1, yb, yf, c0, c1, c2, c3, own, p0, p1, p2, p3, arrived, field, back,
+        layers.apply(1, one, below, round_into(w_high), True)
+
+
+def last_kernel(info, xb, x0, x1, yb, yf, c0, c1, own, p0, p1, p2, p3, arrived, field, back,
                 held, weights, rhs, forward, below, sems, csems, fsems):
     @pl.when(info[info_member] == 1)
     def _():
-        layers = Layers(info, (xb, x0, x1), (yb, yf), (c0, c1, c2, c3), held, weights, fsems, csems)
+        layers = Layers(info, (xb, x0, x1), (yb, yf), (c0, c1), held, weights, fsems, csems)
         fields = (own, (p0, p1, p2, p3), rhs, sems)
         layers.start(0, *fields)
         layers.wait(0, *fields)
-        layers.ready(0, 1)
         layers.start(1, *fields)
         low, high = field.at[0], field.at[1]
         two = reduced(rhs, info, 0, weights, lambda plane, rows: arrived[plane, rows].astype(f32))
-        layers.apply(0, two, below, round_into(forward), (0,))
+        layers.apply(0, two, below, round_into(forward), True)
         layers.wait(1, *fields)
         three = reduced(rhs, info, 1, weights, lambda plane, rows: forward[plane, rows].astype(f32))
-        layers.apply(1, three, below, round_into(high), (0, 1))
-        layers.apply(0, sent(weights, 1, high), below, subtract_into(low, forward), ())
+        layers.apply(1, three, below, round_into(high), True)
+        layers.apply(0, sent(weights, 1, high), below, subtract_into(low, forward), False)
         last = sent(weights, 0, low)
         for plane in range(2):
             for rows in row_chunks(weights.shape[1], 256):
                 back[plane, rows] = last(plane, rows)
 
 
-def back_kernel(info, xb, x0, x1, yb, yf, c0, c1, c2, c3, w_low, w_high, arrived, field,
+def back_kernel(info, xb, x0, x1, yb, yf, c0, c1, w_low, w_high, arrived, field,
                 p0, p1, p2, p3, held, weights, kept, below, csems, fsems, osems):
     def start_pieces(source, slot):
         for index, piece in enumerate((p0, p1, p2, p3)):
@@ -477,21 +466,18 @@
 
     @pl.when(info[info_member] == 0)
     def _():
-        layers = Layers(info, (xb, x0, x1), (yb, yf), (c0, c1, c2, c3), held, weights, fsems, csems)
-        layers.start_y(1)
+        layers = Layers(info, (xb, x0, x1), (yb, yf), (c0, c1), held, weights, fsems, csems)
         layers.start_x(1)
-        layers.ready(1, 1)
         high_rows = layers.weight_copies(1)
         start_all(high_rows)
-        layers.start_y(0)
         layers.start_x(0)
         low, high = kept.at[0], kept.at[1]
         layers.apply(
-            1, lambda plane, rows: arrived[plane, rows], below, subtract_into(high, w_high), (0,)
+            1, lambda plane, rows: arrived[plane, rows], below, subtract_into(high, w_high), True
         )
         start_pieces(kept, 1)
         wait_all(high_rows)
-        layers.apply(0, sent(weights, 1, high), below, subtract_into(low, w_low), (0, 1))
+        layers.apply(0, sent(weights, 1, high), below, subtract_into(low, w_low), True)
         start_pieces(kept, 0)
 
     @pl.when(info[info_member] != 0)
@@ -542,21 +528,19 @@
     for a, b in rounds:
         entries += [(group + a) % 2, (own_x - b) % px_count]
     entries += [group, (group + 1) % 2, own_x, (own_x + 1) % 2]
-    pair = own_y // 2 * 2
-    entries += [own_y, pair + (own_y + 1) % 2, (own_y + 2) % 4, (pair + 2) % 4 + (own_y + 1) % 2]
-    entries += [group == member]
+    entries += [own_y % 2, (own_y + 1) % 2, group == member]
     info = jnp.stack([jnp.asarray(entry, jnp.int32) for entry in entries])
 
     sends_to = jnp.stack(
         [((member + a) % 2) * px_count + (own_x + b) % px_count for a, b in rounds]
-        + [own_y, group == member]
+        + [own_y % 2, group == member]
     ).astype(jnp.int32)
     piece_shape = jax.ShapeDtypeStruct((2, rows_here, order), bf16)
     shard = jnp.concatenate([x_factor[0], y_factor[0]], axis=0)
     blocks = jnp.broadcast_to(shard[None], (py_count,) + shard.shape)
     packed = pl.pallas_call(
         pack_kernel,
-        out_shape=[jax.ShapeDtypeStruct((2 * rows_here + height, order), bf16)] * len(rounds),
+        out_shape=[jax.ShapeDtypeStruct((2 * rows_here + rows_here // 2, order), bf16)] * len(rounds),
         in_specs=[in_smem] + [anywhere] * 2,
         out_specs=[in_vmem] * len(rounds),
         scratch_shapes=[
@@ -571,7 +555,7 @@
     blocks = lax.all_to_all(blocks, "py", split_axis=0, concat_axis=0, tiled=True)
 
     column_shape = jax.ShapeDtypeStruct((2, rows_here, order), bf16)
-    rows_shape = jax.ShapeDtypeStruct((len(rounds), height, order), bf16)
+    rows_shape = jax.ShapeDtypeStruct((len(rounds), rows_here // 2, order), bf16)
     x_column, y_column, rows_held = pl.pallas_call(
         column_kernel,
         out_shape=[column_shape, column_shape, rows_shape],
@@ -596,27 +580,27 @@
     y_near = [across(y_column, a) for a in range(2)]
     x_aside = aside(x_column)
     rows_next = over_z(rows_held, 1)
-    rows_far = over_z(rows_held, 2)
     x_both, y_both = pl.pallas_call(
         both_kernel,
         out_shape=[jax.ShapeDtypeStruct((2,) + column_shape.shape, bf16)] * 2,
-        in_specs=[in_smem] + [anywhere] * 7,
+        in_specs=[in_smem] + [anywhere] * 6,
         out_specs=[in_vmem] * 2,
         scratch_shapes=[pltpu.SemaphoreType.DMA((4,))],
         compiler_params=params,
-    )(info, x_column, x_aside, y_column, *y_near, rows_next, rows_far)
+    )(info, x_column, x_aside, y_column, *y_near, rows_next)
     y_far = aside(y_both)
     x_across = [across(x_both, a) for a in range(2)]
-    factors = [x_both, *x_across, y_both, y_far, rows_held, rows_next, rows_far, over_z(rows_next, 2)]
+    factors = [x_both, *x_across, y_both, y_far, rows_held, rows_next]
 
     full_shape = jax.ShapeDtypeStruct((2, order, order), bf16)
-    factor_scratch = pltpu.VMEM((2, 2, order, 2 * order), bf16)
+    factor_scratch = pltpu.VMEM((2, order, 2 * order), bf16)
     weight_scratch = pltpu.VMEM((2, order, order), bf16)
     field_scratch = pltpu.VMEM((2, 2, order, order), bf16)
     below_scratch = pltpu.VMEM((2 * order, 2 * order), bf16)
-    factor_sems = pltpu.SemaphoreType.DMA((2, 2, 2, 2))
-    weight_sems = pltpu.SemaphoreType.DMA((2, py_count, 2))
+    factor_sems = pltpu.SemaphoreType.DMA((2, 2, 2))
+    weight_sems = pltpu.SemaphoreType.DMA((2, 2, 2))
     field_sems = pltpu.SemaphoreType.DMA((2, 2, 2))
+    solver_specs = [in_smem] + [anywhere] * 3 + [in_vmem] * 2 + [anywhere] * 2
     solve_flops = 16 * order**3
     fields = (packed[0], *pieces)
 
@@ -628,7 +612,7 @@
     w_low, w_high = pl.pallas_call(
         first_kernel,
         out_shape=[full_shape] * 2,
-        in_specs=[in_smem] + [anywhere] * 14,
+        in_specs=solver_specs + [anywhere] * 5,
         out_specs=[in_vmem] * 2,
         scratch_shapes=[
             factor_scratch,
@@ -648,7 +632,7 @@
     solved, back = pl.pallas_call(
         last_kernel,
         out_shape=[jax.ShapeDtypeStruct((2, 2, order, order), bf16), full_shape],
-        in_specs=[in_smem] + [anywhere] * 14 + [in_vmem],
+        in_specs=solver_specs + [anywhere] * 5 + [in_vmem],
         out_specs=[in_vmem] * 2,
         scratch_shapes=[
             factor_scratch,
@@ -669,7 +653,7 @@
     results = pl.pallas_call(
         back_kernel,
         out_shape=[piece_shape] * len(rounds),
-        in_specs=[in_smem] + [anywhere] * 9 + [in_vmem] * 3 + [anywhere],
+        in_specs=solver_specs + [in_vmem] * 3 + [anywhere],
         out_specs=[anywhere] * len(rounds),
         scratch_shapes=[
             factor_scratch,

time: 150 us -> 153 us (1.020)
  waiting for transfers between devices: 83.2 us -> 88.5 us
  starting transfers between devices: 40.6 us -> 37.1 us
    ppermute x2, waiting for transfers between devices: 7.6 us -> 28.9 us  [aside(): return lax.ppermute(block, 'px', [(y, (y + 1) % 2) for y in range(2)])]
    ppermute x3 -> x1, waiting for transfers between devices: 23.7 us -> 2.94 us  [over_z(): return lax.ppermute(block, 'py', [(z, z ^ bit) for z in range(py_count)])]
    ppermute x3 -> x1, starting transfers between devices: 5.07 us -> 1.79 us  [over_z(): return lax.ppermute(block, 'py', [(z, z ^ bit) for z in range(py_count)])]
    ppermute x4, waiting for transfers between devices: 19.4 us -> 22.5 us  [on_device(): lax.ppermute(piece, ('sec', 'px'), pairs(a, b))]
  transfers between devices with their start and end apart: 20 -> 18, of which waited for: 13 -> 13; matrix products, arithmetic and copies ran while one was open for 1% -> 1% of each run, Pallas kernels for 2% -> 2%
where the time goes in v9:
time: 153 us; the launch traced here: 152 us
  waiting for transfers between devices  88.5 us (58%)
  starting transfers between devices  37.1 us (24%)
  Pallas kernels  21.1 us (14%)
  between operations  2.79 us (2%)
  local copies, waits for them, and re-layouts  1.86 us (1%)
    ppermute x2, waiting for transfers between devices, aside(): return lax.ppermute(block, 'px', [(y, (y + 1) % 2) for y in range(2)])  28.9 us
    ppermute x4, waiting for transfers between devices, on_device(): lax.ppermute(piece, ('sec', 'px'), pairs(a, b))  22.5 us
    ppermute x4, waiting for transfers between devices, on_device(): lax.ppermute(piece, ('sec', 'px'), back_pairs(a, b))  19.6 us
    ppermute x4, starting transfers between devices, on_device(): lax.ppermute(piece, ('sec', 'px'), back_pairs(a, b))  12.3 us
    pallas_call x1, Pallas kernels, on_device(): pl.pallas_call(last_kernel, out_shape=[jax.ShapeDtypeStruct((2, 2, order,...  11.5 us
    ppermute x1, waiting for transfers between devices, on_device(): incoming = lax.ppermute(w_high, 'sec', up)  9.96 us
    ppermute x4, starting transfers between devices, on_device(): lax.ppermute(piece, ('sec', 'px'), pairs(a, b))  6.94 us
    ppermute x4, starting transfers between devices, across(): return lax.ppermute(block, ('sec', 'px'), pairs(a, 0))  6.46 us
  transfers between devices with their start and end apart: 18, of which 13 were waited for; matrix products, arithmetic and copies ran while one was open for 1% of the time, Pallas kernels for 2%

profile of v9, /device:TPU:1, one launch (start us, length us, event | category | flops | bytes accessed | tf_op | source)
XLA Modules:
  0.0 152.4 jit_solution(17233701001629803466)
XLA Ops:
  0.0 1.1 pad_maximum_fusion
  1.1 1.1 broadcast_in_dim.4
  2.2 5.6 %all-to-all-start = ((bf16[4,4,64,512]{3,2,1,0:T(8,128)(2,1)}), bf16[4,4,64,512]{3,2,1,0:T(8,128)(2,1)S(1)}, u32[]{:S(2)}, u32[]{:S(2)}) async-start(bf16[4,4,64,512]{3,2,1,0:T(8,128)(2,1)} %broadcast_in_dim.4), calls=%async_computation | async-start | bytes 2097152 | tf_op jit(solution)/shard_map/all_to_all | solution.py:555
  7.9 3.0 %shard_map.55 = (bf16[640,512]{1,0:T(8,128)(2,1)}, bf16[640,512]{1,0:T(8,128)(2,1)}, bf16[640,512]{1,0:T(8,128)(2,1)}, bf16[640,512]{1,0:T(8,128)(2,1)}) custom-call(s32[6]{0:T(128)S(1)} %stack.77.place, bf16[2,256,2048]{2,1,0:T(8,128)(2,1)S(1)} %bitcast.26, bf16[256,512]{1,0:T(8,128)(2,1)S(1)} %bitcast.27), custom_call_target="tpu_custom_call" | custom-call | tf_op jit(solution)/shard_map/pallas_call | solution.py:541
  10.9 3.1 %collective-permute-start.1 = (bf16[640,512]{1,0:T(8,128)(2,1)}, bf16[640,512]{1,0:T(8,128)(2,1)S(1)}, u32[]{:S(2)}, u32[]{:S(2)}) collective-permute-start(bf16[640,512]{1,0:T(8,128)(2,1)} %get-tuple-element.23), channel_id=1, source_target_pairs={{0,4},{4,0},{8,20},{12,16},{16,12},{20,8},{24,28},{28,24},{1,5},{5... | collective-permute-start | bytes 1966088 | tf_op jit(solution)/shard_map/ppermute | solution.py:553
  14.5 3.3 %collective-permute-start = (bf16[640,512]{1,0:T(8,128)(2,1)}, bf16[640,512]{1,0:T(8,128)(2,1)}, u32[]{:S(2)}, u32[]{:S(2)}) collective-permute-start(bf16[640,512]{1,0:T(8,128)(2,1)} %get-tuple-element.22.own), channel_id=1, source_target_pairs={{8,16},{12,20},{16,8},{20,12},{9,17},{13,21},{17,9},{21,13},{10,18... | collective-permute-start | bytes 1966088 | tf_op jit(solution)/shard_map/ppermute | solution.py:553
  21.0 7.5 %collective-permute-done.1.p1 = bf16[640,512]{1,0:T(8,128)(2,1)S(1)} collective-permute-done((bf16[640,512]{1,0:T(8,128)(2,1)}, bf16[640,512]{1,0:T(8,128)(2,1)S(1)}, u32[]{:S(2)}, u32[]{:S(2)}) %collective-permute-start.1) | collective-permute-done | bytes 655392 | tf_op jit(solution)/shard_map/ppermute | solution.py:553
  28.5 2.4 %collective-permute-done.2.p2 = bf16[640,512]{1,0:T(8,128)(2,1)S(1)} collective-permute-done((bf16[640,512]{1,0:T(8,128)(2,1)}, bf16[640,512]{1,0:T(8,128)(2,1)S(1)}, u32[]{:S(2)}, u32[]{:S(2)}) %collective-permute-start.2) | collective-permute-done | bytes 655392 | tf_op jit(solution)/shard_map/ppermute | solution.py:553
  31.0 12.6 %collective-permute-done.3.p3 = bf16[640,512]{1,0:T(8,128)(2,1)S(1)} collective-permute-done((bf16[640,512]{1,0:T(8,128)(2,1)}, bf16[640,512]{1,0:T(8,128)(2,1)S(1)}, u32[]{:S(2)}, u32[]{:S(2)}) %collective-permute-start.3) | collective-permute-done | bytes 655392 | tf_op jit(solution)/shard_map/ppermute | solution.py:553
  43.5 2.2 %shard_map.56 = (bf16[2,256,512]{2,1,0:T(8,128)(2,1)S(1)}, bf16[2,256,512]{2,1,0:T(8,128)(2,1)S(1)}, bf16[4,128,512]{2,1,0:T(8,128)(2,1)S(1)}) custom-call(s32[19]{0:T(128)S(1)} %stack.90.info, bf16[4,4,64,512]{3,2,1,0:T(8,128)(2,1)S(1)} %all-to-all-done.blocks, bf16[640,512]{1,0:T(8,128)(2,1)} %get-tuple-element.22.own, ...), custom_call_target="tpu_custom_call" | custom-call | tf_op jit(solution)/shard_map/pallas_call | solution.py:559
  45.8 0.9 collective-permute-start.4
  46.7 4.2 %collective-permute-start.5 = (bf16[2,256,512]{2,1,0:T(8,128)(2,1)S(1)}, bf16[2,256,512]{2,1,0:T(8,128)(2,1)S(1)}, u32[]{:S(2)}, u32[]{:S(2)}) collective-permute-start(bf16[2,256,512]{2,1,0:T(8,128)(2,1)S(1)} %get-tuple-element.27.y_column), channel_id=1, source_target_pairs={{8,16},{12,20},{16,8},{20,12},{9,17},{13,21},{17,9},{21,13},{10,18... | collective-permute-start | bytes 1572872 | tf_op jit(solution)/shard_map/ppermute | solution.py:572
  50.9 1.8 %collective-permute-start.7 = (bf16[4,128,512]{2,1,0:T(8,128)(2,1)S(1)}, bf16[4,128,512]{2,1,0:T(8,128)(2,1)S(1)}, u32[]{:S(2)}, u32[]{:S(2)}) collective-permute-start(bf16[4,128,512]{2,1,0:T(8,128)(2,1)S(1)} %get-tuple-element.28.c0), channel_id=1, source_target_pairs={{0,1},{1,0},{2,3},{3,2},{4,5},{5,4},{6,7},{7,6},{8,9},{9,8},{10,11... | collective-permute-start | bytes 1572872 | tf_op jit(solution)/shard_map/ppermute | solution.py:578
  52.7 6.9 %collective-permute-done.4.x_aside = bf16[2,256,512]{2,1,0:T(8,128)(2,1)S(1)} collective-permute-done((bf16[2,256,512]{2,1,0:T(8,128)(2,1)S(1)}, bf16[2,256,512]{2,1,0:T(8,128)(2,1)S(1)}, u32[]{:S(2)}, u32[]{:S(2)}) %collective-permute-start.4) | collective-permute-done | bytes 524320 | tf_op jit(solution)/shard_map/ppermute | solution.py:575
  59.6 1.7 %collective-permute-done.5.y0 = bf16[2,256,512]{2,1,0:T(8,128)(2,1)S(1)} collective-permute-done((bf16[2,256,512]{2,1,0:T(8,128)(2,1)S(1)}, bf16[2,256,512]{2,1,0:T(8,128)(2,1)S(1)}, u32[]{:S(2)}, u32[]{:S(2)}) %collective-permute-start.5) | collective-permute-done | bytes 524320 | tf_op jit(solution)/shard_map/ppermute | solution.py:572
  61.3 2.9 %collective-permute-done.7.rows_next.c1 = bf16[4,128,512]{2,1,0:T(8,128)(2,1)S(1)} collective-permute-done((bf16[4,128,512]{2,1,0:T(8,128)(2,1)S(1)}, bf16[4,128,512]{2,1,0:T(8,128)(2,1)S(1)}, u32[]{:S(2)}, u32[]{:S(2)}) %collective-permute-start.7) | collective-permute-done | bytes 524320 | tf_op jit(solution)/shard_map/ppermute | solution.py:578
  64.3 0.7 shard_map.57
  65.8 1.9 %collective-permute-start.8 = (bf16[2,2,256,512]{3,2,1,0:T(8,128)(2,1)S(1)}, bf16[2,2,256,512]{3,2,1,0:T(8,128)(2,1)S(1)}, u32[]{:S(2)}, u32[]{:S(2)}) collective-permute-start(bf16[2,2,256,512]{3,2,1,0:T(8,128)(2,1)S(1)} %get-tuple-element.29.xb), channel_id=1, source_target_pairs={{8,16},{12,20},{16,8},{20,12},{9,17},{13,21},{17,9},{21,13},{10,18... | collective-permute-start | bytes 3145736 | tf_op jit(solution)/shard_map/ppermute | solution.py:572
  67.8 22.0 %collective-permute-done.10.yf = bf16[2,2,256,512]{3,2,1,0:T(8,128)(2,1)S(1)} collective-permute-done((bf16[2,2,256,512]{3,2,1,0:T(8,128)(2,1)S(1)}, bf16[2,2,256,512]{3,2,1,0:T(8,128)(2,1)S(1)}, u32[]{:S(2)}, u32[]{:S(2)}) %collective-permute-start.10) | collective-permute-done | bytes 1048608 | tf_op jit(solution)/shard_map/ppermute | solution.py:575
  90.4 0.8 shard_map.58
  91.1 1.3 collective-permute-start.11
  92.4 10.0 %collective-permute-done.11.arrived = bf16[2,512,512]{2,1,0:T(8,128)(2,1)S(1)} collective-permute-done((bf16[2,512,512]{2,1,0:T(8,128)(2,1)S(1)}, bf16[2,512,512]{2,1,0:T(8,128)(2,1)S(1)}, u32[]{:S(2)}, u32[]{:S(2)}) %collective-permute-start.11) | collective-permute-done | bytes 1048608 | tf_op jit(solution)/shard_map/ppermute | solution.py:631
  102.4 11.5 %shard_map.59 = (bf16[2,2,512,512]{3,2,1,0:T(8,128)(2,1)S(1)}, bf16[2,512,512]{2,1,0:T(8,128)(2,1)S(1)}) custom-call(s32[19]{0:T(128)S(1)} %stack.90.info, bf16[2,2,256,512]{3,2,1,0:T(8,128)(2,1)S(1)} %get-tuple-element.29.xb, bf16[2,2,256,512]{3,2,1,0:T(8,128)(2,1)S(1)} %collective-permute-done.8.x0, ...), custom_call_target="tpu_custom_call" | custom-call | flops 6442450944 | bytes 8388608 | tf_op jit(solution)/shard_map/pallas_call | solution.py:632
  113.9 1.4 collective-permute-start.12
  115.3 2.2 %collective-permute-done.12.arrived = bf16[2,512,512]{2,1,0:T(8,128)(2,1)S(1)} collective-permute-done((bf16[2,512,512]{2,1,0:T(8,128)(2,1)S(1)}, bf16[2,512,512]{2,1,0:T(8,128)(2,1)S(1)}, u32[]{:S(2)}, u32[]{:S(2)}) %collective-permute-start.12) | collective-permute-done | bytes 1048608 | tf_op jit(solution)/shard_map/ppermute | solution.py:652
  117.5 0.9 shard_map.60
  118.4 8.2 %collective-permute-start.14 = (bf16[2,256,512]{2,1,0:T(8,128)(2,1)S(1)}, bf16[2,256,512]{2,1,0:T(8,128)(2,1)S(1)}, u32[]{:S(2)}, u32[]{:S(2)}) collective-permute-start(bf16[2,256,512]{2,1,0:T(8,128)(2,1)S(1)} %get-tuple-element.36), channel_id=1, source_target_pairs={{4,0},{0,4},{20,8},{16,12},{12,16},{8,20},{28,24},{24,28},{5,1},{1... | collective-permute-start | bytes 1572872 | tf_op jit(solution)/shard_map/ppermute | solution.py:671
  126.8 4.0 %collective-permute-start.13 = (bf16[2,256,512]{2,1,0:T(8,128)(2,1)S(1)}, bf16[2,256,512]{2,1,0:T(8,128)(2,1)S(1)}, u32[]{:S(2)}, u32[]{:S(2)}) collective-permute-start(bf16[2,256,512]{2,1,0:T(8,128)(2,1)S(1)} %get-tuple-element.35.own), channel_id=1, source_target_pairs={{16,8},{20,12},{8,16},{12,20},{17,9},{21,13},{9,17},{13,21},{18,10... | collective-permute-start | bytes 1572872 | tf_op jit(solution)/shard_map/ppermute | solution.py:671
  130.7 2.9 %collective-permute-done.14.rest_1_ = bf16[2,256,512]{2,1,0:T(8,128)(2,1)S(1)} collective-permute-done((bf16[2,256,512]{2,1,0:T(8,128)(2,1)S(1)}, bf16[2,256,512]{2,1,0:T(8,128)(2,1)S(1)}, u32[]{:S(2)}, u32[]{:S(2)}) %collective-permute-start.14) | collective-permute-done | bytes 524320 | tf_op jit(solution)/shard_map/ppermute | solution.py:671
  133.6 4.8 %collective-permute-done.15.rest_2_ = bf16[2,256,512]{2,1,0:T(8,128)(2,1)S(1)} collective-permute-done((bf16[2,256,512]{2,1,0:T(8,128)(2,1)S(1)}, bf16[2,256,512]{2,1,0:T(8,128)(2,1)S(1)}, u32[]{:S(2)}, u32[]{:S(2)}) %collective-permute-start.15) | collective-permute-done | bytes 524320 | tf_op jit(solution)/shard_map/ppermute | solution.py:671
  138.4 11.9 %collective-permute-done.16.rest_3_ = bf16[2,256,512]{2,1,0:T(8,128)(2,1)S(1)} collective-permute-done((bf16[2,256,512]{2,1,0:T(8,128)(2,1)S(1)}, bf16[2,256,512]{2,1,0:T(8,128)(2,1)S(1)}, u32[]{:S(2)}, u32[]{:S(2)}) %collective-permute-start.16) | collective-permute-done | bytes 524320 | tf_op jit(solution)/shard_map/ppermute | solution.py:671
  150.3 1.9 %shard_map.61 = bf16[2,256,2048]{2,1,0:T(8,128)(2,1)} custom-call(s32[6]{0:T(128)S(1)} %stack.77.place, bf16[2,256,512]{2,1,0:T(8,128)(2,1)S(1)} %get-tuple-element.35.own, bf16[2,256,512]{2,1,0:T(8,128)(2,1)S(1)} %collective-permute-done.13.rest_0_, bf16[2,256,512]{2,1,0:T(8,128)(2,1)S(1)} %collective-permute-done.14.rest_1_, ...), custom_call_target="tpu_custom_call" | custom-call | tf_op jit(solution)/shard_map/pallas_call | solution.py:673
  (22 shorter events, 3.0 us)
Async XLA Ops:
  0.0 7.9 %copy-start.1 = (bf16[1,256,512]{2,1,0:T(8,128)(2,1)S(1)}, bf16[1,256,512]{2,1,0:T(8,128)(2,1)}, u32[]{:S(2)}) copy-start(bf16[1,256,512]{2,1,0:T(8,128)(2,1)} %param.7) | copy-start | bytes 786436
  0.0 7.9 %copy-start = (bf16[2,1,256,2048]{3,2,1,0:T(8,128)(2,1)S(1)}, bf16[2,1,256,2048]{3,2,1,0:T(8,128)(2,1)}, u32[]{:S(2)}) copy-start(bf16[2,1,256,2048]{3,2,1,0:T(8,128)(2,1)} %param.5) | copy-start | bytes 6291460
  2.2 15.7 %copy-start.2 = (s32[16]{0:T(128)S(1)}, s32[16]{0:T(128)}, u32[]{:S(2)}) copy-start(s32[16]{0:T(128)} %param.6) | copy-start | bytes 196
  2.2 41.3 %all-to-all-start = ((bf16[4,4,64,512]{3,2,1,0:T(8,128)(2,1)}), bf16[4,4,64,512]{3,2,1,0:T(8,128)(2,1)S(1)}, u32[]{:S(2)}, u32[]{:S(2)}) async-start(bf16[4,4,64,512]{3,2,1,0:T(8,128)(2,1)} %broadcast_in_dim.4), calls=%async_computation | async-start | bytes 2097152 | tf_op jit(solution)/shard_map/all_to_all | solution.py:555
  10.9 17.7 %collective-permute-start.1 = (bf16[640,512]{1,0:T(8,128)(2,1)}, bf16[640,512]{1,0:T(8,128)(2,1)S(1)}, u32[]{:S(2)}, u32[]{:S(2)}) collective-permute-start(bf16[640,512]{1,0:T(8,128)(2,1)} %get-tuple-element.23), channel_id=1, source_target_pairs={{0,4},{4,0},{8,20},{12,16},{16,12},{20,8},{24,28},{28,24},{1,5},{5... | collective-permute-start | bytes 1966088 | tf_op jit(solution)/shard_map/ppermute | solution.py:553
  13.9 17.0 %collective-permute-start.2 = (bf16[640,512]{1,0:T(8,128)(2,1)}, bf16[640,512]{1,0:T(8,128)(2,1)S(1)}, u32[]{:S(2)}, u32[]{:S(2)}) collective-permute-start(bf16[640,512]{1,0:T(8,128)(2,1)} %get-tuple-element.24), channel_id=1, source_target_pairs={{0,16},{4,20},{8,0},{12,4},{16,24},{20,28},{24,8},{28,12},{1,17},{... | collective-permute-start | bytes 1966088 | tf_op jit(solution)/shard_map/ppermute | solution.py:553
  13.9 29.6 %collective-permute-start.3 = (bf16[640,512]{1,0:T(8,128)(2,1)}, bf16[640,512]{1,0:T(8,128)(2,1)S(1)}, u32[]{:S(2)}, u32[]{:S(2)}) collective-permute-start(bf16[640,512]{1,0:T(8,128)(2,1)} %get-tuple-element.25), channel_id=1, source_target_pairs={{0,20},{4,16},{8,4},{12,0},{16,28},{20,24},{24,12},{28,8},{1,21},{... | collective-permute-start | bytes 1966088 | tf_op jit(solution)/shard_map/ppermute | solution.py:553
  14.5 29.0 %collective-permute-start = (bf16[640,512]{1,0:T(8,128)(2,1)}, bf16[640,512]{1,0:T(8,128)(2,1)}, u32[]{:S(2)}, u32[]{:S(2)}) collective-permute-start(bf16[640,512]{1,0:T(8,128)(2,1)} %get-tuple-element.22.own), channel_id=1, source_target_pairs={{8,16},{12,20},{16,8},{20,12},{9,17},{13,21},{17,9},{21,13},{10,18... | collective-permute-start | bytes 1966088 | tf_op jit(solution)/shard_map/ppermute | solution.py:553
  45.8 13.8 %collective-permute-start.4 = (bf16[2,256,512]{2,1,0:T(8,128)(2,1)S(1)}, bf16[2,256,512]{2,1,0:T(8,128)(2,1)S(1)}, u32[]{:S(2)}, u32[]{:S(2)}) collective-permute-start(bf16[2,256,512]{2,1,0:T(8,128)(2,1)S(1)} %get-tuple-element.26.x_column), channel_id=1, source_target_pairs={{0,4},{4,0},{1,5},{5,1},{2,6},{6,2},{3,7},{7,3},{8,12},{12,8},{9,1... | collective-permute-start | bytes 1572872 | tf_op jit(solution)/shard_map/ppermute | solution.py:575
  46.7 12.9 %collective-permute-start.6 = (bf16[2,256,512]{2,1,0:T(8,128)(2,1)S(1)}, bf16[2,256,512]{2,1,0:T(8,128)(2,1)S(1)}, u32[]{:S(2)}, u32[]{:S(2)}) collective-permute-start(bf16[2,256,512]{2,1,0:T(8,128)(2,1)S(1)} %get-tuple-element.27.y_column), channel_id=1, source_target_pairs={{0,16},{4,20},{8,0},{12,4},{16,24},{20,28},{24,8},{28,12},{1,17},{... | collective-permute-start | bytes 1572872 | tf_op jit(solution)/shard_map/ppermute | solution.py:572
  46.7 14.6 %collective-permute-start.5 = (bf16[2,256,512]{2,1,0:T(8,128)(2,1)S(1)}, bf16[2,256,512]{2,1,0:T(8,128)(2,1)S(1)}, u32[]{:S(2)}, u32[]{:S(2)}) collective-permute-start(bf16[2,256,512]{2,1,0:T(8,128)(2,1)S(1)} %get-tuple-element.27.y_column), channel_id=1, source_target_pairs={{8,16},{12,20},{16,8},{20,12},{9,17},{13,21},{17,9},{21,13},{10,18... | collective-permute-start | bytes 1572872 | tf_op jit(solution)/shard_map/ppermute | solution.py:572
  50.9 13.4 %collective-permute-start.7 = (bf16[4,128,512]{2,1,0:T(8,128)(2,1)S(1)}, bf16[4,128,512]{2,1,0:T(8,128)(2,1)S(1)}, u32[]{:S(2)}, u32[]{:S(2)}) collective-permute-start(bf16[4,128,512]{2,1,0:T(8,128)(2,1)S(1)} %get-tuple-element.28.c0), channel_id=1, source_target_pairs={{0,1},{1,0},{2,3},{3,2},{4,5},{5,4},{6,7},{7,6},{8,9},{9,8},{10,11... | collective-permute-start | bytes 1572872 | tf_op jit(solution)/shard_map/ppermute | solution.py:578
  65.0 24.7 %collective-permute-start.10 = (bf16[2,2,256,512]{3,2,1,0:T(8,128)(2,1)S(1)}, bf16[2,2,256,512]{3,2,1,0:T(8,128)(2,1)S(1)}, u32[]{:S(2)}, u32[]{:S(2)}) collective-permute-start(bf16[2,2,256,512]{3,2,1,0:T(8,128)(2,1)S(1)} %get-tuple-element.30.yb), channel_id=1, source_target_pairs={{0,4},{4,0},{1,5},{5,1},{2,6},{6,2},{3,7},{7,3},{8,12},{12,8},{9,1... | collective-permute-start | bytes 3145736 | tf_op jit(solution)/shard_map/ppermute | solution.py:575
  65.5 24.2 %collective-permute-start.9 = (bf16[2,2,256,512]{3,2,1,0:T(8,128)(2,1)S(1)}, bf16[2,2,256,512]{3,2,1,0:T(8,128)(2,1)S(1)}, u32[]{:S(2)}, u32[]{:S(2)}) collective-permute-start(bf16[2,2,256,512]{3,2,1,0:T(8,128)(2,1)S(1)} %get-tuple-element.29.xb), channel_id=1, source_target_pairs={{0,16},{4,20},{8,0},{12,4},{16,24},{20,28},{24,8},{28,12},{1,17},{... | collective-permute-start | bytes 3145736 | tf_op jit(solution)/shard_map/ppermute | solution.py:572
  65.8 24.5 %collective-permute-start.8 = (bf16[2,2,256,512]{3,2,1,0:T(8,128)(2,1)S(1)}, bf16[2,2,256,512]{3,2,1,0:T(8,128)(2,1)S(1)}, u32[]{:S(2)}, u32[]{:S(2)}) collective-permute-start(bf16[2,2,256,512]{3,2,1,0:T(8,128)(2,1)S(1)} %get-tuple-element.29.xb), channel_id=1, source_target_pairs={{8,16},{12,20},{16,8},{20,12},{9,17},{13,21},{17,9},{21,13},{10,18... | collective-permute-start | bytes 3145736 | tf_op jit(solution)/shard_map/ppermute | solution.py:572
  91.1 11.3 %collective-permute-start.11 = (bf16[2,512,512]{2,1,0:T(8,128)(2,1)S(1)}, bf16[2,512,512]{2,1,0:T(8,128)(2,1)S(1)}, u32[]{:S(2)}, u32[]{:S(2)}) collective-permute-start(bf16[2,512,512]{2,1,0:T(8,128)(2,1)S(1)} %get-tuple-element.32.w_high), channel_id=1, source_target_pairs={{0,8},{16,24},{1,9},{17,25},{2,10},{18,26},{3,11},{19,27},{4,12},{... | collective-permute-start | bytes 3145736 | tf_op jit(solution)/shard_map/ppermute | solution.py:631
  113.9 3.6 %collective-permute-start.12 = (bf16[2,512,512]{2,1,0:T(8,128)(2,1)S(1)}, bf16[2,512,512]{2,1,0:T(8,128)(2,1)S(1)}, u32[]{:S(2)}, u32[]{:S(2)}) collective-permute-start(bf16[2,512,512]{2,1,0:T(8,128)(2,1)S(1)} %get-tuple-element.33), channel_id=1, source_target_pairs={{8,0},{24,16},{9,1},{25,17},{10,2},{26,18},{11,3},{27,19},{12,4},{... | collective-permute-start | bytes 3145736 | tf_op jit(solution)/shard_map/ppermute | solution.py:652
  118.4 15.2 %collective-permute-start.14 = (bf16[2,256,512]{2,1,0:T(8,128)(2,1)S(1)}, bf16[2,256,512]{2,1,0:T(8,128)(2,1)S(1)}, u32[]{:S(2)}, u32[]{:S(2)}) collective-permute-start(bf16[2,256,512]{2,1,0:T(8,128)(2,1)S(1)} %get-tuple-element.36), channel_id=1, source_target_pairs={{4,0},{0,4},{20,8},{16,12},{12,16},{8,20},{28,24},{24,28},{5,1},{1... | collective-permute-start | bytes 1572872 | tf_op jit(solution)/shard_map/ppermute | solution.py:671
  126.6 11.8 %collective-permute-start.15 = (bf16[2,256,512]{2,1,0:T(8,128)(2,1)S(1)}, bf16[2,256,512]{2,1,0:T(8,128)(2,1)S(1)}, u32[]{:S(2)}, u32[]{:S(2)}) collective-permute-start(bf16[2,256,512]{2,1,0:T(8,128)(2,1)S(1)} %get-tuple-element.37), channel_id=1, source_target_pairs={{16,0},{20,4},{0,8},{4,12},{24,16},{28,20},{8,24},{12,28},{17,1},{... | collective-permute-start | bytes 1572872 | tf_op jit(solution)/shard_map/ppermute | solution.py:671
  126.6 23.7 %collective-permute-start.16 = (bf16[2,256,512]{2,1,0:T(8,128)(2,1)S(1)}, bf16[2,256,512]{2,1,0:T(8,128)(2,1)S(1)}, u32[]{:S(2)}, u32[]{:S(2)}) collective-permute-start(bf16[2,256,512]{2,1,0:T(8,128)(2,1)S(1)} %get-tuple-element.38), channel_id=1, source_target_pairs={{20,0},{16,4},{4,8},{0,12},{28,16},{24,20},{12,24},{8,28},{21,1},{... | collective-permute-start | bytes 1572872 | tf_op jit(solution)/shard_map/ppermute | solution.py:671
  126.8 23.6 %collective-permute-start.13 = (bf16[2,256,512]{2,1,0:T(8,128)(2,1)S(1)}, bf16[2,256,512]{2,1,0:T(8,128)(2,1)S(1)}, u32[]{:S(2)}, u32[]{:S(2)}) collective-permute-start(bf16[2,256,512]{2,1,0:T(8,128)(2,1)S(1)} %get-tuple-element.35.own), channel_id=1, source_target_pairs={{16,8},{20,12},{8,16},{12,20},{17,9},{21,13},{9,17},{13,21},{18,10... | collective-permute-start | bytes 1572872 | tf_op jit(solution)/shard_map/ppermute | solution.py:671

commit v10 on v8

--- a/solution.py
+++ b/solution.py
@@ -15,7 +15,7 @@
 in_smem = pl.BlockSpec(memory_space=pltpu.SMEM)
 in_vmem = pl.BlockSpec(memory_space=pltpu.VMEM)
 
-info_member, info_piece, info_slot, info_half, info_block, info_self = 3, 4, 12, 14, 16, 20
+info_member, info_piece, info_slot, info_half, info_self = 3, 4, 12, 14, 16
 
 
 def shifted(x, axis, by):
@@ -180,27 +180,14 @@
         self.received.wait()
 
 
-def pack_kernel(place, field, coupling, *rest):
-    pieces, (sems, csems) = rest[:-2], rest[-2:]
-    rows_here = field.shape[1]
-    height = pieces[0].shape[0] - 2 * rows_here
-    own = pl.ds(pl.multiple_of(place[len(pieces)] * height, height), height)
+def pack_kernel(place, field, *rest):
+    pieces, sems = rest[:-1], rest[-1]
     copies = []
     for index, piece in enumerate(pieces):
-        width = piece.shape[1]
+        width = piece.shape[2]
         offset = pl.multiple_of(place[index] * width, width)
-        for plane in range(2):
-            copies.append(
-                pltpu.make_async_copy(
-                    field.at[plane, :, pl.ds(offset, width)],
-                    piece.at[pl.ds(plane * rows_here, rows_here)],
-                    sems.at[index, plane],
-                )
-            )
         copies.append(
-            pltpu.make_async_copy(
-                coupling.at[own], piece.at[pl.ds(2 * rows_here, height)], csems.at[index]
-            )
+            pltpu.make_async_copy(field.at[:, :, pl.ds(offset, width)], piece, sems.at[index])
         )
     start_all(copies)
     wait_all(copies)
@@ -216,34 +203,39 @@
         if index:
             copies.append(pltpu.make_async_copy(piece, target, sems.at[index]))
         else:
-            copies.append(Either(place[len(pieces) + 1], own, piece, target, sems.at[index]))
+            copies.append(Either(place[len(pieces)], own, piece, target, sems.at[index]))
     start_all(copies)
     wait_all(copies)
 
 
-def column_kernel(info, blocks, own, p0, p1, p2, p3, x_column, y_column, rows_held, sems, csems):
+def column_kernel(blocks, coupling, p0, p1, p2, p3, x_column, y_column, sems, csems):
     count, planes, height, order = blocks.shape
     copies = []
+    rows_here = coupling.shape[0]
     for index in range(count):
         for which, column in enumerate((x_column, y_column)):
-            copies.append(
-                pltpu.make_async_copy(
-                    blocks.at[index, pl.ds(2 * which, 2)],
-                    column.at[:, pl.ds(index * height, height), :],
-                    sems.at[index, which],
+            for plane in range(2):
+                copies.append(
+                    pltpu.make_async_copy(
+                        blocks.at[index, 2 * which + plane],
+                        column.at[pl.ds(plane * rows_here + index * height, height)],
+                        sems.at[index, which, plane],
+                    )
                 )
+    part = rows_here // 2
+    for which, column in enumerate((x_column, y_column)):
+        copies.append(
+            pltpu.make_async_copy(
+                coupling.at[pl.ds(which * part, part)],
+                column.at[pl.ds(2 * rows_here, part)],
+                csems.at[which],
             )
-    last = pl.ds(own.shape[0] - height, height)
-    copies.append(Either(info[info_self], own.at[last], p0.at[last], rows_held.at[0], csems.at[0]))
-    for index, piece in enumerate((p1, p2, p3)):
-        copies.append(
-            pltpu.make_async_copy(piece.at[last], rows_held.at[index + 1], csems.at[index + 1])
         )
     start_all(copies)
     wait_all(copies)
 
 
-def both_kernel(info, x_column, x_aside, y_column, y0, y1, rows_next, rows_far, x_both, y_both, sems):
+def both_kernel(info, x_column, x_aside, y_column, y0, y1, x_both, y_both, sems):
     copies = [
         pltpu.make_async_copy(x_column, x_both.at[0], sems.at[0]),
         pltpu.make_async_copy(x_aside, x_both.at[1], sems.at[1]),
@@ -255,9 +247,9 @@
 
 
 class Layers:
-    def __init__(self, info, x_parts, y_parts, row_blocks, held, weights, sems, csems):
+    def __init__(self, info, x_parts, y_parts, held, weights, sems, csems):
         self.info, self.order = info, held.shape[2]
-        self.x_parts, self.y_parts, self.row_blocks = x_parts, y_parts, row_blocks
+        self.x_parts, self.y_parts = x_parts, y_parts
         self.held, self.weights, self.sems, self.csems = held, weights, sems, csems
 
     def half_rows(self, far):
@@ -265,9 +257,10 @@
         return pl.ds(pl.multiple_of(self.info[info_half + far] * height, height), height)
 
     def factor_copies(self, slot, which, parts):
+        height = self.order // 2
         return [
             pltpu.make_async_copy(
-                part.at[plane],
+                part.at[pl.ds(plane * height, height)],
                 self.held.at[
                     slot, which, self.half_rows(far), pl.ds(plane * self.order, self.order)
                 ],
@@ -277,14 +270,30 @@
             for plane in range(2)
         ]
 
-    def y_copies(self, slot):
+    def weight_copies(self, slot, which, parts):
+        height = self.order // 2
+        tall = height // 2
+        copies = []
+        for far, part in enumerate(parts):
+            start = self.info[info_half + far] * height + which * tall
+            rows = pl.ds(pl.multiple_of(start, tall), tall)
+            copies.append(
+                pltpu.make_async_copy(
+                    part.at[pl.ds(2 * height, tall)],
+                    self.weights.at[slot, rows, :],
+                    self.csems.at[slot, which, far],
+                )
+            )
+        return copies
+
+    def start_y(self, slot, with_weights=True):
         turn = self.info[info_slot + slot]
-        return self.factor_copies(slot, 1, [part.at[turn] for part in self.y_parts])
-
-    def start_y(self, slot):
-        start_all(self.y_copies(slot))
-
-    def start_x(self, slot):
+        parts = [part.at[turn] for part in self.y_parts]
+        start_all(self.factor_copies(slot, 1, parts))
+        if with_weights:
+            start_all(self.weight_copies(slot, 1, parts))
+
+    def start_x(self, slot, with_weights=True):
         own, first, second = self.x_parts
         turn, same = self.info[info_slot + slot], self.info[info_self]
         for hit, part in (
@@ -295,38 +304,26 @@
 
             @pl.when(hit)
             def _():
-                start_all(self.factor_copies(slot, 0, [part.at[0], part.at[1]]))
+                parts = [part.at[0], part.at[1]]
+                if with_weights:
+                    start_all(self.weight_copies(slot, 0, parts))
+                start_all(self.factor_copies(slot, 0, parts))
 
     def ready(self, slot, which):
         part = self.x_parts[0].at[0]
         wait_all(self.factor_copies(slot, which, [part, part]))
 
-    def weight_copies(self, slot):
-        height = self.row_blocks[0].shape[1]
-        copies = []
-        for index, block in enumerate(self.row_blocks):
-            for far in range(2):
-                turn = 2 * self.info[info_slot + slot] + far
-                start = self.info[info_half + far] * (self.order // 2)
-                start = start + self.info[info_block + index] * height
-                rows = pl.ds(pl.multiple_of(start, height), height)
-                copies.append(
-                    pltpu.make_async_copy(
-                        block.at[turn], self.weights.at[slot, rows, :], self.csems.at[slot, index, far]
-                    )
-                )
-        return copies
+    def ready_weights(self, slot):
+        part = self.x_parts[0].at[0]
+        for which in range(2):
+            wait_all(self.weight_copies(slot, which, [part, part]))
 
     def rhs_copies(self, slot, pair, rhs, sems):
-        height = self.order // 2
         return [
             pltpu.make_async_copy(
-                piece.at[pl.ds(plane * height, height)],
-                rhs.at[slot, plane, self.half_rows(far), :],
-                sems.at[slot, far, plane],
+                piece, rhs.at[slot, :, self.half_rows(far), :], sems.at[slot, far]
             )
             for far, piece in enumerate(pair)
-            for plane in range(2)
         ]
 
     def start_rhs(self, slot, own, pieces, rhs, sems):
@@ -344,12 +341,11 @@
     def start(self, slot, own, pieces, rhs, sems):
         self.start_y(slot)
         self.start_rhs(slot, own, pieces, rhs, sems)
-        start_all(self.weight_copies(slot))
         self.start_x(slot)
 
     def wait(self, slot, own, pieces, rhs, sems):
         wait_all(self.rhs_copies(slot, pieces[:2], rhs, sems))
-        wait_all(self.weight_copies(slot))
+        self.ready_weights(slot)
 
     def apply(self, slot, source, below, store, fresh):
         order = self.order
@@ -387,31 +383,24 @@
 
 def reduced(rhs, info, slot, weights, incoming):
     def source(plane, rows):
-        values = rhs[slot, plane, rows].astype(f32)
+        values = rhs[slot, plane, rows]
         if plane == 0:
             row = lax.broadcasted_iota(jnp.int32, values.shape, 0) + rows.start
-            column = lax.broadcasted_iota(jnp.int32, (1, values.shape[1]), 1)
-            hit = (column == info[2]) & (info[0] == slot)
-            cell = jnp.where(hit, f32(source_amplitude), f32(0.0))
-            values = values + jnp.where(row == info[1], cell, f32(0.0))
-        scaled = weights[slot, rows].astype(f32) * incoming(plane, rows)
-        return (values - scaled).astype(bf16)
+            column = lax.broadcasted_iota(jnp.int32, values.shape, 1)
+            hit = (row == info[1]) & (column == info[2]) & (info[0] == slot)
+            values = values + jnp.where(hit, f32(source_amplitude), f32(0.0)).astype(bf16)
+        return values - weights[slot, rows] * incoming(plane, rows)
 
     return source
 
 
 def sent(weights, slot, field):
-    def source(plane, rows):
-        scaled = weights[slot, rows].astype(f32) * field[plane, rows].astype(f32)
-        return scaled.astype(bf16)
-
-    return source
+    return lambda plane, rows: weights[slot, rows] * field[plane, rows]
 
 
 def subtract_into(target, forward):
     def store(plane, columns, values):
-        solved = values.astype(bf16).astype(f32)
-        target[plane, :, columns] = (forward[plane, :, columns].astype(f32) - solved).astype(bf16)
+        target[plane, :, columns] = forward[plane, :, columns] - values.astype(bf16)
 
     return store
 
@@ -423,38 +412,38 @@
     return store
 
 
-def first_kernel(info, xb, x0, x1, yb, yf, c0, c1, c2, c3, own, p0, p1, p2, p3, w_low, w_high,
+def first_kernel(info, xb, x0, x1, yb, yf, own, p0, p1, p2, p3, w_low, w_high,
                  held, weights, rhs, below, sems, csems, fsems):
     @pl.when(info[info_member] == 0)
     def _():
-        layers = Layers(info, (xb, x0, x1), (yb, yf), (c0, c1, c2, c3), held, weights, fsems, csems)
+        layers = Layers(info, (xb, x0, x1), (yb, yf), held, weights, fsems, csems)
         fields = (own, (p0, p1, p2, p3), rhs, sems)
         layers.start(0, *fields)
         layers.wait(0, *fields)
         layers.ready(0, 1)
         layers.start(1, *fields)
-        zero = reduced(rhs, info, 0, weights, lambda plane, rows: f32(0.0))
+        zero = reduced(rhs, info, 0, weights, lambda plane, rows: bf16(0.0))
         layers.apply(0, zero, below, round_into(w_low), (0,))
         layers.wait(1, *fields)
-        one = reduced(rhs, info, 1, weights, lambda plane, rows: w_low[plane, rows].astype(f32))
+        one = reduced(rhs, info, 1, weights, lambda plane, rows: w_low[plane, rows])
         layers.apply(1, one, below, round_into(w_high), (0, 1))
 
 
-def last_kernel(info, xb, x0, x1, yb, yf, c0, c1, c2, c3, own, p0, p1, p2, p3, arrived, field, back,
+def last_kernel(info, xb, x0, x1, yb, yf, own, p0, p1, p2, p3, arrived, field, back,
                 held, weights, rhs, forward, below, sems, csems, fsems):
     @pl.when(info[info_member] == 1)
     def _():
-        layers = Layers(info, (xb, x0, x1), (yb, yf), (c0, c1, c2, c3), held, weights, fsems, csems)
+        layers = Layers(info, (xb, x0, x1), (yb, yf), held, weights, fsems, csems)
         fields = (own, (p0, p1, p2, p3), rhs, sems)
         layers.start(0, *fields)
         layers.wait(0, *fields)
         layers.ready(0, 1)
         layers.start(1, *fields)
         low, high = field.at[0], field.at[1]
-        two = reduced(rhs, info, 0, weights, lambda plane, rows: arrived[plane, rows].astype(f32))
+        two = reduced(rhs, info, 0, weights, lambda plane, rows: arrived[plane, rows])
         layers.apply(0, two, below, round_into(forward), (0,))
         layers.wait(1, *fields)
-        three = reduced(rhs, info, 1, weights, lambda plane, rows: forward[plane, rows].astype(f32))
+        three = reduced(rhs, info, 1, weights, lambda plane, rows: forward[plane, rows])
         layers.apply(1, three, below, round_into(high), (0, 1))
         layers.apply(0, sent(weights, 1, high), below, subtract_into(low, forward), ())
         last = sent(weights, 0, low)
@@ -463,7 +452,7 @@
                 back[plane, rows] = last(plane, rows)
 
 
-def back_kernel(info, xb, x0, x1, yb, yf, c0, c1, c2, c3, w_low, w_high, arrived, field,
+def back_kernel(info, xb, x0, x1, yb, yf, w_low, w_high, arrived, field,
                 p0, p1, p2, p3, held, weights, kept, below, csems, fsems, osems):
     def start_pieces(source, slot):
         for index, piece in enumerate((p0, p1, p2, p3)):
@@ -477,20 +466,18 @@
 
     @pl.when(info[info_member] == 0)
     def _():
-        layers = Layers(info, (xb, x0, x1), (yb, yf), (c0, c1, c2, c3), held, weights, fsems, csems)
+        layers = Layers(info, (xb, x0, x1), (yb, yf), held, weights, fsems, csems)
         layers.start_y(1)
         layers.start_x(1)
         layers.ready(1, 1)
-        high_rows = layers.weight_copies(1)
-        start_all(high_rows)
-        layers.start_y(0)
-        layers.start_x(0)
+        layers.start_y(0, False)
+        layers.start_x(0, False)
         low, high = kept.at[0], kept.at[1]
         layers.apply(
             1, lambda plane, rows: arrived[plane, rows], below, subtract_into(high, w_high), (0,)
         )
         start_pieces(kept, 1)
-        wait_all(high_rows)
+        layers.ready_weights(1)
         layers.apply(0, sent(weights, 1, high), below, subtract_into(low, w_low), (0, 1))
         start_pieces(kept, 0)
 
@@ -542,47 +529,41 @@
     for a, b in rounds:
         entries += [(group + a) % 2, (own_x - b) % px_count]
     entries += [group, (group + 1) % 2, own_x, (own_x + 1) % 2]
-    pair = own_y // 2 * 2
-    entries += [own_y, pair + (own_y + 1) % 2, (own_y + 2) % 4, (pair + 2) % 4 + (own_y + 1) % 2]
     entries += [group == member]
     info = jnp.stack([jnp.asarray(entry, jnp.int32) for entry in entries])
 
     sends_to = jnp.stack(
         [((member + a) % 2) * px_count + (own_x + b) % px_count for a, b in rounds]
-        + [own_y, group == member]
+        + [group == member]
     ).astype(jnp.int32)
     piece_shape = jax.ShapeDtypeStruct((2, rows_here, order), bf16)
     shard = jnp.concatenate([x_factor[0], y_factor[0]], axis=0)
     blocks = jnp.broadcast_to(shard[None], (py_count,) + shard.shape)
     packed = pl.pallas_call(
         pack_kernel,
-        out_shape=[jax.ShapeDtypeStruct((2 * rows_here + height, order), bf16)] * len(rounds),
-        in_specs=[in_smem] + [anywhere] * 2,
+        out_shape=[piece_shape] * len(rounds),
+        in_specs=[in_smem, anywhere],
         out_specs=[in_vmem] * len(rounds),
-        scratch_shapes=[
-            pltpu.SemaphoreType.DMA((len(rounds), 2)),
-            pltpu.SemaphoreType.DMA((len(rounds),)),
-        ],
+        scratch_shapes=[pltpu.SemaphoreType.DMA((len(rounds),))],
         compiler_params=params,
-    )(sends_to, field, coupling[0])
+    )(sends_to, field)
     pieces = [
         lax.ppermute(piece, ("sec", "px"), pairs(a, b)) for piece, (a, b) in zip(packed, rounds)
     ]
     blocks = lax.all_to_all(blocks, "py", split_axis=0, concat_axis=0, tiled=True)
 
-    column_shape = jax.ShapeDtypeStruct((2, rows_here, order), bf16)
-    rows_shape = jax.ShapeDtypeStruct((len(rounds), height, order), bf16)
-    x_column, y_column, rows_held = pl.pallas_call(
+    column_shape = jax.ShapeDtypeStruct((2 * rows_here + rows_here // 2, order), bf16)
+    x_column, y_column = pl.pallas_call(
         column_kernel,
-        out_shape=[column_shape, column_shape, rows_shape],
-        in_specs=[in_smem] + [anywhere] * 6,
-        out_specs=[in_vmem] * 3,
+        out_shape=[column_shape] * 2,
+        in_specs=[anywhere] * 6,
+        out_specs=[in_vmem] * 2,
         scratch_shapes=[
-            pltpu.SemaphoreType.DMA((py_count, 2)),
-            pltpu.SemaphoreType.DMA((len(rounds),)),
+            pltpu.SemaphoreType.DMA((py_count, 2, 2)),
+            pltpu.SemaphoreType.DMA((2,)),
         ],
         compiler_params=params,
-    )(info, blocks, packed[0], *pieces)
+    )(blocks, coupling[0], *pieces)
 
     def across(block, a):
         return lax.ppermute(block, ("sec", "px"), pairs(a, 0))
@@ -590,24 +571,19 @@
     def aside(block):
         return lax.ppermute(block, "px", [(y, (y + 1) % 2) for y in range(2)])
 
-    def over_z(block, bit):
-        return lax.ppermute(block, "py", [(z, z ^ bit) for z in range(py_count)])
-
     y_near = [across(y_column, a) for a in range(2)]
     x_aside = aside(x_column)
-    rows_next = over_z(rows_held, 1)
-    rows_far = over_z(rows_held, 2)
     x_both, y_both = pl.pallas_call(
         both_kernel,
         out_shape=[jax.ShapeDtypeStruct((2,) + column_shape.shape, bf16)] * 2,
-        in_specs=[in_smem] + [anywhere] * 7,
+        in_specs=[in_smem] + [anywhere] * 5,
         out_specs=[in_vmem] * 2,
         scratch_shapes=[pltpu.SemaphoreType.DMA((4,))],
         compiler_params=params,
-    )(info, x_column, x_aside, y_column, *y_near, rows_next, rows_far)
+    )(info, x_column, x_aside, y_column, *y_near)
     y_far = aside(y_both)
     x_across = [across(x_both, a) for a in range(2)]
-    factors = [x_both, *x_across, y_both, y_far, rows_held, rows_next, rows_far, over_z(rows_next, 2)]
+    factors = [x_both, *x_across, y_both, y_far]
 
     full_shape = jax.ShapeDtypeStruct((2, order, order), bf16)
     factor_scratch = pltpu.VMEM((2, 2, order, 2 * order), bf16)
@@ -615,8 +591,8 @@
     field_scratch = pltpu.VMEM((2, 2, order, order), bf16)
     below_scratch = pltpu.VMEM((2 * order, 2 * order), bf16)
     factor_sems = pltpu.SemaphoreType.DMA((2, 2, 2, 2))
-    weight_sems = pltpu.SemaphoreType.DMA((2, py_count, 2))
-    field_sems = pltpu.SemaphoreType.DMA((2, 2, 2))
+    weight_sems = pltpu.SemaphoreType.DMA((2, 2, 2))
+    field_sems = pltpu.SemaphoreType.DMA((2, 2))
     solve_flops = 16 * order**3
     fields = (packed[0], *pieces)
 
@@ -628,7 +604,7 @@
     w_low, w_high = pl.pallas_call(
         first_kernel,
         out_shape=[full_shape] * 2,
-        in_specs=[in_smem] + [anywhere] * 14,
+        in_specs=[in_smem] + [anywhere] * 10,
         out_specs=[in_vmem] * 2,
         scratch_shapes=[
             factor_scratch,
@@ -648,7 +624,7 @@
     solved, back = pl.pallas_call(
         last_kernel,
         out_shape=[jax.ShapeDtypeStruct((2, 2, order, order), bf16), full_shape],
-        in_specs=[in_smem] + [anywhere] * 14 + [in_vmem],
+        in_specs=[in_smem] + [anywhere] * 10 + [in_vmem],
         out_specs=[in_vmem] * 2,
         scratch_shapes=[
             factor_scratch,
@@ -669,7 +645,7 @@
     results = pl.pallas_call(
         back_kernel,
         out_shape=[piece_shape] * len(rounds),
-        in_specs=[in_smem] + [anywhere] * 9 + [in_vmem] * 3 + [anywhere],
+        in_specs=[in_smem] + [anywhere] * 5 + [in_vmem] * 3 + [anywhere],
         out_specs=[anywhere] * len(rounds),
         scratch_shapes=[
             factor_scratch,

time: 150 us -> 157 us (1.047)
  local copies, waits for them, and re-layouts: 1.88 us -> 7.33 us
  waiting for transfers between devices: 83.2 us -> 85.5 us
    ppermute x2, waiting for transfers between devices: 7.6 us -> 32.4 us  [aside(): return lax.ppermute(block, 'px', [(y, (y + 1) % 2) for y in range(2)])]
    ppermute x3 -> x0, waiting for transfers between devices: 23.7 us -> none  [over_z(): return lax.ppermute(block, 'py', [(z, z ^ bit) for z in range(py_count)])]
    unnamed x6 -> x26, local copies, waits for them, and re-layouts: 0.01 us -> 5.48 us
    ppermute x3 -> x0, starting transfers between devices: 5.07 us -> none  [over_z(): return lax.ppermute(block, 'py', [(z, z ^ bit) for z in range(py_count)])]
    ppermute x4, waiting for transfers between devices: 0.84 us -> 4.54 us  [across(): return lax.ppermute(block, ('sec', 'px'), pairs(a, 0))]
    ppermute x4, starting transfers between devices: 12.4 us -> 15 us  [on_device(): lax.ppermute(piece, ('sec', 'px'), back_pairs(a, b))]
    ppermute x4, starting transfers between devices: 6.77 us -> 8.95 us  [across(): return lax.ppermute(block, ('sec', 'px'), pairs(a, 0))]
    ppermute x1, waiting for transfers between devices: 9.81 us -> 8.24 us  [on_device(): incoming = lax.ppermute(w_high, 'sec', up)]
  transfers between devices with their start and end apart: 20 -> 17, of which waited for: 13 -> 13; matrix products, arithmetic and copies ran while one was open for 1% -> 0% of each run, Pallas kernels for 2% -> 1%
where the time goes in v10:
time: 157 us; the launch traced here: 156 us
  waiting for transfers between devices  85.5 us (54%)
  starting transfers between devices  40.3 us (26%)
  Pallas kernels  19 us (12%)
  local copies, waits for them, and re-layouts  7.33 us (5%)
  between operations  3.13 us (2%)
    ppermute x2, waiting for transfers between devices, aside(): return lax.ppermute(block, 'px', [(y, (y + 1) % 2) for y in range(2)])  32.4 us
    ppermute x4, waiting for transfers between devices, on_device(): lax.ppermute(piece, ('sec', 'px'), pairs(a, b))  19.1 us
    ppermute x4, waiting for transfers between devices, on_device(): lax.ppermute(piece, ('sec', 'px'), back_pairs(a, b))  19 us
    ppermute x4, starting transfers between devices, on_device(): lax.ppermute(piece, ('sec', 'px'), back_pairs(a, b))  15 us
    pallas_call x1, Pallas kernels, on_device(): pl.pallas_call(last_kernel, out_shape=[jax.ShapeDtypeStruct((2, 2, order,...  10.5 us
    ppermute x4, starting transfers between devices, across(): return lax.ppermute(block, ('sec', 'px'), pairs(a, 0))  8.95 us
    ppermute x1, waiting for transfers between devices, on_device(): incoming = lax.ppermute(w_high, 'sec', up)  8.24 us
    ppermute x4, starting transfers between devices, on_device(): lax.ppermute(piece, ('sec', 'px'), pairs(a, b))  6.94 us
  transfers between devices with their start and end apart: 17, of which 13 were waited for; matrix products, arithmetic and copies ran while one was open for 0% of the time, Pallas kernels for 1%

profile of v10, /device:TPU:1, one launch (start us, length us, event | category | flops | bytes accessed | tf_op | source)
XLA Modules:
  0.0 156.3 jit_solution(17604919033818881797)
XLA Ops:
  0.0 1.0 pad_maximum_fusion
  1.0 1.1 broadcast_in_dim.4
  2.1 5.6 %all-to-all-start = ((bf16[4,4,64,512]{3,2,1,0:T(8,128)(2,1)}), bf16[4,4,64,512]{3,2,1,0:T(8,128)(2,1)S(1)}, u32[]{:S(2)}, u32[]{:S(2)}) async-start(bf16[4,4,64,512]{3,2,1,0:T(8,128)(2,1)} %broadcast_in_dim.4), calls=%async_computation | async-start | bytes 2097152 | tf_op jit(solution)/shard_map/all_to_all | solution.py:553
  8.6 3.1 %collective-permute-start.1 = (bf16[2,256,512]{2,1,0:T(8,128)(2,1)S(1)}, bf16[2,256,512]{2,1,0:T(8,128)(2,1)S(1)}, u32[]{:S(2)}, u32[]{:S(2)}) collective-permute-start(bf16[2,256,512]{2,1,0:T(8,128)(2,1)S(1)} %get-tuple-element.22), channel_id=1, source_target_pairs={{0,4},{4,0},{8,20},{12,16},{16,12},{20,8},{24,28},{28,24},{1,5},{5... | collective-permute-start | bytes 1572872 | tf_op jit(solution)/shard_map/ppermute | solution.py:551
  12.3 3.3 %collective-permute-start = (bf16[2,256,512]{2,1,0:T(8,128)(2,1)S(1)}, bf16[2,256,512]{2,1,0:T(8,128)(2,1)S(1)}, u32[]{:S(2)}, u32[]{:S(2)}) collective-permute-start(bf16[2,256,512]{2,1,0:T(8,128)(2,1)S(1)} %get-tuple-element.21.own), channel_id=1, source_target_pairs={{8,16},{12,20},{16,8},{20,12},{9,17},{13,21},{17,9},{21,13},{10,18... | collective-permute-start | bytes 1572872 | tf_op jit(solution)/shard_map/ppermute | solution.py:551
  16.4 6.8 %collective-permute-done.1.p1 = bf16[2,256,512]{2,1,0:T(8,128)(2,1)S(1)} collective-permute-done((bf16[2,256,512]{2,1,0:T(8,128)(2,1)S(1)}, bf16[2,256,512]{2,1,0:T(8,128)(2,1)S(1)}, u32[]{:S(2)}, u32[]{:S(2)}) %collective-permute-start.1) | collective-permute-done | bytes 524320 | tf_op jit(solution)/shard_map/ppermute | solution.py:551
  23.2 2.5 %collective-permute-done.2.p2 = bf16[2,256,512]{2,1,0:T(8,128)(2,1)S(1)} collective-permute-done((bf16[2,256,512]{2,1,0:T(8,128)(2,1)S(1)}, bf16[2,256,512]{2,1,0:T(8,128)(2,1)S(1)}, u32[]{:S(2)}, u32[]{:S(2)}) %collective-permute-start.2) | collective-permute-done | bytes 524320 | tf_op jit(solution)/shard_map/ppermute | solution.py:551
  25.7 9.8 %collective-permute-done.3.p3 = bf16[2,256,512]{2,1,0:T(8,128)(2,1)S(1)} collective-permute-done((bf16[2,256,512]{2,1,0:T(8,128)(2,1)S(1)}, bf16[2,256,512]{2,1,0:T(8,128)(2,1)S(1)}, u32[]{:S(2)}, u32[]{:S(2)}) %collective-permute-start.3) | collective-permute-done | bytes 524320 | tf_op jit(solution)/shard_map/ppermute | solution.py:551
  37.1 1.0 copy-done.4
  38.1 1.0 copy-done.7
  39.2 0.9 copy-done.9
  40.1 1.9 %shard_map.56 = (bf16[640,512]{1,0:T(8,128)(2,1)S(1)}, bf16[640,512]{1,0:T(8,128)(2,1)S(1)}) custom-call(bf16[4,4,64,512]{3,2,1,0:T(8,128)(2,1)S(1)} %all-to-all-done.blocks, bf16[256,512]{1,0:T(8,128)(2,1)S(1)} %bitcast.25, bf16[2,256,512]{2,1,0:T(8,128)(2,1)S(1)} %copy-done.7, bf16[2,256,512]{2,1,0:T(8,128)(2,1)S(1)} %collective-permute-done.1.p1, ...), custom_call_target="tpu_custom_call" | custom-call | tf_op jit(solution)/shard_map/pallas_call | solution.py:556
  42.9 4.2 %collective-permute-start.5 = (bf16[640,512]{1,0:T(8,128)(2,1)S(1)}, bf16[640,512]{1,0:T(8,128)(2,1)}, u32[]{:S(2)}, u32[]{:S(2)}) collective-permute-start(bf16[640,512]{1,0:T(8,128)(2,1)S(1)} %get-tuple-element.26.y_column), channel_id=1, source_target_pairs={{8,16},{12,20},{16,8},{20,12},{9,17},{13,21},{17,9},{21,13},{10,18... | collective-permute-start | bytes 1966088 | tf_op jit(solution)/shard_map/ppermute | solution.py:569
  50.6 8.1 %collective-permute-done.4.x_aside = bf16[640,512]{1,0:T(8,128)(2,1)S(1)} collective-permute-done((bf16[640,512]{1,0:T(8,128)(2,1)S(1)}, bf16[640,512]{1,0:T(8,128)(2,1)S(1)}, u32[]{:S(2)}, u32[]{:S(2)}) %collective-permute-start.4) | collective-permute-done | bytes 655392 | tf_op jit(solution)/shard_map/ppermute | solution.py:572
  58.8 1.6 %collective-permute-done.5.y0 = bf16[640,512]{1,0:T(8,128)(2,1)} collective-permute-done((bf16[640,512]{1,0:T(8,128)(2,1)S(1)}, bf16[640,512]{1,0:T(8,128)(2,1)}, u32[]{:S(2)}, u32[]{:S(2)}) %collective-permute-start.5) | collective-permute-done | bytes 655392 | tf_op jit(solution)/shard_map/ppermute | solution.py:569
  60.4 2.1 %shard_map.57 = (bf16[2,640,512]{2,1,0:T(8,128)(2,1)S(1)}, bf16[2,640,512]{2,1,0:T(8,128)(2,1)S(1)}) custom-call(s32[17]{0:T(128)S(1)} %stack.81.info, bf16[640,512]{1,0:T(8,128)(2,1)S(1)} %get-tuple-element.25.x_column, bf16[640,512]{1,0:T(8,128)(2,1)S(1)} %collective-permute-done.4.x_aside, bf16[640,512]{1,0:T(8,128)(2,1)S(1)} %get-tuple-element.26.y_column, ...), custom_call_target="tpu_custom_call" | custom-call | tf_op jit(solution)/shard_map/pallas_call | solution.py:576
  62.7 4.8 %collective-permute-start.7 = (bf16[2,640,512]{2,1,0:T(8,128)(2,1)S(1)}, bf16[2,640,512]{2,1,0:T(8,128)(2,1)S(1)}, u32[]{:S(2)}, u32[]{:S(2)}) collective-permute-start(bf16[2,640,512]{2,1,0:T(8,128)(2,1)S(1)} %get-tuple-element.27.xb), channel_id=1, source_target_pairs={{8,16},{12,20},{16,8},{20,12},{9,17},{13,21},{17,9},{21,13},{10,18... | collective-permute-start | bytes 3932168 | tf_op jit(solution)/shard_map/ppermute | solution.py:569
  67.5 24.3 %collective-permute-done.9.yf = bf16[2,640,512]{2,1,0:T(8,128)(2,1)S(1)} collective-permute-done((bf16[2,640,512]{2,1,0:T(8,128)(2,1)S(1)}, bf16[2,640,512]{2,1,0:T(8,128)(2,1)S(1)}, u32[]{:S(2)}, u32[]{:S(2)}) %collective-permute-start.9) | collective-permute-done | bytes 1310752 | tf_op jit(solution)/shard_map/ppermute | solution.py:572
  91.8 2.9 %collective-permute-done.7.x0 = bf16[2,640,512]{2,1,0:T(8,128)(2,1)S(1)} collective-permute-done((bf16[2,640,512]{2,1,0:T(8,128)(2,1)S(1)}, bf16[2,640,512]{2,1,0:T(8,128)(2,1)S(1)}, u32[]{:S(2)}, u32[]{:S(2)}) %collective-permute-start.7) | collective-permute-done | bytes 1310752 | tf_op jit(solution)/shard_map/ppermute | solution.py:569
  95.6 1.3 collective-permute-start.10
  96.9 8.2 %collective-permute-done.10.arrived = bf16[2,512,512]{2,1,0:T(8,128)(2,1)S(1)} collective-permute-done((bf16[2,512,512]{2,1,0:T(8,128)(2,1)S(1)}, bf16[2,512,512]{2,1,0:T(8,128)(2,1)S(1)}, u32[]{:S(2)}, u32[]{:S(2)}) %collective-permute-start.10) | collective-permute-done | bytes 1048608 | tf_op jit(solution)/shard_map/ppermute | solution.py:623
  105.1 10.5 %shard_map.59 = (bf16[2,2,512,512]{3,2,1,0:T(8,128)(2,1)S(1)}, bf16[2,512,512]{2,1,0:T(8,128)(2,1)S(1)}) custom-call(s32[17]{0:T(128)S(1)} %stack.81.info, bf16[2,640,512]{2,1,0:T(8,128)(2,1)S(1)} %get-tuple-element.27.xb, bf16[2,640,512]{2,1,0:T(8,128)(2,1)S(1)} %collective-permute-done.7.x0, bf16[2,640,512]{2,1,0:T(8,128)(2,1)S(1)} %collective-permute-done.8.x1, ...), custom_call_target="tpu_custom_call" | custom-call | flops 6442450944 | bytes 8388608 | tf_op jit(solution)/shard_map/pallas_call | solution.py:624
  115.6 1.4 collective-permute-start.11
  117.0 2.2 %collective-permute-done.11.arrived = bf16[2,512,512]{2,1,0:T(8,128)(2,1)S(1)} collective-permute-done((bf16[2,512,512]{2,1,0:T(8,128)(2,1)S(1)}, bf16[2,512,512]{2,1,0:T(8,128)(2,1)S(1)}, u32[]{:S(2)}, u32[]{:S(2)}) %collective-permute-start.11) | collective-permute-done | bytes 1048608 | tf_op jit(solution)/shard_map/ppermute | solution.py:644
  119.2 1.0 shard_map.60
  120.2 11.0 %collective-permute-start.13 = (bf16[2,256,512]{2,1,0:T(8,128)(2,1)S(1)}, bf16[2,256,512]{2,1,0:T(8,128)(2,1)S(1)}, u32[]{:S(2)}, u32[]{:S(2)}) collective-permute-start(bf16[2,256,512]{2,1,0:T(8,128)(2,1)S(1)} %get-tuple-element.34), channel_id=1, source_target_pairs={{4,0},{0,4},{20,8},{16,12},{12,16},{8,20},{28,24},{24,28},{5,1},{1... | collective-permute-start | bytes 1572872 | tf_op jit(solution)/shard_map/ppermute | solution.py:663
  131.4 3.8 %collective-permute-start.12 = (bf16[2,256,512]{2,1,0:T(8,128)(2,1)S(1)}, bf16[2,256,512]{2,1,0:T(8,128)(2,1)S(1)}, u32[]{:S(2)}, u32[]{:S(2)}) collective-permute-start(bf16[2,256,512]{2,1,0:T(8,128)(2,1)S(1)} %get-tuple-element.33.own), channel_id=1, source_target_pairs={{16,8},{20,12},{8,16},{12,20},{17,9},{21,13},{9,17},{13,21},{18,10... | collective-permute-start | bytes 1572872 | tf_op jit(solution)/shard_map/ppermute | solution.py:663
  135.2 3.0 %collective-permute-done.13.rest_1_ = bf16[2,256,512]{2,1,0:T(8,128)(2,1)S(1)} collective-permute-done((bf16[2,256,512]{2,1,0:T(8,128)(2,1)S(1)}, bf16[2,256,512]{2,1,0:T(8,128)(2,1)S(1)}, u32[]{:S(2)}, u32[]{:S(2)}) %collective-permute-start.13) | collective-permute-done | bytes 524320 | tf_op jit(solution)/shard_map/ppermute | solution.py:663
  138.2 4.8 %collective-permute-done.14.rest_2_ = bf16[2,256,512]{2,1,0:T(8,128)(2,1)S(1)} collective-permute-done((bf16[2,256,512]{2,1,0:T(8,128)(2,1)S(1)}, bf16[2,256,512]{2,1,0:T(8,128)(2,1)S(1)}, u32[]{:S(2)}, u32[]{:S(2)}) %collective-permute-start.14) | collective-permute-done | bytes 524320 | tf_op jit(solution)/shard_map/ppermute | solution.py:663
  143.0 9.2 %collective-permute-done.15.rest_3_ = bf16[2,256,512]{2,1,0:T(8,128)(2,1)S(1)} collective-permute-done((bf16[2,256,512]{2,1,0:T(8,128)(2,1)S(1)}, bf16[2,256,512]{2,1,0:T(8,128)(2,1)S(1)}, u32[]{:S(2)}, u32[]{:S(2)}) %collective-permute-start.15) | collective-permute-done | bytes 524320 | tf_op jit(solution)/shard_map/ppermute | solution.py:663
  152.2 2.1 %collective-permute-done.12.rest_0_ = bf16[2,256,512]{2,1,0:T(8,128)(2,1)S(1)} collective-permute-done((bf16[2,256,512]{2,1,0:T(8,128)(2,1)S(1)}, bf16[2,256,512]{2,1,0:T(8,128)(2,1)S(1)}, u32[]{:S(2)}, u32[]{:S(2)}) %collective-permute-start.12) | collective-permute-done | bytes 524320 | tf_op jit(solution)/shard_map/ppermute | solution.py:663
  154.3 1.9 %shard_map.61 = bf16[2,256,2048]{2,1,0:T(8,128)(2,1)} custom-call(s32[5]{0:T(128)S(1)} %stack.69.place, bf16[2,256,512]{2,1,0:T(8,128)(2,1)S(1)} %get-tuple-element.33.own, bf16[2,256,512]{2,1,0:T(8,128)(2,1)S(1)} %collective-permute-done.12.rest_0_, bf16[2,256,512]{2,1,0:T(8,128)(2,1)S(1)} %collective-permute-done.13.rest_1_, ...), custom_call_target="tpu_custom_call" | custom-call | tf_op jit(solution)/shard_map/pallas_call | solution.py:665
  (40 shorter events, 6.9 us)
Async XLA Ops:
  2.1 5.6 %copy-start = (bf16[2,1,256,2048]{3,2,1,0:T(8,128)(2,1)S(1)}, bf16[2,1,256,2048]{3,2,1,0:T(8,128)(2,1)}, u32[]{:S(2)}) copy-start(bf16[2,1,256,2048]{3,2,1,0:T(8,128)(2,1)} %param.5) | copy-start | bytes 6291460
  2.1 35.0 %all-to-all-start = ((bf16[4,4,64,512]{3,2,1,0:T(8,128)(2,1)}), bf16[4,4,64,512]{3,2,1,0:T(8,128)(2,1)S(1)}, u32[]{:S(2)}, u32[]{:S(2)}) async-start(bf16[4,4,64,512]{3,2,1,0:T(8,128)(2,1)} %broadcast_in_dim.4), calls=%async_computation | async-start | bytes 2097152 | tf_op jit(solution)/shard_map/all_to_all | solution.py:553
  8.6 14.5 %collective-permute-start.1 = (bf16[2,256,512]{2,1,0:T(8,128)(2,1)S(1)}, bf16[2,256,512]{2,1,0:T(8,128)(2,1)S(1)}, u32[]{:S(2)}, u32[]{:S(2)}) collective-permute-start(bf16[2,256,512]{2,1,0:T(8,128)(2,1)S(1)} %get-tuple-element.22), channel_id=1, source_target_pairs={{0,4},{4,0},{8,20},{12,16},{16,12},{20,8},{24,28},{28,24},{1,5},{5... | collective-permute-start | bytes 1572872 | tf_op jit(solution)/shard_map/ppermute | solution.py:551
  11.7 14.0 %collective-permute-start.2 = (bf16[2,256,512]{2,1,0:T(8,128)(2,1)S(1)}, bf16[2,256,512]{2,1,0:T(8,128)(2,1)S(1)}, u32[]{:S(2)}, u32[]{:S(2)}) collective-permute-start(bf16[2,256,512]{2,1,0:T(8,128)(2,1)S(1)} %get-tuple-element.23), channel_id=1, source_target_pairs={{0,16},{4,20},{8,0},{12,4},{16,24},{20,28},{24,8},{28,12},{1,17},{... | collective-permute-start | bytes 1572872 | tf_op jit(solution)/shard_map/ppermute | solution.py:551
  11.7 23.8 %collective-permute-start.3 = (bf16[2,256,512]{2,1,0:T(8,128)(2,1)S(1)}, bf16[2,256,512]{2,1,0:T(8,128)(2,1)S(1)}, u32[]{:S(2)}, u32[]{:S(2)}) collective-permute-start(bf16[2,256,512]{2,1,0:T(8,128)(2,1)S(1)} %get-tuple-element.24), channel_id=1, source_target_pairs={{0,20},{4,16},{8,4},{12,0},{16,28},{20,24},{24,12},{28,8},{1,21},{... | collective-permute-start | bytes 1572872 | tf_op jit(solution)/shard_map/ppermute | solution.py:551
  12.3 24.0 %collective-permute-start = (bf16[2,256,512]{2,1,0:T(8,128)(2,1)S(1)}, bf16[2,256,512]{2,1,0:T(8,128)(2,1)S(1)}, u32[]{:S(2)}, u32[]{:S(2)}) collective-permute-start(bf16[2,256,512]{2,1,0:T(8,128)(2,1)S(1)} %get-tuple-element.21.own), channel_id=1, source_target_pairs={{8,16},{12,20},{16,8},{20,12},{9,17},{13,21},{17,9},{21,13},{10,18... | collective-permute-start | bytes 1572872 | tf_op jit(solution)/shard_map/ppermute | solution.py:551
  15.6 0.8 copy-start.10
  25.7 16.3 %copy-start.1 = (bf16[2,256,512]{2,1,0:T(8,128)(2,1)}, bf16[2,256,512]{2,1,0:T(8,128)(2,1)S(1)}, u32[]{:S(2)}) copy-start(bf16[2,256,512]{2,1,0:T(8,128)(2,1)S(1)} %collective-permute-done.2.p2) | copy-start | bytes 1572868
  35.5 0.8 copy-start.3
  36.3 0.8 copy-start.6
  37.1 1.0 copy-start.4
  38.1 1.0 copy-start.7
  39.2 0.9 copy-start.9
  40.1 7.1 %copy-start.12 = (s32[16]{0:T(128)S(1)}, s32[16]{0:T(128)}, u32[]{:S(2)}) copy-start(s32[16]{0:T(128)} %param.6) | copy-start | bytes 196
  42.0 16.7 %collective-permute-start.4 = (bf16[640,512]{1,0:T(8,128)(2,1)S(1)}, bf16[640,512]{1,0:T(8,128)(2,1)S(1)}, u32[]{:S(2)}, u32[]{:S(2)}) collective-permute-start(bf16[640,512]{1,0:T(8,128)(2,1)S(1)} %get-tuple-element.25.x_column), channel_id=1, source_target_pairs={{0,4},{4,0},{1,5},{5,1},{2,6},{6,2},{3,7},{7,3},{8,12},{12,8},{9,1... | collective-permute-start | bytes 1966088 | tf_op jit(solution)/shard_map/ppermute | solution.py:572
  42.9 15.8 %collective-permute-start.6 = (bf16[640,512]{1,0:T(8,128)(2,1)S(1)}, bf16[640,512]{1,0:T(8,128)(2,1)S(1)}, u32[]{:S(2)}, u32[]{:S(2)}) collective-permute-start(bf16[640,512]{1,0:T(8,128)(2,1)S(1)} %get-tuple-element.26.y_column), channel_id=1, source_target_pairs={{0,16},{4,20},{8,0},{12,4},{16,24},{20,28},{24,8},{28,12},{1,17},{... | collective-permute-start | bytes 1966088 | tf_op jit(solution)/shard_map/ppermute | solution.py:569
  42.9 17.4 %collective-permute-start.5 = (bf16[640,512]{1,0:T(8,128)(2,1)S(1)}, bf16[640,512]{1,0:T(8,128)(2,1)}, u32[]{:S(2)}, u32[]{:S(2)}) collective-permute-start(bf16[640,512]{1,0:T(8,128)(2,1)S(1)} %get-tuple-element.26.y_column), channel_id=1, source_target_pairs={{8,16},{12,20},{16,8},{20,12},{9,17},{13,21},{17,9},{21,13},{10,18... | collective-permute-start | bytes 1966088 | tf_op jit(solution)/shard_map/ppermute | solution.py:569
  50.6 44.2 %copy-start.2 = (bf16[2,256,512]{2,1,0:T(8,128)(2,1)S(1)}, bf16[2,256,512]{2,1,0:T(8,128)(2,1)}, u32[]{:S(2)}) copy-start(bf16[2,256,512]{2,1,0:T(8,128)(2,1)} %copy-done.1) | copy-start | bytes 1572868
  50.6 44.2 %copy-start.5 = (bf16[2,256,512]{2,1,0:T(8,128)(2,1)S(1)}, bf16[2,256,512]{2,1,0:T(8,128)(2,1)}, u32[]{:S(2)}) copy-start(bf16[2,256,512]{2,1,0:T(8,128)(2,1)} %copy-done.3) | copy-start | bytes 1572868
  50.6 44.2 %copy-start.8 = (bf16[2,256,512]{2,1,0:T(8,128)(2,1)S(1)}, bf16[2,256,512]{2,1,0:T(8,128)(2,1)}, u32[]{:S(2)}) copy-start(bf16[2,256,512]{2,1,0:T(8,128)(2,1)} %copy-done.6) | copy-start | bytes 1572868
  50.6 44.2 %copy-start.11 = (bf16[2,256,512]{2,1,0:T(8,128)(2,1)S(1)}, bf16[2,256,512]{2,1,0:T(8,128)(2,1)}, u32[]{:S(2)}) copy-start(bf16[2,256,512]{2,1,0:T(8,128)(2,1)} %copy-done.10) | copy-start | bytes 1572868
  62.4 29.4 %collective-permute-start.9 = (bf16[2,640,512]{2,1,0:T(8,128)(2,1)S(1)}, bf16[2,640,512]{2,1,0:T(8,128)(2,1)S(1)}, u32[]{:S(2)}, u32[]{:S(2)}) collective-permute-start(bf16[2,640,512]{2,1,0:T(8,128)(2,1)S(1)} %get-tuple-element.28.yb), channel_id=1, source_target_pairs={{0,4},{4,0},{1,5},{5,1},{2,6},{6,2},{3,7},{7,3},{8,12},{12,8},{9,1... | collective-permute-start | bytes 3932168 | tf_op jit(solution)/shard_map/ppermute | solution.py:572
  62.7 29.1 %collective-permute-start.8 = (bf16[2,640,512]{2,1,0:T(8,128)(2,1)S(1)}, bf16[2,640,512]{2,1,0:T(8,128)(2,1)S(1)}, u32[]{:S(2)}, u32[]{:S(2)}) collective-permute-start(bf16[2,640,512]{2,1,0:T(8,128)(2,1)S(1)} %get-tuple-element.27.xb), channel_id=1, source_target_pairs={{0,16},{4,20},{8,0},{12,4},{16,24},{20,28},{24,8},{28,12},{1,17},{... | collective-permute-start | bytes 3932168 | tf_op jit(solution)/shard_map/ppermute | solution.py:569
  62.7 32.0 %collective-permute-start.7 = (bf16[2,640,512]{2,1,0:T(8,128)(2,1)S(1)}, bf16[2,640,512]{2,1,0:T(8,128)(2,1)S(1)}, u32[]{:S(2)}, u32[]{:S(2)}) collective-permute-start(bf16[2,640,512]{2,1,0:T(8,128)(2,1)S(1)} %get-tuple-element.27.xb), channel_id=1, source_target_pairs={{8,16},{12,20},{16,8},{20,12},{9,17},{13,21},{17,9},{21,13},{10,18... | collective-permute-start | bytes 3932168 | tf_op jit(solution)/shard_map/ppermute | solution.py:569
  95.6 9.5 %collective-permute-start.10 = (bf16[2,512,512]{2,1,0:T(8,128)(2,1)S(1)}, bf16[2,512,512]{2,1,0:T(8,128)(2,1)S(1)}, u32[]{:S(2)}, u32[]{:S(2)}) collective-permute-start(bf16[2,512,512]{2,1,0:T(8,128)(2,1)S(1)} %get-tuple-element.30.w_high), channel_id=1, source_target_pairs={{0,8},{16,24},{1,9},{17,25},{2,10},{18,26},{3,11},{19,27},{4,12},{... | collective-permute-start | bytes 3145736 | tf_op jit(solution)/shard_map/ppermute | solution.py:623
  115.6 3.6 %collective-permute-start.11 = (bf16[2,512,512]{2,1,0:T(8,128)(2,1)S(1)}, bf16[2,512,512]{2,1,0:T(8,128)(2,1)S(1)}, u32[]{:S(2)}, u32[]{:S(2)}) collective-permute-start(bf16[2,512,512]{2,1,0:T(8,128)(2,1)S(1)} %get-tuple-element.31), channel_id=1, source_target_pairs={{8,0},{24,16},{9,1},{25,17},{10,2},{26,18},{11,3},{27,19},{12,4},{... | collective-permute-start | bytes 3145736 | tf_op jit(solution)/shard_map/ppermute | solution.py:644
  120.2 18.0 %collective-permute-start.13 = (bf16[2,256,512]{2,1,0:T(8,128)(2,1)S(1)}, bf16[2,256,512]{2,1,0:T(8,128)(2,1)S(1)}, u32[]{:S(2)}, u32[]{:S(2)}) collective-permute-start(bf16[2,256,512]{2,1,0:T(8,128)(2,1)S(1)} %get-tuple-element.34), channel_id=1, source_target_pairs={{4,0},{0,4},{20,8},{16,12},{12,16},{8,20},{28,24},{24,28},{5,1},{1... | collective-permute-start | bytes 1572872 | tf_op jit(solution)/shard_map/ppermute | solution.py:663
  131.3 11.8 %collective-permute-start.14 = (bf16[2,256,512]{2,1,0:T(8,128)(2,1)S(1)}, bf16[2,256,512]{2,1,0:T(8,128)(2,1)S(1)}, u32[]{:S(2)}, u32[]{:S(2)}) collective-permute-start(bf16[2,256,512]{2,1,0:T(8,128)(2,1)S(1)} %get-tuple-element.35), channel_id=1, source_target_pairs={{16,0},{20,4},{0,8},{4,12},{24,16},{28,20},{8,24},{12,28},{17,1},{... | collective-permute-start | bytes 1572872 | tf_op jit(solution)/shard_map/ppermute | solution.py:663
  131.3 20.9 %collective-permute-start.15 = (bf16[2,256,512]{2,1,0:T(8,128)(2,1)S(1)}, bf16[2,256,512]{2,1,0:T(8,128)(2,1)S(1)}, u32[]{:S(2)}, u32[]{:S(2)}) collective-permute-start(bf16[2,256,512]{2,1,0:T(8,128)(2,1)S(1)} %get-tuple-element.36), channel_id=1, source_target_pairs={{20,0},{16,4},{4,8},{0,12},{28,16},{24,20},{12,24},{8,28},{21,1},{... | collective-permute-start | bytes 1572872 | tf_op jit(solution)/shard_map/ppermute | solution.py:663
  131.4 22.9 %collective-permute-start.12 = (bf16[2,256,512]{2,1,0:T(8,128)(2,1)S(1)}, bf16[2,256,512]{2,1,0:T(8,128)(2,1)S(1)}, u32[]{:S(2)}, u32[]{:S(2)}) collective-permute-start(bf16[2,256,512]{2,1,0:T(8,128)(2,1)S(1)} %get-tuple-element.33.own), channel_id=1, source_target_pairs={{16,8},{20,12},{8,16},{12,20},{17,9},{21,13},{9,17},{13,21},{18,10... | collective-permute-start | bytes 1572872 | tf_op jit(solution)/shard_map/ppermute | solution.py:663

commit v11 on v8

--- a/solution.py
+++ b/solution.py
@@ -255,34 +255,46 @@
 
 
 class Layers:
-    def __init__(self, info, x_parts, y_parts, row_blocks, held, weights, sems, csems):
-        self.info, self.order = info, held.shape[2]
+    def __init__(self, info, x_parts, y_parts, row_blocks, held_x, held_y, weights, sems, csems):
+        self.info, self.order = info, held_y.shape[1]
         self.x_parts, self.y_parts, self.row_blocks = x_parts, y_parts, row_blocks
-        self.held, self.weights, self.sems, self.csems = held, weights, sems, csems
+        self.held_x, self.held_y, self.weights = held_x, held_y, weights
+        self.sems, self.csems = sems, csems
 
     def half_rows(self, far):
         height = self.order // 2
         return pl.ds(pl.multiple_of(self.info[info_half + far] * height, height), height)
 
-    def factor_copies(self, slot, which, parts):
+    def y_copies(self, slot, parts):
         return [
             pltpu.make_async_copy(
                 part.at[plane],
-                self.held.at[
-                    slot, which, self.half_rows(far), pl.ds(plane * self.order, self.order)
-                ],
-                self.sems.at[slot, which, far, plane],
+                self.held_y.at[slot, self.half_rows(far), pl.ds(plane * self.order, self.order)],
+                self.sems.at[slot, far, plane],
             )
             for far, part in enumerate(parts)
             for plane in range(2)
         ]
 
-    def y_copies(self, slot):
+    def x_copies(self, slot, part):
+        height = self.order // 2
+        copies = []
+        for far in range(2):
+            start = self.info[info_half + far] * height
+            for index, (plane, lower, right) in enumerate(((0, 0, 0), (1, 0, 1), (1, 1, 0), (0, 1, 1))):
+                rows = pl.ds(pl.multiple_of(lower * self.order + start, height), height)
+                copies.append(
+                    pltpu.make_async_copy(
+                        part.at[far, plane],
+                        self.held_x.at[slot, rows, pl.ds(right * self.order, self.order)],
+                        self.sems.at[slot, far, 2 + index],
+                    )
+                )
+        return copies
+
+    def start_y(self, slot):
         turn = self.info[info_slot + slot]
-        return self.factor_copies(slot, 1, [part.at[turn] for part in self.y_parts])
-
-    def start_y(self, slot):
-        start_all(self.y_copies(slot))
+        start_all(self.y_copies(slot, [part.at[turn] for part in self.y_parts]))
 
     def start_x(self, slot):
         own, first, second = self.x_parts
@@ -295,11 +307,15 @@
 
             @pl.when(hit)
             def _():
-                start_all(self.factor_copies(slot, 0, [part.at[0], part.at[1]]))
-
-    def ready(self, slot, which):
-        part = self.x_parts[0].at[0]
-        wait_all(self.factor_copies(slot, which, [part, part]))
+                start_all(self.x_copies(slot, part))
+
+    def ready_y(self, slot):
+        wait_all(self.y_copies(slot, [part.at[0] for part in self.y_parts]))
+
+    def ready_x(self, slot):
+        wait_all(self.x_copies(slot, self.x_parts[0]))
+        order = self.order
+        self.held_x[slot, :order, order:] = -self.held_x[slot, :order, order:]
 
     def weight_copies(self, slot):
         height = self.row_blocks[0].shape[1]
@@ -351,67 +367,49 @@
         wait_all(self.rhs_copies(slot, pieces[:2], rhs, sems))
         wait_all(self.weight_copies(slot))
 
-    def apply(self, slot, source, below, store, fresh):
+    def apply(self, slot, source, beside, below, store, fresh):
         order = self.order
         turned = (((1,), (1,)), ((), ()))
-        if 1 in fresh:
-            self.ready(slot, 1)
         for rows in row_chunks(order, 256):
+            further = slice(rows.start + order, rows.stop + order)
             real, imag = source(0, rows), source(1, rows)
-            upper = jnp.concatenate([real, -imag], axis=1)
-            lower = jnp.concatenate([imag, real], axis=1)
-            part = lax.dot_general(
-                jnp.concatenate([upper, lower], axis=0),
-                self.held[slot, 1],
-                turned,
-                preferred_element_type=f32,
-            ).astype(bf16)
-            height = rows.stop - rows.start
-            real, imag = part[:height], part[height:]
-            further = slice(rows.start + order, rows.stop + order)
-            below[rows, :order] = real
-            below[rows, order:] = imag
-            below[further, :order] = -imag
-            below[further, order:] = real
-        if 0 in fresh:
-            self.ready(slot, 0)
-        for plane in range(2):
-            for columns in row_chunks(order, 256):
-                along = slice(columns.start + plane * order, columns.stop + plane * order)
-                store(
-                    plane,
-                    columns,
-                    jnp.dot(self.held[slot, 0], below[:, along], preferred_element_type=f32),
-                )
+            beside[rows, :order] = real
+            beside[rows, order:] = -imag
+            beside[further, :order] = imag
+            beside[further, order:] = real
+        for columns in row_chunks(order, 256):
+            product = lax.dot_general(
+                beside[...], self.held_y[slot, columns], turned, preferred_element_type=f32
+            )
+            below[:, columns] = product.astype(bf16)
+        if fresh:
+            self.ready_x(slot)
+        for columns in row_chunks(order, 256):
+            product = jnp.dot(self.held_x[slot], below[:, columns], preferred_element_type=f32)
+            store(0, columns, product[:order])
+            store(1, columns, product[order:])
 
 
 def reduced(rhs, info, slot, weights, incoming):
     def source(plane, rows):
-        values = rhs[slot, plane, rows].astype(f32)
+        values = rhs[slot, plane, rows]
         if plane == 0:
             row = lax.broadcasted_iota(jnp.int32, values.shape, 0) + rows.start
-            column = lax.broadcasted_iota(jnp.int32, (1, values.shape[1]), 1)
-            hit = (column == info[2]) & (info[0] == slot)
-            cell = jnp.where(hit, f32(source_amplitude), f32(0.0))
-            values = values + jnp.where(row == info[1], cell, f32(0.0))
-        scaled = weights[slot, rows].astype(f32) * incoming(plane, rows)
-        return (values - scaled).astype(bf16)
+            column = lax.broadcasted_iota(jnp.int32, values.shape, 1)
+            hit = (row == info[1]) & (column == info[2]) & (info[0] == slot)
+            values = values + jnp.where(hit, f32(source_amplitude), f32(0.0)).astype(bf16)
+        return values - weights[slot, rows] * incoming(plane, rows)
 
     return source
 
 
 def sent(weights, slot, field):
-    def source(plane, rows):
-        scaled = weights[slot, rows].astype(f32) * field[plane, rows].astype(f32)
-        return scaled.astype(bf16)
-
-    return source
+    return lambda plane, rows: weights[slot, rows] * field[plane, rows]
 
 
 def subtract_into(target, forward):
     def store(plane, columns, values):
-        solved = values.astype(bf16).astype(f32)
-        target[plane, :, columns] = (forward[plane, :, columns].astype(f32) - solved).astype(bf16)
+        target[plane, :, columns] = forward[plane, :, columns] - values.astype(bf16)
 
     return store
 
@@ -424,39 +422,41 @@
 
 
 def first_kernel(info, xb, x0, x1, yb, yf, c0, c1, c2, c3, own, p0, p1, p2, p3, w_low, w_high,
-                 held, weights, rhs, below, sems, csems, fsems):
+                 held_x, held_y, weights, rhs, beside, below, sems, csems, fsems):
     @pl.when(info[info_member] == 0)
     def _():
-        layers = Layers(info, (xb, x0, x1), (yb, yf), (c0, c1, c2, c3), held, weights, fsems, csems)
+        layers = Layers(info, (xb, x0, x1), (yb, yf), (c0, c1, c2, c3), held_x, held_y, weights, fsems, csems)
         fields = (own, (p0, p1, p2, p3), rhs, sems)
         layers.start(0, *fields)
         layers.wait(0, *fields)
-        layers.ready(0, 1)
+        layers.ready_y(0)
         layers.start(1, *fields)
-        zero = reduced(rhs, info, 0, weights, lambda plane, rows: f32(0.0))
-        layers.apply(0, zero, below, round_into(w_low), (0,))
+        zero = reduced(rhs, info, 0, weights, lambda plane, rows: bf16(0.0))
+        layers.apply(0, zero, beside, below, round_into(w_low), True)
         layers.wait(1, *fields)
-        one = reduced(rhs, info, 1, weights, lambda plane, rows: w_low[plane, rows].astype(f32))
-        layers.apply(1, one, below, round_into(w_high), (0, 1))
+        one = reduced(rhs, info, 1, weights, lambda plane, rows: w_low[plane, rows])
+        layers.ready_y(1)
+        layers.apply(1, one, beside, below, round_into(w_high), True)
 
 
 def last_kernel(info, xb, x0, x1, yb, yf, c0, c1, c2, c3, own, p0, p1, p2, p3, arrived, field, back,
-                held, weights, rhs, forward, below, sems, csems, fsems):
+                held_x, held_y, weights, rhs, forward, beside, below, sems, csems, fsems):
     @pl.when(info[info_member] == 1)
     def _():
-        layers = Layers(info, (xb, x0, x1), (yb, yf), (c0, c1, c2, c3), held, weights, fsems, csems)
+        layers = Layers(info, (xb, x0, x1), (yb, yf), (c0, c1, c2, c3), held_x, held_y, weights, fsems, csems)
         fields = (own, (p0, p1, p2, p3), rhs, sems)
         layers.start(0, *fields)
         layers.wait(0, *fields)
-        layers.ready(0, 1)
+        layers.ready_y(0)
         layers.start(1, *fields)
         low, high = field.at[0], field.at[1]
-        two = reduced(rhs, info, 0, weights, lambda plane, rows: arrived[plane, rows].astype(f32))
-        layers.apply(0, two, below, round_into(forward), (0,))
+        two = reduced(rhs, info, 0, weights, lambda plane, rows: arrived[plane, rows])
+        layers.apply(0, two, beside, below, round_into(forward), True)
         layers.wait(1, *fields)
-        three = reduced(rhs, info, 1, weights, lambda plane, rows: forward[plane, rows].astype(f32))
-        layers.apply(1, three, below, round_into(high), (0, 1))
-        layers.apply(0, sent(weights, 1, high), below, subtract_into(low, forward), ())
+        three = reduced(rhs, info, 1, weights, lambda plane, rows: forward[plane, rows])
+        layers.ready_y(1)
+        layers.apply(1, three, beside, below, round_into(high), True)
+        layers.apply(0, sent(weights, 1, high), beside, below, subtract_into(low, forward), False)
         last = sent(weights, 0, low)
         for plane in range(2):
             for rows in row_chunks(weights.shape[1], 256):
@@ -464,7 +464,7 @@
 
 
 def back_kernel(info, xb, x0, x1, yb, yf, c0, c1, c2, c3, w_low, w_high, arrived, field,
-                p0, p1, p2, p3, held, weights, kept, below, csems, fsems, osems):
+                p0, p1, p2, p3, held_x, held_y, weights, kept, beside, below, csems, fsems, osems):
     def start_pieces(source, slot):
         for index, piece in enumerate((p0, p1, p2, p3)):
             height = piece.shape[1]
@@ -477,21 +477,22 @@
 
     @pl.when(info[info_member] == 0)
     def _():
-        layers = Layers(info, (xb, x0, x1), (yb, yf), (c0, c1, c2, c3), held, weights, fsems, csems)
+        layers = Layers(info, (xb, x0, x1), (yb, yf), (c0, c1, c2, c3), held_x, held_y, weights, fsems, csems)
         layers.start_y(1)
         layers.start_x(1)
-        layers.ready(1, 1)
+        layers.ready_y(1)
         high_rows = layers.weight_copies(1)
         start_all(high_rows)
         layers.start_y(0)
         layers.start_x(0)
         low, high = kept.at[0], kept.at[1]
         layers.apply(
-            1, lambda plane, rows: arrived[plane, rows], below, subtract_into(high, w_high), (0,)
+            1, lambda plane, rows: arrived[plane, rows], beside, below, subtract_into(high, w_high), True
         )
         start_pieces(kept, 1)
         wait_all(high_rows)
-        layers.apply(0, sent(weights, 1, high), below, subtract_into(low, w_low), (0, 1))
+        layers.ready_y(0)
+        layers.apply(0, sent(weights, 1, high), beside, below, subtract_into(low, w_low), True)
         start_pieces(kept, 0)
 
     @pl.when(info[info_member] != 0)
@@ -610,11 +611,13 @@
     factors = [x_both, *x_across, y_both, y_far, rows_held, rows_next, rows_far, over_z(rows_next, 2)]
 
     full_shape = jax.ShapeDtypeStruct((2, order, order), bf16)
-    factor_scratch = pltpu.VMEM((2, 2, order, 2 * order), bf16)
+    x_scratch = pltpu.VMEM((2, 2 * order, 2 * order), bf16)
+    y_scratch = pltpu.VMEM((2, order, 2 * order), bf16)
+    beside_scratch = pltpu.VMEM((2 * order, 2 * order), bf16)
     weight_scratch = pltpu.VMEM((2, order, order), bf16)
     field_scratch = pltpu.VMEM((2, 2, order, order), bf16)
-    below_scratch = pltpu.VMEM((2 * order, 2 * order), bf16)
-    factor_sems = pltpu.SemaphoreType.DMA((2, 2, 2, 2))
+    below_scratch = pltpu.VMEM((2 * order, order), bf16)
+    factor_sems = pltpu.SemaphoreType.DMA((2, 2, 6))
     weight_sems = pltpu.SemaphoreType.DMA((2, py_count, 2))
     field_sems = pltpu.SemaphoreType.DMA((2, 2, 2))
     solve_flops = 16 * order**3
@@ -631,9 +634,11 @@
         in_specs=[in_smem] + [anywhere] * 14,
         out_specs=[in_vmem] * 2,
         scratch_shapes=[
-            factor_scratch,
+            x_scratch,
+            y_scratch,
             weight_scratch,
             field_scratch,
+            beside_scratch,
             below_scratch,
             field_sems,
             weight_sems,
@@ -651,10 +656,12 @@
         in_specs=[in_smem] + [anywhere] * 14 + [in_vmem],
         out_specs=[in_vmem] * 2,
         scratch_shapes=[
-            factor_scratch,
+            x_scratch,
+            y_scratch,
             weight_scratch,
             field_scratch,
             pltpu.VMEM((2, order, order), bf16),
+            beside_scratch,
             below_scratch,
             field_sems,
             weight_sems,
@@ -672,9 +679,11 @@
         in_specs=[in_smem] + [anywhere] * 9 + [in_vmem] * 3 + [anywhere],
         out_specs=[anywhere] * len(rounds),
         scratch_shapes=[
-            factor_scratch,
+            x_scratch,
+            y_scratch,
             weight_scratch,
             field_scratch,
+            beside_scratch,
             below_scratch,
             weight_sems,
             factor_sems,
@@ -690,7 +699,7 @@
         unpack_kernel,
         out_shape=jax.ShapeDtypeStruct(field.shape, bf16),
         in_specs=[in_smem] + [anywhere] * (len(rounds) + 1),
-        out_specs=anywhere,
+        out_specs=in_vmem,
         scratch_shapes=[pltpu.SemaphoreType.DMA((len(rounds),))],
         compiler_params=params,
     )(sends_to, results[0], *received)

time: 150 us -> 151 us (level)
  no operation moved by 1% of the time
where the time goes in v11:
time: 151 us; the launch traced here: 150 us
  waiting for transfers between devices  83.2 us (55%)
  starting transfers between devices  40.8 us (27%)
  Pallas kernels  20.2 us (13%)
  between operations  3.09 us (2%)
  local copies, waits for them, and re-layouts  1.88 us (1%)
    ppermute x3, waiting for transfers between devices, over_z(): return lax.ppermute(block, 'py', [(z, z ^ bit) for z in range(py_count)])  23.7 us
    ppermute x4, waiting for transfers between devices, on_device(): lax.ppermute(piece, ('sec', 'px'), back_pairs(a, b))  19.5 us
    ppermute x4, waiting for transfers between devices, on_device(): lax.ppermute(piece, ('sec', 'px'), pairs(a, b))  19.4 us
    ppermute x4, starting transfers between devices, on_device(): lax.ppermute(piece, ('sec', 'px'), back_pairs(a, b))  12.6 us
    pallas_call x1, Pallas kernels, on_device(): pl.pallas_call(last_kernel, out_shape=[jax.ShapeDtypeStruct((2, 2, order,...  10.9 us
    ppermute x1, waiting for transfers between devices, on_device(): incoming = lax.ppermute(w_high, 'sec', up)  9.88 us
    ppermute x2, waiting for transfers between devices, aside(): return lax.ppermute(block, 'px', [(y, (y + 1) % 2) for y in range(2)])  7.6 us
    ppermute x4, starting transfers between devices, on_device(): lax.ppermute(piece, ('sec', 'px'), pairs(a, b))  6.94 us
  transfers between devices with their start and end apart: 20, of which 13 were waited for; matrix products, arithmetic and copies ran while one was open for 1% of the time, Pallas kernels for 2%

profile of v11, /device:TPU:1, one launch (start us, length us, event | category | flops | bytes accessed | tf_op | source)
XLA Modules:
  0.0 150.3 jit_solution(904853927728195919)
XLA Ops:
  0.0 1.1 pad_maximum_fusion
  1.1 1.1 broadcast_in_dim.4
  2.2 5.6 %all-to-all-start = ((bf16[4,4,64,512]{3,2,1,0:T(8,128)(2,1)}), bf16[4,4,64,512]{3,2,1,0:T(8,128)(2,1)S(1)}, u32[]{:S(2)}, u32[]{:S(2)}) async-start(bf16[4,4,64,512]{3,2,1,0:T(8,128)(2,1)} %broadcast_in_dim.4), calls=%async_computation | async-start | bytes 2097152 | tf_op jit(solution)/shard_map/all_to_all | solution.py:572
  7.9 2.6 %shard_map.55 = (bf16[576,512]{1,0:T(8,128)(2,1)}, bf16[576,512]{1,0:T(8,128)(2,1)}, bf16[576,512]{1,0:T(8,128)(2,1)}, bf16[576,512]{1,0:T(8,128)(2,1)}) custom-call(s32[6]{0:T(128)S(1)} %stack.83.place, bf16[2,256,2048]{2,1,0:T(8,128)(2,1)S(1)} %bitcast.28, bf16[256,512]{1,0:T(8,128)(2,1)S(1)} %bitcast.29), custom_call_target="tpu_custom_call" | custom-call | tf_op jit(solution)/shard_map/pallas_call | solution.py:558
  10.5 3.1 %collective-permute-start.1 = (bf16[576,512]{1,0:T(8,128)(2,1)}, bf16[576,512]{1,0:T(8,128)(2,1)S(1)}, u32[]{:S(2)}, u32[]{:S(2)}) collective-permute-start(bf16[576,512]{1,0:T(8,128)(2,1)} %get-tuple-element.23), channel_id=1, source_target_pairs={{0,4},{4,0},{8,20},{12,16},{16,12},{20,8},{24,28},{28,24},{1,5},{5... | collective-permute-start | bytes 1769480 | tf_op jit(solution)/shard_map/ppermute | solution.py:570
  14.1 3.3 %collective-permute-start = (bf16[576,512]{1,0:T(8,128)(2,1)}, bf16[576,512]{1,0:T(8,128)(2,1)S(1)}, u32[]{:S(2)}, u32[]{:S(2)}) collective-permute-start(bf16[576,512]{1,0:T(8,128)(2,1)} %get-tuple-element.22.own), channel_id=1, source_target_pairs={{8,16},{12,20},{16,8},{20,12},{9,17},{13,21},{17,9},{21,13},{10,18... | collective-permute-start | bytes 1769480 | tf_op jit(solution)/shard_map/ppermute | solution.py:570
  20.9 5.8 %collective-permute-done.1.p1 = bf16[576,512]{1,0:T(8,128)(2,1)S(1)} collective-permute-done((bf16[576,512]{1,0:T(8,128)(2,1)}, bf16[576,512]{1,0:T(8,128)(2,1)S(1)}, u32[]{:S(2)}, u32[]{:S(2)}) %collective-permute-start.1) | collective-permute-done | bytes 589856 | tf_op jit(solution)/shard_map/ppermute | solution.py:570
  26.7 2.4 %collective-permute-done.2.p2 = bf16[576,512]{1,0:T(8,128)(2,1)S(1)} collective-permute-done((bf16[576,512]{1,0:T(8,128)(2,1)}, bf16[576,512]{1,0:T(8,128)(2,1)S(1)}, u32[]{:S(2)}, u32[]{:S(2)}) %collective-permute-start.2) | collective-permute-done | bytes 589856 | tf_op jit(solution)/shard_map/ppermute | solution.py:570
  29.1 11.2 %collective-permute-done.3.p3 = bf16[576,512]{1,0:T(8,128)(2,1)S(1)} collective-permute-done((bf16[576,512]{1,0:T(8,128)(2,1)}, bf16[576,512]{1,0:T(8,128)(2,1)S(1)}, u32[]{:S(2)}, u32[]{:S(2)}) %collective-permute-start.3) | collective-permute-done | bytes 589856 | tf_op jit(solution)/shard_map/ppermute | solution.py:570
  40.3 1.7 %shard_map.56 = (bf16[2,256,512]{2,1,0:T(8,128)(2,1)S(1)}, bf16[2,256,512]{2,1,0:T(8,128)(2,1)S(1)}, bf16[4,64,512]{2,1,0:T(8,128)(2,1)S(1)}) custom-call(s32[21]{0:T(128)S(1)} %stack.98.info, bf16[4,4,64,512]{3,2,1,0:T(8,128)(2,1)S(1)} %all-to-all-done.blocks, bf16[576,512]{1,0:T(8,128)(2,1)} %get-tuple-element.22.own, ...), custom_call_target="tpu_custom_call" | custom-call | tf_op jit(solution)/shard_map/pallas_call | solution.py:576
  42.0 0.9 collective-permute-start.4
  43.0 4.2 %collective-permute-start.5 = (bf16[2,256,512]{2,1,0:T(8,128)(2,1)S(1)}, bf16[2,256,512]{2,1,0:T(8,128)(2,1)S(1)}, u32[]{:S(2)}, u32[]{:S(2)}) collective-permute-start(bf16[2,256,512]{2,1,0:T(8,128)(2,1)S(1)} %get-tuple-element.27.y_column), channel_id=1, source_target_pairs={{8,16},{12,20},{16,8},{20,12},{9,17},{13,21},{17,9},{21,13},{10,18... | collective-permute-start | bytes 1572872 | tf_op jit(solution)/shard_map/ppermute | solution.py:589
  47.1 2.7 %collective-permute-start.8 = (bf16[4,64,512]{2,1,0:T(8,128)(2,1)S(1)}, bf16[4,64,512]{2,1,0:T(8,128)(2,1)S(1)}, u32[]{:S(2)}, u32[]{:S(2)}) collective-permute-start(bf16[4,64,512]{2,1,0:T(8,128)(2,1)S(1)} %get-tuple-element.28.c0), channel_id=1, source_target_pairs={{0,2},{1,3},{2,0},{3,1},{4,6},{5,7},{6,4},{7,5},{8,10},{9,11},{10,... | collective-permute-start | bytes 786440 | tf_op jit(solution)/shard_map/ppermute | solution.py:595
  49.8 1.2 collective-permute-start.7
  51.0 10.5 %collective-permute-done.8.rows_far.c2 = bf16[4,64,512]{2,1,0:T(8,128)(2,1)S(1)} collective-permute-done((bf16[4,64,512]{2,1,0:T(8,128)(2,1)S(1)}, bf16[4,64,512]{2,1,0:T(8,128)(2,1)S(1)}, u32[]{:S(2)}, u32[]{:S(2)}) %collective-permute-start.8) | collective-permute-done | bytes 262176 | tf_op jit(solution)/shard_map/ppermute | solution.py:595
  63.8 1.9 %collective-permute-start.9 = (bf16[2,2,256,512]{3,2,1,0:T(8,128)(2,1)S(1)}, bf16[2,2,256,512]{3,2,1,0:T(8,128)(2,1)S(1)}, u32[]{:S(2)}, u32[]{:S(2)}) collective-permute-start(bf16[2,2,256,512]{3,2,1,0:T(8,128)(2,1)S(1)} %get-tuple-element.29.xb), channel_id=1, source_target_pairs={{8,16},{12,20},{16,8},{20,12},{9,17},{13,21},{17,9},{21,13},{10,18... | collective-permute-start | bytes 3145736 | tf_op jit(solution)/shard_map/ppermute | solution.py:589
  65.8 1.2 collective-permute-start.12
  67.0 12.7 %collective-permute-done.12.c3 = bf16[4,64,512]{2,1,0:T(8,128)(2,1)S(1)} collective-permute-done((bf16[4,64,512]{2,1,0:T(8,128)(2,1)S(1)}, bf16[4,64,512]{2,1,0:T(8,128)(2,1)S(1)}, u32[]{:S(2)}, u32[]{:S(2)}) %collective-permute-start.12) | collective-permute-done | bytes 262176 | tf_op jit(solution)/shard_map/ppermute | solution.py:595
  79.6 7.6 %collective-permute-done.11.yf = bf16[2,2,256,512]{3,2,1,0:T(8,128)(2,1)S(1)} collective-permute-done((bf16[2,2,256,512]{3,2,1,0:T(8,128)(2,1)S(1)}, bf16[2,2,256,512]{3,2,1,0:T(8,128)(2,1)S(1)}, u32[]{:S(2)}, u32[]{:S(2)}) %collective-permute-start.11) | collective-permute-done | bytes 1048608 | tf_op jit(solution)/shard_map/ppermute | solution.py:592
  88.1 1.0 shard_map.58
  89.1 1.3 collective-permute-start.13
  90.4 9.9 %collective-permute-done.13.arrived = bf16[2,512,512]{2,1,0:T(8,128)(2,1)S(1)} collective-permute-done((bf16[2,512,512]{2,1,0:T(8,128)(2,1)S(1)}, bf16[2,512,512]{2,1,0:T(8,128)(2,1)S(1)}, u32[]{:S(2)}, u32[]{:S(2)}) %collective-permute-start.13) | collective-permute-done | bytes 1048608 | tf_op jit(solution)/shard_map/ppermute | solution.py:652
  100.2 10.9 %shard_map.59 = (bf16[2,2,512,512]{3,2,1,0:T(8,128)(2,1)S(1)}, bf16[2,512,512]{2,1,0:T(8,128)(2,1)S(1)}) custom-call(s32[21]{0:T(128)S(1)} %stack.98.info, bf16[2,2,256,512]{3,2,1,0:T(8,128)(2,1)S(1)} %get-tuple-element.29.xb, bf16[2,2,256,512]{3,2,1,0:T(8,128)(2,1)S(1)} %collective-permute-done.9.x0, ...), custom_call_target="tpu_custom_call" | custom-call | flops 6442450944 | bytes 8388608 | tf_op jit(solution)/shard_map/pallas_call | solution.py:653
  111.1 1.4 collective-permute-start.14
  112.5 2.2 %collective-permute-done.14.arrived = bf16[2,512,512]{2,1,0:T(8,128)(2,1)S(1)} collective-permute-done((bf16[2,512,512]{2,1,0:T(8,128)(2,1)S(1)}, bf16[2,512,512]{2,1,0:T(8,128)(2,1)S(1)}, u32[]{:S(2)}, u32[]{:S(2)}) %collective-permute-start.14) | collective-permute-done | bytes 1048608 | tf_op jit(solution)/shard_map/ppermute | solution.py:675
  114.7 1.2 shard_map.60
  115.8 8.6 %collective-permute-start.16 = (bf16[2,256,512]{2,1,0:T(8,128)(2,1)S(1)}, bf16[2,256,512]{2,1,0:T(8,128)(2,1)S(1)}, u32[]{:S(2)}, u32[]{:S(2)}) collective-permute-start(bf16[2,256,512]{2,1,0:T(8,128)(2,1)S(1)} %get-tuple-element.36), channel_id=1, source_target_pairs={{4,0},{0,4},{20,8},{16,12},{12,16},{8,20},{28,24},{24,28},{5,1},{1... | collective-permute-start | bytes 1572872 | tf_op jit(solution)/shard_map/ppermute | solution.py:696
  124.5 3.9 %collective-permute-start.15 = (bf16[2,256,512]{2,1,0:T(8,128)(2,1)S(1)}, bf16[2,256,512]{2,1,0:T(8,128)(2,1)S(1)}, u32[]{:S(2)}, u32[]{:S(2)}) collective-permute-start(bf16[2,256,512]{2,1,0:T(8,128)(2,1)S(1)} %get-tuple-element.35.own), channel_id=1, source_target_pairs={{16,8},{20,12},{8,16},{12,20},{17,9},{21,13},{9,17},{13,21},{18,10... | collective-permute-start | bytes 1572872 | tf_op jit(solution)/shard_map/ppermute | solution.py:696
  128.4 2.9 %collective-permute-done.16.rest_1_ = bf16[2,256,512]{2,1,0:T(8,128)(2,1)S(1)} collective-permute-done((bf16[2,256,512]{2,1,0:T(8,128)(2,1)S(1)}, bf16[2,256,512]{2,1,0:T(8,128)(2,1)S(1)}, u32[]{:S(2)}, u32[]{:S(2)}) %collective-permute-start.16) | collective-permute-done | bytes 524320 | tf_op jit(solution)/shard_map/ppermute | solution.py:696
  131.4 4.8 %collective-permute-done.17.rest_2_ = bf16[2,256,512]{2,1,0:T(8,128)(2,1)S(1)} collective-permute-done((bf16[2,256,512]{2,1,0:T(8,128)(2,1)S(1)}, bf16[2,256,512]{2,1,0:T(8,128)(2,1)S(1)}, u32[]{:S(2)}, u32[]{:S(2)}) %collective-permute-start.17) | collective-permute-done | bytes 524320 | tf_op jit(solution)/shard_map/ppermute | solution.py:696
  136.2 11.7 %collective-permute-done.18.rest_3_ = bf16[2,256,512]{2,1,0:T(8,128)(2,1)S(1)} collective-permute-done((bf16[2,256,512]{2,1,0:T(8,128)(2,1)S(1)}, bf16[2,256,512]{2,1,0:T(8,128)(2,1)S(1)}, u32[]{:S(2)}, u32[]{:S(2)}) %collective-permute-start.18) | collective-permute-done | bytes 524320 | tf_op jit(solution)/shard_map/ppermute | solution.py:696
  147.9 2.2 %shard_map.61 = bf16[2,256,2048]{2,1,0:T(8,128)(2,1)} custom-call(s32[6]{0:T(128)S(1)} %stack.83.place, bf16[2,256,512]{2,1,0:T(8,128)(2,1)S(1)} %get-tuple-element.35.own, bf16[2,256,512]{2,1,0:T(8,128)(2,1)S(1)} %collective-permute-done.15.rest_0_, bf16[2,256,512]{2,1,0:T(8,128)(2,1)S(1)} %collective-permute-done.16.rest_1_, ...), custom_call_target="tpu_custom_call" | custom-call | tf_op jit(solution)/shard_map/pallas_call | solution.py:698
  (26 shorter events, 4.7 us)
Async XLA Ops:
  0.0 7.9 %copy-start.1 = (bf16[1,256,512]{2,1,0:T(8,128)(2,1)S(1)}, bf16[1,256,512]{2,1,0:T(8,128)(2,1)}, u32[]{:S(2)}) copy-start(bf16[1,256,512]{2,1,0:T(8,128)(2,1)} %param.7) | copy-start | bytes 786436
  0.0 7.9 %copy-start = (bf16[2,1,256,2048]{3,2,1,0:T(8,128)(2,1)S(1)}, bf16[2,1,256,2048]{3,2,1,0:T(8,128)(2,1)}, u32[]{:S(2)}) copy-start(bf16[2,1,256,2048]{3,2,1,0:T(8,128)(2,1)} %param.5) | copy-start | bytes 6291460
  2.2 15.3 %copy-start.2 = (s32[16]{0:T(128)S(1)}, s32[16]{0:T(128)}, u32[]{:S(2)}) copy-start(s32[16]{0:T(128)} %param.6) | copy-start | bytes 196
  2.2 38.1 %all-to-all-start = ((bf16[4,4,64,512]{3,2,1,0:T(8,128)(2,1)}), bf16[4,4,64,512]{3,2,1,0:T(8,128)(2,1)S(1)}, u32[]{:S(2)}, u32[]{:S(2)}) async-start(bf16[4,4,64,512]{3,2,1,0:T(8,128)(2,1)} %broadcast_in_dim.4), calls=%async_computation | async-start | bytes 2097152 | tf_op jit(solution)/shard_map/all_to_all | solution.py:572
  10.5 16.3 %collective-permute-start.1 = (bf16[576,512]{1,0:T(8,128)(2,1)}, bf16[576,512]{1,0:T(8,128)(2,1)S(1)}, u32[]{:S(2)}, u32[]{:S(2)}) collective-permute-start(bf16[576,512]{1,0:T(8,128)(2,1)} %get-tuple-element.23), channel_id=1, source_target_pairs={{0,4},{4,0},{8,20},{12,16},{16,12},{20,8},{24,28},{28,24},{1,5},{5... | collective-permute-start | bytes 1769480 | tf_op jit(solution)/shard_map/ppermute | solution.py:570
  13.5 15.6 %collective-permute-start.2 = (bf16[576,512]{1,0:T(8,128)(2,1)}, bf16[576,512]{1,0:T(8,128)(2,1)S(1)}, u32[]{:S(2)}, u32[]{:S(2)}) collective-permute-start(bf16[576,512]{1,0:T(8,128)(2,1)} %get-tuple-element.24), channel_id=1, source_target_pairs={{0,16},{4,20},{8,0},{12,4},{16,24},{20,28},{24,8},{28,12},{1,17},{... | collective-permute-start | bytes 1769480 | tf_op jit(solution)/shard_map/ppermute | solution.py:570
  13.5 26.8 %collective-permute-start.3 = (bf16[576,512]{1,0:T(8,128)(2,1)}, bf16[576,512]{1,0:T(8,128)(2,1)S(1)}, u32[]{:S(2)}, u32[]{:S(2)}) collective-permute-start(bf16[576,512]{1,0:T(8,128)(2,1)} %get-tuple-element.25), channel_id=1, source_target_pairs={{0,20},{4,16},{8,4},{12,0},{16,28},{20,24},{24,12},{28,8},{1,21},{... | collective-permute-start | bytes 1769480 | tf_op jit(solution)/shard_map/ppermute | solution.py:570
  14.1 26.2 %collective-permute-start = (bf16[576,512]{1,0:T(8,128)(2,1)}, bf16[576,512]{1,0:T(8,128)(2,1)S(1)}, u32[]{:S(2)}, u32[]{:S(2)}) collective-permute-start(bf16[576,512]{1,0:T(8,128)(2,1)} %get-tuple-element.22.own), channel_id=1, source_target_pairs={{8,16},{12,20},{16,8},{20,12},{9,17},{13,21},{17,9},{21,13},{10,18... | collective-permute-start | bytes 1769480 | tf_op jit(solution)/shard_map/ppermute | solution.py:570
  42.0 20.1 %collective-permute-start.4 = (bf16[2,256,512]{2,1,0:T(8,128)(2,1)S(1)}, bf16[2,256,512]{2,1,0:T(8,128)(2,1)S(1)}, u32[]{:S(2)}, u32[]{:S(2)}) collective-permute-start(bf16[2,256,512]{2,1,0:T(8,128)(2,1)S(1)} %get-tuple-element.26.x_column), channel_id=1, source_target_pairs={{0,4},{4,0},{1,5},{5,1},{2,6},{6,2},{3,7},{7,3},{8,12},{12,8},{9,1... | collective-permute-start | bytes 1572872 | tf_op jit(solution)/shard_map/ppermute | solution.py:592
  43.0 19.1 %collective-permute-start.6 = (bf16[2,256,512]{2,1,0:T(8,128)(2,1)S(1)}, bf16[2,256,512]{2,1,0:T(8,128)(2,1)S(1)}, u32[]{:S(2)}, u32[]{:S(2)}) collective-permute-start(bf16[2,256,512]{2,1,0:T(8,128)(2,1)S(1)} %get-tuple-element.27.y_column), channel_id=1, source_target_pairs={{0,16},{4,20},{8,0},{12,4},{16,24},{20,28},{24,8},{28,12},{1,17},{... | collective-permute-start | bytes 1572872 | tf_op jit(solution)/shard_map/ppermute | solution.py:589
  43.0 19.1 %collective-permute-start.5 = (bf16[2,256,512]{2,1,0:T(8,128)(2,1)S(1)}, bf16[2,256,512]{2,1,0:T(8,128)(2,1)S(1)}, u32[]{:S(2)}, u32[]{:S(2)}) collective-permute-start(bf16[2,256,512]{2,1,0:T(8,128)(2,1)S(1)} %get-tuple-element.27.y_column), channel_id=1, source_target_pairs={{8,16},{12,20},{16,8},{20,12},{9,17},{13,21},{17,9},{21,13},{10,18... | collective-permute-start | bytes 1572872 | tf_op jit(solution)/shard_map/ppermute | solution.py:589
  47.1 14.4 %collective-permute-start.8 = (bf16[4,64,512]{2,1,0:T(8,128)(2,1)S(1)}, bf16[4,64,512]{2,1,0:T(8,128)(2,1)S(1)}, u32[]{:S(2)}, u32[]{:S(2)}) collective-permute-start(bf16[4,64,512]{2,1,0:T(8,128)(2,1)S(1)} %get-tuple-element.28.c0), channel_id=1, source_target_pairs={{0,2},{1,3},{2,0},{3,1},{4,6},{5,7},{6,4},{7,5},{8,10},{9,11},{10,... | collective-permute-start | bytes 786440 | tf_op jit(solution)/shard_map/ppermute | solution.py:595
  49.8 12.2 %collective-permute-start.7 = (bf16[4,64,512]{2,1,0:T(8,128)(2,1)S(1)}, bf16[4,64,512]{2,1,0:T(8,128)(2,1)S(1)}, u32[]{:S(2)}, u32[]{:S(2)}) collective-permute-start(bf16[4,64,512]{2,1,0:T(8,128)(2,1)S(1)} %get-tuple-element.28.c0), channel_id=1, source_target_pairs={{0,1},{1,0},{2,3},{3,2},{4,5},{5,4},{6,7},{7,6},{8,9},{9,8},{10,11... | collective-permute-start | bytes 786440 | tf_op jit(solution)/shard_map/ppermute | solution.py:595
  62.8 24.4 %collective-permute-start.11 = (bf16[2,2,256,512]{3,2,1,0:T(8,128)(2,1)S(1)}, bf16[2,2,256,512]{3,2,1,0:T(8,128)(2,1)S(1)}, u32[]{:S(2)}, u32[]{:S(2)}) collective-permute-start(bf16[2,2,256,512]{3,2,1,0:T(8,128)(2,1)S(1)} %get-tuple-element.30.yb), channel_id=1, source_target_pairs={{0,4},{4,0},{1,5},{5,1},{2,6},{6,2},{3,7},{7,3},{8,12},{12,8},{9,1... | collective-permute-start | bytes 3145736 | tf_op jit(solution)/shard_map/ppermute | solution.py:592
  63.2 24.1 %collective-permute-start.10 = (bf16[2,2,256,512]{3,2,1,0:T(8,128)(2,1)S(1)}, bf16[2,2,256,512]{3,2,1,0:T(8,128)(2,1)S(1)}, u32[]{:S(2)}, u32[]{:S(2)}) collective-permute-start(bf16[2,2,256,512]{3,2,1,0:T(8,128)(2,1)S(1)} %get-tuple-element.29.xb), channel_id=1, source_target_pairs={{0,16},{4,20},{8,0},{12,4},{16,24},{20,28},{24,8},{28,12},{1,17},{... | collective-permute-start | bytes 3145736 | tf_op jit(solution)/shard_map/ppermute | solution.py:589
  63.8 24.2 %collective-permute-start.9 = (bf16[2,2,256,512]{3,2,1,0:T(8,128)(2,1)S(1)}, bf16[2,2,256,512]{3,2,1,0:T(8,128)(2,1)S(1)}, u32[]{:S(2)}, u32[]{:S(2)}) collective-permute-start(bf16[2,2,256,512]{3,2,1,0:T(8,128)(2,1)S(1)} %get-tuple-element.29.xb), channel_id=1, source_target_pairs={{8,16},{12,20},{16,8},{20,12},{9,17},{13,21},{17,9},{21,13},{10,18... | collective-permute-start | bytes 3145736 | tf_op jit(solution)/shard_map/ppermute | solution.py:589
  65.8 13.9 %collective-permute-start.12 = (bf16[4,64,512]{2,1,0:T(8,128)(2,1)S(1)}, bf16[4,64,512]{2,1,0:T(8,128)(2,1)S(1)}, u32[]{:S(2)}, u32[]{:S(2)}) collective-permute-start(bf16[4,64,512]{2,1,0:T(8,128)(2,1)S(1)} %collective-permute-done.7.rows_next.c1), channel_id=1, source_target_pairs={{0,2},{1,3},{2,0},{3,1},{4,6},{5,7},{6,4},{7,5},{8,10},{9,11},{10,... | collective-permute-start | bytes 786440 | tf_op jit(solution)/shard_map/ppermute | solution.py:595
  89.1 11.2 %collective-permute-start.13 = (bf16[2,512,512]{2,1,0:T(8,128)(2,1)S(1)}, bf16[2,512,512]{2,1,0:T(8,128)(2,1)S(1)}, u32[]{:S(2)}, u32[]{:S(2)}) collective-permute-start(bf16[2,512,512]{2,1,0:T(8,128)(2,1)S(1)} %get-tuple-element.32.w_high), channel_id=1, source_target_pairs={{0,8},{16,24},{1,9},{17,25},{2,10},{18,26},{3,11},{19,27},{4,12},{... | collective-permute-start | bytes 3145736 | tf_op jit(solution)/shard_map/ppermute | solution.py:652
  111.1 3.6 %collective-permute-start.14 = (bf16[2,512,512]{2,1,0:T(8,128)(2,1)S(1)}, bf16[2,512,512]{2,1,0:T(8,128)(2,1)S(1)}, u32[]{:S(2)}, u32[]{:S(2)}) collective-permute-start(bf16[2,512,512]{2,1,0:T(8,128)(2,1)S(1)} %get-tuple-element.33), channel_id=1, source_target_pairs={{8,0},{24,16},{9,1},{25,17},{10,2},{26,18},{11,3},{27,19},{12,4},{... | collective-permute-start | bytes 3145736 | tf_op jit(solution)/shard_map/ppermute | solution.py:675
  115.8 15.5 %collective-permute-start.16 = (bf16[2,256,512]{2,1,0:T(8,128)(2,1)S(1)}, bf16[2,256,512]{2,1,0:T(8,128)(2,1)S(1)}, u32[]{:S(2)}, u32[]{:S(2)}) collective-permute-start(bf16[2,256,512]{2,1,0:T(8,128)(2,1)S(1)} %get-tuple-element.36), channel_id=1, source_target_pairs={{4,0},{0,4},{20,8},{16,12},{12,16},{8,20},{28,24},{24,28},{5,1},{1... | collective-permute-start | bytes 1572872 | tf_op jit(solution)/shard_map/ppermute | solution.py:696
  124.4 11.8 %collective-permute-start.17 = (bf16[2,256,512]{2,1,0:T(8,128)(2,1)S(1)}, bf16[2,256,512]{2,1,0:T(8,128)(2,1)S(1)}, u32[]{:S(2)}, u32[]{:S(2)}) collective-permute-start(bf16[2,256,512]{2,1,0:T(8,128)(2,1)S(1)} %get-tuple-element.37), channel_id=1, source_target_pairs={{16,0},{20,4},{0,8},{4,12},{24,16},{28,20},{8,24},{12,28},{17,1},{... | collective-permute-start | bytes 1572872 | tf_op jit(solution)/shard_map/ppermute | solution.py:696
  124.4 23.5 %collective-permute-start.18 = (bf16[2,256,512]{2,1,0:T(8,128)(2,1)S(1)}, bf16[2,256,512]{2,1,0:T(8,128)(2,1)S(1)}, u32[]{:S(2)}, u32[]{:S(2)}) collective-permute-start(bf16[2,256,512]{2,1,0:T(8,128)(2,1)S(1)} %get-tuple-element.38), channel_id=1, source_target_pairs={{20,0},{16,4},{4,8},{0,12},{28,16},{24,20},{12,24},{8,28},{21,1},{... | collective-permute-start | bytes 1572872 | tf_op jit(solution)/shard_map/ppermute | solution.py:696
  124.5 23.4 %collective-permute-start.15 = (bf16[2,256,512]{2,1,0:T(8,128)(2,1)S(1)}, bf16[2,256,512]{2,1,0:T(8,128)(2,1)S(1)}, u32[]{:S(2)}, u32[]{:S(2)}) collective-permute-start(bf16[2,256,512]{2,1,0:T(8,128)(2,1)S(1)} %get-tuple-element.35.own), channel_id=1, source_target_pairs={{16,8},{20,12},{8,16},{12,20},{17,9},{21,13},{9,17},{13,21},{18,10... | collective-permute-start | bytes 1572872 | tf_op jit(solution)/shard_map/ppermute | solution.py:696

commit v12 on v11

--- a/solution.py
+++ b/solution.py
@@ -222,14 +222,14 @@
 
 
 def column_kernel(info, blocks, own, p0, p1, p2, p3, x_column, y_column, rows_held, sems, csems):
-    count, planes, height, order = blocks.shape
+    count, factors, height, width = blocks.shape
     copies = []
     for index in range(count):
         for which, column in enumerate((x_column, y_column)):
             copies.append(
                 pltpu.make_async_copy(
-                    blocks.at[index, pl.ds(2 * which, 2)],
-                    column.at[:, pl.ds(index * height, height), :],
+                    blocks.at[index, which],
+                    column.at[pl.ds(index * height, height)],
                     sems.at[index, which],
                 )
             )
@@ -243,7 +243,43 @@
     wait_all(copies)
 
 
-def both_kernel(info, x_column, x_aside, y_column, y0, y1, rows_next, rows_far, x_both, y_both, sems):
+def field_kernel(info, own, p0, p1, p2, p3, rhs, sems):
+    height = rhs.shape[2] // 2
+    copies = []
+    for index, piece in enumerate((p0, p1, p2, p3)):
+        slot, half = info[info_piece + 2 * index], info[info_piece + 2 * index + 1]
+        rows = pl.ds(pl.multiple_of(half * height, height), height)
+        for plane in range(2):
+            part = pl.ds(plane * height, height)
+            ends = (rhs.at[slot, plane, rows, :], sems.at[index, plane])
+            if index:
+                copies.append(pltpu.make_async_copy(piece.at[part], *ends))
+            else:
+                copies.append(Either(info[info_self], own.at[part], piece.at[part], *ends))
+    start_all(copies)
+    wait_all(copies)
+
+
+def weight_kernel(info, c0, c1, c2, c3, weights, sems):
+    height = c0.shape[1]
+    half_height = weights.shape[1] // 2
+    copies = []
+    for index, block in enumerate((c0, c1, c2, c3)):
+        for turn in range(block.shape[0]):
+            slot, half = info[info_piece + 2 * turn], info[info_piece + 2 * turn + 1]
+            start = half * half_height + info[info_block + index] * height
+            rows = pl.ds(pl.multiple_of(start, height), height)
+            copies.append(
+                pltpu.make_async_copy(
+                    block.at[turn], weights.at[slot, rows, :], sems.at[index, turn]
+                )
+            )
+    start_all(copies)
+    wait_all(copies)
+
+
+def both_kernel(info, x_column, x_aside, y_column, y0, y1, rows_next, rows_far, rhs, x_both, y_both,
+                sems):
     copies = [
         pltpu.make_async_copy(x_column, x_both.at[0], sems.at[0]),
         pltpu.make_async_copy(x_aside, x_both.at[1], sems.at[1]),
@@ -255,48 +291,24 @@
 
 
 class Layers:
-    def __init__(self, info, x_parts, y_parts, row_blocks, held_x, held_y, weights, sems, csems):
-        self.info, self.order = info, held_y.shape[1]
-        self.x_parts, self.y_parts, self.row_blocks = x_parts, y_parts, row_blocks
-        self.held_x, self.held_y, self.weights = held_x, held_y, weights
-        self.sems, self.csems = sems, csems
-
-    def half_rows(self, far):
-        height = self.order // 2
-        return pl.ds(pl.multiple_of(self.info[info_half + far] * height, height), height)
-
-    def y_copies(self, slot, parts):
-        return [
-            pltpu.make_async_copy(
-                part.at[plane],
-                self.held_y.at[slot, self.half_rows(far), pl.ds(plane * self.order, self.order)],
-                self.sems.at[slot, far, plane],
-            )
-            for far, part in enumerate(parts)
-            for plane in range(2)
-        ]
+    def __init__(self, info, x_parts, y_parts, held, beside, below, sems):
+        self.info, self.order = info, held.shape[1]
+        self.x_parts, self.y_parts, self.held = x_parts, y_parts, held
+        self.beside, self.below, self.sems = beside, below, sems
 
     def x_copies(self, slot, part):
         height = self.order // 2
         copies = []
         for far in range(2):
-            start = self.info[info_half + far] * height
-            for index, (plane, lower, right) in enumerate(((0, 0, 0), (1, 0, 1), (1, 1, 0), (0, 1, 1))):
-                rows = pl.ds(pl.multiple_of(lower * self.order + start, height), height)
-                copies.append(
-                    pltpu.make_async_copy(
-                        part.at[far, plane],
-                        self.held_x.at[slot, rows, pl.ds(right * self.order, self.order)],
-                        self.sems.at[slot, far, 2 + index],
-                    )
+            rows = pl.ds(pl.multiple_of(self.info[info_half + far] * height, height), height)
+            copies.append(
+                pltpu.make_async_copy(
+                    part.at[far], self.held.at[slot, rows], self.sems.at[slot, far]
                 )
+            )
         return copies
 
-    def start_y(self, slot):
-        turn = self.info[info_slot + slot]
-        start_all(self.y_copies(slot, [part.at[turn] for part in self.y_parts]))
-
-    def start_x(self, slot):
+    def start(self, slot):
         own, first, second = self.x_parts
         turn, same = self.info[info_slot + slot], self.info[info_self]
         for hit, part in (
@@ -309,67 +321,10 @@
             def _():
                 start_all(self.x_copies(slot, part))
 
-    def ready_y(self, slot):
-        wait_all(self.y_copies(slot, [part.at[0] for part in self.y_parts]))
-
-    def ready_x(self, slot):
-        wait_all(self.x_copies(slot, self.x_parts[0]))
-        order = self.order
-        self.held_x[slot, :order, order:] = -self.held_x[slot, :order, order:]
-
-    def weight_copies(self, slot):
-        height = self.row_blocks[0].shape[1]
-        copies = []
-        for index, block in enumerate(self.row_blocks):
-            for far in range(2):
-                turn = 2 * self.info[info_slot + slot] + far
-                start = self.info[info_half + far] * (self.order // 2)
-                start = start + self.info[info_block + index] * height
-                rows = pl.ds(pl.multiple_of(start, height), height)
-                copies.append(
-                    pltpu.make_async_copy(
-                        block.at[turn], self.weights.at[slot, rows, :], self.csems.at[slot, index, far]
-                    )
-                )
-        return copies
-
-    def rhs_copies(self, slot, pair, rhs, sems):
-        height = self.order // 2
-        return [
-            pltpu.make_async_copy(
-                piece.at[pl.ds(plane * height, height)],
-                rhs.at[slot, plane, self.half_rows(far), :],
-                sems.at[slot, far, plane],
-            )
-            for far, piece in enumerate(pair)
-            for plane in range(2)
-        ]
-
-    def start_rhs(self, slot, own, pieces, rhs, sems):
-        turn, same = self.info[info_slot + slot], self.info[info_self]
-        for hit, pair in (
-            ((turn == 0) & (same != 0), (own, pieces[1])),
-            ((turn == 0) & (same == 0), pieces[:2]),
-            (turn == 1, pieces[2:]),
-        ):
-
-            @pl.when(hit)
-            def _():
-                start_all(self.rhs_copies(slot, pair, rhs, sems))
-
-    def start(self, slot, own, pieces, rhs, sems):
-        self.start_y(slot)
-        self.start_rhs(slot, own, pieces, rhs, sems)
-        start_all(self.weight_copies(slot))
-        self.start_x(slot)
-
-    def wait(self, slot, own, pieces, rhs, sems):
-        wait_all(self.rhs_copies(slot, pieces[:2], rhs, sems))
-        wait_all(self.weight_copies(slot))
-
-    def apply(self, slot, source, beside, below, store, fresh):
-        order = self.order
+    def apply(self, slot, source, store, fresh):
+        order, beside, below = self.order, self.beside, self.below
         turned = (((1,), (1,)), ((), ()))
+        turn = self.info[info_slot + slot]
         for rows in row_chunks(order, 256):
             further = slice(rows.start + order, rows.stop + order)
             real, imag = source(0, rows), source(1, rows)
@@ -377,17 +332,28 @@
             beside[rows, order:] = -imag
             beside[further, :order] = imag
             beside[further, order:] = real
-        for columns in row_chunks(order, 256):
+        height = order // 2
+        for far, part in enumerate(self.y_parts):
             product = lax.dot_general(
-                beside[...], self.held_y[slot, columns], turned, preferred_element_type=f32
-            )
-            below[:, columns] = product.astype(bf16)
+                beside[...], part[turn], turned, preferred_element_type=f32
+            ).astype(bf16)
+            start = self.info[info_half + far] * height
+            columns = pl.ds(pl.multiple_of(start, height), height)
+            beyond = pl.ds(pl.multiple_of(order + start, height), height)
+            below[:order, columns] = product[:order]
+            below[:order, beyond] = product[order:]
+            below[order:, columns] = -product[order:]
+            below[order:, beyond] = product[:order]
         if fresh:
-            self.ready_x(slot)
-        for columns in row_chunks(order, 256):
-            product = jnp.dot(self.held_x[slot], below[:, columns], preferred_element_type=f32)
-            store(0, columns, product[:order])
-            store(1, columns, product[order:])
+            wait_all(self.x_copies(slot, self.x_parts[0]))
+        for plane in range(2):
+            for columns in row_chunks(order, 256):
+                along = slice(columns.start + plane * order, columns.stop + plane * order)
+                store(
+                    plane,
+                    columns,
+                    jnp.dot(self.held[slot], below[:, along], preferred_element_type=f32),
+                )
 
 
 def reduced(rhs, info, slot, weights, incoming):
@@ -421,50 +387,39 @@
     return store
 
 
-def first_kernel(info, xb, x0, x1, yb, yf, c0, c1, c2, c3, own, p0, p1, p2, p3, w_low, w_high,
-                 held_x, held_y, weights, rhs, beside, below, sems, csems, fsems):
+def first_kernel(info, xb, x0, x1, yb, yf, weights, rhs, w_low, w_high, held, beside, below, sems):
     @pl.when(info[info_member] == 0)
     def _():
-        layers = Layers(info, (xb, x0, x1), (yb, yf), (c0, c1, c2, c3), held_x, held_y, weights, fsems, csems)
-        fields = (own, (p0, p1, p2, p3), rhs, sems)
-        layers.start(0, *fields)
-        layers.wait(0, *fields)
-        layers.ready_y(0)
-        layers.start(1, *fields)
+        layers = Layers(info, (xb, x0, x1), (yb, yf), held, beside, below, sems)
+        layers.start(0)
+        layers.start(1)
         zero = reduced(rhs, info, 0, weights, lambda plane, rows: bf16(0.0))
-        layers.apply(0, zero, beside, below, round_into(w_low), True)
-        layers.wait(1, *fields)
+        layers.apply(0, zero, round_into(w_low), True)
         one = reduced(rhs, info, 1, weights, lambda plane, rows: w_low[plane, rows])
-        layers.ready_y(1)
-        layers.apply(1, one, beside, below, round_into(w_high), True)
-
-
-def last_kernel(info, xb, x0, x1, yb, yf, c0, c1, c2, c3, own, p0, p1, p2, p3, arrived, field, back,
-                held_x, held_y, weights, rhs, forward, beside, below, sems, csems, fsems):
+        layers.apply(1, one, round_into(w_high), True)
+
+
+def last_kernel(info, xb, x0, x1, yb, yf, weights, rhs, arrived, field, back, forward, held, beside,
+                below, sems):
     @pl.when(info[info_member] == 1)
     def _():
-        layers = Layers(info, (xb, x0, x1), (yb, yf), (c0, c1, c2, c3), held_x, held_y, weights, fsems, csems)
-        fields = (own, (p0, p1, p2, p3), rhs, sems)
-        layers.start(0, *fields)
-        layers.wait(0, *fields)
-        layers.ready_y(0)
-        layers.start(1, *fields)
+        layers = Layers(info, (xb, x0, x1), (yb, yf), held, beside, below, sems)
+        layers.start(0)
+        layers.start(1)
         low, high = field.at[0], field.at[1]
         two = reduced(rhs, info, 0, weights, lambda plane, rows: arrived[plane, rows])
-        layers.apply(0, two, beside, below, round_into(forward), True)
-        layers.wait(1, *fields)
+        layers.apply(0, two, round_into(forward), True)
         three = reduced(rhs, info, 1, weights, lambda plane, rows: forward[plane, rows])
-        layers.ready_y(1)
-        layers.apply(1, three, beside, below, round_into(high), True)
-        layers.apply(0, sent(weights, 1, high), beside, below, subtract_into(low, forward), False)
+        layers.apply(1, three, round_into(high), True)
+        layers.apply(0, sent(weights, 1, high), subtract_into(low, forward), False)
         last = sent(weights, 0, low)
         for plane in range(2):
             for rows in row_chunks(weights.shape[1], 256):
                 back[plane, rows] = last(plane, rows)
 
 
-def back_kernel(info, xb, x0, x1, yb, yf, c0, c1, c2, c3, w_low, w_high, arrived, field,
-                p0, p1, p2, p3, held_x, held_y, weights, kept, beside, below, csems, fsems, osems):
+def back_kernel(info, xb, x0, x1, yb, yf, weights, w_low, w_high, arrived, field, p0, p1, p2, p3,
+                kept, held, beside, below, sems, osems):
     def start_pieces(source, slot):
         for index, piece in enumerate((p0, p1, p2, p3)):
             height = piece.shape[1]
@@ -477,22 +432,15 @@
 
     @pl.when(info[info_member] == 0)
     def _():
-        layers = Layers(info, (xb, x0, x1), (yb, yf), (c0, c1, c2, c3), held_x, held_y, weights, fsems, csems)
-        layers.start_y(1)
-        layers.start_x(1)
-        layers.ready_y(1)
-        high_rows = layers.weight_copies(1)
-        start_all(high_rows)
-        layers.start_y(0)
-        layers.start_x(0)
+        layers = Layers(info, (xb, x0, x1), (yb, yf), held, beside, below, sems)
+        layers.start(1)
+        layers.start(0)
         low, high = kept.at[0], kept.at[1]
         layers.apply(
-            1, lambda plane, rows: arrived[plane, rows], beside, below, subtract_into(high, w_high), True
+            1, lambda plane, rows: arrived[plane, rows], subtract_into(high, w_high), True
         )
         start_pieces(kept, 1)
-        wait_all(high_rows)
-        layers.ready_y(0)
-        layers.apply(0, sent(weights, 1, high), beside, below, subtract_into(low, w_low), True)
+        layers.apply(0, sent(weights, 1, high), subtract_into(low, w_low), True)
         start_pieces(kept, 0)
 
     @pl.when(info[info_member] != 0)
@@ -553,7 +501,9 @@
         + [own_y, group == member]
     ).astype(jnp.int32)
     piece_shape = jax.ShapeDtypeStruct((2, rows_here, order), bf16)
-    shard = jnp.concatenate([x_factor[0], y_factor[0]], axis=0)
+    shard = jnp.stack(
+        [jnp.concatenate([factor[0, 0], factor[0, 1]], axis=1) for factor in (x_factor, y_factor)]
+    )
     blocks = jnp.broadcast_to(shard[None], (py_count,) + shard.shape)
     packed = pl.pallas_call(
         pack_kernel,
@@ -571,7 +521,7 @@
     ]
     blocks = lax.all_to_all(blocks, "py", split_axis=0, concat_axis=0, tiled=True)
 
-    column_shape = jax.ShapeDtypeStruct((2, rows_here, order), bf16)
+    column_shape = jax.ShapeDtypeStruct((rows_here, 2 * order), bf16)
     rows_shape = jax.ShapeDtypeStruct((len(rounds), height, order), bf16)
     x_column, y_column, rows_held = pl.pallas_call(
         column_kernel,
@@ -598,100 +548,83 @@
     x_aside = aside(x_column)
     rows_next = over_z(rows_held, 1)
     rows_far = over_z(rows_held, 2)
+    full_shape = jax.ShapeDtypeStruct((2, order, order), bf16)
+    double_shape = jax.ShapeDtypeStruct((2, 2, order, order), bf16)
+    rhs = pl.pallas_call(
+        field_kernel,
+        out_shape=double_shape,
+        in_specs=[in_smem] + [anywhere] * 5,
+        out_specs=in_vmem,
+        scratch_shapes=[pltpu.SemaphoreType.DMA((len(rounds), 2))],
+        compiler_params=params,
+    )(info, packed[0], *pieces)
     x_both, y_both = pl.pallas_call(
         both_kernel,
         out_shape=[jax.ShapeDtypeStruct((2,) + column_shape.shape, bf16)] * 2,
-        in_specs=[in_smem] + [anywhere] * 7,
+        in_specs=[in_smem] + [anywhere] * 8,
         out_specs=[in_vmem] * 2,
         scratch_shapes=[pltpu.SemaphoreType.DMA((4,))],
         compiler_params=params,
-    )(info, x_column, x_aside, y_column, *y_near, rows_next, rows_far)
+    )(info, x_column, x_aside, y_column, *y_near, rows_next, rows_far, rhs)
     y_far = aside(y_both)
     x_across = [across(x_both, a) for a in range(2)]
-    factors = [x_both, *x_across, y_both, y_far, rows_held, rows_next, rows_far, over_z(rows_next, 2)]
-
-    full_shape = jax.ShapeDtypeStruct((2, order, order), bf16)
-    x_scratch = pltpu.VMEM((2, 2 * order, 2 * order), bf16)
-    y_scratch = pltpu.VMEM((2, order, 2 * order), bf16)
-    beside_scratch = pltpu.VMEM((2 * order, 2 * order), bf16)
-    weight_scratch = pltpu.VMEM((2, order, order), bf16)
-    field_scratch = pltpu.VMEM((2, 2, order, order), bf16)
-    below_scratch = pltpu.VMEM((2 * order, order), bf16)
-    factor_sems = pltpu.SemaphoreType.DMA((2, 2, 6))
-    weight_sems = pltpu.SemaphoreType.DMA((2, py_count, 2))
-    field_sems = pltpu.SemaphoreType.DMA((2, 2, 2))
-    solve_flops = 16 * order**3
-    fields = (packed[0], *pieces)
+    weights = pl.pallas_call(
+        weight_kernel,
+        out_shape=full_shape,
+        in_specs=[in_smem] + [anywhere] * 4,
+        out_specs=in_vmem,
+        scratch_shapes=[pltpu.SemaphoreType.DMA((4, len(rounds)))],
+        compiler_params=params,
+    )(info, rows_held, rows_next, rows_far, over_z(rows_next, 2))
+    layers = (info, x_both, *x_across, y_both, y_far, weights)
+    layer_specs = [in_smem] + [anywhere] * 3 + [in_vmem] * 3
+    solver_scratch = [
+        pltpu.VMEM((2, order, 2 * order), bf16),
+        pltpu.VMEM((2 * order, 2 * order), bf16),
+        pltpu.VMEM((2 * order, 2 * order), bf16),
+        pltpu.SemaphoreType.DMA((2, 2)),
+    ]
 
     def cost(solves):
         return pl.CostEstimate(
-            flops=solves * solve_flops, bytes_accessed=16 * order * order * 2, transcendentals=0
+            flops=solves * 16 * order**3, bytes_accessed=16 * order**2 * 2, transcendentals=0
         )
 
     w_low, w_high = pl.pallas_call(
         first_kernel,
         out_shape=[full_shape] * 2,
-        in_specs=[in_smem] + [anywhere] * 14,
+        in_specs=layer_specs + [in_vmem],
         out_specs=[in_vmem] * 2,
-        scratch_shapes=[
-            x_scratch,
-            y_scratch,
-            weight_scratch,
-            field_scratch,
-            beside_scratch,
-            below_scratch,
-            field_sems,
-            weight_sems,
-            factor_sems,
-        ],
+        scratch_shapes=solver_scratch,
         compiler_params=params,
         cost_estimate=cost(2),
-    )(info, *factors, *fields)
+    )(*layers, rhs)
 
     up = [(2 * x, 2 * x + 1) for x in range(groups)]
     incoming = lax.ppermute(w_high, "sec", up)
     solved, back = pl.pallas_call(
         last_kernel,
-        out_shape=[jax.ShapeDtypeStruct((2, 2, order, order), bf16), full_shape],
-        in_specs=[in_smem] + [anywhere] * 14 + [in_vmem],
+        out_shape=[double_shape, full_shape],
+        in_specs=layer_specs + [in_vmem] * 2,
         out_specs=[in_vmem] * 2,
-        scratch_shapes=[
-            x_scratch,
-            y_scratch,
-            weight_scratch,
-            field_scratch,
-            pltpu.VMEM((2, order, order), bf16),
-            beside_scratch,
-            below_scratch,
-            field_sems,
-            weight_sems,
-            factor_sems,
-        ],
+        scratch_shapes=[pltpu.VMEM((2, order, order), bf16)] + solver_scratch,
         compiler_params=params,
         cost_estimate=cost(3),
-    )(info, *factors, *fields, incoming)
+    )(*layers, rhs, incoming)
 
     down = [(target, source) for source, target in up]
     incoming = lax.ppermute(back, "sec", down)
     results = pl.pallas_call(
         back_kernel,
         out_shape=[piece_shape] * len(rounds),
-        in_specs=[in_smem] + [anywhere] * 9 + [in_vmem] * 3 + [anywhere],
+        in_specs=layer_specs + [in_vmem] * 3 + [anywhere],
         out_specs=[anywhere] * len(rounds),
-        scratch_shapes=[
-            x_scratch,
-            y_scratch,
-            weight_scratch,
-            field_scratch,
-            beside_scratch,
-            below_scratch,
-            weight_sems,
-            factor_sems,
-            pltpu.SemaphoreType.DMA((len(rounds),)),
-        ],
+        scratch_shapes=[pltpu.VMEM((2, 2, order, order), bf16)]
+        + solver_scratch
+        + [pltpu.SemaphoreType.DMA((len(rounds),))],
         compiler_params=params,
         cost_estimate=cost(2),
-    )(info, *factors, w_low, w_high, incoming, solved)
+    )(*layers, w_low, w_high, incoming, solved)
     received = [
         lax.ppermute(piece, ("sec", "px"), back_pairs(a, b)) for piece, (a, b) in zip(results, rounds)
     ]

time: 151 us -> 149 us (0.987)
  waiting for transfers between devices: 83.2 us -> 77.1 us
  local copies, waits for them, and re-layouts: 1.88 us -> 5.29 us
  Pallas kernels: 20.2 us -> 22.7 us
    ppermute x2, waiting for transfers between devices: 7.6 us -> 5.17 us  [aside(): return lax.ppermute(block, 'px', [(y, (y + 1) % 2) for y in range(2)])]
    pallas_call x2 -> x4, Pallas kernels: 11.8 us -> 13.7 us  [the longest x1 9.15 us: on_device(): pl.pallas_call(last_kernel, out_shape=[double_shape, full_shape], in_spec...]
    ppermute x1, waiting for transfers between devices: 9.88 us -> 8.03 us  [on_device(): incoming = lax.ppermute(w_high, 'sec', up)]
    squeeze x0 -> x2, local copies, waits for them, and re-layouts: none -> 1.76 us  [on_device(): factor[0, 0]]
    ppermute x3, waiting for transfers between devices: 23.7 us -> 22.1 us  [over_z(): return lax.ppermute(block, 'py', [(z, z ^ bit) for z in range(py_count)])]
    unnamed x6, local copies, waits for them, and re-layouts: 0.01 us -> 1.6 us
  transfers between devices with their start and end apart: 20 -> 20, of which waited for: 13 -> 13; matrix products, arithmetic and copies ran while one was open for 1% -> 1% of each run, Pallas kernels for 2% -> 4%
where the time goes in v12:
time: 149 us
  waiting for transfers between devices  77.1 us (52%)
  starting transfers between devices  40.5 us (27%)
  Pallas kernels  22.7 us (15%)
  local copies, waits for them, and re-layouts  5.29 us (4%)
  between operations  3.08 us (2%)
    ppermute x3, waiting for transfers between devices, over_z(): return lax.ppermute(block, 'py', [(z, z ^ bit) for z in range(py_count)])  22.1 us
    ppermute x4, waiting for transfers between devices, on_device(): lax.ppermute(piece, ('sec', 'px'), pairs(a, b))  19.4 us
    ppermute x4, waiting for transfers between devices, on_device(): lax.ppermute(piece, ('sec', 'px'), back_pairs(a, b))  19.3 us
    ppermute x4, starting transfers between devices, on_device(): lax.ppermute(piece, ('sec', 'px'), back_pairs(a, b))  12.2 us
    pallas_call x1, Pallas kernels, on_device(): pl.pallas_call(last_kernel, out_shape=[double_shape, full_shape], in_spec...  9.15 us
    ppermute x1, waiting for transfers between devices, on_device(): incoming = lax.ppermute(w_high, 'sec', up)  8.03 us
    ppermute x4, starting transfers between devices, on_device(): lax.ppermute(piece, ('sec', 'px'), pairs(a, b))  6.94 us
    ppermute x4, starting transfers between devices, across(): return lax.ppermute(block, ('sec', 'px'), pairs(a, 0))  6.77 us
  transfers between devices with their start and end apart: 20, of which 13 were waited for; matrix products, arithmetic and copies ran while one was open for 1% of the time, Pallas kernels for 4%

profile of v12, /device:TPU:1, one launch (start us, length us, event | category | flops | bytes accessed | tf_op | source)
XLA Modules:
  0.0 148.7 jit_solution(10229924202181288323)
XLA Ops:
  1.8 1.1 broadcast_in_dim.4
  2.9 5.6 %all-to-all-start = ((bf16[4,2,64,1024]{3,2,1,0:T(8,128)(2,1)}), bf16[4,2,64,1024]{3,2,1,0:T(8,128)(2,1)S(1)}, u32[]{:S(2)}, u32[]{:S(2)}) async-start(bf16[4,2,64,1024]{3,2,1,0:T(8,128)(2,1)} %broadcast_in_dim.4), calls=%async_computation | async-start | bytes 2097152 | tf_op jit(solution)/shard_map/all_to_all | solution.py:522
  8.6 1.6 %copy-done = bf16[2,1,256,2048]{3,2,1,0:T(8,128)(2,1)S(1)} copy-done((bf16[2,1,256,2048]{3,2,1,0:T(8,128)(2,1)S(1)}, bf16[2,1,256,2048]{3,2,1,0:T(8,128)(2,1)}, u32[]{:S(2)}) %copy-start) | copy-done | bytes 2097176
  10.2 2.4 %shard_map.55 = (bf16[576,512]{1,0:T(8,128)(2,1)S(1)}, bf16[576,512]{1,0:T(8,128)(2,1)}, bf16[576,512]{1,0:T(8,128)(2,1)}, bf16[576,512]{1,0:T(8,128)(2,1)}) custom-call(s32[6]{0:T(128)S(1)} %stack.92.place, bf16[2,256,2048]{2,1,0:T(8,128)(2,1)S(1)} %bitcast.38, bf16[256,512]{1,0:T(8,128)(2,1)S(1)} %bitcast.39), custom_call_target="tpu_custom_call" | custom-call | tf_op jit(solution)/shard_map/pallas_call | solution.py:508
  12.6 3.1 %collective-permute-start.1 = (bf16[576,512]{1,0:T(8,128)(2,1)}, bf16[576,512]{1,0:T(8,128)(2,1)S(1)}, u32[]{:S(2)}, u32[]{:S(2)}) collective-permute-start(bf16[576,512]{1,0:T(8,128)(2,1)} %get-tuple-element.23), channel_id=1, source_target_pairs={{0,4},{4,0},{8,20},{12,16},{16,12},{20,8},{24,28},{28,24},{1,5},{5... | collective-permute-start | bytes 1769480 | tf_op jit(solution)/shard_map/ppermute | solution.py:520
  16.2 3.3 %collective-permute-start = (bf16[576,512]{1,0:T(8,128)(2,1)S(1)}, bf16[576,512]{1,0:T(8,128)(2,1)}, u32[]{:S(2)}, u32[]{:S(2)}) collective-permute-start(bf16[576,512]{1,0:T(8,128)(2,1)S(1)} %get-tuple-element.22.own), channel_id=1, source_target_pairs={{8,16},{12,20},{16,8},{20,12},{9,17},{13,21},{17,9},{21,13},{10,18... | collective-permute-start | bytes 1769480 | tf_op jit(solution)/shard_map/ppermute | solution.py:520
  23.0 5.8 %collective-permute-done.1.p1 = bf16[576,512]{1,0:T(8,128)(2,1)S(1)} collective-permute-done((bf16[576,512]{1,0:T(8,128)(2,1)}, bf16[576,512]{1,0:T(8,128)(2,1)S(1)}, u32[]{:S(2)}, u32[]{:S(2)}) %collective-permute-start.1) | collective-permute-done | bytes 589856 | tf_op jit(solution)/shard_map/ppermute | solution.py:520
  28.8 2.4 %collective-permute-done.2.p2 = bf16[576,512]{1,0:T(8,128)(2,1)S(1)} collective-permute-done((bf16[576,512]{1,0:T(8,128)(2,1)}, bf16[576,512]{1,0:T(8,128)(2,1)S(1)}, u32[]{:S(2)}, u32[]{:S(2)}) %collective-permute-start.2) | collective-permute-done | bytes 589856 | tf_op jit(solution)/shard_map/ppermute | solution.py:520
  31.3 11.2 %collective-permute-done.3.p3 = bf16[576,512]{1,0:T(8,128)(2,1)S(1)} collective-permute-done((bf16[576,512]{1,0:T(8,128)(2,1)}, bf16[576,512]{1,0:T(8,128)(2,1)S(1)}, u32[]{:S(2)}, u32[]{:S(2)}) %collective-permute-start.3) | collective-permute-done | bytes 589856 | tf_op jit(solution)/shard_map/ppermute | solution.py:520
  42.4 2.8 %shard_map.56 = (bf16[256,1024]{1,0:T(8,128)(2,1)S(1)}, bf16[256,1024]{1,0:T(8,128)(2,1)S(1)}, bf16[4,64,512]{2,1,0:T(8,128)(2,1)S(1)}) custom-call(s32[21]{0:T(128)S(1)} %stack.107.info, bf16[4,2,64,1024]{3,2,1,0:T(8,128)(2,1)S(1)} %all-to-all-done.blocks, bf16[576,512]{1,0:T(8,128)(2,1)S(1)} %get-tuple-element.22.own, ...), custom_call_target="tpu_custom_call" | custom-call | tf_op jit(solution)/shard_map/pallas_call | solution.py:526
  45.3 0.9 collective-permute-start.4
  46.2 4.2 %collective-permute-start.5 = (bf16[256,1024]{1,0:T(8,128)(2,1)S(1)}, bf16[256,1024]{1,0:T(8,128)(2,1)S(1)}, u32[]{:S(2)}, u32[]{:S(2)}) collective-permute-start(bf16[256,1024]{1,0:T(8,128)(2,1)S(1)} %get-tuple-element.27.y_column), channel_id=1, source_target_pairs={{8,16},{12,20},{16,8},{20,12},{9,17},{13,21},{17,9},{21,13},{10,18... | collective-permute-start | bytes 1572872 | tf_op jit(solution)/shard_map/ppermute | solution.py:539
  50.4 2.7 %collective-permute-start.8 = (bf16[4,64,512]{2,1,0:T(8,128)(2,1)S(1)}, bf16[4,64,512]{2,1,0:T(8,128)(2,1)S(1)}, u32[]{:S(2)}, u32[]{:S(2)}) collective-permute-start(bf16[4,64,512]{2,1,0:T(8,128)(2,1)S(1)} %get-tuple-element.28.c0), channel_id=1, source_target_pairs={{0,2},{1,3},{2,0},{3,1},{4,6},{5,7},{6,4},{7,5},{8,10},{9,11},{10,... | collective-permute-start | bytes 786440 | tf_op jit(solution)/shard_map/ppermute | solution.py:545
  53.1 1.2 collective-permute-start.7
  54.3 1.7 %shard_map.57.rhs = bf16[2,2,512,512]{3,2,1,0:T(8,128)(2,1)S(1)} custom-call(s32[21]{0:T(128)S(1)} %stack.107.info, bf16[576,512]{1,0:T(8,128)(2,1)S(1)} %get-tuple-element.22.own, bf16[576,512]{1,0:T(8,128)(2,1)} %collective-permute-done.p0, bf16[576,512]{1,0:T(8,128)(2,1)S(1)} %collective-permute-done.1.p1, ...), custom_call_target="tpu_custom_call" | custom-call | tf_op jit(solution)/shard_map/pallas_call | solution.py:553
  56.0 8.8 %collective-permute-done.8.rows_far.c2 = bf16[4,64,512]{2,1,0:T(8,128)(2,1)S(1)} collective-permute-done((bf16[4,64,512]{2,1,0:T(8,128)(2,1)S(1)}, bf16[4,64,512]{2,1,0:T(8,128)(2,1)S(1)}, u32[]{:S(2)}, u32[]{:S(2)}) %collective-permute-start.8) | collective-permute-done | bytes 262176 | tf_op jit(solution)/shard_map/ppermute | solution.py:545
  67.2 1.9 %collective-permute-start.9 = (bf16[2,256,1024]{2,1,0:T(8,128)(2,1)S(1)}, bf16[2,256,1024]{2,1,0:T(8,128)(2,1)S(1)}, u32[]{:S(2)}, u32[]{:S(2)}) collective-permute-start(bf16[2,256,1024]{2,1,0:T(8,128)(2,1)S(1)} %get-tuple-element.29.xb), channel_id=1, source_target_pairs={{8,16},{12,20},{16,8},{20,12},{9,17},{13,21},{17,9},{21,13},{10,18... | collective-permute-start | bytes 3145736 | tf_op jit(solution)/shard_map/ppermute | solution.py:539
  69.1 1.2 collective-permute-start.12
  70.3 12.7 %collective-permute-done.12.c3 = bf16[4,64,512]{2,1,0:T(8,128)(2,1)S(1)} collective-permute-done((bf16[4,64,512]{2,1,0:T(8,128)(2,1)S(1)}, bf16[4,64,512]{2,1,0:T(8,128)(2,1)S(1)}, u32[]{:S(2)}, u32[]{:S(2)}) %collective-permute-start.12) | collective-permute-done | bytes 262176 | tf_op jit(solution)/shard_map/ppermute | solution.py:545
  83.0 2.3 %shard_map.59.weights = bf16[2,512,512]{2,1,0:T(8,128)(2,1)S(1)} custom-call(s32[21]{0:T(128)S(1)} %stack.107.info, bf16[4,64,512]{2,1,0:T(8,128)(2,1)S(1)} %get-tuple-element.28.c0, bf16[4,64,512]{2,1,0:T(8,128)(2,1)S(1)} %collective-permute-done.7.rows_next.c1, bf16[4,64,512]{2,1,0:T(8,128)(2,1)S(1)} %collective-permute-done.8.rows_far.c2, ...), custom_call_target="tpu_custom_call" | custom-call | tf_op jit(solution)/shard_map/pallas_call | solution.py:571
  85.3 5.2 %collective-permute-done.11.yf = bf16[2,256,1024]{2,1,0:T(8,128)(2,1)S(1)} collective-permute-done((bf16[2,256,1024]{2,1,0:T(8,128)(2,1)S(1)}, bf16[2,256,1024]{2,1,0:T(8,128)(2,1)S(1)}, u32[]{:S(2)}, u32[]{:S(2)}) %collective-permute-start.11) | collective-permute-done | bytes 1048608 | tf_op jit(solution)/shard_map/ppermute | solution.py:542
  92.0 1.3 collective-permute-start.13
  93.3 8.0 %collective-permute-done.13.arrived = bf16[2,512,512]{2,1,0:T(8,128)(2,1)S(1)} collective-permute-done((bf16[2,512,512]{2,1,0:T(8,128)(2,1)S(1)}, bf16[2,512,512]{2,1,0:T(8,128)(2,1)S(1)}, u32[]{:S(2)}, u32[]{:S(2)}) %collective-permute-start.13) | collective-permute-done | bytes 1048608 | tf_op jit(solution)/shard_map/ppermute | solution.py:604
  101.3 9.1 %shard_map.61 = (bf16[2,2,512,512]{3,2,1,0:T(8,128)(2,1)S(1)}, bf16[2,512,512]{2,1,0:T(8,128)(2,1)S(1)}) custom-call(s32[21]{0:T(128)S(1)} %stack.107.info, bf16[2,256,1024]{2,1,0:T(8,128)(2,1)S(1)} %get-tuple-element.29.xb, bf16[2,256,1024]{2,1,0:T(8,128)(2,1)S(1)} %collective-permute-done.9.x0, bf16[2,256,1024]{2,1,0:T(8,128)(2,1)S(1)} %collective-permute-done.10.x1, ...), custom_call_target="tpu_custom_call" | custom-call | flops 6442450944 | bytes 8388608 | tf_op jit(solution)/shard_map/pallas_call | solution.py:605
  110.5 1.4 collective-permute-start.14
  111.9 2.2 %collective-permute-done.14.arrived = bf16[2,512,512]{2,1,0:T(8,128)(2,1)S(1)} collective-permute-done((bf16[2,512,512]{2,1,0:T(8,128)(2,1)S(1)}, bf16[2,512,512]{2,1,0:T(8,128)(2,1)S(1)}, u32[]{:S(2)}, u32[]{:S(2)}) %collective-permute-start.14) | collective-permute-done | bytes 1048608 | tf_op jit(solution)/shard_map/ppermute | solution.py:616
  114.9 8.0 %collective-permute-start.16 = (bf16[2,256,512]{2,1,0:T(8,128)(2,1)S(1)}, bf16[2,256,512]{2,1,0:T(8,128)(2,1)S(1)}, u32[]{:S(2)}, u32[]{:S(2)}) collective-permute-start(bf16[2,256,512]{2,1,0:T(8,128)(2,1)S(1)} %get-tuple-element.36), channel_id=1, source_target_pairs={{4,0},{0,4},{20,8},{16,12},{12,16},{8,20},{28,24},{24,28},{5,1},{1... | collective-permute-start | bytes 1572872 | tf_op jit(solution)/shard_map/ppermute | solution.py:629
  123.1 4.0 %collective-permute-start.15 = (bf16[2,256,512]{2,1,0:T(8,128)(2,1)S(1)}, bf16[2,256,512]{2,1,0:T(8,128)(2,1)S(1)}, u32[]{:S(2)}, u32[]{:S(2)}) collective-permute-start(bf16[2,256,512]{2,1,0:T(8,128)(2,1)S(1)} %get-tuple-element.35.own), channel_id=1, source_target_pairs={{16,8},{20,12},{8,16},{12,20},{17,9},{21,13},{9,17},{13,21},{18,10... | collective-permute-start | bytes 1572872 | tf_op jit(solution)/shard_map/ppermute | solution.py:629
  127.1 2.8 %collective-permute-done.16.rest_1_ = bf16[2,256,512]{2,1,0:T(8,128)(2,1)S(1)} collective-permute-done((bf16[2,256,512]{2,1,0:T(8,128)(2,1)S(1)}, bf16[2,256,512]{2,1,0:T(8,128)(2,1)S(1)}, u32[]{:S(2)}, u32[]{:S(2)}) %collective-permute-start.16) | collective-permute-done | bytes 524320 | tf_op jit(solution)/shard_map/ppermute | solution.py:629
  129.9 4.8 %collective-permute-done.17.rest_2_ = bf16[2,256,512]{2,1,0:T(8,128)(2,1)S(1)} collective-permute-done((bf16[2,256,512]{2,1,0:T(8,128)(2,1)S(1)}, bf16[2,256,512]{2,1,0:T(8,128)(2,1)S(1)}, u32[]{:S(2)}, u32[]{:S(2)}) %collective-permute-start.17) | collective-permute-done | bytes 524320 | tf_op jit(solution)/shard_map/ppermute | solution.py:629
  134.7 11.6 %collective-permute-done.18.rest_3_ = bf16[2,256,512]{2,1,0:T(8,128)(2,1)S(1)} collective-permute-done((bf16[2,256,512]{2,1,0:T(8,128)(2,1)S(1)}, bf16[2,256,512]{2,1,0:T(8,128)(2,1)S(1)}, u32[]{:S(2)}, u32[]{:S(2)}) %collective-permute-start.18) | collective-permute-done | bytes 524320 | tf_op jit(solution)/shard_map/ppermute | solution.py:629
  146.4 2.2 %shard_map.63 = bf16[2,256,2048]{2,1,0:T(8,128)(2,1)} custom-call(s32[6]{0:T(128)S(1)} %stack.92.place, bf16[2,256,512]{2,1,0:T(8,128)(2,1)S(1)} %get-tuple-element.35.own, bf16[2,256,512]{2,1,0:T(8,128)(2,1)S(1)} %collective-permute-done.15.rest_0_, bf16[2,256,512]{2,1,0:T(8,128)(2,1)S(1)} %collective-permute-done.16.rest_1_, ...), custom_call_target="tpu_custom_call" | custom-call | tf_op jit(solution)/shard_map/pallas_call | solution.py:631
  (31 shorter events, 8.2 us)
Async XLA Ops:
  1.8 6.8 %copy-start.1 = (bf16[1,256,512]{2,1,0:T(8,128)(2,1)S(1)}, bf16[1,256,512]{2,1,0:T(8,128)(2,1)}, u32[]{:S(2)}) copy-start(bf16[1,256,512]{2,1,0:T(8,128)(2,1)} %param.7) | copy-start | bytes 786436
  2.9 16.7 %copy-start.2 = (s32[16]{0:T(128)S(1)}, s32[16]{0:T(128)}, u32[]{:S(2)}) copy-start(s32[16]{0:T(128)} %param.6) | copy-start | bytes 196
  2.9 39.5 %all-to-all-start = ((bf16[4,2,64,1024]{3,2,1,0:T(8,128)(2,1)}), bf16[4,2,64,1024]{3,2,1,0:T(8,128)(2,1)S(1)}, u32[]{:S(2)}, u32[]{:S(2)}) async-start(bf16[4,2,64,1024]{3,2,1,0:T(8,128)(2,1)} %broadcast_in_dim.4), calls=%async_computation | async-start | bytes 2097152 | tf_op jit(solution)/shard_map/all_to_all | solution.py:522
  8.6 1.6 %copy-start = (bf16[2,1,256,2048]{3,2,1,0:T(8,128)(2,1)S(1)}, bf16[2,1,256,2048]{3,2,1,0:T(8,128)(2,1)}, u32[]{:S(2)}) copy-start(bf16[2,1,256,2048]{3,2,1,0:T(8,128)(2,1)} %param.5) | copy-start | bytes 6291460
  12.6 16.3 %collective-permute-start.1 = (bf16[576,512]{1,0:T(8,128)(2,1)}, bf16[576,512]{1,0:T(8,128)(2,1)S(1)}, u32[]{:S(2)}, u32[]{:S(2)}) collective-permute-start(bf16[576,512]{1,0:T(8,128)(2,1)} %get-tuple-element.23), channel_id=1, source_target_pairs={{0,4},{4,0},{8,20},{12,16},{16,12},{20,8},{24,28},{28,24},{1,5},{5... | collective-permute-start | bytes 1769480 | tf_op jit(solution)/shard_map/ppermute | solution.py:520
  15.6 15.6 %collective-permute-start.2 = (bf16[576,512]{1,0:T(8,128)(2,1)}, bf16[576,512]{1,0:T(8,128)(2,1)S(1)}, u32[]{:S(2)}, u32[]{:S(2)}) collective-permute-start(bf16[576,512]{1,0:T(8,128)(2,1)} %get-tuple-element.24), channel_id=1, source_target_pairs={{0,16},{4,20},{8,0},{12,4},{16,24},{20,28},{24,8},{28,12},{1,17},{... | collective-permute-start | bytes 1769480 | tf_op jit(solution)/shard_map/ppermute | solution.py:520
  15.6 26.8 %collective-permute-start.3 = (bf16[576,512]{1,0:T(8,128)(2,1)}, bf16[576,512]{1,0:T(8,128)(2,1)S(1)}, u32[]{:S(2)}, u32[]{:S(2)}) collective-permute-start(bf16[576,512]{1,0:T(8,128)(2,1)} %get-tuple-element.25), channel_id=1, source_target_pairs={{0,20},{4,16},{8,4},{12,0},{16,28},{20,24},{24,12},{28,8},{1,21},{... | collective-permute-start | bytes 1769480 | tf_op jit(solution)/shard_map/ppermute | solution.py:520
  16.2 26.2 %collective-permute-start = (bf16[576,512]{1,0:T(8,128)(2,1)S(1)}, bf16[576,512]{1,0:T(8,128)(2,1)}, u32[]{:S(2)}, u32[]{:S(2)}) collective-permute-start(bf16[576,512]{1,0:T(8,128)(2,1)S(1)} %get-tuple-element.22.own), channel_id=1, source_target_pairs={{8,16},{12,20},{16,8},{20,12},{9,17},{13,21},{17,9},{21,13},{10,18... | collective-permute-start | bytes 1769480 | tf_op jit(solution)/shard_map/ppermute | solution.py:520
  45.3 20.1 %collective-permute-start.4 = (bf16[256,1024]{1,0:T(8,128)(2,1)S(1)}, bf16[256,1024]{1,0:T(8,128)(2,1)S(1)}, u32[]{:S(2)}, u32[]{:S(2)}) collective-permute-start(bf16[256,1024]{1,0:T(8,128)(2,1)S(1)} %get-tuple-element.26.x_column), channel_id=1, source_target_pairs={{0,4},{4,0},{1,5},{5,1},{2,6},{6,2},{3,7},{7,3},{8,12},{12,8},{9,1... | collective-permute-start | bytes 1572872 | tf_op jit(solution)/shard_map/ppermute | solution.py:542
  46.2 19.1 %collective-permute-start.6 = (bf16[256,1024]{1,0:T(8,128)(2,1)S(1)}, bf16[256,1024]{1,0:T(8,128)(2,1)S(1)}, u32[]{:S(2)}, u32[]{:S(2)}) collective-permute-start(bf16[256,1024]{1,0:T(8,128)(2,1)S(1)} %get-tuple-element.27.y_column), channel_id=1, source_target_pairs={{0,16},{4,20},{8,0},{12,4},{16,24},{20,28},{24,8},{28,12},{1,17},{... | collective-permute-start | bytes 1572872 | tf_op jit(solution)/shard_map/ppermute | solution.py:539
  46.2 19.1 %collective-permute-start.5 = (bf16[256,1024]{1,0:T(8,128)(2,1)S(1)}, bf16[256,1024]{1,0:T(8,128)(2,1)S(1)}, u32[]{:S(2)}, u32[]{:S(2)}) collective-permute-start(bf16[256,1024]{1,0:T(8,128)(2,1)S(1)} %get-tuple-element.27.y_column), channel_id=1, source_target_pairs={{8,16},{12,20},{16,8},{20,12},{9,17},{13,21},{17,9},{21,13},{10,18... | collective-permute-start | bytes 1572872 | tf_op jit(solution)/shard_map/ppermute | solution.py:539
  50.4 14.4 %collective-permute-start.8 = (bf16[4,64,512]{2,1,0:T(8,128)(2,1)S(1)}, bf16[4,64,512]{2,1,0:T(8,128)(2,1)S(1)}, u32[]{:S(2)}, u32[]{:S(2)}) collective-permute-start(bf16[4,64,512]{2,1,0:T(8,128)(2,1)S(1)} %get-tuple-element.28.c0), channel_id=1, source_target_pairs={{0,2},{1,3},{2,0},{3,1},{4,6},{5,7},{6,4},{7,5},{8,10},{9,11},{10,... | collective-permute-start | bytes 786440 | tf_op jit(solution)/shard_map/ppermute | solution.py:545
  53.1 12.2 %collective-permute-start.7 = (bf16[4,64,512]{2,1,0:T(8,128)(2,1)S(1)}, bf16[4,64,512]{2,1,0:T(8,128)(2,1)S(1)}, u32[]{:S(2)}, u32[]{:S(2)}) collective-permute-start(bf16[4,64,512]{2,1,0:T(8,128)(2,1)S(1)} %get-tuple-element.28.c0), channel_id=1, source_target_pairs={{0,1},{1,0},{2,3},{3,2},{4,5},{5,4},{6,7},{7,6},{8,9},{9,8},{10,11... | collective-permute-start | bytes 786440 | tf_op jit(solution)/shard_map/ppermute | solution.py:545
  66.1 24.4 %collective-permute-start.11 = (bf16[2,256,1024]{2,1,0:T(8,128)(2,1)S(1)}, bf16[2,256,1024]{2,1,0:T(8,128)(2,1)S(1)}, u32[]{:S(2)}, u32[]{:S(2)}) collective-permute-start(bf16[2,256,1024]{2,1,0:T(8,128)(2,1)S(1)} %get-tuple-element.30.yb), channel_id=1, source_target_pairs={{0,4},{4,0},{1,5},{5,1},{2,6},{6,2},{3,7},{7,3},{8,12},{12,8},{9,1... | collective-permute-start | bytes 3145736 | tf_op jit(solution)/shard_map/ppermute | solution.py:542
  66.5 24.0 %collective-permute-start.10 = (bf16[2,256,1024]{2,1,0:T(8,128)(2,1)S(1)}, bf16[2,256,1024]{2,1,0:T(8,128)(2,1)S(1)}, u32[]{:S(2)}, u32[]{:S(2)}) collective-permute-start(bf16[2,256,1024]{2,1,0:T(8,128)(2,1)S(1)} %get-tuple-element.29.xb), channel_id=1, source_target_pairs={{0,16},{4,20},{8,0},{12,4},{16,24},{20,28},{24,8},{28,12},{1,17},{... | collective-permute-start | bytes 3145736 | tf_op jit(solution)/shard_map/ppermute | solution.py:539
  67.2 24.2 %collective-permute-start.9 = (bf16[2,256,1024]{2,1,0:T(8,128)(2,1)S(1)}, bf16[2,256,1024]{2,1,0:T(8,128)(2,1)S(1)}, u32[]{:S(2)}, u32[]{:S(2)}) collective-permute-start(bf16[2,256,1024]{2,1,0:T(8,128)(2,1)S(1)} %get-tuple-element.29.xb), channel_id=1, source_target_pairs={{8,16},{12,20},{16,8},{20,12},{9,17},{13,21},{17,9},{21,13},{10,18... | collective-permute-start | bytes 3145736 | tf_op jit(solution)/shard_map/ppermute | solution.py:539
  69.1 13.9 %collective-permute-start.12 = (bf16[4,64,512]{2,1,0:T(8,128)(2,1)S(1)}, bf16[4,64,512]{2,1,0:T(8,128)(2,1)S(1)}, u32[]{:S(2)}, u32[]{:S(2)}) collective-permute-start(bf16[4,64,512]{2,1,0:T(8,128)(2,1)S(1)} %collective-permute-done.7.rows_next.c1), channel_id=1, source_target_pairs={{0,2},{1,3},{2,0},{3,1},{4,6},{5,7},{6,4},{7,5},{8,10},{9,11},{10,... | collective-permute-start | bytes 786440 | tf_op jit(solution)/shard_map/ppermute | solution.py:545
  92.0 9.3 %collective-permute-start.13 = (bf16[2,512,512]{2,1,0:T(8,128)(2,1)S(1)}, bf16[2,512,512]{2,1,0:T(8,128)(2,1)S(1)}, u32[]{:S(2)}, u32[]{:S(2)}) collective-permute-start(bf16[2,512,512]{2,1,0:T(8,128)(2,1)S(1)} %get-tuple-element.32.w_high), channel_id=1, source_target_pairs={{0,8},{16,24},{1,9},{17,25},{2,10},{18,26},{3,11},{19,27},{4,12},{... | collective-permute-start | bytes 3145736 | tf_op jit(solution)/shard_map/ppermute | solution.py:604
  110.5 3.6 %collective-permute-start.14 = (bf16[2,512,512]{2,1,0:T(8,128)(2,1)S(1)}, bf16[2,512,512]{2,1,0:T(8,128)(2,1)S(1)}, u32[]{:S(2)}, u32[]{:S(2)}) collective-permute-start(bf16[2,512,512]{2,1,0:T(8,128)(2,1)S(1)} %get-tuple-element.33), channel_id=1, source_target_pairs={{8,0},{24,16},{9,1},{25,17},{10,2},{26,18},{11,3},{27,19},{12,4},{... | collective-permute-start | bytes 3145736 | tf_op jit(solution)/shard_map/ppermute | solution.py:616
  114.9 15.0 %collective-permute-start.16 = (bf16[2,256,512]{2,1,0:T(8,128)(2,1)S(1)}, bf16[2,256,512]{2,1,0:T(8,128)(2,1)S(1)}, u32[]{:S(2)}, u32[]{:S(2)}) collective-permute-start(bf16[2,256,512]{2,1,0:T(8,128)(2,1)S(1)} %get-tuple-element.36), channel_id=1, source_target_pairs={{4,0},{0,4},{20,8},{16,12},{12,16},{8,20},{28,24},{24,28},{5,1},{1... | collective-permute-start | bytes 1572872 | tf_op jit(solution)/shard_map/ppermute | solution.py:629
  123.0 11.8 %collective-permute-start.17 = (bf16[2,256,512]{2,1,0:T(8,128)(2,1)S(1)}, bf16[2,256,512]{2,1,0:T(8,128)(2,1)S(1)}, u32[]{:S(2)}, u32[]{:S(2)}) collective-permute-start(bf16[2,256,512]{2,1,0:T(8,128)(2,1)S(1)} %get-tuple-element.37), channel_id=1, source_target_pairs={{16,0},{20,4},{0,8},{4,12},{24,16},{28,20},{8,24},{12,28},{17,1},{... | collective-permute-start | bytes 1572872 | tf_op jit(solution)/shard_map/ppermute | solution.py:629
  123.0 23.4 %collective-permute-start.18 = (bf16[2,256,512]{2,1,0:T(8,128)(2,1)S(1)}, bf16[2,256,512]{2,1,0:T(8,128)(2,1)S(1)}, u32[]{:S(2)}, u32[]{:S(2)}) collective-permute-start(bf16[2,256,512]{2,1,0:T(8,128)(2,1)S(1)} %get-tuple-element.38), channel_id=1, source_target_pairs={{20,0},{16,4},{4,8},{0,12},{28,16},{24,20},{12,24},{8,28},{21,1},{... | collective-permute-start | bytes 1572872 | tf_op jit(solution)/shard_map/ppermute | solution.py:629
  123.1 23.3 %collective-permute-start.15 = (bf16[2,256,512]{2,1,0:T(8,128)(2,1)S(1)}, bf16[2,256,512]{2,1,0:T(8,128)(2,1)S(1)}, u32[]{:S(2)}, u32[]{:S(2)}) collective-permute-start(bf16[2,256,512]{2,1,0:T(8,128)(2,1)S(1)} %get-tuple-element.35.own), channel_id=1, source_target_pairs={{16,8},{20,12},{8,16},{12,20},{17,9},{21,13},{9,17},{13,21},{18,10... | collective-permute-start | bytes 1572872 | tf_op jit(solution)/shard_map/ppermute | solution.py:629

commit v13 on v12

--- a/solution.py
+++ b/solution.py
@@ -12,6 +12,7 @@
 bf16 = jnp.bfloat16
 f32 = jnp.float32
 anywhere = pl.BlockSpec(memory_space=pl.ANY)
+in_hbm = pl.BlockSpec(memory_space=pltpu.HBM)
 in_smem = pl.BlockSpec(memory_space=pltpu.SMEM)
 in_vmem = pl.BlockSpec(memory_space=pltpu.VMEM)
 
@@ -180,66 +181,80 @@
         self.received.wait()
 
 
+def block_kernel(x_factor, y_factor, blocks, sems):
+    order = x_factor.shape[2]
+    copies = []
+    for target in range(blocks.shape[0]):
+        for which, factor in enumerate((x_factor, y_factor)):
+            for plane in range(2):
+                copies.append(
+                    pltpu.make_async_copy(
+                        factor.at[plane],
+                        blocks.at[target, which, :, pl.ds(plane * order, order)],
+                        sems.at[target, which, plane],
+                    )
+                )
+    start_all(copies)
+    wait_all(copies)
+
+
 def pack_kernel(place, field, coupling, *rest):
-    pieces, (sems, csems) = rest[:-2], rest[-2:]
+    pieces, sems = rest[:-1], rest[-1]
     rows_here = field.shape[1]
-    height = pieces[0].shape[0] - 2 * rows_here
-    own = pl.ds(pl.multiple_of(place[len(pieces)] * height, height), height)
+    tall = coupling.shape[1]
+    own = pl.ds(2 * place[len(pieces)], 2)
     copies = []
     for index, piece in enumerate(pieces):
-        width = piece.shape[1]
+        width = piece.shape[2]
         offset = pl.multiple_of(place[index] * width, width)
-        for plane in range(2):
-            copies.append(
-                pltpu.make_async_copy(
-                    field.at[plane, :, pl.ds(offset, width)],
-                    piece.at[pl.ds(plane * rows_here, rows_here)],
-                    sems.at[index, plane],
-                )
-            )
-        copies.append(
+        copies += [
             pltpu.make_async_copy(
-                coupling.at[own], piece.at[pl.ds(2 * rows_here, height)], csems.at[index]
-            )
-        )
+                field.at[:, :, pl.ds(offset, width)],
+                piece.at[:, pl.ds(0, rows_here), :],
+                sems.at[index, 0],
+            ),
+            pltpu.make_async_copy(
+                coupling.at[own], piece.at[:, pl.ds(rows_here, tall), :], sems.at[index, 1]
+            ),
+        ]
     start_all(copies)
     wait_all(copies)
 
 
-def unpack_kernel(place, own, *rest):
-    pieces, field, sems = rest[:-2], rest[-2], rest[-1]
+def early_unpack_kernel(place, own, p0, p1, p2, field, sems):
     copies = []
-    for index, piece in enumerate(pieces):
+    for index, piece in enumerate((p0, p1, p2)):
         width = piece.shape[2]
         offset = pl.multiple_of(place[index] * width, width)
         target = field.at[:, :, pl.ds(offset, width)]
         if index:
             copies.append(pltpu.make_async_copy(piece, target, sems.at[index]))
         else:
-            copies.append(Either(place[len(pieces) + 1], own, piece, target, sems.at[index]))
+            copies.append(Either(place[5], own, piece, target, sems.at[index]))
     start_all(copies)
     wait_all(copies)
 
 
-def column_kernel(info, blocks, own, p0, p1, p2, p3, x_column, y_column, rows_held, sems, csems):
+def late_unpack_kernel(place, piece, started, field, sem):
+    width = piece.shape[2]
+    offset = pl.multiple_of(place[3] * width, width)
+    copy = pltpu.make_async_copy(piece, field.at[:, :, pl.ds(offset, width)], sem)
+    copy.start()
+    copy.wait()
+
+
+def column_kernel(info, blocks, own, p0, p1, p2, p3, x_column, y_turned, rows_held, sems):
     count, factors, height, width = blocks.shape
-    copies = []
+    last = pl.ds(own.shape[1] - rows_held.shape[2], rows_held.shape[2])
+    parts = [piece.at[:, last, :] for piece in (p0, p1, p2, p3)]
+    copies = [Either(info[info_self], own.at[:, last, :], parts[0], rows_held.at[0], sems.at[0])]
+    for index in range(1, len(parts)):
+        copies.append(pltpu.make_async_copy(parts[index], rows_held.at[index], sems.at[index]))
+    start_all(copies)
     for index in range(count):
-        for which, column in enumerate((x_column, y_column)):
-            copies.append(
-                pltpu.make_async_copy(
-                    blocks.at[index, which],
-                    column.at[pl.ds(index * height, height)],
-                    sems.at[index, which],
-                )
-            )
-    last = pl.ds(own.shape[0] - height, height)
-    copies.append(Either(info[info_self], own.at[last], p0.at[last], rows_held.at[0], csems.at[0]))
-    for index, piece in enumerate((p1, p2, p3)):
-        copies.append(
-            pltpu.make_async_copy(piece.at[last], rows_held.at[index + 1], csems.at[index + 1])
-        )
-    start_all(copies)
+        x_column[index * height : (index + 1) * height] = blocks[index, 0]
+    column = blocks[:, 1].reshape(count * height, width)
+    y_turned[...] = column.astype(f32).T.astype(bf16)
     wait_all(copies)
 
 
@@ -249,13 +264,12 @@
     for index, piece in enumerate((p0, p1, p2, p3)):
         slot, half = info[info_piece + 2 * index], info[info_piece + 2 * index + 1]
         rows = pl.ds(pl.multiple_of(half * height, height), height)
-        for plane in range(2):
-            part = pl.ds(plane * height, height)
-            ends = (rhs.at[slot, plane, rows, :], sems.at[index, plane])
-            if index:
-                copies.append(pltpu.make_async_copy(piece.at[part], *ends))
-            else:
-                copies.append(Either(info[info_self], own.at[part], piece.at[part], *ends))
+        part = (slice(None), pl.ds(0, height), slice(None))
+        ends = (rhs.at[slot, :, rows, :], sems.at[index])
+        if index:
+            copies.append(pltpu.make_async_copy(piece.at[part], *ends))
+        else:
+            copies.append(Either(info[info_self], own.at[part], piece.at[part], *ends))
     start_all(copies)
     wait_all(copies)
 
@@ -323,7 +337,6 @@
 
     def apply(self, slot, source, store, fresh):
         order, beside, below = self.order, self.beside, self.below
-        turned = (((1,), (1,)), ((), ()))
         turn = self.info[info_slot + slot]
         for rows in row_chunks(order, 256):
             further = slice(rows.start + order, rows.stop + order)
@@ -334,9 +347,7 @@
             beside[further, order:] = real
         height = order // 2
         for far, part in enumerate(self.y_parts):
-            product = lax.dot_general(
-                beside[...], part[turn], turned, preferred_element_type=f32
-            ).astype(bf16)
+            product = jnp.dot(beside[...], part[turn], preferred_element_type=f32).astype(bf16)
             start = self.info[info_half + far] * height
             columns = pl.ds(pl.multiple_of(start, height), height)
             beyond = pl.ds(pl.multiple_of(order + start, height), height)
@@ -501,39 +512,43 @@
         + [own_y, group == member]
     ).astype(jnp.int32)
     piece_shape = jax.ShapeDtypeStruct((2, rows_here, order), bf16)
-    shard = jnp.stack(
-        [jnp.concatenate([factor[0, 0], factor[0, 1]], axis=1) for factor in (x_factor, y_factor)]
-    )
-    blocks = jnp.broadcast_to(shard[None], (py_count,) + shard.shape)
+    blocks = pl.pallas_call(
+        block_kernel,
+        out_shape=jax.ShapeDtypeStruct((py_count, 2, height, 2 * order), bf16),
+        in_specs=[in_hbm] * 2,
+        out_specs=in_vmem,
+        scratch_shapes=[pltpu.SemaphoreType.DMA((py_count, 2, 2))],
+        compiler_params=params,
+    )(x_factor[0], y_factor[0])
+    tall = height // 2
     packed = pl.pallas_call(
         pack_kernel,
-        out_shape=[jax.ShapeDtypeStruct((2 * rows_here + height, order), bf16)] * len(rounds),
-        in_specs=[in_smem] + [anywhere] * 2,
+        out_shape=[jax.ShapeDtypeStruct((2, rows_here + tall, order), bf16)] * len(rounds),
+        in_specs=[in_smem] + [in_hbm] * 2,
         out_specs=[in_vmem] * len(rounds),
-        scratch_shapes=[
-            pltpu.SemaphoreType.DMA((len(rounds), 2)),
-            pltpu.SemaphoreType.DMA((len(rounds),)),
-        ],
-        compiler_params=params,
-    )(sends_to, field, coupling[0])
+        scratch_shapes=[pltpu.SemaphoreType.DMA((len(rounds), 2))],
+        compiler_params=params,
+    )(sends_to, field, coupling[0].reshape(rows_here // tall, tall, order))
     pieces = [
         lax.ppermute(piece, ("sec", "px"), pairs(a, b)) for piece, (a, b) in zip(packed, rounds)
     ]
     blocks = lax.all_to_all(blocks, "py", split_axis=0, concat_axis=0, tiled=True)
 
     column_shape = jax.ShapeDtypeStruct((rows_here, 2 * order), bf16)
-    rows_shape = jax.ShapeDtypeStruct((len(rounds), height, order), bf16)
-    x_column, y_column, rows_held = pl.pallas_call(
+    turned_shape = jax.ShapeDtypeStruct((2 * order, rows_here), bf16)
+    x_column, y_turned, rows_held = pl.pallas_call(
         column_kernel,
-        out_shape=[column_shape, column_shape, rows_shape],
-        in_specs=[in_smem] + [anywhere] * 6,
+        out_shape=[
+            column_shape,
+            turned_shape,
+            jax.ShapeDtypeStruct((len(rounds), 2, tall, order), bf16),
+        ],
+        in_specs=[in_smem, in_vmem] + [anywhere] * 5,
         out_specs=[in_vmem] * 3,
-        scratch_shapes=[
-            pltpu.SemaphoreType.DMA((py_count, 2)),
-            pltpu.SemaphoreType.DMA((len(rounds),)),
-        ],
+        scratch_shapes=[pltpu.SemaphoreType.DMA((len(rounds),))],
         compiler_params=params,
     )(info, blocks, packed[0], *pieces)
+    rows_held = rows_held.reshape(len(rounds), height, order)
 
     def across(block, a):
         return lax.ppermute(block, ("sec", "px"), pairs(a, 0))
@@ -544,7 +559,7 @@
     def over_z(block, bit):
         return lax.ppermute(block, "py", [(z, z ^ bit) for z in range(py_count)])
 
-    y_near = [across(y_column, a) for a in range(2)]
+    y_near = [across(y_turned, a) for a in range(2)]
     x_aside = aside(x_column)
     rows_next = over_z(rows_held, 1)
     rows_far = over_z(rows_held, 2)
@@ -555,17 +570,19 @@
         out_shape=double_shape,
         in_specs=[in_smem] + [anywhere] * 5,
         out_specs=in_vmem,
-        scratch_shapes=[pltpu.SemaphoreType.DMA((len(rounds), 2))],
+        scratch_shapes=[pltpu.SemaphoreType.DMA((len(rounds),))],
         compiler_params=params,
     )(info, packed[0], *pieces)
     x_both, y_both = pl.pallas_call(
         both_kernel,
-        out_shape=[jax.ShapeDtypeStruct((2,) + column_shape.shape, bf16)] * 2,
+        out_shape=[
+            jax.ShapeDtypeStruct((2,) + one.shape, bf16) for one in (column_shape, turned_shape)
+        ],
         in_specs=[in_smem] + [anywhere] * 8,
         out_specs=[in_vmem] * 2,
         scratch_shapes=[pltpu.SemaphoreType.DMA((4,))],
         compiler_params=params,
-    )(info, x_column, x_aside, y_column, *y_near, rows_next, rows_far, rhs)
+    )(info, x_column, x_aside, y_turned, *y_near, rows_next, rows_far, rhs)
     y_far = aside(y_both)
     x_across = [across(x_both, a) for a in range(2)]
     weights = pl.pallas_call(
@@ -628,14 +645,24 @@
     received = [
         lax.ppermute(piece, ("sec", "px"), back_pairs(a, b)) for piece, (a, b) in zip(results, rounds)
     ]
+    whole_shape = jax.ShapeDtypeStruct(field.shape, bf16)
+    started = pl.pallas_call(
+        early_unpack_kernel,
+        out_shape=whole_shape,
+        in_specs=[in_smem] + [in_vmem] * 4,
+        out_specs=in_hbm,
+        scratch_shapes=[pltpu.SemaphoreType.DMA((3,))],
+        compiler_params=params,
+    )(sends_to, results[0], *received[:3])
     output = pl.pallas_call(
-        unpack_kernel,
-        out_shape=jax.ShapeDtypeStruct(field.shape, bf16),
-        in_specs=[in_smem] + [anywhere] * (len(rounds) + 1),
-        out_specs=in_vmem,
-        scratch_shapes=[pltpu.SemaphoreType.DMA((len(rounds),))],
-        compiler_params=params,
-    )(sends_to, results[0], *received)
+        late_unpack_kernel,
+        out_shape=whole_shape,
+        in_specs=[in_smem, in_vmem, in_hbm],
+        out_specs=in_hbm,
+        scratch_shapes=[pltpu.SemaphoreType.DMA(())],
+        input_output_aliases={2: 0},
+        compiler_params=params,
+    )(sends_to, received[3], started)
     return output[:, None]
 
 

time: 149 us -> 148 us (level); the launches traced: 149 us -> 146 us
  starting transfers between devices: 40.5 us -> 38.5 us
    ppermute x4, starting transfers between devices: 12.2 us -> 10.3 us  [on_device(): lax.ppermute(piece, ('sec', 'px'), back_pairs(a, b))]
    unnamed x6 -> x10, local copies, waits for them, and re-layouts: 1.6 us -> 3.45 us
    squeeze x2 -> x0, local copies, waits for them, and re-layouts: 1.76 us -> none  [on_device(): factor[0, 0]]
    pallas_call x4 -> x6, Pallas kernels: 8.14 us -> 8.82 us  [the longest x1 2.3 us: on_device(): pl.pallas_call(pack_kernel, out_shape=[jax.ShapeDtypeStruct((2, rows_here...]
  transfers between devices with their start and end apart: 20 -> 20, of which waited for: 13 -> 14; matrix products, arithmetic and copies ran while one was open for 1% -> 1% of each run, Pallas kernels for 4% -> 5%
where the time goes in v13:
time: 148 us; the launch traced here: 146 us
  waiting for transfers between devices  76.8 us (52%)
  starting transfers between devices  38.5 us (26%)
  Pallas kernels  23.3 us (16%)
  local copies, waits for them, and re-layouts  4.24 us (3%)
  between operations  3.09 us (2%)
    ppermute x3, waiting for transfers between devices, over_z(): return lax.ppermute(block, 'py', [(z, z ^ bit) for z in range(py_count)])  22.1 us
    ppermute x4, waiting for transfers between devices, on_device(): lax.ppermute(piece, ('sec', 'px'), pairs(a, b))  19.5 us
    ppermute x4, waiting for transfers between devices, on_device(): lax.ppermute(piece, ('sec', 'px'), back_pairs(a, b))  19 us
    ppermute x4, starting transfers between devices, on_device(): lax.ppermute(piece, ('sec', 'px'), back_pairs(a, b))  10.3 us
    pallas_call x1, Pallas kernels, on_device(): pl.pallas_call(last_kernel, out_shape=[double_shape, full_shape], in_spec...  9.12 us
    ppermute x1, waiting for transfers between devices, on_device(): incoming = lax.ppermute(w_high, 'sec', up)  8.01 us
    ppermute x4, starting transfers between devices, on_device(): lax.ppermute(piece, ('sec', 'px'), pairs(a, b))  6.94 us
    ppermute x4, starting transfers between devices, across(): return lax.ppermute(block, ('sec', 'px'), pairs(a, 0))  6.77 us
  transfers between devices with their start and end apart: 20, of which 14 were waited for; matrix products, arithmetic and copies ran while one was open for 1% of the time, Pallas kernels for 5%

profile of v13, /device:TPU:1, one launch (start us, length us, event | category | flops | bytes accessed | tf_op | source)
XLA Modules:
  0.0 146.0 jit_solution(14648348133198539081)
XLA Ops:
  1.9 1.3 shard_map.55
  3.2 5.4 %all-to-all-start = ((bf16[4,2,64,1024]{3,2,1,0:T(8,128)(2,1)}), bf16[4,2,64,1024]{3,2,1,0:T(8,128)(2,1)S(1)}, u32[]{:S(2)}, u32[]{:S(2)}) async-start(bf16[4,2,64,1024]{3,2,1,0:T(8,128)(2,1)} %shard_map.55), calls=%async_computation | async-start | bytes 2097152 | tf_op jit(solution)/shard_map/all_to_all | solution.py:535
  8.7 1.6 %copy-done = bf16[2,1,256,2048]{3,2,1,0:T(8,128)(2,1)S(1)} copy-done((bf16[2,1,256,2048]{3,2,1,0:T(8,128)(2,1)S(1)}, bf16[2,1,256,2048]{3,2,1,0:T(8,128)(2,1)}, u32[]{:S(2)}) %copy-start) | copy-done | bytes 2097176
  10.3 2.3 %shard_map.56 = (bf16[2,288,512]{2,1,0:T(8,128)(2,1)S(1)}, bf16[2,288,512]{2,1,0:T(8,128)(2,1)}, bf16[2,288,512]{2,1,0:T(8,128)(2,1)}, bf16[2,288,512]{2,1,0:T(8,128)(2,1)}) custom-call(s32[6]{0:T(128)S(1)} %stack.83.place, bf16[2,256,2048]{2,1,0:T(8,128)(2,1)S(1)} %bitcast.29, bf16[8,32,512]{2,1,0:T(8,128)(2,1)S(1)} %bitcast.30), custom_call_target="tpu_custom_call" | custom-call | tf_op jit(solution)/shard_map/pallas_call | solution.py:524
  12.6 3.1 %collective-permute-start.1 = (bf16[2,288,512]{2,1,0:T(8,128)(2,1)}, bf16[2,288,512]{2,1,0:T(8,128)(2,1)S(1)}, u32[]{:S(2)}, u32[]{:S(2)}) collective-permute-start(bf16[2,288,512]{2,1,0:T(8,128)(2,1)} %get-tuple-element.23), channel_id=1, source_target_pairs={{0,4},{4,0},{8,20},{12,16},{16,12},{20,8},{24,28},{28,24},{1,5},{5... | collective-permute-start | bytes 1769480 | tf_op jit(solution)/shard_map/ppermute | solution.py:533
  16.3 3.3 %collective-permute-start = (bf16[2,288,512]{2,1,0:T(8,128)(2,1)S(1)}, bf16[2,288,512]{2,1,0:T(8,128)(2,1)}, u32[]{:S(2)}, u32[]{:S(2)}) collective-permute-start(bf16[2,288,512]{2,1,0:T(8,128)(2,1)S(1)} %get-tuple-element.22.own), channel_id=1, source_target_pairs={{8,16},{12,20},{16,8},{20,12},{9,17},{13,21},{17,9},{21,13},{10,18... | collective-permute-start | bytes 1769480 | tf_op jit(solution)/shard_map/ppermute | solution.py:533
  23.0 5.9 %collective-permute-done.1.p1 = bf16[2,288,512]{2,1,0:T(8,128)(2,1)S(1)} collective-permute-done((bf16[2,288,512]{2,1,0:T(8,128)(2,1)}, bf16[2,288,512]{2,1,0:T(8,128)(2,1)S(1)}, u32[]{:S(2)}, u32[]{:S(2)}) %collective-permute-start.1) | collective-permute-done | bytes 589856 | tf_op jit(solution)/shard_map/ppermute | solution.py:533
  28.9 2.4 %collective-permute-done.2.p2 = bf16[2,288,512]{2,1,0:T(8,128)(2,1)S(1)} collective-permute-done((bf16[2,288,512]{2,1,0:T(8,128)(2,1)}, bf16[2,288,512]{2,1,0:T(8,128)(2,1)S(1)}, u32[]{:S(2)}, u32[]{:S(2)}) %collective-permute-start.2) | collective-permute-done | bytes 589856 | tf_op jit(solution)/shard_map/ppermute | solution.py:533
  31.3 11.2 %collective-permute-done.3.p3 = bf16[2,288,512]{2,1,0:T(8,128)(2,1)S(1)} collective-permute-done((bf16[2,288,512]{2,1,0:T(8,128)(2,1)}, bf16[2,288,512]{2,1,0:T(8,128)(2,1)S(1)}, u32[]{:S(2)}, u32[]{:S(2)}) %collective-permute-start.3) | collective-permute-done | bytes 589856 | tf_op jit(solution)/shard_map/ppermute | solution.py:533
  42.5 1.4 shard_map.57
  44.8 4.2 %collective-permute-start.5 = (bf16[1024,256]{1,0:T(8,128)(2,1)S(1)}, bf16[1024,256]{1,0:T(8,128)(2,1)S(1)}, u32[]{:S(2)}, u32[]{:S(2)}) collective-permute-start(bf16[1024,256]{1,0:T(8,128)(2,1)S(1)} %get-tuple-element.27.y_column), channel_id=1, source_target_pairs={{8,16},{12,20},{16,8},{20,12},{9,17},{13,21},{17,9},{21,13},{10,18... | collective-permute-start | bytes 1572872 | tf_op jit(solution)/shard_map/ppermute | solution.py:554
  49.0 2.7 %collective-permute-start.8 = (bf16[4,64,512]{2,1,0:T(8,128)(2,1)S(1)}, bf16[4,64,512]{2,1,0:T(8,128)(2,1)S(1)}, u32[]{:S(2)}, u32[]{:S(2)}) collective-permute-start(bf16[4,64,512]{2,1,0:T(8,128)(2,1)S(1)} %bitcast.31), channel_id=1, source_target_pairs={{0,2},{1,3},{2,0},{3,1},{4,6},{5,7},{6,4},{7,5},{8,10},{9,11},{10,... | collective-permute-start | bytes 786440 | tf_op jit(solution)/shard_map/ppermute | solution.py:560
  52.9 1.6 %shard_map.58.rhs = bf16[2,2,512,512]{3,2,1,0:T(8,128)(2,1)S(1)} custom-call(s32[21]{0:T(128)S(1)} %stack.98.info, bf16[2,288,512]{2,1,0:T(8,128)(2,1)S(1)} %get-tuple-element.22.own, bf16[2,288,512]{2,1,0:T(8,128)(2,1)} %collective-permute-done.p0, bf16[2,288,512]{2,1,0:T(8,128)(2,1)S(1)} %collective-permute-done.1.p1, ...), custom_call_target="tpu_custom_call" | custom-call | tf_op jit(solution)/shard_map/pallas_call | solution.py:568
  54.5 8.8 %collective-permute-done.8.rows_far.c2 = bf16[4,64,512]{2,1,0:T(8,128)(2,1)S(1)} collective-permute-done((bf16[4,64,512]{2,1,0:T(8,128)(2,1)S(1)}, bf16[4,64,512]{2,1,0:T(8,128)(2,1)S(1)}, u32[]{:S(2)}, u32[]{:S(2)}) %collective-permute-start.8) | collective-permute-done | bytes 262176 | tf_op jit(solution)/shard_map/ppermute | solution.py:560
  65.8 1.9 %collective-permute-start.9 = (bf16[2,256,1024]{2,1,0:T(8,128)(2,1)S(1)}, bf16[2,256,1024]{2,1,0:T(8,128)(2,1)S(1)}, u32[]{:S(2)}, u32[]{:S(2)}) collective-permute-start(bf16[2,256,1024]{2,1,0:T(8,128)(2,1)S(1)} %get-tuple-element.29.xb), channel_id=1, source_target_pairs={{8,16},{12,20},{16,8},{20,12},{9,17},{13,21},{17,9},{21,13},{10,18... | collective-permute-start | bytes 3145736 | tf_op jit(solution)/shard_map/ppermute | solution.py:554
  67.7 1.2 collective-permute-start.12
  68.9 12.7 %collective-permute-done.12.c3 = bf16[4,64,512]{2,1,0:T(8,128)(2,1)S(1)} collective-permute-done((bf16[4,64,512]{2,1,0:T(8,128)(2,1)S(1)}, bf16[4,64,512]{2,1,0:T(8,128)(2,1)S(1)}, u32[]{:S(2)}, u32[]{:S(2)}) %collective-permute-start.12) | collective-permute-done | bytes 262176 | tf_op jit(solution)/shard_map/ppermute | solution.py:560
  81.6 2.3 %shard_map.60.weights = bf16[2,512,512]{2,1,0:T(8,128)(2,1)S(1)} custom-call(s32[21]{0:T(128)S(1)} %stack.98.info, bf16[4,64,512]{2,1,0:T(8,128)(2,1)S(1)} %bitcast.33, bf16[4,64,512]{2,1,0:T(8,128)(2,1)S(1)} %collective-permute-done.7.rows_next.c1, bf16[4,64,512]{2,1,0:T(8,128)(2,1)S(1)} %collective-permute-done.8.rows_far.c2, ...), custom_call_target="tpu_custom_call" | custom-call | tf_op jit(solution)/shard_map/pallas_call | solution.py:588
  84.0 5.2 %collective-permute-done.11.yf = bf16[2,1024,256]{2,1,0:T(8,128)(2,1)S(1)} collective-permute-done((bf16[2,1024,256]{2,1,0:T(8,128)(2,1)S(1)}, bf16[2,1024,256]{2,1,0:T(8,128)(2,1)S(1)}, u32[]{:S(2)}, u32[]{:S(2)}) %collective-permute-start.11) | collective-permute-done | bytes 1048608 | tf_op jit(solution)/shard_map/ppermute | solution.py:557
  90.6 1.3 collective-permute-start.13
  91.9 8.0 %collective-permute-done.13.arrived = bf16[2,512,512]{2,1,0:T(8,128)(2,1)S(1)} collective-permute-done((bf16[2,512,512]{2,1,0:T(8,128)(2,1)S(1)}, bf16[2,512,512]{2,1,0:T(8,128)(2,1)S(1)}, u32[]{:S(2)}, u32[]{:S(2)}) %collective-permute-start.13) | collective-permute-done | bytes 1048608 | tf_op jit(solution)/shard_map/ppermute | solution.py:621
  99.9 9.1 %shard_map.62 = (bf16[2,2,512,512]{3,2,1,0:T(8,128)(2,1)S(1)}, bf16[2,512,512]{2,1,0:T(8,128)(2,1)S(1)}) custom-call(s32[21]{0:T(128)S(1)} %stack.98.info, bf16[2,256,1024]{2,1,0:T(8,128)(2,1)S(1)} %get-tuple-element.29.xb, bf16[2,256,1024]{2,1,0:T(8,128)(2,1)S(1)} %collective-permute-done.9.x0, bf16[2,256,1024]{2,1,0:T(8,128)(2,1)S(1)} %collective-permute-done.10.x1, ...), custom_call_target="tpu_custom_call" | custom-call | flops 6442450944 | bytes 8388608 | tf_op jit(solution)/shard_map/pallas_call | solution.py:622
  109.1 1.4 collective-permute-start.14
  110.4 2.2 %collective-permute-done.14.arrived = bf16[2,512,512]{2,1,0:T(8,128)(2,1)S(1)} collective-permute-done((bf16[2,512,512]{2,1,0:T(8,128)(2,1)S(1)}, bf16[2,512,512]{2,1,0:T(8,128)(2,1)S(1)}, u32[]{:S(2)}, u32[]{:S(2)}) %collective-permute-start.14) | collective-permute-done | bytes 1048608 | tf_op jit(solution)/shard_map/ppermute | solution.py:633
  113.5 8.0 %collective-permute-start.17 = (bf16[2,256,512]{2,1,0:T(8,128)(2,1)S(1)}, bf16[2,256,512]{2,1,0:T(8,128)(2,1)S(1)}, u32[]{:S(2)}, u32[]{:S(2)}) collective-permute-start(bf16[2,256,512]{2,1,0:T(8,128)(2,1)S(1)} %get-tuple-element.37), channel_id=1, source_target_pairs={{4,0},{0,4},{20,8},{16,12},{12,16},{8,20},{28,24},{24,28},{5,1},{1... | collective-permute-start | bytes 1572872 | tf_op jit(solution)/shard_map/ppermute | solution.py:646
  121.4 2.3 %collective-permute-start.16 = (bf16[2,256,512]{2,1,0:T(8,128)(2,1)S(1)}, bf16[2,256,512]{2,1,0:T(8,128)(2,1)S(1)}, u32[]{:S(2)}, u32[]{:S(2)}) collective-permute-start(bf16[2,256,512]{2,1,0:T(8,128)(2,1)S(1)} %get-tuple-element.36.own), channel_id=1, source_target_pairs={{16,8},{20,12},{8,16},{12,20},{17,9},{21,13},{9,17},{13,21},{18,10... | collective-permute-start | bytes 1572872 | tf_op jit(solution)/shard_map/ppermute | solution.py:646
  123.8 4.6 %collective-permute-done.17.p1 = bf16[2,256,512]{2,1,0:T(8,128)(2,1)S(1)} collective-permute-done((bf16[2,256,512]{2,1,0:T(8,128)(2,1)S(1)}, bf16[2,256,512]{2,1,0:T(8,128)(2,1)S(1)}, u32[]{:S(2)}, u32[]{:S(2)}) %collective-permute-start.17) | collective-permute-done | bytes 524320 | tf_op jit(solution)/shard_map/ppermute | solution.py:646
  128.4 4.8 %collective-permute-done.18.p2 = bf16[2,256,512]{2,1,0:T(8,128)(2,1)S(1)} collective-permute-done((bf16[2,256,512]{2,1,0:T(8,128)(2,1)S(1)}, bf16[2,256,512]{2,1,0:T(8,128)(2,1)S(1)}, u32[]{:S(2)}, u32[]{:S(2)}) %collective-permute-start.18) | collective-permute-done | bytes 524320 | tf_op jit(solution)/shard_map/ppermute | solution.py:646
  133.2 5.6 %collective-permute-done.16.p0 = bf16[2,256,512]{2,1,0:T(8,128)(2,1)S(1)} collective-permute-done((bf16[2,256,512]{2,1,0:T(8,128)(2,1)S(1)}, bf16[2,256,512]{2,1,0:T(8,128)(2,1)S(1)}, u32[]{:S(2)}, u32[]{:S(2)}) %collective-permute-start.16) | collective-permute-done | bytes 524320 | tf_op jit(solution)/shard_map/ppermute | solution.py:646
  138.8 1.7 %shard_map.64.started = bf16[2,256,2048]{2,1,0:T(8,128)(2,1)} custom-call(s32[6]{0:T(128)S(1)} %stack.83.place, bf16[2,256,512]{2,1,0:T(8,128)(2,1)S(1)} %get-tuple-element.36.own, bf16[2,256,512]{2,1,0:T(8,128)(2,1)S(1)} %collective-permute-done.16.p0, bf16[2,256,512]{2,1,0:T(8,128)(2,1)S(1)} %collective-permute-done.17.p1, ...), custom_call_target="tpu_custom_call" | custom-call | tf_op jit(solution)/shard_map/pallas_call | solution.py:649
  140.6 3.9 %collective-permute-done.15.piece = bf16[2,256,512]{2,1,0:T(8,128)(2,1)S(1)} collective-permute-done((bf16[2,256,512]{2,1,0:T(8,128)(2,1)S(1)}, bf16[2,256,512]{2,1,0:T(8,128)(2,1)S(1)}, u32[]{:S(2)}, u32[]{:S(2)}) %collective-permute-start.15) | collective-permute-done | bytes 524320 | tf_op jit(solution)/shard_map/ppermute | solution.py:646
  144.5 1.3 shard_map.65
  (32 shorter events, 10.2 us)
Async XLA Ops:
  0.0 8.7 %copy-start.1 = (bf16[1,256,512]{2,1,0:T(8,128)(2,1)S(1)}, bf16[1,256,512]{2,1,0:T(8,128)(2,1)}, u32[]{:S(2)}) copy-start(bf16[1,256,512]{2,1,0:T(8,128)(2,1)} %param.7) | copy-start | bytes 786436
  0.0 0.9 copy-start.2
  1.0 0.9 copy-start.3
  3.2 16.5 %copy-start.4 = (s32[16]{0:T(128)S(1)}, s32[16]{0:T(128)}, u32[]{:S(2)}) copy-start(s32[16]{0:T(128)} %param.6) | copy-start | bytes 196
  3.2 39.3 %all-to-all-start = ((bf16[4,2,64,1024]{3,2,1,0:T(8,128)(2,1)}), bf16[4,2,64,1024]{3,2,1,0:T(8,128)(2,1)S(1)}, u32[]{:S(2)}, u32[]{:S(2)}) async-start(bf16[4,2,64,1024]{3,2,1,0:T(8,128)(2,1)} %shard_map.55), calls=%async_computation | async-start | bytes 2097152 | tf_op jit(solution)/shard_map/all_to_all | solution.py:535
  8.7 1.6 %copy-start = (bf16[2,1,256,2048]{3,2,1,0:T(8,128)(2,1)S(1)}, bf16[2,1,256,2048]{3,2,1,0:T(8,128)(2,1)}, u32[]{:S(2)}) copy-start(bf16[2,1,256,2048]{3,2,1,0:T(8,128)(2,1)} %param.5) | copy-start | bytes 6291460
  12.6 16.3 %collective-permute-start.1 = (bf16[2,288,512]{2,1,0:T(8,128)(2,1)}, bf16[2,288,512]{2,1,0:T(8,128)(2,1)S(1)}, u32[]{:S(2)}, u32[]{:S(2)}) collective-permute-start(bf16[2,288,512]{2,1,0:T(8,128)(2,1)} %get-tuple-element.23), channel_id=1, source_target_pairs={{0,4},{4,0},{8,20},{12,16},{16,12},{20,8},{24,28},{28,24},{1,5},{5... | collective-permute-start | bytes 1769480 | tf_op jit(solution)/shard_map/ppermute | solution.py:533
  15.7 15.6 %collective-permute-start.2 = (bf16[2,288,512]{2,1,0:T(8,128)(2,1)}, bf16[2,288,512]{2,1,0:T(8,128)(2,1)S(1)}, u32[]{:S(2)}, u32[]{:S(2)}) collective-permute-start(bf16[2,288,512]{2,1,0:T(8,128)(2,1)} %get-tuple-element.24), channel_id=1, source_target_pairs={{0,16},{4,20},{8,0},{12,4},{16,24},{20,28},{24,8},{28,12},{1,17},{... | collective-permute-start | bytes 1769480 | tf_op jit(solution)/shard_map/ppermute | solution.py:533
  15.7 26.8 %collective-permute-start.3 = (bf16[2,288,512]{2,1,0:T(8,128)(2,1)}, bf16[2,288,512]{2,1,0:T(8,128)(2,1)S(1)}, u32[]{:S(2)}, u32[]{:S(2)}) collective-permute-start(bf16[2,288,512]{2,1,0:T(8,128)(2,1)} %get-tuple-element.25), channel_id=1, source_target_pairs={{0,20},{4,16},{8,4},{12,0},{16,28},{20,24},{24,12},{28,8},{1,21},{... | collective-permute-start | bytes 1769480 | tf_op jit(solution)/shard_map/ppermute | solution.py:533
  16.3 26.2 %collective-permute-start = (bf16[2,288,512]{2,1,0:T(8,128)(2,1)S(1)}, bf16[2,288,512]{2,1,0:T(8,128)(2,1)}, u32[]{:S(2)}, u32[]{:S(2)}) collective-permute-start(bf16[2,288,512]{2,1,0:T(8,128)(2,1)S(1)} %get-tuple-element.22.own), channel_id=1, source_target_pairs={{8,16},{12,20},{16,8},{20,12},{9,17},{13,21},{17,9},{21,13},{10,18... | collective-permute-start | bytes 1769480 | tf_op jit(solution)/shard_map/ppermute | solution.py:533
  43.9 20.1 %collective-permute-start.4 = (bf16[256,1024]{1,0:T(8,128)(2,1)S(1)}, bf16[256,1024]{1,0:T(8,128)(2,1)S(1)}, u32[]{:S(2)}, u32[]{:S(2)}) collective-permute-start(bf16[256,1024]{1,0:T(8,128)(2,1)S(1)} %get-tuple-element.26.x_column), channel_id=1, source_target_pairs={{0,4},{4,0},{1,5},{5,1},{2,6},{6,2},{3,7},{7,3},{8,12},{12,8},{9,1... | collective-permute-start | bytes 1572872 | tf_op jit(solution)/shard_map/ppermute | solution.py:557
  44.8 19.1 %collective-permute-start.6 = (bf16[1024,256]{1,0:T(8,128)(2,1)S(1)}, bf16[1024,256]{1,0:T(8,128)(2,1)S(1)}, u32[]{:S(2)}, u32[]{:S(2)}) collective-permute-start(bf16[1024,256]{1,0:T(8,128)(2,1)S(1)} %get-tuple-element.27.y_column), channel_id=1, source_target_pairs={{0,16},{4,20},{8,0},{12,4},{16,24},{20,28},{24,8},{28,12},{1,17},{... | collective-permute-start | bytes 1572872 | tf_op jit(solution)/shard_map/ppermute | solution.py:554
  44.8 19.1 %collective-permute-start.5 = (bf16[1024,256]{1,0:T(8,128)(2,1)S(1)}, bf16[1024,256]{1,0:T(8,128)(2,1)S(1)}, u32[]{:S(2)}, u32[]{:S(2)}) collective-permute-start(bf16[1024,256]{1,0:T(8,128)(2,1)S(1)} %get-tuple-element.27.y_column), channel_id=1, source_target_pairs={{8,16},{12,20},{16,8},{20,12},{9,17},{13,21},{17,9},{21,13},{10,18... | collective-permute-start | bytes 1572872 | tf_op jit(solution)/shard_map/ppermute | solution.py:554
  49.0 14.4 %collective-permute-start.8 = (bf16[4,64,512]{2,1,0:T(8,128)(2,1)S(1)}, bf16[4,64,512]{2,1,0:T(8,128)(2,1)S(1)}, u32[]{:S(2)}, u32[]{:S(2)}) collective-permute-start(bf16[4,64,512]{2,1,0:T(8,128)(2,1)S(1)} %bitcast.31), channel_id=1, source_target_pairs={{0,2},{1,3},{2,0},{3,1},{4,6},{5,7},{6,4},{7,5},{8,10},{9,11},{10,... | collective-permute-start | bytes 786440 | tf_op jit(solution)/shard_map/ppermute | solution.py:560
  51.7 12.2 %collective-permute-start.7 = (bf16[4,64,512]{2,1,0:T(8,128)(2,1)S(1)}, bf16[4,64,512]{2,1,0:T(8,128)(2,1)S(1)}, u32[]{:S(2)}, u32[]{:S(2)}) collective-permute-start(bf16[4,64,512]{2,1,0:T(8,128)(2,1)S(1)} %bitcast.32), channel_id=1, source_target_pairs={{0,1},{1,0},{2,3},{3,2},{4,5},{5,4},{6,7},{7,6},{8,9},{9,8},{10,11... | collective-permute-start | bytes 786440 | tf_op jit(solution)/shard_map/ppermute | solution.py:560
  64.7 24.4 %collective-permute-start.11 = (bf16[2,1024,256]{2,1,0:T(8,128)(2,1)S(1)}, bf16[2,1024,256]{2,1,0:T(8,128)(2,1)S(1)}, u32[]{:S(2)}, u32[]{:S(2)}) collective-permute-start(bf16[2,1024,256]{2,1,0:T(8,128)(2,1)S(1)} %get-tuple-element.30.yb), channel_id=1, source_target_pairs={{0,4},{4,0},{1,5},{5,1},{2,6},{6,2},{3,7},{7,3},{8,12},{12,8},{9,1... | collective-permute-start | bytes 3145736 | tf_op jit(solution)/shard_map/ppermute | solution.py:557
  65.2 24.0 %collective-permute-start.10 = (bf16[2,256,1024]{2,1,0:T(8,128)(2,1)S(1)}, bf16[2,256,1024]{2,1,0:T(8,128)(2,1)S(1)}, u32[]{:S(2)}, u32[]{:S(2)}) collective-permute-start(bf16[2,256,1024]{2,1,0:T(8,128)(2,1)S(1)} %get-tuple-element.29.xb), channel_id=1, source_target_pairs={{0,16},{4,20},{8,0},{12,4},{16,24},{20,28},{24,8},{28,12},{1,17},{... | collective-permute-start | bytes 3145736 | tf_op jit(solution)/shard_map/ppermute | solution.py:554
  65.8 24.2 %collective-permute-start.9 = (bf16[2,256,1024]{2,1,0:T(8,128)(2,1)S(1)}, bf16[2,256,1024]{2,1,0:T(8,128)(2,1)S(1)}, u32[]{:S(2)}, u32[]{:S(2)}) collective-permute-start(bf16[2,256,1024]{2,1,0:T(8,128)(2,1)S(1)} %get-tuple-element.29.xb), channel_id=1, source_target_pairs={{8,16},{12,20},{16,8},{20,12},{9,17},{13,21},{17,9},{21,13},{10,18... | collective-permute-start | bytes 3145736 | tf_op jit(solution)/shard_map/ppermute | solution.py:554
  67.7 13.9 %collective-permute-start.12 = (bf16[4,64,512]{2,1,0:T(8,128)(2,1)S(1)}, bf16[4,64,512]{2,1,0:T(8,128)(2,1)S(1)}, u32[]{:S(2)}, u32[]{:S(2)}) collective-permute-start(bf16[4,64,512]{2,1,0:T(8,128)(2,1)S(1)} %collective-permute-done.7.rows_next.c1), channel_id=1, source_target_pairs={{0,2},{1,3},{2,0},{3,1},{4,6},{5,7},{6,4},{7,5},{8,10},{9,11},{10,... | collective-permute-start | bytes 786440 | tf_op jit(solution)/shard_map/ppermute | solution.py:560
  90.6 9.3 %collective-permute-start.13 = (bf16[2,512,512]{2,1,0:T(8,128)(2,1)S(1)}, bf16[2,512,512]{2,1,0:T(8,128)(2,1)S(1)}, u32[]{:S(2)}, u32[]{:S(2)}) collective-permute-start(bf16[2,512,512]{2,1,0:T(8,128)(2,1)S(1)} %get-tuple-element.32.w_high), channel_id=1, source_target_pairs={{0,8},{16,24},{1,9},{17,25},{2,10},{18,26},{3,11},{19,27},{4,12},{... | collective-permute-start | bytes 3145736 | tf_op jit(solution)/shard_map/ppermute | solution.py:621
  109.1 3.6 %collective-permute-start.14 = (bf16[2,512,512]{2,1,0:T(8,128)(2,1)S(1)}, bf16[2,512,512]{2,1,0:T(8,128)(2,1)S(1)}, u32[]{:S(2)}, u32[]{:S(2)}) collective-permute-start(bf16[2,512,512]{2,1,0:T(8,128)(2,1)S(1)} %get-tuple-element.33), channel_id=1, source_target_pairs={{8,0},{24,16},{9,1},{25,17},{10,2},{26,18},{11,3},{27,19},{12,4},{... | collective-permute-start | bytes 3145736 | tf_op jit(solution)/shard_map/ppermute | solution.py:633
  113.5 14.9 %collective-permute-start.17 = (bf16[2,256,512]{2,1,0:T(8,128)(2,1)S(1)}, bf16[2,256,512]{2,1,0:T(8,128)(2,1)S(1)}, u32[]{:S(2)}, u32[]{:S(2)}) collective-permute-start(bf16[2,256,512]{2,1,0:T(8,128)(2,1)S(1)} %get-tuple-element.37), channel_id=1, source_target_pairs={{4,0},{0,4},{20,8},{16,12},{12,16},{8,20},{28,24},{24,28},{5,1},{1... | collective-permute-start | bytes 1572872 | tf_op jit(solution)/shard_map/ppermute | solution.py:646
  121.4 11.8 %collective-permute-start.18 = (bf16[2,256,512]{2,1,0:T(8,128)(2,1)S(1)}, bf16[2,256,512]{2,1,0:T(8,128)(2,1)S(1)}, u32[]{:S(2)}, u32[]{:S(2)}) collective-permute-start(bf16[2,256,512]{2,1,0:T(8,128)(2,1)S(1)} %get-tuple-element.38), channel_id=1, source_target_pairs={{16,0},{20,4},{0,8},{4,12},{24,16},{28,20},{8,24},{12,28},{17,1},{... | collective-permute-start | bytes 1572872 | tf_op jit(solution)/shard_map/ppermute | solution.py:646
  121.4 17.4 %collective-permute-start.16 = (bf16[2,256,512]{2,1,0:T(8,128)(2,1)S(1)}, bf16[2,256,512]{2,1,0:T(8,128)(2,1)S(1)}, u32[]{:S(2)}, u32[]{:S(2)}) collective-permute-start(bf16[2,256,512]{2,1,0:T(8,128)(2,1)S(1)} %get-tuple-element.36.own), channel_id=1, source_target_pairs={{16,8},{20,12},{8,16},{12,20},{17,9},{21,13},{9,17},{13,21},{18,10... | collective-permute-start | bytes 1572872 | tf_op jit(solution)/shard_map/ppermute | solution.py:646
  123.7 20.8 %collective-permute-start.15 = (bf16[2,256,512]{2,1,0:T(8,128)(2,1)S(1)}, bf16[2,256,512]{2,1,0:T(8,128)(2,1)S(1)}, u32[]{:S(2)}, u32[]{:S(2)}) collective-permute-start(bf16[2,256,512]{2,1,0:T(8,128)(2,1)S(1)} %get-tuple-element.35), channel_id=1, source_target_pairs={{20,0},{16,4},{4,8},{0,12},{28,16},{24,20},{12,24},{8,28},{21,1},{... | collective-permute-start | bytes 1572872 | tf_op jit(solution)/shard_map/ppermute | solution.py:646

commit v14 on v13

--- a/solution.py
+++ b/solution.py
@@ -16,7 +16,7 @@
 in_smem = pl.BlockSpec(memory_space=pltpu.SMEM)
 in_vmem = pl.BlockSpec(memory_space=pltpu.VMEM)
 
-info_member, info_piece, info_slot, info_half, info_block, info_self = 3, 4, 12, 14, 16, 20
+info_member, info_piece, info_slot, info_half, info_self = 3, 4, 12, 14, 16
 
 
 def shifted(x, axis, by):
@@ -181,81 +181,48 @@
         self.received.wait()
 
 
-def block_kernel(x_factor, y_factor, blocks, sems):
-    order = x_factor.shape[2]
-    copies = []
-    for target in range(blocks.shape[0]):
-        for which, factor in enumerate((x_factor, y_factor)):
-            for plane in range(2):
-                copies.append(
-                    pltpu.make_async_copy(
-                        factor.at[plane],
-                        blocks.at[target, which, :, pl.ds(plane * order, order)],
-                        sems.at[target, which, plane],
-                    )
-                )
-    start_all(copies)
-    wait_all(copies)
-
-
-def pack_kernel(place, field, coupling, *rest):
+def pack_kernel(place, field, c0, c1, c2, c3, *rest):
     pieces, sems = rest[:-1], rest[-1]
-    rows_here = field.shape[1]
-    tall = coupling.shape[1]
-    own = pl.ds(2 * place[len(pieces)], 2)
     copies = []
     for index, piece in enumerate(pieces):
         width = piece.shape[2]
         offset = pl.multiple_of(place[index] * width, width)
-        copies += [
-            pltpu.make_async_copy(
-                field.at[:, :, pl.ds(offset, width)],
-                piece.at[:, pl.ds(0, rows_here), :],
-                sems.at[index, 0],
-            ),
-            pltpu.make_async_copy(
-                coupling.at[own], piece.at[:, pl.ds(rows_here, tall), :], sems.at[index, 1]
-            ),
-        ]
+        copies.append(
+            pltpu.make_async_copy(field.at[:, :, pl.ds(offset, width)], piece, sems.at[index])
+        )
     start_all(copies)
     wait_all(copies)
 
 
-def early_unpack_kernel(place, own, p0, p1, p2, field, sems):
+def early_unpack_kernel(place, p1, p2, p3, field, sems):
     copies = []
-    for index, piece in enumerate((p0, p1, p2)):
+    for index, piece in enumerate((p1, p2, p3)):
         width = piece.shape[2]
-        offset = pl.multiple_of(place[index] * width, width)
-        target = field.at[:, :, pl.ds(offset, width)]
-        if index:
-            copies.append(pltpu.make_async_copy(piece, target, sems.at[index]))
-        else:
-            copies.append(Either(place[5], own, piece, target, sems.at[index]))
+        offset = pl.multiple_of(place[index + 1] * width, width)
+        copies.append(
+            pltpu.make_async_copy(piece, field.at[:, :, pl.ds(offset, width)], sems.at[index])
+        )
     start_all(copies)
     wait_all(copies)
 
 
-def late_unpack_kernel(place, piece, started, field, sem):
+def late_unpack_kernel(place, own, piece, started, field, sem):
     width = piece.shape[2]
-    offset = pl.multiple_of(place[3] * width, width)
-    copy = pltpu.make_async_copy(piece, field.at[:, :, pl.ds(offset, width)], sem)
+    offset = pl.multiple_of(place[0] * width, width)
+    copy = Either(place[4], own, piece, field.at[:, :, pl.ds(offset, width)], sem)
     copy.start()
     copy.wait()
 
 
-def column_kernel(info, blocks, own, p0, p1, p2, p3, x_column, y_turned, rows_held, sems):
-    count, factors, height, width = blocks.shape
-    last = pl.ds(own.shape[1] - rows_held.shape[2], rows_held.shape[2])
-    parts = [piece.at[:, last, :] for piece in (p0, p1, p2, p3)]
-    copies = [Either(info[info_self], own.at[:, last, :], parts[0], rows_held.at[0], sems.at[0])]
-    for index in range(1, len(parts)):
-        copies.append(pltpu.make_async_copy(parts[index], rows_held.at[index], sems.at[index]))
-    start_all(copies)
+def column_kernel(blocks, weights, p0, p1, p2, p3, x_column, y_turned):
+    count, planes, height, order = blocks.shape
     for index in range(count):
-        x_column[index * height : (index + 1) * height] = blocks[index, 0]
-    column = blocks[:, 1].reshape(count * height, width)
-    y_turned[...] = column.astype(f32).T.astype(bf16)
-    wait_all(copies)
+        rows = slice(index * height, (index + 1) * height)
+        for plane in range(2):
+            x_column[rows, plane * order : (plane + 1) * order] = blocks[index, plane]
+    for plane in range(2):
+        column = blocks[:, 2 + plane].reshape(count * height, order)
+        y_turned[plane * order : (plane + 1) * order] = column.astype(f32).T.astype(bf16)
 
 
 def field_kernel(info, own, p0, p1, p2, p3, rhs, sems):
@@ -264,36 +231,29 @@
     for index, piece in enumerate((p0, p1, p2, p3)):
         slot, half = info[info_piece + 2 * index], info[info_piece + 2 * index + 1]
         rows = pl.ds(pl.multiple_of(half * height, height), height)
-        part = (slice(None), pl.ds(0, height), slice(None))
         ends = (rhs.at[slot, :, rows, :], sems.at[index])
-        if index:
-            copies.append(pltpu.make_async_copy(piece.at[part], *ends))
-        else:
-            copies.append(Either(info[info_self], own.at[part], piece.at[part], *ends))
+        copies.append(
+            pltpu.make_async_copy(piece, *ends) if index else Either(info[info_self], own, piece, *ends)
+        )
     start_all(copies)
     wait_all(copies)
 
 
-def weight_kernel(info, c0, c1, c2, c3, weights, sems):
-    height = c0.shape[1]
-    half_height = weights.shape[1] // 2
+def weight_kernel(info, own, c0, c1, c2, c3, weights, sems):
+    height = own.shape[0]
     copies = []
     for index, block in enumerate((c0, c1, c2, c3)):
-        for turn in range(block.shape[0]):
-            slot, half = info[info_piece + 2 * turn], info[info_piece + 2 * turn + 1]
-            start = half * half_height + info[info_block + index] * height
-            rows = pl.ds(pl.multiple_of(start, height), height)
-            copies.append(
-                pltpu.make_async_copy(
-                    block.at[turn], weights.at[slot, rows, :], sems.at[index, turn]
-                )
-            )
+        slot, half = info[info_piece + 2 * index], info[info_piece + 2 * index + 1]
+        rows = pl.ds(pl.multiple_of(half * height, height), height)
+        ends = (weights.at[slot, rows, :], sems.at[index])
+        copies.append(
+            pltpu.make_async_copy(block, *ends) if index else Either(info[info_self], own, block, *ends)
+        )
     start_all(copies)
     wait_all(copies)
 
 
-def both_kernel(info, x_column, x_aside, y_column, y0, y1, rows_next, rows_far, rhs, x_both, y_both,
-                sems):
+def both_kernel(info, x_column, x_aside, y_column, y0, y1, rhs, x_both, y_both, sems):
     copies = [
         pltpu.make_async_copy(x_column, x_both.at[0], sems.at[0]),
         pltpu.make_async_copy(x_aside, x_both.at[1], sems.at[1]),
@@ -502,53 +462,49 @@
     for a, b in rounds:
         entries += [(group + a) % 2, (own_x - b) % px_count]
     entries += [group, (group + 1) % 2, own_x, (own_x + 1) % 2]
-    pair = own_y // 2 * 2
-    entries += [own_y, pair + (own_y + 1) % 2, (own_y + 2) % 4, (pair + 2) % 4 + (own_y + 1) % 2]
     entries += [group == member]
     info = jnp.stack([jnp.asarray(entry, jnp.int32) for entry in entries])
 
     sends_to = jnp.stack(
         [((member + a) % 2) * px_count + (own_x + b) % px_count for a, b in rounds]
-        + [own_y, group == member]
+        + [group == member]
     ).astype(jnp.int32)
     piece_shape = jax.ShapeDtypeStruct((2, rows_here, order), bf16)
-    blocks = pl.pallas_call(
-        block_kernel,
-        out_shape=jax.ShapeDtypeStruct((py_count, 2, height, 2 * order), bf16),
-        in_specs=[in_hbm] * 2,
-        out_specs=in_vmem,
-        scratch_shapes=[pltpu.SemaphoreType.DMA((py_count, 2, 2))],
-        compiler_params=params,
-    )(x_factor[0], y_factor[0])
-    tall = height // 2
+    layer_rows = [lax.ppermute(coupling[0], ("sec", "px"), pairs(a, b)) for a, b in rounds]
+    shard = jnp.concatenate([x_factor[0], y_factor[0]], axis=0)
+    blocks = jnp.broadcast_to(shard[None], (py_count,) + shard.shape)
     packed = pl.pallas_call(
         pack_kernel,
-        out_shape=[jax.ShapeDtypeStruct((2, rows_here + tall, order), bf16)] * len(rounds),
-        in_specs=[in_smem] + [in_hbm] * 2,
+        out_shape=[piece_shape] * len(rounds),
+        in_specs=[in_smem] + [anywhere] * 5,
         out_specs=[in_vmem] * len(rounds),
-        scratch_shapes=[pltpu.SemaphoreType.DMA((len(rounds), 2))],
-        compiler_params=params,
-    )(sends_to, field, coupling[0].reshape(rows_here // tall, tall, order))
+        scratch_shapes=[pltpu.SemaphoreType.DMA((len(rounds),))],
+        compiler_params=params,
+    )(sends_to, field, *layer_rows)
     pieces = [
         lax.ppermute(piece, ("sec", "px"), pairs(a, b)) for piece, (a, b) in zip(packed, rounds)
     ]
     blocks = lax.all_to_all(blocks, "py", split_axis=0, concat_axis=0, tiled=True)
 
+    full_shape = jax.ShapeDtypeStruct((2, order, order), bf16)
+    double_shape = jax.ShapeDtypeStruct((2, 2, order, order), bf16)
+    weights = pl.pallas_call(
+        weight_kernel,
+        out_shape=full_shape,
+        in_specs=[in_smem] + [anywhere] * 5,
+        out_specs=in_vmem,
+        scratch_shapes=[pltpu.SemaphoreType.DMA((len(rounds),))],
+        compiler_params=params,
+    )(info, coupling[0], *layer_rows)
     column_shape = jax.ShapeDtypeStruct((rows_here, 2 * order), bf16)
     turned_shape = jax.ShapeDtypeStruct((2 * order, rows_here), bf16)
-    x_column, y_turned, rows_held = pl.pallas_call(
+    x_column, y_turned = pl.pallas_call(
         column_kernel,
-        out_shape=[
-            column_shape,
-            turned_shape,
-            jax.ShapeDtypeStruct((len(rounds), 2, tall, order), bf16),
-        ],
-        in_specs=[in_smem, in_vmem] + [anywhere] * 5,
-        out_specs=[in_vmem] * 3,
-        scratch_shapes=[pltpu.SemaphoreType.DMA((len(rounds),))],
-        compiler_params=params,
-    )(info, blocks, packed[0], *pieces)
-    rows_held = rows_held.reshape(len(rounds), height, order)
+        out_shape=[column_shape, turned_shape],
+        in_specs=[in_vmem] + [anywhere] * 5,
+        out_specs=[in_vmem] * 2,
+        compiler_params=params,
+    )(blocks, weights, *pieces)
 
     def across(block, a):
         return lax.ppermute(block, ("sec", "px"), pairs(a, 0))
@@ -556,15 +512,8 @@
     def aside(block):
         return lax.ppermute(block, "px", [(y, (y + 1) % 2) for y in range(2)])
 
-    def over_z(block, bit):
-        return lax.ppermute(block, "py", [(z, z ^ bit) for z in range(py_count)])
-
     y_near = [across(y_turned, a) for a in range(2)]
     x_aside = aside(x_column)
-    rows_next = over_z(rows_held, 1)
-    rows_far = over_z(rows_held, 2)
-    full_shape = jax.ShapeDtypeStruct((2, order, order), bf16)
-    double_shape = jax.ShapeDtypeStruct((2, 2, order, order), bf16)
     rhs = pl.pallas_call(
         field_kernel,
         out_shape=double_shape,
@@ -578,21 +527,13 @@
         out_shape=[
             jax.ShapeDtypeStruct((2,) + one.shape, bf16) for one in (column_shape, turned_shape)
         ],
-        in_specs=[in_smem] + [anywhere] * 8,
+        in_specs=[in_smem] + [anywhere] * 6,
         out_specs=[in_vmem] * 2,
         scratch_shapes=[pltpu.SemaphoreType.DMA((4,))],
         compiler_params=params,
-    )(info, x_column, x_aside, y_turned, *y_near, rows_next, rows_far, rhs)
+    )(info, x_column, x_aside, y_turned, *y_near, rhs)
     y_far = aside(y_both)
     x_across = [across(x_both, a) for a in range(2)]
-    weights = pl.pallas_call(
-        weight_kernel,
-        out_shape=full_shape,
-        in_specs=[in_smem] + [anywhere] * 4,
-        out_specs=in_vmem,
-        scratch_shapes=[pltpu.SemaphoreType.DMA((4, len(rounds)))],
-        compiler_params=params,
-    )(info, rows_held, rows_next, rows_far, over_z(rows_next, 2))
     layers = (info, x_both, *x_across, y_both, y_far, weights)
     layer_specs = [in_smem] + [anywhere] * 3 + [in_vmem] * 3
     solver_scratch = [
@@ -649,20 +590,20 @@
     started = pl.pallas_call(
         early_unpack_kernel,
         out_shape=whole_shape,
-        in_specs=[in_smem] + [in_vmem] * 4,
+        in_specs=[in_smem] + [in_vmem] * 3,
         out_specs=in_hbm,
         scratch_shapes=[pltpu.SemaphoreType.DMA((3,))],
         compiler_params=params,
-    )(sends_to, results[0], *received[:3])
+    )(sends_to, *received[1:])
     output = pl.pallas_call(
         late_unpack_kernel,
         out_shape=whole_shape,
-        in_specs=[in_smem, in_vmem, in_hbm],
+        in_specs=[in_smem, in_vmem, in_vmem, in_hbm],
         out_specs=in_hbm,
         scratch_shapes=[pltpu.SemaphoreType.DMA(())],
-        input_output_aliases={2: 0},
-        compiler_params=params,
-    )(sends_to, received[3], started)
+        input_output_aliases={3: 0},
+        compiler_params=params,
+    )(sends_to, results[0], received[0], started)
     return output[:, None]
 
 

time: 148 us -> 155 us (1.047)
  starting transfers between devices: 38.5 us -> 47.7 us
  Pallas kernels: 23.3 us -> 19.2 us
  local copies, waits for them, and re-layouts: 4.24 us -> 7.41 us
    ppermute x2, waiting for transfers between devices: 5.17 us -> 26.1 us  [aside(): return lax.ppermute(block, 'px', [(y, (y + 1) % 2) for y in range(2)])]
    ppermute x3 -> x4, waiting for transfers between devices: 22.1 us -> 7.85 us  [on_device(): lax.ppermute(coupling[0], ('sec', 'px'), pairs(a, b))]
    ppermute x4, waiting for transfers between devices: 19.5 us -> 11.2 us  [on_device(): lax.ppermute(piece, ('sec', 'px'), pairs(a, b))]
    ppermute x4, starting transfers between devices: 10.3 us -> 14.5 us  [on_device(): lax.ppermute(piece, ('sec', 'px'), back_pairs(a, b))]
    ppermute x4, waiting for transfers between devices: 0.92 us -> 4.12 us  [across(): return lax.ppermute(block, ('sec', 'px'), pairs(a, 0))]
    pallas_call x3 -> x2, Pallas kernels: 5.03 us -> 2.39 us  [the longest x1 2.18 us: on_device(): pl.pallas_call(pack_kernel, out_shape=[piece_shape] * len(rounds), in_spe...]
    unnamed x10 -> x20, local copies, waits for them, and re-layouts: 3.45 us -> 5.5 us
    ppermute x3 -> x4, starting transfers between devices: 5.07 us -> 6.99 us  [on_device(): lax.ppermute(coupling[0], ('sec', 'px'), pairs(a, b))]
  transfers between devices with their start and end apart: 20 -> 21, of which waited for: 14 -> 14; matrix products, arithmetic and copies ran while one was open for 1% -> 1% of each run, Pallas kernels for 5% -> 4%
where the time goes in v14:
time: 155 us; the launch traced here: 154 us
  waiting for transfers between devices  75.3 us (49%)
  starting transfers between devices  47.7 us (31%)
  Pallas kernels  19.2 us (12%)
  local copies, waits for them, and re-layouts  7.41 us (5%)
  between operations  3.17 us (2%)
    ppermute x2, waiting for transfers between devices, aside(): return lax.ppermute(block, 'px', [(y, (y + 1) % 2) for y in range(2)])  26.1 us
    ppermute x4, waiting for transfers between devices, on_device(): lax.ppermute(piece, ('sec', 'px'), back_pairs(a, b))  17.1 us
    ppermute x4, starting transfers between devices, on_device(): lax.ppermute(piece, ('sec', 'px'), back_pairs(a, b))  14.5 us
    ppermute x4, waiting for transfers between devices, on_device(): lax.ppermute(piece, ('sec', 'px'), pairs(a, b))  11.2 us
    pallas_call x1, Pallas kernels, on_device(): pl.pallas_call(last_kernel, out_shape=[double_shape, full_shape], in_spec...  9.09 us
    ppermute x4, starting transfers between devices, across(): return lax.ppermute(block, ('sec', 'px'), pairs(a, 0))  8.45 us
    ppermute x4, waiting for transfers between devices, on_device(): lax.ppermute(coupling[0], ('sec', 'px'), pairs(a, b))  7.85 us
    ppermute x4, starting transfers between devices, on_device(): lax.ppermute(piece, ('sec', 'px'), pairs(a, b))  7.76 us
  transfers between devices with their start and end apart: 21, of which 14 were waited for; matrix products, arithmetic and copies ran while one was open for 1% of the time, Pallas kernels for 4%

profile of v14, /device:TPU:1, one launch (start us, length us, event | category | flops | bytes accessed | tf_op | source)
XLA Modules:
  0.0 153.8 jit_solution(6708945671217210086)
XLA Ops:
  2.1 5.4 %all-to-all-start = ((bf16[4,4,64,512]{3,2,1,0:T(8,128)(2,1)}), bf16[4,4,64,512]{3,2,1,0:T(8,128)(2,1)S(1)}, u32[]{:S(2)}, u32[]{:S(2)}) async-start(bf16[4,4,64,512]{3,2,1,0:T(8,128)(2,1)} %broadcast_in_dim.4), calls=%async_computation | async-start | bytes 2097152 | tf_op jit(solution)/shard_map/all_to_all | solution.py:487
  7.5 2.1 %collective-permute-start.3 = (bf16[256,512]{1,0:T(8,128)(2,1)S(1)}, bf16[256,512]{1,0:T(8,128)(2,1)S(1)}, u32[]{:S(2)}, u32[]{:S(2)}) collective-permute-start(bf16[256,512]{1,0:T(8,128)(2,1)S(1)} %bitcast.25), channel_id=1, source_target_pairs={{0,20},{4,16},{8,4},{12,0},{16,28},{20,24},{24,12},{28,8},{1,21},{... | collective-permute-start | bytes 786440 | tf_op jit(solution)/shard_map/ppermute | solution.py:473
  9.6 1.3 collective-permute-start.2
  10.9 3.6 %collective-permute-start = (bf16[256,512]{1,0:T(8,128)(2,1)S(1)}, bf16[256,512]{1,0:T(8,128)(2,1)S(1)}, u32[]{:S(2)}, u32[]{:S(2)}) collective-permute-start(bf16[256,512]{1,0:T(8,128)(2,1)S(1)} %bitcast.28), channel_id=1, source_target_pairs={{8,16},{12,20},{16,8},{20,12},{9,17},{13,21},{17,9},{21,13},{10,18... | collective-permute-start | bytes 786440 | tf_op jit(solution)/shard_map/ppermute | solution.py:473
  14.7 6.5 %collective-permute-done.3.c3 = bf16[256,512]{1,0:T(8,128)(2,1)S(1)} collective-permute-done((bf16[256,512]{1,0:T(8,128)(2,1)S(1)}, bf16[256,512]{1,0:T(8,128)(2,1)S(1)}, u32[]{:S(2)}, u32[]{:S(2)}) %collective-permute-start.3) | collective-permute-done | bytes 262176 | tf_op jit(solution)/shard_map/ppermute | solution.py:473
  21.2 1.3 collective-permute-done.c0
  22.6 1.7 %copy-done = bf16[2,1,256,2048]{3,2,1,0:T(8,128)(2,1)S(1)} copy-done((bf16[2,1,256,2048]{3,2,1,0:T(8,128)(2,1)S(1)}, bf16[2,1,256,2048]{3,2,1,0:T(8,128)(2,1)}, u32[]{:S(2)}) %copy-start) | copy-done | bytes 2097176
  24.2 2.2 %shard_map.56 = (bf16[2,256,512]{2,1,0:T(8,128)(2,1)}, bf16[2,256,512]{2,1,0:T(8,128)(2,1)}, bf16[2,256,512]{2,1,0:T(8,128)(2,1)}, bf16[2,256,512]{2,1,0:T(8,128)(2,1)}) custom-call(s32[5]{0:T(128)S(1)} %stack.69.place, bf16[2,256,2048]{2,1,0:T(8,128)(2,1)S(1)} %bitcast.24, bf16[256,512]{1,0:T(8,128)(2,1)S(1)} %collective-permute-done.c0, ...), custom_call_target="tpu_custom_call" | custom-call | tf_op jit(solution)/shard_map/pallas_call | solution.py:476
  26.4 2.8 %collective-permute-start.5 = (bf16[2,256,512]{2,1,0:T(8,128)(2,1)}, bf16[2,256,512]{2,1,0:T(8,128)(2,1)S(1)}, u32[]{:S(2)}, u32[]{:S(2)}) collective-permute-start(bf16[2,256,512]{2,1,0:T(8,128)(2,1)} %get-tuple-element.22), channel_id=1, source_target_pairs={{0,4},{4,0},{8,20},{12,16},{16,12},{20,8},{24,28},{28,24},{1,5},{5... | collective-permute-start | bytes 1572872 | tf_op jit(solution)/shard_map/ppermute | solution.py:485
  29.9 4.3 %collective-permute-start.4 = (bf16[2,256,512]{2,1,0:T(8,128)(2,1)}, bf16[2,256,512]{2,1,0:T(8,128)(2,1)}, u32[]{:S(2)}, u32[]{:S(2)}) collective-permute-start(bf16[2,256,512]{2,1,0:T(8,128)(2,1)} %get-tuple-element.21.own), channel_id=1, source_target_pairs={{8,16},{12,20},{16,8},{20,12},{9,17},{13,21},{17,9},{21,13},{10,18... | collective-permute-start | bytes 1572872 | tf_op jit(solution)/shard_map/ppermute | solution.py:485
  42.2 1.3 collective-permute-done.6.p2
  43.5 9.8 %collective-permute-done.7.p3 = bf16[2,256,512]{2,1,0:T(8,128)(2,1)} collective-permute-done((bf16[2,256,512]{2,1,0:T(8,128)(2,1)}, bf16[2,256,512]{2,1,0:T(8,128)(2,1)}, u32[]{:S(2)}, u32[]{:S(2)}) %collective-permute-start.7) | collective-permute-done | bytes 524320 | tf_op jit(solution)/shard_map/ppermute | solution.py:485
  53.6 1.3 collective-permute-start.8
  54.9 3.8 %collective-permute-start.9 = (bf16[1024,256]{1,0:T(8,128)(2,1)S(1)}, bf16[1024,256]{1,0:T(8,128)(2,1)S(1)}, u32[]{:S(2)}, u32[]{:S(2)}) collective-permute-start(bf16[1024,256]{1,0:T(8,128)(2,1)S(1)} %get-tuple-element.26.y_column), channel_id=1, source_target_pairs={{8,16},{12,20},{16,8},{20,12},{9,17},{13,21},{17,9},{21,13},{10,18... | collective-permute-start | bytes 1572872 | tf_op jit(solution)/shard_map/ppermute | solution.py:510
  58.7 1.8 %shard_map.58.rhs = bf16[2,2,512,512]{3,2,1,0:T(8,128)(2,1)S(1)} custom-call(s32[17]{0:T(128)S(1)} %stack.81.info, bf16[2,256,512]{2,1,0:T(8,128)(2,1)} %get-tuple-element.21.own, bf16[2,256,512]{2,1,0:T(8,128)(2,1)} %collective-permute-done.4.p0, bf16[2,256,512]{2,1,0:T(8,128)(2,1)S(1)} %collective-permute-done.5.p1, ...), custom_call_target="tpu_custom_call" | custom-call | tf_op jit(solution)/shard_map/pallas_call | solution.py:517
  60.5 7.0 %collective-permute-done.8.x_aside = bf16[256,1024]{1,0:T(8,128)(2,1)S(1)} collective-permute-done((bf16[256,1024]{1,0:T(8,128)(2,1)S(1)}, bf16[256,1024]{1,0:T(8,128)(2,1)S(1)}, u32[]{:S(2)}, u32[]{:S(2)}) %collective-permute-start.8) | collective-permute-done | bytes 524320 | tf_op jit(solution)/shard_map/ppermute | solution.py:513
  67.5 1.6 %collective-permute-done.9.y0 = bf16[1024,256]{1,0:T(8,128)(2,1)S(1)} collective-permute-done((bf16[1024,256]{1,0:T(8,128)(2,1)S(1)}, bf16[1024,256]{1,0:T(8,128)(2,1)S(1)}, u32[]{:S(2)}, u32[]{:S(2)}) %collective-permute-start.9) | collective-permute-done | bytes 524320 | tf_op jit(solution)/shard_map/ppermute | solution.py:510
  70.5 4.7 %collective-permute-start.11 = (bf16[2,256,1024]{2,1,0:T(8,128)(2,1)S(1)}, bf16[2,256,1024]{2,1,0:T(8,128)(2,1)S(1)}, u32[]{:S(2)}, u32[]{:S(2)}) collective-permute-start(bf16[2,256,1024]{2,1,0:T(8,128)(2,1)S(1)} %get-tuple-element.27.xb), channel_id=1, source_target_pairs={{8,16},{12,20},{16,8},{20,12},{9,17},{13,21},{17,9},{21,13},{10,18... | collective-permute-start | bytes 3145736 | tf_op jit(solution)/shard_map/ppermute | solution.py:510
  75.2 19.1 %collective-permute-done.13.yf = bf16[2,1024,256]{2,1,0:T(8,128)(2,1)S(1)} collective-permute-done((bf16[2,1024,256]{2,1,0:T(8,128)(2,1)S(1)}, bf16[2,1024,256]{2,1,0:T(8,128)(2,1)S(1)}, u32[]{:S(2)}, u32[]{:S(2)}) %collective-permute-start.13) | collective-permute-done | bytes 1048608 | tf_op jit(solution)/shard_map/ppermute | solution.py:513
  94.3 2.5 %collective-permute-done.11.x0 = bf16[2,256,1024]{2,1,0:T(8,128)(2,1)S(1)} collective-permute-done((bf16[2,256,1024]{2,1,0:T(8,128)(2,1)S(1)}, bf16[2,256,1024]{2,1,0:T(8,128)(2,1)S(1)}, u32[]{:S(2)}, u32[]{:S(2)}) %collective-permute-start.11) | collective-permute-done | bytes 1048608 | tf_op jit(solution)/shard_map/ppermute | solution.py:510
  97.4 1.3 collective-permute-start.14
  98.7 6.7 %collective-permute-done.14.arrived = bf16[2,512,512]{2,1,0:T(8,128)(2,1)S(1)} collective-permute-done((bf16[2,512,512]{2,1,0:T(8,128)(2,1)S(1)}, bf16[2,512,512]{2,1,0:T(8,128)(2,1)S(1)}, u32[]{:S(2)}, u32[]{:S(2)}) %collective-permute-start.14) | collective-permute-done | bytes 1048608 | tf_op jit(solution)/shard_map/ppermute | solution.py:562
  105.5 9.1 %shard_map.61 = (bf16[2,2,512,512]{3,2,1,0:T(8,128)(2,1)S(1)}, bf16[2,512,512]{2,1,0:T(8,128)(2,1)S(1)}) custom-call(s32[17]{0:T(128)S(1)} %stack.81.info, bf16[2,256,1024]{2,1,0:T(8,128)(2,1)S(1)} %get-tuple-element.27.xb, bf16[2,256,1024]{2,1,0:T(8,128)(2,1)S(1)} %collective-permute-done.11.x0, bf16[2,256,1024]{2,1,0:T(8,128)(2,1)S(1)} %collective-permute-done.12.x1, ...), custom_call_target="tpu_custom_call" | custom-call | flops 6442450944 | bytes 8388608 | tf_op jit(solution)/shard_map/pallas_call | solution.py:563
  114.6 1.4 collective-permute-start.15
  115.9 2.2 %collective-permute-done.15.arrived = bf16[2,512,512]{2,1,0:T(8,128)(2,1)S(1)} collective-permute-done((bf16[2,512,512]{2,1,0:T(8,128)(2,1)S(1)}, bf16[2,512,512]{2,1,0:T(8,128)(2,1)S(1)}, u32[]{:S(2)}, u32[]{:S(2)}) %collective-permute-start.15) | collective-permute-done | bytes 1048608 | tf_op jit(solution)/shard_map/ppermute | solution.py:574
  119.0 10.1 %collective-permute-start.17 = (bf16[2,256,512]{2,1,0:T(8,128)(2,1)S(1)}, bf16[2,256,512]{2,1,0:T(8,128)(2,1)S(1)}, u32[]{:S(2)}, u32[]{:S(2)}) collective-permute-start(bf16[2,256,512]{2,1,0:T(8,128)(2,1)S(1)} %get-tuple-element.34), channel_id=1, source_target_pairs={{4,0},{0,4},{20,8},{16,12},{12,16},{8,20},{28,24},{24,28},{5,1},{1... | collective-permute-start | bytes 1572872 | tf_op jit(solution)/shard_map/ppermute | solution.py:587
  129.2 4.2 %collective-permute-start.16 = (bf16[2,256,512]{2,1,0:T(8,128)(2,1)S(1)}, bf16[2,256,512]{2,1,0:T(8,128)(2,1)S(1)}, u32[]{:S(2)}, u32[]{:S(2)}) collective-permute-start(bf16[2,256,512]{2,1,0:T(8,128)(2,1)S(1)} %get-tuple-element.33.own), channel_id=1, source_target_pairs={{16,8},{20,12},{8,16},{12,20},{17,9},{21,13},{9,17},{13,21},{18,10... | collective-permute-start | bytes 1572872 | tf_op jit(solution)/shard_map/ppermute | solution.py:587
  133.4 2.6 %collective-permute-done.17.p1 = bf16[2,256,512]{2,1,0:T(8,128)(2,1)S(1)} collective-permute-done((bf16[2,256,512]{2,1,0:T(8,128)(2,1)S(1)}, bf16[2,256,512]{2,1,0:T(8,128)(2,1)S(1)}, u32[]{:S(2)}, u32[]{:S(2)}) %collective-permute-start.17) | collective-permute-done | bytes 524320 | tf_op jit(solution)/shard_map/ppermute | solution.py:587
  136.0 4.8 %collective-permute-done.18.p2 = bf16[2,256,512]{2,1,0:T(8,128)(2,1)S(1)} collective-permute-done((bf16[2,256,512]{2,1,0:T(8,128)(2,1)S(1)}, bf16[2,256,512]{2,1,0:T(8,128)(2,1)S(1)}, u32[]{:S(2)}, u32[]{:S(2)}) %collective-permute-start.18) | collective-permute-done | bytes 524320 | tf_op jit(solution)/shard_map/ppermute | solution.py:587
  140.8 9.6 %collective-permute-done.19.p3 = bf16[2,256,512]{2,1,0:T(8,128)(2,1)S(1)} collective-permute-done((bf16[2,256,512]{2,1,0:T(8,128)(2,1)S(1)}, bf16[2,256,512]{2,1,0:T(8,128)(2,1)S(1)}, u32[]{:S(2)}, u32[]{:S(2)}) %collective-permute-start.19) | collective-permute-done | bytes 524320 | tf_op jit(solution)/shard_map/ppermute | solution.py:587
  150.4 1.7 %shard_map.63.started = bf16[2,256,2048]{2,1,0:T(8,128)(2,1)} custom-call(s32[5]{0:T(128)S(1)} %stack.69.place, bf16[2,256,512]{2,1,0:T(8,128)(2,1)S(1)} %collective-permute-done.17.p1, bf16[2,256,512]{2,1,0:T(8,128)(2,1)S(1)} %collective-permute-done.18.p2, bf16[2,256,512]{2,1,0:T(8,128)(2,1)S(1)} %collective-permute-done.19.p3), custom_call_target="tpu_custom_call" | custom-call | tf_op jit(solution)/shard_map/pallas_call | solution.py:590
  152.3 1.3 shard_map.64
  (45 shorter events, 11.4 us)
Async XLA Ops:
  0.0 7.5 %copy-start.7 = (bf16[1,256,512]{2,1,0:T(8,128)(2,1)S(1)}, bf16[1,256,512]{2,1,0:T(8,128)(2,1)}, u32[]{:S(2)}) copy-start(bf16[1,256,512]{2,1,0:T(8,128)(2,1)} %param.7) | copy-start | bytes 786436
  2.1 51.3 %all-to-all-start = ((bf16[4,4,64,512]{3,2,1,0:T(8,128)(2,1)}), bf16[4,4,64,512]{3,2,1,0:T(8,128)(2,1)S(1)}, u32[]{:S(2)}, u32[]{:S(2)}) async-start(bf16[4,4,64,512]{3,2,1,0:T(8,128)(2,1)} %broadcast_in_dim.4), calls=%async_computation | async-start | bytes 2097152 | tf_op jit(solution)/shard_map/all_to_all | solution.py:487
  7.5 26.7 %copy-start.9 = (s32[16]{0:T(128)S(1)}, s32[16]{0:T(128)}, u32[]{:S(2)}) copy-start(s32[16]{0:T(128)} %param.6) | copy-start | bytes 196
  7.5 13.7 %collective-permute-start.3 = (bf16[256,512]{1,0:T(8,128)(2,1)S(1)}, bf16[256,512]{1,0:T(8,128)(2,1)S(1)}, u32[]{:S(2)}, u32[]{:S(2)}) collective-permute-start(bf16[256,512]{1,0:T(8,128)(2,1)S(1)} %bitcast.25), channel_id=1, source_target_pairs={{0,20},{4,16},{8,4},{12,0},{16,28},{20,24},{24,12},{28,8},{1,21},{... | collective-permute-start | bytes 786440 | tf_op jit(solution)/shard_map/ppermute | solution.py:473
  9.6 11.6 %collective-permute-start.2 = (bf16[256,512]{1,0:T(8,128)(2,1)S(1)}, bf16[256,512]{1,0:T(8,128)(2,1)S(1)}, u32[]{:S(2)}, u32[]{:S(2)}) collective-permute-start(bf16[256,512]{1,0:T(8,128)(2,1)S(1)} %bitcast.26), channel_id=1, source_target_pairs={{0,16},{4,20},{8,0},{12,4},{16,24},{20,28},{24,8},{28,12},{1,17},{... | collective-permute-start | bytes 786440 | tf_op jit(solution)/shard_map/ppermute | solution.py:473
  10.9 10.3 %collective-permute-start.1 = (bf16[256,512]{1,0:T(8,128)(2,1)S(1)}, bf16[256,512]{1,0:T(8,128)(2,1)S(1)}, u32[]{:S(2)}, u32[]{:S(2)}) collective-permute-start(bf16[256,512]{1,0:T(8,128)(2,1)S(1)} %bitcast.27), channel_id=1, source_target_pairs={{0,4},{4,0},{8,20},{12,16},{16,12},{20,8},{24,28},{28,24},{1,5},{5... | collective-permute-start | bytes 786440 | tf_op jit(solution)/shard_map/ppermute | solution.py:473
  10.9 11.6 %collective-permute-start = (bf16[256,512]{1,0:T(8,128)(2,1)S(1)}, bf16[256,512]{1,0:T(8,128)(2,1)S(1)}, u32[]{:S(2)}, u32[]{:S(2)}) collective-permute-start(bf16[256,512]{1,0:T(8,128)(2,1)S(1)} %bitcast.28), channel_id=1, source_target_pairs={{8,16},{12,20},{16,8},{20,12},{9,17},{13,21},{17,9},{21,13},{10,18... | collective-permute-start | bytes 786440 | tf_op jit(solution)/shard_map/ppermute | solution.py:473
  21.2 16.4 %copy-start.1 = (bf16[256,512]{1,0:T(8,128)(2,1)}, bf16[256,512]{1,0:T(8,128)(2,1)S(1)}, u32[]{:S(2)}) copy-start(bf16[256,512]{1,0:T(8,128)(2,1)S(1)} %collective-permute-done.2.c2) | copy-start | bytes 786436
  21.2 16.4 %copy-start.3 = (bf16[256,512]{1,0:T(8,128)(2,1)}, bf16[256,512]{1,0:T(8,128)(2,1)S(1)}, u32[]{:S(2)}) copy-start(bf16[256,512]{1,0:T(8,128)(2,1)S(1)} %collective-permute-done.1.c1) | copy-start | bytes 786436
  22.6 15.0 %copy-start.5 = (bf16[256,512]{1,0:T(8,128)(2,1)}, bf16[256,512]{1,0:T(8,128)(2,1)S(1)}, u32[]{:S(2)}) copy-start(bf16[256,512]{1,0:T(8,128)(2,1)S(1)} %collective-permute-done.c0) | copy-start | bytes 786436
  22.6 1.7 %copy-start = (bf16[2,1,256,2048]{3,2,1,0:T(8,128)(2,1)S(1)}, bf16[2,1,256,2048]{3,2,1,0:T(8,128)(2,1)}, u32[]{:S(2)}) copy-start(bf16[2,1,256,2048]{3,2,1,0:T(8,128)(2,1)} %param.5) | copy-start | bytes 6291460
  26.4 15.8 %collective-permute-start.5 = (bf16[2,256,512]{2,1,0:T(8,128)(2,1)}, bf16[2,256,512]{2,1,0:T(8,128)(2,1)S(1)}, u32[]{:S(2)}, u32[]{:S(2)}) collective-permute-start(bf16[2,256,512]{2,1,0:T(8,128)(2,1)} %get-tuple-element.22), channel_id=1, source_target_pairs={{0,4},{4,0},{8,20},{12,16},{16,12},{20,8},{24,28},{28,24},{1,5},{5... | collective-permute-start | bytes 1572872 | tf_op jit(solution)/shard_map/ppermute | solution.py:485
  29.3 14.3 %collective-permute-start.6 = (bf16[2,256,512]{2,1,0:T(8,128)(2,1)}, bf16[2,256,512]{2,1,0:T(8,128)(2,1)S(1)}, u32[]{:S(2)}, u32[]{:S(2)}) collective-permute-start(bf16[2,256,512]{2,1,0:T(8,128)(2,1)} %get-tuple-element.23), channel_id=1, source_target_pairs={{0,16},{4,20},{8,0},{12,4},{16,24},{20,28},{24,8},{28,12},{1,17},{... | collective-permute-start | bytes 1572872 | tf_op jit(solution)/shard_map/ppermute | solution.py:485
  29.3 24.1 %collective-permute-start.7 = (bf16[2,256,512]{2,1,0:T(8,128)(2,1)}, bf16[2,256,512]{2,1,0:T(8,128)(2,1)}, u32[]{:S(2)}, u32[]{:S(2)}) collective-permute-start(bf16[2,256,512]{2,1,0:T(8,128)(2,1)} %get-tuple-element.24), channel_id=1, source_target_pairs={{0,20},{4,16},{8,4},{12,0},{16,28},{20,24},{24,12},{28,8},{1,21},{... | collective-permute-start | bytes 1572872 | tf_op jit(solution)/shard_map/ppermute | solution.py:485
  29.9 23.5 %collective-permute-start.4 = (bf16[2,256,512]{2,1,0:T(8,128)(2,1)}, bf16[2,256,512]{2,1,0:T(8,128)(2,1)}, u32[]{:S(2)}, u32[]{:S(2)}) collective-permute-start(bf16[2,256,512]{2,1,0:T(8,128)(2,1)} %get-tuple-element.21.own), channel_id=1, source_target_pairs={{8,16},{12,20},{16,8},{20,12},{9,17},{13,21},{17,9},{21,13},{10,18... | collective-permute-start | bytes 1572872 | tf_op jit(solution)/shard_map/ppermute | solution.py:485
  37.7 1.0 copy-start.2
  38.7 0.9 copy-start.4
  39.6 0.9 copy-start.6
  40.6 0.9 copy-start.8
  53.6 13.9 %collective-permute-start.8 = (bf16[256,1024]{1,0:T(8,128)(2,1)S(1)}, bf16[256,1024]{1,0:T(8,128)(2,1)S(1)}, u32[]{:S(2)}, u32[]{:S(2)}) collective-permute-start(bf16[256,1024]{1,0:T(8,128)(2,1)S(1)} %get-tuple-element.25.x_column), channel_id=1, source_target_pairs={{0,4},{4,0},{1,5},{5,1},{2,6},{6,2},{3,7},{7,3},{8,12},{12,8},{9,1... | collective-permute-start | bytes 1572872 | tf_op jit(solution)/shard_map/ppermute | solution.py:513
  54.9 12.6 %collective-permute-start.10 = (bf16[1024,256]{1,0:T(8,128)(2,1)S(1)}, bf16[1024,256]{1,0:T(8,128)(2,1)S(1)}, u32[]{:S(2)}, u32[]{:S(2)}) collective-permute-start(bf16[1024,256]{1,0:T(8,128)(2,1)S(1)} %get-tuple-element.26.y_column), channel_id=1, source_target_pairs={{0,16},{4,20},{8,0},{12,4},{16,24},{20,28},{24,8},{28,12},{1,17},{... | collective-permute-start | bytes 1572872 | tf_op jit(solution)/shard_map/ppermute | solution.py:510
  54.9 14.2 %collective-permute-start.9 = (bf16[1024,256]{1,0:T(8,128)(2,1)S(1)}, bf16[1024,256]{1,0:T(8,128)(2,1)S(1)}, u32[]{:S(2)}, u32[]{:S(2)}) collective-permute-start(bf16[1024,256]{1,0:T(8,128)(2,1)S(1)} %get-tuple-element.26.y_column), channel_id=1, source_target_pairs={{8,16},{12,20},{16,8},{20,12},{9,17},{13,21},{17,9},{21,13},{10,18... | collective-permute-start | bytes 1572872 | tf_op jit(solution)/shard_map/ppermute | solution.py:510
  69.9 24.5 %collective-permute-start.13 = (bf16[2,1024,256]{2,1,0:T(8,128)(2,1)S(1)}, bf16[2,1024,256]{2,1,0:T(8,128)(2,1)S(1)}, u32[]{:S(2)}, u32[]{:S(2)}) collective-permute-start(bf16[2,1024,256]{2,1,0:T(8,128)(2,1)S(1)} %get-tuple-element.28.yb), channel_id=1, source_target_pairs={{0,4},{4,0},{1,5},{5,1},{2,6},{6,2},{3,7},{7,3},{8,12},{12,8},{9,1... | collective-permute-start | bytes 3145736 | tf_op jit(solution)/shard_map/ppermute | solution.py:513
  70.5 23.8 %collective-permute-start.12 = (bf16[2,256,1024]{2,1,0:T(8,128)(2,1)S(1)}, bf16[2,256,1024]{2,1,0:T(8,128)(2,1)S(1)}, u32[]{:S(2)}, u32[]{:S(2)}) collective-permute-start(bf16[2,256,1024]{2,1,0:T(8,128)(2,1)S(1)} %get-tuple-element.27.xb), channel_id=1, source_target_pairs={{0,16},{4,20},{8,0},{12,4},{16,24},{20,28},{24,8},{28,12},{1,17},{... | collective-permute-start | bytes 3145736 | tf_op jit(solution)/shard_map/ppermute | solution.py:510
  70.5 26.3 %collective-permute-start.11 = (bf16[2,256,1024]{2,1,0:T(8,128)(2,1)S(1)}, bf16[2,256,1024]{2,1,0:T(8,128)(2,1)S(1)}, u32[]{:S(2)}, u32[]{:S(2)}) collective-permute-start(bf16[2,256,1024]{2,1,0:T(8,128)(2,1)S(1)} %get-tuple-element.27.xb), channel_id=1, source_target_pairs={{8,16},{12,20},{16,8},{20,12},{9,17},{13,21},{17,9},{21,13},{10,18... | collective-permute-start | bytes 3145736 | tf_op jit(solution)/shard_map/ppermute | solution.py:510
  97.4 8.0 %collective-permute-start.14 = (bf16[2,512,512]{2,1,0:T(8,128)(2,1)S(1)}, bf16[2,512,512]{2,1,0:T(8,128)(2,1)S(1)}, u32[]{:S(2)}, u32[]{:S(2)}) collective-permute-start(bf16[2,512,512]{2,1,0:T(8,128)(2,1)S(1)} %get-tuple-element.30.w_high), channel_id=1, source_target_pairs={{0,8},{16,24},{1,9},{17,25},{2,10},{18,26},{3,11},{19,27},{4,12},{... | collective-permute-start | bytes 3145736 | tf_op jit(solution)/shard_map/ppermute | solution.py:562
  114.6 3.6 %collective-permute-start.15 = (bf16[2,512,512]{2,1,0:T(8,128)(2,1)S(1)}, bf16[2,512,512]{2,1,0:T(8,128)(2,1)S(1)}, u32[]{:S(2)}, u32[]{:S(2)}) collective-permute-start(bf16[2,512,512]{2,1,0:T(8,128)(2,1)S(1)} %get-tuple-element.31), channel_id=1, source_target_pairs={{8,0},{24,16},{9,1},{25,17},{10,2},{26,18},{11,3},{27,19},{12,4},{... | collective-permute-start | bytes 3145736 | tf_op jit(solution)/shard_map/ppermute | solution.py:574
  119.0 17.1 %collective-permute-start.17 = (bf16[2,256,512]{2,1,0:T(8,128)(2,1)S(1)}, bf16[2,256,512]{2,1,0:T(8,128)(2,1)S(1)}, u32[]{:S(2)}, u32[]{:S(2)}) collective-permute-start(bf16[2,256,512]{2,1,0:T(8,128)(2,1)S(1)} %get-tuple-element.34), channel_id=1, source_target_pairs={{4,0},{0,4},{20,8},{16,12},{12,16},{8,20},{28,24},{24,28},{5,1},{1... | collective-permute-start | bytes 1572872 | tf_op jit(solution)/shard_map/ppermute | solution.py:587
  129.1 11.8 %collective-permute-start.18 = (bf16[2,256,512]{2,1,0:T(8,128)(2,1)S(1)}, bf16[2,256,512]{2,1,0:T(8,128)(2,1)S(1)}, u32[]{:S(2)}, u32[]{:S(2)}) collective-permute-start(bf16[2,256,512]{2,1,0:T(8,128)(2,1)S(1)} %get-tuple-element.35), channel_id=1, source_target_pairs={{16,0},{20,4},{0,8},{4,12},{24,16},{28,20},{8,24},{12,28},{17,1},{... | collective-permute-start | bytes 1572872 | tf_op jit(solution)/shard_map/ppermute | solution.py:587
  129.1 21.3 %collective-permute-start.19 = (bf16[2,256,512]{2,1,0:T(8,128)(2,1)S(1)}, bf16[2,256,512]{2,1,0:T(8,128)(2,1)S(1)}, u32[]{:S(2)}, u32[]{:S(2)}) collective-permute-start(bf16[2,256,512]{2,1,0:T(8,128)(2,1)S(1)} %get-tuple-element.36), channel_id=1, source_target_pairs={{20,0},{16,4},{4,8},{0,12},{28,16},{24,20},{12,24},{8,28},{21,1},{... | collective-permute-start | bytes 1572872 | tf_op jit(solution)/shard_map/ppermute | solution.py:587
  129.2 23.1 %collective-permute-start.16 = (bf16[2,256,512]{2,1,0:T(8,128)(2,1)S(1)}, bf16[2,256,512]{2,1,0:T(8,128)(2,1)S(1)}, u32[]{:S(2)}, u32[]{:S(2)}) collective-permute-start(bf16[2,256,512]{2,1,0:T(8,128)(2,1)S(1)} %get-tuple-element.33.own), channel_id=1, source_target_pairs={{16,8},{20,12},{8,16},{12,20},{17,9},{21,13},{9,17},{13,21},{18,10... | collective-permute-start | bytes 1572872 | tf_op jit(solution)/shard_map/ppermute | solution.py:587

commit v15 on v14

--- a/solution.py
+++ b/solution.py
@@ -12,7 +12,6 @@
 bf16 = jnp.bfloat16
 f32 = jnp.float32
 anywhere = pl.BlockSpec(memory_space=pl.ANY)
-in_hbm = pl.BlockSpec(memory_space=pltpu.HBM)
 in_smem = pl.BlockSpec(memory_space=pltpu.SMEM)
 in_vmem = pl.BlockSpec(memory_space=pltpu.VMEM)
 
@@ -181,7 +180,17 @@
         self.received.wait()
 
 
-def pack_kernel(place, field, c0, c1, c2, c3, *rest):
+def block_kernel(x_factor, y_factor, rows, blocks, sems):
+    copies = []
+    for target in range(blocks.shape[0]):
+        for which, factor in enumerate((x_factor, y_factor)):
+            part = blocks.at[target, pl.ds(2 * which, 2)]
+            copies.append(pltpu.make_async_copy(factor, part, sems.at[target, which]))
+    start_all(copies)
+    wait_all(copies)
+
+
+def pack_kernel(place, field, c1, c2, c3, *rest):
     pieces, sems = rest[:-1], rest[-1]
     copies = []
     for index, piece in enumerate(pieces):
@@ -194,24 +203,19 @@
     wait_all(copies)
 
 
-def early_unpack_kernel(place, p1, p2, p3, field, sems):
+def unpack_kernel(place, own, *rest):
+    pieces, field, sems = rest[:-2], rest[-2], rest[-1]
     copies = []
-    for index, piece in enumerate((p1, p2, p3)):
+    for index, piece in enumerate(pieces):
         width = piece.shape[2]
-        offset = pl.multiple_of(place[index + 1] * width, width)
-        copies.append(
-            pltpu.make_async_copy(piece, field.at[:, :, pl.ds(offset, width)], sems.at[index])
-        )
+        offset = pl.multiple_of(place[index] * width, width)
+        target = field.at[:, :, pl.ds(offset, width)]
+        if index:
+            copies.append(pltpu.make_async_copy(piece, target, sems.at[index]))
+        else:
+            copies.append(Either(place[len(pieces)], own, piece, target, sems.at[index]))
     start_all(copies)
     wait_all(copies)
-
-
-def late_unpack_kernel(place, own, piece, started, field, sem):
-    width = piece.shape[2]
-    offset = pl.multiple_of(place[0] * width, width)
-    copy = Either(place[4], own, piece, field.at[:, :, pl.ds(offset, width)], sem)
-    copy.start()
-    copy.wait()
 
 
 def column_kernel(blocks, weights, p0, p1, p2, p3, x_column, y_turned):
@@ -471,16 +475,22 @@
     ).astype(jnp.int32)
     piece_shape = jax.ShapeDtypeStruct((2, rows_here, order), bf16)
     layer_rows = [lax.ppermute(coupling[0], ("sec", "px"), pairs(a, b)) for a, b in rounds]
-    shard = jnp.concatenate([x_factor[0], y_factor[0]], axis=0)
-    blocks = jnp.broadcast_to(shard[None], (py_count,) + shard.shape)
+    blocks = pl.pallas_call(
+        block_kernel,
+        out_shape=jax.ShapeDtypeStruct((py_count, 4, height, order), bf16),
+        in_specs=[anywhere] * 3,
+        out_specs=in_vmem,
+        scratch_shapes=[pltpu.SemaphoreType.DMA((py_count, 2))],
+        compiler_params=params,
+    )(x_factor[0], y_factor[0], layer_rows[0])
     packed = pl.pallas_call(
         pack_kernel,
         out_shape=[piece_shape] * len(rounds),
-        in_specs=[in_smem] + [anywhere] * 5,
+        in_specs=[in_smem] + [anywhere] * 4,
         out_specs=[in_vmem] * len(rounds),
         scratch_shapes=[pltpu.SemaphoreType.DMA((len(rounds),))],
         compiler_params=params,
-    )(sends_to, field, *layer_rows)
+    )(sends_to, field, *layer_rows[1:])
     pieces = [
         lax.ppermute(piece, ("sec", "px"), pairs(a, b)) for piece, (a, b) in zip(packed, rounds)
     ]
@@ -586,24 +596,14 @@
     received = [
         lax.ppermute(piece, ("sec", "px"), back_pairs(a, b)) for piece, (a, b) in zip(results, rounds)
     ]
-    whole_shape = jax.ShapeDtypeStruct(field.shape, bf16)
-    started = pl.pallas_call(
-        early_unpack_kernel,
-        out_shape=whole_shape,
-        in_specs=[in_smem] + [in_vmem] * 3,
-        out_specs=in_hbm,
-        scratch_shapes=[pltpu.SemaphoreType.DMA((3,))],
-        compiler_params=params,
-    )(sends_to, *received[1:])
     output = pl.pallas_call(
-        late_unpack_kernel,
-        out_shape=whole_shape,
-        in_specs=[in_smem, in_vmem, in_vmem, in_hbm],
-        out_specs=in_hbm,
-        scratch_shapes=[pltpu.SemaphoreType.DMA(())],
-        input_output_aliases={3: 0},
-        compiler_params=params,
-    )(sends_to, results[0], received[0], started)
+        unpack_kernel,
+        out_shape=jax.ShapeDtypeStruct(field.shape, bf16),
+        in_specs=[in_smem] + [anywhere] * (len(rounds) + 1),
+        out_specs=in_vmem,
+        scratch_shapes=[pltpu.SemaphoreType.DMA((len(rounds),))],
+        compiler_params=params,
+    )(sends_to, results[0], *received)
     return output[:, None]
 
 

time: 155 us -> 164 us (1.058)
  waiting for transfers between devices: 75.3 us -> 82.1 us
    ppermute x4, waiting for transfers between devices: 7.85 us -> 12.9 us  [on_device(): lax.ppermute(coupling[0], ('sec', 'px'), pairs(a, b))]
    unnamed x20 -> x24, local copies, waits for them, and re-layouts: 5.5 us -> 7.99 us
    ppermute x4, waiting for transfers between devices: 17.1 us -> 18.9 us  [on_device(): lax.ppermute(piece, ('sec', 'px'), back_pairs(a, b))]
  transfers between devices with their start and end apart: 21 -> 21, of which waited for: 14 -> 16; matrix products, arithmetic and copies ran while one was open for 1% -> 1% of each run, Pallas kernels for 4% -> 3%
where the time goes in v15:
time: 164 us; the launch traced here: 163 us
  waiting for transfers between devices  82.1 us (50%)
  starting transfers between devices  48.3 us (29%)
  Pallas kernels  20.7 us (13%)
  local copies, waits for them, and re-layouts  8.82 us (5%)
  between operations  3.29 us (2%)
    ppermute x2, waiting for transfers between devices, aside(): return lax.ppermute(block, 'px', [(y, (y + 1) % 2) for y in range(2)])  25.7 us
    ppermute x4, waiting for transfers between devices, on_device(): lax.ppermute(piece, ('sec', 'px'), back_pairs(a, b))  18.9 us
    ppermute x4, starting transfers between devices, on_device(): lax.ppermute(piece, ('sec', 'px'), back_pairs(a, b))  14.5 us
    ppermute x4, waiting for transfers between devices, on_device(): lax.ppermute(coupling[0], ('sec', 'px'), pairs(a, b))  12.9 us
    ppermute x4, waiting for transfers between devices, on_device(): lax.ppermute(piece, ('sec', 'px'), pairs(a, b))  11.1 us
    pallas_call x1, Pallas kernels, on_device(): pl.pallas_call(last_kernel, out_shape=[double_shape, full_shape], in_spec...  9.09 us
    ppermute x4, starting transfers between devices, across(): return lax.ppermute(block, ('sec', 'px'), pairs(a, 0))  8.66 us
    ppermute x4, starting transfers between devices, on_device(): lax.ppermute(coupling[0], ('sec', 'px'), pairs(a, b))  8 us
  transfers between devices with their start and end apart: 21, of which 16 were waited for; matrix products, arithmetic and copies ran while one was open for 1% of the time, Pallas kernels for 3%

profile of v15, /device:TPU:1, one launch (start us, length us, event | category | flops | bytes accessed | tf_op | source)
XLA Modules:
  0.0 163.2 jit_solution(17775859376247723137)
XLA Ops:
  0.0 4.6 %collective-permute-start = (bf16[256,512]{1,0:T(8,128)(2,1)}, bf16[256,512]{1,0:T(8,128)(2,1)S(1)}, u32[]{:S(2)}, u32[]{:S(2)}) collective-permute-start(bf16[256,512]{1,0:T(8,128)(2,1)} %bitcast.25), channel_id=1, source_target_pairs={{8,16},{12,20},{16,8},{20,12},{9,17},{13,21},{17,9},{21,13},{10,18... | collective-permute-start | bytes 786440 | tf_op jit(solution)/shard_map/ppermute | solution.py:477
  4.6 4.3 %collective-permute-done.rows.c0 = bf16[256,512]{1,0:T(8,128)(2,1)S(1)} collective-permute-done((bf16[256,512]{1,0:T(8,128)(2,1)}, bf16[256,512]{1,0:T(8,128)(2,1)S(1)}, u32[]{:S(2)}, u32[]{:S(2)}) %collective-permute-start) | collective-permute-done | bytes 262176 | tf_op jit(solution)/shard_map/ppermute | solution.py:477
  10.7 2.4 %shard_map.55 = bf16[4,4,64,512]{3,2,1,0:T(8,128)(2,1)} custom-call(bf16[2,64,512]{2,1,0:T(8,128)(2,1)S(1)} %bitcast.30, bf16[2,64,512]{2,1,0:T(8,128)(2,1)S(1)} %bitcast.31, bf16[256,512]{1,0:T(8,128)(2,1)S(1)} %collective-permute-done.rows.c0), custom_call_target="tpu_custom_call" | custom-call | tf_op jit(solution)/shard_map/pallas_call | solution.py:478
  13.8 4.7 %all-to-all-start = ((bf16[4,4,64,512]{3,2,1,0:T(8,128)(2,1)}), bf16[4,4,64,512]{3,2,1,0:T(8,128)(2,1)S(1)}, u32[]{:S(2)}, u32[]{:S(2)}) async-start(bf16[4,4,64,512]{3,2,1,0:T(8,128)(2,1)} %shard_map.55), calls=%async_computation | async-start | bytes 2097152 | tf_op jit(solution)/shard_map/all_to_all | solution.py:497
  18.5 3.4 %collective-permute-start.2 = (bf16[256,512]{1,0:T(8,128)(2,1)S(1)}, bf16[256,512]{1,0:T(8,128)(2,1)S(1)}, u32[]{:S(2)}, u32[]{:S(2)}) collective-permute-start(bf16[256,512]{1,0:T(8,128)(2,1)S(1)} %bitcast.27), channel_id=1, source_target_pairs={{0,16},{4,20},{8,0},{12,4},{16,24},{20,28},{24,8},{28,12},{1,17},{... | collective-permute-start | bytes 786440 | tf_op jit(solution)/shard_map/ppermute | solution.py:477
  22.0 3.7 %collective-permute-done.3.c3 = bf16[256,512]{1,0:T(8,128)(2,1)S(1)} collective-permute-done((bf16[256,512]{1,0:T(8,128)(2,1)S(1)}, bf16[256,512]{1,0:T(8,128)(2,1)S(1)}, u32[]{:S(2)}, u32[]{:S(2)}) %collective-permute-start.3) | collective-permute-done | bytes 262176 | tf_op jit(solution)/shard_map/ppermute | solution.py:477
  25.6 4.9 %collective-permute-done.2.c2 = bf16[256,512]{1,0:T(8,128)(2,1)S(1)} collective-permute-done((bf16[256,512]{1,0:T(8,128)(2,1)S(1)}, bf16[256,512]{1,0:T(8,128)(2,1)S(1)}, u32[]{:S(2)}, u32[]{:S(2)}) %collective-permute-start.2) | collective-permute-done | bytes 262176 | tf_op jit(solution)/shard_map/ppermute | solution.py:477
  30.6 1.7 %copy-done = bf16[2,1,256,2048]{3,2,1,0:T(8,128)(2,1)S(1)} copy-done((bf16[2,1,256,2048]{3,2,1,0:T(8,128)(2,1)S(1)}, bf16[2,1,256,2048]{3,2,1,0:T(8,128)(2,1)}, u32[]{:S(2)}) %copy-start) | copy-done | bytes 2097176
  32.3 2.2 %shard_map.57 = (bf16[2,256,512]{2,1,0:T(8,128)(2,1)}, bf16[2,256,512]{2,1,0:T(8,128)(2,1)}, bf16[2,256,512]{2,1,0:T(8,128)(2,1)}, bf16[2,256,512]{2,1,0:T(8,128)(2,1)}) custom-call(s32[5]{0:T(128)S(1)} %stack.69.place, bf16[2,256,2048]{2,1,0:T(8,128)(2,1)S(1)} %bitcast.24, bf16[256,512]{1,0:T(8,128)(2,1)S(1)} %collective-permute-done.1.c1, ...), custom_call_target="tpu_custom_call" | custom-call | tf_op jit(solution)/shard_map/pallas_call | solution.py:486
  34.5 3.0 %collective-permute-start.5 = (bf16[2,256,512]{2,1,0:T(8,128)(2,1)}, bf16[2,256,512]{2,1,0:T(8,128)(2,1)S(1)}, u32[]{:S(2)}, u32[]{:S(2)}) collective-permute-start(bf16[2,256,512]{2,1,0:T(8,128)(2,1)} %get-tuple-element.22), channel_id=1, source_target_pairs={{0,4},{4,0},{8,20},{12,16},{16,12},{20,8},{24,28},{28,24},{1,5},{5... | collective-permute-start | bytes 1572872 | tf_op jit(solution)/shard_map/ppermute | solution.py:495
  38.2 4.0 %collective-permute-start.4 = (bf16[2,256,512]{2,1,0:T(8,128)(2,1)}, bf16[2,256,512]{2,1,0:T(8,128)(2,1)}, u32[]{:S(2)}, u32[]{:S(2)}) collective-permute-start(bf16[2,256,512]{2,1,0:T(8,128)(2,1)} %get-tuple-element.21.own), channel_id=1, source_target_pairs={{8,16},{12,20},{16,8},{20,12},{9,17},{13,21},{17,9},{21,13},{10,18... | collective-permute-start | bytes 1572872 | tf_op jit(solution)/shard_map/ppermute | solution.py:495
  50.4 1.4 collective-permute-done.6.p2
  51.8 9.7 %collective-permute-done.7.p3 = bf16[2,256,512]{2,1,0:T(8,128)(2,1)} collective-permute-done((bf16[2,256,512]{2,1,0:T(8,128)(2,1)}, bf16[2,256,512]{2,1,0:T(8,128)(2,1)}, u32[]{:S(2)}, u32[]{:S(2)}) %collective-permute-start.7) | collective-permute-done | bytes 524320 | tf_op jit(solution)/shard_map/ppermute | solution.py:495
  63.0 4.0 %collective-permute-start.9 = (bf16[1024,256]{1,0:T(8,128)(2,1)S(1)}, bf16[1024,256]{1,0:T(8,128)(2,1)S(1)}, u32[]{:S(2)}, u32[]{:S(2)}) collective-permute-start(bf16[1024,256]{1,0:T(8,128)(2,1)S(1)} %get-tuple-element.26.y_column), channel_id=1, source_target_pairs={{8,16},{12,20},{16,8},{20,12},{9,17},{13,21},{17,9},{21,13},{10,18... | collective-permute-start | bytes 1572872 | tf_op jit(solution)/shard_map/ppermute | solution.py:520
  67.0 1.8 %shard_map.59.rhs = bf16[2,2,512,512]{3,2,1,0:T(8,128)(2,1)S(1)} custom-call(s32[17]{0:T(128)S(1)} %stack.81.info, bf16[2,256,512]{2,1,0:T(8,128)(2,1)} %get-tuple-element.21.own, bf16[2,256,512]{2,1,0:T(8,128)(2,1)} %collective-permute-done.4.p0, bf16[2,256,512]{2,1,0:T(8,128)(2,1)S(1)} %collective-permute-done.5.p1, ...), custom_call_target="tpu_custom_call" | custom-call | tf_op jit(solution)/shard_map/pallas_call | solution.py:527
  68.8 6.9 %collective-permute-done.8.x_aside = bf16[256,1024]{1,0:T(8,128)(2,1)S(1)} collective-permute-done((bf16[256,1024]{1,0:T(8,128)(2,1)S(1)}, bf16[256,1024]{1,0:T(8,128)(2,1)S(1)}, u32[]{:S(2)}, u32[]{:S(2)}) %collective-permute-start.8) | collective-permute-done | bytes 524320 | tf_op jit(solution)/shard_map/ppermute | solution.py:523
  75.7 1.7 %collective-permute-done.9.y0 = bf16[1024,256]{1,0:T(8,128)(2,1)S(1)} collective-permute-done((bf16[1024,256]{1,0:T(8,128)(2,1)S(1)}, bf16[1024,256]{1,0:T(8,128)(2,1)S(1)}, u32[]{:S(2)}, u32[]{:S(2)}) %collective-permute-start.9) | collective-permute-done | bytes 524320 | tf_op jit(solution)/shard_map/ppermute | solution.py:520
  79.1 4.7 %collective-permute-start.11 = (bf16[2,256,1024]{2,1,0:T(8,128)(2,1)S(1)}, bf16[2,256,1024]{2,1,0:T(8,128)(2,1)S(1)}, u32[]{:S(2)}, u32[]{:S(2)}) collective-permute-start(bf16[2,256,1024]{2,1,0:T(8,128)(2,1)S(1)} %get-tuple-element.27.xb), channel_id=1, source_target_pairs={{8,16},{12,20},{16,8},{20,12},{9,17},{13,21},{17,9},{21,13},{10,18... | collective-permute-start | bytes 3145736 | tf_op jit(solution)/shard_map/ppermute | solution.py:520
  83.8 18.8 %collective-permute-done.13.yf = bf16[2,1024,256]{2,1,0:T(8,128)(2,1)S(1)} collective-permute-done((bf16[2,1024,256]{2,1,0:T(8,128)(2,1)S(1)}, bf16[2,1024,256]{2,1,0:T(8,128)(2,1)S(1)}, u32[]{:S(2)}, u32[]{:S(2)}) %collective-permute-start.13) | collective-permute-done | bytes 1048608 | tf_op jit(solution)/shard_map/ppermute | solution.py:523
  102.6 2.8 %collective-permute-done.11.x0 = bf16[2,256,1024]{2,1,0:T(8,128)(2,1)S(1)} collective-permute-done((bf16[2,256,1024]{2,1,0:T(8,128)(2,1)S(1)}, bf16[2,256,1024]{2,1,0:T(8,128)(2,1)S(1)}, u32[]{:S(2)}, u32[]{:S(2)}) %collective-permute-start.11) | collective-permute-done | bytes 1048608 | tf_op jit(solution)/shard_map/ppermute | solution.py:520
  106.0 1.3 collective-permute-start.14
  107.3 6.7 %collective-permute-done.14.arrived = bf16[2,512,512]{2,1,0:T(8,128)(2,1)S(1)} collective-permute-done((bf16[2,512,512]{2,1,0:T(8,128)(2,1)S(1)}, bf16[2,512,512]{2,1,0:T(8,128)(2,1)S(1)}, u32[]{:S(2)}, u32[]{:S(2)}) %collective-permute-start.14) | collective-permute-done | bytes 1048608 | tf_op jit(solution)/shard_map/ppermute | solution.py:572
  114.0 9.1 %shard_map.62 = (bf16[2,2,512,512]{3,2,1,0:T(8,128)(2,1)S(1)}, bf16[2,512,512]{2,1,0:T(8,128)(2,1)S(1)}) custom-call(s32[17]{0:T(128)S(1)} %stack.81.info, bf16[2,256,1024]{2,1,0:T(8,128)(2,1)S(1)} %get-tuple-element.27.xb, bf16[2,256,1024]{2,1,0:T(8,128)(2,1)S(1)} %collective-permute-done.11.x0, bf16[2,256,1024]{2,1,0:T(8,128)(2,1)S(1)} %collective-permute-done.12.x1, ...), custom_call_target="tpu_custom_call" | custom-call | flops 6442450944 | bytes 8388608 | tf_op jit(solution)/shard_map/pallas_call | solution.py:573
  123.1 1.4 collective-permute-start.15
  124.5 2.2 %collective-permute-done.15.arrived = bf16[2,512,512]{2,1,0:T(8,128)(2,1)S(1)} collective-permute-done((bf16[2,512,512]{2,1,0:T(8,128)(2,1)S(1)}, bf16[2,512,512]{2,1,0:T(8,128)(2,1)S(1)}, u32[]{:S(2)}, u32[]{:S(2)}) %collective-permute-start.15) | collective-permute-done | bytes 1048608 | tf_op jit(solution)/shard_map/ppermute | solution.py:584
  127.5 9.8 %collective-permute-start.17 = (bf16[2,256,512]{2,1,0:T(8,128)(2,1)S(1)}, bf16[2,256,512]{2,1,0:T(8,128)(2,1)S(1)}, u32[]{:S(2)}, u32[]{:S(2)}) collective-permute-start(bf16[2,256,512]{2,1,0:T(8,128)(2,1)S(1)} %get-tuple-element.34), channel_id=1, source_target_pairs={{4,0},{0,4},{20,8},{16,12},{12,16},{8,20},{28,24},{24,28},{5,1},{1... | collective-permute-start | bytes 1572872 | tf_op jit(solution)/shard_map/ppermute | solution.py:597
  137.4 4.6 %collective-permute-start.16 = (bf16[2,256,512]{2,1,0:T(8,128)(2,1)S(1)}, bf16[2,256,512]{2,1,0:T(8,128)(2,1)S(1)}, u32[]{:S(2)}, u32[]{:S(2)}) collective-permute-start(bf16[2,256,512]{2,1,0:T(8,128)(2,1)S(1)} %get-tuple-element.33.own), channel_id=1, source_target_pairs={{16,8},{20,12},{8,16},{12,20},{17,9},{21,13},{9,17},{13,21},{18,10... | collective-permute-start | bytes 1572872 | tf_op jit(solution)/shard_map/ppermute | solution.py:597
  142.0 2.3 %collective-permute-done.17.rest_1_ = bf16[2,256,512]{2,1,0:T(8,128)(2,1)S(1)} collective-permute-done((bf16[2,256,512]{2,1,0:T(8,128)(2,1)S(1)}, bf16[2,256,512]{2,1,0:T(8,128)(2,1)S(1)}, u32[]{:S(2)}, u32[]{:S(2)}) %collective-permute-start.17) | collective-permute-done | bytes 524320 | tf_op jit(solution)/shard_map/ppermute | solution.py:597
  144.3 4.8 %collective-permute-done.18.rest_2_ = bf16[2,256,512]{2,1,0:T(8,128)(2,1)S(1)} collective-permute-done((bf16[2,256,512]{2,1,0:T(8,128)(2,1)S(1)}, bf16[2,256,512]{2,1,0:T(8,128)(2,1)S(1)}, u32[]{:S(2)}, u32[]{:S(2)}) %collective-permute-start.18) | collective-permute-done | bytes 524320 | tf_op jit(solution)/shard_map/ppermute | solution.py:597
  149.1 9.9 %collective-permute-done.19.rest_3_ = bf16[2,256,512]{2,1,0:T(8,128)(2,1)S(1)} collective-permute-done((bf16[2,256,512]{2,1,0:T(8,128)(2,1)S(1)}, bf16[2,256,512]{2,1,0:T(8,128)(2,1)S(1)}, u32[]{:S(2)}, u32[]{:S(2)}) %collective-permute-start.19) | collective-permute-done | bytes 524320 | tf_op jit(solution)/shard_map/ppermute | solution.py:597
  159.0 1.9 %collective-permute-done.16.rest_0_ = bf16[2,256,512]{2,1,0:T(8,128)(2,1)S(1)} collective-permute-done((bf16[2,256,512]{2,1,0:T(8,128)(2,1)S(1)}, bf16[2,256,512]{2,1,0:T(8,128)(2,1)S(1)}, u32[]{:S(2)}, u32[]{:S(2)}) %collective-permute-start.16) | collective-permute-done | bytes 524320 | tf_op jit(solution)/shard_map/ppermute | solution.py:597
  160.9 2.2 %shard_map.64 = bf16[2,256,2048]{2,1,0:T(8,128)(2,1)} custom-call(s32[5]{0:T(128)S(1)} %stack.69.place, bf16[2,256,512]{2,1,0:T(8,128)(2,1)S(1)} %get-tuple-element.33.own, bf16[2,256,512]{2,1,0:T(8,128)(2,1)S(1)} %collective-permute-done.16.rest_0_, bf16[2,256,512]{2,1,0:T(8,128)(2,1)S(1)} %collective-permute-done.17.rest_1_, ...), custom_call_target="tpu_custom_call" | custom-call | tf_op jit(solution)/shard_map/pallas_call | solution.py:599
  (47 shorter events, 13.3 us)
Async XLA Ops:
  0.0 18.5 %copy-start.7 = (bf16[1,256,512]{2,1,0:T(8,128)(2,1)S(1)}, bf16[1,256,512]{2,1,0:T(8,128)(2,1)}, u32[]{:S(2)}) copy-start(bf16[1,256,512]{2,1,0:T(8,128)(2,1)} %param.7) | copy-start | bytes 786436
  0.0 8.9 %collective-permute-start = (bf16[256,512]{1,0:T(8,128)(2,1)}, bf16[256,512]{1,0:T(8,128)(2,1)S(1)}, u32[]{:S(2)}, u32[]{:S(2)}) collective-permute-start(bf16[256,512]{1,0:T(8,128)(2,1)} %bitcast.25), channel_id=1, source_target_pairs={{8,16},{12,20},{16,8},{20,12},{9,17},{13,21},{17,9},{21,13},{10,18... | collective-permute-start | bytes 786440 | tf_op jit(solution)/shard_map/ppermute | solution.py:477
  8.9 0.9 copy-start.9
  9.8 0.9 copy-start.10
  13.8 28.5 %copy-start.11 = (s32[16]{0:T(128)S(1)}, s32[16]{0:T(128)}, u32[]{:S(2)}) copy-start(s32[16]{0:T(128)} %param.6) | copy-start | bytes 196
  13.8 47.8 %all-to-all-start = ((bf16[4,4,64,512]{3,2,1,0:T(8,128)(2,1)}), bf16[4,4,64,512]{3,2,1,0:T(8,128)(2,1)S(1)}, u32[]{:S(2)}, u32[]{:S(2)}) async-start(bf16[4,4,64,512]{3,2,1,0:T(8,128)(2,1)} %shard_map.55), calls=%async_computation | async-start | bytes 2097152 | tf_op jit(solution)/shard_map/all_to_all | solution.py:497
  18.5 7.1 %collective-permute-start.3 = (bf16[256,512]{1,0:T(8,128)(2,1)S(1)}, bf16[256,512]{1,0:T(8,128)(2,1)S(1)}, u32[]{:S(2)}, u32[]{:S(2)}) collective-permute-start(bf16[256,512]{1,0:T(8,128)(2,1)S(1)} %bitcast.26), channel_id=1, source_target_pairs={{0,20},{4,16},{8,4},{12,0},{16,28},{20,24},{24,12},{28,8},{1,21},{... | collective-permute-start | bytes 786440 | tf_op jit(solution)/shard_map/ppermute | solution.py:477
  18.5 12.0 %collective-permute-start.2 = (bf16[256,512]{1,0:T(8,128)(2,1)S(1)}, bf16[256,512]{1,0:T(8,128)(2,1)S(1)}, u32[]{:S(2)}, u32[]{:S(2)}) collective-permute-start(bf16[256,512]{1,0:T(8,128)(2,1)S(1)} %bitcast.27), channel_id=1, source_target_pairs={{0,16},{4,20},{8,0},{12,4},{16,24},{20,28},{24,8},{28,12},{1,17},{... | collective-permute-start | bytes 786440 | tf_op jit(solution)/shard_map/ppermute | solution.py:477
  21.9 8.8 %collective-permute-start.1 = (bf16[256,512]{1,0:T(8,128)(2,1)S(1)}, bf16[256,512]{1,0:T(8,128)(2,1)S(1)}, u32[]{:S(2)}, u32[]{:S(2)}) collective-permute-start(bf16[256,512]{1,0:T(8,128)(2,1)S(1)} %bitcast.28), channel_id=1, source_target_pairs={{0,4},{4,0},{8,20},{12,16},{16,12},{20,8},{24,28},{28,24},{1,5},{5... | collective-permute-start | bytes 786440 | tf_op jit(solution)/shard_map/ppermute | solution.py:477
  30.5 15.3 %copy-start.1 = (bf16[256,512]{1,0:T(8,128)(2,1)}, bf16[256,512]{1,0:T(8,128)(2,1)S(1)}, u32[]{:S(2)}) copy-start(bf16[256,512]{1,0:T(8,128)(2,1)S(1)} %collective-permute-done.2.c2) | copy-start | bytes 786436
  30.6 15.2 %copy-start.3 = (bf16[256,512]{1,0:T(8,128)(2,1)}, bf16[256,512]{1,0:T(8,128)(2,1)S(1)}, u32[]{:S(2)}) copy-start(bf16[256,512]{1,0:T(8,128)(2,1)S(1)} %collective-permute-done.1.c1) | copy-start | bytes 786436
  30.6 1.7 %copy-start = (bf16[2,1,256,2048]{3,2,1,0:T(8,128)(2,1)S(1)}, bf16[2,1,256,2048]{3,2,1,0:T(8,128)(2,1)}, u32[]{:S(2)}) copy-start(bf16[2,1,256,2048]{3,2,1,0:T(8,128)(2,1)} %param.5) | copy-start | bytes 6291460
  34.5 15.9 %collective-permute-start.5 = (bf16[2,256,512]{2,1,0:T(8,128)(2,1)}, bf16[2,256,512]{2,1,0:T(8,128)(2,1)S(1)}, u32[]{:S(2)}, u32[]{:S(2)}) collective-permute-start(bf16[2,256,512]{2,1,0:T(8,128)(2,1)} %get-tuple-element.22), channel_id=1, source_target_pairs={{0,4},{4,0},{8,20},{12,16},{16,12},{20,8},{24,28},{28,24},{1,5},{5... | collective-permute-start | bytes 1572872 | tf_op jit(solution)/shard_map/ppermute | solution.py:495
  37.5 14.3 %collective-permute-start.6 = (bf16[2,256,512]{2,1,0:T(8,128)(2,1)}, bf16[2,256,512]{2,1,0:T(8,128)(2,1)S(1)}, u32[]{:S(2)}, u32[]{:S(2)}) collective-permute-start(bf16[2,256,512]{2,1,0:T(8,128)(2,1)} %get-tuple-element.23), channel_id=1, source_target_pairs={{0,16},{4,20},{8,0},{12,4},{16,24},{20,28},{24,8},{28,12},{1,17},{... | collective-permute-start | bytes 1572872 | tf_op jit(solution)/shard_map/ppermute | solution.py:495
  37.5 24.0 %collective-permute-start.7 = (bf16[2,256,512]{2,1,0:T(8,128)(2,1)}, bf16[2,256,512]{2,1,0:T(8,128)(2,1)}, u32[]{:S(2)}, u32[]{:S(2)}) collective-permute-start(bf16[2,256,512]{2,1,0:T(8,128)(2,1)} %get-tuple-element.24), channel_id=1, source_target_pairs={{0,20},{4,16},{8,4},{12,0},{16,28},{20,24},{24,12},{28,8},{1,21},{... | collective-permute-start | bytes 1572872 | tf_op jit(solution)/shard_map/ppermute | solution.py:495
  38.2 23.3 %collective-permute-start.4 = (bf16[2,256,512]{2,1,0:T(8,128)(2,1)}, bf16[2,256,512]{2,1,0:T(8,128)(2,1)}, u32[]{:S(2)}, u32[]{:S(2)}) collective-permute-start(bf16[2,256,512]{2,1,0:T(8,128)(2,1)} %get-tuple-element.21.own), channel_id=1, source_target_pairs={{8,16},{12,20},{16,8},{20,12},{9,17},{13,21},{17,9},{21,13},{10,18... | collective-permute-start | bytes 1572872 | tf_op jit(solution)/shard_map/ppermute | solution.py:495
  45.9 1.0 copy-start.2
  46.9 0.9 copy-start.4
  47.8 0.9 copy-start.6
  48.8 0.9 copy-start.8
  61.8 13.9 %collective-permute-start.8 = (bf16[256,1024]{1,0:T(8,128)(2,1)S(1)}, bf16[256,1024]{1,0:T(8,128)(2,1)S(1)}, u32[]{:S(2)}, u32[]{:S(2)}) collective-permute-start(bf16[256,1024]{1,0:T(8,128)(2,1)S(1)} %get-tuple-element.25.x_column), channel_id=1, source_target_pairs={{0,4},{4,0},{1,5},{5,1},{2,6},{6,2},{3,7},{7,3},{8,12},{12,8},{9,1... | collective-permute-start | bytes 1572872 | tf_op jit(solution)/shard_map/ppermute | solution.py:523
  63.0 12.7 %collective-permute-start.10 = (bf16[1024,256]{1,0:T(8,128)(2,1)S(1)}, bf16[1024,256]{1,0:T(8,128)(2,1)S(1)}, u32[]{:S(2)}, u32[]{:S(2)}) collective-permute-start(bf16[1024,256]{1,0:T(8,128)(2,1)S(1)} %get-tuple-element.26.y_column), channel_id=1, source_target_pairs={{0,16},{4,20},{8,0},{12,4},{16,24},{20,28},{24,8},{28,12},{1,17},{... | collective-permute-start | bytes 1572872 | tf_op jit(solution)/shard_map/ppermute | solution.py:520
  63.0 14.4 %collective-permute-start.9 = (bf16[1024,256]{1,0:T(8,128)(2,1)S(1)}, bf16[1024,256]{1,0:T(8,128)(2,1)S(1)}, u32[]{:S(2)}, u32[]{:S(2)}) collective-permute-start(bf16[1024,256]{1,0:T(8,128)(2,1)S(1)} %get-tuple-element.26.y_column), channel_id=1, source_target_pairs={{8,16},{12,20},{16,8},{20,12},{9,17},{13,21},{17,9},{21,13},{10,18... | collective-permute-start | bytes 1572872 | tf_op jit(solution)/shard_map/ppermute | solution.py:520
  78.1 24.5 %collective-permute-start.13 = (bf16[2,1024,256]{2,1,0:T(8,128)(2,1)S(1)}, bf16[2,1024,256]{2,1,0:T(8,128)(2,1)S(1)}, u32[]{:S(2)}, u32[]{:S(2)}) collective-permute-start(bf16[2,1024,256]{2,1,0:T(8,128)(2,1)S(1)} %get-tuple-element.28.yb), channel_id=1, source_target_pairs={{0,4},{4,0},{1,5},{5,1},{2,6},{6,2},{3,7},{7,3},{8,12},{12,8},{9,1... | collective-permute-start | bytes 3145736 | tf_op jit(solution)/shard_map/ppermute | solution.py:523
  79.1 23.5 %collective-permute-start.12 = (bf16[2,256,1024]{2,1,0:T(8,128)(2,1)S(1)}, bf16[2,256,1024]{2,1,0:T(8,128)(2,1)S(1)}, u32[]{:S(2)}, u32[]{:S(2)}) collective-permute-start(bf16[2,256,1024]{2,1,0:T(8,128)(2,1)S(1)} %get-tuple-element.27.xb), channel_id=1, source_target_pairs={{0,16},{4,20},{8,0},{12,4},{16,24},{20,28},{24,8},{28,12},{1,17},{... | collective-permute-start | bytes 3145736 | tf_op jit(solution)/shard_map/ppermute | solution.py:520
  79.1 26.3 %collective-permute-start.11 = (bf16[2,256,1024]{2,1,0:T(8,128)(2,1)S(1)}, bf16[2,256,1024]{2,1,0:T(8,128)(2,1)S(1)}, u32[]{:S(2)}, u32[]{:S(2)}) collective-permute-start(bf16[2,256,1024]{2,1,0:T(8,128)(2,1)S(1)} %get-tuple-element.27.xb), channel_id=1, source_target_pairs={{8,16},{12,20},{16,8},{20,12},{9,17},{13,21},{17,9},{21,13},{10,18... | collective-permute-start | bytes 3145736 | tf_op jit(solution)/shard_map/ppermute | solution.py:520
  106.0 8.0 %collective-permute-start.14 = (bf16[2,512,512]{2,1,0:T(8,128)(2,1)S(1)}, bf16[2,512,512]{2,1,0:T(8,128)(2,1)S(1)}, u32[]{:S(2)}, u32[]{:S(2)}) collective-permute-start(bf16[2,512,512]{2,1,0:T(8,128)(2,1)S(1)} %get-tuple-element.30.w_high), channel_id=1, source_target_pairs={{0,8},{16,24},{1,9},{17,25},{2,10},{18,26},{3,11},{19,27},{4,12},{... | collective-permute-start | bytes 3145736 | tf_op jit(solution)/shard_map/ppermute | solution.py:572
  123.1 3.6 %collective-permute-start.15 = (bf16[2,512,512]{2,1,0:T(8,128)(2,1)S(1)}, bf16[2,512,512]{2,1,0:T(8,128)(2,1)S(1)}, u32[]{:S(2)}, u32[]{:S(2)}) collective-permute-start(bf16[2,512,512]{2,1,0:T(8,128)(2,1)S(1)} %get-tuple-element.31), channel_id=1, source_target_pairs={{8,0},{24,16},{9,1},{25,17},{10,2},{26,18},{11,3},{27,19},{12,4},{... | collective-permute-start | bytes 3145736 | tf_op jit(solution)/shard_map/ppermute | solution.py:584
  127.5 16.7 %collective-permute-start.17 = (bf16[2,256,512]{2,1,0:T(8,128)(2,1)S(1)}, bf16[2,256,512]{2,1,0:T(8,128)(2,1)S(1)}, u32[]{:S(2)}, u32[]{:S(2)}) collective-permute-start(bf16[2,256,512]{2,1,0:T(8,128)(2,1)S(1)} %get-tuple-element.34), channel_id=1, source_target_pairs={{4,0},{0,4},{20,8},{16,12},{12,16},{8,20},{28,24},{24,28},{5,1},{1... | collective-permute-start | bytes 1572872 | tf_op jit(solution)/shard_map/ppermute | solution.py:597
  137.3 11.8 %collective-permute-start.18 = (bf16[2,256,512]{2,1,0:T(8,128)(2,1)S(1)}, bf16[2,256,512]{2,1,0:T(8,128)(2,1)S(1)}, u32[]{:S(2)}, u32[]{:S(2)}) collective-permute-start(bf16[2,256,512]{2,1,0:T(8,128)(2,1)S(1)} %get-tuple-element.35), channel_id=1, source_target_pairs={{16,0},{20,4},{0,8},{4,12},{24,16},{28,20},{8,24},{12,28},{17,1},{... | collective-permute-start | bytes 1572872 | tf_op jit(solution)/shard_map/ppermute | solution.py:597
  137.3 21.7 %collective-permute-start.19 = (bf16[2,256,512]{2,1,0:T(8,128)(2,1)S(1)}, bf16[2,256,512]{2,1,0:T(8,128)(2,1)S(1)}, u32[]{:S(2)}, u32[]{:S(2)}) collective-permute-start(bf16[2,256,512]{2,1,0:T(8,128)(2,1)S(1)} %get-tuple-element.36), channel_id=1, source_target_pairs={{20,0},{16,4},{4,8},{0,12},{28,16},{24,20},{12,24},{8,28},{21,1},{... | collective-permute-start | bytes 1572872 | tf_op jit(solution)/shard_map/ppermute | solution.py:597
  137.4 23.4 %collective-permute-start.16 = (bf16[2,256,512]{2,1,0:T(8,128)(2,1)S(1)}, bf16[2,256,512]{2,1,0:T(8,128)(2,1)S(1)}, u32[]{:S(2)}, u32[]{:S(2)}) collective-permute-start(bf16[2,256,512]{2,1,0:T(8,128)(2,1)S(1)} %get-tuple-element.33.own), channel_id=1, source_target_pairs={{16,8},{20,12},{8,16},{12,20},{17,9},{21,13},{9,17},{13,21},{18,10... | collective-permute-start | bytes 1572872 | tf_op jit(solution)/shard_map/ppermute | solution.py:597
  (1 other events, 0.7 us)

commit v16 on v13

--- a/solution.py
+++ b/solution.py
@@ -221,44 +221,40 @@
     wait_all(copies)
 
 
-def early_unpack_kernel(place, own, p0, p1, p2, field, sems):
+def unpack_kernel(place, own, *rest):
+    pieces, field, sems = rest[:-2], rest[-2], rest[-1]
     copies = []
-    for index, piece in enumerate((p0, p1, p2)):
+    for index, piece in enumerate(pieces):
         width = piece.shape[2]
         offset = pl.multiple_of(place[index] * width, width)
         target = field.at[:, :, pl.ds(offset, width)]
         if index:
             copies.append(pltpu.make_async_copy(piece, target, sems.at[index]))
         else:
-            copies.append(Either(place[5], own, piece, target, sems.at[index]))
+            copies.append(Either(place[len(pieces) + 1], own, piece, target, sems.at[index]))
     start_all(copies)
     wait_all(copies)
 
 
-def late_unpack_kernel(place, piece, started, field, sem):
-    width = piece.shape[2]
-    offset = pl.multiple_of(place[3] * width, width)
-    copy = pltpu.make_async_copy(piece, field.at[:, :, pl.ds(offset, width)], sem)
-    copy.start()
-    copy.wait()
-
-
-def column_kernel(info, blocks, own, p0, p1, p2, p3, x_column, y_turned, rows_held, sems):
-    count, factors, height, width = blocks.shape
+def rows_kernel(info, own, p0, p1, p2, p3, rows_held, sems):
     last = pl.ds(own.shape[1] - rows_held.shape[2], rows_held.shape[2])
     parts = [piece.at[:, last, :] for piece in (p0, p1, p2, p3)]
     copies = [Either(info[info_self], own.at[:, last, :], parts[0], rows_held.at[0], sems.at[0])]
     for index in range(1, len(parts)):
         copies.append(pltpu.make_async_copy(parts[index], rows_held.at[index], sems.at[index]))
     start_all(copies)
+    wait_all(copies)
+
+
+def column_kernel(blocks, rows_held, x_column, y_turned):
+    count, factors, height, width = blocks.shape
     for index in range(count):
         x_column[index * height : (index + 1) * height] = blocks[index, 0]
     column = blocks[:, 1].reshape(count * height, width)
     y_turned[...] = column.astype(f32).T.astype(bf16)
-    wait_all(copies)
-
-
-def field_kernel(info, own, p0, p1, p2, p3, rhs, sems):
+
+
+def field_kernel(info, own, p0, p1, p2, p3, rows_next, rows_far, rhs, sems):
     height = rhs.shape[2] // 2
     copies = []
     for index, piece in enumerate((p0, p1, p2, p3)):
@@ -292,8 +288,7 @@
     wait_all(copies)
 
 
-def both_kernel(info, x_column, x_aside, y_column, y0, y1, rows_next, rows_far, rhs, x_both, y_both,
-                sems):
+def both_kernel(info, x_column, x_aside, y_column, y0, y1, rhs, x_both, y_both, sems):
     copies = [
         pltpu.make_async_copy(x_column, x_both.at[0], sems.at[0]),
         pltpu.make_async_copy(x_aside, x_both.at[1], sems.at[1]),
@@ -536,18 +531,23 @@
 
     column_shape = jax.ShapeDtypeStruct((rows_here, 2 * order), bf16)
     turned_shape = jax.ShapeDtypeStruct((2 * order, rows_here), bf16)
-    x_column, y_turned, rows_held = pl.pallas_call(
+    first = pl.CostEstimate(flops=3 * 10**10, bytes_accessed=2**20, transcendentals=0)
+    rows_held = pl.pallas_call(
+        rows_kernel,
+        out_shape=jax.ShapeDtypeStruct((len(rounds), 2, tall, order), bf16),
+        in_specs=[in_smem] + [anywhere] * 5,
+        out_specs=in_vmem,
+        scratch_shapes=[pltpu.SemaphoreType.DMA((len(rounds),))],
+        compiler_params=params,
+        cost_estimate=first,
+    )(info, packed[0], *pieces)
+    x_column, y_turned = pl.pallas_call(
         column_kernel,
-        out_shape=[
-            column_shape,
-            turned_shape,
-            jax.ShapeDtypeStruct((len(rounds), 2, tall, order), bf16),
-        ],
-        in_specs=[in_smem, in_vmem] + [anywhere] * 5,
-        out_specs=[in_vmem] * 3,
-        scratch_shapes=[pltpu.SemaphoreType.DMA((len(rounds),))],
-        compiler_params=params,
-    )(info, blocks, packed[0], *pieces)
+        out_shape=[column_shape, turned_shape],
+        in_specs=[in_vmem, anywhere],
+        out_specs=[in_vmem] * 2,
+        compiler_params=params,
+    )(blocks, rows_held)
     rows_held = rows_held.reshape(len(rounds), height, order)
 
     def across(block, a):
@@ -568,21 +568,22 @@
     rhs = pl.pallas_call(
         field_kernel,
         out_shape=double_shape,
-        in_specs=[in_smem] + [anywhere] * 5,
+        in_specs=[in_smem] + [anywhere] * 7,
         out_specs=in_vmem,
         scratch_shapes=[pltpu.SemaphoreType.DMA((len(rounds),))],
         compiler_params=params,
-    )(info, packed[0], *pieces)
+        cost_estimate=first,
+    )(info, packed[0], *pieces, rows_next, rows_far)
     x_both, y_both = pl.pallas_call(
         both_kernel,
         out_shape=[
             jax.ShapeDtypeStruct((2,) + one.shape, bf16) for one in (column_shape, turned_shape)
         ],
-        in_specs=[in_smem] + [anywhere] * 8,
+        in_specs=[in_smem] + [anywhere] * 6,
         out_specs=[in_vmem] * 2,
         scratch_shapes=[pltpu.SemaphoreType.DMA((4,))],
         compiler_params=params,
-    )(info, x_column, x_aside, y_turned, *y_near, rows_next, rows_far, rhs)
+    )(info, x_column, x_aside, y_turned, *y_near, rhs)
     y_far = aside(y_both)
     x_across = [across(x_both, a) for a in range(2)]
     weights = pl.pallas_call(
@@ -645,24 +646,14 @@
     received = [
         lax.ppermute(piece, ("sec", "px"), back_pairs(a, b)) for piece, (a, b) in zip(results, rounds)
     ]
-    whole_shape = jax.ShapeDtypeStruct(field.shape, bf16)
-    started = pl.pallas_call(
-        early_unpack_kernel,
-        out_shape=whole_shape,
-        in_specs=[in_smem] + [in_vmem] * 4,
-        out_specs=in_hbm,
-        scratch_shapes=[pltpu.SemaphoreType.DMA((3,))],
-        compiler_params=params,
-    )(sends_to, results[0], *received[:3])
     output = pl.pallas_call(
-        late_unpack_kernel,
-        out_shape=whole_shape,
-        in_specs=[in_smem, in_vmem, in_hbm],
-        out_specs=in_hbm,
-        scratch_shapes=[pltpu.SemaphoreType.DMA(())],
-        input_output_aliases={2: 0},
-        compiler_params=params,
-    )(sends_to, received[3], started)
+        unpack_kernel,
+        out_shape=jax.ShapeDtypeStruct(field.shape, bf16),
+        in_specs=[in_smem] + [anywhere] * (len(rounds) + 1),
+        out_specs=in_vmem,
+        scratch_shapes=[pltpu.SemaphoreType.DMA((len(rounds),))],
+        compiler_params=params,
+    )(sends_to, results[0], *received)
     return output[:, None]
 
 

time: 148 us -> 151 us (1.020); the launches traced: 146 us -> 151 us
  local copies, waits for them, and re-layouts: 4.24 us -> 6.29 us
  starting transfers between devices: 38.5 us -> 40.4 us
    ppermute x3, waiting for transfers between devices: 22.1 us -> 12.7 us  [over_z(): return lax.ppermute(block, 'py', [(z, z ^ bit) for z in range(py_count)])]
    ppermute x2, waiting for transfers between devices: 5.17 us -> 14.1 us  [aside(): return lax.ppermute(block, 'px', [(y, (y + 1) % 2) for y in range(2)])]
    all_to_all x1, waiting for transfers between devices: 0.01 us -> 8.25 us  [on_device(): lax.all_to_all(blocks, 'py', split_axis=0, concat_axis=0, tiled=True)]
    ppermute x4, waiting for transfers between devices: 19.5 us -> 13.3 us  [on_device(): lax.ppermute(piece, ('sec', 'px'), pairs(a, b))]
    ppermute x4, starting transfers between devices: 10.3 us -> 13.8 us  [on_device(): lax.ppermute(piece, ('sec', 'px'), back_pairs(a, b))]
    unnamed x10 -> x16, local copies, waits for them, and re-layouts: 3.45 us -> 5.52 us
    ppermute x2, starting transfers between devices: 1.38 us -> 3.18 us  [aside(): return lax.ppermute(block, 'px', [(y, (y + 1) % 2) for y in range(2)])]
    ppermute x4, starting transfers between devices: 6.77 us -> 4.97 us  [across(): return lax.ppermute(block, ('sec', 'px'), pairs(a, 0))]
  transfers between devices with their start and end apart: 20 -> 20, of which waited for: 14 -> 15; matrix products, arithmetic and copies ran while one was open for 1% -> 0% of each run, Pallas kernels for 5% -> 5%
where the time goes in v16:
time: 151 us
  waiting for transfers between devices  78.1 us (52%)
  starting transfers between devices  40.4 us (27%)
  Pallas kernels  22.9 us (15%)
  local copies, waits for them, and re-layouts  6.29 us (4%)
  between operations  2.81 us (2%)
    ppermute x4, waiting for transfers between devices, on_device(): lax.ppermute(piece, ('sec', 'px'), back_pairs(a, b))  18.9 us
    ppermute x2, waiting for transfers between devices, aside(): return lax.ppermute(block, 'px', [(y, (y + 1) % 2) for y in range(2)])  14.1 us
    ppermute x4, starting transfers between devices, on_device(): lax.ppermute(piece, ('sec', 'px'), back_pairs(a, b))  13.8 us
    ppermute x4, waiting for transfers between devices, on_device(): lax.ppermute(piece, ('sec', 'px'), pairs(a, b))  13.3 us
    ppermute x3, waiting for transfers between devices, over_z(): return lax.ppermute(block, 'py', [(z, z ^ bit) for z in range(py_count)])  12.7 us
    pallas_call x1, Pallas kernels, on_device(): pl.pallas_call(last_kernel, out_shape=[double_shape, full_shape], in_spec...  9.12 us
    all_to_all x1, waiting for transfers between devices, on_device(): lax.all_to_all(blocks, 'py', split_axis=0, concat_axis=0, tiled=True)  8.25 us
    ppermute x4, starting transfers between devices, on_device(): lax.ppermute(piece, ('sec', 'px'), pairs(a, b))  7.49 us
  transfers between devices with their start and end apart: 20, of which 15 were waited for; matrix products, arithmetic and copies ran while one was open for 0% of the time, Pallas kernels for 5%

profile of v16, /device:TPU:1, one launch (start us, length us, event | category | flops | bytes accessed | tf_op | source)
XLA Modules:
  0.0 150.5 jit_solution(15550024104338087359)
XLA Ops:
  0.1 1.6 %copy-done = bf16[2,1,256,2048]{3,2,1,0:T(8,128)(2,1)S(1)} copy-done((bf16[2,1,256,2048]{3,2,1,0:T(8,128)(2,1)S(1)}, bf16[2,1,256,2048]{3,2,1,0:T(8,128)(2,1)}, u32[]{:S(2)}) %copy-start) | copy-done | bytes 2097176
  2.6 2.3 %shard_map.56 = (bf16[2,288,512]{2,1,0:T(8,128)(2,1)S(1)}, bf16[2,288,512]{2,1,0:T(8,128)(2,1)}, bf16[2,288,512]{2,1,0:T(8,128)(2,1)}, bf16[2,288,512]{2,1,0:T(8,128)(2,1)}) custom-call(s32[6]{0:T(128)S(1)} %stack.83.place, bf16[2,256,2048]{2,1,0:T(8,128)(2,1)S(1)} %bitcast.29, bf16[8,32,512]{2,1,0:T(8,128)(2,1)S(1)} %bitcast.33), custom_call_target="tpu_custom_call" | custom-call | tf_op jit(solution)/shard_map/pallas_call | solution.py:519
  4.9 3.6 %collective-permute-start.1 = (bf16[2,288,512]{2,1,0:T(8,128)(2,1)}, bf16[2,288,512]{2,1,0:T(8,128)(2,1)S(1)}, u32[]{:S(2)}, u32[]{:S(2)}) collective-permute-start(bf16[2,288,512]{2,1,0:T(8,128)(2,1)} %get-tuple-element.22), channel_id=1, source_target_pairs={{0,4},{4,0},{8,20},{12,16},{16,12},{20,8},{24,28},{28,24},{1,5},{5... | collective-permute-start | bytes 1769480 | tf_op jit(solution)/shard_map/ppermute | solution.py:528
  9.1 3.3 %collective-permute-start = (bf16[2,288,512]{2,1,0:T(8,128)(2,1)S(1)}, bf16[2,288,512]{2,1,0:T(8,128)(2,1)}, u32[]{:S(2)}, u32[]{:S(2)}) collective-permute-start(bf16[2,288,512]{2,1,0:T(8,128)(2,1)S(1)} %get-tuple-element.21.own), channel_id=1, source_target_pairs={{8,16},{12,20},{16,8},{20,12},{9,17},{13,21},{17,9},{21,13},{10,18... | collective-permute-start | bytes 1769480 | tf_op jit(solution)/shard_map/ppermute | solution.py:528
  12.5 1.3 shard_map.55
  13.8 4.6 %all-to-all-start = ((bf16[4,2,64,1024]{3,2,1,0:T(8,128)(2,1)}), bf16[4,2,64,1024]{3,2,1,0:T(8,128)(2,1)S(1)}, u32[]{:S(2)}, u32[]{:S(2)}) async-start(bf16[4,2,64,1024]{3,2,1,0:T(8,128)(2,1)} %shard_map.55), calls=%async_computation | async-start | bytes 2097152 | tf_op jit(solution)/shard_map/all_to_all | solution.py:530
  21.9 2.3 %collective-permute-done.2.p2 = bf16[2,288,512]{2,1,0:T(8,128)(2,1)S(1)} collective-permute-done((bf16[2,288,512]{2,1,0:T(8,128)(2,1)}, bf16[2,288,512]{2,1,0:T(8,128)(2,1)S(1)}, u32[]{:S(2)}, u32[]{:S(2)}) %collective-permute-start.2) | collective-permute-done | bytes 589856 | tf_op jit(solution)/shard_map/ppermute | solution.py:528
  25.1 10.6 %collective-permute-done.3.p3 = bf16[2,288,512]{2,1,0:T(8,128)(2,1)} collective-permute-done((bf16[2,288,512]{2,1,0:T(8,128)(2,1)}, bf16[2,288,512]{2,1,0:T(8,128)(2,1)}, u32[]{:S(2)}, u32[]{:S(2)}) %collective-permute-start.3) | collective-permute-done | bytes 589856 | tf_op jit(solution)/shard_map/ppermute | solution.py:528
  36.7 1.5 %shard_map.57.rows_held = bf16[4,2,32,512]{3,2,1,0:T(8,128)(2,1)S(1)} custom-call(s32[21]{0:T(128)S(1)} %stack.98.info, bf16[2,288,512]{2,1,0:T(8,128)(2,1)S(1)} %get-tuple-element.21.own, bf16[2,288,512]{2,1,0:T(8,128)(2,1)} %collective-permute-done.p0, bf16[2,288,512]{2,1,0:T(8,128)(2,1)S(1)} %collective-permute-done.1.p1, ...), custom_call_target="tpu_custom_call" | custom-call | flops 30000001024 | bytes 1048576 | tf_op jit(solution)/shard_map/pallas_call | solution.py:535
  38.2 2.2 %collective-permute-start.8 = (bf16[4,64,512]{2,1,0:T(8,128)(2,1)S(1)}, bf16[4,64,512]{2,1,0:T(8,128)(2,1)S(1)}, u32[]{:S(2)}, u32[]{:S(2)}) collective-permute-start(bf16[4,64,512]{2,1,0:T(8,128)(2,1)S(1)} %bitcast.30), channel_id=1, source_target_pairs={{0,2},{1,3},{2,0},{3,1},{4,6},{5,7},{6,4},{7,5},{8,10},{9,11},{10,... | collective-permute-start | bytes 786440 | tf_op jit(solution)/shard_map/ppermute | solution.py:560
  40.4 1.5 collective-permute-start.7
  41.9 8.2 %all-to-all-done.blocks = bf16[4,2,64,1024]{3,2,1,0:T(8,128)(2,1)S(1)} async-done(((bf16[4,2,64,1024]{3,2,1,0:T(8,128)(2,1)}), bf16[4,2,64,1024]{3,2,1,0:T(8,128)(2,1)S(1)}, u32[]{:S(2)}, u32[]{:S(2)}) %all-to-all-start) | async-done | bytes 1048608 | tf_op jit(solution)/shard_map/all_to_all | solution.py:530
  50.4 2.2 %collective-permute-start.5 = (bf16[1024,256]{1,0:T(8,128)(2,1)S(1)}, bf16[1024,256]{1,0:T(8,128)(2,1)S(1)}, u32[]{:S(2)}, u32[]{:S(2)}) collective-permute-start(bf16[1024,256]{1,0:T(8,128)(2,1)S(1)} %get-tuple-element.26.y_column), channel_id=1, source_target_pairs={{8,16},{12,20},{16,8},{20,12},{9,17},{13,21},{17,9},{21,13},{10,18... | collective-permute-start | bytes 1572872 | tf_op jit(solution)/shard_map/ppermute | solution.py:554
  52.6 1.6 %collective-permute-start.4 = (bf16[256,1024]{1,0:T(8,128)(2,1)S(1)}, bf16[256,1024]{1,0:T(8,128)(2,1)S(1)}, u32[]{:S(2)}, u32[]{:S(2)}) collective-permute-start(bf16[256,1024]{1,0:T(8,128)(2,1)S(1)} %get-tuple-element.25.x_column), channel_id=1, source_target_pairs={{0,4},{4,0},{1,5},{5,1},{2,6},{6,2},{3,7},{7,3},{8,12},{12,8},{9,1... | collective-permute-start | bytes 1572872 | tf_op jit(solution)/shard_map/ppermute | solution.py:557
  55.6 1.8 %shard_map.59.rhs = bf16[2,2,512,512]{3,2,1,0:T(8,128)(2,1)S(1)} custom-call(s32[21]{0:T(128)S(1)} %stack.98.info, bf16[2,288,512]{2,1,0:T(8,128)(2,1)S(1)} %get-tuple-element.21.own, bf16[2,288,512]{2,1,0:T(8,128)(2,1)} %collective-permute-done.p0, bf16[2,288,512]{2,1,0:T(8,128)(2,1)S(1)} %collective-permute-done.1.p1, bf16[2,288,512]{2,1,0:T(8,128)(2,1)S(1)} %copy-done.6, ...), custom_call_target="tpu_custom_call" | custom-call | flops 30000001024 | bytes 1048576 | tf_op jit(solution)/shard_map/pallas_call | solution.py:568
  57.4 8.5 %collective-permute-done.4.x_aside = bf16[256,1024]{1,0:T(8,128)(2,1)S(1)} collective-permute-done((bf16[256,1024]{1,0:T(8,128)(2,1)S(1)}, bf16[256,1024]{1,0:T(8,128)(2,1)S(1)}, u32[]{:S(2)}, u32[]{:S(2)}) %collective-permute-start.4) | collective-permute-done | bytes 524320 | tf_op jit(solution)/shard_map/ppermute | solution.py:557
  66.7 1.6 %collective-permute-start.11 = (bf16[2,1024,256]{2,1,0:T(8,128)(2,1)S(1)}, bf16[2,1024,256]{2,1,0:T(8,128)(2,1)S(1)}, u32[]{:S(2)}, u32[]{:S(2)}) collective-permute-start(bf16[2,1024,256]{2,1,0:T(8,128)(2,1)S(1)} %get-tuple-element.28.yb), channel_id=1, source_target_pairs={{0,4},{4,0},{1,5},{5,1},{2,6},{6,2},{3,7},{7,3},{8,12},{12,8},{9,1... | collective-permute-start | bytes 3145736 | tf_op jit(solution)/shard_map/ppermute | solution.py:557
  68.9 2.1 %collective-permute-start.9 = (bf16[2,256,1024]{2,1,0:T(8,128)(2,1)S(1)}, bf16[2,256,1024]{2,1,0:T(8,128)(2,1)S(1)}, u32[]{:S(2)}, u32[]{:S(2)}) collective-permute-start(bf16[2,256,1024]{2,1,0:T(8,128)(2,1)S(1)} %get-tuple-element.27.xb), channel_id=1, source_target_pairs={{8,16},{12,20},{16,8},{20,12},{9,17},{13,21},{17,9},{21,13},{10,18... | collective-permute-start | bytes 3145736 | tf_op jit(solution)/shard_map/ppermute | solution.py:554
  71.1 12.3 %collective-permute-done.12.c3 = bf16[4,64,512]{2,1,0:T(8,128)(2,1)S(1)} collective-permute-done((bf16[4,64,512]{2,1,0:T(8,128)(2,1)S(1)}, bf16[4,64,512]{2,1,0:T(8,128)(2,1)S(1)}, u32[]{:S(2)}, u32[]{:S(2)}) %collective-permute-start.12) | collective-permute-done | bytes 262176 | tf_op jit(solution)/shard_map/ppermute | solution.py:560
  83.5 2.3 %shard_map.61.weights = bf16[2,512,512]{2,1,0:T(8,128)(2,1)S(1)} custom-call(s32[21]{0:T(128)S(1)} %stack.98.info, bf16[4,64,512]{2,1,0:T(8,128)(2,1)S(1)} %bitcast.32, bf16[4,64,512]{2,1,0:T(8,128)(2,1)S(1)} %collective-permute-done.7.rows_next.c1, bf16[4,64,512]{2,1,0:T(8,128)(2,1)S(1)} %collective-permute-done.8.rows_far.c2, ...), custom_call_target="tpu_custom_call" | custom-call | tf_op jit(solution)/shard_map/pallas_call | solution.py:589
  85.8 5.5 %collective-permute-done.11.yf = bf16[2,1024,256]{2,1,0:T(8,128)(2,1)S(1)} collective-permute-done((bf16[2,1024,256]{2,1,0:T(8,128)(2,1)S(1)}, bf16[2,1024,256]{2,1,0:T(8,128)(2,1)S(1)}, u32[]{:S(2)}, u32[]{:S(2)}) %collective-permute-start.11) | collective-permute-done | bytes 1048608 | tf_op jit(solution)/shard_map/ppermute | solution.py:557
  91.3 1.8 %collective-permute-done.9.x0 = bf16[2,256,1024]{2,1,0:T(8,128)(2,1)S(1)} collective-permute-done((bf16[2,256,1024]{2,1,0:T(8,128)(2,1)S(1)}, bf16[2,256,1024]{2,1,0:T(8,128)(2,1)S(1)}, u32[]{:S(2)}, u32[]{:S(2)}) %collective-permute-start.9) | collective-permute-done | bytes 1048608 | tf_op jit(solution)/shard_map/ppermute | solution.py:554
  95.0 6.9 %collective-permute-done.13.arrived = bf16[2,512,512]{2,1,0:T(8,128)(2,1)S(1)} collective-permute-done((bf16[2,512,512]{2,1,0:T(8,128)(2,1)S(1)}, bf16[2,512,512]{2,1,0:T(8,128)(2,1)S(1)}, u32[]{:S(2)}, u32[]{:S(2)}) %collective-permute-start.13) | collective-permute-done | bytes 1048608 | tf_op jit(solution)/shard_map/ppermute | solution.py:622
  102.0 9.1 %shard_map.63 = (bf16[2,2,512,512]{3,2,1,0:T(8,128)(2,1)S(1)}, bf16[2,512,512]{2,1,0:T(8,128)(2,1)S(1)}) custom-call(s32[21]{0:T(128)S(1)} %stack.98.info, bf16[2,256,1024]{2,1,0:T(8,128)(2,1)S(1)} %get-tuple-element.27.xb, bf16[2,256,1024]{2,1,0:T(8,128)(2,1)S(1)} %collective-permute-done.9.x0, bf16[2,256,1024]{2,1,0:T(8,128)(2,1)S(1)} %collective-permute-done.10.x1, ...), custom_call_target="tpu_custom_call" | custom-call | flops 6442450944 | bytes 8388608 | tf_op jit(solution)/shard_map/pallas_call | solution.py:623
  111.1 1.4 collective-permute-start.14
  112.5 2.2 %collective-permute-done.14.arrived = bf16[2,512,512]{2,1,0:T(8,128)(2,1)S(1)} collective-permute-done((bf16[2,512,512]{2,1,0:T(8,128)(2,1)S(1)}, bf16[2,512,512]{2,1,0:T(8,128)(2,1)S(1)}, u32[]{:S(2)}, u32[]{:S(2)}) %collective-permute-start.14) | collective-permute-done | bytes 1048608 | tf_op jit(solution)/shard_map/ppermute | solution.py:634
  115.5 8.8 %collective-permute-start.16 = (bf16[2,256,512]{2,1,0:T(8,128)(2,1)S(1)}, bf16[2,256,512]{2,1,0:T(8,128)(2,1)S(1)}, u32[]{:S(2)}, u32[]{:S(2)}) collective-permute-start(bf16[2,256,512]{2,1,0:T(8,128)(2,1)S(1)} %get-tuple-element.34), channel_id=1, source_target_pairs={{4,0},{0,4},{20,8},{16,12},{12,16},{8,20},{28,24},{24,28},{5,1},{1... | collective-permute-start | bytes 1572872 | tf_op jit(solution)/shard_map/ppermute | solution.py:647
  124.5 4.8 %collective-permute-start.15 = (bf16[2,256,512]{2,1,0:T(8,128)(2,1)S(1)}, bf16[2,256,512]{2,1,0:T(8,128)(2,1)S(1)}, u32[]{:S(2)}, u32[]{:S(2)}) collective-permute-start(bf16[2,256,512]{2,1,0:T(8,128)(2,1)S(1)} %get-tuple-element.33.own), channel_id=1, source_target_pairs={{16,8},{20,12},{8,16},{12,20},{17,9},{21,13},{9,17},{13,21},{18,10... | collective-permute-start | bytes 1572872 | tf_op jit(solution)/shard_map/ppermute | solution.py:647
  129.3 2.0 %collective-permute-done.16.rest_1_ = bf16[2,256,512]{2,1,0:T(8,128)(2,1)S(1)} collective-permute-done((bf16[2,256,512]{2,1,0:T(8,128)(2,1)S(1)}, bf16[2,256,512]{2,1,0:T(8,128)(2,1)S(1)}, u32[]{:S(2)}, u32[]{:S(2)}) %collective-permute-start.16) | collective-permute-done | bytes 524320 | tf_op jit(solution)/shard_map/ppermute | solution.py:647
  131.3 4.8 %collective-permute-done.17.rest_2_ = bf16[2,256,512]{2,1,0:T(8,128)(2,1)S(1)} collective-permute-done((bf16[2,256,512]{2,1,0:T(8,128)(2,1)S(1)}, bf16[2,256,512]{2,1,0:T(8,128)(2,1)S(1)}, u32[]{:S(2)}, u32[]{:S(2)}) %collective-permute-start.17) | collective-permute-done | bytes 524320 | tf_op jit(solution)/shard_map/ppermute | solution.py:647
  136.1 10.8 %collective-permute-done.18.rest_3_ = bf16[2,256,512]{2,1,0:T(8,128)(2,1)S(1)} collective-permute-done((bf16[2,256,512]{2,1,0:T(8,128)(2,1)S(1)}, bf16[2,256,512]{2,1,0:T(8,128)(2,1)S(1)}, u32[]{:S(2)}, u32[]{:S(2)}) %collective-permute-start.18) | collective-permute-done | bytes 524320 | tf_op jit(solution)/shard_map/ppermute | solution.py:647
  148.2 2.2 %shard_map.65 = bf16[2,256,2048]{2,1,0:T(8,128)(2,1)} custom-call(s32[6]{0:T(128)S(1)} %stack.83.place, bf16[2,256,512]{2,1,0:T(8,128)(2,1)S(1)} %get-tuple-element.33.own, bf16[2,256,512]{2,1,0:T(8,128)(2,1)S(1)} %collective-permute-done.15.rest_0_, bf16[2,256,512]{2,1,0:T(8,128)(2,1)S(1)} %collective-permute-done.16.rest_1_, ...), custom_call_target="tpu_custom_call" | custom-call | tf_op jit(solution)/shard_map/pallas_call | solution.py:649
  (38 shorter events, 11.9 us)
Async XLA Ops:
  0.0 12.4 %copy-start.2 = (bf16[1,2,64,512]{3,2,1,0:T(8,128)(2,1)S(1)}, bf16[1,2,64,512]{3,2,1,0:T(8,128)(2,1)}, u32[]{:S(2)}) copy-start(bf16[1,2,64,512]{3,2,1,0:T(8,128)(2,1)} %param.8) | copy-start | bytes 393220
  0.1 1.6 %copy-start = (bf16[2,1,256,2048]{3,2,1,0:T(8,128)(2,1)S(1)}, bf16[2,1,256,2048]{3,2,1,0:T(8,128)(2,1)}, u32[]{:S(2)}) copy-start(bf16[2,1,256,2048]{3,2,1,0:T(8,128)(2,1)} %param.5) | copy-start | bytes 6291460
  1.7 0.9 copy-start.1
  2.6 9.8 %copy-start.3 = (bf16[1,2,64,512]{3,2,1,0:T(8,128)(2,1)S(1)}, bf16[1,2,64,512]{3,2,1,0:T(8,128)(2,1)}, u32[]{:S(2)}) copy-start(bf16[1,2,64,512]{3,2,1,0:T(8,128)(2,1)} %param.9) | copy-start | bytes 393220
  4.9 13.5 %copy-start.7 = (s32[16]{0:T(128)S(1)}, s32[16]{0:T(128)}, u32[]{:S(2)}) copy-start(s32[16]{0:T(128)} %param.6) | copy-start | bytes 196
  4.9 17.0 %collective-permute-start.1 = (bf16[2,288,512]{2,1,0:T(8,128)(2,1)}, bf16[2,288,512]{2,1,0:T(8,128)(2,1)S(1)}, u32[]{:S(2)}, u32[]{:S(2)}) collective-permute-start(bf16[2,288,512]{2,1,0:T(8,128)(2,1)} %get-tuple-element.22), channel_id=1, source_target_pairs={{0,4},{4,0},{8,20},{12,16},{16,12},{20,8},{24,28},{28,24},{1,5},{5... | collective-permute-start | bytes 1769480 | tf_op jit(solution)/shard_map/ppermute | solution.py:528
  8.6 15.7 %collective-permute-start.2 = (bf16[2,288,512]{2,1,0:T(8,128)(2,1)}, bf16[2,288,512]{2,1,0:T(8,128)(2,1)S(1)}, u32[]{:S(2)}, u32[]{:S(2)}) collective-permute-start(bf16[2,288,512]{2,1,0:T(8,128)(2,1)} %get-tuple-element.23), channel_id=1, source_target_pairs={{0,16},{4,20},{8,0},{12,4},{16,24},{20,28},{24,8},{28,12},{1,17},{... | collective-permute-start | bytes 1769480 | tf_op jit(solution)/shard_map/ppermute | solution.py:528
  8.6 27.1 %collective-permute-start.3 = (bf16[2,288,512]{2,1,0:T(8,128)(2,1)}, bf16[2,288,512]{2,1,0:T(8,128)(2,1)}, u32[]{:S(2)}, u32[]{:S(2)}) collective-permute-start(bf16[2,288,512]{2,1,0:T(8,128)(2,1)} %get-tuple-element.24), channel_id=1, source_target_pairs={{0,20},{4,16},{8,4},{12,0},{16,28},{20,24},{24,12},{28,8},{1,21},{... | collective-permute-start | bytes 1769480 | tf_op jit(solution)/shard_map/ppermute | solution.py:528
  9.1 26.5 %collective-permute-start = (bf16[2,288,512]{2,1,0:T(8,128)(2,1)S(1)}, bf16[2,288,512]{2,1,0:T(8,128)(2,1)}, u32[]{:S(2)}, u32[]{:S(2)}) collective-permute-start(bf16[2,288,512]{2,1,0:T(8,128)(2,1)S(1)} %get-tuple-element.21.own), channel_id=1, source_target_pairs={{8,16},{12,20},{16,8},{20,12},{9,17},{13,21},{17,9},{21,13},{10,18... | collective-permute-start | bytes 1769480 | tf_op jit(solution)/shard_map/ppermute | solution.py:528
  13.8 36.4 %all-to-all-start = ((bf16[4,2,64,1024]{3,2,1,0:T(8,128)(2,1)}), bf16[4,2,64,1024]{3,2,1,0:T(8,128)(2,1)S(1)}, u32[]{:S(2)}, u32[]{:S(2)}) async-start(bf16[4,2,64,1024]{3,2,1,0:T(8,128)(2,1)} %shard_map.55), calls=%async_computation | async-start | bytes 2097152 | tf_op jit(solution)/shard_map/all_to_all | solution.py:530
  24.2 0.8 copy-start.4
  35.6 1.1 copy-start.5
  38.2 16.3 %collective-permute-start.8 = (bf16[4,64,512]{2,1,0:T(8,128)(2,1)S(1)}, bf16[4,64,512]{2,1,0:T(8,128)(2,1)S(1)}, u32[]{:S(2)}, u32[]{:S(2)}) collective-permute-start(bf16[4,64,512]{2,1,0:T(8,128)(2,1)S(1)} %bitcast.30), channel_id=1, source_target_pairs={{0,2},{1,3},{2,0},{3,1},{4,6},{5,7},{6,4},{7,5},{8,10},{9,11},{10,... | collective-permute-start | bytes 786440 | tf_op jit(solution)/shard_map/ppermute | solution.py:560
  40.4 14.1 %collective-permute-start.7 = (bf16[4,64,512]{2,1,0:T(8,128)(2,1)S(1)}, bf16[4,64,512]{2,1,0:T(8,128)(2,1)S(1)}, u32[]{:S(2)}, u32[]{:S(2)}) collective-permute-start(bf16[4,64,512]{2,1,0:T(8,128)(2,1)S(1)} %bitcast.31), channel_id=1, source_target_pairs={{0,1},{1,0},{2,3},{3,2},{4,5},{5,4},{6,7},{7,6},{8,9},{9,8},{10,11... | collective-permute-start | bytes 786440 | tf_op jit(solution)/shard_map/ppermute | solution.py:560
  50.4 15.5 %collective-permute-start.6 = (bf16[1024,256]{1,0:T(8,128)(2,1)S(1)}, bf16[1024,256]{1,0:T(8,128)(2,1)S(1)}, u32[]{:S(2)}, u32[]{:S(2)}) collective-permute-start(bf16[1024,256]{1,0:T(8,128)(2,1)S(1)} %get-tuple-element.26.y_column), channel_id=1, source_target_pairs={{0,16},{4,20},{8,0},{12,4},{16,24},{20,28},{24,8},{28,12},{1,17},{... | collective-permute-start | bytes 1572872 | tf_op jit(solution)/shard_map/ppermute | solution.py:554
  50.4 15.5 %collective-permute-start.5 = (bf16[1024,256]{1,0:T(8,128)(2,1)S(1)}, bf16[1024,256]{1,0:T(8,128)(2,1)S(1)}, u32[]{:S(2)}, u32[]{:S(2)}) collective-permute-start(bf16[1024,256]{1,0:T(8,128)(2,1)S(1)} %get-tuple-element.26.y_column), channel_id=1, source_target_pairs={{8,16},{12,20},{16,8},{20,12},{9,17},{13,21},{17,9},{21,13},{10,18... | collective-permute-start | bytes 1572872 | tf_op jit(solution)/shard_map/ppermute | solution.py:554
  52.6 13.3 %collective-permute-start.4 = (bf16[256,1024]{1,0:T(8,128)(2,1)S(1)}, bf16[256,1024]{1,0:T(8,128)(2,1)S(1)}, u32[]{:S(2)}, u32[]{:S(2)}) collective-permute-start(bf16[256,1024]{1,0:T(8,128)(2,1)S(1)} %get-tuple-element.25.x_column), channel_id=1, source_target_pairs={{0,4},{4,0},{1,5},{5,1},{2,6},{6,2},{3,7},{7,3},{8,12},{12,8},{9,1... | collective-permute-start | bytes 1572872 | tf_op jit(solution)/shard_map/ppermute | solution.py:557
  54.5 1.1 copy-start.6
  66.7 24.6 %collective-permute-start.11 = (bf16[2,1024,256]{2,1,0:T(8,128)(2,1)S(1)}, bf16[2,1024,256]{2,1,0:T(8,128)(2,1)S(1)}, u32[]{:S(2)}, u32[]{:S(2)}) collective-permute-start(bf16[2,1024,256]{2,1,0:T(8,128)(2,1)S(1)} %get-tuple-element.28.yb), channel_id=1, source_target_pairs={{0,4},{4,0},{1,5},{5,1},{2,6},{6,2},{3,7},{7,3},{8,12},{12,8},{9,1... | collective-permute-start | bytes 3145736 | tf_op jit(solution)/shard_map/ppermute | solution.py:557
  68.3 23.1 %collective-permute-start.10 = (bf16[2,256,1024]{2,1,0:T(8,128)(2,1)S(1)}, bf16[2,256,1024]{2,1,0:T(8,128)(2,1)S(1)}, u32[]{:S(2)}, u32[]{:S(2)}) collective-permute-start(bf16[2,256,1024]{2,1,0:T(8,128)(2,1)S(1)} %get-tuple-element.27.xb), channel_id=1, source_target_pairs={{0,16},{4,20},{8,0},{12,4},{16,24},{20,28},{24,8},{28,12},{1,17},{... | collective-permute-start | bytes 3145736 | tf_op jit(solution)/shard_map/ppermute | solution.py:554
  68.9 24.2 %collective-permute-start.9 = (bf16[2,256,1024]{2,1,0:T(8,128)(2,1)S(1)}, bf16[2,256,1024]{2,1,0:T(8,128)(2,1)S(1)}, u32[]{:S(2)}, u32[]{:S(2)}) collective-permute-start(bf16[2,256,1024]{2,1,0:T(8,128)(2,1)S(1)} %get-tuple-element.27.xb), channel_id=1, source_target_pairs={{8,16},{12,20},{16,8},{20,12},{9,17},{13,21},{17,9},{21,13},{10,18... | collective-permute-start | bytes 3145736 | tf_op jit(solution)/shard_map/ppermute | solution.py:554
  71.0 12.4 %collective-permute-start.12 = (bf16[4,64,512]{2,1,0:T(8,128)(2,1)S(1)}, bf16[4,64,512]{2,1,0:T(8,128)(2,1)S(1)}, u32[]{:S(2)}, u32[]{:S(2)}) collective-permute-start(bf16[4,64,512]{2,1,0:T(8,128)(2,1)S(1)} %collective-permute-done.7.rows_next.c1), channel_id=1, source_target_pairs={{0,2},{1,3},{2,0},{3,1},{4,6},{5,7},{6,4},{7,5},{8,10},{9,11},{10,... | collective-permute-start | bytes 786440 | tf_op jit(solution)/shard_map/ppermute | solution.py:560
  93.7 8.2 %collective-permute-start.13 = (bf16[2,512,512]{2,1,0:T(8,128)(2,1)S(1)}, bf16[2,512,512]{2,1,0:T(8,128)(2,1)S(1)}, u32[]{:S(2)}, u32[]{:S(2)}) collective-permute-start(bf16[2,512,512]{2,1,0:T(8,128)(2,1)S(1)} %get-tuple-element.30.w_high), channel_id=1, source_target_pairs={{0,8},{16,24},{1,9},{17,25},{2,10},{18,26},{3,11},{19,27},{4,12},{... | collective-permute-start | bytes 3145736 | tf_op jit(solution)/shard_map/ppermute | solution.py:622
  111.1 3.6 %collective-permute-start.14 = (bf16[2,512,512]{2,1,0:T(8,128)(2,1)S(1)}, bf16[2,512,512]{2,1,0:T(8,128)(2,1)S(1)}, u32[]{:S(2)}, u32[]{:S(2)}) collective-permute-start(bf16[2,512,512]{2,1,0:T(8,128)(2,1)S(1)} %get-tuple-element.31), channel_id=1, source_target_pairs={{8,0},{24,16},{9,1},{25,17},{10,2},{26,18},{11,3},{27,19},{12,4},{... | collective-permute-start | bytes 3145736 | tf_op jit(solution)/shard_map/ppermute | solution.py:634
  115.5 15.8 %collective-permute-start.16 = (bf16[2,256,512]{2,1,0:T(8,128)(2,1)S(1)}, bf16[2,256,512]{2,1,0:T(8,128)(2,1)S(1)}, u32[]{:S(2)}, u32[]{:S(2)}) collective-permute-start(bf16[2,256,512]{2,1,0:T(8,128)(2,1)S(1)} %get-tuple-element.34), channel_id=1, source_target_pairs={{4,0},{0,4},{20,8},{16,12},{12,16},{8,20},{28,24},{24,28},{5,1},{1... | collective-permute-start | bytes 1572872 | tf_op jit(solution)/shard_map/ppermute | solution.py:647
  124.3 11.8 %collective-permute-start.17 = (bf16[2,256,512]{2,1,0:T(8,128)(2,1)S(1)}, bf16[2,256,512]{2,1,0:T(8,128)(2,1)S(1)}, u32[]{:S(2)}, u32[]{:S(2)}) collective-permute-start(bf16[2,256,512]{2,1,0:T(8,128)(2,1)S(1)} %get-tuple-element.35), channel_id=1, source_target_pairs={{16,0},{20,4},{0,8},{4,12},{24,16},{28,20},{8,24},{12,28},{17,1},{... | collective-permute-start | bytes 1572872 | tf_op jit(solution)/shard_map/ppermute | solution.py:647
  124.3 22.6 %collective-permute-start.18 = (bf16[2,256,512]{2,1,0:T(8,128)(2,1)S(1)}, bf16[2,256,512]{2,1,0:T(8,128)(2,1)S(1)}, u32[]{:S(2)}, u32[]{:S(2)}) collective-permute-start(bf16[2,256,512]{2,1,0:T(8,128)(2,1)S(1)} %get-tuple-element.36), channel_id=1, source_target_pairs={{20,0},{16,4},{4,8},{0,12},{28,16},{24,20},{12,24},{8,28},{21,1},{... | collective-permute-start | bytes 1572872 | tf_op jit(solution)/shard_map/ppermute | solution.py:647
  124.5 23.7 %collective-permute-start.15 = (bf16[2,256,512]{2,1,0:T(8,128)(2,1)S(1)}, bf16[2,256,512]{2,1,0:T(8,128)(2,1)S(1)}, u32[]{:S(2)}, u32[]{:S(2)}) collective-permute-start(bf16[2,256,512]{2,1,0:T(8,128)(2,1)S(1)} %get-tuple-element.33.own), channel_id=1, source_target_pairs={{16,8},{20,12},{8,16},{12,20},{17,9},{21,13},{9,17},{13,21},{18,10... | collective-permute-start | bytes 1572872 | tf_op jit(solution)/shard_map/ppermute | solution.py:647

commit v17 on v16

--- a/solution.py
+++ b/solution.py
@@ -236,25 +236,22 @@
     wait_all(copies)
 
 
-def rows_kernel(info, own, p0, p1, p2, p3, rows_held, sems):
+def column_kernel(info, blocks, own, p0, p1, p2, p3, x_column, y_turned, rows_held, sems):
+    count, factors, height, width = blocks.shape
     last = pl.ds(own.shape[1] - rows_held.shape[2], rows_held.shape[2])
     parts = [piece.at[:, last, :] for piece in (p0, p1, p2, p3)]
     copies = [Either(info[info_self], own.at[:, last, :], parts[0], rows_held.at[0], sems.at[0])]
     for index in range(1, len(parts)):
         copies.append(pltpu.make_async_copy(parts[index], rows_held.at[index], sems.at[index]))
     start_all(copies)
-    wait_all(copies)
-
-
-def column_kernel(blocks, rows_held, x_column, y_turned):
-    count, factors, height, width = blocks.shape
     for index in range(count):
         x_column[index * height : (index + 1) * height] = blocks[index, 0]
     column = blocks[:, 1].reshape(count * height, width)
     y_turned[...] = column.astype(f32).T.astype(bf16)
-
-
-def field_kernel(info, own, p0, p1, p2, p3, rows_next, rows_far, rhs, sems):
+    wait_all(copies)
+
+
+def field_kernel(info, own, p0, p1, p2, p3, rhs, sems):
     height = rhs.shape[2] // 2
     copies = []
     for index, piece in enumerate((p0, p1, p2, p3)):
@@ -531,23 +528,18 @@
 
     column_shape = jax.ShapeDtypeStruct((rows_here, 2 * order), bf16)
     turned_shape = jax.ShapeDtypeStruct((2 * order, rows_here), bf16)
-    first = pl.CostEstimate(flops=3 * 10**10, bytes_accessed=2**20, transcendentals=0)
-    rows_held = pl.pallas_call(
-        rows_kernel,
-        out_shape=jax.ShapeDtypeStruct((len(rounds), 2, tall, order), bf16),
-        in_specs=[in_smem] + [anywhere] * 5,
-        out_specs=in_vmem,
+    x_column, y_turned, rows_held = pl.pallas_call(
+        column_kernel,
+        out_shape=[
+            column_shape,
+            turned_shape,
+            jax.ShapeDtypeStruct((len(rounds), 2, tall, order), bf16),
+        ],
+        in_specs=[in_smem, in_vmem] + [anywhere] * 5,
+        out_specs=[in_vmem] * 3,
         scratch_shapes=[pltpu.SemaphoreType.DMA((len(rounds),))],
         compiler_params=params,
-        cost_estimate=first,
-    )(info, packed[0], *pieces)
-    x_column, y_turned = pl.pallas_call(
-        column_kernel,
-        out_shape=[column_shape, turned_shape],
-        in_specs=[in_vmem, anywhere],
-        out_specs=[in_vmem] * 2,
-        compiler_params=params,
-    )(blocks, rows_held)
+    )(info, blocks, packed[0], *pieces)
     rows_held = rows_held.reshape(len(rounds), height, order)
 
     def across(block, a):
@@ -568,12 +560,11 @@
     rhs = pl.pallas_call(
         field_kernel,
         out_shape=double_shape,
-        in_specs=[in_smem] + [anywhere] * 7,
+        in_specs=[in_smem] + [anywhere] * 5,
         out_specs=in_vmem,
         scratch_shapes=[pltpu.SemaphoreType.DMA((len(rounds),))],
         compiler_params=params,
-        cost_estimate=first,
-    )(info, packed[0], *pieces, rows_next, rows_far)
+    )(info, packed[0], *pieces)
     x_both, y_both = pl.pallas_call(
         both_kernel,
         out_shape=[
@@ -593,6 +584,9 @@
         out_specs=in_vmem,
         scratch_shapes=[pltpu.SemaphoreType.DMA((4, len(rounds)))],
         compiler_params=params,
+        cost_estimate=pl.CostEstimate(
+            flops=3 * 10**10, bytes_accessed=2**21, transcendentals=0
+        ),
     )(info, rows_held, rows_next, rows_far, over_z(rows_next, 2))
     layers = (info, x_both, *x_across, y_both, y_far, weights)
     layer_specs = [in_smem] + [anywhere] * 3 + [in_vmem] * 3

time: 151 us -> 149 us (0.987)
  local copies, waits for them, and re-layouts: 6.29 us -> 4.24 us
    all_to_all x1, waiting for transfers between devices: 8.25 us -> 0.01 us  [on_device(): lax.all_to_all(blocks, 'py', split_axis=0, concat_axis=0, tiled=True)]
    ppermute x4, waiting for transfers between devices: 13.3 us -> 19.5 us  [on_device(): lax.ppermute(piece, ('sec', 'px'), pairs(a, b))]
    ppermute x3, waiting for transfers between devices: 12.7 us -> 18.3 us  [over_z(): return lax.ppermute(block, 'py', [(z, z ^ bit) for z in range(py_count)])]
    ppermute x2, waiting for transfers between devices: 14.1 us -> 11.9 us  [aside(): return lax.ppermute(block, 'px', [(y, (y + 1) % 2) for y in range(2)])]
    unnamed x16 -> x10, local copies, waits for them, and re-layouts: 5.52 us -> 3.45 us
    ppermute x4, waiting for transfers between devices: 1.83 us -> 0.01 us  [across(): return lax.ppermute(block, ('sec', 'px'), pairs(a, 0))]
    ppermute x2, starting transfers between devices: 3.18 us -> 1.4 us  [aside(): return lax.ppermute(block, 'px', [(y, (y + 1) % 2) for y in range(2)])]
  transfers between devices with their start and end apart: 20 -> 20, of which waited for: 15 -> 12; matrix products, arithmetic and copies ran while one was open for 0% -> 1% of each run, Pallas kernels for 5% -> 5%
where the time goes in v17:
time: 149 us; the launch traced here: 148 us
  waiting for transfers between devices  77.9 us (52%)
  starting transfers between devices  40.7 us (27%)
  Pallas kernels  22.4 us (15%)
  local copies, waits for them, and re-layouts  4.24 us (3%)
  between operations  3.1 us (2%)
    ppermute x4, waiting for transfers between devices, on_device(): lax.ppermute(piece, ('sec', 'px'), pairs(a, b))  19.5 us
    ppermute x4, waiting for transfers between devices, on_device(): lax.ppermute(piece, ('sec', 'px'), back_pairs(a, b))  18.9 us
    ppermute x3, waiting for transfers between devices, over_z(): return lax.ppermute(block, 'py', [(z, z ^ bit) for z in range(py_count)])  18.3 us
    ppermute x4, starting transfers between devices, on_device(): lax.ppermute(piece, ('sec', 'px'), back_pairs(a, b))  13.6 us
    ppermute x2, waiting for transfers between devices, aside(): return lax.ppermute(block, 'px', [(y, (y + 1) % 2) for y in range(2)])  11.9 us
    pallas_call x1, Pallas kernels, on_device(): pl.pallas_call(last_kernel, out_shape=[double_shape, full_shape], in_spec...  9.12 us
    ppermute x1, waiting for transfers between devices, on_device(): incoming = lax.ppermute(w_high, 'sec', up)  7.15 us
    ppermute x4, starting transfers between devices, on_device(): lax.ppermute(piece, ('sec', 'px'), pairs(a, b))  6.94 us
  transfers between devices with their start and end apart: 20, of which 12 were waited for; matrix products, arithmetic and copies ran while one was open for 1% of the time, Pallas kernels for 5%

profile of v17, /device:TPU:1, one launch (start us, length us, event | category | flops | bytes accessed | tf_op | source)
XLA Modules:
  0.0 148.4 jit_solution(3954374535103250243)
XLA Ops:
  0.0 0.9 copy-done.2
  1.9 1.3 shard_map.55
  3.2 5.4 %all-to-all-start = ((bf16[4,2,64,1024]{3,2,1,0:T(8,128)(2,1)}), bf16[4,2,64,1024]{3,2,1,0:T(8,128)(2,1)S(1)}, u32[]{:S(2)}, u32[]{:S(2)}) async-start(bf16[4,2,64,1024]{3,2,1,0:T(8,128)(2,1)} %shard_map.55), calls=%async_computation | async-start | bytes 2097152 | tf_op jit(solution)/shard_map/all_to_all | solution.py:527
  8.7 1.6 %copy-done = bf16[2,1,256,2048]{3,2,1,0:T(8,128)(2,1)S(1)} copy-done((bf16[2,1,256,2048]{3,2,1,0:T(8,128)(2,1)S(1)}, bf16[2,1,256,2048]{3,2,1,0:T(8,128)(2,1)}, u32[]{:S(2)}) %copy-start) | copy-done | bytes 2097176
  10.3 2.3 %shard_map.56 = (bf16[2,288,512]{2,1,0:T(8,128)(2,1)S(1)}, bf16[2,288,512]{2,1,0:T(8,128)(2,1)}, bf16[2,288,512]{2,1,0:T(8,128)(2,1)}, bf16[2,288,512]{2,1,0:T(8,128)(2,1)}) custom-call(s32[6]{0:T(128)S(1)} %stack.83.place, bf16[2,256,2048]{2,1,0:T(8,128)(2,1)S(1)} %bitcast.29, bf16[8,32,512]{2,1,0:T(8,128)(2,1)S(1)} %bitcast.30), custom_call_target="tpu_custom_call" | custom-call | tf_op jit(solution)/shard_map/pallas_call | solution.py:516
  12.6 3.1 %collective-permute-start.1 = (bf16[2,288,512]{2,1,0:T(8,128)(2,1)}, bf16[2,288,512]{2,1,0:T(8,128)(2,1)S(1)}, u32[]{:S(2)}, u32[]{:S(2)}) collective-permute-start(bf16[2,288,512]{2,1,0:T(8,128)(2,1)} %get-tuple-element.23), channel_id=1, source_target_pairs={{0,4},{4,0},{8,20},{12,16},{16,12},{20,8},{24,28},{28,24},{1,5},{5... | collective-permute-start | bytes 1769480 | tf_op jit(solution)/shard_map/ppermute | solution.py:525
  16.3 3.3 %collective-permute-start = (bf16[2,288,512]{2,1,0:T(8,128)(2,1)S(1)}, bf16[2,288,512]{2,1,0:T(8,128)(2,1)}, u32[]{:S(2)}, u32[]{:S(2)}) collective-permute-start(bf16[2,288,512]{2,1,0:T(8,128)(2,1)S(1)} %get-tuple-element.22.own), channel_id=1, source_target_pairs={{8,16},{12,20},{16,8},{20,12},{9,17},{13,21},{17,9},{21,13},{10,18... | collective-permute-start | bytes 1769480 | tf_op jit(solution)/shard_map/ppermute | solution.py:525
  23.0 5.9 %collective-permute-done.1.p1 = bf16[2,288,512]{2,1,0:T(8,128)(2,1)S(1)} collective-permute-done((bf16[2,288,512]{2,1,0:T(8,128)(2,1)}, bf16[2,288,512]{2,1,0:T(8,128)(2,1)S(1)}, u32[]{:S(2)}, u32[]{:S(2)}) %collective-permute-start.1) | collective-permute-done | bytes 589856 | tf_op jit(solution)/shard_map/ppermute | solution.py:525
  28.9 2.4 %collective-permute-done.2.p2 = bf16[2,288,512]{2,1,0:T(8,128)(2,1)S(1)} collective-permute-done((bf16[2,288,512]{2,1,0:T(8,128)(2,1)}, bf16[2,288,512]{2,1,0:T(8,128)(2,1)S(1)}, u32[]{:S(2)}, u32[]{:S(2)}) %collective-permute-start.2) | collective-permute-done | bytes 589856 | tf_op jit(solution)/shard_map/ppermute | solution.py:525
  31.3 11.2 %collective-permute-done.3.p3 = bf16[2,288,512]{2,1,0:T(8,128)(2,1)S(1)} collective-permute-done((bf16[2,288,512]{2,1,0:T(8,128)(2,1)}, bf16[2,288,512]{2,1,0:T(8,128)(2,1)S(1)}, u32[]{:S(2)}, u32[]{:S(2)}) %collective-permute-start.3) | collective-permute-done | bytes 589856 | tf_op jit(solution)/shard_map/ppermute | solution.py:525
  42.5 1.4 shard_map.57
  44.8 4.2 %collective-permute-start.5 = (bf16[1024,256]{1,0:T(8,128)(2,1)S(1)}, bf16[1024,256]{1,0:T(8,128)(2,1)S(1)}, u32[]{:S(2)}, u32[]{:S(2)}) collective-permute-start(bf16[1024,256]{1,0:T(8,128)(2,1)S(1)} %get-tuple-element.27.y_column), channel_id=1, source_target_pairs={{8,16},{12,20},{16,8},{20,12},{9,17},{13,21},{17,9},{21,13},{10,18... | collective-permute-start | bytes 1572872 | tf_op jit(solution)/shard_map/ppermute | solution.py:546
  49.0 1.8 %collective-permute-start.10 = (bf16[4,64,512]{2,1,0:T(8,128)(2,1)S(1)}, bf16[4,64,512]{2,1,0:T(8,128)(2,1)S(1)}, u32[]{:S(2)}, u32[]{:S(2)}) collective-permute-start(bf16[4,64,512]{2,1,0:T(8,128)(2,1)S(1)} %bitcast.33), channel_id=1, source_target_pairs={{0,1},{1,0},{2,3},{3,2},{4,5},{5,4},{6,7},{7,6},{8,9},{9,8},{10,11... | collective-permute-start | bytes 786440 | tf_op jit(solution)/shard_map/ppermute | solution.py:552
  50.8 2.1 %collective-permute-start.11 = (bf16[4,64,512]{2,1,0:T(8,128)(2,1)S(1)}, bf16[4,64,512]{2,1,0:T(8,128)(2,1)S(1)}, u32[]{:S(2)}, u32[]{:S(2)}) collective-permute-start(bf16[4,64,512]{2,1,0:T(8,128)(2,1)S(1)} %bitcast.34), channel_id=1, source_target_pairs={{0,2},{1,3},{2,0},{3,1},{4,6},{5,7},{6,4},{7,5},{8,10},{9,11},{10,... | collective-permute-start | bytes 786440 | tf_op jit(solution)/shard_map/ppermute | solution.py:552
  52.9 9.3 %collective-permute-done.10.c1 = bf16[4,64,512]{2,1,0:T(8,128)(2,1)S(1)} collective-permute-done((bf16[4,64,512]{2,1,0:T(8,128)(2,1)S(1)}, bf16[4,64,512]{2,1,0:T(8,128)(2,1)S(1)}, u32[]{:S(2)}, u32[]{:S(2)}) %collective-permute-start.10) | collective-permute-done | bytes 262176 | tf_op jit(solution)/shard_map/ppermute | solution.py:552
  62.9 1.6 %shard_map.58.rhs = bf16[2,2,512,512]{3,2,1,0:T(8,128)(2,1)S(1)} custom-call(s32[21]{0:T(128)S(1)} %stack.98.info, bf16[2,288,512]{2,1,0:T(8,128)(2,1)S(1)} %get-tuple-element.22.own, bf16[2,288,512]{2,1,0:T(8,128)(2,1)} %collective-permute-done.p0, bf16[2,288,512]{2,1,0:T(8,128)(2,1)S(1)} %collective-permute-done.1.p1, ...), custom_call_target="tpu_custom_call" | custom-call | tf_op jit(solution)/shard_map/pallas_call | solution.py:560
  65.3 1.9 %collective-permute-start.7 = (bf16[2,256,1024]{2,1,0:T(8,128)(2,1)S(1)}, bf16[2,256,1024]{2,1,0:T(8,128)(2,1)S(1)}, u32[]{:S(2)}, u32[]{:S(2)}) collective-permute-start(bf16[2,256,1024]{2,1,0:T(8,128)(2,1)S(1)} %get-tuple-element.28.xb), channel_id=1, source_target_pairs={{8,16},{12,20},{16,8},{20,12},{9,17},{13,21},{17,9},{21,13},{10,18... | collective-permute-start | bytes 3145736 | tf_op jit(solution)/shard_map/ppermute | solution.py:546
  67.7 9.0 %collective-permute-done.12.c3 = bf16[4,64,512]{2,1,0:T(8,128)(2,1)S(1)} collective-permute-done((bf16[4,64,512]{2,1,0:T(8,128)(2,1)S(1)}, bf16[4,64,512]{2,1,0:T(8,128)(2,1)S(1)}, u32[]{:S(2)}, u32[]{:S(2)}) %collective-permute-start.12) | collective-permute-done | bytes 262176 | tf_op jit(solution)/shard_map/ppermute | solution.py:552
  76.7 2.3 %shard_map.60.weights = bf16[2,512,512]{2,1,0:T(8,128)(2,1)S(1)} custom-call(s32[21]{0:T(128)S(1)} %stack.98.info, bf16[4,64,512]{2,1,0:T(8,128)(2,1)S(1)} %bitcast.35, bf16[4,64,512]{2,1,0:T(8,128)(2,1)S(1)} %collective-permute-done.10.c1, bf16[4,64,512]{2,1,0:T(8,128)(2,1)S(1)} %collective-permute-done.11.c2, ...), custom_call_target="tpu_custom_call" | custom-call | flops 30000001024 | bytes 2097152 | tf_op jit(solution)/shard_map/pallas_call | solution.py:580
  79.1 11.9 %collective-permute-done.9.yf = bf16[2,1024,256]{2,1,0:T(8,128)(2,1)S(1)} collective-permute-done((bf16[2,1024,256]{2,1,0:T(8,128)(2,1)S(1)}, bf16[2,1024,256]{2,1,0:T(8,128)(2,1)S(1)}, u32[]{:S(2)}, u32[]{:S(2)}) %collective-permute-start.9) | collective-permute-done | bytes 1048608 | tf_op jit(solution)/shard_map/ppermute | solution.py:549
  91.6 1.3 collective-permute-start.13
  92.9 7.2 %collective-permute-done.13.arrived = bf16[2,512,512]{2,1,0:T(8,128)(2,1)S(1)} collective-permute-done((bf16[2,512,512]{2,1,0:T(8,128)(2,1)S(1)}, bf16[2,512,512]{2,1,0:T(8,128)(2,1)S(1)}, u32[]{:S(2)}, u32[]{:S(2)}) %collective-permute-start.13) | collective-permute-done | bytes 1048608 | tf_op jit(solution)/shard_map/ppermute | solution.py:616
  100.1 9.1 %shard_map.62 = (bf16[2,2,512,512]{3,2,1,0:T(8,128)(2,1)S(1)}, bf16[2,512,512]{2,1,0:T(8,128)(2,1)S(1)}) custom-call(s32[21]{0:T(128)S(1)} %stack.98.info, bf16[2,256,1024]{2,1,0:T(8,128)(2,1)S(1)} %get-tuple-element.28.xb, bf16[2,256,1024]{2,1,0:T(8,128)(2,1)S(1)} %collective-permute-done.7.x0, bf16[2,256,1024]{2,1,0:T(8,128)(2,1)S(1)} %collective-permute-done.8.x1, ...), custom_call_target="tpu_custom_call" | custom-call | flops 6442450944 | bytes 8388608 | tf_op jit(solution)/shard_map/pallas_call | solution.py:617
  109.2 1.4 collective-permute-start.14
  110.5 2.2 %collective-permute-done.14.arrived = bf16[2,512,512]{2,1,0:T(8,128)(2,1)S(1)} collective-permute-done((bf16[2,512,512]{2,1,0:T(8,128)(2,1)S(1)}, bf16[2,512,512]{2,1,0:T(8,128)(2,1)S(1)}, u32[]{:S(2)}, u32[]{:S(2)}) %collective-permute-start.14) | collective-permute-done | bytes 1048608 | tf_op jit(solution)/shard_map/ppermute | solution.py:628
  113.6 8.7 %collective-permute-start.16 = (bf16[2,256,512]{2,1,0:T(8,128)(2,1)S(1)}, bf16[2,256,512]{2,1,0:T(8,128)(2,1)S(1)}, u32[]{:S(2)}, u32[]{:S(2)}) collective-permute-start(bf16[2,256,512]{2,1,0:T(8,128)(2,1)S(1)} %get-tuple-element.36), channel_id=1, source_target_pairs={{4,0},{0,4},{20,8},{16,12},{12,16},{8,20},{28,24},{24,28},{5,1},{1... | collective-permute-start | bytes 1572872 | tf_op jit(solution)/shard_map/ppermute | solution.py:641
  122.5 4.7 %collective-permute-start.15 = (bf16[2,256,512]{2,1,0:T(8,128)(2,1)S(1)}, bf16[2,256,512]{2,1,0:T(8,128)(2,1)S(1)}, u32[]{:S(2)}, u32[]{:S(2)}) collective-permute-start(bf16[2,256,512]{2,1,0:T(8,128)(2,1)S(1)} %get-tuple-element.35.own), channel_id=1, source_target_pairs={{16,8},{20,12},{8,16},{12,20},{17,9},{21,13},{9,17},{13,21},{18,10... | collective-permute-start | bytes 1572872 | tf_op jit(solution)/shard_map/ppermute | solution.py:641
  127.2 2.1 %collective-permute-done.16.rest_1_ = bf16[2,256,512]{2,1,0:T(8,128)(2,1)S(1)} collective-permute-done((bf16[2,256,512]{2,1,0:T(8,128)(2,1)S(1)}, bf16[2,256,512]{2,1,0:T(8,128)(2,1)S(1)}, u32[]{:S(2)}, u32[]{:S(2)}) %collective-permute-start.16) | collective-permute-done | bytes 524320 | tf_op jit(solution)/shard_map/ppermute | solution.py:641
  129.3 4.8 %collective-permute-done.17.rest_2_ = bf16[2,256,512]{2,1,0:T(8,128)(2,1)S(1)} collective-permute-done((bf16[2,256,512]{2,1,0:T(8,128)(2,1)S(1)}, bf16[2,256,512]{2,1,0:T(8,128)(2,1)S(1)}, u32[]{:S(2)}, u32[]{:S(2)}) %collective-permute-start.17) | collective-permute-done | bytes 524320 | tf_op jit(solution)/shard_map/ppermute | solution.py:641
  134.1 10.9 %collective-permute-done.18.rest_3_ = bf16[2,256,512]{2,1,0:T(8,128)(2,1)S(1)} collective-permute-done((bf16[2,256,512]{2,1,0:T(8,128)(2,1)S(1)}, bf16[2,256,512]{2,1,0:T(8,128)(2,1)S(1)}, u32[]{:S(2)}, u32[]{:S(2)}) %collective-permute-start.18) | collective-permute-done | bytes 524320 | tf_op jit(solution)/shard_map/ppermute | solution.py:641
  145.0 1.0 collective-permute-done.15.rest_0_
  146.0 2.2 %shard_map.64 = bf16[2,256,2048]{2,1,0:T(8,128)(2,1)} custom-call(s32[6]{0:T(128)S(1)} %stack.83.place, bf16[2,256,512]{2,1,0:T(8,128)(2,1)S(1)} %get-tuple-element.35.own, bf16[2,256,512]{2,1,0:T(8,128)(2,1)S(1)} %collective-permute-done.15.rest_0_, bf16[2,256,512]{2,1,0:T(8,128)(2,1)S(1)} %collective-permute-done.16.rest_1_, ...), custom_call_target="tpu_custom_call" | custom-call | tf_op jit(solution)/shard_map/pallas_call | solution.py:643
  (31 shorter events, 6.7 us)
Async XLA Ops:
  0.0 8.7 %copy-start.1 = (bf16[1,256,512]{2,1,0:T(8,128)(2,1)S(1)}, bf16[1,256,512]{2,1,0:T(8,128)(2,1)}, u32[]{:S(2)}) copy-start(bf16[1,256,512]{2,1,0:T(8,128)(2,1)} %param.7) | copy-start | bytes 786436
  0.0 0.9 copy-start.2
  1.0 0.9 copy-start.3
  3.2 16.5 %copy-start.4 = (s32[16]{0:T(128)S(1)}, s32[16]{0:T(128)}, u32[]{:S(2)}) copy-start(s32[16]{0:T(128)} %param.6) | copy-start | bytes 196
  3.2 39.3 %all-to-all-start = ((bf16[4,2,64,1024]{3,2,1,0:T(8,128)(2,1)}), bf16[4,2,64,1024]{3,2,1,0:T(8,128)(2,1)S(1)}, u32[]{:S(2)}, u32[]{:S(2)}) async-start(bf16[4,2,64,1024]{3,2,1,0:T(8,128)(2,1)} %shard_map.55), calls=%async_computation | async-start | bytes 2097152 | tf_op jit(solution)/shard_map/all_to_all | solution.py:527
  8.7 1.6 %copy-start = (bf16[2,1,256,2048]{3,2,1,0:T(8,128)(2,1)S(1)}, bf16[2,1,256,2048]{3,2,1,0:T(8,128)(2,1)}, u32[]{:S(2)}) copy-start(bf16[2,1,256,2048]{3,2,1,0:T(8,128)(2,1)} %param.5) | copy-start | bytes 6291460
  12.6 16.3 %collective-permute-start.1 = (bf16[2,288,512]{2,1,0:T(8,128)(2,1)}, bf16[2,288,512]{2,1,0:T(8,128)(2,1)S(1)}, u32[]{:S(2)}, u32[]{:S(2)}) collective-permute-start(bf16[2,288,512]{2,1,0:T(8,128)(2,1)} %get-tuple-element.23), channel_id=1, source_target_pairs={{0,4},{4,0},{8,20},{12,16},{16,12},{20,8},{24,28},{28,24},{1,5},{5... | collective-permute-start | bytes 1769480 | tf_op jit(solution)/shard_map/ppermute | solution.py:525
  15.7 15.6 %collective-permute-start.2 = (bf16[2,288,512]{2,1,0:T(8,128)(2,1)}, bf16[2,288,512]{2,1,0:T(8,128)(2,1)S(1)}, u32[]{:S(2)}, u32[]{:S(2)}) collective-permute-start(bf16[2,288,512]{2,1,0:T(8,128)(2,1)} %get-tuple-element.24), channel_id=1, source_target_pairs={{0,16},{4,20},{8,0},{12,4},{16,24},{20,28},{24,8},{28,12},{1,17},{... | collective-permute-start | bytes 1769480 | tf_op jit(solution)/shard_map/ppermute | solution.py:525
  15.7 26.8 %collective-permute-start.3 = (bf16[2,288,512]{2,1,0:T(8,128)(2,1)}, bf16[2,288,512]{2,1,0:T(8,128)(2,1)S(1)}, u32[]{:S(2)}, u32[]{:S(2)}) collective-permute-start(bf16[2,288,512]{2,1,0:T(8,128)(2,1)} %get-tuple-element.25), channel_id=1, source_target_pairs={{0,20},{4,16},{8,4},{12,0},{16,28},{20,24},{24,12},{28,8},{1,21},{... | collective-permute-start | bytes 1769480 | tf_op jit(solution)/shard_map/ppermute | solution.py:525
  16.3 26.2 %collective-permute-start = (bf16[2,288,512]{2,1,0:T(8,128)(2,1)S(1)}, bf16[2,288,512]{2,1,0:T(8,128)(2,1)}, u32[]{:S(2)}, u32[]{:S(2)}) collective-permute-start(bf16[2,288,512]{2,1,0:T(8,128)(2,1)S(1)} %get-tuple-element.22.own), channel_id=1, source_target_pairs={{8,16},{12,20},{16,8},{20,12},{9,17},{13,21},{17,9},{21,13},{10,18... | collective-permute-start | bytes 1769480 | tf_op jit(solution)/shard_map/ppermute | solution.py:525
  43.9 20.6 %collective-permute-start.4 = (bf16[256,1024]{1,0:T(8,128)(2,1)S(1)}, bf16[256,1024]{1,0:T(8,128)(2,1)S(1)}, u32[]{:S(2)}, u32[]{:S(2)}) collective-permute-start(bf16[256,1024]{1,0:T(8,128)(2,1)S(1)} %get-tuple-element.26.x_column), channel_id=1, source_target_pairs={{0,4},{4,0},{1,5},{5,1},{2,6},{6,2},{3,7},{7,3},{8,12},{12,8},{9,1... | collective-permute-start | bytes 1572872 | tf_op jit(solution)/shard_map/ppermute | solution.py:549
  44.8 19.7 %collective-permute-start.6 = (bf16[1024,256]{1,0:T(8,128)(2,1)S(1)}, bf16[1024,256]{1,0:T(8,128)(2,1)S(1)}, u32[]{:S(2)}, u32[]{:S(2)}) collective-permute-start(bf16[1024,256]{1,0:T(8,128)(2,1)S(1)} %get-tuple-element.27.y_column), channel_id=1, source_target_pairs={{0,16},{4,20},{8,0},{12,4},{16,24},{20,28},{24,8},{28,12},{1,17},{... | collective-permute-start | bytes 1572872 | tf_op jit(solution)/shard_map/ppermute | solution.py:546
  44.8 19.7 %collective-permute-start.5 = (bf16[1024,256]{1,0:T(8,128)(2,1)S(1)}, bf16[1024,256]{1,0:T(8,128)(2,1)S(1)}, u32[]{:S(2)}, u32[]{:S(2)}) collective-permute-start(bf16[1024,256]{1,0:T(8,128)(2,1)S(1)} %get-tuple-element.27.y_column), channel_id=1, source_target_pairs={{8,16},{12,20},{16,8},{20,12},{9,17},{13,21},{17,9},{21,13},{10,18... | collective-permute-start | bytes 1572872 | tf_op jit(solution)/shard_map/ppermute | solution.py:546
  49.0 13.1 %collective-permute-start.10 = (bf16[4,64,512]{2,1,0:T(8,128)(2,1)S(1)}, bf16[4,64,512]{2,1,0:T(8,128)(2,1)S(1)}, u32[]{:S(2)}, u32[]{:S(2)}) collective-permute-start(bf16[4,64,512]{2,1,0:T(8,128)(2,1)S(1)} %bitcast.33), channel_id=1, source_target_pairs={{0,1},{1,0},{2,3},{3,2},{4,5},{5,4},{6,7},{7,6},{8,9},{9,8},{10,11... | collective-permute-start | bytes 786440 | tf_op jit(solution)/shard_map/ppermute | solution.py:552
  50.8 16.9 %collective-permute-start.11 = (bf16[4,64,512]{2,1,0:T(8,128)(2,1)S(1)}, bf16[4,64,512]{2,1,0:T(8,128)(2,1)S(1)}, u32[]{:S(2)}, u32[]{:S(2)}) collective-permute-start(bf16[4,64,512]{2,1,0:T(8,128)(2,1)S(1)} %bitcast.34), channel_id=1, source_target_pairs={{0,2},{1,3},{2,0},{3,1},{4,6},{5,7},{6,4},{7,5},{8,10},{9,11},{10,... | collective-permute-start | bytes 786440 | tf_op jit(solution)/shard_map/ppermute | solution.py:552
  62.2 14.6 %collective-permute-start.12 = (bf16[4,64,512]{2,1,0:T(8,128)(2,1)S(1)}, bf16[4,64,512]{2,1,0:T(8,128)(2,1)S(1)}, u32[]{:S(2)}, u32[]{:S(2)}) collective-permute-start(bf16[4,64,512]{2,1,0:T(8,128)(2,1)S(1)} %collective-permute-done.10.c1), channel_id=1, source_target_pairs={{0,2},{1,3},{2,0},{3,1},{4,6},{5,7},{6,4},{7,5},{8,10},{9,11},{10,... | collective-permute-start | bytes 786440 | tf_op jit(solution)/shard_map/ppermute | solution.py:552
  65.3 25.7 %collective-permute-start.8 = (bf16[2,256,1024]{2,1,0:T(8,128)(2,1)S(1)}, bf16[2,256,1024]{2,1,0:T(8,128)(2,1)S(1)}, u32[]{:S(2)}, u32[]{:S(2)}) collective-permute-start(bf16[2,256,1024]{2,1,0:T(8,128)(2,1)S(1)} %get-tuple-element.28.xb), channel_id=1, source_target_pairs={{0,16},{4,20},{8,0},{12,4},{16,24},{20,28},{24,8},{28,12},{1,17},{... | collective-permute-start | bytes 3145736 | tf_op jit(solution)/shard_map/ppermute | solution.py:546
  65.3 25.7 %collective-permute-start.7 = (bf16[2,256,1024]{2,1,0:T(8,128)(2,1)S(1)}, bf16[2,256,1024]{2,1,0:T(8,128)(2,1)S(1)}, u32[]{:S(2)}, u32[]{:S(2)}) collective-permute-start(bf16[2,256,1024]{2,1,0:T(8,128)(2,1)S(1)} %get-tuple-element.28.xb), channel_id=1, source_target_pairs={{8,16},{12,20},{16,8},{20,12},{9,17},{13,21},{17,9},{21,13},{10,18... | collective-permute-start | bytes 3145736 | tf_op jit(solution)/shard_map/ppermute | solution.py:546
  67.2 23.8 %collective-permute-start.9 = (bf16[2,1024,256]{2,1,0:T(8,128)(2,1)S(1)}, bf16[2,1024,256]{2,1,0:T(8,128)(2,1)S(1)}, u32[]{:S(2)}, u32[]{:S(2)}) collective-permute-start(bf16[2,1024,256]{2,1,0:T(8,128)(2,1)S(1)} %get-tuple-element.29.yb), channel_id=1, source_target_pairs={{0,4},{4,0},{1,5},{5,1},{2,6},{6,2},{3,7},{7,3},{8,12},{12,8},{9,1... | collective-permute-start | bytes 3145736 | tf_op jit(solution)/shard_map/ppermute | solution.py:549
  91.6 8.5 %collective-permute-start.13 = (bf16[2,512,512]{2,1,0:T(8,128)(2,1)S(1)}, bf16[2,512,512]{2,1,0:T(8,128)(2,1)S(1)}, u32[]{:S(2)}, u32[]{:S(2)}) collective-permute-start(bf16[2,512,512]{2,1,0:T(8,128)(2,1)S(1)} %get-tuple-element.32.w_high), channel_id=1, source_target_pairs={{0,8},{16,24},{1,9},{17,25},{2,10},{18,26},{3,11},{19,27},{4,12},{... | collective-permute-start | bytes 3145736 | tf_op jit(solution)/shard_map/ppermute | solution.py:616
  109.2 3.6 %collective-permute-start.14 = (bf16[2,512,512]{2,1,0:T(8,128)(2,1)S(1)}, bf16[2,512,512]{2,1,0:T(8,128)(2,1)S(1)}, u32[]{:S(2)}, u32[]{:S(2)}) collective-permute-start(bf16[2,512,512]{2,1,0:T(8,128)(2,1)S(1)} %get-tuple-element.33), channel_id=1, source_target_pairs={{8,0},{24,16},{9,1},{25,17},{10,2},{26,18},{11,3},{27,19},{12,4},{... | collective-permute-start | bytes 3145736 | tf_op jit(solution)/shard_map/ppermute | solution.py:628
  113.6 15.7 %collective-permute-start.16 = (bf16[2,256,512]{2,1,0:T(8,128)(2,1)S(1)}, bf16[2,256,512]{2,1,0:T(8,128)(2,1)S(1)}, u32[]{:S(2)}, u32[]{:S(2)}) collective-permute-start(bf16[2,256,512]{2,1,0:T(8,128)(2,1)S(1)} %get-tuple-element.36), channel_id=1, source_target_pairs={{4,0},{0,4},{20,8},{16,12},{12,16},{8,20},{28,24},{24,28},{5,1},{1... | collective-permute-start | bytes 1572872 | tf_op jit(solution)/shard_map/ppermute | solution.py:641
  122.3 11.8 %collective-permute-start.17 = (bf16[2,256,512]{2,1,0:T(8,128)(2,1)S(1)}, bf16[2,256,512]{2,1,0:T(8,128)(2,1)S(1)}, u32[]{:S(2)}, u32[]{:S(2)}) collective-permute-start(bf16[2,256,512]{2,1,0:T(8,128)(2,1)S(1)} %get-tuple-element.37), channel_id=1, source_target_pairs={{16,0},{20,4},{0,8},{4,12},{24,16},{28,20},{8,24},{12,28},{17,1},{... | collective-permute-start | bytes 1572872 | tf_op jit(solution)/shard_map/ppermute | solution.py:641
  122.3 22.7 %collective-permute-start.18 = (bf16[2,256,512]{2,1,0:T(8,128)(2,1)S(1)}, bf16[2,256,512]{2,1,0:T(8,128)(2,1)S(1)}, u32[]{:S(2)}, u32[]{:S(2)}) collective-permute-start(bf16[2,256,512]{2,1,0:T(8,128)(2,1)S(1)} %get-tuple-element.38), channel_id=1, source_target_pairs={{20,0},{16,4},{4,8},{0,12},{28,16},{24,20},{12,24},{8,28},{21,1},{... | collective-permute-start | bytes 1572872 | tf_op jit(solution)/shard_map/ppermute | solution.py:641
  122.5 23.6 %collective-permute-start.15 = (bf16[2,256,512]{2,1,0:T(8,128)(2,1)S(1)}, bf16[2,256,512]{2,1,0:T(8,128)(2,1)S(1)}, u32[]{:S(2)}, u32[]{:S(2)}) collective-permute-start(bf16[2,256,512]{2,1,0:T(8,128)(2,1)S(1)} %get-tuple-element.35.own), channel_id=1, source_target_pairs={{16,8},{20,12},{8,16},{12,20},{17,9},{21,13},{9,17},{13,21},{18,10... | collective-permute-start | bytes 1572872 | tf_op jit(solution)/shard_map/ppermute | solution.py:641

commit v18 on v17

--- a/solution.py
+++ b/solution.py
@@ -16,7 +16,7 @@
 in_smem = pl.BlockSpec(memory_space=pltpu.SMEM)
 in_vmem = pl.BlockSpec(memory_space=pltpu.VMEM)
 
-info_member, info_piece, info_slot, info_half, info_block, info_self = 3, 4, 12, 14, 16, 20
+info_member, info_piece, info_slot, info_half, info_block, info_self = 3, 4, 12, 14, 16, 18
 
 
 def shifted(x, axis, by):
@@ -267,11 +267,11 @@
     wait_all(copies)
 
 
-def weight_kernel(info, c0, c1, c2, c3, weights, sems):
+def weight_kernel(info, c0, c1, weights, sems):
     height = c0.shape[1]
     half_height = weights.shape[1] // 2
     copies = []
-    for index, block in enumerate((c0, c1, c2, c3)):
+    for index, block in enumerate((c0, c1)):
         for turn in range(block.shape[0]):
             slot, half = info[info_piece + 2 * turn], info[info_piece + 2 * turn + 1]
             start = half * half_height + info[info_block + index] * height
@@ -494,14 +494,12 @@
     for a, b in rounds:
         entries += [(group + a) % 2, (own_x - b) % px_count]
     entries += [group, (group + 1) % 2, own_x, (own_x + 1) % 2]
-    pair = own_y // 2 * 2
-    entries += [own_y, pair + (own_y + 1) % 2, (own_y + 2) % 4, (pair + 2) % 4 + (own_y + 1) % 2]
-    entries += [group == member]
+    entries += [own_y % 2, (own_y + 1) % 2, group == member]
     info = jnp.stack([jnp.asarray(entry, jnp.int32) for entry in entries])
 
     sends_to = jnp.stack(
         [((member + a) % 2) * px_count + (own_x + b) % px_count for a, b in rounds]
-        + [own_y, group == member]
+        + [own_y % 2, group == member]
     ).astype(jnp.int32)
     piece_shape = jax.ShapeDtypeStruct((2, rows_here, order), bf16)
     blocks = pl.pallas_call(
@@ -512,7 +510,7 @@
         scratch_shapes=[pltpu.SemaphoreType.DMA((py_count, 2, 2))],
         compiler_params=params,
     )(x_factor[0], y_factor[0])
-    tall = height // 2
+    tall = rows_here // 4
     packed = pl.pallas_call(
         pack_kernel,
         out_shape=[jax.ShapeDtypeStruct((2, rows_here + tall, order), bf16)] * len(rounds),
@@ -540,7 +538,7 @@
         scratch_shapes=[pltpu.SemaphoreType.DMA((len(rounds),))],
         compiler_params=params,
     )(info, blocks, packed[0], *pieces)
-    rows_held = rows_held.reshape(len(rounds), height, order)
+    rows_held = rows_held.reshape(len(rounds), 2 * tall, order)
 
     def across(block, a):
         return lax.ppermute(block, ("sec", "px"), pairs(a, 0))
@@ -554,7 +552,6 @@
     y_near = [across(y_turned, a) for a in range(2)]
     x_aside = aside(x_column)
     rows_next = over_z(rows_held, 1)
-    rows_far = over_z(rows_held, 2)
     full_shape = jax.ShapeDtypeStruct((2, order, order), bf16)
     double_shape = jax.ShapeDtypeStruct((2, 2, order, order), bf16)
     rhs = pl.pallas_call(
@@ -580,14 +577,11 @@
     weights = pl.pallas_call(
         weight_kernel,
         out_shape=full_shape,
-        in_specs=[in_smem] + [anywhere] * 4,
+        in_specs=[in_smem] + [anywhere] * 2,
         out_specs=in_vmem,
-        scratch_shapes=[pltpu.SemaphoreType.DMA((4, len(rounds)))],
-        compiler_params=params,
-        cost_estimate=pl.CostEstimate(
-            flops=3 * 10**10, bytes_accessed=2**21, transcendentals=0
-        ),
-    )(info, rows_held, rows_next, rows_far, over_z(rows_next, 2))
+        scratch_shapes=[pltpu.SemaphoreType.DMA((2, len(rounds)))],
+        compiler_params=params,
+    )(info, rows_held, rows_next)
     layers = (info, x_both, *x_across, y_both, y_far, weights)
     layer_specs = [in_smem] + [anywhere] * 3 + [in_vmem] * 3
     solver_scratch = [

time: 149 us -> 149 us (level)
    ppermute x3 -> x1, waiting for transfers between devices: 18.3 us -> 11.9 us  [over_z(): return lax.ppermute(block, 'py', [(z, z ^ bit) for z in range(py_count)])]
    ppermute x4, waiting for transfers between devices: 0.01 us -> 3.82 us  [across(): return lax.ppermute(block, ('sec', 'px'), pairs(a, 0))]
    ppermute x4, waiting for transfers between devices: 19.5 us -> 22.8 us  [on_device(): lax.ppermute(piece, ('sec', 'px'), pairs(a, b))]
    ppermute x4, starting transfers between devices: 6.13 us -> 8.85 us  [across(): return lax.ppermute(block, ('sec', 'px'), pairs(a, 0))]
    ppermute x3 -> x1, starting transfers between devices: 4.57 us -> 1.85 us  [over_z(): return lax.ppermute(block, 'py', [(z, z ^ bit) for z in range(py_count)])]
  transfers between devices with their start and end apart: 20 -> 18, of which waited for: 12 -> 14; matrix products, arithmetic and copies ran while one was open for 1% -> 0% of each run, Pallas kernels for 5% -> 4%
where the time goes in v18:
time: 149 us; the launch traced here: 148 us
  waiting for transfers between devices  77.1 us (52%)
  starting transfers between devices  41.4 us (28%)
  Pallas kernels  22.8 us (15%)
  local copies, waits for them, and re-layouts  4.19 us (3%)
  between operations  2.71 us (2%)
    ppermute x4, waiting for transfers between devices, on_device(): lax.ppermute(piece, ('sec', 'px'), pairs(a, b))  22.8 us
    ppermute x4, waiting for transfers between devices, on_device(): lax.ppermute(piece, ('sec', 'px'), back_pairs(a, b))  19 us
    ppermute x4, starting transfers between devices, on_device(): lax.ppermute(piece, ('sec', 'px'), back_pairs(a, b))  14.5 us
    ppermute x1, waiting for transfers between devices, over_z(): return lax.ppermute(block, 'py', [(z, z ^ bit) for z in range(py_count)])  11.9 us
    ppermute x2, waiting for transfers between devices, aside(): return lax.ppermute(block, 'px', [(y, (y + 1) % 2) for y in range(2)])  10.7 us
    pallas_call x1, Pallas kernels, on_device(): pl.pallas_call(last_kernel, out_shape=[double_shape, full_shape], in_spec...  9.12 us
    ppermute x4, starting transfers between devices, across(): return lax.ppermute(block, ('sec', 'px'), pairs(a, 0))  8.85 us
    ppermute x4, starting transfers between devices, on_device(): lax.ppermute(piece, ('sec', 'px'), pairs(a, b))  6.94 us
  transfers between devices with their start and end apart: 18, of which 14 were waited for; matrix products, arithmetic and copies ran while one was open for 0% of the time, Pallas kernels for 4%

profile of v18, /device:TPU:1, one launch (start us, length us, event | category | flops | bytes accessed | tf_op | source)
XLA Modules:
  0.0 148.2 jit_solution(15901027908586246296)
XLA Ops:
  1.9 1.3 shard_map.55
  3.2 5.4 %all-to-all-start = ((bf16[4,2,64,1024]{3,2,1,0:T(8,128)(2,1)}), bf16[4,2,64,1024]{3,2,1,0:T(8,128)(2,1)S(1)}, u32[]{:S(2)}, u32[]{:S(2)}) async-start(bf16[4,2,64,1024]{3,2,1,0:T(8,128)(2,1)} %shard_map.55), calls=%async_computation | async-start | bytes 2097152 | tf_op jit(solution)/shard_map/all_to_all | solution.py:525
  8.7 1.6 %copy-done = bf16[2,1,256,2048]{3,2,1,0:T(8,128)(2,1)S(1)} copy-done((bf16[2,1,256,2048]{3,2,1,0:T(8,128)(2,1)S(1)}, bf16[2,1,256,2048]{3,2,1,0:T(8,128)(2,1)}, u32[]{:S(2)}) %copy-start) | copy-done | bytes 2097176
  10.3 2.5 %shard_map.56 = (bf16[2,320,512]{2,1,0:T(8,128)(2,1)S(1)}, bf16[2,320,512]{2,1,0:T(8,128)(2,1)}, bf16[2,320,512]{2,1,0:T(8,128)(2,1)}, bf16[2,320,512]{2,1,0:T(8,128)(2,1)}) custom-call(s32[6]{0:T(128)S(1)} %stack.77.place, bf16[2,256,2048]{2,1,0:T(8,128)(2,1)S(1)} %bitcast.27, bf16[4,64,512]{2,1,0:T(8,128)(2,1)S(1)} %bitcast.30), custom_call_target="tpu_custom_call" | custom-call | tf_op jit(solution)/shard_map/pallas_call | solution.py:514
  12.8 3.1 %collective-permute-start.1 = (bf16[2,320,512]{2,1,0:T(8,128)(2,1)}, bf16[2,320,512]{2,1,0:T(8,128)(2,1)S(1)}, u32[]{:S(2)}, u32[]{:S(2)}) collective-permute-start(bf16[2,320,512]{2,1,0:T(8,128)(2,1)} %get-tuple-element.23), channel_id=1, source_target_pairs={{0,4},{4,0},{8,20},{12,16},{16,12},{20,8},{24,28},{28,24},{1,5},{5... | collective-permute-start | bytes 1966088 | tf_op jit(solution)/shard_map/ppermute | solution.py:523
  16.5 3.3 %collective-permute-start = (bf16[2,320,512]{2,1,0:T(8,128)(2,1)S(1)}, bf16[2,320,512]{2,1,0:T(8,128)(2,1)}, u32[]{:S(2)}, u32[]{:S(2)}) collective-permute-start(bf16[2,320,512]{2,1,0:T(8,128)(2,1)S(1)} %get-tuple-element.22.own), channel_id=1, source_target_pairs={{8,16},{12,20},{16,8},{20,12},{9,17},{13,21},{17,9},{21,13},{10,18... | collective-permute-start | bytes 1966088 | tf_op jit(solution)/shard_map/ppermute | solution.py:523
  22.8 7.8 %collective-permute-done.1.p1 = bf16[2,320,512]{2,1,0:T(8,128)(2,1)S(1)} collective-permute-done((bf16[2,320,512]{2,1,0:T(8,128)(2,1)}, bf16[2,320,512]{2,1,0:T(8,128)(2,1)S(1)}, u32[]{:S(2)}, u32[]{:S(2)}) %collective-permute-start.1) | collective-permute-done | bytes 655392 | tf_op jit(solution)/shard_map/ppermute | solution.py:523
  30.7 2.4 %collective-permute-done.2.p2 = bf16[2,320,512]{2,1,0:T(8,128)(2,1)S(1)} collective-permute-done((bf16[2,320,512]{2,1,0:T(8,128)(2,1)}, bf16[2,320,512]{2,1,0:T(8,128)(2,1)S(1)}, u32[]{:S(2)}, u32[]{:S(2)}) %collective-permute-start.2) | collective-permute-done | bytes 655392 | tf_op jit(solution)/shard_map/ppermute | solution.py:523
  33.0 12.6 %collective-permute-done.3.p3 = bf16[2,320,512]{2,1,0:T(8,128)(2,1)} collective-permute-done((bf16[2,320,512]{2,1,0:T(8,128)(2,1)}, bf16[2,320,512]{2,1,0:T(8,128)(2,1)}, u32[]{:S(2)}, u32[]{:S(2)}) %collective-permute-start.3) | collective-permute-done | bytes 655392 | tf_op jit(solution)/shard_map/ppermute | solution.py:523
  45.6 1.7 %shard_map.57 = (bf16[256,1024]{1,0:T(8,128)(2,1)S(1)}, bf16[1024,256]{1,0:T(8,128)(2,1)S(1)}, bf16[4,2,64,512]{3,2,1,0:T(8,128)(2,1)S(1)}) custom-call(s32[19]{0:T(128)S(1)} %stack.90.info, bf16[4,2,64,1024]{3,2,1,0:T(8,128)(2,1)S(1)} %all-to-all-done.blocks, bf16[2,320,512]{2,1,0:T(8,128)(2,1)S(1)} %get-tuple-element.22.own, ...), custom_call_target="tpu_custom_call" | custom-call | tf_op jit(solution)/shard_map/pallas_call | solution.py:529
  48.3 4.2 %collective-permute-start.5 = (bf16[1024,256]{1,0:T(8,128)(2,1)S(1)}, bf16[1024,256]{1,0:T(8,128)(2,1)S(1)}, u32[]{:S(2)}, u32[]{:S(2)}) collective-permute-start(bf16[1024,256]{1,0:T(8,128)(2,1)S(1)} %get-tuple-element.27.y_column), channel_id=1, source_target_pairs={{8,16},{12,20},{16,8},{20,12},{9,17},{13,21},{17,9},{21,13},{10,18... | collective-permute-start | bytes 1572872 | tf_op jit(solution)/shard_map/ppermute | solution.py:544
  52.4 1.8 %shard_map.58.rhs = bf16[2,2,512,512]{3,2,1,0:T(8,128)(2,1)S(1)} custom-call(s32[19]{0:T(128)S(1)} %stack.90.info, bf16[2,320,512]{2,1,0:T(8,128)(2,1)S(1)} %get-tuple-element.22.own, bf16[2,320,512]{2,1,0:T(8,128)(2,1)} %collective-permute-done.p0, bf16[2,320,512]{2,1,0:T(8,128)(2,1)S(1)} %collective-permute-done.1.p1, ...), custom_call_target="tpu_custom_call" | custom-call | tf_op jit(solution)/shard_map/pallas_call | solution.py:557
  54.3 6.9 %collective-permute-done.4.x_aside = bf16[256,1024]{1,0:T(8,128)(2,1)S(1)} collective-permute-done((bf16[256,1024]{1,0:T(8,128)(2,1)S(1)}, bf16[256,1024]{1,0:T(8,128)(2,1)S(1)}, u32[]{:S(2)}, u32[]{:S(2)}) %collective-permute-start.4) | collective-permute-done | bytes 524320 | tf_op jit(solution)/shard_map/ppermute | solution.py:547
  61.2 1.7 %collective-permute-done.5.y0 = bf16[1024,256]{1,0:T(8,128)(2,1)S(1)} collective-permute-done((bf16[1024,256]{1,0:T(8,128)(2,1)S(1)}, bf16[1024,256]{1,0:T(8,128)(2,1)S(1)}, u32[]{:S(2)}, u32[]{:S(2)}) %collective-permute-start.5) | collective-permute-done | bytes 524320 | tf_op jit(solution)/shard_map/ppermute | solution.py:544
  63.9 4.7 %collective-permute-start.7 = (bf16[2,256,1024]{2,1,0:T(8,128)(2,1)S(1)}, bf16[2,256,1024]{2,1,0:T(8,128)(2,1)S(1)}, u32[]{:S(2)}, u32[]{:S(2)}) collective-permute-start(bf16[2,256,1024]{2,1,0:T(8,128)(2,1)S(1)} %get-tuple-element.28.xb), channel_id=1, source_target_pairs={{8,16},{12,20},{16,8},{20,12},{9,17},{13,21},{17,9},{21,13},{10,18... | collective-permute-start | bytes 3145736 | tf_op jit(solution)/shard_map/ppermute | solution.py:544
  68.6 1.9 %collective-permute-start.10 = (bf16[4,128,512]{2,1,0:T(8,128)(2,1)S(1)}, bf16[4,128,512]{2,1,0:T(8,128)(2,1)S(1)}, u32[]{:S(2)}, u32[]{:S(2)}) collective-permute-start(bf16[4,128,512]{2,1,0:T(8,128)(2,1)S(1)} %bitcast.28), channel_id=1, source_target_pairs={{0,1},{1,0},{2,3},{3,2},{4,5},{5,4},{6,7},{7,6},{8,9},{9,8},{10,11... | collective-permute-start | bytes 1572872 | tf_op jit(solution)/shard_map/ppermute | solution.py:550
  70.4 11.9 %collective-permute-done.10.c1 = bf16[4,128,512]{2,1,0:T(8,128)(2,1)S(1)} collective-permute-done((bf16[4,128,512]{2,1,0:T(8,128)(2,1)S(1)}, bf16[4,128,512]{2,1,0:T(8,128)(2,1)S(1)}, u32[]{:S(2)}, u32[]{:S(2)}) %collective-permute-start.10) | collective-permute-done | bytes 524320 | tf_op jit(solution)/shard_map/ppermute | solution.py:550
  82.3 2.0 %shard_map.60.weights = bf16[2,512,512]{2,1,0:T(8,128)(2,1)S(1)} custom-call(s32[19]{0:T(128)S(1)} %stack.90.info, bf16[4,128,512]{2,1,0:T(8,128)(2,1)S(1)} %bitcast.29, bf16[4,128,512]{2,1,0:T(8,128)(2,1)S(1)} %collective-permute-done.10.c1), custom_call_target="tpu_custom_call" | custom-call | tf_op jit(solution)/shard_map/pallas_call | solution.py:577
  84.3 3.8 %collective-permute-done.9.yf = bf16[2,1024,256]{2,1,0:T(8,128)(2,1)S(1)} collective-permute-done((bf16[2,1024,256]{2,1,0:T(8,128)(2,1)S(1)}, bf16[2,1024,256]{2,1,0:T(8,128)(2,1)S(1)}, u32[]{:S(2)}, u32[]{:S(2)}) %collective-permute-start.9) | collective-permute-done | bytes 1048608 | tf_op jit(solution)/shard_map/ppermute | solution.py:547
  88.1 2.2 %collective-permute-done.7.x0 = bf16[2,256,1024]{2,1,0:T(8,128)(2,1)S(1)} collective-permute-done((bf16[2,256,1024]{2,1,0:T(8,128)(2,1)S(1)}, bf16[2,256,1024]{2,1,0:T(8,128)(2,1)S(1)}, u32[]{:S(2)}, u32[]{:S(2)}) %collective-permute-start.7) | collective-permute-done | bytes 1048608 | tf_op jit(solution)/shard_map/ppermute | solution.py:544
  90.8 1.3 collective-permute-start.11
  92.1 6.7 %collective-permute-done.11.arrived = bf16[2,512,512]{2,1,0:T(8,128)(2,1)S(1)} collective-permute-done((bf16[2,512,512]{2,1,0:T(8,128)(2,1)S(1)}, bf16[2,512,512]{2,1,0:T(8,128)(2,1)S(1)}, u32[]{:S(2)}, u32[]{:S(2)}) %collective-permute-start.11) | collective-permute-done | bytes 1048608 | tf_op jit(solution)/shard_map/ppermute | solution.py:610
  98.8 9.1 %shard_map.62 = (bf16[2,2,512,512]{3,2,1,0:T(8,128)(2,1)S(1)}, bf16[2,512,512]{2,1,0:T(8,128)(2,1)S(1)}) custom-call(s32[19]{0:T(128)S(1)} %stack.90.info, bf16[2,256,1024]{2,1,0:T(8,128)(2,1)S(1)} %get-tuple-element.28.xb, bf16[2,256,1024]{2,1,0:T(8,128)(2,1)S(1)} %collective-permute-done.7.x0, bf16[2,256,1024]{2,1,0:T(8,128)(2,1)S(1)} %collective-permute-done.8.x1, ...), custom_call_target="tpu_custom_call" | custom-call | flops 6442450944 | bytes 8388608 | tf_op jit(solution)/shard_map/pallas_call | solution.py:611
  108.0 1.4 collective-permute-start.12
  109.3 2.2 %collective-permute-done.12.arrived = bf16[2,512,512]{2,1,0:T(8,128)(2,1)S(1)} collective-permute-done((bf16[2,512,512]{2,1,0:T(8,128)(2,1)S(1)}, bf16[2,512,512]{2,1,0:T(8,128)(2,1)S(1)}, u32[]{:S(2)}, u32[]{:S(2)}) %collective-permute-start.12) | collective-permute-done | bytes 1048608 | tf_op jit(solution)/shard_map/ppermute | solution.py:622
  112.4 10.4 %collective-permute-start.14 = (bf16[2,256,512]{2,1,0:T(8,128)(2,1)S(1)}, bf16[2,256,512]{2,1,0:T(8,128)(2,1)S(1)}, u32[]{:S(2)}, u32[]{:S(2)}) collective-permute-start(bf16[2,256,512]{2,1,0:T(8,128)(2,1)S(1)} %get-tuple-element.36), channel_id=1, source_target_pairs={{4,0},{0,4},{20,8},{16,12},{12,16},{8,20},{28,24},{24,28},{5,1},{1... | collective-permute-start | bytes 1572872 | tf_op jit(solution)/shard_map/ppermute | solution.py:635
  123.0 3.9 %collective-permute-start.13 = (bf16[2,256,512]{2,1,0:T(8,128)(2,1)S(1)}, bf16[2,256,512]{2,1,0:T(8,128)(2,1)S(1)}, u32[]{:S(2)}, u32[]{:S(2)}) collective-permute-start(bf16[2,256,512]{2,1,0:T(8,128)(2,1)S(1)} %get-tuple-element.35.own), channel_id=1, source_target_pairs={{16,8},{20,12},{8,16},{12,20},{17,9},{21,13},{9,17},{13,21},{18,10... | collective-permute-start | bytes 1572872 | tf_op jit(solution)/shard_map/ppermute | solution.py:635
  126.8 3.0 %collective-permute-done.14.rest_1_ = bf16[2,256,512]{2,1,0:T(8,128)(2,1)S(1)} collective-permute-done((bf16[2,256,512]{2,1,0:T(8,128)(2,1)S(1)}, bf16[2,256,512]{2,1,0:T(8,128)(2,1)S(1)}, u32[]{:S(2)}, u32[]{:S(2)}) %collective-permute-start.14) | collective-permute-done | bytes 524320 | tf_op jit(solution)/shard_map/ppermute | solution.py:635
  129.8 4.8 %collective-permute-done.15.rest_2_ = bf16[2,256,512]{2,1,0:T(8,128)(2,1)S(1)} collective-permute-done((bf16[2,256,512]{2,1,0:T(8,128)(2,1)S(1)}, bf16[2,256,512]{2,1,0:T(8,128)(2,1)S(1)}, u32[]{:S(2)}, u32[]{:S(2)}) %collective-permute-start.15) | collective-permute-done | bytes 524320 | tf_op jit(solution)/shard_map/ppermute | solution.py:635
  134.6 9.2 %collective-permute-done.16.rest_3_ = bf16[2,256,512]{2,1,0:T(8,128)(2,1)S(1)} collective-permute-done((bf16[2,256,512]{2,1,0:T(8,128)(2,1)S(1)}, bf16[2,256,512]{2,1,0:T(8,128)(2,1)S(1)}, u32[]{:S(2)}, u32[]{:S(2)}) %collective-permute-start.16) | collective-permute-done | bytes 524320 | tf_op jit(solution)/shard_map/ppermute | solution.py:635
  143.8 2.0 %collective-permute-done.13.rest_0_ = bf16[2,256,512]{2,1,0:T(8,128)(2,1)S(1)} collective-permute-done((bf16[2,256,512]{2,1,0:T(8,128)(2,1)S(1)}, bf16[2,256,512]{2,1,0:T(8,128)(2,1)S(1)}, u32[]{:S(2)}, u32[]{:S(2)}) %collective-permute-start.13) | collective-permute-done | bytes 524320 | tf_op jit(solution)/shard_map/ppermute | solution.py:635
  145.8 2.2 %shard_map.64 = bf16[2,256,2048]{2,1,0:T(8,128)(2,1)} custom-call(s32[6]{0:T(128)S(1)} %stack.77.place, bf16[2,256,512]{2,1,0:T(8,128)(2,1)S(1)} %get-tuple-element.35.own, bf16[2,256,512]{2,1,0:T(8,128)(2,1)S(1)} %collective-permute-done.13.rest_0_, bf16[2,256,512]{2,1,0:T(8,128)(2,1)S(1)} %collective-permute-done.14.rest_1_, ...), custom_call_target="tpu_custom_call" | custom-call | tf_op jit(solution)/shard_map/pallas_call | solution.py:637
  (27 shorter events, 6.7 us)
Async XLA Ops:
  0.0 8.7 %copy-start.1 = (bf16[1,256,512]{2,1,0:T(8,128)(2,1)S(1)}, bf16[1,256,512]{2,1,0:T(8,128)(2,1)}, u32[]{:S(2)}) copy-start(bf16[1,256,512]{2,1,0:T(8,128)(2,1)} %param.7) | copy-start | bytes 786436
  0.0 0.9 copy-start.2
  1.0 0.9 copy-start.3
  3.2 16.7 %copy-start.4 = (s32[16]{0:T(128)S(1)}, s32[16]{0:T(128)}, u32[]{:S(2)}) copy-start(s32[16]{0:T(128)} %param.6) | copy-start | bytes 196
  3.2 42.4 %all-to-all-start = ((bf16[4,2,64,1024]{3,2,1,0:T(8,128)(2,1)}), bf16[4,2,64,1024]{3,2,1,0:T(8,128)(2,1)S(1)}, u32[]{:S(2)}, u32[]{:S(2)}) async-start(bf16[4,2,64,1024]{3,2,1,0:T(8,128)(2,1)} %shard_map.55), calls=%async_computation | async-start | bytes 2097152 | tf_op jit(solution)/shard_map/all_to_all | solution.py:525
  8.7 1.6 %copy-start = (bf16[2,1,256,2048]{3,2,1,0:T(8,128)(2,1)S(1)}, bf16[2,1,256,2048]{3,2,1,0:T(8,128)(2,1)}, u32[]{:S(2)}) copy-start(bf16[2,1,256,2048]{3,2,1,0:T(8,128)(2,1)} %param.5) | copy-start | bytes 6291460
  12.8 17.8 %collective-permute-start.1 = (bf16[2,320,512]{2,1,0:T(8,128)(2,1)}, bf16[2,320,512]{2,1,0:T(8,128)(2,1)S(1)}, u32[]{:S(2)}, u32[]{:S(2)}) collective-permute-start(bf16[2,320,512]{2,1,0:T(8,128)(2,1)} %get-tuple-element.23), channel_id=1, source_target_pairs={{0,4},{4,0},{8,20},{12,16},{16,12},{20,8},{24,28},{28,24},{1,5},{5... | collective-permute-start | bytes 1966088 | tf_op jit(solution)/shard_map/ppermute | solution.py:523
  15.9 17.1 %collective-permute-start.2 = (bf16[2,320,512]{2,1,0:T(8,128)(2,1)}, bf16[2,320,512]{2,1,0:T(8,128)(2,1)S(1)}, u32[]{:S(2)}, u32[]{:S(2)}) collective-permute-start(bf16[2,320,512]{2,1,0:T(8,128)(2,1)} %get-tuple-element.24), channel_id=1, source_target_pairs={{0,16},{4,20},{8,0},{12,4},{16,24},{20,28},{24,8},{28,12},{1,17},{... | collective-permute-start | bytes 1966088 | tf_op jit(solution)/shard_map/ppermute | solution.py:523
  15.9 29.7 %collective-permute-start.3 = (bf16[2,320,512]{2,1,0:T(8,128)(2,1)}, bf16[2,320,512]{2,1,0:T(8,128)(2,1)}, u32[]{:S(2)}, u32[]{:S(2)}) collective-permute-start(bf16[2,320,512]{2,1,0:T(8,128)(2,1)} %get-tuple-element.25), channel_id=1, source_target_pairs={{0,20},{4,16},{8,4},{12,0},{16,28},{20,24},{24,12},{28,8},{1,21},{... | collective-permute-start | bytes 1966088 | tf_op jit(solution)/shard_map/ppermute | solution.py:523
  16.5 29.1 %collective-permute-start = (bf16[2,320,512]{2,1,0:T(8,128)(2,1)S(1)}, bf16[2,320,512]{2,1,0:T(8,128)(2,1)}, u32[]{:S(2)}, u32[]{:S(2)}) collective-permute-start(bf16[2,320,512]{2,1,0:T(8,128)(2,1)S(1)} %get-tuple-element.22.own), channel_id=1, source_target_pairs={{8,16},{12,20},{16,8},{20,12},{9,17},{13,21},{17,9},{21,13},{10,18... | collective-permute-start | bytes 1966088 | tf_op jit(solution)/shard_map/ppermute | solution.py:523
  47.3 13.9 %collective-permute-start.4 = (bf16[256,1024]{1,0:T(8,128)(2,1)S(1)}, bf16[256,1024]{1,0:T(8,128)(2,1)S(1)}, u32[]{:S(2)}, u32[]{:S(2)}) collective-permute-start(bf16[256,1024]{1,0:T(8,128)(2,1)S(1)} %get-tuple-element.26.x_column), channel_id=1, source_target_pairs={{0,4},{4,0},{1,5},{5,1},{2,6},{6,2},{3,7},{7,3},{8,12},{12,8},{9,1... | collective-permute-start | bytes 1572872 | tf_op jit(solution)/shard_map/ppermute | solution.py:547
  48.2 12.9 %collective-permute-start.6 = (bf16[1024,256]{1,0:T(8,128)(2,1)S(1)}, bf16[1024,256]{1,0:T(8,128)(2,1)S(1)}, u32[]{:S(2)}, u32[]{:S(2)}) collective-permute-start(bf16[1024,256]{1,0:T(8,128)(2,1)S(1)} %get-tuple-element.27.y_column), channel_id=1, source_target_pairs={{0,16},{4,20},{8,0},{12,4},{16,24},{20,28},{24,8},{28,12},{1,17},{... | collective-permute-start | bytes 1572872 | tf_op jit(solution)/shard_map/ppermute | solution.py:544
  48.3 14.6 %collective-permute-start.5 = (bf16[1024,256]{1,0:T(8,128)(2,1)S(1)}, bf16[1024,256]{1,0:T(8,128)(2,1)S(1)}, u32[]{:S(2)}, u32[]{:S(2)}) collective-permute-start(bf16[1024,256]{1,0:T(8,128)(2,1)S(1)} %get-tuple-element.27.y_column), channel_id=1, source_target_pairs={{8,16},{12,20},{16,8},{20,12},{9,17},{13,21},{17,9},{21,13},{10,18... | collective-permute-start | bytes 1572872 | tf_op jit(solution)/shard_map/ppermute | solution.py:544
  63.6 24.5 %collective-permute-start.9 = (bf16[2,1024,256]{2,1,0:T(8,128)(2,1)S(1)}, bf16[2,1024,256]{2,1,0:T(8,128)(2,1)S(1)}, u32[]{:S(2)}, u32[]{:S(2)}) collective-permute-start(bf16[2,1024,256]{2,1,0:T(8,128)(2,1)S(1)} %get-tuple-element.29.yb), channel_id=1, source_target_pairs={{0,4},{4,0},{1,5},{5,1},{2,6},{6,2},{3,7},{7,3},{8,12},{12,8},{9,1... | collective-permute-start | bytes 3145736 | tf_op jit(solution)/shard_map/ppermute | solution.py:547
  63.9 24.2 %collective-permute-start.8 = (bf16[2,256,1024]{2,1,0:T(8,128)(2,1)S(1)}, bf16[2,256,1024]{2,1,0:T(8,128)(2,1)S(1)}, u32[]{:S(2)}, u32[]{:S(2)}) collective-permute-start(bf16[2,256,1024]{2,1,0:T(8,128)(2,1)S(1)} %get-tuple-element.28.xb), channel_id=1, source_target_pairs={{0,16},{4,20},{8,0},{12,4},{16,24},{20,28},{24,8},{28,12},{1,17},{... | collective-permute-start | bytes 3145736 | tf_op jit(solution)/shard_map/ppermute | solution.py:544
  63.9 26.3 %collective-permute-start.7 = (bf16[2,256,1024]{2,1,0:T(8,128)(2,1)S(1)}, bf16[2,256,1024]{2,1,0:T(8,128)(2,1)S(1)}, u32[]{:S(2)}, u32[]{:S(2)}) collective-permute-start(bf16[2,256,1024]{2,1,0:T(8,128)(2,1)S(1)} %get-tuple-element.28.xb), channel_id=1, source_target_pairs={{8,16},{12,20},{16,8},{20,12},{9,17},{13,21},{17,9},{21,13},{10,18... | collective-permute-start | bytes 3145736 | tf_op jit(solution)/shard_map/ppermute | solution.py:544
  68.6 13.7 %collective-permute-start.10 = (bf16[4,128,512]{2,1,0:T(8,128)(2,1)S(1)}, bf16[4,128,512]{2,1,0:T(8,128)(2,1)S(1)}, u32[]{:S(2)}, u32[]{:S(2)}) collective-permute-start(bf16[4,128,512]{2,1,0:T(8,128)(2,1)S(1)} %bitcast.28), channel_id=1, source_target_pairs={{0,1},{1,0},{2,3},{3,2},{4,5},{5,4},{6,7},{7,6},{8,9},{9,8},{10,11... | collective-permute-start | bytes 1572872 | tf_op jit(solution)/shard_map/ppermute | solution.py:550
  90.8 8.0 %collective-permute-start.11 = (bf16[2,512,512]{2,1,0:T(8,128)(2,1)S(1)}, bf16[2,512,512]{2,1,0:T(8,128)(2,1)S(1)}, u32[]{:S(2)}, u32[]{:S(2)}) collective-permute-start(bf16[2,512,512]{2,1,0:T(8,128)(2,1)S(1)} %get-tuple-element.32.w_high), channel_id=1, source_target_pairs={{0,8},{16,24},{1,9},{17,25},{2,10},{18,26},{3,11},{19,27},{4,12},{... | collective-permute-start | bytes 3145736 | tf_op jit(solution)/shard_map/ppermute | solution.py:610
  108.0 3.6 %collective-permute-start.12 = (bf16[2,512,512]{2,1,0:T(8,128)(2,1)S(1)}, bf16[2,512,512]{2,1,0:T(8,128)(2,1)S(1)}, u32[]{:S(2)}, u32[]{:S(2)}) collective-permute-start(bf16[2,512,512]{2,1,0:T(8,128)(2,1)S(1)} %get-tuple-element.33), channel_id=1, source_target_pairs={{8,0},{24,16},{9,1},{25,17},{10,2},{26,18},{11,3},{27,19},{12,4},{... | collective-permute-start | bytes 3145736 | tf_op jit(solution)/shard_map/ppermute | solution.py:622
  112.4 17.4 %collective-permute-start.14 = (bf16[2,256,512]{2,1,0:T(8,128)(2,1)S(1)}, bf16[2,256,512]{2,1,0:T(8,128)(2,1)S(1)}, u32[]{:S(2)}, u32[]{:S(2)}) collective-permute-start(bf16[2,256,512]{2,1,0:T(8,128)(2,1)S(1)} %get-tuple-element.36), channel_id=1, source_target_pairs={{4,0},{0,4},{20,8},{16,12},{12,16},{8,20},{28,24},{24,28},{5,1},{1... | collective-permute-start | bytes 1572872 | tf_op jit(solution)/shard_map/ppermute | solution.py:635
  122.8 11.8 %collective-permute-start.15 = (bf16[2,256,512]{2,1,0:T(8,128)(2,1)S(1)}, bf16[2,256,512]{2,1,0:T(8,128)(2,1)S(1)}, u32[]{:S(2)}, u32[]{:S(2)}) collective-permute-start(bf16[2,256,512]{2,1,0:T(8,128)(2,1)S(1)} %get-tuple-element.37), channel_id=1, source_target_pairs={{16,0},{20,4},{0,8},{4,12},{24,16},{28,20},{8,24},{12,28},{17,1},{... | collective-permute-start | bytes 1572872 | tf_op jit(solution)/shard_map/ppermute | solution.py:635
  122.8 21.0 %collective-permute-start.16 = (bf16[2,256,512]{2,1,0:T(8,128)(2,1)S(1)}, bf16[2,256,512]{2,1,0:T(8,128)(2,1)S(1)}, u32[]{:S(2)}, u32[]{:S(2)}) collective-permute-start(bf16[2,256,512]{2,1,0:T(8,128)(2,1)S(1)} %get-tuple-element.38), channel_id=1, source_target_pairs={{20,0},{16,4},{4,8},{0,12},{28,16},{24,20},{12,24},{8,28},{21,1},{... | collective-permute-start | bytes 1572872 | tf_op jit(solution)/shard_map/ppermute | solution.py:635
  123.0 22.9 %collective-permute-start.13 = (bf16[2,256,512]{2,1,0:T(8,128)(2,1)S(1)}, bf16[2,256,512]{2,1,0:T(8,128)(2,1)S(1)}, u32[]{:S(2)}, u32[]{:S(2)}) collective-permute-start(bf16[2,256,512]{2,1,0:T(8,128)(2,1)S(1)} %get-tuple-element.35.own), channel_id=1, source_target_pairs={{16,8},{20,12},{8,16},{12,20},{17,9},{21,13},{9,17},{13,21},{18,10... | collective-permute-start | bytes 1572872 | tf_op jit(solution)/shard_map/ppermute | solution.py:635

commit v19 on v17

--- a/solution.py
+++ b/solution.py
@@ -285,7 +285,8 @@
     wait_all(copies)
 
 
-def both_kernel(info, x_column, x_aside, y_column, y0, y1, rhs, x_both, y_both, sems):
+def both_kernel(info, x_column, x_aside, y_column, y0, y1, rows_next, rows_far, rhs, x_both, y_both,
+                sems):
     copies = [
         pltpu.make_async_copy(x_column, x_both.at[0], sems.at[0]),
         pltpu.make_async_copy(x_aside, x_both.at[1], sems.at[1]),
@@ -466,7 +467,7 @@
     rows_here = field.shape[1]
     height = x_factor.shape[2]
     params = pltpu.CompilerParams(vmem_limit_bytes=vmem_bytes)
-    rounds = [(a, b) for a in range(groups) for b in range(px_count)]
+    rounds = [(0, 0), (1, 0), (1, 1), (0, 1)]
 
     def pairs(a, b):
         return [
@@ -570,11 +571,11 @@
         out_shape=[
             jax.ShapeDtypeStruct((2,) + one.shape, bf16) for one in (column_shape, turned_shape)
         ],
-        in_specs=[in_smem] + [anywhere] * 6,
+        in_specs=[in_smem] + [anywhere] * 8,
         out_specs=[in_vmem] * 2,
         scratch_shapes=[pltpu.SemaphoreType.DMA((4,))],
         compiler_params=params,
-    )(info, x_column, x_aside, y_turned, *y_near, rhs)
+    )(info, x_column, x_aside, y_turned, *y_near, rows_next, rows_far, rhs)
     y_far = aside(y_both)
     x_across = [across(x_both, a) for a in range(2)]
     weights = pl.pallas_call(
@@ -584,9 +585,6 @@
         out_specs=in_vmem,
         scratch_shapes=[pltpu.SemaphoreType.DMA((4, len(rounds)))],
         compiler_params=params,
-        cost_estimate=pl.CostEstimate(
-            flops=3 * 10**10, bytes_accessed=2**21, transcendentals=0
-        ),
     )(info, rows_held, rows_next, rows_far, over_z(rows_next, 2))
     layers = (info, x_both, *x_across, y_both, y_far, weights)
     layer_specs = [in_smem] + [anywhere] * 3 + [in_vmem] * 3

time: 149 us -> 148 us (level)
  waiting for transfers between devices: 77.9 us -> 75.3 us
    ppermute x2, waiting for transfers between devices: 11.9 us -> 4.49 us  [aside(): return lax.ppermute(block, 'px', [(y, (y + 1) % 2) for y in range(2)])]
    ppermute x3, waiting for transfers between devices: 18.3 us -> 22.1 us  [over_z(): return lax.ppermute(block, 'py', [(z, z ^ bit) for z in range(py_count)])]
    ppermute x4, waiting for transfers between devices: 0.01 us -> 1.61 us  [across(): return lax.ppermute(block, ('sec', 'px'), pairs(a, 0))]
  transfers between devices with their start and end apart: 20 -> 20, of which waited for: 12 -> 12; matrix products, arithmetic and copies ran while one was open for 1% -> 1% of each run, Pallas kernels for 5% -> 4%
where the time goes in v19:
time: 148 us; the launch traced here: 147 us
  waiting for transfers between devices  75.3 us (51%)
  starting transfers between devices  42.1 us (28%)
  Pallas kernels  22.4 us (15%)
  local copies, waits for them, and re-layouts  4.24 us (3%)
  between operations  3.08 us (2%)
    ppermute x3, waiting for transfers between devices, over_z(): return lax.ppermute(block, 'py', [(z, z ^ bit) for z in range(py_count)])  22.1 us
    ppermute x4, waiting for transfers between devices, on_device(): lax.ppermute(piece, ('sec', 'px'), back_pairs(a, b))  19.1 us
    ppermute x4, waiting for transfers between devices, on_device(): lax.ppermute(piece, ('sec', 'px'), pairs(a, b))  18.5 us
    ppermute x4, starting transfers between devices, on_device(): lax.ppermute(piece, ('sec', 'px'), back_pairs(a, b))  12.5 us
    pallas_call x1, Pallas kernels, on_device(): pl.pallas_call(last_kernel, out_shape=[double_shape, full_shape], in_spec...  9.12 us
    ppermute x4, starting transfers between devices, across(): return lax.ppermute(block, ('sec', 'px'), pairs(a, 0))  7.35 us
    ppermute x1, waiting for transfers between devices, on_device(): incoming = lax.ppermute(w_high, 'sec', up)  7.32 us
    ppermute x4, starting transfers between devices, on_device(): lax.ppermute(piece, ('sec', 'px'), pairs(a, b))  7.17 us
  transfers between devices with their start and end apart: 20, of which 12 were waited for; matrix products, arithmetic and copies ran while one was open for 1% of the time, Pallas kernels for 4%

profile of v19, /device:TPU:1, one launch (start us, length us, event | category | flops | bytes accessed | tf_op | source)
XLA Modules:
  0.0 147.1 jit_solution(15323203572411083395)
XLA Ops:
  1.9 1.3 shard_map.55
  3.2 5.4 %all-to-all-start = ((bf16[4,2,64,1024]{3,2,1,0:T(8,128)(2,1)}), bf16[4,2,64,1024]{3,2,1,0:T(8,128)(2,1)S(1)}, u32[]{:S(2)}, u32[]{:S(2)}) async-start(bf16[4,2,64,1024]{3,2,1,0:T(8,128)(2,1)} %shard_map.55), calls=%async_computation | async-start | bytes 2097152 | tf_op jit(solution)/shard_map/all_to_all | solution.py:528
  8.7 1.6 %copy-done = bf16[2,1,256,2048]{3,2,1,0:T(8,128)(2,1)S(1)} copy-done((bf16[2,1,256,2048]{3,2,1,0:T(8,128)(2,1)S(1)}, bf16[2,1,256,2048]{3,2,1,0:T(8,128)(2,1)}, u32[]{:S(2)}) %copy-start) | copy-done | bytes 2097176
  10.3 2.3 %shard_map.56 = (bf16[2,288,512]{2,1,0:T(8,128)(2,1)S(1)}, bf16[2,288,512]{2,1,0:T(8,128)(2,1)}, bf16[2,288,512]{2,1,0:T(8,128)(2,1)}, bf16[2,288,512]{2,1,0:T(8,128)(2,1)}) custom-call(s32[6]{0:T(128)S(1)} %stack.83.place, bf16[2,256,2048]{2,1,0:T(8,128)(2,1)S(1)} %bitcast.29, bf16[8,32,512]{2,1,0:T(8,128)(2,1)S(1)} %bitcast.30), custom_call_target="tpu_custom_call" | custom-call | tf_op jit(solution)/shard_map/pallas_call | solution.py:517
  13.6 2.6 %collective-permute-start.2 = (bf16[2,288,512]{2,1,0:T(8,128)(2,1)}, bf16[2,288,512]{2,1,0:T(8,128)(2,1)S(1)}, u32[]{:S(2)}, u32[]{:S(2)}) collective-permute-start(bf16[2,288,512]{2,1,0:T(8,128)(2,1)} %get-tuple-element.24), channel_id=1, source_target_pairs={{0,20},{4,16},{8,4},{12,0},{16,28},{20,24},{24,12},{28,8},{1,21},{... | collective-permute-start | bytes 1769480 | tf_op jit(solution)/shard_map/ppermute | solution.py:526
  16.2 3.6 %collective-permute-start = (bf16[2,288,512]{2,1,0:T(8,128)(2,1)S(1)}, bf16[2,288,512]{2,1,0:T(8,128)(2,1)}, u32[]{:S(2)}, u32[]{:S(2)}) collective-permute-start(bf16[2,288,512]{2,1,0:T(8,128)(2,1)S(1)} %get-tuple-element.22.own), channel_id=1, source_target_pairs={{8,16},{12,20},{16,8},{20,12},{9,17},{13,21},{17,9},{21,13},{10,18... | collective-permute-start | bytes 1769480 | tf_op jit(solution)/shard_map/ppermute | solution.py:526
  24.0 17.7 %collective-permute-done.2.p2 = bf16[2,288,512]{2,1,0:T(8,128)(2,1)S(1)} collective-permute-done((bf16[2,288,512]{2,1,0:T(8,128)(2,1)}, bf16[2,288,512]{2,1,0:T(8,128)(2,1)S(1)}, u32[]{:S(2)}, u32[]{:S(2)}) %collective-permute-start.2) | collective-permute-done | bytes 589856 | tf_op jit(solution)/shard_map/ppermute | solution.py:526
  41.7 1.4 shard_map.57
  44.0 2.1 %collective-permute-start.6 = (bf16[1024,256]{1,0:T(8,128)(2,1)S(1)}, bf16[1024,256]{1,0:T(8,128)(2,1)S(1)}, u32[]{:S(2)}, u32[]{:S(2)}) collective-permute-start(bf16[1024,256]{1,0:T(8,128)(2,1)S(1)} %get-tuple-element.27.y_column), channel_id=1, source_target_pairs={{0,16},{4,20},{8,0},{12,4},{16,24},{20,28},{24,8},{28,12},{1,17},{... | collective-permute-start | bytes 1572872 | tf_op jit(solution)/shard_map/ppermute | solution.py:547
  46.1 2.6 %collective-permute-start.5 = (bf16[1024,256]{1,0:T(8,128)(2,1)S(1)}, bf16[1024,256]{1,0:T(8,128)(2,1)S(1)}, u32[]{:S(2)}, u32[]{:S(2)}) collective-permute-start(bf16[1024,256]{1,0:T(8,128)(2,1)S(1)} %get-tuple-element.27.y_column), channel_id=1, source_target_pairs={{8,16},{12,20},{16,8},{20,12},{9,17},{13,21},{17,9},{21,13},{10,18... | collective-permute-start | bytes 1572872 | tf_op jit(solution)/shard_map/ppermute | solution.py:547
  48.8 2.7 %collective-permute-start.8 = (bf16[4,64,512]{2,1,0:T(8,128)(2,1)S(1)}, bf16[4,64,512]{2,1,0:T(8,128)(2,1)S(1)}, u32[]{:S(2)}, u32[]{:S(2)}) collective-permute-start(bf16[4,64,512]{2,1,0:T(8,128)(2,1)S(1)} %bitcast.31), channel_id=1, source_target_pairs={{0,2},{1,3},{2,0},{3,1},{4,6},{5,7},{6,4},{7,5},{8,10},{9,11},{10,... | collective-permute-start | bytes 786440 | tf_op jit(solution)/shard_map/ppermute | solution.py:553
  51.5 1.2 collective-permute-start.7
  52.6 1.6 %shard_map.58.rhs = bf16[2,2,512,512]{3,2,1,0:T(8,128)(2,1)S(1)} custom-call(s32[21]{0:T(128)S(1)} %stack.98.info, bf16[2,288,512]{2,1,0:T(8,128)(2,1)S(1)} %get-tuple-element.22.own, bf16[2,288,512]{2,1,0:T(8,128)(2,1)} %collective-permute-done.p0, bf16[2,288,512]{2,1,0:T(8,128)(2,1)S(1)} %collective-permute-done.1.p1, ...), custom_call_target="tpu_custom_call" | custom-call | tf_op jit(solution)/shard_map/pallas_call | solution.py:561
  54.3 8.8 %collective-permute-done.8.rows_far.c2 = bf16[4,64,512]{2,1,0:T(8,128)(2,1)S(1)} collective-permute-done((bf16[4,64,512]{2,1,0:T(8,128)(2,1)S(1)}, bf16[4,64,512]{2,1,0:T(8,128)(2,1)S(1)}, u32[]{:S(2)}, u32[]{:S(2)}) %collective-permute-start.8) | collective-permute-done | bytes 262176 | tf_op jit(solution)/shard_map/ppermute | solution.py:553
  66.2 1.9 %collective-permute-start.9 = (bf16[2,256,1024]{2,1,0:T(8,128)(2,1)S(1)}, bf16[2,256,1024]{2,1,0:T(8,128)(2,1)S(1)}, u32[]{:S(2)}, u32[]{:S(2)}) collective-permute-start(bf16[2,256,1024]{2,1,0:T(8,128)(2,1)S(1)} %get-tuple-element.29.xb), channel_id=1, source_target_pairs={{8,16},{12,20},{16,8},{20,12},{9,17},{13,21},{17,9},{21,13},{10,18... | collective-permute-start | bytes 3145736 | tf_op jit(solution)/shard_map/ppermute | solution.py:547
  68.2 1.2 collective-permute-start.12
  69.4 12.7 %collective-permute-done.12.c3 = bf16[4,64,512]{2,1,0:T(8,128)(2,1)S(1)} collective-permute-done((bf16[4,64,512]{2,1,0:T(8,128)(2,1)S(1)}, bf16[4,64,512]{2,1,0:T(8,128)(2,1)S(1)}, u32[]{:S(2)}, u32[]{:S(2)}) %collective-permute-start.12) | collective-permute-done | bytes 262176 | tf_op jit(solution)/shard_map/ppermute | solution.py:553
  82.0 2.3 %shard_map.60.weights = bf16[2,512,512]{2,1,0:T(8,128)(2,1)S(1)} custom-call(s32[21]{0:T(128)S(1)} %stack.98.info, bf16[4,64,512]{2,1,0:T(8,128)(2,1)S(1)} %bitcast.33, bf16[4,64,512]{2,1,0:T(8,128)(2,1)S(1)} %collective-permute-done.7.rows_next.c1, bf16[4,64,512]{2,1,0:T(8,128)(2,1)S(1)} %collective-permute-done.8.rows_far.c2, ...), custom_call_target="tpu_custom_call" | custom-call | tf_op jit(solution)/shard_map/pallas_call | solution.py:581
  84.4 4.5 %collective-permute-done.11.yf = bf16[2,1024,256]{2,1,0:T(8,128)(2,1)S(1)} collective-permute-done((bf16[2,1024,256]{2,1,0:T(8,128)(2,1)S(1)}, bf16[2,1024,256]{2,1,0:T(8,128)(2,1)S(1)}, u32[]{:S(2)}, u32[]{:S(2)}) %collective-permute-start.11) | collective-permute-done | bytes 1048608 | tf_op jit(solution)/shard_map/ppermute | solution.py:550
  88.9 1.6 %collective-permute-done.9.x0 = bf16[2,256,1024]{2,1,0:T(8,128)(2,1)S(1)} collective-permute-done((bf16[2,256,1024]{2,1,0:T(8,128)(2,1)S(1)}, bf16[2,256,1024]{2,1,0:T(8,128)(2,1)S(1)}, u32[]{:S(2)}, u32[]{:S(2)}) %collective-permute-start.9) | collective-permute-done | bytes 1048608 | tf_op jit(solution)/shard_map/ppermute | solution.py:547
  91.0 1.3 collective-permute-start.13
  92.3 7.3 %collective-permute-done.13.arrived = bf16[2,512,512]{2,1,0:T(8,128)(2,1)S(1)} collective-permute-done((bf16[2,512,512]{2,1,0:T(8,128)(2,1)S(1)}, bf16[2,512,512]{2,1,0:T(8,128)(2,1)S(1)}, u32[]{:S(2)}, u32[]{:S(2)}) %collective-permute-start.13) | collective-permute-done | bytes 1048608 | tf_op jit(solution)/shard_map/ppermute | solution.py:614
  99.7 9.1 %shard_map.62 = (bf16[2,2,512,512]{3,2,1,0:T(8,128)(2,1)S(1)}, bf16[2,512,512]{2,1,0:T(8,128)(2,1)S(1)}) custom-call(s32[21]{0:T(128)S(1)} %stack.98.info, bf16[2,256,1024]{2,1,0:T(8,128)(2,1)S(1)} %get-tuple-element.29.xb, bf16[2,256,1024]{2,1,0:T(8,128)(2,1)S(1)} %collective-permute-done.9.x0, bf16[2,256,1024]{2,1,0:T(8,128)(2,1)S(1)} %collective-permute-done.10.x1, ...), custom_call_target="tpu_custom_call" | custom-call | flops 6442450944 | bytes 8388608 | tf_op jit(solution)/shard_map/pallas_call | solution.py:615
  108.8 1.4 collective-permute-start.14
  110.2 2.2 %collective-permute-done.14.arrived = bf16[2,512,512]{2,1,0:T(8,128)(2,1)S(1)} collective-permute-done((bf16[2,512,512]{2,1,0:T(8,128)(2,1)S(1)}, bf16[2,512,512]{2,1,0:T(8,128)(2,1)S(1)}, u32[]{:S(2)}, u32[]{:S(2)}) %collective-permute-start.14) | collective-permute-done | bytes 1048608 | tf_op jit(solution)/shard_map/ppermute | solution.py:626
  113.2 1.9 %collective-permute-start.16 = (bf16[2,256,512]{2,1,0:T(8,128)(2,1)S(1)}, bf16[2,256,512]{2,1,0:T(8,128)(2,1)S(1)}, u32[]{:S(2)}, u32[]{:S(2)}) collective-permute-start(bf16[2,256,512]{2,1,0:T(8,128)(2,1)S(1)} %get-tuple-element.36), channel_id=1, source_target_pairs={{16,0},{20,4},{0,8},{4,12},{24,16},{28,20},{8,24},{12,28},{17,1},{... | collective-permute-start | bytes 1572872 | tf_op jit(solution)/shard_map/ppermute | solution.py:639
  115.1 6.1 %collective-permute-start.17 = (bf16[2,256,512]{2,1,0:T(8,128)(2,1)S(1)}, bf16[2,256,512]{2,1,0:T(8,128)(2,1)S(1)}, u32[]{:S(2)}, u32[]{:S(2)}) collective-permute-start(bf16[2,256,512]{2,1,0:T(8,128)(2,1)S(1)} %get-tuple-element.37), channel_id=1, source_target_pairs={{20,0},{16,4},{4,8},{0,12},{28,16},{24,20},{12,24},{8,28},{21,1},{... | collective-permute-start | bytes 1572872 | tf_op jit(solution)/shard_map/ppermute | solution.py:639
  121.8 3.8 %collective-permute-start.15 = (bf16[2,256,512]{2,1,0:T(8,128)(2,1)S(1)}, bf16[2,256,512]{2,1,0:T(8,128)(2,1)S(1)}, u32[]{:S(2)}, u32[]{:S(2)}) collective-permute-start(bf16[2,256,512]{2,1,0:T(8,128)(2,1)S(1)} %get-tuple-element.35.own), channel_id=1, source_target_pairs={{16,8},{20,12},{8,16},{12,20},{17,9},{21,13},{9,17},{13,21},{18,10... | collective-permute-start | bytes 1572872 | tf_op jit(solution)/shard_map/ppermute | solution.py:639
  125.7 1.7 %collective-permute-done.17.rest_2_ = bf16[2,256,512]{2,1,0:T(8,128)(2,1)S(1)} collective-permute-done((bf16[2,256,512]{2,1,0:T(8,128)(2,1)S(1)}, bf16[2,256,512]{2,1,0:T(8,128)(2,1)S(1)}, u32[]{:S(2)}, u32[]{:S(2)}) %collective-permute-start.17) | collective-permute-done | bytes 524320 | tf_op jit(solution)/shard_map/ppermute | solution.py:639
  127.4 12.4 %collective-permute-done.18.rest_3_ = bf16[2,256,512]{2,1,0:T(8,128)(2,1)S(1)} collective-permute-done((bf16[2,256,512]{2,1,0:T(8,128)(2,1)S(1)}, bf16[2,256,512]{2,1,0:T(8,128)(2,1)S(1)}, u32[]{:S(2)}, u32[]{:S(2)}) %collective-permute-start.18) | collective-permute-done | bytes 524320 | tf_op jit(solution)/shard_map/ppermute | solution.py:639
  139.8 5.0 %collective-permute-done.15.rest_0_ = bf16[2,256,512]{2,1,0:T(8,128)(2,1)S(1)} collective-permute-done((bf16[2,256,512]{2,1,0:T(8,128)(2,1)S(1)}, bf16[2,256,512]{2,1,0:T(8,128)(2,1)S(1)}, u32[]{:S(2)}, u32[]{:S(2)}) %collective-permute-start.15) | collective-permute-done | bytes 524320 | tf_op jit(solution)/shard_map/ppermute | solution.py:639
  144.8 2.2 %shard_map.64 = bf16[2,256,2048]{2,1,0:T(8,128)(2,1)} custom-call(s32[6]{0:T(128)S(1)} %stack.83.place, bf16[2,256,512]{2,1,0:T(8,128)(2,1)S(1)} %get-tuple-element.35.own, bf16[2,256,512]{2,1,0:T(8,128)(2,1)S(1)} %collective-permute-done.15.rest_0_, bf16[2,256,512]{2,1,0:T(8,128)(2,1)S(1)} %collective-permute-done.16.rest_1_, ...), custom_call_target="tpu_custom_call" | custom-call | tf_op jit(solution)/shard_map/pallas_call | solution.py:641
  (31 shorter events, 10.4 us)
Async XLA Ops:
  0.0 8.7 %copy-start.1 = (bf16[1,256,512]{2,1,0:T(8,128)(2,1)S(1)}, bf16[1,256,512]{2,1,0:T(8,128)(2,1)}, u32[]{:S(2)}) copy-start(bf16[1,256,512]{2,1,0:T(8,128)(2,1)} %param.7) | copy-start | bytes 786436
  0.0 0.9 copy-start.2
  1.0 0.9 copy-start.3
  3.2 16.7 %copy-start.4 = (s32[16]{0:T(128)S(1)}, s32[16]{0:T(128)}, u32[]{:S(2)}) copy-start(s32[16]{0:T(128)} %param.6) | copy-start | bytes 196
  3.2 38.6 %all-to-all-start = ((bf16[4,2,64,1024]{3,2,1,0:T(8,128)(2,1)}), bf16[4,2,64,1024]{3,2,1,0:T(8,128)(2,1)S(1)}, u32[]{:S(2)}, u32[]{:S(2)}) async-start(bf16[4,2,64,1024]{3,2,1,0:T(8,128)(2,1)} %shard_map.55), calls=%async_computation | async-start | bytes 2097152 | tf_op jit(solution)/shard_map/all_to_all | solution.py:528
  8.7 1.6 %copy-start = (bf16[2,1,256,2048]{3,2,1,0:T(8,128)(2,1)S(1)}, bf16[2,1,256,2048]{3,2,1,0:T(8,128)(2,1)}, u32[]{:S(2)}) copy-start(bf16[2,1,256,2048]{3,2,1,0:T(8,128)(2,1)} %param.5) | copy-start | bytes 6291460
  12.6 11.4 %collective-permute-start.1 = (bf16[2,288,512]{2,1,0:T(8,128)(2,1)}, bf16[2,288,512]{2,1,0:T(8,128)(2,1)S(1)}, u32[]{:S(2)}, u32[]{:S(2)}) collective-permute-start(bf16[2,288,512]{2,1,0:T(8,128)(2,1)} %get-tuple-element.23), channel_id=1, source_target_pairs={{0,16},{4,20},{8,0},{12,4},{16,24},{20,28},{24,8},{28,12},{1,17},{... | collective-permute-start | bytes 1769480 | tf_op jit(solution)/shard_map/ppermute | solution.py:526
  13.6 28.2 %collective-permute-start.2 = (bf16[2,288,512]{2,1,0:T(8,128)(2,1)}, bf16[2,288,512]{2,1,0:T(8,128)(2,1)S(1)}, u32[]{:S(2)}, u32[]{:S(2)}) collective-permute-start(bf16[2,288,512]{2,1,0:T(8,128)(2,1)} %get-tuple-element.24), channel_id=1, source_target_pairs={{0,20},{4,16},{8,4},{12,0},{16,28},{20,24},{24,12},{28,8},{1,21},{... | collective-permute-start | bytes 1769480 | tf_op jit(solution)/shard_map/ppermute | solution.py:526
  16.2 25.6 %collective-permute-start.3 = (bf16[2,288,512]{2,1,0:T(8,128)(2,1)}, bf16[2,288,512]{2,1,0:T(8,128)(2,1)S(1)}, u32[]{:S(2)}, u32[]{:S(2)}) collective-permute-start(bf16[2,288,512]{2,1,0:T(8,128)(2,1)} %get-tuple-element.25), channel_id=1, source_target_pairs={{0,4},{4,0},{8,20},{12,16},{16,12},{20,8},{24,28},{28,24},{1,5},{5... | collective-permute-start | bytes 1769480 | tf_op jit(solution)/shard_map/ppermute | solution.py:526
  16.2 25.6 %collective-permute-start = (bf16[2,288,512]{2,1,0:T(8,128)(2,1)S(1)}, bf16[2,288,512]{2,1,0:T(8,128)(2,1)}, u32[]{:S(2)}, u32[]{:S(2)}) collective-permute-start(bf16[2,288,512]{2,1,0:T(8,128)(2,1)S(1)} %get-tuple-element.22.own), channel_id=1, source_target_pairs={{8,16},{12,20},{16,8},{20,12},{9,17},{13,21},{17,9},{21,13},{10,18... | collective-permute-start | bytes 1769480 | tf_op jit(solution)/shard_map/ppermute | solution.py:526
  43.2 20.5 %collective-permute-start.4 = (bf16[256,1024]{1,0:T(8,128)(2,1)S(1)}, bf16[256,1024]{1,0:T(8,128)(2,1)S(1)}, u32[]{:S(2)}, u32[]{:S(2)}) collective-permute-start(bf16[256,1024]{1,0:T(8,128)(2,1)S(1)} %get-tuple-element.26.x_column), channel_id=1, source_target_pairs={{0,4},{4,0},{1,5},{5,1},{2,6},{6,2},{3,7},{7,3},{8,12},{12,8},{9,1... | collective-permute-start | bytes 1572872 | tf_op jit(solution)/shard_map/ppermute | solution.py:550
  44.0 19.7 %collective-permute-start.6 = (bf16[1024,256]{1,0:T(8,128)(2,1)S(1)}, bf16[1024,256]{1,0:T(8,128)(2,1)S(1)}, u32[]{:S(2)}, u32[]{:S(2)}) collective-permute-start(bf16[1024,256]{1,0:T(8,128)(2,1)S(1)} %get-tuple-element.27.y_column), channel_id=1, source_target_pairs={{0,16},{4,20},{8,0},{12,4},{16,24},{20,28},{24,8},{28,12},{1,17},{... | collective-permute-start | bytes 1572872 | tf_op jit(solution)/shard_map/ppermute | solution.py:547
  46.1 17.6 %collective-permute-start.5 = (bf16[1024,256]{1,0:T(8,128)(2,1)S(1)}, bf16[1024,256]{1,0:T(8,128)(2,1)S(1)}, u32[]{:S(2)}, u32[]{:S(2)}) collective-permute-start(bf16[1024,256]{1,0:T(8,128)(2,1)S(1)} %get-tuple-element.27.y_column), channel_id=1, source_target_pairs={{8,16},{12,20},{16,8},{20,12},{9,17},{13,21},{17,9},{21,13},{10,18... | collective-permute-start | bytes 1572872 | tf_op jit(solution)/shard_map/ppermute | solution.py:547
  48.8 14.4 %collective-permute-start.8 = (bf16[4,64,512]{2,1,0:T(8,128)(2,1)S(1)}, bf16[4,64,512]{2,1,0:T(8,128)(2,1)S(1)}, u32[]{:S(2)}, u32[]{:S(2)}) collective-permute-start(bf16[4,64,512]{2,1,0:T(8,128)(2,1)S(1)} %bitcast.31), channel_id=1, source_target_pairs={{0,2},{1,3},{2,0},{3,1},{4,6},{5,7},{6,4},{7,5},{8,10},{9,11},{10,... | collective-permute-start | bytes 786440 | tf_op jit(solution)/shard_map/ppermute | solution.py:553
  51.5 12.2 %collective-permute-start.7 = (bf16[4,64,512]{2,1,0:T(8,128)(2,1)S(1)}, bf16[4,64,512]{2,1,0:T(8,128)(2,1)S(1)}, u32[]{:S(2)}, u32[]{:S(2)}) collective-permute-start(bf16[4,64,512]{2,1,0:T(8,128)(2,1)S(1)} %bitcast.32), channel_id=1, source_target_pairs={{0,1},{1,0},{2,3},{3,2},{4,5},{5,4},{6,7},{7,6},{8,9},{9,8},{10,11... | collective-permute-start | bytes 786440 | tf_op jit(solution)/shard_map/ppermute | solution.py:553
  64.4 24.4 %collective-permute-start.11 = (bf16[2,1024,256]{2,1,0:T(8,128)(2,1)S(1)}, bf16[2,1024,256]{2,1,0:T(8,128)(2,1)S(1)}, u32[]{:S(2)}, u32[]{:S(2)}) collective-permute-start(bf16[2,1024,256]{2,1,0:T(8,128)(2,1)S(1)} %get-tuple-element.30.yb), channel_id=1, source_target_pairs={{0,4},{4,0},{1,5},{5,1},{2,6},{6,2},{3,7},{7,3},{8,12},{12,8},{9,1... | collective-permute-start | bytes 3145736 | tf_op jit(solution)/shard_map/ppermute | solution.py:550
  65.6 23.3 %collective-permute-start.10 = (bf16[2,256,1024]{2,1,0:T(8,128)(2,1)S(1)}, bf16[2,256,1024]{2,1,0:T(8,128)(2,1)S(1)}, u32[]{:S(2)}, u32[]{:S(2)}) collective-permute-start(bf16[2,256,1024]{2,1,0:T(8,128)(2,1)S(1)} %get-tuple-element.29.xb), channel_id=1, source_target_pairs={{0,16},{4,20},{8,0},{12,4},{16,24},{20,28},{24,8},{28,12},{1,17},{... | collective-permute-start | bytes 3145736 | tf_op jit(solution)/shard_map/ppermute | solution.py:547
  66.2 24.2 %collective-permute-start.9 = (bf16[2,256,1024]{2,1,0:T(8,128)(2,1)S(1)}, bf16[2,256,1024]{2,1,0:T(8,128)(2,1)S(1)}, u32[]{:S(2)}, u32[]{:S(2)}) collective-permute-start(bf16[2,256,1024]{2,1,0:T(8,128)(2,1)S(1)} %get-tuple-element.29.xb), channel_id=1, source_target_pairs={{8,16},{12,20},{16,8},{20,12},{9,17},{13,21},{17,9},{21,13},{10,18... | collective-permute-start | bytes 3145736 | tf_op jit(solution)/shard_map/ppermute | solution.py:547
  68.2 13.9 %collective-permute-start.12 = (bf16[4,64,512]{2,1,0:T(8,128)(2,1)S(1)}, bf16[4,64,512]{2,1,0:T(8,128)(2,1)S(1)}, u32[]{:S(2)}, u32[]{:S(2)}) collective-permute-start(bf16[4,64,512]{2,1,0:T(8,128)(2,1)S(1)} %collective-permute-done.7.rows_next.c1), channel_id=1, source_target_pairs={{0,2},{1,3},{2,0},{3,1},{4,6},{5,7},{6,4},{7,5},{8,10},{9,11},{10,... | collective-permute-start | bytes 786440 | tf_op jit(solution)/shard_map/ppermute | solution.py:553
  91.0 8.6 %collective-permute-start.13 = (bf16[2,512,512]{2,1,0:T(8,128)(2,1)S(1)}, bf16[2,512,512]{2,1,0:T(8,128)(2,1)S(1)}, u32[]{:S(2)}, u32[]{:S(2)}) collective-permute-start(bf16[2,512,512]{2,1,0:T(8,128)(2,1)S(1)} %get-tuple-element.32.w_high), channel_id=1, source_target_pairs={{0,8},{16,24},{1,9},{17,25},{2,10},{18,26},{3,11},{19,27},{4,12},{... | collective-permute-start | bytes 3145736 | tf_op jit(solution)/shard_map/ppermute | solution.py:614
  108.8 3.6 %collective-permute-start.14 = (bf16[2,512,512]{2,1,0:T(8,128)(2,1)S(1)}, bf16[2,512,512]{2,1,0:T(8,128)(2,1)S(1)}, u32[]{:S(2)}, u32[]{:S(2)}) collective-permute-start(bf16[2,512,512]{2,1,0:T(8,128)(2,1)S(1)} %get-tuple-element.33), channel_id=1, source_target_pairs={{8,0},{24,16},{9,1},{25,17},{10,2},{26,18},{11,3},{27,19},{12,4},{... | collective-permute-start | bytes 3145736 | tf_op jit(solution)/shard_map/ppermute | solution.py:626
  113.2 12.5 %collective-permute-start.16 = (bf16[2,256,512]{2,1,0:T(8,128)(2,1)S(1)}, bf16[2,256,512]{2,1,0:T(8,128)(2,1)S(1)}, u32[]{:S(2)}, u32[]{:S(2)}) collective-permute-start(bf16[2,256,512]{2,1,0:T(8,128)(2,1)S(1)} %get-tuple-element.36), channel_id=1, source_target_pairs={{16,0},{20,4},{0,8},{4,12},{24,16},{28,20},{8,24},{12,28},{17,1},{... | collective-permute-start | bytes 1572872 | tf_op jit(solution)/shard_map/ppermute | solution.py:639
  115.1 12.3 %collective-permute-start.17 = (bf16[2,256,512]{2,1,0:T(8,128)(2,1)S(1)}, bf16[2,256,512]{2,1,0:T(8,128)(2,1)S(1)}, u32[]{:S(2)}, u32[]{:S(2)}) collective-permute-start(bf16[2,256,512]{2,1,0:T(8,128)(2,1)S(1)} %get-tuple-element.37), channel_id=1, source_target_pairs={{20,0},{16,4},{4,8},{0,12},{28,16},{24,20},{12,24},{8,28},{21,1},{... | collective-permute-start | bytes 1572872 | tf_op jit(solution)/shard_map/ppermute | solution.py:639
  121.2 18.6 %collective-permute-start.18 = (bf16[2,256,512]{2,1,0:T(8,128)(2,1)S(1)}, bf16[2,256,512]{2,1,0:T(8,128)(2,1)S(1)}, u32[]{:S(2)}, u32[]{:S(2)}) collective-permute-start(bf16[2,256,512]{2,1,0:T(8,128)(2,1)S(1)} %get-tuple-element.38), channel_id=1, source_target_pairs={{4,0},{0,4},{20,8},{16,12},{12,16},{8,20},{28,24},{24,28},{5,1},{1... | collective-permute-start | bytes 1572872 | tf_op jit(solution)/shard_map/ppermute | solution.py:639
  121.8 23.0 %collective-permute-start.15 = (bf16[2,256,512]{2,1,0:T(8,128)(2,1)S(1)}, bf16[2,256,512]{2,1,0:T(8,128)(2,1)S(1)}, u32[]{:S(2)}, u32[]{:S(2)}) collective-permute-start(bf16[2,256,512]{2,1,0:T(8,128)(2,1)S(1)} %get-tuple-element.35.own), channel_id=1, source_target_pairs={{16,8},{20,12},{8,16},{12,20},{17,9},{21,13},{9,17},{13,21},{18,10... | collective-permute-start | bytes 1572872 | tf_op jit(solution)/shard_map/ppermute | solution.py:639

commit v20 on v17

--- a/solution.py
+++ b/solution.py
@@ -181,23 +181,6 @@
         self.received.wait()
 
 
-def block_kernel(x_factor, y_factor, blocks, sems):
-    order = x_factor.shape[2]
-    copies = []
-    for target in range(blocks.shape[0]):
-        for which, factor in enumerate((x_factor, y_factor)):
-            for plane in range(2):
-                copies.append(
-                    pltpu.make_async_copy(
-                        factor.at[plane],
-                        blocks.at[target, which, :, pl.ds(plane * order, order)],
-                        sems.at[target, which, plane],
-                    )
-                )
-    start_all(copies)
-    wait_all(copies)
-
-
 def pack_kernel(place, field, coupling, *rest):
     pieces, sems = rest[:-1], rest[-1]
     rows_here = field.shape[1]
@@ -237,7 +220,7 @@
 
 
 def column_kernel(info, blocks, own, p0, p1, p2, p3, x_column, y_turned, rows_held, sems):
-    count, factors, height, width = blocks.shape
+    count, planes, height, order = blocks.shape
     last = pl.ds(own.shape[1] - rows_held.shape[2], rows_held.shape[2])
     parts = [piece.at[:, last, :] for piece in (p0, p1, p2, p3)]
     copies = [Either(info[info_self], own.at[:, last, :], parts[0], rows_held.at[0], sems.at[0])]
@@ -245,9 +228,12 @@
         copies.append(pltpu.make_async_copy(parts[index], rows_held.at[index], sems.at[index]))
     start_all(copies)
     for index in range(count):
-        x_column[index * height : (index + 1) * height] = blocks[index, 0]
-    column = blocks[:, 1].reshape(count * height, width)
-    y_turned[...] = column.astype(f32).T.astype(bf16)
+        rows = slice(index * height, (index + 1) * height)
+        for plane in range(2):
+            x_column[rows, plane * order : (plane + 1) * order] = blocks[index, plane]
+    for plane in range(2):
+        column = blocks[:, 2 + plane].reshape(count * height, order)
+        y_turned[plane * order : (plane + 1) * order] = column.astype(f32).T.astype(bf16)
     wait_all(copies)
 
 
@@ -267,22 +253,38 @@
     wait_all(copies)
 
 
-def weight_kernel(info, c0, c1, c2, c3, weights, sems):
-    height = c0.shape[1]
+def weight_copies(info, block, index, weights, sems):
+    height = block.shape[1]
     half_height = weights.shape[1] // 2
     copies = []
-    for index, block in enumerate((c0, c1, c2, c3)):
-        for turn in range(block.shape[0]):
-            slot, half = info[info_piece + 2 * turn], info[info_piece + 2 * turn + 1]
-            start = half * half_height + info[info_block + index] * height
-            rows = pl.ds(pl.multiple_of(start, height), height)
-            copies.append(
-                pltpu.make_async_copy(
-                    block.at[turn], weights.at[slot, rows, :], sems.at[index, turn]
-                )
-            )
+    for turn in range(block.shape[0]):
+        slot, half = info[info_piece + 2 * turn], info[info_piece + 2 * turn + 1]
+        start = half * half_height + info[info_block + index] * height
+        rows = pl.ds(pl.multiple_of(start, height), height)
+        copies.append(
+            pltpu.make_async_copy(block.at[turn], weights.at[slot, rows, :], sems.at[index, turn])
+        )
+    return copies
+
+
+def weight_kernel(info, c0, c1, c2, weights, sems):
+    copies = []
+    for index, block in enumerate((c0, c1, c2)):
+        copies += weight_copies(info, block, index, weights, sems)
     start_all(copies)
     wait_all(copies)
+
+
+def last_weight_kernel(info, c3, begun, weights, sems):
+    copies = weight_copies(info, c3, 3, weights, sems)
+    start_all(copies)
+    wait_all(copies)
+
+
+def after_kernel(rows, x_both, held, sem):
+    copy = pltpu.make_async_copy(rows, held, sem)
+    copy.start()
+    copy.wait()
 
 
 def both_kernel(info, x_column, x_aside, y_column, y0, y1, rhs, x_both, y_both, sems):
@@ -466,7 +468,7 @@
     rows_here = field.shape[1]
     height = x_factor.shape[2]
     params = pltpu.CompilerParams(vmem_limit_bytes=vmem_bytes)
-    rounds = [(a, b) for a in range(groups) for b in range(px_count)]
+    rounds = [(0, 0), (1, 0), (1, 1), (0, 1)]
 
     def pairs(a, b):
         return [
@@ -504,14 +506,8 @@
         + [own_y, group == member]
     ).astype(jnp.int32)
     piece_shape = jax.ShapeDtypeStruct((2, rows_here, order), bf16)
-    blocks = pl.pallas_call(
-        block_kernel,
-        out_shape=jax.ShapeDtypeStruct((py_count, 2, height, 2 * order), bf16),
-        in_specs=[in_hbm] * 2,
-        out_specs=in_vmem,
-        scratch_shapes=[pltpu.SemaphoreType.DMA((py_count, 2, 2))],
-        compiler_params=params,
-    )(x_factor[0], y_factor[0])
+    shard = jnp.concatenate([x_factor[0], y_factor[0]], axis=0)
+    blocks = jnp.broadcast_to(shard[None], (py_count,) + shard.shape)
     tall = height // 2
     packed = pl.pallas_call(
         pack_kernel,
@@ -577,17 +573,35 @@
     )(info, x_column, x_aside, y_turned, *y_near, rhs)
     y_far = aside(y_both)
     x_across = [across(x_both, a) for a in range(2)]
-    weights = pl.pallas_call(
+    weight_sems = [pltpu.SemaphoreType.DMA((4, len(rounds)))]
+    begun = pl.pallas_call(
         weight_kernel,
         out_shape=full_shape,
-        in_specs=[in_smem] + [anywhere] * 4,
+        in_specs=[in_smem] + [anywhere] * 3,
         out_specs=in_vmem,
-        scratch_shapes=[pltpu.SemaphoreType.DMA((4, len(rounds)))],
+        scratch_shapes=weight_sems,
         compiler_params=params,
         cost_estimate=pl.CostEstimate(
             flops=3 * 10**10, bytes_accessed=2**21, transcendentals=0
         ),
-    )(info, rows_held, rows_next, rows_far, over_z(rows_next, 2))
+    )(info, rows_held, rows_next, rows_far)
+    rows_after = pl.pallas_call(
+        after_kernel,
+        out_shape=jax.ShapeDtypeStruct(rows_next.shape, bf16),
+        in_specs=[anywhere] * 2,
+        out_specs=in_vmem,
+        scratch_shapes=[pltpu.SemaphoreType.DMA(())],
+        compiler_params=params,
+    )(rows_next, x_both)
+    weights = pl.pallas_call(
+        last_weight_kernel,
+        out_shape=full_shape,
+        in_specs=[in_smem] + [anywhere] * 2,
+        out_specs=anywhere,
+        scratch_shapes=weight_sems,
+        input_output_aliases={2: 0},
+        compiler_params=params,
+    )(info, over_z(rows_after, 2), begun)
     layers = (info, x_both, *x_across, y_both, y_far, weights)
     layer_specs = [in_smem] + [anywhere] * 3 + [in_vmem] * 3
     solver_scratch = [

time: 149 us -> 149 us (level)
  starting transfers between devices: 40.7 us -> 43.5 us
  waiting for transfers between devices: 77.9 us -> 75.5 us
    ppermute x3, waiting for transfers between devices: 18.3 us -> 8.61 us  [over_z(): return lax.ppermute(block, 'py', [(z, z ^ bit) for z in range(py_count)])]
    ppermute x4, waiting for transfers between devices: 0.01 us -> 3.84 us  [across(): return lax.ppermute(block, ('sec', 'px'), pairs(a, 0))]
    ppermute x4, starting transfers between devices: 6.13 us -> 9.17 us  [across(): return lax.ppermute(block, ('sec', 'px'), pairs(a, 0))]
    ppermute x4, starting transfers between devices: 13.6 us -> 10.5 us  [on_device(): lax.ppermute(piece, ('sec', 'px'), back_pairs(a, b))]
    ppermute x3, starting transfers between devices: 4.57 us -> 6.6 us  [over_z(): return lax.ppermute(block, 'py', [(z, z ^ bit) for z in range(py_count)])]
    ppermute x4, waiting for transfers between devices: 18.9 us -> 20.9 us  [on_device(): lax.ppermute(piece, ('sec', 'px'), back_pairs(a, b))]
    unnamed x10 -> x6, local copies, waits for them, and re-layouts: 3.45 us -> 1.6 us
    ppermute x2, waiting for transfers between devices: 11.9 us -> 13.5 us  [aside(): return lax.ppermute(block, 'px', [(y, (y + 1) % 2) for y in range(2)])]
  transfers between devices with their start and end apart: 20 -> 20, of which waited for: 12 -> 11; matrix products, arithmetic and copies ran while one was open for 1% -> 1% of each run, Pallas kernels for 5% -> 5%
where the time goes in v20:
time: 149 us
  waiting for transfers between devices  75.5 us (51%)
  starting transfers between devices  43.5 us (29%)
  Pallas kernels  21.8 us (15%)
  local copies, waits for them, and re-layouts  3.47 us (2%)
  between operations  3.16 us (2%)
    ppermute x4, waiting for transfers between devices, on_device(): lax.ppermute(piece, ('sec', 'px'), back_pairs(a, b))  20.9 us
    ppermute x4, waiting for transfers between devices, on_device(): lax.ppermute(piece, ('sec', 'px'), pairs(a, b))  18.4 us
    ppermute x2, waiting for transfers between devices, aside(): return lax.ppermute(block, 'px', [(y, (y + 1) % 2) for y in range(2)])  13.5 us
    ppermute x4, starting transfers between devices, on_device(): lax.ppermute(piece, ('sec', 'px'), back_pairs(a, b))  10.5 us
    ppermute x4, starting transfers between devices, across(): return lax.ppermute(block, ('sec', 'px'), pairs(a, 0))  9.17 us
    pallas_call x1, Pallas kernels, on_device(): pl.pallas_call(last_kernel, out_shape=[double_shape, full_shape], in_spec...  9.12 us
    ppermute x3, waiting for transfers between devices, over_z(): return lax.ppermute(block, 'py', [(z, z ^ bit) for z in range(py_count)])  8.61 us
    ppermute x1, waiting for transfers between devices, on_device(): incoming = lax.ppermute(w_high, 'sec', up)  8.08 us
  transfers between devices with their start and end apart: 20, of which 11 were waited for; matrix products, arithmetic and copies ran while one was open for 1% of the time, Pallas kernels for 5%

profile of v20, /device:TPU:1, one launch (start us, length us, event | category | flops | bytes accessed | tf_op | source)
XLA Modules:
  0.0 148.5 jit_solution(15066991984939769906)
XLA Ops:
  1.0 1.1 broadcast_in_dim.4
  2.1 5.6 %all-to-all-start = ((bf16[4,4,64,512]{3,2,1,0:T(8,128)(2,1)}), bf16[4,4,64,512]{3,2,1,0:T(8,128)(2,1)S(1)}, u32[]{:S(2)}, u32[]{:S(2)}) async-start(bf16[4,4,64,512]{3,2,1,0:T(8,128)(2,1)} %broadcast_in_dim.4), calls=%async_computation | async-start | bytes 2097152 | tf_op jit(solution)/shard_map/all_to_all | solution.py:523
  7.8 1.6 %copy-done = bf16[2,1,256,2048]{3,2,1,0:T(8,128)(2,1)S(1)} copy-done((bf16[2,1,256,2048]{3,2,1,0:T(8,128)(2,1)S(1)}, bf16[2,1,256,2048]{3,2,1,0:T(8,128)(2,1)}, u32[]{:S(2)}) %copy-start) | copy-done | bytes 2097176
  9.4 2.3 %shard_map.55 = (bf16[2,288,512]{2,1,0:T(8,128)(2,1)S(1)}, bf16[2,288,512]{2,1,0:T(8,128)(2,1)}, bf16[2,288,512]{2,1,0:T(8,128)(2,1)}, bf16[2,288,512]{2,1,0:T(8,128)(2,1)}) custom-call(s32[6]{0:T(128)S(1)} %stack.83.place, bf16[2,256,2048]{2,1,0:T(8,128)(2,1)S(1)} %bitcast.29, bf16[8,32,512]{2,1,0:T(8,128)(2,1)S(1)} %bitcast.30), custom_call_target="tpu_custom_call" | custom-call | tf_op jit(solution)/shard_map/pallas_call | solution.py:512
  12.7 2.6 %collective-permute-start.2 = (bf16[2,288,512]{2,1,0:T(8,128)(2,1)}, bf16[2,288,512]{2,1,0:T(8,128)(2,1)S(1)}, u32[]{:S(2)}, u32[]{:S(2)}) collective-permute-start(bf16[2,288,512]{2,1,0:T(8,128)(2,1)} %get-tuple-element.24), channel_id=1, source_target_pairs={{0,20},{4,16},{8,4},{12,0},{16,28},{20,24},{24,12},{28,8},{1,21},{... | collective-permute-start | bytes 1769480 | tf_op jit(solution)/shard_map/ppermute | solution.py:521
  15.3 3.6 %collective-permute-start = (bf16[2,288,512]{2,1,0:T(8,128)(2,1)S(1)}, bf16[2,288,512]{2,1,0:T(8,128)(2,1)}, u32[]{:S(2)}, u32[]{:S(2)}) collective-permute-start(bf16[2,288,512]{2,1,0:T(8,128)(2,1)S(1)} %get-tuple-element.22.own), channel_id=1, source_target_pairs={{8,16},{12,20},{16,8},{20,12},{9,17},{13,21},{17,9},{21,13},{10,18... | collective-permute-start | bytes 1769480 | tf_op jit(solution)/shard_map/ppermute | solution.py:521
  23.1 17.7 %collective-permute-done.2.p2 = bf16[2,288,512]{2,1,0:T(8,128)(2,1)S(1)} collective-permute-done((bf16[2,288,512]{2,1,0:T(8,128)(2,1)}, bf16[2,288,512]{2,1,0:T(8,128)(2,1)S(1)}, u32[]{:S(2)}, u32[]{:S(2)}) %collective-permute-start.2) | collective-permute-done | bytes 589856 | tf_op jit(solution)/shard_map/ppermute | solution.py:521
  40.8 1.4 shard_map.56
  43.1 2.1 %collective-permute-start.6 = (bf16[1024,256]{1,0:T(8,128)(2,1)S(1)}, bf16[1024,256]{1,0:T(8,128)(2,1)S(1)}, u32[]{:S(2)}, u32[]{:S(2)}) collective-permute-start(bf16[1024,256]{1,0:T(8,128)(2,1)S(1)} %get-tuple-element.27.y_column), channel_id=1, source_target_pairs={{0,16},{4,20},{8,0},{12,4},{16,24},{20,28},{24,8},{28,12},{1,17},{... | collective-permute-start | bytes 1572872 | tf_op jit(solution)/shard_map/ppermute | solution.py:542
  45.2 2.6 %collective-permute-start.5 = (bf16[1024,256]{1,0:T(8,128)(2,1)S(1)}, bf16[1024,256]{1,0:T(8,128)(2,1)S(1)}, u32[]{:S(2)}, u32[]{:S(2)}) collective-permute-start(bf16[1024,256]{1,0:T(8,128)(2,1)S(1)} %get-tuple-element.27.y_column), channel_id=1, source_target_pairs={{8,16},{12,20},{16,8},{20,12},{9,17},{13,21},{17,9},{21,13},{10,18... | collective-permute-start | bytes 1572872 | tf_op jit(solution)/shard_map/ppermute | solution.py:542
  47.8 1.8 %collective-permute-start.10 = (bf16[4,64,512]{2,1,0:T(8,128)(2,1)S(1)}, bf16[4,64,512]{2,1,0:T(8,128)(2,1)S(1)}, u32[]{:S(2)}, u32[]{:S(2)}) collective-permute-start(bf16[4,64,512]{2,1,0:T(8,128)(2,1)S(1)} %bitcast.31), channel_id=1, source_target_pairs={{0,1},{1,0},{2,3},{3,2},{4,5},{5,4},{6,7},{7,6},{8,9},{9,8},{10,11... | collective-permute-start | bytes 786440 | tf_op jit(solution)/shard_map/ppermute | solution.py:548
  49.7 2.1 %collective-permute-start.12 = (bf16[4,64,512]{2,1,0:T(8,128)(2,1)S(1)}, bf16[4,64,512]{2,1,0:T(8,128)(2,1)S(1)}, u32[]{:S(2)}, u32[]{:S(2)}) collective-permute-start(bf16[4,64,512]{2,1,0:T(8,128)(2,1)S(1)} %bitcast.32), channel_id=1, source_target_pairs={{0,2},{1,3},{2,0},{3,1},{4,6},{5,7},{6,4},{7,5},{8,10},{9,11},{10,... | collective-permute-start | bytes 786440 | tf_op jit(solution)/shard_map/ppermute | solution.py:548
  51.7 1.6 %shard_map.57.rhs = bf16[2,2,512,512]{3,2,1,0:T(8,128)(2,1)S(1)} custom-call(s32[21]{0:T(128)S(1)} %stack.98.info, bf16[2,288,512]{2,1,0:T(8,128)(2,1)S(1)} %get-tuple-element.22.own, bf16[2,288,512]{2,1,0:T(8,128)(2,1)} %collective-permute-done.p0, bf16[2,288,512]{2,1,0:T(8,128)(2,1)S(1)} %collective-permute-done.1.p1, ...), custom_call_target="tpu_custom_call" | custom-call | tf_op jit(solution)/shard_map/pallas_call | solution.py:556
  54.4 3.8 %collective-permute-done.5.y0 = bf16[1024,256]{1,0:T(8,128)(2,1)S(1)} collective-permute-done((bf16[1024,256]{1,0:T(8,128)(2,1)S(1)}, bf16[1024,256]{1,0:T(8,128)(2,1)S(1)}, u32[]{:S(2)}, u32[]{:S(2)}) %collective-permute-start.5) | collective-permute-done | bytes 524320 | tf_op jit(solution)/shard_map/ppermute | solution.py:542
  59.0 4.4 %collective-permute-start.7 = (bf16[2,256,1024]{2,1,0:T(8,128)(2,1)S(1)}, bf16[2,256,1024]{2,1,0:T(8,128)(2,1)S(1)}, u32[]{:S(2)}, u32[]{:S(2)}) collective-permute-start(bf16[2,256,1024]{2,1,0:T(8,128)(2,1)S(1)} %get-tuple-element.28.x_both.xb), channel_id=1, source_target_pairs={{8,16},{12,20},{16,8},{20,12},{9,17},{13,21},{17,9},{21,13},{10,18... | collective-permute-start | bytes 3145736 | tf_op jit(solution)/shard_map/ppermute | solution.py:542
  63.5 2.7 %collective-permute-start.11 = (bf16[4,64,512]{2,1,0:T(8,128)(2,1)S(1)}, bf16[4,64,512]{2,1,0:T(8,128)(2,1)S(1)}, u32[]{:S(2)}, u32[]{:S(2)}) collective-permute-start(bf16[4,64,512]{2,1,0:T(8,128)(2,1)S(1)} %shard_map.59), channel_id=1, source_target_pairs={{0,2},{1,3},{2,0},{3,1},{4,6},{5,7},{6,4},{7,5},{8,10},{9,11},{10,... | collective-permute-start | bytes 786440 | tf_op jit(solution)/shard_map/ppermute | solution.py:548
  66.2 1.1 collective-permute-start.9
  67.2 1.9 %shard_map.60.begun = bf16[2,512,512]{2,1,0:T(8,128)(2,1)S(1)} custom-call(s32[21]{0:T(128)S(1)} %stack.98.info, bf16[4,64,512]{2,1,0:T(8,128)(2,1)S(1)} %bitcast.33, bf16[4,64,512]{2,1,0:T(8,128)(2,1)S(1)} %collective-permute-done.10.rows.c1, bf16[4,64,512]{2,1,0:T(8,128)(2,1)S(1)} %collective-permute-done.12.c2), custom_call_target="tpu_custom_call" | custom-call | flops 30000001024 | bytes 2097152 | tf_op jit(solution)/shard_map/pallas_call | solution.py:577
  69.1 8.6 %collective-permute-done.11.c3 = bf16[4,64,512]{2,1,0:T(8,128)(2,1)S(1)} collective-permute-done((bf16[4,64,512]{2,1,0:T(8,128)(2,1)S(1)}, bf16[4,64,512]{2,1,0:T(8,128)(2,1)S(1)}, u32[]{:S(2)}, u32[]{:S(2)}) %collective-permute-start.11) | collective-permute-done | bytes 262176 | tf_op jit(solution)/shard_map/ppermute | solution.py:548
  78.8 12.4 %collective-permute-done.9.yf = bf16[2,1024,256]{2,1,0:T(8,128)(2,1)S(1)} collective-permute-done((bf16[2,1024,256]{2,1,0:T(8,128)(2,1)S(1)}, bf16[2,1024,256]{2,1,0:T(8,128)(2,1)S(1)}, u32[]{:S(2)}, u32[]{:S(2)}) %collective-permute-start.9) | collective-permute-done | bytes 1048608 | tf_op jit(solution)/shard_map/ppermute | solution.py:545
  91.8 1.3 collective-permute-start.13
  93.1 8.1 %collective-permute-done.13.arrived = bf16[2,512,512]{2,1,0:T(8,128)(2,1)S(1)} collective-permute-done((bf16[2,512,512]{2,1,0:T(8,128)(2,1)S(1)}, bf16[2,512,512]{2,1,0:T(8,128)(2,1)S(1)}, u32[]{:S(2)}, u32[]{:S(2)}) %collective-permute-start.13) | collective-permute-done | bytes 1048608 | tf_op jit(solution)/shard_map/ppermute | solution.py:630
  101.2 9.1 %shard_map.63 = (bf16[2,2,512,512]{3,2,1,0:T(8,128)(2,1)S(1)}, bf16[2,512,512]{2,1,0:T(8,128)(2,1)S(1)}) custom-call(s32[21]{0:T(128)S(1)} %stack.98.info, bf16[2,256,1024]{2,1,0:T(8,128)(2,1)S(1)} %get-tuple-element.28.x_both.xb, bf16[2,256,1024]{2,1,0:T(8,128)(2,1)S(1)} %collective-permute-done.7.x0, bf16[2,256,1024]{2,1,0:T(8,128)(2,1)S(1)} %collective-permute-done.8.x1, ...), custom_call_target="tpu_custom_call" | custom-call | flops 6442450944 | bytes 8388608 | tf_op jit(solution)/shard_map/pallas_call | solution.py:631
  110.3 1.4 collective-permute-start.14
  111.7 2.2 %collective-permute-done.14.arrived = bf16[2,512,512]{2,1,0:T(8,128)(2,1)S(1)} collective-permute-done((bf16[2,512,512]{2,1,0:T(8,128)(2,1)S(1)}, bf16[2,512,512]{2,1,0:T(8,128)(2,1)S(1)}, u32[]{:S(2)}, u32[]{:S(2)}) %collective-permute-start.14) | collective-permute-done | bytes 1048608 | tf_op jit(solution)/shard_map/ppermute | solution.py:642
  114.8 4.7 %collective-permute-start.17 = (bf16[2,256,512]{2,1,0:T(8,128)(2,1)S(1)}, bf16[2,256,512]{2,1,0:T(8,128)(2,1)S(1)}, u32[]{:S(2)}, u32[]{:S(2)}) collective-permute-start(bf16[2,256,512]{2,1,0:T(8,128)(2,1)S(1)} %get-tuple-element.37), channel_id=1, source_target_pairs={{20,0},{16,4},{4,8},{0,12},{28,16},{24,20},{12,24},{8,28},{21,1},{... | collective-permute-start | bytes 1572872 | tf_op jit(solution)/shard_map/ppermute | solution.py:655
  119.5 3.9 %collective-permute-start.18 = (bf16[2,256,512]{2,1,0:T(8,128)(2,1)S(1)}, bf16[2,256,512]{2,1,0:T(8,128)(2,1)S(1)}, u32[]{:S(2)}, u32[]{:S(2)}) collective-permute-start(bf16[2,256,512]{2,1,0:T(8,128)(2,1)S(1)} %get-tuple-element.38), channel_id=1, source_target_pairs={{4,0},{0,4},{20,8},{16,12},{12,16},{8,20},{28,24},{24,28},{5,1},{1... | collective-permute-start | bytes 1572872 | tf_op jit(solution)/shard_map/ppermute | solution.py:655
  123.4 1.9 %collective-permute-start.15 = (bf16[2,256,512]{2,1,0:T(8,128)(2,1)S(1)}, bf16[2,256,512]{2,1,0:T(8,128)(2,1)S(1)}, u32[]{:S(2)}, u32[]{:S(2)}) collective-permute-start(bf16[2,256,512]{2,1,0:T(8,128)(2,1)S(1)} %get-tuple-element.35.own), channel_id=1, source_target_pairs={{16,8},{20,12},{8,16},{12,20},{17,9},{21,13},{9,17},{13,21},{18,10... | collective-permute-start | bytes 1572872 | tf_op jit(solution)/shard_map/ppermute | solution.py:655
  125.3 3.6 %collective-permute-done.17.rest_2_ = bf16[2,256,512]{2,1,0:T(8,128)(2,1)S(1)} collective-permute-done((bf16[2,256,512]{2,1,0:T(8,128)(2,1)S(1)}, bf16[2,256,512]{2,1,0:T(8,128)(2,1)S(1)}, u32[]{:S(2)}, u32[]{:S(2)}) %collective-permute-start.17) | collective-permute-done | bytes 524320 | tf_op jit(solution)/shard_map/ppermute | solution.py:655
  128.9 12.4 %collective-permute-done.18.rest_3_ = bf16[2,256,512]{2,1,0:T(8,128)(2,1)S(1)} collective-permute-done((bf16[2,256,512]{2,1,0:T(8,128)(2,1)S(1)}, bf16[2,256,512]{2,1,0:T(8,128)(2,1)S(1)}, u32[]{:S(2)}, u32[]{:S(2)}) %collective-permute-start.18) | collective-permute-done | bytes 524320 | tf_op jit(solution)/shard_map/ppermute | solution.py:655
  141.4 4.8 %collective-permute-done.15.rest_0_ = bf16[2,256,512]{2,1,0:T(8,128)(2,1)S(1)} collective-permute-done((bf16[2,256,512]{2,1,0:T(8,128)(2,1)S(1)}, bf16[2,256,512]{2,1,0:T(8,128)(2,1)S(1)}, u32[]{:S(2)}, u32[]{:S(2)}) %collective-permute-start.15) | collective-permute-done | bytes 524320 | tf_op jit(solution)/shard_map/ppermute | solution.py:655
  146.2 2.2 %shard_map.65 = bf16[2,256,2048]{2,1,0:T(8,128)(2,1)} custom-call(s32[6]{0:T(128)S(1)} %stack.83.place, bf16[2,256,512]{2,1,0:T(8,128)(2,1)S(1)} %get-tuple-element.35.own, bf16[2,256,512]{2,1,0:T(8,128)(2,1)S(1)} %collective-permute-done.15.rest_0_, bf16[2,256,512]{2,1,0:T(8,128)(2,1)S(1)} %collective-permute-done.16.rest_1_, ...), custom_call_target="tpu_custom_call" | custom-call | tf_op jit(solution)/shard_map/pallas_call | solution.py:657
  (30 shorter events, 8.7 us)
Async XLA Ops:
  0.0 7.8 %copy-start.1 = (bf16[1,256,512]{2,1,0:T(8,128)(2,1)S(1)}, bf16[1,256,512]{2,1,0:T(8,128)(2,1)}, u32[]{:S(2)}) copy-start(bf16[1,256,512]{2,1,0:T(8,128)(2,1)} %param.7) | copy-start | bytes 786436
  2.1 16.9 %copy-start.2 = (s32[16]{0:T(128)S(1)}, s32[16]{0:T(128)}, u32[]{:S(2)}) copy-start(s32[16]{0:T(128)} %param.6) | copy-start | bytes 196
  2.1 38.7 %all-to-all-start = ((bf16[4,4,64,512]{3,2,1,0:T(8,128)(2,1)}), bf16[4,4,64,512]{3,2,1,0:T(8,128)(2,1)S(1)}, u32[]{:S(2)}, u32[]{:S(2)}) async-start(bf16[4,4,64,512]{3,2,1,0:T(8,128)(2,1)} %broadcast_in_dim.4), calls=%async_computation | async-start | bytes 2097152 | tf_op jit(solution)/shard_map/all_to_all | solution.py:523
  7.8 1.6 %copy-start = (bf16[2,1,256,2048]{3,2,1,0:T(8,128)(2,1)S(1)}, bf16[2,1,256,2048]{3,2,1,0:T(8,128)(2,1)}, u32[]{:S(2)}) copy-start(bf16[2,1,256,2048]{3,2,1,0:T(8,128)(2,1)} %param.5) | copy-start | bytes 6291460
  11.7 11.4 %collective-permute-start.1 = (bf16[2,288,512]{2,1,0:T(8,128)(2,1)}, bf16[2,288,512]{2,1,0:T(8,128)(2,1)S(1)}, u32[]{:S(2)}, u32[]{:S(2)}) collective-permute-start(bf16[2,288,512]{2,1,0:T(8,128)(2,1)} %get-tuple-element.23), channel_id=1, source_target_pairs={{0,16},{4,20},{8,0},{12,4},{16,24},{20,28},{24,8},{28,12},{1,17},{... | collective-permute-start | bytes 1769480 | tf_op jit(solution)/shard_map/ppermute | solution.py:521
  12.7 28.2 %collective-permute-start.2 = (bf16[2,288,512]{2,1,0:T(8,128)(2,1)}, bf16[2,288,512]{2,1,0:T(8,128)(2,1)S(1)}, u32[]{:S(2)}, u32[]{:S(2)}) collective-permute-start(bf16[2,288,512]{2,1,0:T(8,128)(2,1)} %get-tuple-element.24), channel_id=1, source_target_pairs={{0,20},{4,16},{8,4},{12,0},{16,28},{20,24},{24,12},{28,8},{1,21},{... | collective-permute-start | bytes 1769480 | tf_op jit(solution)/shard_map/ppermute | solution.py:521
  15.3 25.6 %collective-permute-start.3 = (bf16[2,288,512]{2,1,0:T(8,128)(2,1)}, bf16[2,288,512]{2,1,0:T(8,128)(2,1)S(1)}, u32[]{:S(2)}, u32[]{:S(2)}) collective-permute-start(bf16[2,288,512]{2,1,0:T(8,128)(2,1)} %get-tuple-element.25), channel_id=1, source_target_pairs={{0,4},{4,0},{8,20},{12,16},{16,12},{20,8},{24,28},{28,24},{1,5},{5... | collective-permute-start | bytes 1769480 | tf_op jit(solution)/shard_map/ppermute | solution.py:521
  15.3 25.6 %collective-permute-start = (bf16[2,288,512]{2,1,0:T(8,128)(2,1)S(1)}, bf16[2,288,512]{2,1,0:T(8,128)(2,1)}, u32[]{:S(2)}, u32[]{:S(2)}) collective-permute-start(bf16[2,288,512]{2,1,0:T(8,128)(2,1)S(1)} %get-tuple-element.22.own), channel_id=1, source_target_pairs={{8,16},{12,20},{16,8},{20,12},{9,17},{13,21},{17,9},{21,13},{10,18... | collective-permute-start | bytes 1769480 | tf_op jit(solution)/shard_map/ppermute | solution.py:521
  42.3 12.1 %collective-permute-start.4 = (bf16[256,1024]{1,0:T(8,128)(2,1)S(1)}, bf16[256,1024]{1,0:T(8,128)(2,1)S(1)}, u32[]{:S(2)}, u32[]{:S(2)}) collective-permute-start(bf16[256,1024]{1,0:T(8,128)(2,1)S(1)} %get-tuple-element.26.x_column), channel_id=1, source_target_pairs={{0,4},{4,0},{1,5},{5,1},{2,6},{6,2},{3,7},{7,3},{8,12},{12,8},{9,1... | collective-permute-start | bytes 1572872 | tf_op jit(solution)/shard_map/ppermute | solution.py:545
  43.1 11.4 %collective-permute-start.6 = (bf16[1024,256]{1,0:T(8,128)(2,1)S(1)}, bf16[1024,256]{1,0:T(8,128)(2,1)S(1)}, u32[]{:S(2)}, u32[]{:S(2)}) collective-permute-start(bf16[1024,256]{1,0:T(8,128)(2,1)S(1)} %get-tuple-element.27.y_column), channel_id=1, source_target_pairs={{0,16},{4,20},{8,0},{12,4},{16,24},{20,28},{24,8},{28,12},{1,17},{... | collective-permute-start | bytes 1572872 | tf_op jit(solution)/shard_map/ppermute | solution.py:542
  45.2 13.1 %collective-permute-start.5 = (bf16[1024,256]{1,0:T(8,128)(2,1)S(1)}, bf16[1024,256]{1,0:T(8,128)(2,1)S(1)}, u32[]{:S(2)}, u32[]{:S(2)}) collective-permute-start(bf16[1024,256]{1,0:T(8,128)(2,1)S(1)} %get-tuple-element.27.y_column), channel_id=1, source_target_pairs={{8,16},{12,20},{16,8},{20,12},{9,17},{13,21},{17,9},{21,13},{10,18... | collective-permute-start | bytes 1572872 | tf_op jit(solution)/shard_map/ppermute | solution.py:542
  47.8 15.6 %collective-permute-start.10 = (bf16[4,64,512]{2,1,0:T(8,128)(2,1)S(1)}, bf16[4,64,512]{2,1,0:T(8,128)(2,1)S(1)}, u32[]{:S(2)}, u32[]{:S(2)}) collective-permute-start(bf16[4,64,512]{2,1,0:T(8,128)(2,1)S(1)} %bitcast.31), channel_id=1, source_target_pairs={{0,1},{1,0},{2,3},{3,2},{4,5},{5,4},{6,7},{7,6},{8,9},{9,8},{10,11... | collective-permute-start | bytes 786440 | tf_op jit(solution)/shard_map/ppermute | solution.py:548
  49.7 17.6 %collective-permute-start.12 = (bf16[4,64,512]{2,1,0:T(8,128)(2,1)S(1)}, bf16[4,64,512]{2,1,0:T(8,128)(2,1)S(1)}, u32[]{:S(2)}, u32[]{:S(2)}) collective-permute-start(bf16[4,64,512]{2,1,0:T(8,128)(2,1)S(1)} %bitcast.32), channel_id=1, source_target_pairs={{0,2},{1,3},{2,0},{3,1},{4,6},{5,7},{6,4},{7,5},{8,10},{9,11},{10,... | collective-permute-start | bytes 786440 | tf_op jit(solution)/shard_map/ppermute | solution.py:548
  59.0 32.2 %collective-permute-start.8 = (bf16[2,256,1024]{2,1,0:T(8,128)(2,1)S(1)}, bf16[2,256,1024]{2,1,0:T(8,128)(2,1)S(1)}, u32[]{:S(2)}, u32[]{:S(2)}) collective-permute-start(bf16[2,256,1024]{2,1,0:T(8,128)(2,1)S(1)} %get-tuple-element.28.x_both.xb), channel_id=1, source_target_pairs={{0,16},{4,20},{8,0},{12,4},{16,24},{20,28},{24,8},{28,12},{1,17},{... | collective-permute-start | bytes 3145736 | tf_op jit(solution)/shard_map/ppermute | solution.py:542
  59.0 32.2 %collective-permute-start.7 = (bf16[2,256,1024]{2,1,0:T(8,128)(2,1)S(1)}, bf16[2,256,1024]{2,1,0:T(8,128)(2,1)S(1)}, u32[]{:S(2)}, u32[]{:S(2)}) collective-permute-start(bf16[2,256,1024]{2,1,0:T(8,128)(2,1)S(1)} %get-tuple-element.28.x_both.xb), channel_id=1, source_target_pairs={{8,16},{12,20},{16,8},{20,12},{9,17},{13,21},{17,9},{21,13},{10,18... | collective-permute-start | bytes 3145736 | tf_op jit(solution)/shard_map/ppermute | solution.py:542
  63.5 14.3 %collective-permute-start.11 = (bf16[4,64,512]{2,1,0:T(8,128)(2,1)S(1)}, bf16[4,64,512]{2,1,0:T(8,128)(2,1)S(1)}, u32[]{:S(2)}, u32[]{:S(2)}) collective-permute-start(bf16[4,64,512]{2,1,0:T(8,128)(2,1)S(1)} %shard_map.59), channel_id=1, source_target_pairs={{0,2},{1,3},{2,0},{3,1},{4,6},{5,7},{6,4},{7,5},{8,10},{9,11},{10,... | collective-permute-start | bytes 786440 | tf_op jit(solution)/shard_map/ppermute | solution.py:548
  66.2 25.0 %collective-permute-start.9 = (bf16[2,1024,256]{2,1,0:T(8,128)(2,1)S(1)}, bf16[2,1024,256]{2,1,0:T(8,128)(2,1)S(1)}, u32[]{:S(2)}, u32[]{:S(2)}) collective-permute-start(bf16[2,1024,256]{2,1,0:T(8,128)(2,1)S(1)} %get-tuple-element.29.yb), channel_id=1, source_target_pairs={{0,4},{4,0},{1,5},{5,1},{2,6},{6,2},{3,7},{7,3},{8,12},{12,8},{9,1... | collective-permute-start | bytes 3145736 | tf_op jit(solution)/shard_map/ppermute | solution.py:545
  91.8 9.4 %collective-permute-start.13 = (bf16[2,512,512]{2,1,0:T(8,128)(2,1)S(1)}, bf16[2,512,512]{2,1,0:T(8,128)(2,1)S(1)}, u32[]{:S(2)}, u32[]{:S(2)}) collective-permute-start(bf16[2,512,512]{2,1,0:T(8,128)(2,1)S(1)} %get-tuple-element.32.w_high), channel_id=1, source_target_pairs={{0,8},{16,24},{1,9},{17,25},{2,10},{18,26},{3,11},{19,27},{4,12},{... | collective-permute-start | bytes 3145736 | tf_op jit(solution)/shard_map/ppermute | solution.py:630
  110.3 3.6 %collective-permute-start.14 = (bf16[2,512,512]{2,1,0:T(8,128)(2,1)S(1)}, bf16[2,512,512]{2,1,0:T(8,128)(2,1)S(1)}, u32[]{:S(2)}, u32[]{:S(2)}) collective-permute-start(bf16[2,512,512]{2,1,0:T(8,128)(2,1)S(1)} %get-tuple-element.33), channel_id=1, source_target_pairs={{8,0},{24,16},{9,1},{25,17},{10,2},{26,18},{11,3},{27,19},{12,4},{... | collective-permute-start | bytes 3145736 | tf_op jit(solution)/shard_map/ppermute | solution.py:642
  114.7 10.6 %collective-permute-start.16 = (bf16[2,256,512]{2,1,0:T(8,128)(2,1)S(1)}, bf16[2,256,512]{2,1,0:T(8,128)(2,1)S(1)}, u32[]{:S(2)}, u32[]{:S(2)}) collective-permute-start(bf16[2,256,512]{2,1,0:T(8,128)(2,1)S(1)} %get-tuple-element.36), channel_id=1, source_target_pairs={{16,0},{20,4},{0,8},{4,12},{24,16},{28,20},{8,24},{12,28},{17,1},{... | collective-permute-start | bytes 1572872 | tf_op jit(solution)/shard_map/ppermute | solution.py:655
  114.8 14.2 %collective-permute-start.17 = (bf16[2,256,512]{2,1,0:T(8,128)(2,1)S(1)}, bf16[2,256,512]{2,1,0:T(8,128)(2,1)S(1)}, u32[]{:S(2)}, u32[]{:S(2)}) collective-permute-start(bf16[2,256,512]{2,1,0:T(8,128)(2,1)S(1)} %get-tuple-element.37), channel_id=1, source_target_pairs={{20,0},{16,4},{4,8},{0,12},{28,16},{24,20},{12,24},{8,28},{21,1},{... | collective-permute-start | bytes 1572872 | tf_op jit(solution)/shard_map/ppermute | solution.py:655
  119.5 21.9 %collective-permute-start.18 = (bf16[2,256,512]{2,1,0:T(8,128)(2,1)S(1)}, bf16[2,256,512]{2,1,0:T(8,128)(2,1)S(1)}, u32[]{:S(2)}, u32[]{:S(2)}) collective-permute-start(bf16[2,256,512]{2,1,0:T(8,128)(2,1)S(1)} %get-tuple-element.38), channel_id=1, source_target_pairs={{4,0},{0,4},{20,8},{16,12},{12,16},{8,20},{28,24},{24,28},{5,1},{1... | collective-permute-start | bytes 1572872 | tf_op jit(solution)/shard_map/ppermute | solution.py:655
  123.4 22.8 %collective-permute-start.15 = (bf16[2,256,512]{2,1,0:T(8,128)(2,1)S(1)}, bf16[2,256,512]{2,1,0:T(8,128)(2,1)S(1)}, u32[]{:S(2)}, u32[]{:S(2)}) collective-permute-start(bf16[2,256,512]{2,1,0:T(8,128)(2,1)S(1)} %get-tuple-element.35.own), channel_id=1, source_target_pairs={{16,8},{20,12},{8,16},{12,20},{17,9},{21,13},{9,17},{13,21},{18,10... | collective-permute-start | bytes 1572872 | tf_op jit(solution)/shard_map/ppermute | solution.py:655

commit v21 on v20

--- a/solution.py
+++ b/solution.py
@@ -281,18 +281,14 @@
     wait_all(copies)
 
 
-def after_kernel(rows, x_both, held, sem):
-    copy = pltpu.make_async_copy(rows, held, sem)
-    copy.start()
-    copy.wait()
-
-
-def both_kernel(info, x_column, x_aside, y_column, y0, y1, rhs, x_both, y_both, sems):
+def both_kernel(info, x_column, x_aside, y_column, y0, y1, rhs, rows_next, x_both, y_both,
+                rows_after, sems):
     copies = [
         pltpu.make_async_copy(x_column, x_both.at[0], sems.at[0]),
         pltpu.make_async_copy(x_aside, x_both.at[1], sems.at[1]),
         Either(info[info_self], y_column, y0, y_both.at[0], sems.at[2]),
         pltpu.make_async_copy(y1, y_both.at[1], sems.at[3]),
+        pltpu.make_async_copy(rows_next, rows_after, sems.at[4]),
     ]
     start_all(copies)
     wait_all(copies)
@@ -561,16 +557,17 @@
         scratch_shapes=[pltpu.SemaphoreType.DMA((len(rounds),))],
         compiler_params=params,
     )(info, packed[0], *pieces)
-    x_both, y_both = pl.pallas_call(
+    x_both, y_both, rows_after = pl.pallas_call(
         both_kernel,
         out_shape=[
             jax.ShapeDtypeStruct((2,) + one.shape, bf16) for one in (column_shape, turned_shape)
-        ],
-        in_specs=[in_smem] + [anywhere] * 6,
-        out_specs=[in_vmem] * 2,
-        scratch_shapes=[pltpu.SemaphoreType.DMA((4,))],
-        compiler_params=params,
-    )(info, x_column, x_aside, y_turned, *y_near, rhs)
+        ]
+        + [jax.ShapeDtypeStruct(rows_next.shape, bf16)],
+        in_specs=[in_smem] + [anywhere] * 7,
+        out_specs=[in_vmem] * 3,
+        scratch_shapes=[pltpu.SemaphoreType.DMA((5,))],
+        compiler_params=params,
+    )(info, x_column, x_aside, y_turned, *y_near, rhs, rows_next)
     y_far = aside(y_both)
     x_across = [across(x_both, a) for a in range(2)]
     weight_sems = [pltpu.SemaphoreType.DMA((4, len(rounds)))]
@@ -585,14 +582,6 @@
             flops=3 * 10**10, bytes_accessed=2**21, transcendentals=0
         ),
     )(info, rows_held, rows_next, rows_far)
-    rows_after = pl.pallas_call(
-        after_kernel,
-        out_shape=jax.ShapeDtypeStruct(rows_next.shape, bf16),
-        in_specs=[anywhere] * 2,
-        out_specs=in_vmem,
-        scratch_shapes=[pltpu.SemaphoreType.DMA(())],
-        compiler_params=params,
-    )(rows_next, x_both)
     weights = pl.pallas_call(
         last_weight_kernel,
         out_shape=full_shape,

time: 149 us -> 149 us (level)
  starting transfers between devices: 43.5 us -> 40.8 us
  waiting for transfers between devices: 75.5 us -> 78.2 us
    ppermute x3, waiting for transfers between devices: 8.61 us -> 16.2 us  [over_z(): return lax.ppermute(block, 'py', [(z, z ^ bit) for z in range(py_count)])]
    ppermute x4, waiting for transfers between devices: 3.84 us -> 0.01 us  [across(): return lax.ppermute(block, ('sec', 'px'), pairs(a, 0))]
    ppermute x4, starting transfers between devices: 9.17 us -> 6.71 us  [across(): return lax.ppermute(block, ('sec', 'px'), pairs(a, 0))]
  transfers between devices with their start and end apart: 20 -> 20, of which waited for: 11 -> 10; matrix products, arithmetic and copies ran while one was open for 1% -> 1% of each run, Pallas kernels for 5% -> 5%
where the time goes in v21:
time: 149 us; the launch traced here: 148 us
  waiting for transfers between devices  78.2 us (52%)
  starting transfers between devices  40.8 us (27%)
  Pallas kernels  21.8 us (15%)
  local copies, waits for them, and re-layouts  3.47 us (2%)
  between operations  3.15 us (2%)
    ppermute x4, waiting for transfers between devices, on_device(): lax.ppermute(piece, ('sec', 'px'), back_pairs(a, b))  20.9 us
    ppermute x4, waiting for transfers between devices, on_device(): lax.ppermute(piece, ('sec', 'px'), pairs(a, b))  18.4 us
    ppermute x3, waiting for transfers between devices, over_z(): return lax.ppermute(block, 'py', [(z, z ^ bit) for z in range(py_count)])  16.2 us
    ppermute x2, waiting for transfers between devices, aside(): return lax.ppermute(block, 'px', [(y, (y + 1) % 2) for y in range(2)])  12.4 us
    ppermute x4, starting transfers between devices, on_device(): lax.ppermute(piece, ('sec', 'px'), back_pairs(a, b))  10.5 us
    pallas_call x1, Pallas kernels, on_device(): pl.pallas_call(last_kernel, out_shape=[double_shape, full_shape], in_spec...  9.12 us
    ppermute x1, waiting for transfers between devices, on_device(): incoming = lax.ppermute(w_high, 'sec', up)  8.08 us
    ppermute x4, starting transfers between devices, on_device(): lax.ppermute(piece, ('sec', 'px'), pairs(a, b))  7.17 us
  transfers between devices with their start and end apart: 20, of which 10 were waited for; matrix products, arithmetic and copies ran while one was open for 1% of the time, Pallas kernels for 5%

profile of v21, /device:TPU:1, one launch (start us, length us, event | category | flops | bytes accessed | tf_op | source)
XLA Modules:
  0.0 148.5 jit_solution(14023987141967374058)
XLA Ops:
  1.0 1.1 broadcast_in_dim.4
  2.1 5.6 %all-to-all-start = ((bf16[4,4,64,512]{3,2,1,0:T(8,128)(2,1)}), bf16[4,4,64,512]{3,2,1,0:T(8,128)(2,1)S(1)}, u32[]{:S(2)}, u32[]{:S(2)}) async-start(bf16[4,4,64,512]{3,2,1,0:T(8,128)(2,1)} %broadcast_in_dim.4), calls=%async_computation | async-start | bytes 2097152 | tf_op jit(solution)/shard_map/all_to_all | solution.py:519
  7.8 1.6 %copy-done = bf16[2,1,256,2048]{3,2,1,0:T(8,128)(2,1)S(1)} copy-done((bf16[2,1,256,2048]{3,2,1,0:T(8,128)(2,1)S(1)}, bf16[2,1,256,2048]{3,2,1,0:T(8,128)(2,1)}, u32[]{:S(2)}) %copy-start) | copy-done | bytes 2097176
  9.4 2.3 %shard_map.55 = (bf16[2,288,512]{2,1,0:T(8,128)(2,1)S(1)}, bf16[2,288,512]{2,1,0:T(8,128)(2,1)}, bf16[2,288,512]{2,1,0:T(8,128)(2,1)}, bf16[2,288,512]{2,1,0:T(8,128)(2,1)}) custom-call(s32[6]{0:T(128)S(1)} %stack.83.place, bf16[2,256,2048]{2,1,0:T(8,128)(2,1)S(1)} %bitcast.29, bf16[8,32,512]{2,1,0:T(8,128)(2,1)S(1)} %bitcast.30), custom_call_target="tpu_custom_call" | custom-call | tf_op jit(solution)/shard_map/pallas_call | solution.py:508
  12.7 2.6 %collective-permute-start.2 = (bf16[2,288,512]{2,1,0:T(8,128)(2,1)}, bf16[2,288,512]{2,1,0:T(8,128)(2,1)S(1)}, u32[]{:S(2)}, u32[]{:S(2)}) collective-permute-start(bf16[2,288,512]{2,1,0:T(8,128)(2,1)} %get-tuple-element.25), channel_id=1, source_target_pairs={{0,20},{4,16},{8,4},{12,0},{16,28},{20,24},{24,12},{28,8},{1,21},{... | collective-permute-start | bytes 1769480 | tf_op jit(solution)/shard_map/ppermute | solution.py:517
  15.3 3.6 %collective-permute-start = (bf16[2,288,512]{2,1,0:T(8,128)(2,1)S(1)}, bf16[2,288,512]{2,1,0:T(8,128)(2,1)}, u32[]{:S(2)}, u32[]{:S(2)}) collective-permute-start(bf16[2,288,512]{2,1,0:T(8,128)(2,1)S(1)} %get-tuple-element.23.own), channel_id=1, source_target_pairs={{8,16},{12,20},{16,8},{20,12},{9,17},{13,21},{17,9},{21,13},{10,18... | collective-permute-start | bytes 1769480 | tf_op jit(solution)/shard_map/ppermute | solution.py:517
  23.1 17.7 %collective-permute-done.2.p2 = bf16[2,288,512]{2,1,0:T(8,128)(2,1)S(1)} collective-permute-done((bf16[2,288,512]{2,1,0:T(8,128)(2,1)}, bf16[2,288,512]{2,1,0:T(8,128)(2,1)S(1)}, u32[]{:S(2)}, u32[]{:S(2)}) %collective-permute-start.2) | collective-permute-done | bytes 589856 | tf_op jit(solution)/shard_map/ppermute | solution.py:517
  40.8 1.4 shard_map.56
  43.1 2.1 %collective-permute-start.6 = (bf16[1024,256]{1,0:T(8,128)(2,1)S(1)}, bf16[1024,256]{1,0:T(8,128)(2,1)S(1)}, u32[]{:S(2)}, u32[]{:S(2)}) collective-permute-start(bf16[1024,256]{1,0:T(8,128)(2,1)S(1)} %get-tuple-element.28.y_column), channel_id=1, source_target_pairs={{0,16},{4,20},{8,0},{12,4},{16,24},{20,28},{24,8},{28,12},{1,17},{... | collective-permute-start | bytes 1572872 | tf_op jit(solution)/shard_map/ppermute | solution.py:538
  45.2 2.6 %collective-permute-start.5 = (bf16[1024,256]{1,0:T(8,128)(2,1)S(1)}, bf16[1024,256]{1,0:T(8,128)(2,1)S(1)}, u32[]{:S(2)}, u32[]{:S(2)}) collective-permute-start(bf16[1024,256]{1,0:T(8,128)(2,1)S(1)} %get-tuple-element.28.y_column), channel_id=1, source_target_pairs={{8,16},{12,20},{16,8},{20,12},{9,17},{13,21},{17,9},{21,13},{10,18... | collective-permute-start | bytes 1572872 | tf_op jit(solution)/shard_map/ppermute | solution.py:538
  47.8 1.8 %collective-permute-start.7 = (bf16[4,64,512]{2,1,0:T(8,128)(2,1)S(1)}, bf16[4,64,512]{2,1,0:T(8,128)(2,1)S(1)}, u32[]{:S(2)}, u32[]{:S(2)}) collective-permute-start(bf16[4,64,512]{2,1,0:T(8,128)(2,1)S(1)} %bitcast.31), channel_id=1, source_target_pairs={{0,1},{1,0},{2,3},{3,2},{4,5},{5,4},{6,7},{7,6},{8,9},{9,8},{10,11... | collective-permute-start | bytes 786440 | tf_op jit(solution)/shard_map/ppermute | solution.py:544
  49.7 2.1 %collective-permute-start.12 = (bf16[4,64,512]{2,1,0:T(8,128)(2,1)S(1)}, bf16[4,64,512]{2,1,0:T(8,128)(2,1)S(1)}, u32[]{:S(2)}, u32[]{:S(2)}) collective-permute-start(bf16[4,64,512]{2,1,0:T(8,128)(2,1)S(1)} %bitcast.32), channel_id=1, source_target_pairs={{0,2},{1,3},{2,0},{3,1},{4,6},{5,7},{6,4},{7,5},{8,10},{9,11},{10,... | collective-permute-start | bytes 786440 | tf_op jit(solution)/shard_map/ppermute | solution.py:544
  51.7 1.6 %shard_map.57.rhs = bf16[2,2,512,512]{3,2,1,0:T(8,128)(2,1)S(1)} custom-call(s32[21]{0:T(128)S(1)} %stack.98.info, bf16[2,288,512]{2,1,0:T(8,128)(2,1)S(1)} %get-tuple-element.23.own, bf16[2,288,512]{2,1,0:T(8,128)(2,1)} %collective-permute-done.p0, bf16[2,288,512]{2,1,0:T(8,128)(2,1)S(1)} %collective-permute-done.1.p1, ...), custom_call_target="tpu_custom_call" | custom-call | tf_op jit(solution)/shard_map/pallas_call | solution.py:552
  53.4 7.6 %collective-permute-done.7.rows_next.c1 = bf16[4,64,512]{2,1,0:T(8,128)(2,1)S(1)} collective-permute-done((bf16[4,64,512]{2,1,0:T(8,128)(2,1)S(1)}, bf16[4,64,512]{2,1,0:T(8,128)(2,1)S(1)}, u32[]{:S(2)}, u32[]{:S(2)}) %collective-permute-start.7) | collective-permute-done | bytes 262176 | tf_op jit(solution)/shard_map/ppermute | solution.py:544
  61.8 1.9 %collective-permute-start.8 = (bf16[2,256,1024]{2,1,0:T(8,128)(2,1)S(1)}, bf16[2,256,1024]{2,1,0:T(8,128)(2,1)S(1)}, u32[]{:S(2)}, u32[]{:S(2)}) collective-permute-start(bf16[2,256,1024]{2,1,0:T(8,128)(2,1)S(1)} %get-tuple-element.30.xb), channel_id=1, source_target_pairs={{8,16},{12,20},{16,8},{20,12},{9,17},{13,21},{17,9},{21,13},{10,18... | collective-permute-start | bytes 3145736 | tf_op jit(solution)/shard_map/ppermute | solution.py:538
  63.7 2.4 %collective-permute-start.11 = (bf16[4,64,512]{2,1,0:T(8,128)(2,1)S(1)}, bf16[4,64,512]{2,1,0:T(8,128)(2,1)S(1)}, u32[]{:S(2)}, u32[]{:S(2)}) collective-permute-start(bf16[4,64,512]{2,1,0:T(8,128)(2,1)S(1)} %get-tuple-element.32), channel_id=1, source_target_pairs={{0,2},{1,3},{2,0},{3,1},{4,6},{5,7},{6,4},{7,5},{8,10},{9,11},{10,... | collective-permute-start | bytes 786440 | tf_op jit(solution)/shard_map/ppermute | solution.py:544
  66.2 1.1 collective-permute-start.10
  67.2 1.9 %shard_map.59.begun = bf16[2,512,512]{2,1,0:T(8,128)(2,1)S(1)} custom-call(s32[21]{0:T(128)S(1)} %stack.98.info, bf16[4,64,512]{2,1,0:T(8,128)(2,1)S(1)} %bitcast.33, bf16[4,64,512]{2,1,0:T(8,128)(2,1)S(1)} %collective-permute-done.7.rows_next.c1, bf16[4,64,512]{2,1,0:T(8,128)(2,1)S(1)} %collective-permute-done.12.c2), custom_call_target="tpu_custom_call" | custom-call | flops 30000001024 | bytes 2097152 | tf_op jit(solution)/shard_map/pallas_call | solution.py:574
  69.1 8.6 %collective-permute-done.11.c3 = bf16[4,64,512]{2,1,0:T(8,128)(2,1)S(1)} collective-permute-done((bf16[4,64,512]{2,1,0:T(8,128)(2,1)S(1)}, bf16[4,64,512]{2,1,0:T(8,128)(2,1)S(1)}, u32[]{:S(2)}, u32[]{:S(2)}) %collective-permute-start.11) | collective-permute-done | bytes 262176 | tf_op jit(solution)/shard_map/ppermute | solution.py:544
  78.8 12.4 %collective-permute-done.10.yf = bf16[2,1024,256]{2,1,0:T(8,128)(2,1)S(1)} collective-permute-done((bf16[2,1024,256]{2,1,0:T(8,128)(2,1)S(1)}, bf16[2,1024,256]{2,1,0:T(8,128)(2,1)S(1)}, u32[]{:S(2)}, u32[]{:S(2)}) %collective-permute-start.10) | collective-permute-done | bytes 1048608 | tf_op jit(solution)/shard_map/ppermute | solution.py:541
  91.8 1.3 collective-permute-start.13
  93.1 8.1 %collective-permute-done.13.arrived = bf16[2,512,512]{2,1,0:T(8,128)(2,1)S(1)} collective-permute-done((bf16[2,512,512]{2,1,0:T(8,128)(2,1)S(1)}, bf16[2,512,512]{2,1,0:T(8,128)(2,1)S(1)}, u32[]{:S(2)}, u32[]{:S(2)}) %collective-permute-start.13) | collective-permute-done | bytes 1048608 | tf_op jit(solution)/shard_map/ppermute | solution.py:619
  101.2 9.1 %shard_map.62 = (bf16[2,2,512,512]{3,2,1,0:T(8,128)(2,1)S(1)}, bf16[2,512,512]{2,1,0:T(8,128)(2,1)S(1)}) custom-call(s32[21]{0:T(128)S(1)} %stack.98.info, bf16[2,256,1024]{2,1,0:T(8,128)(2,1)S(1)} %get-tuple-element.30.xb, bf16[2,256,1024]{2,1,0:T(8,128)(2,1)S(1)} %collective-permute-done.8.x0, bf16[2,256,1024]{2,1,0:T(8,128)(2,1)S(1)} %collective-permute-done.9.x1, ...), custom_call_target="tpu_custom_call" | custom-call | flops 6442450944 | bytes 8388608 | tf_op jit(solution)/shard_map/pallas_call | solution.py:620
  110.3 1.4 collective-permute-start.14
  111.7 2.2 %collective-permute-done.14.arrived = bf16[2,512,512]{2,1,0:T(8,128)(2,1)S(1)} collective-permute-done((bf16[2,512,512]{2,1,0:T(8,128)(2,1)S(1)}, bf16[2,512,512]{2,1,0:T(8,128)(2,1)S(1)}, u32[]{:S(2)}, u32[]{:S(2)}) %collective-permute-start.14) | collective-permute-done | bytes 1048608 | tf_op jit(solution)/shard_map/ppermute | solution.py:631
  114.8 5.5 %collective-permute-start.17 = (bf16[2,256,512]{2,1,0:T(8,128)(2,1)S(1)}, bf16[2,256,512]{2,1,0:T(8,128)(2,1)S(1)}, u32[]{:S(2)}, u32[]{:S(2)}) collective-permute-start(bf16[2,256,512]{2,1,0:T(8,128)(2,1)S(1)} %get-tuple-element.39), channel_id=1, source_target_pairs={{20,0},{16,4},{4,8},{0,12},{28,16},{24,20},{12,24},{8,28},{21,1},{... | collective-permute-start | bytes 1572872 | tf_op jit(solution)/shard_map/ppermute | solution.py:644
  120.3 3.1 %collective-permute-start.18 = (bf16[2,256,512]{2,1,0:T(8,128)(2,1)S(1)}, bf16[2,256,512]{2,1,0:T(8,128)(2,1)S(1)}, u32[]{:S(2)}, u32[]{:S(2)}) collective-permute-start(bf16[2,256,512]{2,1,0:T(8,128)(2,1)S(1)} %get-tuple-element.40), channel_id=1, source_target_pairs={{4,0},{0,4},{20,8},{16,12},{12,16},{8,20},{28,24},{24,28},{5,1},{1... | collective-permute-start | bytes 1572872 | tf_op jit(solution)/shard_map/ppermute | solution.py:644
  123.4 1.9 %collective-permute-start.15 = (bf16[2,256,512]{2,1,0:T(8,128)(2,1)S(1)}, bf16[2,256,512]{2,1,0:T(8,128)(2,1)S(1)}, u32[]{:S(2)}, u32[]{:S(2)}) collective-permute-start(bf16[2,256,512]{2,1,0:T(8,128)(2,1)S(1)} %get-tuple-element.37.own), channel_id=1, source_target_pairs={{16,8},{20,12},{8,16},{12,20},{17,9},{21,13},{9,17},{13,21},{18,10... | collective-permute-start | bytes 1572872 | tf_op jit(solution)/shard_map/ppermute | solution.py:644
  125.3 3.6 %collective-permute-done.17.rest_2_ = bf16[2,256,512]{2,1,0:T(8,128)(2,1)S(1)} collective-permute-done((bf16[2,256,512]{2,1,0:T(8,128)(2,1)S(1)}, bf16[2,256,512]{2,1,0:T(8,128)(2,1)S(1)}, u32[]{:S(2)}, u32[]{:S(2)}) %collective-permute-start.17) | collective-permute-done | bytes 524320 | tf_op jit(solution)/shard_map/ppermute | solution.py:644
  128.9 12.4 %collective-permute-done.18.rest_3_ = bf16[2,256,512]{2,1,0:T(8,128)(2,1)S(1)} collective-permute-done((bf16[2,256,512]{2,1,0:T(8,128)(2,1)S(1)}, bf16[2,256,512]{2,1,0:T(8,128)(2,1)S(1)}, u32[]{:S(2)}, u32[]{:S(2)}) %collective-permute-start.18) | collective-permute-done | bytes 524320 | tf_op jit(solution)/shard_map/ppermute | solution.py:644
  141.3 4.8 %collective-permute-done.15.rest_0_ = bf16[2,256,512]{2,1,0:T(8,128)(2,1)S(1)} collective-permute-done((bf16[2,256,512]{2,1,0:T(8,128)(2,1)S(1)}, bf16[2,256,512]{2,1,0:T(8,128)(2,1)S(1)}, u32[]{:S(2)}, u32[]{:S(2)}) %collective-permute-start.15) | collective-permute-done | bytes 524320 | tf_op jit(solution)/shard_map/ppermute | solution.py:644
  146.1 2.2 %shard_map.64 = bf16[2,256,2048]{2,1,0:T(8,128)(2,1)} custom-call(s32[6]{0:T(128)S(1)} %stack.83.place, bf16[2,256,512]{2,1,0:T(8,128)(2,1)S(1)} %get-tuple-element.37.own, bf16[2,256,512]{2,1,0:T(8,128)(2,1)S(1)} %collective-permute-done.15.rest_0_, bf16[2,256,512]{2,1,0:T(8,128)(2,1)S(1)} %collective-permute-done.16.rest_1_, ...), custom_call_target="tpu_custom_call" | custom-call | tf_op jit(solution)/shard_map/pallas_call | solution.py:646
  (29 shorter events, 7.6 us)
Async XLA Ops:
  0.0 7.8 %copy-start.1 = (bf16[1,256,512]{2,1,0:T(8,128)(2,1)S(1)}, bf16[1,256,512]{2,1,0:T(8,128)(2,1)}, u32[]{:S(2)}) copy-start(bf16[1,256,512]{2,1,0:T(8,128)(2,1)} %param.7) | copy-start | bytes 786436
  2.1 16.9 %copy-start.2 = (s32[16]{0:T(128)S(1)}, s32[16]{0:T(128)}, u32[]{:S(2)}) copy-start(s32[16]{0:T(128)} %param.6) | copy-start | bytes 196
  2.1 38.7 %all-to-all-start = ((bf16[4,4,64,512]{3,2,1,0:T(8,128)(2,1)}), bf16[4,4,64,512]{3,2,1,0:T(8,128)(2,1)S(1)}, u32[]{:S(2)}, u32[]{:S(2)}) async-start(bf16[4,4,64,512]{3,2,1,0:T(8,128)(2,1)} %broadcast_in_dim.4), calls=%async_computation | async-start | bytes 2097152 | tf_op jit(solution)/shard_map/all_to_all | solution.py:519
  7.8 1.6 %copy-start = (bf16[2,1,256,2048]{3,2,1,0:T(8,128)(2,1)S(1)}, bf16[2,1,256,2048]{3,2,1,0:T(8,128)(2,1)}, u32[]{:S(2)}) copy-start(bf16[2,1,256,2048]{3,2,1,0:T(8,128)(2,1)} %param.5) | copy-start | bytes 6291460
  11.7 11.4 %collective-permute-start.1 = (bf16[2,288,512]{2,1,0:T(8,128)(2,1)}, bf16[2,288,512]{2,1,0:T(8,128)(2,1)S(1)}, u32[]{:S(2)}, u32[]{:S(2)}) collective-permute-start(bf16[2,288,512]{2,1,0:T(8,128)(2,1)} %get-tuple-element.24), channel_id=1, source_target_pairs={{0,16},{4,20},{8,0},{12,4},{16,24},{20,28},{24,8},{28,12},{1,17},{... | collective-permute-start | bytes 1769480 | tf_op jit(solution)/shard_map/ppermute | solution.py:517
  12.7 28.2 %collective-permute-start.2 = (bf16[2,288,512]{2,1,0:T(8,128)(2,1)}, bf16[2,288,512]{2,1,0:T(8,128)(2,1)S(1)}, u32[]{:S(2)}, u32[]{:S(2)}) collective-permute-start(bf16[2,288,512]{2,1,0:T(8,128)(2,1)} %get-tuple-element.25), channel_id=1, source_target_pairs={{0,20},{4,16},{8,4},{12,0},{16,28},{20,24},{24,12},{28,8},{1,21},{... | collective-permute-start | bytes 1769480 | tf_op jit(solution)/shard_map/ppermute | solution.py:517
  15.3 25.6 %collective-permute-start.3 = (bf16[2,288,512]{2,1,0:T(8,128)(2,1)}, bf16[2,288,512]{2,1,0:T(8,128)(2,1)S(1)}, u32[]{:S(2)}, u32[]{:S(2)}) collective-permute-start(bf16[2,288,512]{2,1,0:T(8,128)(2,1)} %get-tuple-element.26), channel_id=1, source_target_pairs={{0,4},{4,0},{8,20},{12,16},{16,12},{20,8},{24,28},{28,24},{1,5},{5... | collective-permute-start | bytes 1769480 | tf_op jit(solution)/shard_map/ppermute | solution.py:517
  15.3 25.6 %collective-permute-start = (bf16[2,288,512]{2,1,0:T(8,128)(2,1)S(1)}, bf16[2,288,512]{2,1,0:T(8,128)(2,1)}, u32[]{:S(2)}, u32[]{:S(2)}) collective-permute-start(bf16[2,288,512]{2,1,0:T(8,128)(2,1)S(1)} %get-tuple-element.23.own), channel_id=1, source_target_pairs={{8,16},{12,20},{16,8},{20,12},{9,17},{13,21},{17,9},{21,13},{10,18... | collective-permute-start | bytes 1769480 | tf_op jit(solution)/shard_map/ppermute | solution.py:517
  42.3 18.7 %collective-permute-start.4 = (bf16[256,1024]{1,0:T(8,128)(2,1)S(1)}, bf16[256,1024]{1,0:T(8,128)(2,1)S(1)}, u32[]{:S(2)}, u32[]{:S(2)}) collective-permute-start(bf16[256,1024]{1,0:T(8,128)(2,1)S(1)} %get-tuple-element.27.x_column), channel_id=1, source_target_pairs={{0,4},{4,0},{1,5},{5,1},{2,6},{6,2},{3,7},{7,3},{8,12},{12,8},{9,1... | collective-permute-start | bytes 1572872 | tf_op jit(solution)/shard_map/ppermute | solution.py:541
  43.1 17.9 %collective-permute-start.6 = (bf16[1024,256]{1,0:T(8,128)(2,1)S(1)}, bf16[1024,256]{1,0:T(8,128)(2,1)S(1)}, u32[]{:S(2)}, u32[]{:S(2)}) collective-permute-start(bf16[1024,256]{1,0:T(8,128)(2,1)S(1)} %get-tuple-element.28.y_column), channel_id=1, source_target_pairs={{0,16},{4,20},{8,0},{12,4},{16,24},{20,28},{24,8},{28,12},{1,17},{... | collective-permute-start | bytes 1572872 | tf_op jit(solution)/shard_map/ppermute | solution.py:538
  45.2 15.8 %collective-permute-start.5 = (bf16[1024,256]{1,0:T(8,128)(2,1)S(1)}, bf16[1024,256]{1,0:T(8,128)(2,1)S(1)}, u32[]{:S(2)}, u32[]{:S(2)}) collective-permute-start(bf16[1024,256]{1,0:T(8,128)(2,1)S(1)} %get-tuple-element.28.y_column), channel_id=1, source_target_pairs={{8,16},{12,20},{16,8},{20,12},{9,17},{13,21},{17,9},{21,13},{10,18... | collective-permute-start | bytes 1572872 | tf_op jit(solution)/shard_map/ppermute | solution.py:538
  47.8 13.1 %collective-permute-start.7 = (bf16[4,64,512]{2,1,0:T(8,128)(2,1)S(1)}, bf16[4,64,512]{2,1,0:T(8,128)(2,1)S(1)}, u32[]{:S(2)}, u32[]{:S(2)}) collective-permute-start(bf16[4,64,512]{2,1,0:T(8,128)(2,1)S(1)} %bitcast.31), channel_id=1, source_target_pairs={{0,1},{1,0},{2,3},{3,2},{4,5},{5,4},{6,7},{7,6},{8,9},{9,8},{10,11... | collective-permute-start | bytes 786440 | tf_op jit(solution)/shard_map/ppermute | solution.py:544
  49.7 17.6 %collective-permute-start.12 = (bf16[4,64,512]{2,1,0:T(8,128)(2,1)S(1)}, bf16[4,64,512]{2,1,0:T(8,128)(2,1)S(1)}, u32[]{:S(2)}, u32[]{:S(2)}) collective-permute-start(bf16[4,64,512]{2,1,0:T(8,128)(2,1)S(1)} %bitcast.32), channel_id=1, source_target_pairs={{0,2},{1,3},{2,0},{3,1},{4,6},{5,7},{6,4},{7,5},{8,10},{9,11},{10,... | collective-permute-start | bytes 786440 | tf_op jit(solution)/shard_map/ppermute | solution.py:544
  61.8 29.4 %collective-permute-start.9 = (bf16[2,256,1024]{2,1,0:T(8,128)(2,1)S(1)}, bf16[2,256,1024]{2,1,0:T(8,128)(2,1)S(1)}, u32[]{:S(2)}, u32[]{:S(2)}) collective-permute-start(bf16[2,256,1024]{2,1,0:T(8,128)(2,1)S(1)} %get-tuple-element.30.xb), channel_id=1, source_target_pairs={{0,16},{4,20},{8,0},{12,4},{16,24},{20,28},{24,8},{28,12},{1,17},{... | collective-permute-start | bytes 3145736 | tf_op jit(solution)/shard_map/ppermute | solution.py:538
  61.8 29.4 %collective-permute-start.8 = (bf16[2,256,1024]{2,1,0:T(8,128)(2,1)S(1)}, bf16[2,256,1024]{2,1,0:T(8,128)(2,1)S(1)}, u32[]{:S(2)}, u32[]{:S(2)}) collective-permute-start(bf16[2,256,1024]{2,1,0:T(8,128)(2,1)S(1)} %get-tuple-element.30.xb), channel_id=1, source_target_pairs={{8,16},{12,20},{16,8},{20,12},{9,17},{13,21},{17,9},{21,13},{10,18... | collective-permute-start | bytes 3145736 | tf_op jit(solution)/shard_map/ppermute | solution.py:538
  63.7 14.0 %collective-permute-start.11 = (bf16[4,64,512]{2,1,0:T(8,128)(2,1)S(1)}, bf16[4,64,512]{2,1,0:T(8,128)(2,1)S(1)}, u32[]{:S(2)}, u32[]{:S(2)}) collective-permute-start(bf16[4,64,512]{2,1,0:T(8,128)(2,1)S(1)} %get-tuple-element.32), channel_id=1, source_target_pairs={{0,2},{1,3},{2,0},{3,1},{4,6},{5,7},{6,4},{7,5},{8,10},{9,11},{10,... | collective-permute-start | bytes 786440 | tf_op jit(solution)/shard_map/ppermute | solution.py:544
  66.2 25.0 %collective-permute-start.10 = (bf16[2,1024,256]{2,1,0:T(8,128)(2,1)S(1)}, bf16[2,1024,256]{2,1,0:T(8,128)(2,1)S(1)}, u32[]{:S(2)}, u32[]{:S(2)}) collective-permute-start(bf16[2,1024,256]{2,1,0:T(8,128)(2,1)S(1)} %get-tuple-element.31.yb), channel_id=1, source_target_pairs={{0,4},{4,0},{1,5},{5,1},{2,6},{6,2},{3,7},{7,3},{8,12},{12,8},{9,1... | collective-permute-start | bytes 3145736 | tf_op jit(solution)/shard_map/ppermute | solution.py:541
  91.8 9.4 %collective-permute-start.13 = (bf16[2,512,512]{2,1,0:T(8,128)(2,1)S(1)}, bf16[2,512,512]{2,1,0:T(8,128)(2,1)S(1)}, u32[]{:S(2)}, u32[]{:S(2)}) collective-permute-start(bf16[2,512,512]{2,1,0:T(8,128)(2,1)S(1)} %get-tuple-element.34.w_high), channel_id=1, source_target_pairs={{0,8},{16,24},{1,9},{17,25},{2,10},{18,26},{3,11},{19,27},{4,12},{... | collective-permute-start | bytes 3145736 | tf_op jit(solution)/shard_map/ppermute | solution.py:619
  110.3 3.6 %collective-permute-start.14 = (bf16[2,512,512]{2,1,0:T(8,128)(2,1)S(1)}, bf16[2,512,512]{2,1,0:T(8,128)(2,1)S(1)}, u32[]{:S(2)}, u32[]{:S(2)}) collective-permute-start(bf16[2,512,512]{2,1,0:T(8,128)(2,1)S(1)} %get-tuple-element.35), channel_id=1, source_target_pairs={{8,0},{24,16},{9,1},{25,17},{10,2},{26,18},{11,3},{27,19},{12,4},{... | collective-permute-start | bytes 3145736 | tf_op jit(solution)/shard_map/ppermute | solution.py:631
  114.7 10.6 %collective-permute-start.16 = (bf16[2,256,512]{2,1,0:T(8,128)(2,1)S(1)}, bf16[2,256,512]{2,1,0:T(8,128)(2,1)S(1)}, u32[]{:S(2)}, u32[]{:S(2)}) collective-permute-start(bf16[2,256,512]{2,1,0:T(8,128)(2,1)S(1)} %get-tuple-element.38), channel_id=1, source_target_pairs={{16,0},{20,4},{0,8},{4,12},{24,16},{28,20},{8,24},{12,28},{17,1},{... | collective-permute-start | bytes 1572872 | tf_op jit(solution)/shard_map/ppermute | solution.py:644
  114.8 14.2 %collective-permute-start.17 = (bf16[2,256,512]{2,1,0:T(8,128)(2,1)S(1)}, bf16[2,256,512]{2,1,0:T(8,128)(2,1)S(1)}, u32[]{:S(2)}, u32[]{:S(2)}) collective-permute-start(bf16[2,256,512]{2,1,0:T(8,128)(2,1)S(1)} %get-tuple-element.39), channel_id=1, source_target_pairs={{20,0},{16,4},{4,8},{0,12},{28,16},{24,20},{12,24},{8,28},{21,1},{... | collective-permute-start | bytes 1572872 | tf_op jit(solution)/shard_map/ppermute | solution.py:644
  120.3 21.1 %collective-permute-start.18 = (bf16[2,256,512]{2,1,0:T(8,128)(2,1)S(1)}, bf16[2,256,512]{2,1,0:T(8,128)(2,1)S(1)}, u32[]{:S(2)}, u32[]{:S(2)}) collective-permute-start(bf16[2,256,512]{2,1,0:T(8,128)(2,1)S(1)} %get-tuple-element.40), channel_id=1, source_target_pairs={{4,0},{0,4},{20,8},{16,12},{12,16},{8,20},{28,24},{24,28},{5,1},{1... | collective-permute-start | bytes 1572872 | tf_op jit(solution)/shard_map/ppermute | solution.py:644
  123.4 22.8 %collective-permute-start.15 = (bf16[2,256,512]{2,1,0:T(8,128)(2,1)S(1)}, bf16[2,256,512]{2,1,0:T(8,128)(2,1)S(1)}, u32[]{:S(2)}, u32[]{:S(2)}) collective-permute-start(bf16[2,256,512]{2,1,0:T(8,128)(2,1)S(1)} %get-tuple-element.37.own), channel_id=1, source_target_pairs={{16,8},{20,12},{8,16},{12,20},{17,9},{21,13},{9,17},{13,21},{18,10... | collective-permute-start | bytes 1572872 | tf_op jit(solution)/shard_map/ppermute | solution.py:644

commit v22 on v21

--- a/solution.py
+++ b/solution.py
@@ -579,7 +579,7 @@
         scratch_shapes=weight_sems,
         compiler_params=params,
         cost_estimate=pl.CostEstimate(
-            flops=3 * 10**10, bytes_accessed=2**21, transcendentals=0
+            flops=10**10, bytes_accessed=2**21, transcendentals=0
         ),
     )(info, rows_held, rows_next, rows_far)
     weights = pl.pallas_call(

time: 149 us -> 145 us (0.973)
  waiting for transfers between devices: 78.2 us -> 72.4 us
  starting transfers between devices: 40.8 us -> 42.5 us
    ppermute x2, waiting for transfers between devices: 12.4 us -> 6.6 us  [aside(): return lax.ppermute(block, 'px', [(y, (y + 1) % 2) for y in range(2)])]
  transfers between devices with their start and end apart: 20 -> 20, of which waited for: 10 -> 11; matrix products, arithmetic and copies ran while one was open for 1% -> 1% of each run, Pallas kernels for 5% -> 5%
where the time goes in v22:
time: 145 us; the launch traced here: 144 us
  waiting for transfers between devices  72.4 us (50%)
  starting transfers between devices  42.5 us (29%)
  Pallas kernels  21.8 us (15%)
  local copies, waits for them, and re-layouts  3.47 us (2%)
  between operations  3.13 us (2%)
    ppermute x4, waiting for transfers between devices, on_device(): lax.ppermute(piece, ('sec', 'px'), back_pairs(a, b))  19.5 us
    ppermute x4, waiting for transfers between devices, on_device(): lax.ppermute(piece, ('sec', 'px'), pairs(a, b))  18.4 us
    ppermute x3, waiting for transfers between devices, over_z(): return lax.ppermute(block, 'py', [(z, z ^ bit) for z in range(py_count)])  17.3 us
    ppermute x4, starting transfers between devices, on_device(): lax.ppermute(piece, ('sec', 'px'), back_pairs(a, b))  11.9 us
    pallas_call x1, Pallas kernels, on_device(): pl.pallas_call(last_kernel, out_shape=[double_shape, full_shape], in_spec...  9.12 us
    ppermute x1, waiting for transfers between devices, on_device(): incoming = lax.ppermute(w_high, 'sec', up)  7.32 us
    ppermute x4, starting transfers between devices, on_device(): lax.ppermute(piece, ('sec', 'px'), pairs(a, b))  7.17 us
    ppermute x4, starting transfers between devices, across(): return lax.ppermute(block, ('sec', 'px'), pairs(a, 0))  6.76 us
  transfers between devices with their start and end apart: 20, of which 11 were waited for; matrix products, arithmetic and copies ran while one was open for 1% of the time, Pallas kernels for 5%

profile of v22, /device:TPU:1, one launch (start us, length us, event | category | flops | bytes accessed | tf_op | source)
XLA Modules:
  0.0 144.3 jit_solution(12517475096126008247)
XLA Ops:
  1.0 1.1 broadcast_in_dim.4
  2.1 5.6 %all-to-all-start = ((bf16[4,4,64,512]{3,2,1,0:T(8,128)(2,1)}), bf16[4,4,64,512]{3,2,1,0:T(8,128)(2,1)S(1)}, u32[]{:S(2)}, u32[]{:S(2)}) async-start(bf16[4,4,64,512]{3,2,1,0:T(8,128)(2,1)} %broadcast_in_dim.4), calls=%async_computation | async-start | bytes 2097152 | tf_op jit(solution)/shard_map/all_to_all | solution.py:519
  7.8 1.6 %copy-done = bf16[2,1,256,2048]{3,2,1,0:T(8,128)(2,1)S(1)} copy-done((bf16[2,1,256,2048]{3,2,1,0:T(8,128)(2,1)S(1)}, bf16[2,1,256,2048]{3,2,1,0:T(8,128)(2,1)}, u32[]{:S(2)}) %copy-start) | copy-done | bytes 2097176
  9.4 2.3 %shard_map.55 = (bf16[2,288,512]{2,1,0:T(8,128)(2,1)S(1)}, bf16[2,288,512]{2,1,0:T(8,128)(2,1)}, bf16[2,288,512]{2,1,0:T(8,128)(2,1)}, bf16[2,288,512]{2,1,0:T(8,128)(2,1)}) custom-call(s32[6]{0:T(128)S(1)} %stack.83.place, bf16[2,256,2048]{2,1,0:T(8,128)(2,1)S(1)} %bitcast.29, bf16[8,32,512]{2,1,0:T(8,128)(2,1)S(1)} %bitcast.30), custom_call_target="tpu_custom_call" | custom-call | tf_op jit(solution)/shard_map/pallas_call | solution.py:508
  12.7 2.6 %collective-permute-start.2 = (bf16[2,288,512]{2,1,0:T(8,128)(2,1)}, bf16[2,288,512]{2,1,0:T(8,128)(2,1)S(1)}, u32[]{:S(2)}, u32[]{:S(2)}) collective-permute-start(bf16[2,288,512]{2,1,0:T(8,128)(2,1)} %get-tuple-element.25), channel_id=1, source_target_pairs={{0,20},{4,16},{8,4},{12,0},{16,28},{20,24},{24,12},{28,8},{1,21},{... | collective-permute-start | bytes 1769480 | tf_op jit(solution)/shard_map/ppermute | solution.py:517
  15.3 3.6 %collective-permute-start = (bf16[2,288,512]{2,1,0:T(8,128)(2,1)S(1)}, bf16[2,288,512]{2,1,0:T(8,128)(2,1)}, u32[]{:S(2)}, u32[]{:S(2)}) collective-permute-start(bf16[2,288,512]{2,1,0:T(8,128)(2,1)S(1)} %get-tuple-element.23.own), channel_id=1, source_target_pairs={{8,16},{12,20},{16,8},{20,12},{9,17},{13,21},{17,9},{21,13},{10,18... | collective-permute-start | bytes 1769480 | tf_op jit(solution)/shard_map/ppermute | solution.py:517
  23.1 17.7 %collective-permute-done.2.p2 = bf16[2,288,512]{2,1,0:T(8,128)(2,1)S(1)} collective-permute-done((bf16[2,288,512]{2,1,0:T(8,128)(2,1)}, bf16[2,288,512]{2,1,0:T(8,128)(2,1)S(1)}, u32[]{:S(2)}, u32[]{:S(2)}) %collective-permute-start.2) | collective-permute-done | bytes 589856 | tf_op jit(solution)/shard_map/ppermute | solution.py:517
  40.8 1.4 shard_map.56
  43.1 2.1 %collective-permute-start.6 = (bf16[1024,256]{1,0:T(8,128)(2,1)S(1)}, bf16[1024,256]{1,0:T(8,128)(2,1)S(1)}, u32[]{:S(2)}, u32[]{:S(2)}) collective-permute-start(bf16[1024,256]{1,0:T(8,128)(2,1)S(1)} %get-tuple-element.28.y_column), channel_id=1, source_target_pairs={{0,16},{4,20},{8,0},{12,4},{16,24},{20,28},{24,8},{28,12},{1,17},{... | collective-permute-start | bytes 1572872 | tf_op jit(solution)/shard_map/ppermute | solution.py:538
  45.2 2.6 %collective-permute-start.5 = (bf16[1024,256]{1,0:T(8,128)(2,1)S(1)}, bf16[1024,256]{1,0:T(8,128)(2,1)S(1)}, u32[]{:S(2)}, u32[]{:S(2)}) collective-permute-start(bf16[1024,256]{1,0:T(8,128)(2,1)S(1)} %get-tuple-element.28.y_column), channel_id=1, source_target_pairs={{8,16},{12,20},{16,8},{20,12},{9,17},{13,21},{17,9},{21,13},{10,18... | collective-permute-start | bytes 1572872 | tf_op jit(solution)/shard_map/ppermute | solution.py:538
  47.8 1.8 %collective-permute-start.7 = (bf16[4,64,512]{2,1,0:T(8,128)(2,1)S(1)}, bf16[4,64,512]{2,1,0:T(8,128)(2,1)S(1)}, u32[]{:S(2)}, u32[]{:S(2)}) collective-permute-start(bf16[4,64,512]{2,1,0:T(8,128)(2,1)S(1)} %bitcast.31), channel_id=1, source_target_pairs={{0,1},{1,0},{2,3},{3,2},{4,5},{5,4},{6,7},{7,6},{8,9},{9,8},{10,11... | collective-permute-start | bytes 786440 | tf_op jit(solution)/shard_map/ppermute | solution.py:544
  49.7 2.1 %collective-permute-start.12 = (bf16[4,64,512]{2,1,0:T(8,128)(2,1)S(1)}, bf16[4,64,512]{2,1,0:T(8,128)(2,1)S(1)}, u32[]{:S(2)}, u32[]{:S(2)}) collective-permute-start(bf16[4,64,512]{2,1,0:T(8,128)(2,1)S(1)} %bitcast.32), channel_id=1, source_target_pairs={{0,2},{1,3},{2,0},{3,1},{4,6},{5,7},{6,4},{7,5},{8,10},{9,11},{10,... | collective-permute-start | bytes 786440 | tf_op jit(solution)/shard_map/ppermute | solution.py:544
  51.7 1.6 %shard_map.57.rhs = bf16[2,2,512,512]{3,2,1,0:T(8,128)(2,1)S(1)} custom-call(s32[21]{0:T(128)S(1)} %stack.98.info, bf16[2,288,512]{2,1,0:T(8,128)(2,1)S(1)} %get-tuple-element.23.own, bf16[2,288,512]{2,1,0:T(8,128)(2,1)} %collective-permute-done.p0, bf16[2,288,512]{2,1,0:T(8,128)(2,1)S(1)} %collective-permute-done.1.p1, ...), custom_call_target="tpu_custom_call" | custom-call | tf_op jit(solution)/shard_map/pallas_call | solution.py:552
  53.4 7.6 %collective-permute-done.7.rows_next.c1 = bf16[4,64,512]{2,1,0:T(8,128)(2,1)S(1)} collective-permute-done((bf16[4,64,512]{2,1,0:T(8,128)(2,1)S(1)}, bf16[4,64,512]{2,1,0:T(8,128)(2,1)S(1)}, u32[]{:S(2)}, u32[]{:S(2)}) %collective-permute-start.7) | collective-permute-done | bytes 262176 | tf_op jit(solution)/shard_map/ppermute | solution.py:544
  61.8 1.1 collective-permute-start.10
  63.0 1.9 %collective-permute-start.8 = (bf16[2,256,1024]{2,1,0:T(8,128)(2,1)S(1)}, bf16[2,256,1024]{2,1,0:T(8,128)(2,1)S(1)}, u32[]{:S(2)}, u32[]{:S(2)}) collective-permute-start(bf16[2,256,1024]{2,1,0:T(8,128)(2,1)S(1)} %get-tuple-element.30.xb), channel_id=1, source_target_pairs={{8,16},{12,20},{16,8},{20,12},{9,17},{13,21},{17,9},{21,13},{10,18... | collective-permute-start | bytes 3145736 | tf_op jit(solution)/shard_map/ppermute | solution.py:538
  64.9 2.6 %collective-permute-start.11 = (bf16[4,64,512]{2,1,0:T(8,128)(2,1)S(1)}, bf16[4,64,512]{2,1,0:T(8,128)(2,1)S(1)}, u32[]{:S(2)}, u32[]{:S(2)}) collective-permute-start(bf16[4,64,512]{2,1,0:T(8,128)(2,1)S(1)} %get-tuple-element.32), channel_id=1, source_target_pairs={{0,2},{1,3},{2,0},{3,1},{4,6},{5,7},{6,4},{7,5},{8,10},{9,11},{10,... | collective-permute-start | bytes 786440 | tf_op jit(solution)/shard_map/ppermute | solution.py:544
  67.5 1.9 %shard_map.59.begun = bf16[2,512,512]{2,1,0:T(8,128)(2,1)S(1)} custom-call(s32[21]{0:T(128)S(1)} %stack.98.info, bf16[4,64,512]{2,1,0:T(8,128)(2,1)S(1)} %bitcast.33, bf16[4,64,512]{2,1,0:T(8,128)(2,1)S(1)} %collective-permute-done.7.rows_next.c1, bf16[4,64,512]{2,1,0:T(8,128)(2,1)S(1)} %collective-permute-done.12.c2), custom_call_target="tpu_custom_call" | custom-call | flops 10000000000 | bytes 2097152 | tf_op jit(solution)/shard_map/pallas_call | solution.py:574
  69.4 9.7 %collective-permute-done.11.c3 = bf16[4,64,512]{2,1,0:T(8,128)(2,1)S(1)} collective-permute-done((bf16[4,64,512]{2,1,0:T(8,128)(2,1)S(1)}, bf16[4,64,512]{2,1,0:T(8,128)(2,1)S(1)}, u32[]{:S(2)}, u32[]{:S(2)}) %collective-permute-start.11) | collective-permute-done | bytes 262176 | tf_op jit(solution)/shard_map/ppermute | solution.py:544
  80.2 6.6 %collective-permute-done.10.yf = bf16[2,1024,256]{2,1,0:T(8,128)(2,1)S(1)} collective-permute-done((bf16[2,1024,256]{2,1,0:T(8,128)(2,1)S(1)}, bf16[2,1024,256]{2,1,0:T(8,128)(2,1)S(1)}, u32[]{:S(2)}, u32[]{:S(2)}) %collective-permute-start.10) | collective-permute-done | bytes 1048608 | tf_op jit(solution)/shard_map/ppermute | solution.py:541
  88.4 1.3 collective-permute-start.13
  89.7 7.3 %collective-permute-done.13.arrived = bf16[2,512,512]{2,1,0:T(8,128)(2,1)S(1)} collective-permute-done((bf16[2,512,512]{2,1,0:T(8,128)(2,1)S(1)}, bf16[2,512,512]{2,1,0:T(8,128)(2,1)S(1)}, u32[]{:S(2)}, u32[]{:S(2)}) %collective-permute-start.13) | collective-permute-done | bytes 1048608 | tf_op jit(solution)/shard_map/ppermute | solution.py:619
  97.0 9.1 %shard_map.62 = (bf16[2,2,512,512]{3,2,1,0:T(8,128)(2,1)S(1)}, bf16[2,512,512]{2,1,0:T(8,128)(2,1)S(1)}) custom-call(s32[21]{0:T(128)S(1)} %stack.98.info, bf16[2,256,1024]{2,1,0:T(8,128)(2,1)S(1)} %get-tuple-element.30.xb, bf16[2,256,1024]{2,1,0:T(8,128)(2,1)S(1)} %collective-permute-done.8.x0, bf16[2,256,1024]{2,1,0:T(8,128)(2,1)S(1)} %collective-permute-done.9.x1, ...), custom_call_target="tpu_custom_call" | custom-call | flops 6442450944 | bytes 8388608 | tf_op jit(solution)/shard_map/pallas_call | solution.py:620
  106.1 1.4 collective-permute-start.14
  107.5 2.2 %collective-permute-done.14.arrived = bf16[2,512,512]{2,1,0:T(8,128)(2,1)S(1)} collective-permute-done((bf16[2,512,512]{2,1,0:T(8,128)(2,1)S(1)}, bf16[2,512,512]{2,1,0:T(8,128)(2,1)S(1)}, u32[]{:S(2)}, u32[]{:S(2)}) %collective-permute-start.14) | collective-permute-done | bytes 1048608 | tf_op jit(solution)/shard_map/ppermute | solution.py:631
  110.5 1.4 collective-permute-start.16
  111.9 6.4 %collective-permute-start.17 = (bf16[2,256,512]{2,1,0:T(8,128)(2,1)S(1)}, bf16[2,256,512]{2,1,0:T(8,128)(2,1)S(1)}, u32[]{:S(2)}, u32[]{:S(2)}) collective-permute-start(bf16[2,256,512]{2,1,0:T(8,128)(2,1)S(1)} %get-tuple-element.39), channel_id=1, source_target_pairs={{20,0},{16,4},{4,8},{0,12},{28,16},{24,20},{12,24},{8,28},{21,1},{... | collective-permute-start | bytes 1572872 | tf_op jit(solution)/shard_map/ppermute | solution.py:644
  119.2 3.3 %collective-permute-start.15 = (bf16[2,256,512]{2,1,0:T(8,128)(2,1)S(1)}, bf16[2,256,512]{2,1,0:T(8,128)(2,1)S(1)}, u32[]{:S(2)}, u32[]{:S(2)}) collective-permute-start(bf16[2,256,512]{2,1,0:T(8,128)(2,1)S(1)} %get-tuple-element.37.own), channel_id=1, source_target_pairs={{16,8},{20,12},{8,16},{12,20},{17,9},{21,13},{9,17},{13,21},{18,10... | collective-permute-start | bytes 1572872 | tf_op jit(solution)/shard_map/ppermute | solution.py:644
  122.5 2.2 %collective-permute-done.17.rest_2_ = bf16[2,256,512]{2,1,0:T(8,128)(2,1)S(1)} collective-permute-done((bf16[2,256,512]{2,1,0:T(8,128)(2,1)S(1)}, bf16[2,256,512]{2,1,0:T(8,128)(2,1)S(1)}, u32[]{:S(2)}, u32[]{:S(2)}) %collective-permute-start.17) | collective-permute-done | bytes 524320 | tf_op jit(solution)/shard_map/ppermute | solution.py:644
  124.7 12.4 %collective-permute-done.18.rest_3_ = bf16[2,256,512]{2,1,0:T(8,128)(2,1)S(1)} collective-permute-done((bf16[2,256,512]{2,1,0:T(8,128)(2,1)S(1)}, bf16[2,256,512]{2,1,0:T(8,128)(2,1)S(1)}, u32[]{:S(2)}, u32[]{:S(2)}) %collective-permute-start.18) | collective-permute-done | bytes 524320 | tf_op jit(solution)/shard_map/ppermute | solution.py:644
  137.2 4.8 %collective-permute-done.15.rest_0_ = bf16[2,256,512]{2,1,0:T(8,128)(2,1)S(1)} collective-permute-done((bf16[2,256,512]{2,1,0:T(8,128)(2,1)S(1)}, bf16[2,256,512]{2,1,0:T(8,128)(2,1)S(1)}, u32[]{:S(2)}, u32[]{:S(2)}) %collective-permute-start.15) | collective-permute-done | bytes 524320 | tf_op jit(solution)/shard_map/ppermute | solution.py:644
  142.0 2.2 %shard_map.64 = bf16[2,256,2048]{2,1,0:T(8,128)(2,1)} custom-call(s32[6]{0:T(128)S(1)} %stack.83.place, bf16[2,256,512]{2,1,0:T(8,128)(2,1)S(1)} %get-tuple-element.37.own, bf16[2,256,512]{2,1,0:T(8,128)(2,1)S(1)} %collective-permute-done.15.rest_0_, bf16[2,256,512]{2,1,0:T(8,128)(2,1)S(1)} %collective-permute-done.16.rest_1_, ...), custom_call_target="tpu_custom_call" | custom-call | tf_op jit(solution)/shard_map/pallas_call | solution.py:646
  (29 shorter events, 9.6 us)
Async XLA Ops:
  0.0 7.8 %copy-start.1 = (bf16[1,256,512]{2,1,0:T(8,128)(2,1)S(1)}, bf16[1,256,512]{2,1,0:T(8,128)(2,1)}, u32[]{:S(2)}) copy-start(bf16[1,256,512]{2,1,0:T(8,128)(2,1)} %param.7) | copy-start | bytes 786436
  2.1 16.9 %copy-start.2 = (s32[16]{0:T(128)S(1)}, s32[16]{0:T(128)}, u32[]{:S(2)}) copy-start(s32[16]{0:T(128)} %param.6) | copy-start | bytes 196
  2.1 38.7 %all-to-all-start = ((bf16[4,4,64,512]{3,2,1,0:T(8,128)(2,1)}), bf16[4,4,64,512]{3,2,1,0:T(8,128)(2,1)S(1)}, u32[]{:S(2)}, u32[]{:S(2)}) async-start(bf16[4,4,64,512]{3,2,1,0:T(8,128)(2,1)} %broadcast_in_dim.4), calls=%async_computation | async-start | bytes 2097152 | tf_op jit(solution)/shard_map/all_to_all | solution.py:519
  7.8 1.6 %copy-start = (bf16[2,1,256,2048]{3,2,1,0:T(8,128)(2,1)S(1)}, bf16[2,1,256,2048]{3,2,1,0:T(8,128)(2,1)}, u32[]{:S(2)}) copy-start(bf16[2,1,256,2048]{3,2,1,0:T(8,128)(2,1)} %param.5) | copy-start | bytes 6291460
  11.7 11.4 %collective-permute-start.1 = (bf16[2,288,512]{2,1,0:T(8,128)(2,1)}, bf16[2,288,512]{2,1,0:T(8,128)(2,1)S(1)}, u32[]{:S(2)}, u32[]{:S(2)}) collective-permute-start(bf16[2,288,512]{2,1,0:T(8,128)(2,1)} %get-tuple-element.24), channel_id=1, source_target_pairs={{0,16},{4,20},{8,0},{12,4},{16,24},{20,28},{24,8},{28,12},{1,17},{... | collective-permute-start | bytes 1769480 | tf_op jit(solution)/shard_map/ppermute | solution.py:517
  12.7 28.2 %collective-permute-start.2 = (bf16[2,288,512]{2,1,0:T(8,128)(2,1)}, bf16[2,288,512]{2,1,0:T(8,128)(2,1)S(1)}, u32[]{:S(2)}, u32[]{:S(2)}) collective-permute-start(bf16[2,288,512]{2,1,0:T(8,128)(2,1)} %get-tuple-element.25), channel_id=1, source_target_pairs={{0,20},{4,16},{8,4},{12,0},{16,28},{20,24},{24,12},{28,8},{1,21},{... | collective-permute-start | bytes 1769480 | tf_op jit(solution)/shard_map/ppermute | solution.py:517
  15.3 25.6 %collective-permute-start.3 = (bf16[2,288,512]{2,1,0:T(8,128)(2,1)}, bf16[2,288,512]{2,1,0:T(8,128)(2,1)S(1)}, u32[]{:S(2)}, u32[]{:S(2)}) collective-permute-start(bf16[2,288,512]{2,1,0:T(8,128)(2,1)} %get-tuple-element.26), channel_id=1, source_target_pairs={{0,4},{4,0},{8,20},{12,16},{16,12},{20,8},{24,28},{28,24},{1,5},{5... | collective-permute-start | bytes 1769480 | tf_op jit(solution)/shard_map/ppermute | solution.py:517
  15.3 25.6 %collective-permute-start = (bf16[2,288,512]{2,1,0:T(8,128)(2,1)S(1)}, bf16[2,288,512]{2,1,0:T(8,128)(2,1)}, u32[]{:S(2)}, u32[]{:S(2)}) collective-permute-start(bf16[2,288,512]{2,1,0:T(8,128)(2,1)S(1)} %get-tuple-element.23.own), channel_id=1, source_target_pairs={{8,16},{12,20},{16,8},{20,12},{9,17},{13,21},{17,9},{21,13},{10,18... | collective-permute-start | bytes 1769480 | tf_op jit(solution)/shard_map/ppermute | solution.py:517
  42.3 18.7 %collective-permute-start.4 = (bf16[256,1024]{1,0:T(8,128)(2,1)S(1)}, bf16[256,1024]{1,0:T(8,128)(2,1)S(1)}, u32[]{:S(2)}, u32[]{:S(2)}) collective-permute-start(bf16[256,1024]{1,0:T(8,128)(2,1)S(1)} %get-tuple-element.27.x_column), channel_id=1, source_target_pairs={{0,4},{4,0},{1,5},{5,1},{2,6},{6,2},{3,7},{7,3},{8,12},{12,8},{9,1... | collective-permute-start | bytes 1572872 | tf_op jit(solution)/shard_map/ppermute | solution.py:541
  43.1 17.9 %collective-permute-start.6 = (bf16[1024,256]{1,0:T(8,128)(2,1)S(1)}, bf16[1024,256]{1,0:T(8,128)(2,1)S(1)}, u32[]{:S(2)}, u32[]{:S(2)}) collective-permute-start(bf16[1024,256]{1,0:T(8,128)(2,1)S(1)} %get-tuple-element.28.y_column), channel_id=1, source_target_pairs={{0,16},{4,20},{8,0},{12,4},{16,24},{20,28},{24,8},{28,12},{1,17},{... | collective-permute-start | bytes 1572872 | tf_op jit(solution)/shard_map/ppermute | solution.py:538
  45.2 15.8 %collective-permute-start.5 = (bf16[1024,256]{1,0:T(8,128)(2,1)S(1)}, bf16[1024,256]{1,0:T(8,128)(2,1)S(1)}, u32[]{:S(2)}, u32[]{:S(2)}) collective-permute-start(bf16[1024,256]{1,0:T(8,128)(2,1)S(1)} %get-tuple-element.28.y_column), channel_id=1, source_target_pairs={{8,16},{12,20},{16,8},{20,12},{9,17},{13,21},{17,9},{21,13},{10,18... | collective-permute-start | bytes 1572872 | tf_op jit(solution)/shard_map/ppermute | solution.py:538
  47.8 13.1 %collective-permute-start.7 = (bf16[4,64,512]{2,1,0:T(8,128)(2,1)S(1)}, bf16[4,64,512]{2,1,0:T(8,128)(2,1)S(1)}, u32[]{:S(2)}, u32[]{:S(2)}) collective-permute-start(bf16[4,64,512]{2,1,0:T(8,128)(2,1)S(1)} %bitcast.31), channel_id=1, source_target_pairs={{0,1},{1,0},{2,3},{3,2},{4,5},{5,4},{6,7},{7,6},{8,9},{9,8},{10,11... | collective-permute-start | bytes 786440 | tf_op jit(solution)/shard_map/ppermute | solution.py:544
  49.7 17.9 %collective-permute-start.12 = (bf16[4,64,512]{2,1,0:T(8,128)(2,1)S(1)}, bf16[4,64,512]{2,1,0:T(8,128)(2,1)S(1)}, u32[]{:S(2)}, u32[]{:S(2)}) collective-permute-start(bf16[4,64,512]{2,1,0:T(8,128)(2,1)S(1)} %bitcast.32), channel_id=1, source_target_pairs={{0,2},{1,3},{2,0},{3,1},{4,6},{5,7},{6,4},{7,5},{8,10},{9,11},{10,... | collective-permute-start | bytes 786440 | tf_op jit(solution)/shard_map/ppermute | solution.py:544
  61.8 25.0 %collective-permute-start.10 = (bf16[2,1024,256]{2,1,0:T(8,128)(2,1)S(1)}, bf16[2,1024,256]{2,1,0:T(8,128)(2,1)S(1)}, u32[]{:S(2)}, u32[]{:S(2)}) collective-permute-start(bf16[2,1024,256]{2,1,0:T(8,128)(2,1)S(1)} %get-tuple-element.31.yb), channel_id=1, source_target_pairs={{0,4},{4,0},{1,5},{5,1},{2,6},{6,2},{3,7},{7,3},{8,12},{12,8},{9,1... | collective-permute-start | bytes 3145736 | tf_op jit(solution)/shard_map/ppermute | solution.py:541
  62.9 23.9 %collective-permute-start.9 = (bf16[2,256,1024]{2,1,0:T(8,128)(2,1)S(1)}, bf16[2,256,1024]{2,1,0:T(8,128)(2,1)S(1)}, u32[]{:S(2)}, u32[]{:S(2)}) collective-permute-start(bf16[2,256,1024]{2,1,0:T(8,128)(2,1)S(1)} %get-tuple-element.30.xb), channel_id=1, source_target_pairs={{0,16},{4,20},{8,0},{12,4},{16,24},{20,28},{24,8},{28,12},{1,17},{... | collective-permute-start | bytes 3145736 | tf_op jit(solution)/shard_map/ppermute | solution.py:538
  63.0 24.8 %collective-permute-start.8 = (bf16[2,256,1024]{2,1,0:T(8,128)(2,1)S(1)}, bf16[2,256,1024]{2,1,0:T(8,128)(2,1)S(1)}, u32[]{:S(2)}, u32[]{:S(2)}) collective-permute-start(bf16[2,256,1024]{2,1,0:T(8,128)(2,1)S(1)} %get-tuple-element.30.xb), channel_id=1, source_target_pairs={{8,16},{12,20},{16,8},{20,12},{9,17},{13,21},{17,9},{21,13},{10,18... | collective-permute-start | bytes 3145736 | tf_op jit(solution)/shard_map/ppermute | solution.py:538
  64.9 14.2 %collective-permute-start.11 = (bf16[4,64,512]{2,1,0:T(8,128)(2,1)S(1)}, bf16[4,64,512]{2,1,0:T(8,128)(2,1)S(1)}, u32[]{:S(2)}, u32[]{:S(2)}) collective-permute-start(bf16[4,64,512]{2,1,0:T(8,128)(2,1)S(1)} %get-tuple-element.32), channel_id=1, source_target_pairs={{0,2},{1,3},{2,0},{3,1},{4,6},{5,7},{6,4},{7,5},{8,10},{9,11},{10,... | collective-permute-start | bytes 786440 | tf_op jit(solution)/shard_map/ppermute | solution.py:544
  88.4 8.6 %collective-permute-start.13 = (bf16[2,512,512]{2,1,0:T(8,128)(2,1)S(1)}, bf16[2,512,512]{2,1,0:T(8,128)(2,1)S(1)}, u32[]{:S(2)}, u32[]{:S(2)}) collective-permute-start(bf16[2,512,512]{2,1,0:T(8,128)(2,1)S(1)} %get-tuple-element.34.w_high), channel_id=1, source_target_pairs={{0,8},{16,24},{1,9},{17,25},{2,10},{18,26},{3,11},{19,27},{4,12},{... | collective-permute-start | bytes 3145736 | tf_op jit(solution)/shard_map/ppermute | solution.py:619
  106.1 3.6 %collective-permute-start.14 = (bf16[2,512,512]{2,1,0:T(8,128)(2,1)S(1)}, bf16[2,512,512]{2,1,0:T(8,128)(2,1)S(1)}, u32[]{:S(2)}, u32[]{:S(2)}) collective-permute-start(bf16[2,512,512]{2,1,0:T(8,128)(2,1)S(1)} %get-tuple-element.35), channel_id=1, source_target_pairs={{8,0},{24,16},{9,1},{25,17},{10,2},{26,18},{11,3},{27,19},{12,4},{... | collective-permute-start | bytes 3145736 | tf_op jit(solution)/shard_map/ppermute | solution.py:631
  110.5 11.9 %collective-permute-start.16 = (bf16[2,256,512]{2,1,0:T(8,128)(2,1)S(1)}, bf16[2,256,512]{2,1,0:T(8,128)(2,1)S(1)}, u32[]{:S(2)}, u32[]{:S(2)}) collective-permute-start(bf16[2,256,512]{2,1,0:T(8,128)(2,1)S(1)} %get-tuple-element.38), channel_id=1, source_target_pairs={{16,0},{20,4},{0,8},{4,12},{24,16},{28,20},{8,24},{12,28},{17,1},{... | collective-permute-start | bytes 1572872 | tf_op jit(solution)/shard_map/ppermute | solution.py:644
  111.9 12.8 %collective-permute-start.17 = (bf16[2,256,512]{2,1,0:T(8,128)(2,1)S(1)}, bf16[2,256,512]{2,1,0:T(8,128)(2,1)S(1)}, u32[]{:S(2)}, u32[]{:S(2)}) collective-permute-start(bf16[2,256,512]{2,1,0:T(8,128)(2,1)S(1)} %get-tuple-element.39), channel_id=1, source_target_pairs={{20,0},{16,4},{4,8},{0,12},{28,16},{24,20},{12,24},{8,28},{21,1},{... | collective-permute-start | bytes 1572872 | tf_op jit(solution)/shard_map/ppermute | solution.py:644
  118.3 18.8 %collective-permute-start.18 = (bf16[2,256,512]{2,1,0:T(8,128)(2,1)S(1)}, bf16[2,256,512]{2,1,0:T(8,128)(2,1)S(1)}, u32[]{:S(2)}, u32[]{:S(2)}) collective-permute-start(bf16[2,256,512]{2,1,0:T(8,128)(2,1)S(1)} %get-tuple-element.40), channel_id=1, source_target_pairs={{4,0},{0,4},{20,8},{16,12},{12,16},{8,20},{28,24},{24,28},{5,1},{1... | collective-permute-start | bytes 1572872 | tf_op jit(solution)/shard_map/ppermute | solution.py:644
  119.2 22.8 %collective-permute-start.15 = (bf16[2,256,512]{2,1,0:T(8,128)(2,1)S(1)}, bf16[2,256,512]{2,1,0:T(8,128)(2,1)S(1)}, u32[]{:S(2)}, u32[]{:S(2)}) collective-permute-start(bf16[2,256,512]{2,1,0:T(8,128)(2,1)S(1)} %get-tuple-element.37.own), channel_id=1, source_target_pairs={{16,8},{20,12},{8,16},{12,20},{17,9},{21,13},{9,17},{13,21},{18,10... | collective-permute-start | bytes 1572872 | tf_op jit(solution)/shard_map/ppermute | solution.py:644

commit v23 on v20

--- a/solution.py
+++ b/solution.py
@@ -582,7 +582,7 @@
         scratch_shapes=weight_sems,
         compiler_params=params,
         cost_estimate=pl.CostEstimate(
-            flops=3 * 10**10, bytes_accessed=2**21, transcendentals=0
+            flops=10**10, bytes_accessed=2**21, transcendentals=0
         ),
     )(info, rows_held, rows_next, rows_far)
     rows_after = pl.pallas_call(

time: 149 us -> 144 us (0.966)
  waiting for transfers between devices: 75.5 us -> 67 us
  starting transfers between devices: 43.5 us -> 47.5 us
    ppermute x2, waiting for transfers between devices: 13.5 us -> 4.32 us  [aside(): return lax.ppermute(block, 'px', [(y, (y + 1) % 2) for y in range(2)])]
    ppermute x4, starting transfers between devices: 10.5 us -> 14.1 us  [on_device(): lax.ppermute(piece, ('sec', 'px'), back_pairs(a, b))]
    ppermute x4, waiting for transfers between devices: 3.84 us -> 6.54 us  [across(): return lax.ppermute(block, ('sec', 'px'), pairs(a, 0))]
    ppermute x4, waiting for transfers between devices: 20.9 us -> 19.1 us  [on_device(): lax.ppermute(piece, ('sec', 'px'), back_pairs(a, b))]
  transfers between devices with their start and end apart: 20 -> 20, of which waited for: 11 -> 12; matrix products, arithmetic and copies ran while one was open for 1% -> 1% of each run, Pallas kernels for 5% -> 5%
where the time goes in v23:
time: 144 us
  waiting for transfers between devices  67 us (47%)
  starting transfers between devices  47.5 us (33%)
  Pallas kernels  21.8 us (15%)
  local copies, waits for them, and re-layouts  3.47 us (2%)
  between operations  3.14 us (2%)
    ppermute x4, waiting for transfers between devices, on_device(): lax.ppermute(piece, ('sec', 'px'), back_pairs(a, b))  19.1 us
    ppermute x4, waiting for transfers between devices, on_device(): lax.ppermute(piece, ('sec', 'px'), pairs(a, b))  18.4 us
    ppermute x4, starting transfers between devices, on_device(): lax.ppermute(piece, ('sec', 'px'), back_pairs(a, b))  14.1 us
    ppermute x3, waiting for transfers between devices, over_z(): return lax.ppermute(block, 'py', [(z, z ^ bit) for z in range(py_count)])  9.69 us
    ppermute x4, starting transfers between devices, across(): return lax.ppermute(block, ('sec', 'px'), pairs(a, 0))  9.43 us
    pallas_call x1, Pallas kernels, on_device(): pl.pallas_call(last_kernel, out_shape=[double_shape, full_shape], in_spec...  9.12 us
    ppermute x4, starting transfers between devices, on_device(): lax.ppermute(piece, ('sec', 'px'), pairs(a, b))  7.17 us
    ppermute x3, starting transfers between devices, over_z(): return lax.ppermute(block, 'py', [(z, z ^ bit) for z in range(py_count)])  6.88 us
  transfers between devices with their start and end apart: 20, of which 12 were waited for; matrix products, arithmetic and copies ran while one was open for 1% of the time, Pallas kernels for 5%

profile of v23, /device:TPU:1, one launch (start us, length us, event | category | flops | bytes accessed | tf_op | source)
XLA Modules:
  0.0 143.9 jit_solution(11412411899168494100)
XLA Ops:
  1.0 1.1 broadcast_in_dim.4
  2.1 5.6 %all-to-all-start = ((bf16[4,4,64,512]{3,2,1,0:T(8,128)(2,1)}), bf16[4,4,64,512]{3,2,1,0:T(8,128)(2,1)S(1)}, u32[]{:S(2)}, u32[]{:S(2)}) async-start(bf16[4,4,64,512]{3,2,1,0:T(8,128)(2,1)} %broadcast_in_dim.4), calls=%async_computation | async-start | bytes 2097152 | tf_op jit(solution)/shard_map/all_to_all | solution.py:523
  7.8 1.6 %copy-done = bf16[2,1,256,2048]{3,2,1,0:T(8,128)(2,1)S(1)} copy-done((bf16[2,1,256,2048]{3,2,1,0:T(8,128)(2,1)S(1)}, bf16[2,1,256,2048]{3,2,1,0:T(8,128)(2,1)}, u32[]{:S(2)}) %copy-start) | copy-done | bytes 2097176
  9.4 2.3 %shard_map.55 = (bf16[2,288,512]{2,1,0:T(8,128)(2,1)S(1)}, bf16[2,288,512]{2,1,0:T(8,128)(2,1)}, bf16[2,288,512]{2,1,0:T(8,128)(2,1)}, bf16[2,288,512]{2,1,0:T(8,128)(2,1)}) custom-call(s32[6]{0:T(128)S(1)} %stack.83.place, bf16[2,256,2048]{2,1,0:T(8,128)(2,1)S(1)} %bitcast.29, bf16[8,32,512]{2,1,0:T(8,128)(2,1)S(1)} %bitcast.30), custom_call_target="tpu_custom_call" | custom-call | tf_op jit(solution)/shard_map/pallas_call | solution.py:512
  12.7 2.6 %collective-permute-start.2 = (bf16[2,288,512]{2,1,0:T(8,128)(2,1)}, bf16[2,288,512]{2,1,0:T(8,128)(2,1)S(1)}, u32[]{:S(2)}, u32[]{:S(2)}) collective-permute-start(bf16[2,288,512]{2,1,0:T(8,128)(2,1)} %get-tuple-element.24), channel_id=1, source_target_pairs={{0,20},{4,16},{8,4},{12,0},{16,28},{20,24},{24,12},{28,8},{1,21},{... | collective-permute-start | bytes 1769480 | tf_op jit(solution)/shard_map/ppermute | solution.py:521
  15.3 3.6 %collective-permute-start = (bf16[2,288,512]{2,1,0:T(8,128)(2,1)S(1)}, bf16[2,288,512]{2,1,0:T(8,128)(2,1)}, u32[]{:S(2)}, u32[]{:S(2)}) collective-permute-start(bf16[2,288,512]{2,1,0:T(8,128)(2,1)S(1)} %get-tuple-element.22.own), channel_id=1, source_target_pairs={{8,16},{12,20},{16,8},{20,12},{9,17},{13,21},{17,9},{21,13},{10,18... | collective-permute-start | bytes 1769480 | tf_op jit(solution)/shard_map/ppermute | solution.py:521
  23.1 17.7 %collective-permute-done.2.p2 = bf16[2,288,512]{2,1,0:T(8,128)(2,1)S(1)} collective-permute-done((bf16[2,288,512]{2,1,0:T(8,128)(2,1)}, bf16[2,288,512]{2,1,0:T(8,128)(2,1)S(1)}, u32[]{:S(2)}, u32[]{:S(2)}) %collective-permute-start.2) | collective-permute-done | bytes 589856 | tf_op jit(solution)/shard_map/ppermute | solution.py:521
  40.8 1.4 shard_map.56
  43.1 2.1 %collective-permute-start.6 = (bf16[1024,256]{1,0:T(8,128)(2,1)S(1)}, bf16[1024,256]{1,0:T(8,128)(2,1)S(1)}, u32[]{:S(2)}, u32[]{:S(2)}) collective-permute-start(bf16[1024,256]{1,0:T(8,128)(2,1)S(1)} %get-tuple-element.27.y_column), channel_id=1, source_target_pairs={{0,16},{4,20},{8,0},{12,4},{16,24},{20,28},{24,8},{28,12},{1,17},{... | collective-permute-start | bytes 1572872 | tf_op jit(solution)/shard_map/ppermute | solution.py:542
  45.2 2.6 %collective-permute-start.5 = (bf16[1024,256]{1,0:T(8,128)(2,1)S(1)}, bf16[1024,256]{1,0:T(8,128)(2,1)S(1)}, u32[]{:S(2)}, u32[]{:S(2)}) collective-permute-start(bf16[1024,256]{1,0:T(8,128)(2,1)S(1)} %get-tuple-element.27.y_column), channel_id=1, source_target_pairs={{8,16},{12,20},{16,8},{20,12},{9,17},{13,21},{17,9},{21,13},{10,18... | collective-permute-start | bytes 1572872 | tf_op jit(solution)/shard_map/ppermute | solution.py:542
  47.8 1.8 %collective-permute-start.10 = (bf16[4,64,512]{2,1,0:T(8,128)(2,1)S(1)}, bf16[4,64,512]{2,1,0:T(8,128)(2,1)S(1)}, u32[]{:S(2)}, u32[]{:S(2)}) collective-permute-start(bf16[4,64,512]{2,1,0:T(8,128)(2,1)S(1)} %bitcast.31), channel_id=1, source_target_pairs={{0,1},{1,0},{2,3},{3,2},{4,5},{5,4},{6,7},{7,6},{8,9},{9,8},{10,11... | collective-permute-start | bytes 786440 | tf_op jit(solution)/shard_map/ppermute | solution.py:548
  49.7 2.1 %collective-permute-start.12 = (bf16[4,64,512]{2,1,0:T(8,128)(2,1)S(1)}, bf16[4,64,512]{2,1,0:T(8,128)(2,1)S(1)}, u32[]{:S(2)}, u32[]{:S(2)}) collective-permute-start(bf16[4,64,512]{2,1,0:T(8,128)(2,1)S(1)} %bitcast.32), channel_id=1, source_target_pairs={{0,2},{1,3},{2,0},{3,1},{4,6},{5,7},{6,4},{7,5},{8,10},{9,11},{10,... | collective-permute-start | bytes 786440 | tf_op jit(solution)/shard_map/ppermute | solution.py:548
  51.7 1.6 %shard_map.57.rhs = bf16[2,2,512,512]{3,2,1,0:T(8,128)(2,1)S(1)} custom-call(s32[21]{0:T(128)S(1)} %stack.98.info, bf16[2,288,512]{2,1,0:T(8,128)(2,1)S(1)} %get-tuple-element.22.own, bf16[2,288,512]{2,1,0:T(8,128)(2,1)} %collective-permute-done.p0, bf16[2,288,512]{2,1,0:T(8,128)(2,1)S(1)} %collective-permute-done.1.p1, ...), custom_call_target="tpu_custom_call" | custom-call | tf_op jit(solution)/shard_map/pallas_call | solution.py:556
  54.4 3.8 %collective-permute-done.5.y0 = bf16[1024,256]{1,0:T(8,128)(2,1)S(1)} collective-permute-done((bf16[1024,256]{1,0:T(8,128)(2,1)S(1)}, bf16[1024,256]{1,0:T(8,128)(2,1)S(1)}, u32[]{:S(2)}, u32[]{:S(2)}) %collective-permute-start.5) | collective-permute-done | bytes 524320 | tf_op jit(solution)/shard_map/ppermute | solution.py:542
  59.9 4.7 %collective-permute-start.7 = (bf16[2,256,1024]{2,1,0:T(8,128)(2,1)S(1)}, bf16[2,256,1024]{2,1,0:T(8,128)(2,1)S(1)}, u32[]{:S(2)}, u32[]{:S(2)}) collective-permute-start(bf16[2,256,1024]{2,1,0:T(8,128)(2,1)S(1)} %get-tuple-element.28.x_both.xb), channel_id=1, source_target_pairs={{8,16},{12,20},{16,8},{20,12},{9,17},{13,21},{17,9},{21,13},{10,18... | collective-permute-start | bytes 3145736 | tf_op jit(solution)/shard_map/ppermute | solution.py:542
  64.6 3.0 %collective-permute-start.11 = (bf16[4,64,512]{2,1,0:T(8,128)(2,1)S(1)}, bf16[4,64,512]{2,1,0:T(8,128)(2,1)S(1)}, u32[]{:S(2)}, u32[]{:S(2)}) collective-permute-start(bf16[4,64,512]{2,1,0:T(8,128)(2,1)S(1)} %shard_map.59), channel_id=1, source_target_pairs={{0,2},{1,3},{2,0},{3,1},{4,6},{5,7},{6,4},{7,5},{8,10},{9,11},{10,... | collective-permute-start | bytes 786440 | tf_op jit(solution)/shard_map/ppermute | solution.py:548
  67.6 1.9 %shard_map.60.begun = bf16[2,512,512]{2,1,0:T(8,128)(2,1)S(1)} custom-call(s32[21]{0:T(128)S(1)} %stack.98.info, bf16[4,64,512]{2,1,0:T(8,128)(2,1)S(1)} %bitcast.33, bf16[4,64,512]{2,1,0:T(8,128)(2,1)S(1)} %collective-permute-done.10.rows.c1, bf16[4,64,512]{2,1,0:T(8,128)(2,1)S(1)} %collective-permute-done.12.c2), custom_call_target="tpu_custom_call" | custom-call | flops 10000000000 | bytes 2097152 | tf_op jit(solution)/shard_map/pallas_call | solution.py:577
  69.4 9.7 %collective-permute-done.11.c3 = bf16[4,64,512]{2,1,0:T(8,128)(2,1)S(1)} collective-permute-done((bf16[4,64,512]{2,1,0:T(8,128)(2,1)S(1)}, bf16[4,64,512]{2,1,0:T(8,128)(2,1)S(1)}, u32[]{:S(2)}, u32[]{:S(2)}) %collective-permute-start.11) | collective-permute-done | bytes 262176 | tf_op jit(solution)/shard_map/ppermute | solution.py:548
  80.2 3.3 %collective-permute-done.9.yf = bf16[2,1024,256]{2,1,0:T(8,128)(2,1)S(1)} collective-permute-done((bf16[2,1024,256]{2,1,0:T(8,128)(2,1)S(1)}, bf16[2,1024,256]{2,1,0:T(8,128)(2,1)S(1)}, u32[]{:S(2)}, u32[]{:S(2)}) %collective-permute-start.9) | collective-permute-done | bytes 1048608 | tf_op jit(solution)/shard_map/ppermute | solution.py:545
  83.5 2.7 %collective-permute-done.7.x0 = bf16[2,256,1024]{2,1,0:T(8,128)(2,1)S(1)} collective-permute-done((bf16[2,256,1024]{2,1,0:T(8,128)(2,1)S(1)}, bf16[2,256,1024]{2,1,0:T(8,128)(2,1)S(1)}, u32[]{:S(2)}, u32[]{:S(2)}) %collective-permute-start.7) | collective-permute-done | bytes 1048608 | tf_op jit(solution)/shard_map/ppermute | solution.py:542
  86.8 1.3 collective-permute-start.13
  88.1 6.7 %collective-permute-done.13.arrived = bf16[2,512,512]{2,1,0:T(8,128)(2,1)S(1)} collective-permute-done((bf16[2,512,512]{2,1,0:T(8,128)(2,1)S(1)}, bf16[2,512,512]{2,1,0:T(8,128)(2,1)S(1)}, u32[]{:S(2)}, u32[]{:S(2)}) %collective-permute-start.13) | collective-permute-done | bytes 1048608 | tf_op jit(solution)/shard_map/ppermute | solution.py:630
  94.8 9.1 %shard_map.63 = (bf16[2,2,512,512]{3,2,1,0:T(8,128)(2,1)S(1)}, bf16[2,512,512]{2,1,0:T(8,128)(2,1)S(1)}) custom-call(s32[21]{0:T(128)S(1)} %stack.98.info, bf16[2,256,1024]{2,1,0:T(8,128)(2,1)S(1)} %get-tuple-element.28.x_both.xb, bf16[2,256,1024]{2,1,0:T(8,128)(2,1)S(1)} %collective-permute-done.7.x0, bf16[2,256,1024]{2,1,0:T(8,128)(2,1)S(1)} %collective-permute-done.8.x1, ...), custom_call_target="tpu_custom_call" | custom-call | flops 6442450944 | bytes 8388608 | tf_op jit(solution)/shard_map/pallas_call | solution.py:631
  103.9 1.4 collective-permute-start.14
  105.3 2.2 %collective-permute-done.14.arrived = bf16[2,512,512]{2,1,0:T(8,128)(2,1)S(1)} collective-permute-done((bf16[2,512,512]{2,1,0:T(8,128)(2,1)S(1)}, bf16[2,512,512]{2,1,0:T(8,128)(2,1)S(1)}, u32[]{:S(2)}, u32[]{:S(2)}) %collective-permute-start.14) | collective-permute-done | bytes 1048608 | tf_op jit(solution)/shard_map/ppermute | solution.py:642
  108.3 3.6 %collective-permute-start.16 = (bf16[2,256,512]{2,1,0:T(8,128)(2,1)S(1)}, bf16[2,256,512]{2,1,0:T(8,128)(2,1)S(1)}, u32[]{:S(2)}, u32[]{:S(2)}) collective-permute-start(bf16[2,256,512]{2,1,0:T(8,128)(2,1)S(1)} %get-tuple-element.36), channel_id=1, source_target_pairs={{16,0},{20,4},{0,8},{4,12},{24,16},{28,20},{8,24},{12,28},{17,1},{... | collective-permute-start | bytes 1572872 | tf_op jit(solution)/shard_map/ppermute | solution.py:655
  111.9 6.4 %collective-permute-start.17 = (bf16[2,256,512]{2,1,0:T(8,128)(2,1)S(1)}, bf16[2,256,512]{2,1,0:T(8,128)(2,1)S(1)}, u32[]{:S(2)}, u32[]{:S(2)}) collective-permute-start(bf16[2,256,512]{2,1,0:T(8,128)(2,1)S(1)} %get-tuple-element.37), channel_id=1, source_target_pairs={{20,0},{16,4},{4,8},{0,12},{28,16},{24,20},{12,24},{8,28},{21,1},{... | collective-permute-start | bytes 1572872 | tf_op jit(solution)/shard_map/ppermute | solution.py:655
  118.3 4.1 %collective-permute-start.15 = (bf16[2,256,512]{2,1,0:T(8,128)(2,1)S(1)}, bf16[2,256,512]{2,1,0:T(8,128)(2,1)S(1)}, u32[]{:S(2)}, u32[]{:S(2)}) collective-permute-start(bf16[2,256,512]{2,1,0:T(8,128)(2,1)S(1)} %get-tuple-element.35.own), channel_id=1, source_target_pairs={{16,8},{20,12},{8,16},{12,20},{17,9},{21,13},{9,17},{13,21},{18,10... | collective-permute-start | bytes 1572872 | tf_op jit(solution)/shard_map/ppermute | solution.py:655
  122.5 2.0 %collective-permute-done.17.rest_2_ = bf16[2,256,512]{2,1,0:T(8,128)(2,1)S(1)} collective-permute-done((bf16[2,256,512]{2,1,0:T(8,128)(2,1)S(1)}, bf16[2,256,512]{2,1,0:T(8,128)(2,1)S(1)}, u32[]{:S(2)}, u32[]{:S(2)}) %collective-permute-start.17) | collective-permute-done | bytes 524320 | tf_op jit(solution)/shard_map/ppermute | solution.py:655
  124.5 11.9 %collective-permute-done.18.rest_3_ = bf16[2,256,512]{2,1,0:T(8,128)(2,1)S(1)} collective-permute-done((bf16[2,256,512]{2,1,0:T(8,128)(2,1)S(1)}, bf16[2,256,512]{2,1,0:T(8,128)(2,1)S(1)}, u32[]{:S(2)}, u32[]{:S(2)}) %collective-permute-start.18) | collective-permute-done | bytes 524320 | tf_op jit(solution)/shard_map/ppermute | solution.py:655
  136.4 5.2 %collective-permute-done.15.rest_0_ = bf16[2,256,512]{2,1,0:T(8,128)(2,1)S(1)} collective-permute-done((bf16[2,256,512]{2,1,0:T(8,128)(2,1)S(1)}, bf16[2,256,512]{2,1,0:T(8,128)(2,1)S(1)}, u32[]{:S(2)}, u32[]{:S(2)}) %collective-permute-start.15) | collective-permute-done | bytes 524320 | tf_op jit(solution)/shard_map/ppermute | solution.py:655
  141.6 2.2 %shard_map.65 = bf16[2,256,2048]{2,1,0:T(8,128)(2,1)} custom-call(s32[6]{0:T(128)S(1)} %stack.83.place, bf16[2,256,512]{2,1,0:T(8,128)(2,1)S(1)} %get-tuple-element.35.own, bf16[2,256,512]{2,1,0:T(8,128)(2,1)S(1)} %collective-permute-done.15.rest_0_, bf16[2,256,512]{2,1,0:T(8,128)(2,1)S(1)} %collective-permute-done.16.rest_1_, ...), custom_call_target="tpu_custom_call" | custom-call | tf_op jit(solution)/shard_map/pallas_call | solution.py:657
  (30 shorter events, 9.5 us)
Async XLA Ops:
  0.0 7.8 %copy-start.1 = (bf16[1,256,512]{2,1,0:T(8,128)(2,1)S(1)}, bf16[1,256,512]{2,1,0:T(8,128)(2,1)}, u32[]{:S(2)}) copy-start(bf16[1,256,512]{2,1,0:T(8,128)(2,1)} %param.7) | copy-start | bytes 786436
  2.1 16.9 %copy-start.2 = (s32[16]{0:T(128)S(1)}, s32[16]{0:T(128)}, u32[]{:S(2)}) copy-start(s32[16]{0:T(128)} %param.6) | copy-start | bytes 196
  2.1 38.7 %all-to-all-start = ((bf16[4,4,64,512]{3,2,1,0:T(8,128)(2,1)}), bf16[4,4,64,512]{3,2,1,0:T(8,128)(2,1)S(1)}, u32[]{:S(2)}, u32[]{:S(2)}) async-start(bf16[4,4,64,512]{3,2,1,0:T(8,128)(2,1)} %broadcast_in_dim.4), calls=%async_computation | async-start | bytes 2097152 | tf_op jit(solution)/shard_map/all_to_all | solution.py:523
  7.8 1.6 %copy-start = (bf16[2,1,256,2048]{3,2,1,0:T(8,128)(2,1)S(1)}, bf16[2,1,256,2048]{3,2,1,0:T(8,128)(2,1)}, u32[]{:S(2)}) copy-start(bf16[2,1,256,2048]{3,2,1,0:T(8,128)(2,1)} %param.5) | copy-start | bytes 6291460
  11.7 11.4 %collective-permute-start.1 = (bf16[2,288,512]{2,1,0:T(8,128)(2,1)}, bf16[2,288,512]{2,1,0:T(8,128)(2,1)S(1)}, u32[]{:S(2)}, u32[]{:S(2)}) collective-permute-start(bf16[2,288,512]{2,1,0:T(8,128)(2,1)} %get-tuple-element.23), channel_id=1, source_target_pairs={{0,16},{4,20},{8,0},{12,4},{16,24},{20,28},{24,8},{28,12},{1,17},{... | collective-permute-start | bytes 1769480 | tf_op jit(solution)/shard_map/ppermute | solution.py:521
  12.7 28.2 %collective-permute-start.2 = (bf16[2,288,512]{2,1,0:T(8,128)(2,1)}, bf16[2,288,512]{2,1,0:T(8,128)(2,1)S(1)}, u32[]{:S(2)}, u32[]{:S(2)}) collective-permute-start(bf16[2,288,512]{2,1,0:T(8,128)(2,1)} %get-tuple-element.24), channel_id=1, source_target_pairs={{0,20},{4,16},{8,4},{12,0},{16,28},{20,24},{24,12},{28,8},{1,21},{... | collective-permute-start | bytes 1769480 | tf_op jit(solution)/shard_map/ppermute | solution.py:521
  15.3 25.6 %collective-permute-start.3 = (bf16[2,288,512]{2,1,0:T(8,128)(2,1)}, bf16[2,288,512]{2,1,0:T(8,128)(2,1)S(1)}, u32[]{:S(2)}, u32[]{:S(2)}) collective-permute-start(bf16[2,288,512]{2,1,0:T(8,128)(2,1)} %get-tuple-element.25), channel_id=1, source_target_pairs={{0,4},{4,0},{8,20},{12,16},{16,12},{20,8},{24,28},{28,24},{1,5},{5... | collective-permute-start | bytes 1769480 | tf_op jit(solution)/shard_map/ppermute | solution.py:521
  15.3 25.6 %collective-permute-start = (bf16[2,288,512]{2,1,0:T(8,128)(2,1)S(1)}, bf16[2,288,512]{2,1,0:T(8,128)(2,1)}, u32[]{:S(2)}, u32[]{:S(2)}) collective-permute-start(bf16[2,288,512]{2,1,0:T(8,128)(2,1)S(1)} %get-tuple-element.22.own), channel_id=1, source_target_pairs={{8,16},{12,20},{16,8},{20,12},{9,17},{13,21},{17,9},{21,13},{10,18... | collective-permute-start | bytes 1769480 | tf_op jit(solution)/shard_map/ppermute | solution.py:521
  42.3 12.1 %collective-permute-start.4 = (bf16[256,1024]{1,0:T(8,128)(2,1)S(1)}, bf16[256,1024]{1,0:T(8,128)(2,1)S(1)}, u32[]{:S(2)}, u32[]{:S(2)}) collective-permute-start(bf16[256,1024]{1,0:T(8,128)(2,1)S(1)} %get-tuple-element.26.x_column), channel_id=1, source_target_pairs={{0,4},{4,0},{1,5},{5,1},{2,6},{6,2},{3,7},{7,3},{8,12},{12,8},{9,1... | collective-permute-start | bytes 1572872 | tf_op jit(solution)/shard_map/ppermute | solution.py:545
  43.1 11.4 %collective-permute-start.6 = (bf16[1024,256]{1,0:T(8,128)(2,1)S(1)}, bf16[1024,256]{1,0:T(8,128)(2,1)S(1)}, u32[]{:S(2)}, u32[]{:S(2)}) collective-permute-start(bf16[1024,256]{1,0:T(8,128)(2,1)S(1)} %get-tuple-element.27.y_column), channel_id=1, source_target_pairs={{0,16},{4,20},{8,0},{12,4},{16,24},{20,28},{24,8},{28,12},{1,17},{... | collective-permute-start | bytes 1572872 | tf_op jit(solution)/shard_map/ppermute | solution.py:542
  45.2 13.1 %collective-permute-start.5 = (bf16[1024,256]{1,0:T(8,128)(2,1)S(1)}, bf16[1024,256]{1,0:T(8,128)(2,1)S(1)}, u32[]{:S(2)}, u32[]{:S(2)}) collective-permute-start(bf16[1024,256]{1,0:T(8,128)(2,1)S(1)} %get-tuple-element.27.y_column), channel_id=1, source_target_pairs={{8,16},{12,20},{16,8},{20,12},{9,17},{13,21},{17,9},{21,13},{10,18... | collective-permute-start | bytes 1572872 | tf_op jit(solution)/shard_map/ppermute | solution.py:542
  47.8 16.7 %collective-permute-start.10 = (bf16[4,64,512]{2,1,0:T(8,128)(2,1)S(1)}, bf16[4,64,512]{2,1,0:T(8,128)(2,1)S(1)}, u32[]{:S(2)}, u32[]{:S(2)}) collective-permute-start(bf16[4,64,512]{2,1,0:T(8,128)(2,1)S(1)} %bitcast.31), channel_id=1, source_target_pairs={{0,1},{1,0},{2,3},{3,2},{4,5},{5,4},{6,7},{7,6},{8,9},{9,8},{10,11... | collective-permute-start | bytes 786440 | tf_op jit(solution)/shard_map/ppermute | solution.py:548
  49.7 17.9 %collective-permute-start.12 = (bf16[4,64,512]{2,1,0:T(8,128)(2,1)S(1)}, bf16[4,64,512]{2,1,0:T(8,128)(2,1)S(1)}, u32[]{:S(2)}, u32[]{:S(2)}) collective-permute-start(bf16[4,64,512]{2,1,0:T(8,128)(2,1)S(1)} %bitcast.32), channel_id=1, source_target_pairs={{0,2},{1,3},{2,0},{3,1},{4,6},{5,7},{6,4},{7,5},{8,10},{9,11},{10,... | collective-permute-start | bytes 786440 | tf_op jit(solution)/shard_map/ppermute | solution.py:548
  59.0 24.5 %collective-permute-start.9 = (bf16[2,1024,256]{2,1,0:T(8,128)(2,1)S(1)}, bf16[2,1024,256]{2,1,0:T(8,128)(2,1)S(1)}, u32[]{:S(2)}, u32[]{:S(2)}) collective-permute-start(bf16[2,1024,256]{2,1,0:T(8,128)(2,1)S(1)} %get-tuple-element.29.yb), channel_id=1, source_target_pairs={{0,4},{4,0},{1,5},{5,1},{2,6},{6,2},{3,7},{7,3},{8,12},{12,8},{9,1... | collective-permute-start | bytes 3145736 | tf_op jit(solution)/shard_map/ppermute | solution.py:545
  59.8 23.6 %collective-permute-start.8 = (bf16[2,256,1024]{2,1,0:T(8,128)(2,1)S(1)}, bf16[2,256,1024]{2,1,0:T(8,128)(2,1)S(1)}, u32[]{:S(2)}, u32[]{:S(2)}) collective-permute-start(bf16[2,256,1024]{2,1,0:T(8,128)(2,1)S(1)} %get-tuple-element.28.x_both.xb), channel_id=1, source_target_pairs={{0,16},{4,20},{8,0},{12,4},{16,24},{20,28},{24,8},{28,12},{1,17},{... | collective-permute-start | bytes 3145736 | tf_op jit(solution)/shard_map/ppermute | solution.py:542
  59.9 26.3 %collective-permute-start.7 = (bf16[2,256,1024]{2,1,0:T(8,128)(2,1)S(1)}, bf16[2,256,1024]{2,1,0:T(8,128)(2,1)S(1)}, u32[]{:S(2)}, u32[]{:S(2)}) collective-permute-start(bf16[2,256,1024]{2,1,0:T(8,128)(2,1)S(1)} %get-tuple-element.28.x_both.xb), channel_id=1, source_target_pairs={{8,16},{12,20},{16,8},{20,12},{9,17},{13,21},{17,9},{21,13},{10,18... | collective-permute-start | bytes 3145736 | tf_op jit(solution)/shard_map/ppermute | solution.py:542
  64.6 14.6 %collective-permute-start.11 = (bf16[4,64,512]{2,1,0:T(8,128)(2,1)S(1)}, bf16[4,64,512]{2,1,0:T(8,128)(2,1)S(1)}, u32[]{:S(2)}, u32[]{:S(2)}) collective-permute-start(bf16[4,64,512]{2,1,0:T(8,128)(2,1)S(1)} %shard_map.59), channel_id=1, source_target_pairs={{0,2},{1,3},{2,0},{3,1},{4,6},{5,7},{6,4},{7,5},{8,10},{9,11},{10,... | collective-permute-start | bytes 786440 | tf_op jit(solution)/shard_map/ppermute | solution.py:548
  86.8 8.0 %collective-permute-start.13 = (bf16[2,512,512]{2,1,0:T(8,128)(2,1)S(1)}, bf16[2,512,512]{2,1,0:T(8,128)(2,1)S(1)}, u32[]{:S(2)}, u32[]{:S(2)}) collective-permute-start(bf16[2,512,512]{2,1,0:T(8,128)(2,1)S(1)} %get-tuple-element.32.w_high), channel_id=1, source_target_pairs={{0,8},{16,24},{1,9},{17,25},{2,10},{18,26},{3,11},{19,27},{4,12},{... | collective-permute-start | bytes 3145736 | tf_op jit(solution)/shard_map/ppermute | solution.py:630
  103.9 3.6 %collective-permute-start.14 = (bf16[2,512,512]{2,1,0:T(8,128)(2,1)S(1)}, bf16[2,512,512]{2,1,0:T(8,128)(2,1)S(1)}, u32[]{:S(2)}, u32[]{:S(2)}) collective-permute-start(bf16[2,512,512]{2,1,0:T(8,128)(2,1)S(1)} %get-tuple-element.33), channel_id=1, source_target_pairs={{8,0},{24,16},{9,1},{25,17},{10,2},{26,18},{11,3},{27,19},{12,4},{... | collective-permute-start | bytes 3145736 | tf_op jit(solution)/shard_map/ppermute | solution.py:642
  108.3 14.1 %collective-permute-start.16 = (bf16[2,256,512]{2,1,0:T(8,128)(2,1)S(1)}, bf16[2,256,512]{2,1,0:T(8,128)(2,1)S(1)}, u32[]{:S(2)}, u32[]{:S(2)}) collective-permute-start(bf16[2,256,512]{2,1,0:T(8,128)(2,1)S(1)} %get-tuple-element.36), channel_id=1, source_target_pairs={{16,0},{20,4},{0,8},{4,12},{24,16},{28,20},{8,24},{12,28},{17,1},{... | collective-permute-start | bytes 1572872 | tf_op jit(solution)/shard_map/ppermute | solution.py:655
  111.9 12.6 %collective-permute-start.17 = (bf16[2,256,512]{2,1,0:T(8,128)(2,1)S(1)}, bf16[2,256,512]{2,1,0:T(8,128)(2,1)S(1)}, u32[]{:S(2)}, u32[]{:S(2)}) collective-permute-start(bf16[2,256,512]{2,1,0:T(8,128)(2,1)S(1)} %get-tuple-element.37), channel_id=1, source_target_pairs={{20,0},{16,4},{4,8},{0,12},{28,16},{24,20},{12,24},{8,28},{21,1},{... | collective-permute-start | bytes 1572872 | tf_op jit(solution)/shard_map/ppermute | solution.py:655
  118.3 18.1 %collective-permute-start.18 = (bf16[2,256,512]{2,1,0:T(8,128)(2,1)S(1)}, bf16[2,256,512]{2,1,0:T(8,128)(2,1)S(1)}, u32[]{:S(2)}, u32[]{:S(2)}) collective-permute-start(bf16[2,256,512]{2,1,0:T(8,128)(2,1)S(1)} %get-tuple-element.38), channel_id=1, source_target_pairs={{4,0},{0,4},{20,8},{16,12},{12,16},{8,20},{28,24},{24,28},{5,1},{1... | collective-permute-start | bytes 1572872 | tf_op jit(solution)/shard_map/ppermute | solution.py:655
  118.3 23.2 %collective-permute-start.15 = (bf16[2,256,512]{2,1,0:T(8,128)(2,1)S(1)}, bf16[2,256,512]{2,1,0:T(8,128)(2,1)S(1)}, u32[]{:S(2)}, u32[]{:S(2)}) collective-permute-start(bf16[2,256,512]{2,1,0:T(8,128)(2,1)S(1)} %get-tuple-element.35.own), channel_id=1, source_target_pairs={{16,8},{20,12},{8,16},{12,20},{17,9},{21,13},{9,17},{13,21},{18,10... | collective-permute-start | bytes 1572872 | tf_op jit(solution)/shard_map/ppermute | solution.py:655

commit v24 on v23

--- a/solution.py
+++ b/solution.py
@@ -658,7 +658,7 @@
         unpack_kernel,
         out_shape=jax.ShapeDtypeStruct(field.shape, bf16),
         in_specs=[in_smem] + [anywhere] * (len(rounds) + 1),
-        out_specs=in_vmem,
+        out_specs=anywhere,
         scratch_shapes=[pltpu.SemaphoreType.DMA((len(rounds),))],
         compiler_params=params,
     )(sends_to, results[0], *received)

time: 144 us -> 144 us (level)
  no operation moved by 1% of the time
where the time goes in v24:
time: 144 us
  waiting for transfers between devices  67 us (47%)
  starting transfers between devices  47.5 us (33%)
  Pallas kernels  21.5 us (15%)
  local copies, waits for them, and re-layouts  3.47 us (2%)
  between operations  3.14 us (2%)
    ppermute x4, waiting for transfers between devices, on_device(): lax.ppermute(piece, ('sec', 'px'), back_pairs(a, b))  19.1 us
    ppermute x4, waiting for transfers between devices, on_device(): lax.ppermute(piece, ('sec', 'px'), pairs(a, b))  18.4 us
    ppermute x4, starting transfers between devices, on_device(): lax.ppermute(piece, ('sec', 'px'), back_pairs(a, b))  14.1 us
    ppermute x3, waiting for transfers between devices, over_z(): return lax.ppermute(block, 'py', [(z, z ^ bit) for z in range(py_count)])  9.69 us
    ppermute x4, starting transfers between devices, across(): return lax.ppermute(block, ('sec', 'px'), pairs(a, 0))  9.43 us
    pallas_call x1, Pallas kernels, on_device(): pl.pallas_call(last_kernel, out_shape=[double_shape, full_shape], in_spec...  9.12 us
    ppermute x4, starting transfers between devices, on_device(): lax.ppermute(piece, ('sec', 'px'), pairs(a, b))  7.17 us
    ppermute x3, starting transfers between devices, over_z(): return lax.ppermute(block, 'py', [(z, z ^ bit) for z in range(py_count)])  6.88 us
  transfers between devices with their start and end apart: 20, of which 12 were waited for; matrix products, arithmetic and copies ran while one was open for 1% of the time, Pallas kernels for 5%

profile of v24, /device:TPU:1, one launch (start us, length us, event | category | flops | bytes accessed | tf_op | source)
XLA Modules:
  0.0 143.6 jit_solution(8177443578636762627)
XLA Ops:
  1.0 1.1 broadcast_in_dim.4
  2.1 5.6 %all-to-all-start = ((bf16[4,4,64,512]{3,2,1,0:T(8,128)(2,1)}), bf16[4,4,64,512]{3,2,1,0:T(8,128)(2,1)S(1)}, u32[]{:S(2)}, u32[]{:S(2)}) async-start(bf16[4,4,64,512]{3,2,1,0:T(8,128)(2,1)} %broadcast_in_dim.4), calls=%async_computation | async-start | bytes 2097152 | tf_op jit(solution)/shard_map/all_to_all | solution.py:523
  7.8 1.6 %copy-done = bf16[2,1,256,2048]{3,2,1,0:T(8,128)(2,1)S(1)} copy-done((bf16[2,1,256,2048]{3,2,1,0:T(8,128)(2,1)S(1)}, bf16[2,1,256,2048]{3,2,1,0:T(8,128)(2,1)}, u32[]{:S(2)}) %copy-start) | copy-done | bytes 2097176
  9.4 2.3 %shard_map.55 = (bf16[2,288,512]{2,1,0:T(8,128)(2,1)S(1)}, bf16[2,288,512]{2,1,0:T(8,128)(2,1)}, bf16[2,288,512]{2,1,0:T(8,128)(2,1)}, bf16[2,288,512]{2,1,0:T(8,128)(2,1)}) custom-call(s32[6]{0:T(128)S(1)} %stack.83.place, bf16[2,256,2048]{2,1,0:T(8,128)(2,1)S(1)} %bitcast.29, bf16[8,32,512]{2,1,0:T(8,128)(2,1)S(1)} %bitcast.30), custom_call_target="tpu_custom_call" | custom-call | tf_op jit(solution)/shard_map/pallas_call | solution.py:512
  12.7 2.6 %collective-permute-start.2 = (bf16[2,288,512]{2,1,0:T(8,128)(2,1)}, bf16[2,288,512]{2,1,0:T(8,128)(2,1)S(1)}, u32[]{:S(2)}, u32[]{:S(2)}) collective-permute-start(bf16[2,288,512]{2,1,0:T(8,128)(2,1)} %get-tuple-element.24), channel_id=1, source_target_pairs={{0,20},{4,16},{8,4},{12,0},{16,28},{20,24},{24,12},{28,8},{1,21},{... | collective-permute-start | bytes 1769480 | tf_op jit(solution)/shard_map/ppermute | solution.py:521
  15.3 3.6 %collective-permute-start = (bf16[2,288,512]{2,1,0:T(8,128)(2,1)S(1)}, bf16[2,288,512]{2,1,0:T(8,128)(2,1)}, u32[]{:S(2)}, u32[]{:S(2)}) collective-permute-start(bf16[2,288,512]{2,1,0:T(8,128)(2,1)S(1)} %get-tuple-element.22.own), channel_id=1, source_target_pairs={{8,16},{12,20},{16,8},{20,12},{9,17},{13,21},{17,9},{21,13},{10,18... | collective-permute-start | bytes 1769480 | tf_op jit(solution)/shard_map/ppermute | solution.py:521
  23.1 17.7 %collective-permute-done.2.p2 = bf16[2,288,512]{2,1,0:T(8,128)(2,1)S(1)} collective-permute-done((bf16[2,288,512]{2,1,0:T(8,128)(2,1)}, bf16[2,288,512]{2,1,0:T(8,128)(2,1)S(1)}, u32[]{:S(2)}, u32[]{:S(2)}) %collective-permute-start.2) | collective-permute-done | bytes 589856 | tf_op jit(solution)/shard_map/ppermute | solution.py:521
  40.8 1.4 shard_map.56
  43.1 2.1 %collective-permute-start.6 = (bf16[1024,256]{1,0:T(8,128)(2,1)S(1)}, bf16[1024,256]{1,0:T(8,128)(2,1)S(1)}, u32[]{:S(2)}, u32[]{:S(2)}) collective-permute-start(bf16[1024,256]{1,0:T(8,128)(2,1)S(1)} %get-tuple-element.27.y_column), channel_id=1, source_target_pairs={{0,16},{4,20},{8,0},{12,4},{16,24},{20,28},{24,8},{28,12},{1,17},{... | collective-permute-start | bytes 1572872 | tf_op jit(solution)/shard_map/ppermute | solution.py:542
  45.2 2.6 %collective-permute-start.5 = (bf16[1024,256]{1,0:T(8,128)(2,1)S(1)}, bf16[1024,256]{1,0:T(8,128)(2,1)S(1)}, u32[]{:S(2)}, u32[]{:S(2)}) collective-permute-start(bf16[1024,256]{1,0:T(8,128)(2,1)S(1)} %get-tuple-element.27.y_column), channel_id=1, source_target_pairs={{8,16},{12,20},{16,8},{20,12},{9,17},{13,21},{17,9},{21,13},{10,18... | collective-permute-start | bytes 1572872 | tf_op jit(solution)/shard_map/ppermute | solution.py:542
  47.8 1.8 %collective-permute-start.10 = (bf16[4,64,512]{2,1,0:T(8,128)(2,1)S(1)}, bf16[4,64,512]{2,1,0:T(8,128)(2,1)S(1)}, u32[]{:S(2)}, u32[]{:S(2)}) collective-permute-start(bf16[4,64,512]{2,1,0:T(8,128)(2,1)S(1)} %bitcast.31), channel_id=1, source_target_pairs={{0,1},{1,0},{2,3},{3,2},{4,5},{5,4},{6,7},{7,6},{8,9},{9,8},{10,11... | collective-permute-start | bytes 786440 | tf_op jit(solution)/shard_map/ppermute | solution.py:548
  49.7 2.1 %collective-permute-start.12 = (bf16[4,64,512]{2,1,0:T(8,128)(2,1)S(1)}, bf16[4,64,512]{2,1,0:T(8,128)(2,1)S(1)}, u32[]{:S(2)}, u32[]{:S(2)}) collective-permute-start(bf16[4,64,512]{2,1,0:T(8,128)(2,1)S(1)} %bitcast.32), channel_id=1, source_target_pairs={{0,2},{1,3},{2,0},{3,1},{4,6},{5,7},{6,4},{7,5},{8,10},{9,11},{10,... | collective-permute-start | bytes 786440 | tf_op jit(solution)/shard_map/ppermute | solution.py:548
  51.7 1.6 %shard_map.57.rhs = bf16[2,2,512,512]{3,2,1,0:T(8,128)(2,1)S(1)} custom-call(s32[21]{0:T(128)S(1)} %stack.98.info, bf16[2,288,512]{2,1,0:T(8,128)(2,1)S(1)} %get-tuple-element.22.own, bf16[2,288,512]{2,1,0:T(8,128)(2,1)} %collective-permute-done.p0, bf16[2,288,512]{2,1,0:T(8,128)(2,1)S(1)} %collective-permute-done.1.p1, ...), custom_call_target="tpu_custom_call" | custom-call | tf_op jit(solution)/shard_map/pallas_call | solution.py:556
  54.4 3.8 %collective-permute-done.5.y0 = bf16[1024,256]{1,0:T(8,128)(2,1)S(1)} collective-permute-done((bf16[1024,256]{1,0:T(8,128)(2,1)S(1)}, bf16[1024,256]{1,0:T(8,128)(2,1)S(1)}, u32[]{:S(2)}, u32[]{:S(2)}) %collective-permute-start.5) | collective-permute-done | bytes 524320 | tf_op jit(solution)/shard_map/ppermute | solution.py:542
  59.9 4.7 %collective-permute-start.7 = (bf16[2,256,1024]{2,1,0:T(8,128)(2,1)S(1)}, bf16[2,256,1024]{2,1,0:T(8,128)(2,1)S(1)}, u32[]{:S(2)}, u32[]{:S(2)}) collective-permute-start(bf16[2,256,1024]{2,1,0:T(8,128)(2,1)S(1)} %get-tuple-element.28.x_both.xb), channel_id=1, source_target_pairs={{8,16},{12,20},{16,8},{20,12},{9,17},{13,21},{17,9},{21,13},{10,18... | collective-permute-start | bytes 3145736 | tf_op jit(solution)/shard_map/ppermute | solution.py:542
  64.6 3.0 %collective-permute-start.11 = (bf16[4,64,512]{2,1,0:T(8,128)(2,1)S(1)}, bf16[4,64,512]{2,1,0:T(8,128)(2,1)S(1)}, u32[]{:S(2)}, u32[]{:S(2)}) collective-permute-start(bf16[4,64,512]{2,1,0:T(8,128)(2,1)S(1)} %shard_map.59), channel_id=1, source_target_pairs={{0,2},{1,3},{2,0},{3,1},{4,6},{5,7},{6,4},{7,5},{8,10},{9,11},{10,... | collective-permute-start | bytes 786440 | tf_op jit(solution)/shard_map/ppermute | solution.py:548
  67.6 1.9 %shard_map.60.begun = bf16[2,512,512]{2,1,0:T(8,128)(2,1)S(1)} custom-call(s32[21]{0:T(128)S(1)} %stack.98.info, bf16[4,64,512]{2,1,0:T(8,128)(2,1)S(1)} %bitcast.33, bf16[4,64,512]{2,1,0:T(8,128)(2,1)S(1)} %collective-permute-done.10.rows.c1, bf16[4,64,512]{2,1,0:T(8,128)(2,1)S(1)} %collective-permute-done.12.c2), custom_call_target="tpu_custom_call" | custom-call | flops 10000000000 | bytes 2097152 | tf_op jit(solution)/shard_map/pallas_call | solution.py:577
  69.4 9.7 %collective-permute-done.11.c3 = bf16[4,64,512]{2,1,0:T(8,128)(2,1)S(1)} collective-permute-done((bf16[4,64,512]{2,1,0:T(8,128)(2,1)S(1)}, bf16[4,64,512]{2,1,0:T(8,128)(2,1)S(1)}, u32[]{:S(2)}, u32[]{:S(2)}) %collective-permute-start.11) | collective-permute-done | bytes 262176 | tf_op jit(solution)/shard_map/ppermute | solution.py:548
  80.2 3.3 %collective-permute-done.9.yf = bf16[2,1024,256]{2,1,0:T(8,128)(2,1)S(1)} collective-permute-done((bf16[2,1024,256]{2,1,0:T(8,128)(2,1)S(1)}, bf16[2,1024,256]{2,1,0:T(8,128)(2,1)S(1)}, u32[]{:S(2)}, u32[]{:S(2)}) %collective-permute-start.9) | collective-permute-done | bytes 1048608 | tf_op jit(solution)/shard_map/ppermute | solution.py:545
  83.5 2.7 %collective-permute-done.7.x0 = bf16[2,256,1024]{2,1,0:T(8,128)(2,1)S(1)} collective-permute-done((bf16[2,256,1024]{2,1,0:T(8,128)(2,1)S(1)}, bf16[2,256,1024]{2,1,0:T(8,128)(2,1)S(1)}, u32[]{:S(2)}, u32[]{:S(2)}) %collective-permute-start.7) | collective-permute-done | bytes 1048608 | tf_op jit(solution)/shard_map/ppermute | solution.py:542
  86.8 1.3 collective-permute-start.13
  88.1 6.7 %collective-permute-done.13.arrived = bf16[2,512,512]{2,1,0:T(8,128)(2,1)S(1)} collective-permute-done((bf16[2,512,512]{2,1,0:T(8,128)(2,1)S(1)}, bf16[2,512,512]{2,1,0:T(8,128)(2,1)S(1)}, u32[]{:S(2)}, u32[]{:S(2)}) %collective-permute-start.13) | collective-permute-done | bytes 1048608 | tf_op jit(solution)/shard_map/ppermute | solution.py:630
  94.8 9.1 %shard_map.63 = (bf16[2,2,512,512]{3,2,1,0:T(8,128)(2,1)S(1)}, bf16[2,512,512]{2,1,0:T(8,128)(2,1)S(1)}) custom-call(s32[21]{0:T(128)S(1)} %stack.98.info, bf16[2,256,1024]{2,1,0:T(8,128)(2,1)S(1)} %get-tuple-element.28.x_both.xb, bf16[2,256,1024]{2,1,0:T(8,128)(2,1)S(1)} %collective-permute-done.7.x0, bf16[2,256,1024]{2,1,0:T(8,128)(2,1)S(1)} %collective-permute-done.8.x1, ...), custom_call_target="tpu_custom_call" | custom-call | flops 6442450944 | bytes 8388608 | tf_op jit(solution)/shard_map/pallas_call | solution.py:631
  103.9 1.4 collective-permute-start.14
  105.3 2.2 %collective-permute-done.14.arrived = bf16[2,512,512]{2,1,0:T(8,128)(2,1)S(1)} collective-permute-done((bf16[2,512,512]{2,1,0:T(8,128)(2,1)S(1)}, bf16[2,512,512]{2,1,0:T(8,128)(2,1)S(1)}, u32[]{:S(2)}, u32[]{:S(2)}) %collective-permute-start.14) | collective-permute-done | bytes 1048608 | tf_op jit(solution)/shard_map/ppermute | solution.py:642
  108.3 3.6 %collective-permute-start.16 = (bf16[2,256,512]{2,1,0:T(8,128)(2,1)S(1)}, bf16[2,256,512]{2,1,0:T(8,128)(2,1)S(1)}, u32[]{:S(2)}, u32[]{:S(2)}) collective-permute-start(bf16[2,256,512]{2,1,0:T(8,128)(2,1)S(1)} %get-tuple-element.36), channel_id=1, source_target_pairs={{16,0},{20,4},{0,8},{4,12},{24,16},{28,20},{8,24},{12,28},{17,1},{... | collective-permute-start | bytes 1572872 | tf_op jit(solution)/shard_map/ppermute | solution.py:655
  111.9 6.4 %collective-permute-start.17 = (bf16[2,256,512]{2,1,0:T(8,128)(2,1)S(1)}, bf16[2,256,512]{2,1,0:T(8,128)(2,1)S(1)}, u32[]{:S(2)}, u32[]{:S(2)}) collective-permute-start(bf16[2,256,512]{2,1,0:T(8,128)(2,1)S(1)} %get-tuple-element.37), channel_id=1, source_target_pairs={{20,0},{16,4},{4,8},{0,12},{28,16},{24,20},{12,24},{8,28},{21,1},{... | collective-permute-start | bytes 1572872 | tf_op jit(solution)/shard_map/ppermute | solution.py:655
  118.3 4.1 %collective-permute-start.15 = (bf16[2,256,512]{2,1,0:T(8,128)(2,1)S(1)}, bf16[2,256,512]{2,1,0:T(8,128)(2,1)S(1)}, u32[]{:S(2)}, u32[]{:S(2)}) collective-permute-start(bf16[2,256,512]{2,1,0:T(8,128)(2,1)S(1)} %get-tuple-element.35.own), channel_id=1, source_target_pairs={{16,8},{20,12},{8,16},{12,20},{17,9},{21,13},{9,17},{13,21},{18,10... | collective-permute-start | bytes 1572872 | tf_op jit(solution)/shard_map/ppermute | solution.py:655
  122.5 2.0 %collective-permute-done.17.rest_2_ = bf16[2,256,512]{2,1,0:T(8,128)(2,1)S(1)} collective-permute-done((bf16[2,256,512]{2,1,0:T(8,128)(2,1)S(1)}, bf16[2,256,512]{2,1,0:T(8,128)(2,1)S(1)}, u32[]{:S(2)}, u32[]{:S(2)}) %collective-permute-start.17) | collective-permute-done | bytes 524320 | tf_op jit(solution)/shard_map/ppermute | solution.py:655
  124.5 11.9 %collective-permute-done.18.rest_3_ = bf16[2,256,512]{2,1,0:T(8,128)(2,1)S(1)} collective-permute-done((bf16[2,256,512]{2,1,0:T(8,128)(2,1)S(1)}, bf16[2,256,512]{2,1,0:T(8,128)(2,1)S(1)}, u32[]{:S(2)}, u32[]{:S(2)}) %collective-permute-start.18) | collective-permute-done | bytes 524320 | tf_op jit(solution)/shard_map/ppermute | solution.py:655
  136.4 5.2 %collective-permute-done.15.rest_0_ = bf16[2,256,512]{2,1,0:T(8,128)(2,1)S(1)} collective-permute-done((bf16[2,256,512]{2,1,0:T(8,128)(2,1)S(1)}, bf16[2,256,512]{2,1,0:T(8,128)(2,1)S(1)}, u32[]{:S(2)}, u32[]{:S(2)}) %collective-permute-start.15) | collective-permute-done | bytes 524320 | tf_op jit(solution)/shard_map/ppermute | solution.py:655
  141.6 1.9 %shard_map.65 = bf16[2,256,2048]{2,1,0:T(8,128)(2,1)} custom-call(s32[6]{0:T(128)S(1)} %stack.83.place, bf16[2,256,512]{2,1,0:T(8,128)(2,1)S(1)} %get-tuple-element.35.own, bf16[2,256,512]{2,1,0:T(8,128)(2,1)S(1)} %collective-permute-done.15.rest_0_, bf16[2,256,512]{2,1,0:T(8,128)(2,1)S(1)} %collective-permute-done.16.rest_1_, ...), custom_call_target="tpu_custom_call" | custom-call | tf_op jit(solution)/shard_map/pallas_call | solution.py:657
  (30 shorter events, 9.5 us)
Async XLA Ops:
  0.0 7.8 %copy-start.1 = (bf16[1,256,512]{2,1,0:T(8,128)(2,1)S(1)}, bf16[1,256,512]{2,1,0:T(8,128)(2,1)}, u32[]{:S(2)}) copy-start(bf16[1,256,512]{2,1,0:T(8,128)(2,1)} %param.7) | copy-start | bytes 786436
  2.1 16.9 %copy-start.2 = (s32[16]{0:T(128)S(1)}, s32[16]{0:T(128)}, u32[]{:S(2)}) copy-start(s32[16]{0:T(128)} %param.6) | copy-start | bytes 196
  2.1 38.7 %all-to-all-start = ((bf16[4,4,64,512]{3,2,1,0:T(8,128)(2,1)}), bf16[4,4,64,512]{3,2,1,0:T(8,128)(2,1)S(1)}, u32[]{:S(2)}, u32[]{:S(2)}) async-start(bf16[4,4,64,512]{3,2,1,0:T(8,128)(2,1)} %broadcast_in_dim.4), calls=%async_computation | async-start | bytes 2097152 | tf_op jit(solution)/shard_map/all_to_all | solution.py:523
  7.8 1.6 %copy-start = (bf16[2,1,256,2048]{3,2,1,0:T(8,128)(2,1)S(1)}, bf16[2,1,256,2048]{3,2,1,0:T(8,128)(2,1)}, u32[]{:S(2)}) copy-start(bf16[2,1,256,2048]{3,2,1,0:T(8,128)(2,1)} %param.5) | copy-start | bytes 6291460
  11.7 11.4 %collective-permute-start.1 = (bf16[2,288,512]{2,1,0:T(8,128)(2,1)}, bf16[2,288,512]{2,1,0:T(8,128)(2,1)S(1)}, u32[]{:S(2)}, u32[]{:S(2)}) collective-permute-start(bf16[2,288,512]{2,1,0:T(8,128)(2,1)} %get-tuple-element.23), channel_id=1, source_target_pairs={{0,16},{4,20},{8,0},{12,4},{16,24},{20,28},{24,8},{28,12},{1,17},{... | collective-permute-start | bytes 1769480 | tf_op jit(solution)/shard_map/ppermute | solution.py:521
  12.7 28.2 %collective-permute-start.2 = (bf16[2,288,512]{2,1,0:T(8,128)(2,1)}, bf16[2,288,512]{2,1,0:T(8,128)(2,1)S(1)}, u32[]{:S(2)}, u32[]{:S(2)}) collective-permute-start(bf16[2,288,512]{2,1,0:T(8,128)(2,1)} %get-tuple-element.24), channel_id=1, source_target_pairs={{0,20},{4,16},{8,4},{12,0},{16,28},{20,24},{24,12},{28,8},{1,21},{... | collective-permute-start | bytes 1769480 | tf_op jit(solution)/shard_map/ppermute | solution.py:521
  15.3 25.6 %collective-permute-start.3 = (bf16[2,288,512]{2,1,0:T(8,128)(2,1)}, bf16[2,288,512]{2,1,0:T(8,128)(2,1)S(1)}, u32[]{:S(2)}, u32[]{:S(2)}) collective-permute-start(bf16[2,288,512]{2,1,0:T(8,128)(2,1)} %get-tuple-element.25), channel_id=1, source_target_pairs={{0,4},{4,0},{8,20},{12,16},{16,12},{20,8},{24,28},{28,24},{1,5},{5... | collective-permute-start | bytes 1769480 | tf_op jit(solution)/shard_map/ppermute | solution.py:521
  15.3 25.6 %collective-permute-start = (bf16[2,288,512]{2,1,0:T(8,128)(2,1)S(1)}, bf16[2,288,512]{2,1,0:T(8,128)(2,1)}, u32[]{:S(2)}, u32[]{:S(2)}) collective-permute-start(bf16[2,288,512]{2,1,0:T(8,128)(2,1)S(1)} %get-tuple-element.22.own), channel_id=1, source_target_pairs={{8,16},{12,20},{16,8},{20,12},{9,17},{13,21},{17,9},{21,13},{10,18... | collective-permute-start | bytes 1769480 | tf_op jit(solution)/shard_map/ppermute | solution.py:521
  42.3 12.1 %collective-permute-start.4 = (bf16[256,1024]{1,0:T(8,128)(2,1)S(1)}, bf16[256,1024]{1,0:T(8,128)(2,1)S(1)}, u32[]{:S(2)}, u32[]{:S(2)}) collective-permute-start(bf16[256,1024]{1,0:T(8,128)(2,1)S(1)} %get-tuple-element.26.x_column), channel_id=1, source_target_pairs={{0,4},{4,0},{1,5},{5,1},{2,6},{6,2},{3,7},{7,3},{8,12},{12,8},{9,1... | collective-permute-start | bytes 1572872 | tf_op jit(solution)/shard_map/ppermute | solution.py:545
  43.1 11.4 %collective-permute-start.6 = (bf16[1024,256]{1,0:T(8,128)(2,1)S(1)}, bf16[1024,256]{1,0:T(8,128)(2,1)S(1)}, u32[]{:S(2)}, u32[]{:S(2)}) collective-permute-start(bf16[1024,256]{1,0:T(8,128)(2,1)S(1)} %get-tuple-element.27.y_column), channel_id=1, source_target_pairs={{0,16},{4,20},{8,0},{12,4},{16,24},{20,28},{24,8},{28,12},{1,17},{... | collective-permute-start | bytes 1572872 | tf_op jit(solution)/shard_map/ppermute | solution.py:542
  45.2 13.1 %collective-permute-start.5 = (bf16[1024,256]{1,0:T(8,128)(2,1)S(1)}, bf16[1024,256]{1,0:T(8,128)(2,1)S(1)}, u32[]{:S(2)}, u32[]{:S(2)}) collective-permute-start(bf16[1024,256]{1,0:T(8,128)(2,1)S(1)} %get-tuple-element.27.y_column), channel_id=1, source_target_pairs={{8,16},{12,20},{16,8},{20,12},{9,17},{13,21},{17,9},{21,13},{10,18... | collective-permute-start | bytes 1572872 | tf_op jit(solution)/shard_map/ppermute | solution.py:542
  47.8 16.7 %collective-permute-start.10 = (bf16[4,64,512]{2,1,0:T(8,128)(2,1)S(1)}, bf16[4,64,512]{2,1,0:T(8,128)(2,1)S(1)}, u32[]{:S(2)}, u32[]{:S(2)}) collective-permute-start(bf16[4,64,512]{2,1,0:T(8,128)(2,1)S(1)} %bitcast.31), channel_id=1, source_target_pairs={{0,1},{1,0},{2,3},{3,2},{4,5},{5,4},{6,7},{7,6},{8,9},{9,8},{10,11... | collective-permute-start | bytes 786440 | tf_op jit(solution)/shard_map/ppermute | solution.py:548
  49.7 17.9 %collective-permute-start.12 = (bf16[4,64,512]{2,1,0:T(8,128)(2,1)S(1)}, bf16[4,64,512]{2,1,0:T(8,128)(2,1)S(1)}, u32[]{:S(2)}, u32[]{:S(2)}) collective-permute-start(bf16[4,64,512]{2,1,0:T(8,128)(2,1)S(1)} %bitcast.32), channel_id=1, source_target_pairs={{0,2},{1,3},{2,0},{3,1},{4,6},{5,7},{6,4},{7,5},{8,10},{9,11},{10,... | collective-permute-start | bytes 786440 | tf_op jit(solution)/shard_map/ppermute | solution.py:548
  59.0 24.5 %collective-permute-start.9 = (bf16[2,1024,256]{2,1,0:T(8,128)(2,1)S(1)}, bf16[2,1024,256]{2,1,0:T(8,128)(2,1)S(1)}, u32[]{:S(2)}, u32[]{:S(2)}) collective-permute-start(bf16[2,1024,256]{2,1,0:T(8,128)(2,1)S(1)} %get-tuple-element.29.yb), channel_id=1, source_target_pairs={{0,4},{4,0},{1,5},{5,1},{2,6},{6,2},{3,7},{7,3},{8,12},{12,8},{9,1... | collective-permute-start | bytes 3145736 | tf_op jit(solution)/shard_map/ppermute | solution.py:545
  59.8 23.6 %collective-permute-start.8 = (bf16[2,256,1024]{2,1,0:T(8,128)(2,1)S(1)}, bf16[2,256,1024]{2,1,0:T(8,128)(2,1)S(1)}, u32[]{:S(2)}, u32[]{:S(2)}) collective-permute-start(bf16[2,256,1024]{2,1,0:T(8,128)(2,1)S(1)} %get-tuple-element.28.x_both.xb), channel_id=1, source_target_pairs={{0,16},{4,20},{8,0},{12,4},{16,24},{20,28},{24,8},{28,12},{1,17},{... | collective-permute-start | bytes 3145736 | tf_op jit(solution)/shard_map/ppermute | solution.py:542
  59.9 26.3 %collective-permute-start.7 = (bf16[2,256,1024]{2,1,0:T(8,128)(2,1)S(1)}, bf16[2,256,1024]{2,1,0:T(8,128)(2,1)S(1)}, u32[]{:S(2)}, u32[]{:S(2)}) collective-permute-start(bf16[2,256,1024]{2,1,0:T(8,128)(2,1)S(1)} %get-tuple-element.28.x_both.xb), channel_id=1, source_target_pairs={{8,16},{12,20},{16,8},{20,12},{9,17},{13,21},{17,9},{21,13},{10,18... | collective-permute-start | bytes 3145736 | tf_op jit(solution)/shard_map/ppermute | solution.py:542
  64.6 14.6 %collective-permute-start.11 = (bf16[4,64,512]{2,1,0:T(8,128)(2,1)S(1)}, bf16[4,64,512]{2,1,0:T(8,128)(2,1)S(1)}, u32[]{:S(2)}, u32[]{:S(2)}) collective-permute-start(bf16[4,64,512]{2,1,0:T(8,128)(2,1)S(1)} %shard_map.59), channel_id=1, source_target_pairs={{0,2},{1,3},{2,0},{3,1},{4,6},{5,7},{6,4},{7,5},{8,10},{9,11},{10,... | collective-permute-start | bytes 786440 | tf_op jit(solution)/shard_map/ppermute | solution.py:548
  86.8 8.0 %collective-permute-start.13 = (bf16[2,512,512]{2,1,0:T(8,128)(2,1)S(1)}, bf16[2,512,512]{2,1,0:T(8,128)(2,1)S(1)}, u32[]{:S(2)}, u32[]{:S(2)}) collective-permute-start(bf16[2,512,512]{2,1,0:T(8,128)(2,1)S(1)} %get-tuple-element.32.w_high), channel_id=1, source_target_pairs={{0,8},{16,24},{1,9},{17,25},{2,10},{18,26},{3,11},{19,27},{4,12},{... | collective-permute-start | bytes 3145736 | tf_op jit(solution)/shard_map/ppermute | solution.py:630
  103.9 3.6 %collective-permute-start.14 = (bf16[2,512,512]{2,1,0:T(8,128)(2,1)S(1)}, bf16[2,512,512]{2,1,0:T(8,128)(2,1)S(1)}, u32[]{:S(2)}, u32[]{:S(2)}) collective-permute-start(bf16[2,512,512]{2,1,0:T(8,128)(2,1)S(1)} %get-tuple-element.33), channel_id=1, source_target_pairs={{8,0},{24,16},{9,1},{25,17},{10,2},{26,18},{11,3},{27,19},{12,4},{... | collective-permute-start | bytes 3145736 | tf_op jit(solution)/shard_map/ppermute | solution.py:642
  108.3 14.1 %collective-permute-start.16 = (bf16[2,256,512]{2,1,0:T(8,128)(2,1)S(1)}, bf16[2,256,512]{2,1,0:T(8,128)(2,1)S(1)}, u32[]{:S(2)}, u32[]{:S(2)}) collective-permute-start(bf16[2,256,512]{2,1,0:T(8,128)(2,1)S(1)} %get-tuple-element.36), channel_id=1, source_target_pairs={{16,0},{20,4},{0,8},{4,12},{24,16},{28,20},{8,24},{12,28},{17,1},{... | collective-permute-start | bytes 1572872 | tf_op jit(solution)/shard_map/ppermute | solution.py:655
  111.9 12.6 %collective-permute-start.17 = (bf16[2,256,512]{2,1,0:T(8,128)(2,1)S(1)}, bf16[2,256,512]{2,1,0:T(8,128)(2,1)S(1)}, u32[]{:S(2)}, u32[]{:S(2)}) collective-permute-start(bf16[2,256,512]{2,1,0:T(8,128)(2,1)S(1)} %get-tuple-element.37), channel_id=1, source_target_pairs={{20,0},{16,4},{4,8},{0,12},{28,16},{24,20},{12,24},{8,28},{21,1},{... | collective-permute-start | bytes 1572872 | tf_op jit(solution)/shard_map/ppermute | solution.py:655
  118.3 18.1 %collective-permute-start.18 = (bf16[2,256,512]{2,1,0:T(8,128)(2,1)S(1)}, bf16[2,256,512]{2,1,0:T(8,128)(2,1)S(1)}, u32[]{:S(2)}, u32[]{:S(2)}) collective-permute-start(bf16[2,256,512]{2,1,0:T(8,128)(2,1)S(1)} %get-tuple-element.38), channel_id=1, source_target_pairs={{4,0},{0,4},{20,8},{16,12},{12,16},{8,20},{28,24},{24,28},{5,1},{1... | collective-permute-start | bytes 1572872 | tf_op jit(solution)/shard_map/ppermute | solution.py:655
  118.3 23.2 %collective-permute-start.15 = (bf16[2,256,512]{2,1,0:T(8,128)(2,1)S(1)}, bf16[2,256,512]{2,1,0:T(8,128)(2,1)S(1)}, u32[]{:S(2)}, u32[]{:S(2)}) collective-permute-start(bf16[2,256,512]{2,1,0:T(8,128)(2,1)S(1)} %get-tuple-element.35.own), channel_id=1, source_target_pairs={{16,8},{20,12},{8,16},{12,20},{17,9},{21,13},{9,17},{13,21},{18,10... | collective-permute-start | bytes 1572872 | tf_op jit(solution)/shard_map/ppermute | solution.py:655
